TPU v7x, 32 devices: a whole 2x2x4 slice. The times are simulated.
32 devices in a mesh: seq: 8 (over z, y), tp: 4 (over x, core).
Axes of the slice: x: 2, y: 2, z: 4, core: 2. Of those that a mesh axis runs over, the one named last changes fastest.
Arguments:
- normed: bfloat16 [4, 8192, 1024], P(None, 'seq'), may hold values from -6 to 6
- grad_out: bfloat16 [4, 8192, 1024], P(None, 'seq'), may hold values from -16 to 16
- value_weight: bfloat16 [1024, 1024], P(None, 'tp'), may hold values from -0.1875 to 0.1875
- gate_weight: bfloat16 [1024, 1024], P(None, 'tp'), may hold values from -0.1875 to 0.1875
- depth_taps: float32 [9, 1024], P(None, 'tp'), may hold values from -2 to 2
- norm_gain: float32 [1024], P('tp'), may hold values from 0.1 to 1.9
- norm_shift: float32 [1024], P('tp'), may hold values from -1 to 1
- out_weight: bfloat16 [1024, 1024], P(None, 'tp'), may hold values from -0.1875 to 0.1875
- lengths: int32 [4], replicated, may hold values from 2048 to 8192, as said below
Outputs:
- grad_in: bfloat16 [4, 1024, 8192], P(None, ('seq', 'tp'))
- grad_w_value: float32 [1024, 1024], P('seq', 'tp')
- grad_w_gate: float32 [1024, 1024], P('seq', 'tp')
- grad_w_out: float32 [1024, 1024], P('seq', 'tp')
- grad_taps: float32 [9, 1024], P(None, 'tp')
- grad_gain: float32 [1024], P('tp')
- grad_shift: float32 [1024], P('tp')
Inputs may be any that keep to these rules, and one draw needn't show every extreme that they name: `lengths`: frames of each recording that are valid; some recording is valid to its last frame.
All inputs are finite; a program needn't handle non-finite values.
Results may differ from a plain program's by a relative error of at most 0.01.
Values may be sent and summed in bfloat16 or wider, within the bound.
No kernel may reach another device: no remote copies, remote signals or barrier semaphores. Data moves between devices by JAX's collectives and lax.ppermute only.
A program may use at most 128 MiB of HBM per device.

v0:
```python
import jax
import jax.numpy as jnp
from jax import lax
from jax.sharding import PartitionSpec as P

epsilon = 1e-05


def extended(block, sides, width):
    for axis, dim in sides:
        count = lax.axis_size(axis)
        forward = [(i, i + 1) for i in range(count - 1)]
        backward = [(target, source) for source, target in forward]
        low = lax.ppermute(
            lax.slice_in_dim(block, block.shape[dim] - width, None, axis=dim), axis, forward
        )
        high = lax.ppermute(lax.slice_in_dim(block, 0, width, axis=dim), axis, backward)
        block = jnp.concatenate([low, block, high], axis=dim)
    return block


def frame_edges(field, margin):
    return extended(field, (("seq", 1),), margin)


def channel_sums(parts):
    return lax.psum(parts, "seq")


def per_device(
    normed,
    grad_out,
    value_weight,
    gate_weight,
    depth_taps,
    norm_gain,
    norm_shift,
    out_weight,
    lengths,
):
    record_count, frames, model_width = normed.shape
    kernel = depth_taps.shape[0]
    margin = (kernel - 1) // 2
    local_width = value_weight.shape[1]
    seq_count = lax.axis_size("seq")
    tp_count = lax.axis_size("tp")
    piece_width = model_width // (seq_count * tp_count)
    group_place = lax.axis_index("tp")
    positions = lax.axis_index("seq") * frames + jnp.arange(frames, dtype=jnp.int32)
    valid_mask = (positions[None, :] < lengths[:, None]).astype(jnp.float32)[:, :, None]
    frame_count = jnp.sum(lengths).astype(jnp.float32)
    rows_in = normed.reshape(record_count * frames, model_width)
    value_lin = jnp.dot(rows_in, value_weight, preferred_element_type=jnp.float32).reshape(
        record_count, frames, local_width
    )
    gate_lin = jnp.dot(rows_in, gate_weight, preferred_element_type=jnp.float32).reshape(
        record_count, frames, local_width
    )
    gate_sig = jax.nn.sigmoid(gate_lin)
    gated_units = valid_mask * value_lin * gate_sig
    gated_pad = frame_edges(gated_units, margin)
    conv_out = jnp.zeros((record_count, frames, local_width), jnp.float32)
    for tap_index in range(kernel):
        conv_out = conv_out + depth_taps[tap_index] * lax.slice_in_dim(
            gated_pad, tap_index, tap_index + frames, axis=1
        )
    channel_sum, channel_sq = channel_sums(
        (
            jnp.sum(valid_mask * conv_out, axis=(0, 1)),
            jnp.sum(valid_mask * conv_out * conv_out, axis=(0, 1)),
        )
    )
    centre = channel_sum / frame_count
    spread = channel_sq / frame_count - centre * centre
    inv_std = lax.rsqrt(spread + epsilon)
    unit_conv = (conv_out - centre) * inv_std
    normalized = unit_conv * norm_gain + norm_shift
    norm_sig = jax.nn.sigmoid(normalized)
    swished = (valid_mask * normalized * norm_sig).astype(jnp.bfloat16)
    grads_flat = grad_out.reshape(record_count * frames, model_width)
    swish_grad = jnp.dot(grads_flat, out_weight, preferred_element_type=jnp.float32).reshape(
        record_count, frames, local_width
    )
    grad_w_out = lax.dot_general(
        grads_flat,
        swished.reshape(record_count * frames, local_width),
        (((0,), (0,)), ((), ())),
        preferred_element_type=jnp.float32,
    )
    grad_norm = swish_grad * valid_mask * norm_sig * (1.0 + normalized * (1.0 - norm_sig))
    shift_part = jnp.sum(grad_norm, axis=(0, 1))
    gain_part = jnp.sum(grad_norm * unit_conv, axis=(0, 1))
    grad_shift, grad_gain = channel_sums((shift_part, gain_part))
    grad_conv = (
        valid_mask
        * norm_gain
        * inv_std
        * (grad_norm - grad_shift / frame_count - unit_conv * grad_gain / frame_count)
    )
    tap_list = []
    for tap_index in range(kernel):
        window = lax.slice_in_dim(gated_pad, tap_index, tap_index + frames, axis=1)
        tap_list.append(jnp.sum(grad_conv * window, axis=(0, 1)))
    grad_taps = channel_sums(jnp.stack(tap_list))
    conv_pad = frame_edges(grad_conv, margin)
    grad_gated = jnp.zeros((record_count, frames, local_width), jnp.float32)
    for tap_index in range(kernel):
        first_row = 2 * margin - tap_index
        grad_gated = grad_gated + depth_taps[tap_index] * lax.slice_in_dim(
            conv_pad, first_row, first_row + frames, axis=1
        )
    grad_gated = valid_mask * grad_gated
    grad_value = (
        (grad_gated * gate_sig).astype(jnp.bfloat16).reshape(record_count * frames, local_width)
    )
    grad_gate = (
        (grad_gated * value_lin * gate_sig * (1.0 - gate_sig))
        .astype(jnp.bfloat16)
        .reshape(record_count * frames, local_width)
    )
    grad_w_value = lax.dot_general(
        rows_in, grad_value, (((0,), (0,)), ((), ())), preferred_element_type=jnp.float32
    )
    grad_w_gate = lax.dot_general(
        rows_in, grad_gate, (((0,), (0,)), ((), ())), preferred_element_type=jnp.float32
    )
    partial_value = lax.dot_general(
        grad_value, value_weight, (((1,), (1,)), ((), ())), preferred_element_type=jnp.float32
    )
    partial_value = partial_value + lax.dot_general(
        grad_gate, gate_weight, (((1,), (1,)), ((), ())), preferred_element_type=jnp.float32
    )
    split_partial = partial_value.reshape(record_count, frames, seq_count, tp_count, piece_width)
    channel_partial = jnp.transpose(split_partial, (0, 2, 3, 4, 1))
    summed = lax.psum_scatter(
        channel_partial.astype(jnp.bfloat16), "tp", scatter_dimension=2, tiled=True
    ).astype(jnp.float32)
    grad_normed = summed.reshape(record_count, seq_count, piece_width, frames)
    split_grads = grad_out.reshape(record_count, frames, seq_count, tp_count, piece_width)
    own_grads = lax.dynamic_slice_in_dim(split_grads, group_place, 1, 3).reshape(
        record_count, frames, seq_count, piece_width
    )
    own_major = jnp.transpose(own_grads, (0, 2, 3, 1))
    grad_slice = (own_major.astype(jnp.float32) + grad_normed).astype(jnp.bfloat16)
    moved = lax.all_to_all(grad_slice, "seq", split_axis=1, concat_axis=3, tiled=True)
    grad_in = moved.reshape(record_count, piece_width, seq_count * frames)
    grad_w_value, grad_w_gate, grad_w_out = (
        lax.psum_scatter(grad_w_value, "seq", scatter_dimension=0, tiled=True),
        lax.psum_scatter(grad_w_gate, "seq", scatter_dimension=0, tiled=True),
        lax.psum_scatter(grad_w_out, "seq", scatter_dimension=0, tiled=True),
    )
    return (grad_in, grad_w_value, grad_w_gate, grad_w_out, grad_taps, grad_gain, grad_shift)


def solution(mesh):
    placed = (
        P(None, "seq", None),
        P(None, "seq", None),
        P(None, "tp"),
        P(None, "tp"),
        P(None, "tp"),
        P("tp"),
        P("tp"),
        P(None, "tp"),
        P(),
    )
    return jax.shard_map(
        per_device,
        mesh=mesh,
        in_specs=placed,
        out_specs=(
            P(None, ("seq", "tp"), None),
            P("seq", "tp"),
            P("seq", "tp"),
            P("seq", "tp"),
            P(None, "tp"),
            P("tp"),
            P("tp"),
        ),
        check_vma=False,
    )
```

profile of v0, /device:TPU:0, one launch (start us, length us, event | category | flops | bytes accessed | tf_op | source)
XLA Modules:
  0.0 506.1 jit_solution(10694722272380437029)
XLA Ops:
  7.2 0.0 reduce-scatter.5.cloned.1.call-start
  7.3 6.1 %fusion.41 = f32[4,1024,256]{2,1,0:T(8,128)S(1)} fusion(bf16[4,1024,1024]{2,1,0:T(8,128)(2,1)} %param.9, bf16[1024,256]{1,0:T(8,128)(2,1)} %param.11), kind=kOutput, calls=%fused_computation.88 | convolution fusion | flops 2147483648 | bytes 13107200 | tf_op jit(solution)/shard_map/dot_general | solution.py:53
  13.4 0.1 compare_convert_fusion
  13.5 4.4 multiply_multiply_fusion.1
  17.9 2.0 copy-done.5
  19.9 1.3 collective-permute-start.1
  21.2 5.5 %collective-permute-start = (f32[4,4,256]{2,1,0:T(4,128)S(1)}, f32[4,4,256]{2,1,0:T(4,128)S(1)}, u32[]{:S(2)}, u32[]{:S(2)}) collective-permute-start(f32[4,4,256]{2,1,0:T(4,128)S(1)} %get-tuple-element.64), channel_id=1, source_target_pairs={{0,4},{4,8},{8,12},{12,16},{16,20},{20,24},{24,28},{1,5},{5,9},{9,... | collective-permute-start | bytes 49160 | tf_op jit(solution)/shard_map/ppermute | solution.py:14
  26.7 0.6 reduce_sum.127
  28.0 0.1 collective-permute-done
  28.1 22.4 %fusion = (f32[256]{0:T(256)S(1)}, f32[256]{0:T(256)S(1)}, f32[4,1024,256]{2,1,0:T(8,128)}) fusion(f32[4,1024]{1,0:T(4,128)S(1)} %compare_convert_fusion, f32[4,4,256]{2,1,0:T(4,128)S(1)} %collective-permute-done.1, f32[4,1024,256]{2,1,0:T(8,128)} %copy-done.5, f32[256]{0:T(256)S(1)} %bitcast.98, f32[256]{0:T(256)S(1)} %bitcast.100, f32[256]{0:T(256)S(1)} %bitcast.86, ...), kind=kLoop, calls=%fused_computation.16 | loop fusion | flops 30408192 | bytes 8449024 | tf_op jit(solution)/shard_map/reduce_sum | solution.py:70
  50.5 22.9 %all-reduce.1 = (f32[256]{0:T(256)S(1)}, f32[256]{0:T(256)S(1)}) all-reduce(f32[256]{0:T(256)S(1)} %get-tuple-element.49, f32[256]{0:T(256)S(1)} %get-tuple-element.48), channel_id=1, replica_groups=mesh['seq'=8,'tp'=4] {'seq'}, use_global_device_ids=true, to_apply=%region_4.0 | all-reduce | flops 512 | bytes 4096 | tf_op jit(solution)/shard_map/psum | solution.py:27
  73.5 8.3 %fusion.44 = (f32[256]{0:T(256)S(1)}, f32[256]{0:T(256)S(1)}, f32[4,1024,256]{2,1,0:T(8,128)}) fusion(f32[256]{0:T(256)S(1)} %get-tuple-element.59, f32[4,1024,256]{2,1,0:T(8,128)} %get-tuple-element.61, f32[256]{0:T(256)S(1)} %get-tuple-element.60, f32[256]{0:T(256)S(1)} %copy-done.16, f32[256]{0:T(256)S(1)} %copy-done.11, ...), kind=kOutput, calls=%fused_computation.97 | convolution fusion | flops 2164260352 | bytes 17324032 | tf_op jit(solution)/shard_map/dot_general | solution.py:81
  81.8 17.1 %all-reduce = (f32[256]{0:T(256)S(1)}, f32[256]{0:T(256)S(1)}) all-reduce(f32[256]{0:T(256)S(1)} %get-tuple-element.51, f32[256]{0:T(256)S(1)} %get-tuple-element.50), channel_id=1, replica_groups=mesh['seq'=8,'tp'=4] {'seq'}, use_global_device_ids=true, to_apply=%region_8.0 | all-reduce | flops 512 | bytes 4096 | tf_op jit(solution)/shard_map/psum | solution.py:27
  98.9 24.1 %multiply_reduce_fusion.1 = (f32[256]{0:T(256)S(1)}, f32[256]{0:T(256)S(1)}, f32[256]{0:T(256)S(1)}, f32[256]{0:T(256)S(1)}, f32[256]{0:T(256)S(1)}, /*index=5*/...) fusion(f32[4,4,256]{2,1,0:T(4,128)S(1)} %collective-permute-done.1, ...), kind=kLoop, calls=%fused_computation.55 | loop fusion | flops 36697856 | bytes 16840708 | tf_op jit(solution)/shard_map/reduce_sum | solution.py:103
  123.1 3.9 collective-permute-start.3
  127.0 1.5 collective-permute-start.2
  128.5 4.1 collective-permute-done.2
  132.6 8.0 %multiply_convert_fusion.1 = (bf16[4,1024,256]{2,1,0:T(8,128)(2,1)S(1)}, f32[4,1024,256]{2,1,0:T(8,128)S(1)}) fusion(f32[4,1024,256]{2,1,0:T(8,128)S(1)} %copy-done.6, f32[4,1024,256]{2,1,0:T(8,128)S(1)} %copy-done.8, f32[4,1024,256]{2,1,0:T(8,128)S(1)} %get-tuple-element.56, f32[4,4,256]{2,1,0:T(4,128)S(1)} %collective-permute-done.3, f32[256]{0:T(256)S(1)} %bitcast.99, ...), kind=kLoop, calls=%fused_computation.65 | loop fusion | flops 32505856 | bytes 18932736 | tf_op jit(solution)/shard_map/convert_element_type | solution.py:118
  140.6 1.0 multiply_convert_fusion.2
  141.6 0.4 copy-done.9
  142.0 8.1 %fusion.49 = f32[4096,1024]{1,0:T(8,128)} fusion(bf16[4096,256]{1,0:T(8,128)(2,1)S(1)} %bitcast.81, bf16[1024,256]{1,0:T(8,128)(2,1)S(1)} %copy-done.9), kind=kOutput, calls=%fused_computation.101 | convolution fusion | flops 2147483648 | bytes 19398656 | tf_op jit(solution)/shard_map/dot_general | solution.py:127
  150.1 11.5 %add_convert_fusion = bf16[4096,1024]{1,0:T(8,128)(2,1)} fusion(f32[4096,1024]{1,0:T(8,128)} %fusion.49, bf16[4096,256]{1,0:T(8,128)(2,1)S(1)} %bitcast.82, bf16[1024,256]{1,0:T(8,128)(2,1)S(1)} %copy-done), kind=kOutput, calls=%fused_computation | convolution fusion | flops 2155872256 | bytes 27787264 | tf_op jit(solution)/shard_map/dot_general | solution.py:130
  161.6 11.3 %copy.44 = bf16[4096,1024]{0,1:T(8,128)(2,1)} copy(bf16[4096,1024]{1,0:T(8,128)(2,1)} %add_convert_fusion) | data formatting | bytes 16777216 | tf_op jit(solution)/shard_map/convert_element_type | solution.py:136
  172.9 14.6 %convert_element_type.49 = bf16[4,1024,8,4,32]{1,0,4,3,2:T(4,128)(2,1)} reshape(bf16[4096,1024]{0,1:T(8,128)(2,1)} %copy.44) | data formatting | bytes 16777216 | tf_op jit(solution)/shard_map/convert_element_type | solution.py:136
  187.5 9.7 %copy.58 = bf16[4,1024,8,4,32]{1,4,2,0,3:T(8,128)(2,1)} copy(bf16[4,1024,8,4,32]{1,0,4,3,2:T(4,128)(2,1)} %convert_element_type.49) | data formatting | bytes 16777216 | tf_op jit(solution)/shard_map/convert_element_type | solution.py:136
  197.1 0.0 reduce-scatter.5.cloned.1.call-update
  197.2 0.3 reduce-scatter.11.cloned.1.call-start
  197.4 9.0 %fusion.38 = f32[1024,256]{0,1:T(8,128)} fusion(bf16[4,1024,1024]{2,1,0:T(8,128)(2,1)} %param.10, f32[4,1024,256]{2,1,0:T(8,128)} %get-tuple-element.61, f32[256]{0:T(256)S(1)} %copy-done.16, f32[256]{0:T(256)S(1)} %get-tuple-element.60, f32[256]{0:T(256)S(1)} %get-tuple-element.59, f32[256]{0:T(256)S(1)} %copy-done.11, f32[4,1024]{1,0:T(4,128)S(1)} %compare_convert_fusion), kind=kOutput, calls=%fused_computation.83 | convolution fusion | flops 2157969408 | bytes 13651968 | tf_op jit(solution)/shard_map/dot_general | solution.py:84
  206.5 0.0 reduce-scatter.11.cloned.1.call-update
  206.5 0.0 reduce-scatter.7.cloned.1.call-start
  206.5 8.0 %convolution_bitcast_fusion.1 = f32[1024,256]{0,1:T(8,128)} fusion(bf16[4,1024,256]{2,1,0:T(8,128)(2,1)S(1)} %multiply_convert_fusion.2, bf16[4,1024,1024]{2,1,0:T(8,128)(2,1)} %param.9), kind=kOutput, calls=%fused_computation.85 | convolution fusion | flops 2147483648 | bytes 11534336 | tf_op jit(solution)/shard_map/dot_general | solution.py:121
  214.5 11.6 %copy.43 = bf16[4,1024,1024]{1,2,0:T(8,128)(2,1)} copy(bf16[4,1024,1024]{2,1,0:T(8,128)(2,1)} %param.10) | data formatting | bytes 16777216 | tf_op args[1]
  226.1 40.5 %reduce-scatter.5.cloned.1.call-done = bf16[4,8,1,32,1024]{4,3,1,0,2:T(8,128)(2,1)} async-done(((bf16[4,8,4,32,1024]{4,3,1,0,2:T(8,128)(2,1)}), bf16[4,8,1,32,1024]{4,3,1,0,2:T(8,128)(2,1)}) %reduce-scatter.5.cloned.1.call-update) | async-done | bytes 2097168 | tf_op jit(solution)/shard_map/reduce_scatter | solution.py:135
  266.6 3.3 fusion.30
  269.9 1.5 copy.46
  271.4 5.5 %all-to-all-start = ((bf16[4,8,32,1024]{3,2,0,1:T(8,128)(2,1)}), bf16[4,8,32,1024]{3,2,0,1:T(8,128)(2,1)}, u32[]{:S(2)}, u32[]{:S(2)}) async-start(bf16[4,8,32,1024]{3,2,0,1:T(8,128)(2,1)} %copy.46), calls=%async_computation.1 | async-start | bytes 4194304 | tf_op jit(solution)/shard_map/all_to_all | solution.py:145
  276.9 0.0 reduce-scatter.9.cloned.1.call-start
  277.0 6.8 %convolution_bitcast_fusion = f32[1024,256]{0,1:T(8,128)} fusion(bf16[4,1024,256]{2,1,0:T(8,128)(2,1)S(1)} %copy-done.4, bf16[4,1024,1024]{2,1,0:T(8,128)(2,1)} %param.9), kind=kOutput, calls=%fused_computation.84 | convolution fusion | flops 2147483648 | bytes 11534336 | tf_op jit(solution)/shard_map/dot_general | solution.py:124
  283.8 0.0 reduce-scatter.9.cloned.1.call-update
  283.8 73.6 %psum.39 = f32[9,256]{1,0:T(8,128)} all-reduce(f32[9,256]{1,0:T(8,128)S(1)} %stack.39), channel_id=1, replica_groups=mesh['seq'=8,'tp'=4] {'seq'}, use_global_device_ids=true, to_apply=%region_22.0 | all-reduce | flops 2304 | bytes 18432 | tf_op jit(solution)/shard_map/psum | solution.py:27
  357.5 2.4 reduce-scatter.11.cloned.1.call-done
  359.8 1.7 copy.53
  361.5 64.6 %reduce-scatter.7.cloned.1.call-done = f32[128,256]{0,1:T(8,128)} async-done(((f32[1024,256]{0,1:T(8,128)}), f32[128,256]{0,1:T(8,128)}) %reduce-scatter.7.cloned.1.call-update) | async-done | bytes 131088 | tf_op jit(solution)/shard_map/reduce_scatter | solution.py:148
  426.1 1.7 copy.51
  427.8 65.0 %reduce-scatter.9.cloned.1.call-done = f32[128,256]{0,1:T(8,128)} async-done(((f32[1024,256]{0,1:T(8,128)}), f32[128,256]{0,1:T(8,128)}) %reduce-scatter.9.cloned.1.call-update) | async-done | bytes 131088 | tf_op jit(solution)/shard_map/reduce_scatter | solution.py:149
  492.8 1.7 copy.52
  494.4 2.8 copy.47
  497.3 2.3 reshape.103
  (43 shorter events, 0.2 us)
Async XLA Ops:
  7.2 6.3 %copy-start = (bf16[1024,256]{1,0:T(8,128)(2,1)S(1)}, bf16[1024,256]{1,0:T(8,128)(2,1)}, u32[]{:S(2)}) copy-start(bf16[1024,256]{1,0:T(8,128)(2,1)} %param.12) | copy-start | bytes 1572868
  7.2 259.4 %reduce-scatter.5.cloned.1.call-start = ((), (), s32[]{:S(2)}) async-start(), calls=%async_computation.5 | async-start | bytes 10485760 | tf_op jit(solution)/shard_map/reduce_scatter | solution.py:135
  7.2 6.1 %copy-start.14 = (s32[4]{0:T(128)S(1)}, s32[4]{0:T(128)}, u32[]{:S(2)}) copy-start(s32[4]{0:T(128)} %param.17) | copy-start | bytes 52
  7.3 6.2 %copy-start.2 = (bf16[4,1024,1024]{2,1,0:T(8,128)(2,1)S(1)}, bf16[4,1024,1024]{2,1,0:T(8,128)(2,1)}, u32[]{:S(2)}) copy-start(bf16[4,1024,1024]{2,1,0:T(8,128)(2,1)} %param.9) | copy-start | bytes 25165828
  13.4 4.5 copy-start.7
  13.5 13.2 %copy-start.10 = (f32[9,256]{1,0:T(8,128)S(1)}, f32[9,256]{1,0:T(8,128)}, u32[]{:S(2)}) copy-start(f32[9,256]{1,0:T(8,128)} %param.13) | copy-start | bytes 27652
  17.9 2.0 copy-start.5
  19.9 8.1 %collective-permute-start.1 = (f32[4,4,256]{2,1,0:T(4,128)S(1)}, f32[4,4,256]{2,1,0:T(4,128)S(1)}, u32[]{:S(2)}, u32[]{:S(2)}) collective-permute-start(f32[4,4,256]{2,1,0:T(4,128)S(1)} %get-tuple-element.65), channel_id=1, source_target_pairs={{4,0},{8,4},{12,8},{16,12},{20,16},{24,20},{28,24},{5,1},{9,5},{13... | collective-permute-start | bytes 49160 | tf_op jit(solution)/shard_map/ppermute | solution.py:17
  21.2 6.9 %collective-permute-start = (f32[4,4,256]{2,1,0:T(4,128)S(1)}, f32[4,4,256]{2,1,0:T(4,128)S(1)}, u32[]{:S(2)}, u32[]{:S(2)}) collective-permute-start(f32[4,4,256]{2,1,0:T(4,128)S(1)} %get-tuple-element.64), channel_id=1, source_target_pairs={{0,4},{4,8},{8,12},{12,16},{16,20},{20,24},{24,28},{1,5},{5,9},{9,... | collective-permute-start | bytes 49160 | tf_op jit(solution)/shard_map/ppermute | solution.py:14
  28.1 45.3 %copy-start.11 = (f32[256]{0:T(256)S(1)}, f32[256]{0:T(256)}, u32[]{:S(2)}) copy-start(f32[256]{0:T(256)} %param.14) | copy-start | bytes 3076
  28.1 45.3 %copy-start.15 = (bf16[1024,256]{1,0:T(8,128)(2,1)S(1)}, bf16[1024,256]{1,0:T(8,128)(2,1)}, u32[]{:S(2)}) copy-start(bf16[1024,256]{1,0:T(8,128)(2,1)} %param.16) | copy-start | bytes 1572868
  28.1 45.3 %copy-start.16 = (f32[256]{0:T(256)S(1)}, f32[256]{0:T(256)}, u32[]{:S(2)}) copy-start(f32[256]{0:T(256)} %param.15) | copy-start | bytes 3076
  98.9 24.1 %copy-start.12 = (f32[256]{0:T(256)}, f32[256]{0:T(256)S(1)}, u32[]{:S(2)}) copy-start(f32[256]{0:T(256)S(1)} %get-tuple-element.52) | copy-start | bytes 3076
  98.9 24.1 %copy-start.13 = (f32[256]{0:T(256)}, f32[256]{0:T(256)S(1)}, u32[]{:S(2)}) copy-start(f32[256]{0:T(256)S(1)} %get-tuple-element.53) | copy-start | bytes 3076
  98.9 33.7 %copy-start.6 = (f32[4,1024,256]{2,1,0:T(8,128)S(1)}, f32[4,1024,256]{2,1,0:T(8,128)}, u32[]{:S(2)}) copy-start(f32[4,1024,256]{2,1,0:T(8,128)} %get-tuple-element.76) | copy-start | bytes 12582916
  98.9 33.7 %copy-start.8 = (f32[4,1024,256]{2,1,0:T(8,128)S(1)}, f32[4,1024,256]{2,1,0:T(8,128)}, u32[]{:S(2)}) copy-start(f32[4,1024,256]{2,1,0:T(8,128)} %copy-done.7) | copy-start | bytes 12582916
  123.1 5.4 %collective-permute-start.3 = (f32[4,4,256]{2,1,0:T(4,128)S(1)}, f32[4,4,256]{2,1,0:T(4,128)S(1)}, u32[]{:S(2)}, u32[]{:S(2)}) collective-permute-start(f32[4,4,256]{2,1,0:T(4,128)S(1)} %get-tuple-element.63), channel_id=1, source_target_pairs={{0,4},{4,8},{8,12},{12,16},{16,20},{20,24},{24,28},{1,5},{5,9},{9,... | collective-permute-start | bytes 49160 | tf_op jit(solution)/shard_map/ppermute | solution.py:14
  127.0 5.6 %collective-permute-start.2 = (f32[4,4,256]{2,1,0:T(4,128)S(1)}, f32[4,4,256]{2,1,0:T(4,128)S(1)}, u32[]{:S(2)}, u32[]{:S(2)}) collective-permute-start(f32[4,4,256]{2,1,0:T(4,128)S(1)} %get-tuple-element.62), channel_id=1, source_target_pairs={{4,0},{8,4},{12,8},{16,12},{20,16},{24,20},{28,24},{5,1},{9,5},{13... | collective-permute-start | bytes 49160 | tf_op jit(solution)/shard_map/ppermute | solution.py:17
  140.6 9.5 %copy-start.3 = (bf16[4,1024,256]{2,1,0:T(8,128)(2,1)}, bf16[4,1024,256]{2,1,0:T(8,128)(2,1)S(1)}, u32[]{:S(2)}) copy-start(bf16[4,1024,256]{2,1,0:T(8,128)(2,1)S(1)} %get-tuple-element.57) | copy-start | bytes 6291460
  140.6 1.4 copy-start.9
  197.2 162.7 %reduce-scatter.11.cloned.1.call-start = ((), (), s32[]{:S(2)}) async-start(), calls=%async_computation.8 | async-start | bytes 1179648 | tf_op jit(solution)/shard_map/reduce_scatter | solution.py:150
  206.5 219.7 %reduce-scatter.7.cloned.1.call-start = ((), (), s32[]{:S(2)}) async-start(), calls=%async_computation.6 | async-start | bytes 1179648 | tf_op jit(solution)/shard_map/reduce_scatter | solution.py:148
  269.9 7.1 %copy-start.4 = (bf16[4,1024,256]{2,1,0:T(8,128)(2,1)S(1)}, bf16[4,1024,256]{2,1,0:T(8,128)(2,1)}, u32[]{:S(2)}) copy-start(bf16[4,1024,256]{2,1,0:T(8,128)(2,1)} %copy-done.3) | copy-start | bytes 6291460
  271.4 223.0 %all-to-all-start = ((bf16[4,8,32,1024]{3,2,0,1:T(8,128)(2,1)}), bf16[4,8,32,1024]{3,2,0,1:T(8,128)(2,1)}, u32[]{:S(2)}, u32[]{:S(2)}) async-start(bf16[4,8,32,1024]{3,2,0,1:T(8,128)(2,1)} %copy.46), calls=%async_computation.1 | async-start | bytes 4194304 | tf_op jit(solution)/shard_map/all_to_all | solution.py:145
  276.9 215.8 %reduce-scatter.9.cloned.1.call-start = ((), (), s32[]{:S(2)}) async-start(), calls=%async_computation.7 | async-start | bytes 1179648 | tf_op jit(solution)/shard_map/reduce_scatter | solution.py:149
  494.4 5.2 %copy-start.1 = (bf16[1024,256]{1,0:T(8,128)(2,1)S(1)}, bf16[1024,256]{1,0:T(8,128)(2,1)}, u32[]{:S(2)}) copy-start(bf16[1024,256]{1,0:T(8,128)(2,1)} %param.12) | copy-start | bytes 1572868
Sparse Core Ops, SparseCore 0:
  197.3 69.2 reduce-scatter.4
  270.4 89.3 reduce-scatter.10
  363.2 62.8 reduce-scatter.6
  429.8 62.9 reduce-scatter.8
where the time goes:
time: 508 us; the launch traced here: 506 us
  waiting for transfers between devices  177 us (35%)
  blocking collectives  114 us (22%)
  matrix products  62.2 us (12%)
  local copies, waits for them, and re-layouts  61.3 us (12%)
  other arithmetic  59.4 us (12%)
  starting transfers between devices  18.1 us (4%)
  between operations  14.7 us (3%)
    psum x3, blocking collectives, channel_sums(): return lax.psum(parts, 'seq')  114 us
    reduce_scatter x1, waiting for transfers between devices, per_device(): lax.psum_scatter(grad_w_gate, 'seq', scatter_dimension=0, tiled=True)  65 us
    reduce_scatter x1, waiting for transfers between devices, per_device(): lax.psum_scatter(grad_w_value, 'seq', scatter_dimension=0, tiled=True)  64.6 us
    reduce_scatter x1, waiting for transfers between devices, per_device(): lax.psum_scatter(channel_partial.astype(jnp.bfloat16), 'tp', scatter_dime...  40.5 us
    convert_element_type x3, local copies, waits for them, and re-layouts, per_device(): channel_partial.astype(jnp.bfloat16)  35.5 us
    reduce_sum x1, other arithmetic, per_device(): tap_list.append(jnp.sum(grad_conv * window, axis=(0, 1)))  24.1 us
    reduce_sum x1, other arithmetic, per_device(): jnp.sum(valid_mask * conv_out * conv_out, axis=(0, 1))  22.4 us
    unnamed x38, local copies, waits for them, and re-layouts  19 us
  transfers between devices with their start and end apart: 9, of which 6 were waited for; matrix products, arithmetic and copies ran while one was open for 9% of the time, Pallas kernels for 0%

commit v1 on v0

v1 whole, which is shorter than its diff:
```python
import functools

import jax
import jax.numpy as jnp
from jax import lax
from jax.experimental import pallas as pl
from jax.experimental.pallas import tpu as pltpu
from jax.sharding import PartitionSpec as P

EPSILON = 1e-05
EDGE = 8
LANES = 128
F32 = jnp.float32
BF16 = jnp.bfloat16


def sigmoid(x):
    return 0.5 * jnp.tanh(0.5 * x) + 0.5


def dot(a, b):
    return jnp.dot(a, b, preferred_element_type=F32)


def dot_nt(a, b):
    return lax.dot_general(a, b, (((1,), (1,)), ((), ())), preferred_element_type=F32)


def dot_tn(a, b):
    return lax.dot_general(a, b, (((0,), (0,)), ((), ())), preferred_element_type=F32)


def rows_of(count, first):
    return first + lax.broadcasted_iota(jnp.int32, (count, 1), 0)


def fold_rows(x):
    return jnp.sum(x.reshape(x.shape[0] // 8, 8, x.shape[1]), axis=0)


def block_rows(total, most):
    return max(b for b in range(8, most + 1, 8) if total % b == 0)


def whole(shape):
    return pl.BlockSpec(shape, lambda *i: (0,) * len(shape))


def per_record(shape):
    return pl.BlockSpec((1,) + shape, lambda r: (r,) + (0,) * len(shape))


def smem():
    return pl.BlockSpec(memory_space=pltpu.SMEM)


def call(kernel, name, grid, in_specs, out_specs, out_shape, scratch, flops, moved, aliases=None):
    return pl.pallas_call(
        kernel,
        name=name,
        grid=grid,
        in_specs=in_specs,
        out_specs=out_specs,
        out_shape=out_shape,
        scratch_shapes=scratch,
        input_output_aliases=aliases or {},
        cost_estimate=pl.CostEstimate(flops=int(flops), bytes_accessed=int(moved), transcendentals=0),
        compiler_params=pltpu.CompilerParams(vmem_limit_bytes=40 * 1024 * 1024),
    )


def pick_kernel(sel, grads, out):
    out[0] = dot_nt(sel[...], grads[0]).astype(BF16)


def gate_kernel(meta, x, halo, wv, wg, taps, vl_o, sg_o, conv_o, st_o, gp):
    r = pl.program_id(0)
    hi = meta[0, r]
    lo = meta[1, r]
    frames = x.shape[1]
    width = wv.shape[1]
    halves = width // LANES

    def put(row, value):
        for h in range(halves):
            gp[h, pl.ds(row, value.shape[0]), :] = value[:, h * LANES : (h + 1) * LANES]

    edge_v = dot(halo[0], wv[...])
    edge_g = dot(halo[0], wg[...])
    row = rows_of(2 * EDGE, 0)
    pos = jnp.where(row < EDGE, row - EDGE, row - EDGE + frames)
    edge = jnp.where((pos >= lo) & (pos < hi), edge_v * sigmoid(edge_g), 0.0)
    zero = jnp.zeros((EDGE, width), F32)
    put(0, zero)
    put(EDGE, edge[:EDGE])
    put(2 * EDGE + frames, edge[EDGE:])
    put(3 * EDGE + frames, zero)
    step = block_rows(frames, 256)

    def project(i, carry):
        base = pl.multiple_of(i * step, step)
        xb = x[0, pl.ds(base, step), :]
        v = dot(xb, wv[...])
        s = sigmoid(dot(xb, wg[...]))
        vl_o[0, pl.ds(base, step), :] = v
        sg_o[0, pl.ds(base, step), :] = s
        put(2 * EDGE + base, jnp.where(rows_of(step, base) < hi, v * s, 0.0))
        return carry

    lax.fori_loop(0, frames // step, project, 0)
    span = frames + 2 * EDGE
    cb = block_rows(span, 104)
    kernel = taps.shape[0]
    margin = (kernel - 1) // 2
    for h in range(halves):
        cols = slice(h * LANES, (h + 1) * LANES)

        def convolve(i, carry):
            s1, s2 = carry
            base = pl.multiple_of(i * cb, 8)
            acc = jnp.zeros((cb, LANES), F32)
            for k in range(kernel):
                acc = acc + taps[k : k + 1, cols] * gp[h, pl.ds(base + EDGE - margin + k, cb), :]
            conv_o[0, pl.ds(base, cb), cols] = acc
            pos = rows_of(cb, base - EDGE)
            kept = jnp.where((pos >= 0) & (pos < jnp.minimum(hi, frames)), acc, 0.0)
            return s1 + fold_rows(kept), s2 + fold_rows(kept * kept)

        none = jnp.zeros((8, LANES), F32)
        s1, s2 = lax.fori_loop(0, span // cb, convolve, (none, none))
        st_o[0, 0:1, cols] = jnp.sum(s1, axis=0, keepdims=True)
        st_o[0, 1:2, cols] = jnp.sum(s2, axis=0, keepdims=True)


def swish_kernel(grads, halo, wo, sw_o):
    frames = grads.shape[1]
    edge = dot(halo[0], wo[...])
    sw_o[0, :EDGE, :] = edge[:EDGE]
    sw_o[0, EDGE + frames :, :] = edge[EDGE:]
    step = block_rows(frames, 256)

    def body(i, carry):
        base = pl.multiple_of(i * step, step)
        sw_o[0, pl.ds(base + EDGE, step), :] = dot(grads[0, pl.ds(base, step), :], wo[...])
        return carry

    lax.fori_loop(0, frames // step, body, 0)


def norm_kernel(meta, conv, sw, vec, swished_o, gn_o, st_o):
    r = pl.program_id(0)
    hi = meta[0, r]
    lo = meta[1, r]
    frames = swished_o.shape[1]
    centre, inv, gain, shift = (vec[i : i + 1, :] for i in range(4))

    def part(row, count):
        unit = (conv[0, pl.ds(row, count), :] - centre) * inv
        normalized = unit * gain + shift
        s = sigmoid(normalized)
        pos = rows_of(count, row - EDGE)
        keep = (pos >= lo) & (pos < hi)
        swished = jnp.where(keep, normalized * s, 0.0)
        gn = jnp.where(keep, sw[0, pl.ds(row, count), :] * (s + normalized * s * (1.0 - s)), 0.0)
        gn_o[0, pl.ds(row, count), :] = gn
        return unit, swished, gn

    part(0, EDGE)
    part(frames + EDGE, EDGE)
    step = block_rows(frames, 64)

    def body(i, carry):
        s1, s2 = carry
        base = pl.multiple_of(i * step, step)
        unit, swished, gn = part(base + EDGE, step)
        swished_o[0, pl.ds(base, step), :] = swished.astype(BF16)
        return s1 + fold_rows(gn), s2 + fold_rows(gn * unit)

    none = jnp.zeros((8, conv.shape[2]), F32)
    s1, s2 = lax.fori_loop(0, frames // step, body, (none, none))
    st_o[0, 0:1, :] = jnp.sum(s1, axis=0, keepdims=True)
    st_o[0, 1:2, :] = jnp.sum(s2, axis=0, keepdims=True)


def outer_kernel(left, right, out, acc):
    r = pl.program_id(0)
    add = dot_tn(left[0], right[0])

    @pl.when(r == 0)
    def _():
        acc[...] = add

    @pl.when(r > 0)
    def _():
        acc[...] += add

    @pl.when(r == pl.num_programs(0) - 1)
    def _():
        width = out.shape[2]
        for s in range(out.shape[0]):
            out[s] = acc[:, s * width : (s + 1) * width].astype(BF16)


def back_kernel(record, meta, gn, conv, vl, sg, vec, taps, out, taps_o, gc):
    hi = meta[0, record]
    lo = meta[1, record]
    frames, width = vl.shape[1:]
    halves = width // LANES
    span = frames + 2 * EDGE
    kernel = taps.shape[0]
    margin = (kernel - 1) // 2
    cb = block_rows(span, 104)
    step = block_rows(frames, 64)
    for h in range(halves):
        cols = slice(h * LANES, (h + 1) * LANES)
        centre, scale, offset, slope = (vec[i : i + 1, cols] for i in range(4))

        def conv_grad(i, carry):
            base = pl.multiple_of(i * cb, 8)
            pos = rows_of(cb, base - EDGE)
            mean = offset + (conv[0, pl.ds(base, cb), cols] - centre) * slope
            gc[h, pl.ds(base, cb), :] = scale * gn[0, pl.ds(base, cb), cols] - jnp.where(
                (pos >= lo) & (pos < hi), mean, 0.0
            )
            return carry

        lax.fori_loop(0, span // cb, conv_grad, 0)

        def body(i, sums):
            base = pl.multiple_of(i * step, step)
            v = vl[0, pl.ds(base, step), cols]
            s = sg[0, pl.ds(base, step), cols]
            keep = rows_of(step, base) < hi
            vs = v * s
            gated = jnp.where(keep, vs, 0.0)
            total = jnp.zeros((step, LANES), F32)
            new = []
            for k in range(kernel):
                window = gc[h, pl.ds(base + EDGE + margin - k, step), :]
                total = total + taps[k : k + 1, cols] * window
                new.append(sums[k] + fold_rows(window * gated))
            total = jnp.where(keep, total, 0.0)
            out[pl.ds(base, step), cols] = (total * s).astype(BF16)
            out[pl.ds(base, step), width + h * LANES : width + (h + 1) * LANES] = (
                total * vs * (1.0 - s)
            ).astype(BF16)
            return tuple(new)

        none = jnp.zeros((8, LANES), F32)
        sums = lax.fori_loop(0, frames // step, body, (none,) * kernel)
        for k in range(kernel):
            taps_o[k : k + 1, cols] = jnp.sum(sums[k], axis=0, keepdims=True)


def partial_kernel(own, sibling, w_own, w_sibling, picked, mine, *others):
    for d in range(w_own.shape[0]):
        total = dot_nt(w_own[d], own[...]) + dot_nt(w_sibling[d], sibling[...])
        if d == 0:
            mine[...] = total + picked[0].astype(F32)
        else:
            others[d - 1][...] = total.astype(BF16)


def weights_kernel(x, *refs):
    count = x.shape[0]
    lefts, out, acc = refs[:-2], refs[-2], refs[-1]
    r = pl.program_id(0)
    for i, left in enumerate(lefts):

        @pl.when(r == i)
        def _(i=i, left=left):
            add = dot_tn(left[...], x[0])
            if i == 0:
                acc[...] = add
            else:
                acc[...] += add

    @pl.when(r == pl.num_programs(0) - 1)
    def _():
        width = out.shape[2]
        for s in range(out.shape[0]):
            out[s] = acc[:, s * width : (s + 1) * width].astype(BF16)


def place_kernel(moved, *refs):
    out = refs[-1]
    frames = moved.shape[2]
    for s in range(moved.shape[0]):
        out[0, :, s * frames : (s + 1) * frames] = moved[s]


def everyone(part, axis):
    count = lax.axis_size(axis)
    copies = jnp.broadcast_to(part[None], (count,) + part.shape)
    return jnp.sum(lax.all_to_all(copies, axis, 0, 0, tiled=True), axis=0)


def per_device(
    normed,
    grad_out,
    value_weight,
    gate_weight,
    depth_taps,
    norm_gain,
    norm_shift,
    out_weight,
    lengths,
):
    recs, frames, model = normed.shape
    kernel = depth_taps.shape[0]
    width = value_weight.shape[1]
    seqs = lax.axis_size("seq")
    tps = lax.axis_size("tp")
    chips = tps // 2
    piece = model // (seqs * tps)
    rows = seqs * piece
    shard = model // seqs
    span = frames + 2 * EDGE
    seq_at = lax.axis_index("seq")
    tp_at = lax.axis_index("tp")
    chip_at, core_at = tp_at // 2, tp_at % 2
    count = jnp.sum(lengths).astype(F32)
    first = (seq_at * frames).astype(jnp.int32)
    meta = jnp.stack([lengths - first, jnp.full((recs,), 0, jnp.int32) - first])
    halves = width // LANES
    sds = jax.ShapeDtypeStruct

    low_edge = jnp.concatenate([normed[:, -EDGE:], grad_out[:, -EDGE:]], axis=2)
    high_edge = jnp.concatenate([normed[:, :EDGE], grad_out[:, :EDGE]], axis=2)
    up = [(i, i + 1) for i in range(seqs - 1)]
    down = [(j, i) for i, j in up]
    halo = jnp.concatenate(
        [lax.ppermute(low_edge, "seq", up), lax.ppermute(high_edge, "seq", down)], axis=1
    )
    halo_x, halo_g = halo[:, :, :model], halo[:, :, model:]

    both = jnp.concatenate([value_weight, gate_weight], axis=1).reshape(seqs, tps, piece, 2 * width)

    def chosen(core):
        picks = [
            lax.dynamic_index_in_dim(both, ((chip_at + d) % chips) * 2 + core, 1, keepdims=False)
            for d in range(chips)
        ]
        return jnp.stack(picks).reshape(chips, rows, 2 * width)

    swap = [(i, i ^ 1) for i in range(tps)]
    w_own = chosen(core_at)
    w_sibling = lax.ppermute(chosen(1 - core_at), "tp", swap)

    channel = (
        jnp.arange(seqs, dtype=jnp.int32)[:, None] * (tps * piece)
        + tp_at * piece
        + jnp.arange(piece, dtype=jnp.int32)[None, :]
    ).reshape(rows, 1)
    select = (channel == jnp.arange(model, dtype=jnp.int32)[None, :]).astype(BF16)
    array_bytes = recs * frames * width * 4
    input_bytes = recs * frames * model * 2
    matmul = 2 * recs * frames * model * width

    picked = call(
        pick_kernel,
        "pick",
        (recs,),
        [whole((rows, model)), per_record((frames, model))],
        per_record((rows, frames)),
        sds((recs, rows, frames), BF16),
        [],
        matmul,
        input_bytes,
    )(select, grad_out)

    vl, sg, conv, stats = call(
        gate_kernel,
        "gate_conv",
        (recs,),
        [
            smem(),
            per_record((frames, model)),
            per_record((2 * EDGE, model)),
            whole((model, width)),
            whole((model, width)),
            whole((kernel, width)),
        ],
        [
            per_record((frames, width)),
            per_record((frames, width)),
            per_record((span, width)),
            per_record((2, width)),
        ],
        [
            sds((recs, frames, width), F32),
            sds((recs, frames, width), F32),
            sds((recs, span, width), F32),
            sds((recs, 2, width), F32),
        ],
        [pltpu.VMEM((halves, frames + 4 * EDGE, LANES), F32)],
        2 * matmul,
        input_bytes + 3 * array_bytes,
    )(meta, normed, halo_x, value_weight, gate_weight, depth_taps)
    channel_sum, channel_sq = everyone(jnp.sum(stats, axis=0), "seq")

    sw = call(
        swish_kernel,
        "swish_grad",
        (recs,),
        [per_record((frames, model)), per_record((2 * EDGE, model)), whole((model, width))],
        per_record((span, width)),
        sds((recs, span, width), F32),
        [],
        matmul,
        input_bytes + array_bytes,
    )(grad_out, halo_g, out_weight)

    centre = channel_sum / count
    spread = channel_sq / count - centre * centre
    inv_std = lax.rsqrt(spread + EPSILON)
    swished, gn, sums = call(
        norm_kernel,
        "norm_swish",
        (recs,),
        [smem(), per_record((span, width)), per_record((span, width)), whole((4, width))],
        [per_record((frames, width)), per_record((span, width)), per_record((2, width))],
        [
            sds((recs, frames, width), BF16),
            sds((recs, span, width), F32),
            sds((recs, 2, width), F32),
        ],
        [],
        20 * recs * frames * width,
        3 * array_bytes,
    )(meta, conv, sw, jnp.stack([centre, inv_std, norm_gain, norm_shift]))
    grad_shift, grad_gain = everyone(jnp.sum(sums, axis=0), "seq")

    w_out_parts = call(
        outer_kernel,
        "outer_w_out",
        (recs,),
        [per_record((frames, width)), per_record((frames, model))],
        whole((seqs, width, shard)),
        sds((seqs, width, shard), BF16),
        [pltpu.VMEM((width, model), F32)],
        matmul,
        input_bytes,
    )(swished, grad_out)

    scale = norm_gain * inv_std
    vec = jnp.stack(
        [centre, scale, scale * grad_shift / count, scale * inv_std * grad_gain / count]
    )
    grads, tap_parts = [], []
    for r in range(recs):

        def at(shape, r=r):
            return pl.BlockSpec((1,) + shape, lambda i: (r,) + (0,) * len(shape))

        both_grads, tap_part = call(
            functools.partial(back_kernel, r),
            "back_conv",
            (1,),
            [
                smem(),
                at((span, width)),
                at((span, width)),
                at((frames, width)),
                at((frames, width)),
                whole((4, width)),
                whole((kernel, width)),
            ],
            [whole((frames, 2 * width)), whole((kernel, width))],
            [sds((frames, 2 * width), BF16), sds((kernel, width), F32)],
            [pltpu.VMEM((halves, span, LANES), F32)],
            60 * frames * width,
            4 * array_bytes // recs,
        )(meta, gn, conv, vl, sg, vec, depth_taps)
        grads.append(both_grads)
        tap_parts.append(tap_part)

    grad_in = None
    moved_parts = []
    for r in range(recs):

        def at(shape, r=r):
            return pl.BlockSpec((1,) + shape, lambda i: (r,) + (0,) * len(shape))

        sibling = lax.ppermute(grads[r], "tp", swap)
        parts = call(
            partial_kernel,
            "partial_in",
            (1,),
            [
                whole((frames, 2 * width)),
                whole((frames, 2 * width)),
                whole((chips, rows, 2 * width)),
                whole((chips, rows, 2 * width)),
                at((rows, frames)),
            ],
            [whole((rows, frames))] * chips,
            [sds((rows, frames), F32)] + [sds((rows, frames), BF16)] * (chips - 1),
            [],
            2 * matmul // recs,
            8 * frames * width + 6 * rows * frames,
        )(grads[r], sibling, w_own, w_sibling, picked)
        total = parts[0]
        for d in range(1, chips):
            send = [(i, ((i // 2 + d) % chips) * 2 + i % 2) for i in range(tps)]
            total = total + lax.ppermute(parts[d], "tp", send).astype(F32)
        own = total.astype(BF16).reshape(seqs, piece, frames)
        moved_parts.append(lax.all_to_all(own, "seq", 0, 0, tiled=True))

    w_in_parts = call(
        weights_kernel,
        "outer_w_in",
        (recs,),
        [per_record((frames, model))] + [whole((frames, 2 * width))] * recs,
        whole((seqs, 2 * width, shard)),
        sds((seqs, 2 * width, shard), BF16),
        [pltpu.VMEM((2 * width, model), F32)],
        2 * matmul,
        input_bytes + 4 * recs * frames * width,
    )(normed, *grads)

    for r in range(recs):
        place = call(
            place_kernel,
            "place",
            (1,),
            [whole((seqs, piece, frames))] + ([] if r == 0 else [pl.BlockSpec(memory_space=pl.ANY)]),
            pl.BlockSpec((1, piece, seqs * frames), lambda i, r=r: (r, 0, 0)),
            sds((recs, piece, seqs * frames), BF16),
            [],
            0,
            4 * piece * seqs * frames,
            None if r == 0 else {1: 0},
        )
        grad_in = place(moved_parts[r]) if r == 0 else place(moved_parts[r], grad_in)

    def owned(parts):
        got = lax.all_to_all(parts, "seq", 0, 0, tiled=True)
        return jnp.sum(got.astype(F32), axis=0).T

    grad_w_out = owned(w_out_parts)
    w_in = owned(w_in_parts)
    grad_taps = everyone(sum(tap_parts), "seq")
    return (
        grad_in,
        w_in[:, :width],
        w_in[:, width:],
        grad_w_out,
        grad_taps,
        grad_gain,
        grad_shift,
    )


def solution(mesh):
    placed = (
        P(None, "seq", None),
        P(None, "seq", None),
        P(None, "tp"),
        P(None, "tp"),
        P(None, "tp"),
        P("tp"),
        P("tp"),
        P(None, "tp"),
        P(),
    )
    return jax.shard_map(
        per_device,
        mesh=mesh,
        in_specs=placed,
        out_specs=(
            P(None, ("seq", "tp"), None),
            P("seq", "tp"),
            P("seq", "tp"),
            P("seq", "tp"),
            P(None, "tp"),
            P("tp"),
            P("tp"),
        ),
        check_vma=False,
    )
```

time: 508 us -> 243 us (0.48)
  waiting for transfers between devices: 177 us -> 46.5 us
  blocking collectives: 114 us -> 12.4 us
  Pallas kernels: 0 us -> 77.5 us
  matrix products: 62.2 us -> 0 us
  other arithmetic: 59.4 us -> 8.57 us
  starting transfers between devices: 18.1 us -> 56.5 us
  local copies, waits for them, and re-layouts: 61.3 us -> 37.9 us
  between operations: 14.7 us -> 1.74 us
    reduce_scatter x4 -> x0, waiting for transfers between devices: 173 us -> none  [the longest x1 65 us: per_device(): lax.psum_scatter(grad_w_gate, 'seq', scatter_dimension=0, tiled=True)]
    psum x3 -> x0, blocking collectives: 114 us -> none  [channel_sums(): return lax.psum(parts, 'seq')]
    pallas_call x0 -> x18, Pallas kernels: none -> 77.5 us  [the longest x4 18.7 us: per_device(): call(functools.partial(back_kernel, r), 'back_conv', (1,), [smem(), at((s...]
    dot_general x8 -> x0, matrix products: 62.2 us -> none  [the longest x1 11.5 us: per_device(): lax.dot_general(grad_gate, gate_weight, (((1,), (1,)), ((), ())), preferr...]
    reduce_sum x3 -> x8, other arithmetic: 47.1 us -> 3.44 us  [the longest x2 1.46 us: owned(): return jnp.sum(got.astype(F32), axis=0).T]
    ppermute x4 -> x11, waiting for transfers between devices: 4.25 us -> 45.8 us  [the longest x4 42.2 us: per_device(): total = total + lax.ppermute(parts[d], 'tp', send).astype(F32)]
    all_to_all x1 -> x8, starting transfers between devices: 5.52 us -> 43.6 us  [the longest x4 22.6 us: per_device(): moved_parts.append(lax.all_to_all(own, 'seq', 0, 0, tiled=True))]
    convert_element_type x4 -> x0, local copies, waits for them, and re-layouts: 37 us -> none  [the longest x3 35.5 us: per_device(): channel_partial.astype(jnp.bfloat16)]
  transfers between devices with their start and end apart: 9 -> 19, of which waited for: 6 -> 7; matrix products, arithmetic and copies ran while one was open for 9% -> 5% of each run, Pallas kernels for 0% -> 16%
where the time goes in v1:
time: 243 us; the launch traced here: 241 us
  Pallas kernels  77.5 us (32%)
  starting transfers between devices  56.5 us (23%)
  waiting for transfers between devices  46.5 us (19%)
  local copies, waits for them, and re-layouts  37.9 us (16%)
  blocking collectives  12.4 us (5%)
  other arithmetic  8.57 us (4%)
    ppermute x4, waiting for transfers between devices, per_device(): total = total + lax.ppermute(parts[d], 'tp', send).astype(F32)  42.2 us
    unnamed x52, local copies, waits for them, and re-layouts  34.7 us
    all_to_all x4, starting transfers between devices, per_device(): moved_parts.append(lax.all_to_all(own, 'seq', 0, 0, tiled=True))  22.6 us
    pallas_call x4, Pallas kernels, per_device(): call(functools.partial(back_kernel, r), 'back_conv', (1,), [smem(), at((s...  18.7 us
    pallas_call x1, Pallas kernels, per_device(): call(gate_kernel, 'gate_conv', (recs,), [smem(), per_record((frames, mode...  14.5 us
    all_to_all x1, blocking collectives, everyone(): return jnp.sum(lax.all_to_all(copies, axis, 0, 0, tiled=True), axis=0)  12.4 us
    all_to_all x2, starting transfers between devices, owned(): got = lax.all_to_all(parts, 'seq', 0, 0, tiled=True)  11.9 us
    pallas_call x4, Pallas kernels, per_device(): call(partial_kernel, 'partial_in', (1,), [whole((frames, 2 * width)), who...  11.3 us
  transfers between devices with their start and end apart: 19, of which 7 were waited for; matrix products, arithmetic and copies ran while one was open for 5% of the time, Pallas kernels for 16%

profile of v1, /device:TPU:0, one launch (start us, length us, event | category | flops | bytes accessed | tf_op | source)
XLA Modules:
  0.0 241.2 jit_solution(1762213164157757921)
XLA Ops:
  1.7 4.9 %collective-permute-start = (bf16[4,8,2048]{2,1,0:T(8,128)(2,1)S(1)}, bf16[4,8,2048]{2,1,0:T(8,128)(2,1)S(1)}, u32[]{:S(2)}, u32[]{:S(2)}) collective-permute-start(bf16[4,8,2048]{2,1,0:T(8,128)(2,1)S(1)} %pad_maximum_fusion.3), channel_id=1, source_target_pairs={{0,4},{4,8},{8,12},{12,16},{16,20},{20,24},{24,28},{1,5},{5,9},{9,... | collective-permute-start | bytes 393224 | tf_op jit(solution)/shard_map/ppermute | solution.py:333
  9.9 3.6 %collective-permute-done.1 = bf16[4,8,2048]{2,1,0:T(8,128)(2,1)S(1)} collective-permute-done((bf16[4,8,2048]{2,1,0:T(8,128)(2,1)S(1)}, bf16[4,8,2048]{2,1,0:T(8,128)(2,1)S(1)}, u32[]{:S(2)}, u32[]{:S(2)}) %collective-permute-start.1) | collective-permute-done | bytes 131104 | tf_op jit(solution)/shard_map/ppermute | solution.py:333
  13.6 14.5 %gate_conv.1 = (f32[4,1024,256]{2,1,0:T(8,128)S(1)}, f32[4,1024,256]{2,1,0:T(8,128)S(1)}, f32[4,1040,256]{2,1,0:T(8,128)S(1)}, f32[4,2,256]{2,1,0:T(2,128)S(1)}) custom-call(s32[2,4]{1,0:T(2,128)S(1)} %stack.50.meta, bf16[4,1024,1024]{2,1,0:T(8,128)(2,1)} %x.5, bf16[4,16,1024]{2,1,0:T(8,128)(2,1)S(1)} %get-tuple-element.89.halo, ...), custom_call_target="tpu_custom_call" | custom-call | flops 4294967296 | bytes 20971520 | tf_op jit(solution)/shard_map/gate_conv/pallas_call | solution.py:372
  28.1 2.0 copy-done
  30.1 2.1 copy-done.7
  32.1 1.9 copy-done.9
  34.7 5.7 %all-to-all-start = ((f32[8,2,256]{2,1,0:T(2,128)}), f32[8,2,256]{2,1,0:T(2,128)S(1)}, u32[]{:S(2)}, u32[]{:S(2)}) async-start(f32[8,2,256]{2,1,0:T(2,128)} %broadcast_in_dim.6), calls=%async_computation | async-start | bytes 32768 | tf_op jit(solution)/shard_map/all_to_all | solution.py:295
  40.4 3.4 %copy-done.2 = bf16[4,1024,1024]{2,1,0:T(8,128)(2,1)S(1)} copy-done((bf16[4,1024,1024]{2,1,0:T(8,128)(2,1)S(1)}, bf16[4,1024,1024]{2,1,0:T(8,128)(2,1)}, u32[]{:S(2)}) %copy-start.2) | copy-done | bytes 8388632
  43.8 5.7 %swish_grad.1.sw = f32[4,1040,256]{2,1,0:T(8,128)S(1)} custom-call(bf16[4,1024,1024]{2,1,0:T(8,128)(2,1)S(1)} %copy-done.2, bf16[4,16,1024]{2,1,0:T(8,128)(2,1)S(1)} %get-tuple-element.88.halo, bf16[1024,256]{1,0:T(8,128)(2,1)S(1)} %copy-done.12), custom_call_target="tpu_custom_call" | custom-call | flops 2147483648 | bytes 12582912 | tf_op jit(solution)/shard_map/swish_grad/pallas_call | solution.py:402
  49.5 2.0 copy-done.11
  51.6 2.2 copy-done.1
  53.8 5.3 %norm_swish.1 = (bf16[4,1024,256]{2,1,0:T(8,128)(2,1)S(1)}, f32[4,1040,256]{2,1,0:T(8,128)S(1)}, f32[4,2,256]{2,1,0:T(2,128)S(1)}) custom-call(s32[2,4]{1,0:T(2,128)S(1)} %stack.50.meta, f32[4,1040,256]{2,1,0:T(8,128)S(1)} %copy-done.1, f32[4,1040,256]{2,1,0:T(8,128)} %copy-done.11, f32[4,256]{1,0:T(4,128)S(1)} %fusion.2.vec), custom_call_target="tpu_custom_call" | custom-call | flops 20971520 | bytes 12582912 | tf_op jit(solution)/shard_map/norm_swish/pallas_call | solution.py:417
  59.2 2.0 copy-done.5
  61.2 12.4 %all_to_all.45 = f32[8,2,256]{2,1,0:T(2,128)S(1)} all-to-all(f32[8,2,256]{2,1,0:T(2,128)S(1)} %broadcast_in_dim.7), channel_id=1, replica_groups=mesh['seq'=8,'tp'=4] {'seq'}, dimensions={0} | all-to-all | bytes 32768 | tf_op jit(solution)/shard_map/all_to_all | solution.py:295
  73.7 2.2 copy-done.6
  75.9 2.2 copy-done.8
  78.1 2.2 copy-done.10
  80.3 4.7 %back_conv.7 = (bf16[1024,512]{1,0:T(8,128)(2,1)}, f32[9,256]{1,0:T(8,128)S(1)}) custom-call(s32[2,4]{1,0:T(2,128)S(1)} %stack.50.meta, f32[4,1040,256]{2,1,0:T(8,128)S(1)} %copy-done.6, f32[4,1040,256]{2,1,0:T(8,128)} %copy-done, f32[4,1024,256]{2,1,0:T(8,128)S(1)} %copy-done.8, f32[4,1024,256]{2,1,0:T(8,128)S(1)} %copy-done.10, f32[4,256]{1,0:T(4,128)S(1)} %fusion.4.vec, ...), custom_call_target="tpu_custom_call" | custom-call | flops 15728640 | bytes 4194304 | tf_op jit(solution)/shard_map/back_conv/pallas_call | solution.py:456
  85.0 4.7 %back_conv.6 = (bf16[1024,512]{1,0:T(8,128)(2,1)}, f32[9,256]{1,0:T(8,128)S(1)}) custom-call(s32[2,4]{1,0:T(2,128)S(1)} %stack.50.meta, f32[4,1040,256]{2,1,0:T(8,128)S(1)} %copy-done.6, f32[4,1040,256]{2,1,0:T(8,128)} %copy-done, f32[4,1024,256]{2,1,0:T(8,128)S(1)} %copy-done.8, f32[4,1024,256]{2,1,0:T(8,128)S(1)} %copy-done.10, f32[4,256]{1,0:T(4,128)S(1)} %fusion.4.vec, ...), custom_call_target="tpu_custom_call" | custom-call | flops 15728640 | bytes 4194304 | tf_op jit(solution)/shard_map/back_conv/pallas_call | solution.py:456
  89.6 4.7 %back_conv.5 = (bf16[1024,512]{1,0:T(8,128)(2,1)}, f32[9,256]{1,0:T(8,128)S(1)}) custom-call(s32[2,4]{1,0:T(2,128)S(1)} %stack.50.meta, f32[4,1040,256]{2,1,0:T(8,128)S(1)} %copy-done.6, f32[4,1040,256]{2,1,0:T(8,128)} %copy-done, f32[4,1024,256]{2,1,0:T(8,128)S(1)} %copy-done.8, f32[4,1024,256]{2,1,0:T(8,128)S(1)} %copy-done.10, f32[4,256]{1,0:T(4,128)S(1)} %fusion.4.vec, ...), custom_call_target="tpu_custom_call" | custom-call | flops 15728640 | bytes 4194304 | tf_op jit(solution)/shard_map/back_conv/pallas_call | solution.py:456
  94.3 4.7 %back_conv.4 = (bf16[1024,512]{1,0:T(8,128)(2,1)}, f32[9,256]{1,0:T(8,128)S(1)}) custom-call(s32[2,4]{1,0:T(2,128)S(1)} %stack.50.meta, f32[4,1040,256]{2,1,0:T(8,128)S(1)} %copy-done.6, f32[4,1040,256]{2,1,0:T(8,128)} %copy-done, f32[4,1024,256]{2,1,0:T(8,128)S(1)} %copy-done.8, f32[4,1024,256]{2,1,0:T(8,128)S(1)} %copy-done.10, f32[4,256]{1,0:T(4,128)S(1)} %fusion.4.vec, ...), custom_call_target="tpu_custom_call" | custom-call | flops 15728640 | bytes 4194304 | tf_op jit(solution)/shard_map/back_conv/pallas_call | solution.py:456
  99.7 3.4 %all-to-all-start.8 = ((f32[8,9,256]{2,1,0:T(8,128)}), f32[8,9,256]{2,1,0:T(8,128)S(1)}, u32[]{:S(2)}, u32[]{:S(2)}) async-start(f32[8,9,256]{2,1,0:T(8,128)} %broadcast_in_dim.8), calls=%async_computation.8 | async-start | bytes 262144 | tf_op jit(solution)/shard_map/all_to_all | solution.py:295
  103.1 3.4 %copy-done.3 = bf16[4,1024,1024]{2,1,0:T(8,128)(2,1)S(1)} copy-done((bf16[4,1024,1024]{2,1,0:T(8,128)(2,1)S(1)}, bf16[4,1024,1024]{2,1,0:T(8,128)(2,1)}, u32[]{:S(2)}) %copy-start.3) | copy-done | bytes 8388632
  106.5 4.2 %outer_w_out.1 = bf16[8,256,128]{2,1,0:T(8,128)(2,1)} custom-call(bf16[4,1024,256]{2,1,0:T(8,128)(2,1)S(1)} %get-tuple-element.48.left, bf16[4,1024,1024]{2,1,0:T(8,128)(2,1)S(1)} %copy-done.3), custom_call_target="tpu_custom_call" | custom-call | flops 2147483648 | bytes 8388608 | tf_op jit(solution)/shard_map/outer_w_out/pallas_call | solution.py:434
  110.7 5.9 %all-to-all-start.7 = ((bf16[8,256,128]{2,1,0:T(8,128)(2,1)}), bf16[8,256,128]{2,1,0:T(8,128)(2,1)S(1)}, u32[]{:S(2)}, u32[]{:S(2)}) async-start(bf16[8,256,128]{2,1,0:T(8,128)(2,1)} %outer_w_out.1), calls=%async_computation.7 | async-start | bytes 1048576 | tf_op jit(solution)/shard_map/all_to_all | solution.py:538
  117.5 3.4 %copy-done.16 = bf16[4,1024,1024]{2,1,0:T(8,128)(2,1)S(1)} copy-done((bf16[4,1024,1024]{2,1,0:T(8,128)(2,1)S(1)}, bf16[4,1024,1024]{2,1,0:T(8,128)(2,1)}, u32[]{:S(2)}) %copy-start.16) | copy-done | bytes 8388632
  120.9 8.4 %outer_w_in.1 = bf16[8,512,128]{2,1,0:T(8,128)(2,1)} custom-call(bf16[4,1024,1024]{2,1,0:T(8,128)(2,1)S(1)} %copy-done.16, bf16[1024,512]{1,0:T(8,128)(2,1)} %get-tuple-element.45.own.refs_0_, bf16[1024,512]{1,0:T(8,128)(2,1)} %get-tuple-element.42.own.refs_1_, bf16[1024,512]{1,0:T(8,128)(2,1)} %get-tuple-element.39.own.refs_2_, ...), custom_call_target="tpu_custom_call" | custom-call | flops 4294967296 | bytes 12582912 | tf_op jit(solution)/shard_map/outer_w_in/pallas_call | solution.py:510
  129.2 6.0 %all-to-all-start.6 = ((bf16[8,512,128]{2,1,0:T(8,128)(2,1)}), bf16[8,512,128]{2,1,0:T(8,128)(2,1)}, u32[]{:S(2)}, u32[]{:S(2)}) async-start(bf16[8,512,128]{2,1,0:T(8,128)(2,1)} %outer_w_in.1), calls=%async_computation.6 | async-start | bytes 2097152 | tf_op jit(solution)/shard_map/all_to_all | solution.py:538
  137.1 3.4 %copy-done.4 = bf16[4,1024,1024]{2,1,0:T(8,128)(2,1)S(1)} copy-done((bf16[4,1024,1024]{2,1,0:T(8,128)(2,1)S(1)}, bf16[4,1024,1024]{2,1,0:T(8,128)(2,1)}, u32[]{:S(2)}) %copy-start.4) | copy-done | bytes 8388632
  140.4 3.0 %pick.1.picked = bf16[4,256,1024]{2,1,0:T(8,128)(2,1)S(1)} custom-call(bf16[256,1024]{1,0:T(8,128)(2,1)S(1)} %fusion.sel, bf16[4,1024,1024]{2,1,0:T(8,128)(2,1)S(1)} %copy-done.4), custom_call_target="tpu_custom_call" | custom-call | flops 2147483648 | bytes 8388608 | tf_op jit(solution)/shard_map/pick/pallas_call | solution.py:360
  143.5 2.8 %partial_in.7 = (f32[256,1024]{1,0:T(8,128)S(1)}, bf16[256,1024]{1,0:T(8,128)(2,1)S(1)}) custom-call(bf16[1024,512]{1,0:T(8,128)(2,1)} %get-tuple-element.45.own.refs_0_, bf16[1024,512]{1,0:T(8,128)(2,1)} %collective-permute-done.9.sibling, bf16[2,256,512]{2,1,0:T(8,128)(2,1)S(1)} %pad_maximum_fusion.1.w_own, ...), custom_call_target="tpu_custom_call" | custom-call | flops 1073741824 | bytes 3670016 | tf_op jit(solution)/shard_map/partial_in/pallas_call | solution.py:486
  146.4 1.5 collective-permute-start.10
  147.9 12.6 %collective-permute-done.10 = bf16[256,1024]{1,0:T(8,128)(2,1)S(1)} collective-permute-done((bf16[256,1024]{1,0:T(8,128)(2,1)S(1)}, bf16[256,1024]{1,0:T(8,128)(2,1)S(1)}, u32[]{:S(2)}, u32[]{:S(2)}) %collective-permute-start.10) | collective-permute-done | bytes 524320 | tf_op jit(solution)/shard_map/ppermute | solution.py:506
  161.8 5.4 %all-to-all-start.5 = ((bf16[8,32,1024]{2,1,0:T(8,128)(2,1)}), bf16[8,32,1024]{2,1,0:T(8,128)(2,1)}, u32[]{:S(2)}, u32[]{:S(2)}) async-start(bf16[8,32,1024]{2,1,0:T(8,128)(2,1)} %bitcast.30), calls=%async_computation.5 | async-start | bytes 1048576 | tf_op jit(solution)/shard_map/all_to_all | solution.py:508
  167.2 2.8 %partial_in.6 = (f32[256,1024]{1,0:T(8,128)S(1)}, bf16[256,1024]{1,0:T(8,128)(2,1)S(1)}) custom-call(bf16[1024,512]{1,0:T(8,128)(2,1)} %get-tuple-element.42.own.refs_1_, bf16[1024,512]{1,0:T(8,128)(2,1)} %collective-permute-done.7.sibling, bf16[2,256,512]{2,1,0:T(8,128)(2,1)S(1)} %pad_maximum_fusion.1.w_own, ...), custom_call_target="tpu_custom_call" | custom-call | flops 1073741824 | bytes 3670016 | tf_op jit(solution)/shard_map/partial_in/pallas_call | solution.py:486
  170.1 1.5 collective-permute-start.8
  171.6 11.3 %collective-permute-done.8 = bf16[256,1024]{1,0:T(8,128)(2,1)S(1)} collective-permute-done((bf16[256,1024]{1,0:T(8,128)(2,1)S(1)}, bf16[256,1024]{1,0:T(8,128)(2,1)S(1)}, u32[]{:S(2)}, u32[]{:S(2)}) %collective-permute-start.8) | collective-permute-done | bytes 524320 | tf_op jit(solution)/shard_map/ppermute | solution.py:506
  183.9 5.7 %all-to-all-start.4 = ((bf16[8,32,1024]{2,1,0:T(8,128)(2,1)}), bf16[8,32,1024]{2,1,0:T(8,128)(2,1)}, u32[]{:S(2)}, u32[]{:S(2)}) async-start(bf16[8,32,1024]{2,1,0:T(8,128)(2,1)} %bitcast.32), calls=%async_computation.4 | async-start | bytes 1048576 | tf_op jit(solution)/shard_map/all_to_all | solution.py:508
  189.6 2.8 %partial_in.5 = (f32[256,1024]{1,0:T(8,128)S(1)}, bf16[256,1024]{1,0:T(8,128)(2,1)S(1)}) custom-call(bf16[1024,512]{1,0:T(8,128)(2,1)} %get-tuple-element.39.own.refs_2_, bf16[1024,512]{1,0:T(8,128)(2,1)} %collective-permute-done.5.sibling, bf16[2,256,512]{2,1,0:T(8,128)(2,1)S(1)} %pad_maximum_fusion.1.w_own, ...), custom_call_target="tpu_custom_call" | custom-call | flops 1073741824 | bytes 3670016 | tf_op jit(solution)/shard_map/partial_in/pallas_call | solution.py:486
  192.5 1.5 collective-permute-start.6
  194.0 9.9 %collective-permute-done.6 = bf16[256,1024]{1,0:T(8,128)(2,1)S(1)} collective-permute-done((bf16[256,1024]{1,0:T(8,128)(2,1)S(1)}, bf16[256,1024]{1,0:T(8,128)(2,1)S(1)}, u32[]{:S(2)}, u32[]{:S(2)}) %collective-permute-start.6) | collective-permute-done | bytes 524320 | tf_op jit(solution)/shard_map/ppermute | solution.py:506
  204.8 5.7 %all-to-all-start.3 = ((bf16[8,32,1024]{2,1,0:T(8,128)(2,1)}), bf16[8,32,1024]{2,1,0:T(8,128)(2,1)}, u32[]{:S(2)}, u32[]{:S(2)}) async-start(bf16[8,32,1024]{2,1,0:T(8,128)(2,1)} %bitcast.31), calls=%async_computation.3 | async-start | bytes 1048576 | tf_op jit(solution)/shard_map/all_to_all | solution.py:508
  210.5 2.8 %partial_in.4 = (f32[256,1024]{1,0:T(8,128)S(1)}, bf16[256,1024]{1,0:T(8,128)(2,1)S(1)}) custom-call(bf16[1024,512]{1,0:T(8,128)(2,1)} %get-tuple-element.36.own.refs_3_, bf16[1024,512]{1,0:T(8,128)(2,1)} %collective-permute-done.2.sibling, bf16[2,256,512]{2,1,0:T(8,128)(2,1)S(1)} %pad_maximum_fusion.1.w_own, ...), custom_call_target="tpu_custom_call" | custom-call | flops 1073741824 | bytes 3670016 | tf_op jit(solution)/shard_map/partial_in/pallas_call | solution.py:486
  214.9 8.5 %collective-permute-done.4 = bf16[256,1024]{1,0:T(8,128)(2,1)S(1)} collective-permute-done((bf16[256,1024]{1,0:T(8,128)(2,1)S(1)}, bf16[256,1024]{1,0:T(8,128)(2,1)S(1)}, u32[]{:S(2)}, u32[]{:S(2)}) %collective-permute-start.4) | collective-permute-done | bytes 524320 | tf_op jit(solution)/shard_map/ppermute | solution.py:506
  224.3 5.7 %all-to-all-start.2 = ((bf16[8,32,1024]{2,1,0:T(8,128)(2,1)}), bf16[8,32,1024]{2,1,0:T(8,128)(2,1)S(1)}, u32[]{:S(2)}, u32[]{:S(2)}) async-start(bf16[8,32,1024]{2,1,0:T(8,128)(2,1)} %bitcast.14), calls=%async_computation.2 | async-start | bytes 1048576 | tf_op jit(solution)/shard_map/all_to_all | solution.py:508
  234.4 1.9 place.4.refs_0_
  236.3 1.9 place.5.refs_0_
  238.2 1.9 place.6.refs_0_
  (98 shorter events, 19.1 us)
Async XLA Ops:
  0.6 12.9 %copy-start.13 = (bf16[1024,256]{1,0:T(8,128)(2,1)S(1)}, bf16[1024,256]{1,0:T(8,128)(2,1)}, u32[]{:S(2)}) copy-start(bf16[1024,256]{1,0:T(8,128)(2,1)} %wv.1) | copy-start | bytes 1572868
  0.6 12.9 %copy-start.14 = (bf16[1024,256]{1,0:T(8,128)(2,1)S(1)}, bf16[1024,256]{1,0:T(8,128)(2,1)}, u32[]{:S(2)}) copy-start(bf16[1024,256]{1,0:T(8,128)(2,1)} %wg.1) | copy-start | bytes 1572868
  0.7 12.9 %copy-start.15 = (f32[9,256]{1,0:T(8,128)S(1)}, f32[9,256]{1,0:T(8,128)}, u32[]{:S(2)}) copy-start(f32[9,256]{1,0:T(8,128)} %taps.9) | copy-start | bytes 27652
  1.7 8.2 %collective-permute-start = (bf16[4,8,2048]{2,1,0:T(8,128)(2,1)S(1)}, bf16[4,8,2048]{2,1,0:T(8,128)(2,1)S(1)}, u32[]{:S(2)}, u32[]{:S(2)}) collective-permute-start(bf16[4,8,2048]{2,1,0:T(8,128)(2,1)S(1)} %pad_maximum_fusion.3), channel_id=1, source_target_pairs={{0,4},{4,8},{8,12},{12,16},{16,20},{20,24},{24,28},{1,5},{5,9},{9,... | collective-permute-start | bytes 393224 | tf_op jit(solution)/shard_map/ppermute | solution.py:333
  6.6 6.9 %collective-permute-start.1 = (bf16[4,8,2048]{2,1,0:T(8,128)(2,1)S(1)}, bf16[4,8,2048]{2,1,0:T(8,128)(2,1)S(1)}, u32[]{:S(2)}, u32[]{:S(2)}) collective-permute-start(bf16[4,8,2048]{2,1,0:T(8,128)(2,1)S(1)} %pad_maximum_fusion.4), channel_id=1, source_target_pairs={{4,0},{8,4},{12,8},{16,12},{20,16},{24,20},{28,24},{5,1},{9,5},{13... | collective-permute-start | bytes 393224 | tf_op jit(solution)/shard_map/ppermute | solution.py:333
  13.6 26.8 %copy-start.12 = (bf16[1024,256]{1,0:T(8,128)(2,1)S(1)}, bf16[1024,256]{1,0:T(8,128)(2,1)}, u32[]{:S(2)}) copy-start(bf16[1024,256]{1,0:T(8,128)(2,1)} %wo.1) | copy-start | bytes 1572868
  28.1 2.0 copy-start
  30.1 2.1 copy-start.7
  32.1 1.9 copy-start.9
  34.7 16.8 %all-to-all-start = ((f32[8,2,256]{2,1,0:T(2,128)}), f32[8,2,256]{2,1,0:T(2,128)S(1)}, u32[]{:S(2)}, u32[]{:S(2)}) async-start(f32[8,2,256]{2,1,0:T(2,128)} %broadcast_in_dim.6), calls=%async_computation | async-start | bytes 32768 | tf_op jit(solution)/shard_map/all_to_all | solution.py:295
  40.4 3.4 %copy-start.2 = (bf16[4,1024,1024]{2,1,0:T(8,128)(2,1)S(1)}, bf16[4,1024,1024]{2,1,0:T(8,128)(2,1)}, u32[]{:S(2)}) copy-start(bf16[4,1024,1024]{2,1,0:T(8,128)(2,1)} %right.1) | copy-start | bytes 25165828
  43.8 7.8 %copy-start.22 = (f32[256]{0:T(256)S(1)}, f32[256]{0:T(256)}, u32[]{:S(2)}) copy-start(f32[256]{0:T(256)} %param.14) | copy-start | bytes 3076
  43.8 7.8 %copy-start.23 = (f32[256]{0:T(256)S(1)}, f32[256]{0:T(256)}, u32[]{:S(2)}) copy-start(f32[256]{0:T(256)} %param.15) | copy-start | bytes 3076
  49.5 2.0 copy-start.11
  51.6 2.2 copy-start.1
  59.2 2.0 copy-start.5
  73.6 11.3 %copy-start.20 = (f32[1,256]{1,0:T(1,128)}, f32[1,256]{1,0:T(1,128)S(1)}, u32[]{:S(2)}) copy-start(f32[1,256]{1,0:T(1,128)S(1)} %get-tuple-element.90) | copy-start | bytes 3076
  73.6 11.3 %copy-start.21 = (f32[1,256]{1,0:T(1,128)}, f32[1,256]{1,0:T(1,128)S(1)}, u32[]{:S(2)}) copy-start(f32[1,256]{1,0:T(1,128)S(1)} %get-tuple-element.91) | copy-start | bytes 3076
  73.7 2.2 copy-start.6
  75.9 2.2 copy-start.8
  78.1 2.2 copy-start.10
  99.7 11.0 %all-to-all-start.8 = ((f32[8,9,256]{2,1,0:T(8,128)}), f32[8,9,256]{2,1,0:T(8,128)S(1)}, u32[]{:S(2)}, u32[]{:S(2)}) async-start(f32[8,9,256]{2,1,0:T(8,128)} %broadcast_in_dim.8), calls=%async_computation.8 | async-start | bytes 262144 | tf_op jit(solution)/shard_map/all_to_all | solution.py:295
  103.1 3.4 %copy-start.3 = (bf16[4,1024,1024]{2,1,0:T(8,128)(2,1)S(1)}, bf16[4,1024,1024]{2,1,0:T(8,128)(2,1)}, u32[]{:S(2)}) copy-start(bf16[4,1024,1024]{2,1,0:T(8,128)(2,1)} %right.1) | copy-start | bytes 25165828
  110.7 18.6 %all-to-all-start.7 = ((bf16[8,256,128]{2,1,0:T(8,128)(2,1)}), bf16[8,256,128]{2,1,0:T(8,128)(2,1)S(1)}, u32[]{:S(2)}, u32[]{:S(2)}) async-start(bf16[8,256,128]{2,1,0:T(8,128)(2,1)} %outer_w_out.1), calls=%async_computation.7 | async-start | bytes 1048576 | tf_op jit(solution)/shard_map/all_to_all | solution.py:538
  117.5 26.0 %collective-permute-start.9 = (bf16[1024,512]{1,0:T(8,128)(2,1)}, bf16[1024,512]{1,0:T(8,128)(2,1)}, u32[]{:S(2)}, u32[]{:S(2)}) collective-permute-start(bf16[1024,512]{1,0:T(8,128)(2,1)} %get-tuple-element.45.own.refs_0_), channel_id=1, source_target_pairs={{0,1},{1,0},{2,3},{3,2},{4,5},{5,4},{6,7},{7,6},{8,9},{9,8},{10,11... | collective-permute-start | bytes 3145736 | tf_op jit(solution)/shard_map/ppermute | solution.py:485
  117.5 3.4 %copy-start.16 = (bf16[4,1024,1024]{2,1,0:T(8,128)(2,1)S(1)}, bf16[4,1024,1024]{2,1,0:T(8,128)(2,1)}, u32[]{:S(2)}) copy-start(bf16[4,1024,1024]{2,1,0:T(8,128)(2,1)} %x.5) | copy-start | bytes 25165828
  129.2 7.4 %copy-start.17 = (bf16[8,256,128]{2,1,0:T(8,128)(2,1)}, bf16[8,256,128]{2,1,0:T(8,128)(2,1)S(1)}, u32[]{:S(2)}) copy-start(bf16[8,256,128]{2,1,0:T(8,128)(2,1)S(1)} %all-to-all-done.7) | copy-start | bytes 1572868
  129.2 32.5 %all-to-all-start.6 = ((bf16[8,512,128]{2,1,0:T(8,128)(2,1)}), bf16[8,512,128]{2,1,0:T(8,128)(2,1)}, u32[]{:S(2)}, u32[]{:S(2)}) async-start(bf16[8,512,128]{2,1,0:T(8,128)(2,1)} %outer_w_in.1), calls=%async_computation.6 | async-start | bytes 2097152 | tf_op jit(solution)/shard_map/all_to_all | solution.py:538
  136.1 7.4 %collective-permute-start.3 = (bf16[2,256,512]{2,1,0:T(8,128)(2,1)}, bf16[2,256,512]{2,1,0:T(8,128)(2,1)S(1)}, u32[]{:S(2)}, u32[]{:S(2)}) collective-permute-start(bf16[2,256,512]{2,1,0:T(8,128)(2,1)} %pad_maximum_fusion.2), channel_id=1, source_target_pairs={{0,1},{1,0},{2,3},{3,2},{4,5},{5,4},{6,7},{7,6},{8,9},{9,8},{10,11... | collective-permute-start | bytes 1572872 | tf_op jit(solution)/shard_map/ppermute | solution.py:348
  136.7 30.5 %collective-permute-start.7 = (bf16[1024,512]{1,0:T(8,128)(2,1)}, bf16[1024,512]{1,0:T(8,128)(2,1)}, u32[]{:S(2)}, u32[]{:S(2)}) collective-permute-start(bf16[1024,512]{1,0:T(8,128)(2,1)} %get-tuple-element.42.own.refs_1_), channel_id=1, source_target_pairs={{0,1},{1,0},{2,3},{3,2},{4,5},{5,4},{6,7},{7,6},{8,9},{9,8},{10,11... | collective-permute-start | bytes 3145736 | tf_op jit(solution)/shard_map/ppermute | solution.py:485
  137.1 3.4 %copy-start.4 = (bf16[4,1024,1024]{2,1,0:T(8,128)(2,1)S(1)}, bf16[4,1024,1024]{2,1,0:T(8,128)(2,1)}, u32[]{:S(2)}) copy-start(bf16[4,1024,1024]{2,1,0:T(8,128)(2,1)} %right.1) | copy-start | bytes 25165828
  140.4 3.0 %copy-start.19 = (bf16[8,1,32,512]{3,2,1,0:T(8,128)(2,1)S(1)}, bf16[8,1,32,512]{3,2,1,0:T(8,128)(2,1)}, u32[]{:S(2)}) copy-start(bf16[8,1,32,512]{3,2,1,0:T(8,128)(2,1)} %get-tuple-element.84) | copy-start | bytes 786436
  146.4 14.1 %collective-permute-start.10 = (bf16[256,1024]{1,0:T(8,128)(2,1)S(1)}, bf16[256,1024]{1,0:T(8,128)(2,1)S(1)}, u32[]{:S(2)}, u32[]{:S(2)}) collective-permute-start(bf16[256,1024]{1,0:T(8,128)(2,1)S(1)} %get-tuple-element.47), channel_id=1, source_target_pairs={{0,2},{1,3},{2,0},{3,1},{4,6},{5,7},{6,4},{7,5},{8,10},{9,11},{10,... | collective-permute-start | bytes 1572872 | tf_op jit(solution)/shard_map/ppermute | solution.py:506
  147.9 41.7 %collective-permute-start.5 = (bf16[1024,512]{1,0:T(8,128)(2,1)}, bf16[1024,512]{1,0:T(8,128)(2,1)}, u32[]{:S(2)}, u32[]{:S(2)}) collective-permute-start(bf16[1024,512]{1,0:T(8,128)(2,1)} %get-tuple-element.39.own.refs_2_), channel_id=1, source_target_pairs={{0,1},{1,0},{2,3},{3,2},{4,5},{5,4},{6,7},{7,6},{8,9},{9,8},{10,11... | collective-permute-start | bytes 3145736 | tf_op jit(solution)/shard_map/ppermute | solution.py:485
  161.8 22.1 %all-to-all-start.5 = ((bf16[8,32,1024]{2,1,0:T(8,128)(2,1)}), bf16[8,32,1024]{2,1,0:T(8,128)(2,1)}, u32[]{:S(2)}, u32[]{:S(2)}) async-start(bf16[8,32,1024]{2,1,0:T(8,128)(2,1)} %bitcast.30), calls=%async_computation.5 | async-start | bytes 1048576 | tf_op jit(solution)/shard_map/all_to_all | solution.py:508
  170.1 12.9 %collective-permute-start.8 = (bf16[256,1024]{1,0:T(8,128)(2,1)S(1)}, bf16[256,1024]{1,0:T(8,128)(2,1)S(1)}, u32[]{:S(2)}, u32[]{:S(2)}) collective-permute-start(bf16[256,1024]{1,0:T(8,128)(2,1)S(1)} %get-tuple-element.44), channel_id=1, source_target_pairs={{0,2},{1,3},{2,0},{3,1},{4,6},{5,7},{6,4},{7,5},{8,10},{9,11},{10,... | collective-permute-start | bytes 1572872 | tf_op jit(solution)/shard_map/ppermute | solution.py:506
  171.6 38.9 %collective-permute-start.2 = (bf16[1024,512]{1,0:T(8,128)(2,1)}, bf16[1024,512]{1,0:T(8,128)(2,1)}, u32[]{:S(2)}, u32[]{:S(2)}) collective-permute-start(bf16[1024,512]{1,0:T(8,128)(2,1)} %get-tuple-element.36.own.refs_3_), channel_id=1, source_target_pairs={{0,1},{1,0},{2,3},{3,2},{4,5},{5,4},{6,7},{7,6},{8,9},{9,8},{10,11... | collective-permute-start | bytes 3145736 | tf_op jit(solution)/shard_map/ppermute | solution.py:485
  183.9 20.9 %all-to-all-start.4 = ((bf16[8,32,1024]{2,1,0:T(8,128)(2,1)}), bf16[8,32,1024]{2,1,0:T(8,128)(2,1)}, u32[]{:S(2)}, u32[]{:S(2)}) async-start(bf16[8,32,1024]{2,1,0:T(8,128)(2,1)} %bitcast.32), calls=%async_computation.4 | async-start | bytes 1048576 | tf_op jit(solution)/shard_map/all_to_all | solution.py:508
  192.5 11.4 %collective-permute-start.6 = (bf16[256,1024]{1,0:T(8,128)(2,1)S(1)}, bf16[256,1024]{1,0:T(8,128)(2,1)S(1)}, u32[]{:S(2)}, u32[]{:S(2)}) collective-permute-start(bf16[256,1024]{1,0:T(8,128)(2,1)S(1)} %get-tuple-element.41), channel_id=1, source_target_pairs={{0,2},{1,3},{2,0},{3,1},{4,6},{5,7},{6,4},{7,5},{8,10},{9,11},{10,... | collective-permute-start | bytes 1572872 | tf_op jit(solution)/shard_map/ppermute | solution.py:506
  204.8 19.5 %all-to-all-start.3 = ((bf16[8,32,1024]{2,1,0:T(8,128)(2,1)}), bf16[8,32,1024]{2,1,0:T(8,128)(2,1)}, u32[]{:S(2)}, u32[]{:S(2)}) async-start(bf16[8,32,1024]{2,1,0:T(8,128)(2,1)} %bitcast.31), calls=%async_computation.3 | async-start | bytes 1048576 | tf_op jit(solution)/shard_map/all_to_all | solution.py:508
  213.4 17.3 %copy-start.18 = (bf16[8,256,128]{2,1,0:T(8,128)(2,1)S(1)}, bf16[8,256,128]{2,1,0:T(8,128)(2,1)}, u32[]{:S(2)}) copy-start(bf16[8,256,128]{2,1,0:T(8,128)(2,1)} %copy-done.17) | copy-start | bytes 1572868
  213.4 10.0 %collective-permute-start.4 = (bf16[256,1024]{1,0:T(8,128)(2,1)S(1)}, bf16[256,1024]{1,0:T(8,128)(2,1)S(1)}, u32[]{:S(2)}, u32[]{:S(2)}) collective-permute-start(bf16[256,1024]{1,0:T(8,128)(2,1)S(1)} %get-tuple-element.38), channel_id=1, source_target_pairs={{0,2},{1,3},{2,0},{3,1},{4,6},{5,7},{6,4},{7,5},{8,10},{9,11},{10,... | collective-permute-start | bytes 1572872 | tf_op jit(solution)/shard_map/ppermute | solution.py:506
  224.3 16.0 %all-to-all-start.2 = ((bf16[8,32,1024]{2,1,0:T(8,128)(2,1)}), bf16[8,32,1024]{2,1,0:T(8,128)(2,1)S(1)}, u32[]{:S(2)}, u32[]{:S(2)}) async-start(bf16[8,32,1024]{2,1,0:T(8,128)(2,1)} %bitcast.14), calls=%async_computation.2 | async-start | bytes 1048576 | tf_op jit(solution)/shard_map/all_to_all | solution.py:508

commit v2 on v1

v2 whole, which is shorter than its diff:
```python
import functools

import jax
import jax.numpy as jnp
from jax import lax
from jax.experimental import pallas as pl
from jax.experimental.pallas import tpu as pltpu
from jax.sharding import PartitionSpec as P

EPSILON = 1e-05
EDGE = 8
LANES = 128
F32 = jnp.float32
BF16 = jnp.bfloat16


def sigmoid(x):
    return 0.5 * jnp.tanh(0.5 * x) + 0.5


def dot(a, b):
    return jnp.dot(a, b, preferred_element_type=F32)


def dot_nt(a, b):
    return lax.dot_general(a, b, (((1,), (1,)), ((), ())), preferred_element_type=F32)


def dot_tn(a, b):
    return lax.dot_general(a, b, (((0,), (0,)), ((), ())), preferred_element_type=F32)


def rows_of(count, first):
    return first + lax.broadcasted_iota(jnp.int32, (count, 1), 0)


def fold_rows(x):
    return jnp.sum(x.reshape(x.shape[0] // 8, 8, x.shape[1]), axis=0)


def block_rows(total, most):
    return max(b for b in range(8, most + 1, 8) if total % b == 0)


def whole(shape):
    return pl.BlockSpec(shape, lambda *i: (0,) * len(shape))


def per_record(shape):
    return pl.BlockSpec((1,) + shape, lambda r: (r,) + (0,) * len(shape))


def smem():
    return pl.BlockSpec(memory_space=pltpu.SMEM)


def anywhere():
    return pl.BlockSpec(memory_space=pl.ANY)


def after(x, *earlier):
    return lax.optimization_barrier((x,) + earlier)[0]


def spread_sums(out, sums):
    for s in range(out.shape[0]):
        out[s] = sums


def call(kernel, name, grid, in_specs, out_specs, out_shape, scratch, flops, moved, aliases=None):
    return pl.pallas_call(
        kernel,
        name=name,
        grid=grid,
        in_specs=in_specs,
        out_specs=out_specs,
        out_shape=out_shape,
        scratch_shapes=scratch,
        input_output_aliases=aliases or {},
        cost_estimate=pl.CostEstimate(flops=int(flops), bytes_accessed=int(moved), transcendentals=0),
        compiler_params=pltpu.CompilerParams(vmem_limit_bytes=60 * 1024 * 1024),
    )


def pick_kernel(sel, grads, out):
    out[0] = dot_nt(sel[...], grads[0]).astype(BF16)


def gate_kernel(meta, x, halo, wv, wg, taps, vl_o, sg_o, conv_o, st_o, gp, st):
    r = pl.program_id(0)
    hi = meta[0, r]
    lo = meta[1, r]
    frames = x.shape[1]
    width = wv.shape[1]
    halves = width // LANES

    def put(row, value):
        for h in range(halves):
            gp[h, pl.ds(row, value.shape[0]), :] = value[:, h * LANES : (h + 1) * LANES]

    edge_v = dot(halo[0], wv[...])
    edge_g = dot(halo[0], wg[...])
    row = rows_of(2 * EDGE, 0)
    pos = jnp.where(row < EDGE, row - EDGE, row - EDGE + frames)
    edge = jnp.where((pos >= lo) & (pos < hi), edge_v * sigmoid(edge_g), 0.0)
    zero = jnp.zeros((EDGE, width), F32)
    put(0, zero)
    put(EDGE, edge[:EDGE])
    put(2 * EDGE + frames, edge[EDGE:])
    put(3 * EDGE + frames, zero)
    step = block_rows(frames, 256)

    def project(i, carry):
        base = pl.multiple_of(i * step, step)
        xb = x[0, pl.ds(base, step), :]
        v = dot(xb, wv[...])
        s = sigmoid(dot(xb, wg[...]))
        vl_o[0, pl.ds(base, step), :] = v
        sg_o[0, pl.ds(base, step), :] = s
        put(2 * EDGE + base, jnp.where(rows_of(step, base) < hi, v * s, 0.0))
        return carry

    lax.fori_loop(0, frames // step, project, 0)
    span = frames + 2 * EDGE
    cb = block_rows(span, 104)
    kernel = taps.shape[0]
    margin = (kernel - 1) // 2
    for h in range(halves):
        cols = slice(h * LANES, (h + 1) * LANES)

        def convolve(i, carry):
            s1, s2 = carry
            base = pl.multiple_of(i * cb, 8)
            acc = jnp.zeros((cb, LANES), F32)
            for k in range(kernel):
                acc = acc + taps[k : k + 1, cols] * gp[h, pl.ds(base + EDGE - margin + k, cb), :]
            conv_o[0, pl.ds(base, cb), cols] = acc
            pos = rows_of(cb, base - EDGE)
            kept = jnp.where((pos >= 0) & (pos < jnp.minimum(hi, frames)), acc, 0.0)
            return s1 + fold_rows(kept), s2 + fold_rows(kept * kept)

        none = jnp.zeros((8, LANES), F32)
        s1, s2 = lax.fori_loop(0, span // cb, convolve, (none, none))
        add = jnp.concatenate(
            [jnp.sum(s1, axis=0, keepdims=True), jnp.sum(s2, axis=0, keepdims=True)], axis=0
        )
        st[:, cols] = jnp.where(r == 0, 0.0, st[:, cols]) + add

    @pl.when(r == pl.num_programs(0) - 1)
    def _():
        spread_sums(st_o, st[...])


def batch_norm(stats, count):
    sums = jnp.sum(stats[...], axis=0)
    centre = sums[0:1] / count
    spread = sums[1:2] / count - centre * centre
    return centre, lax.rsqrt(spread + EPSILON)


def norm_kernel(
    meta, count, stats, affine, grads, halo, wo, conv, swished_o, gn_o, st_o, st, ping, pong
):
    r = pl.program_id(0)
    hi = meta[0, r]
    lo = meta[1, r]
    frames = grads.shape[1]
    centre, inv = batch_norm(stats, count[0, 0])
    gain, shift = affine[0:1, :], affine[1:2, :]

    def part(row, swish_grad):
        size = swish_grad.shape[0]
        unit = (conv[0, pl.ds(row, size), :] - centre) * inv
        normalized = unit * gain + shift
        s = sigmoid(normalized)
        pos = rows_of(size, row - EDGE)
        keep = (pos >= lo) & (pos < hi)
        swished = jnp.where(keep, normalized * s, 0.0)
        gn = jnp.where(keep, swish_grad, 0.0) * (s + normalized * (s - s * s))
        gn_o[0, pl.ds(row, size), :] = gn
        return unit, swished, gn

    edge = dot(halo[0], wo[...])
    part(0, edge[:EDGE])
    part(frames + EDGE, edge[EDGE:])
    step = block_rows(frames, 256)
    small = block_rows(step, 32)
    s1 = jnp.zeros((8, conv.shape[2]), F32)
    s2 = s1
    held = (ping, pong)
    ping[...] = dot(grads[0, :step, :], wo[...])
    for i in range(frames // step):
        now = held[i % 2]
        if (i + 1) * step < frames:
            held[(i + 1) % 2][...] = dot(grads[0, (i + 1) * step : (i + 2) * step, :], wo[...])
        for j in range(step // small):
            base = i * step + j * small
            unit, swished, gn = part(base + EDGE, now[j * small : (j + 1) * small, :])
            swished_o[0, base : base + small, :] = swished.astype(BF16)
            s1 = s1 + fold_rows(gn)
            s2 = s2 + fold_rows(gn * unit)
    add = jnp.concatenate(
        [jnp.sum(s1, axis=0, keepdims=True), jnp.sum(s2, axis=0, keepdims=True)], axis=0
    )
    st[...] = jnp.where(r == 0, 0.0, st[...]) + add

    @pl.when(r == pl.num_programs(0) - 1)
    def _():
        spread_sums(st_o, st[...])


def back_kernel(
    record, meta, count, stats, sums, gain, gn, conv, vl, sg, taps, out, taps_o, gc, acc
):
    i = pl.program_id(0)
    hi = meta[0, record]
    lo = meta[1, record]
    frames, width = vl.shape[1:]
    halves = width // LANES
    span = frames + 2 * EDGE
    kernel = taps.shape[0]
    margin = (kernel - 1) // 2
    cb = block_rows(span, 144)
    step = block_rows(frames, 64)
    total_frames = count[0, 0]
    centre, inv = batch_norm(stats, total_frames)
    grad_sums = jnp.sum(sums[...], axis=0)
    scale = gain[...] * inv
    offset = scale * grad_sums[0:1] / total_frames
    slope = scale * inv * grad_sums[1:2] / total_frames
    first = i * frames

    @pl.when(i == 0)
    def _():
        acc[...] = jnp.zeros_like(acc)

    for h in range(halves):
        cols = slice(h * LANES, (h + 1) * LANES)
        for base in range(0, span, cb):
            pos = rows_of(cb, first + (base - EDGE))
            mean = offset[:, cols] + (conv[0, base : base + cb, cols] - centre[:, cols]) * slope[:, cols]
            gc[h, base : base + cb, :] = scale[:, cols] * gn[0, base : base + cb, cols] - jnp.where(
                (pos >= lo) & (pos < hi), mean, 0.0
            )
        sums_k = [acc[h, k] for k in range(kernel)]
        for base in range(0, frames, step):
            v = vl[0, base : base + step, cols]
            s = sg[0, base : base + step, cols]
            keep = rows_of(step, first + base) < hi
            vs = v * s
            gated = jnp.where(keep, vs, 0.0)
            total = jnp.zeros((step, LANES), F32)
            for k in range(kernel):
                window = gc[h, base + EDGE + margin - k : base + EDGE + margin - k + step, :]
                total = total + taps[k : k + 1, cols] * window
                sums_k[k] = sums_k[k] + fold_rows(window * gated)
            total = jnp.where(keep, total, 0.0)
            out[base : base + step, cols] = (total * s).astype(BF16)
            out[base : base + step, width + h * LANES : width + (h + 1) * LANES] = (
                total * (vs - vs * s)
            ).astype(BF16)
        for k in range(kernel):
            acc[h, k] = sums_k[k]

    @pl.when(i == pl.num_programs(0) - 1)
    def _():
        taps_o[...] = jnp.zeros_like(taps_o)
        for h in range(halves):
            for k in range(kernel):
                taps_o[k : k + 1, h * LANES : (h + 1) * LANES] = jnp.sum(
                    acc[h, k], axis=0, keepdims=True
                )


def partial_kernel(own, sibling, w_own, w_sibling, picked, mine, *others):
    for d in range(w_own.shape[0]):
        total = dot_nt(w_own[d], own[...]) + dot_nt(w_sibling[d], sibling[...])
        if d == 0:
            mine[...] = total + picked[0].astype(F32)
        else:
            others[d - 1][...] = total.astype(BF16)


def outer_kernel(records, parity, x, grads, swished, *refs):
    lefts, taps = refs[:records], refs[records : 2 * records]
    keep, send, acc = refs[2 * records :]
    width = swished.shape[2]
    shard = keep.shape[2]
    r = pl.program_id(0)

    def add(rows, value, first):
        acc[rows, :] = value if first else acc[rows, :] + value

    for i, left in enumerate(lefts):

        @pl.when(r == i)
        def _(i=i, left=left):
            add(slice(0, 2 * width), dot_tn(left[...], x[0]), i == 0)
            add(slice(2 * width, 3 * width), dot_tn(swished[0], grads[0]), i == 0)

    @pl.when(r == records - 1)
    def _():
        tap_sums = taps[0][...]
        for part in taps[1:]:
            tap_sums = tap_sums + part[...]

        def write(place, odd):
            for j in range(place.shape[0]):
                at = (2 * j + odd) * shard
                place[j, : 3 * width, :] = acc[:, at : at + shard].astype(BF16)
                for q in range(width // shard):
                    row = 3 * width + 16 * q
                    place[j, row : row + 16, :] = tap_sums[:, q * shard : (q + 1) * shard].astype(
                        BF16
                    )

        @pl.when(parity[0, 0] == 0)
        def _():
            write(keep, 0)
            write(send, 1)

        @pl.when(parity[0, 0] != 0)
        def _():
            write(keep, 1)
            write(send, 0)


def finish_kernel(kernel, got, value, gate, out, taps):
    width = value.shape[1]
    shard = value.shape[0]

    def total(row, size):
        sums = got[0, row : row + size, :].astype(F32)
        for j in range(1, got.shape[0]):
            sums = sums + got[j, row : row + size, :].astype(F32)
        return sums

    for i, place in enumerate((value, gate, out)):
        place[...] = total(i * width, width).T
    for q in range(width // shard):
        taps[:, q * shard : (q + 1) * shard] = total(3 * width + 16 * q, 16)[:kernel]


def place_kernel(*refs):
    parts, out, sem = refs[:-2], refs[-2], refs[-1]
    frames = parts[0].shape[2]
    copies = [
        pltpu.make_async_copy(
            part.at[s], out.at[r, :, pl.ds(s * frames, frames)], sem.at[r, s]
        )
        for r, part in enumerate(parts)
        for s in range(part.shape[0])
    ]
    for copy in copies:
        copy.start()
    for copy in copies:
        copy.wait()


def exchange(copies, axis):
    return lax.all_to_all(copies, axis, 0, 0, tiled=True)


def per_device(
    normed,
    grad_out,
    value_weight,
    gate_weight,
    depth_taps,
    norm_gain,
    norm_shift,
    out_weight,
    lengths,
):
    recs, frames, model = normed.shape
    kernel = depth_taps.shape[0]
    width = value_weight.shape[1]
    seqs = lax.axis_size("seq")
    tps = lax.axis_size("tp")
    chips = tps // 2
    piece = model // (seqs * tps)
    rows = seqs * piece
    shard = model // seqs
    span = frames + 2 * EDGE
    seq_at = lax.axis_index("seq")
    tp_at = lax.axis_index("tp")
    chip_at, core_at = tp_at // 2, tp_at % 2
    count = jnp.sum(lengths).astype(F32)
    first = (seq_at * frames).astype(jnp.int32)
    meta = jnp.stack([lengths - first, jnp.full((recs,), 0, jnp.int32) - first])
    halves = width // LANES
    counts = count.reshape(1, 1)
    parity = (seq_at % 2).astype(jnp.int32).reshape(1, 1)
    sds = jax.ShapeDtypeStruct

    low_edge = jnp.concatenate([normed[:, -EDGE:], grad_out[:, -EDGE:]], axis=2)
    high_edge = jnp.concatenate([normed[:, :EDGE], grad_out[:, :EDGE]], axis=2)
    up = [(i, i + 1) for i in range(seqs - 1)]
    down = [(j, i) for i, j in up]
    halo = jnp.concatenate(
        [lax.ppermute(low_edge, "seq", up), lax.ppermute(high_edge, "seq", down)], axis=1
    )
    halo_x, halo_g = halo[:, :, :model], halo[:, :, model:]

    both = jnp.concatenate([value_weight, gate_weight], axis=1).reshape(seqs, tps, piece, 2 * width)

    def chosen(core):
        picks = [
            lax.dynamic_index_in_dim(both, ((chip_at + d) % chips) * 2 + core, 1, keepdims=False)
            for d in range(chips)
        ]
        return jnp.stack(picks).reshape(chips, rows, 2 * width)

    swap = [(i, i ^ 1) for i in range(tps)]
    w_own = chosen(core_at)
    w_sibling = lax.ppermute(chosen(1 - core_at), "tp", swap)

    channel = (
        jnp.arange(seqs, dtype=jnp.int32)[:, None] * (tps * piece)
        + tp_at * piece
        + jnp.arange(piece, dtype=jnp.int32)[None, :]
    ).reshape(rows, 1)
    select = (channel == jnp.arange(model, dtype=jnp.int32)[None, :]).astype(BF16)
    array_bytes = recs * frames * width * 4
    input_bytes = recs * frames * model * 2
    matmul = 2 * recs * frames * model * width

    picked = call(
        pick_kernel,
        "pick",
        (recs,),
        [whole((rows, model)), per_record((frames, model))],
        per_record((rows, frames)),
        sds((recs, rows, frames), BF16),
        [],
        matmul,
        input_bytes,
    )(select, grad_out)

    vl, sg, conv, stats = call(
        gate_kernel,
        "gate_conv",
        (recs,),
        [
            smem(),
            per_record((frames, model)),
            per_record((2 * EDGE, model)),
            whole((model, width)),
            whole((model, width)),
            whole((kernel, width)),
        ],
        [
            per_record((frames, width)),
            per_record((frames, width)),
            per_record((span, width)),
            whole((seqs, 2, width)),
        ],
        [
            sds((recs, frames, width), F32),
            sds((recs, frames, width), F32),
            sds((recs, span, width), F32),
            sds((seqs, 2, width), F32),
        ],
        [pltpu.VMEM((halves, frames + 4 * EDGE, LANES), F32), pltpu.VMEM((2, width), F32)],
        2 * matmul,
        input_bytes + 3 * array_bytes,
    )(meta, normed, after(halo_x, picked), value_weight, gate_weight, depth_taps)
    stats = exchange(stats, "seq")

    chunk = block_rows(frames, 256)
    swished, gn, sums = call(
        norm_kernel,
        "swish_norm",
        (recs,),
        [
            smem(),
            smem(),
            whole((seqs, 2, width)),
            whole((2, width)),
            per_record((frames, model)),
            per_record((2 * EDGE, model)),
            whole((model, width)),
            per_record((span, width)),
        ],
        [per_record((frames, width)), per_record((span, width)), whole((seqs, 2, width))],
        [
            sds((recs, frames, width), BF16),
            sds((recs, span, width), F32),
            sds((seqs, 2, width), F32),
        ],
        [
            pltpu.VMEM((2, width), F32),
            pltpu.VMEM((chunk, width), F32),
            pltpu.VMEM((chunk, width), F32),
        ],
        matmul,
        input_bytes + 3 * array_bytes,
    )(meta, counts, stats, jnp.stack([norm_gain, norm_shift]), grad_out, halo_g, out_weight, conv)
    sums = exchange(sums, "seq")
    grad_shift, grad_gain = jnp.sum(sums, axis=0)

    def back(r, marker):
        def window(i):
            return (r, pl.multiple_of(i * chunk, chunk), 0)

        return call(
            functools.partial(back_kernel, r),
            "back_conv",
            (frames // chunk,),
            [
                smem(),
                smem(),
                whole((seqs, 2, width)),
                whole((seqs, 2, width)),
                whole((1, width)),
                pl.BlockSpec((pl.Element(1), pl.Element(chunk + 2 * EDGE), pl.Element(width)), window),
                pl.BlockSpec((pl.Element(1), pl.Element(chunk + 2 * EDGE), pl.Element(width)), window),
                pl.BlockSpec((1, chunk, width), lambda i: (r, i, 0)),
                pl.BlockSpec((1, chunk, width), lambda i: (r, i, 0)),
                whole((kernel, width)),
            ],
            [pl.BlockSpec((chunk, 2 * width), lambda i: (i, 0)), whole((16, width))],
            [sds((frames, 2 * width), BF16), sds((16, width), F32)],
            [
                pltpu.VMEM((halves, chunk + 2 * EDGE, LANES), F32),
                pltpu.VMEM((halves, kernel, 8, LANES), F32),
            ],
            60 * frames * width,
            4 * array_bytes // recs,
        )(meta, counts, stats, sums, norm_gain[None], gn, conv, vl, sg, after(depth_taps, *marker))

    def partials(r, mine):
        sibling = lax.ppermute(mine, "tp", swap)
        return call(
            partial_kernel,
            "partial_in",
            (frames // chunk,),
            [
                pl.BlockSpec((chunk, 2 * width), lambda i: (i, 0)),
                pl.BlockSpec((chunk, 2 * width), lambda i: (i, 0)),
                whole((chips, rows, 2 * width)),
                whole((chips, rows, 2 * width)),
                pl.BlockSpec((1, rows, chunk), lambda i: (r, 0, i)),
            ],
            [pl.BlockSpec((rows, chunk), lambda i: (0, i))] * chips,
            [sds((rows, frames), F32)] + [sds((rows, frames), BF16)] * (chips - 1),
            [],
            2 * matmul // recs,
            8 * frames * width + 6 * rows * frames,
        )(mine, sibling, w_own, w_sibling, picked)

    grads, tap_parts, parts = [], [], []
    for r in range(recs):
        mine, tap_part = back(r, parts[r - 2] if r > 1 else ())
        grads.append(mine)
        tap_parts.append(tap_part)
        if r > 0:
            parts.append(partials(r - 1, grads[r - 1]))
    parts.append(partials(recs - 1, grads[recs - 1]))

    moved = []
    for r in range(recs):
        total = parts[r][0]
        for d in range(1, chips):
            send = [(i, ((i // 2 + d) % chips) * 2 + i % 2) for i in range(tps)]
            total = total + lax.ppermute(parts[r][d], "tp", send).astype(F32)
        own = total.astype(BF16).reshape(seqs, piece, frames)
        moved.append(exchange(own, "seq"))

    slots = 3 * width + 16 * (width // shard)
    half = sds((seqs // 2, slots, shard), BF16)
    keep, send = call(
        functools.partial(outer_kernel, recs),
        "outer",
        (recs,),
        [smem(), per_record((frames, model)), per_record((frames, model)), per_record((frames, width))]
        + [whole((frames, 2 * width))] * recs
        + [whole((16, width))] * recs,
        [whole(half.shape)] * 2,
        [half] * 2,
        [pltpu.VMEM((3 * width, model), F32)],
        3 * matmul,
        2 * input_bytes + 6 * recs * frames * width,
    )(parity, after(normed, *parts[-1]), grad_out, swished, *grads, *tap_parts)
    pairs = [(i, i ^ 1) for i in range(seqs)]
    paired = (keep.astype(F32) + lax.ppermute(send, "seq", pairs).astype(F32)).astype(BF16)
    same = [[i for i in range(seqs) if i % 2 == odd] for odd in range(2)]
    got = lax.all_to_all(paired, "seq", 0, 0, axis_index_groups=same, tiled=True)
    w_value, w_gate, w_out, grad_taps = call(
        functools.partial(finish_kernel, kernel),
        "finish",
        (1,),
        [whole(half.shape)],
        [whole((shard, width))] * 3 + [whole((kernel, width))],
        [sds((shard, width), F32)] * 3 + [sds((kernel, width), F32)],
        [],
        0,
        8 * seqs * slots * shard,
    )(got)
    grad_in = call(
        place_kernel,
        "place",
        (1,),
        [anywhere()] * recs,
        anywhere(),
        sds((recs, piece, seqs * frames), BF16),
        [pltpu.SemaphoreType.DMA((recs, seqs))],
        0,
        4 * recs * piece * seqs * frames,
    )(*moved)
    return (grad_in, w_value, w_gate, w_out, grad_taps, grad_gain, grad_shift)


def solution(mesh):
    placed = (
        P(None, "seq", None),
        P(None, "seq", None),
        P(None, "tp"),
        P(None, "tp"),
        P(None, "tp"),
        P("tp"),
        P("tp"),
        P(None, "tp"),
        P(),
    )
    return jax.shard_map(
        per_device,
        mesh=mesh,
        in_specs=placed,
        out_specs=(
            P(None, ("seq", "tp"), None),
            P("seq", "tp"),
            P("seq", "tp"),
            P("seq", "tp"),
            P(None, "tp"),
            P("tp"),
            P("tp"),
        ),
        check_vma=False,
    )
```

time: 243 us -> 278 us (1.14)
  Pallas kernels: 77.5 us -> 155 us
  local copies, waits for them, and re-layouts: 37.9 us -> 8.91 us
  blocking collectives: 12.4 us -> 0 us
  starting transfers between devices: 56.5 us -> 49.7 us
  waiting for transfers between devices: 46.5 us -> 51.4 us
    pallas_call x16 -> x12, Pallas kernels: 60 us -> 132 us  [the longest x1 64.9 us: per_device(): call(place_kernel, 'place', (1,), [anywhere()] * recs, anywhere(), sds((r...]
    unnamed x52 -> x41, local copies, waits for them, and re-layouts: 34.7 us -> 5.92 us
    all_to_all x1 -> x0, blocking collectives: 12.4 us -> none  [everyone(): return jnp.sum(lax.all_to_all(copies, axis, 0, 0, tiled=True), axis=0)]
    all_to_all x8 -> x7, waiting for transfers between devices: 0.69 us -> 11.8 us  [the longest x6 11.8 us: exchange(): return lax.all_to_all(copies, axis, 0, 0, tiled=True)]
    all_to_all x8 -> x7, starting transfers between devices: 43.6 us -> 34.5 us  [the longest x6 29.7 us: exchange(): return lax.all_to_all(copies, axis, 0, 0, tiled=True)]
    pallas_call x1, Pallas kernels: 3 us -> 6.7 us  [per_device(): call(pick_kernel, 'pick', (recs,), [whole((rows, model)), per_record((fra...]
    ppermute x1, waiting for transfers between devices: 3.57 us -> 0.01 us  [per_device(): lax.ppermute(high_edge, 'seq', down)]
    ppermute x8 -> x9, waiting for transfers between devices: 42.2 us -> 39.5 us  [the longest x4 25.3 us: per_device(): total = total + lax.ppermute(parts[r][d], 'tp', send).astype(F32)]
  transfers between devices with their start and end apart: 19 -> 19, of which waited for: 7 -> 6; matrix products, arithmetic and copies ran while one was open for 5% -> 4% of each run, Pallas kernels for 16% -> 44%
where the time goes in v2:
time: 278 us; the launch traced here: 277 us
  Pallas kernels  155 us (56%)
  waiting for transfers between devices  51.4 us (18%)
  starting transfers between devices  49.7 us (18%)
  other arithmetic  10.1 us (4%)
  local copies, waits for them, and re-layouts  8.91 us (3%)
    pallas_call x1, Pallas kernels, per_device(): call(place_kernel, 'place', (1,), [anywhere()] * recs, anywhere(), sds((r...  64.9 us
    all_to_all x6, starting transfers between devices, exchange(): return lax.all_to_all(copies, axis, 0, 0, tiled=True)  29.7 us
    ppermute x4, waiting for transfers between devices, per_device(): total = total + lax.ppermute(parts[r][d], 'tp', send).astype(F32)  25.3 us
    pallas_call x4, Pallas kernels, partials(): call(partial_kernel, 'partial_in', (frames // chunk,), [pl.BlockSpec((chu...  20.6 us
    pallas_call x4, Pallas kernels, back(): call(functools.partial(back_kernel, r), 'back_conv', (frames // chunk,),...  20.3 us
    pallas_call x1, Pallas kernels, per_device(): call(gate_kernel, 'gate_conv', (recs,), [smem(), per_record((frames, mode...  16.6 us
    ppermute x1, waiting for transfers between devices, per_device(): lax.ppermute(send, 'seq', pairs).astype(F32)  14.1 us
    pallas_call x1, Pallas kernels, per_device(): call(functools.partial(outer_kernel, recs), 'outer', (recs,), [smem(), pe...  13.6 us
  transfers between devices with their start and end apart: 19, of which 6 were waited for; matrix products, arithmetic and copies ran while one was open for 4% of the time, Pallas kernels for 44%

profile of v2, /device:TPU:0, one launch (start us, length us, event | category | flops | bytes accessed | tf_op | source)
XLA Modules:
  0.0 276.6 jit_solution(3988901381405228301)
XLA Ops:
  0.6 1.0 fusion.1
  1.6 4.9 %collective-permute-start = (bf16[4,8,2048]{2,1,0:T(8,128)(2,1)S(1)}, bf16[4,8,2048]{2,1,0:T(8,128)(2,1)S(1)}, u32[]{:S(2)}, u32[]{:S(2)}) collective-permute-start(bf16[4,8,2048]{2,1,0:T(8,128)(2,1)S(1)} %pad_maximum_fusion.3), channel_id=1, source_target_pairs={{0,4},{4,8},{8,12},{12,16},{16,20},{20,24},{24,28},{1,5},{5,9},{9,... | collective-permute-start | bytes 393224 | tf_op jit(solution)/shard_map/ppermute | solution.py:401
  6.5 1.3 collective-permute-start.1
  7.8 1.3 fusion.5
  9.3 0.9 fusion.sel
  10.8 6.7 %pick.1.picked = bf16[4,256,1024]{2,1,0:T(8,128)(2,1)} custom-call(bf16[256,1024]{1,0:T(8,128)(2,1)} %fusion.sel, bf16[4,1024,1024]{2,1,0:T(8,128)(2,1)} %grads.5), custom_call_target="tpu_custom_call" | custom-call | flops 2147483648 | bytes 8388608 | tf_op jit(solution)/shard_map/pick/pallas_call | solution.py:428
  18.3 16.6 %gate_conv.1 = (f32[4,1024,256]{2,1,0:T(8,128)}, f32[4,1024,256]{2,1,0:T(8,128)}, f32[4,1040,256]{2,1,0:T(8,128)}, f32[8,2,256]{2,1,0:T(2,128)}) custom-call(s32[2,4]{1,0:T(2,128)} %stack.35.meta, bf16[4,1024,1024]{2,1,0:T(8,128)(2,1)} %x.4, bf16[4,16,1024]{2,1,0:T(8,128)(2,1)} %get-tuple-element.40.halo, bf16[1024,256]{1,0:T(8,128)(2,1)} %wv.1, ...), custom_call_target="tpu_custom_call" | custom-call | flops 4294967296 | bytes 20971520 | tf_op jit(solution)/shard_map/gate_conv/pallas_call | solution.py:440
  34.8 7.0 %all-to-all-start = ((f32[8,2,256]{2,1,0:T(2,128)}), f32[8,2,256]{2,1,0:T(2,128)S(1)}, u32[]{:S(2)}, u32[]{:S(2)}) async-start(f32[8,2,256]{2,1,0:T(2,128)} %get-tuple-element.41), calls=%async_computation | async-start | bytes 32768 | tf_op jit(solution)/shard_map/all_to_all | solution.py:361
  43.1 5.3 %all-to-all-done.stats = f32[8,2,256]{2,1,0:T(2,128)S(1)} async-done(((f32[8,2,256]{2,1,0:T(2,128)}), f32[8,2,256]{2,1,0:T(2,128)S(1)}, u32[]{:S(2)}, u32[]{:S(2)}) %all-to-all-start) | async-done | bytes 16416 | tf_op jit(solution)/shard_map/all_to_all | solution.py:361
  49.0 10.2 %swish_norm.1 = (bf16[4,1024,256]{2,1,0:T(8,128)(2,1)}, f32[4,1040,256]{2,1,0:T(8,128)}, f32[8,2,256]{2,1,0:T(2,128)}) custom-call(s32[2,4]{1,0:T(2,128)} %stack.35.meta, f32[1,1]{1,0:T(1,128)} %bitcast.1.count, f32[8,2,256]{2,1,0:T(2,128)} %copy-done.13, f32[2,256]{1,0:T(2,128)} %pad_maximum_fusion.5.affine, bf16[4,1024,1024]{2,1,0:T(8,128)(2,1)} %grads.5, ...), custom_call_target="tpu_custom_call" | custom-call | flops 2147483648 | bytes 20971520 | tf_op jit(solution)/shard_map/swish_norm/pallas_call | solution.py:471
  59.2 3.3 %all-to-all-start.1 = ((f32[8,2,256]{2,1,0:T(2,128)}), f32[8,2,256]{2,1,0:T(2,128)S(1)}, u32[]{:S(2)}, u32[]{:S(2)}) async-start(f32[8,2,256]{2,1,0:T(2,128)} %get-tuple-element.43), calls=%async_computation.1 | async-start | bytes 32768 | tf_op jit(solution)/shard_map/all_to_all | solution.py:361
  62.5 6.5 %all-to-all-done.1.sums = f32[8,2,256]{2,1,0:T(2,128)S(1)} async-done(((f32[8,2,256]{2,1,0:T(2,128)}), f32[8,2,256]{2,1,0:T(2,128)S(1)}, u32[]{:S(2)}, u32[]{:S(2)}) %all-to-all-start.1) | async-done | bytes 16416 | tf_op jit(solution)/shard_map/all_to_all | solution.py:361
  69.6 5.1 %back_conv.5 = (bf16[1024,512]{1,0:T(8,128)(2,1)}, f32[16,256]{1,0:T(8,128)}) custom-call(s32[2,4]{1,0:T(2,128)} %stack.35.meta, f32[1,1]{1,0:T(1,128)} %bitcast.1.count, f32[8,2,256]{2,1,0:T(2,128)} %copy-done.13, f32[8,2,256]{2,1,0:T(2,128)} %copy-done.14, f32[1,256]{1,0:T(1,128)} %bitcast.30, f32[4,1040,256]{2,1,0:T(8,128)} %get-tuple-element.44.gn, ...), custom_call_target="tpu_custom_call" | custom-call | flops 15728640 | bytes 4194304 | tf_op jit(solution)/shard_map/back_conv/pallas_call | solution.py:506
  75.6 5.0 %back_conv.4 = (bf16[1024,512]{1,0:T(8,128)(2,1)}, f32[16,256]{1,0:T(8,128)}) custom-call(s32[2,4]{1,0:T(2,128)} %stack.35.meta, f32[1,1]{1,0:T(1,128)} %bitcast.1.count, f32[8,2,256]{2,1,0:T(2,128)} %copy-done.13, f32[8,2,256]{2,1,0:T(2,128)} %copy-done.14, f32[1,256]{1,0:T(1,128)} %bitcast.31, f32[4,1040,256]{2,1,0:T(8,128)} %get-tuple-element.44.gn, ...), custom_call_target="tpu_custom_call" | custom-call | flops 15728640 | bytes 4194304 | tf_op jit(solution)/shard_map/back_conv/pallas_call | solution.py:506
  80.7 0.8 pad_maximum_fusion.1.w_own
  81.6 0.8 copy-done
  82.4 1.0 copy-done.6
  83.4 5.1 %partial_in.5 = (f32[256,1024]{1,0:T(8,128)}, bf16[256,1024]{1,0:T(8,128)(2,1)}) custom-call(bf16[1024,512]{1,0:T(8,128)(2,1)} %get-tuple-element.50.own.refs_1_, bf16[1024,512]{1,0:T(8,128)(2,1)} %copy-done.6, bf16[2,256,512]{2,1,0:T(8,128)(2,1)} %pad_maximum_fusion.1.w_own, bf16[2,256,512]{2,1,0:T(8,128)(2,1)} %copy-done, bf16[4,256,1024]{2,1,0:T(8,128)(2,1)} %pick.1.picked), custom_call_target="tpu_custom_call" | custom-call | flops 1073741824 | bytes 3670016 | tf_op jit(solution)/shard_map/partial_in/pallas_call | solution.py:534
  88.5 1.5 collective-permute-start.6
  90.0 5.1 %back_conv.7 = (bf16[1024,512]{1,0:T(8,128)(2,1)}, f32[16,256]{1,0:T(8,128)}) custom-call(s32[2,4]{1,0:T(2,128)} %stack.35.meta, f32[1,1]{1,0:T(1,128)} %bitcast.1.count, f32[8,2,256]{2,1,0:T(2,128)} %copy-done.13, f32[8,2,256]{2,1,0:T(2,128)} %copy-done.14, f32[1,256]{1,0:T(1,128)} %bitcast.32, f32[4,1040,256]{2,1,0:T(8,128)} %get-tuple-element.44.gn, ...), custom_call_target="tpu_custom_call" | custom-call | flops 15728640 | bytes 4194304 | tf_op jit(solution)/shard_map/back_conv/pallas_call | solution.py:506
  95.3 7.6 %collective-permute-done.6 = bf16[256,1024]{1,0:T(8,128)(2,1)S(1)} collective-permute-done((bf16[256,1024]{1,0:T(8,128)(2,1)}, bf16[256,1024]{1,0:T(8,128)(2,1)S(1)}, u32[]{:S(2)}, u32[]{:S(2)}) %collective-permute-start.6) | collective-permute-done | bytes 524320 | tf_op jit(solution)/shard_map/ppermute | solution.py:566
  103.0 1.0 add_convert_fusion.3
  103.9 3.5 %all-to-all-start.3 = ((bf16[8,32,1024]{2,1,0:T(8,128)(2,1)}), bf16[8,32,1024]{2,1,0:T(8,128)(2,1)S(1)}, u32[]{:S(2)}, u32[]{:S(2)}) async-start(bf16[8,32,1024]{2,1,0:T(8,128)(2,1)} %bitcast.10), calls=%async_computation.3 | async-start | bytes 1048576 | tf_op jit(solution)/shard_map/all_to_all | solution.py:361
  107.4 1.0 copy-done.8
  108.4 5.1 %partial_in.4 = (f32[256,1024]{1,0:T(8,128)}, bf16[256,1024]{1,0:T(8,128)(2,1)}) custom-call(bf16[1024,512]{1,0:T(8,128)(2,1)} %get-tuple-element.47.own.refs_0_, bf16[1024,512]{1,0:T(8,128)(2,1)} %copy-done.8, bf16[2,256,512]{2,1,0:T(8,128)(2,1)} %pad_maximum_fusion.1.w_own, bf16[2,256,512]{2,1,0:T(8,128)(2,1)} %copy-done, bf16[4,256,1024]{2,1,0:T(8,128)(2,1)} %pick.1.picked), custom_call_target="tpu_custom_call" | custom-call | flops 1073741824 | bytes 3670016 | tf_op jit(solution)/shard_map/partial_in/pallas_call | solution.py:534
  113.5 1.5 collective-permute-start.4
  115.0 5.1 %back_conv.6 = (bf16[1024,512]{1,0:T(8,128)(2,1)}, f32[16,256]{1,0:T(8,128)}) custom-call(s32[2,4]{1,0:T(2,128)} %stack.35.meta, f32[1,1]{1,0:T(1,128)} %bitcast.1.count, f32[8,2,256]{2,1,0:T(2,128)} %copy-done.13, f32[8,2,256]{2,1,0:T(2,128)} %copy-done.14, f32[1,256]{1,0:T(1,128)} %bitcast.33, f32[4,1040,256]{2,1,0:T(8,128)} %get-tuple-element.44.gn, ...), custom_call_target="tpu_custom_call" | custom-call | flops 15728640 | bytes 4194304 | tf_op jit(solution)/shard_map/back_conv/pallas_call | solution.py:506
  120.2 7.0 %collective-permute-done.4 = bf16[256,1024]{1,0:T(8,128)(2,1)S(1)} collective-permute-done((bf16[256,1024]{1,0:T(8,128)(2,1)}, bf16[256,1024]{1,0:T(8,128)(2,1)S(1)}, u32[]{:S(2)}, u32[]{:S(2)}) %collective-permute-start.4) | collective-permute-done | bytes 524320 | tf_op jit(solution)/shard_map/ppermute | solution.py:566
  127.2 1.0 add_convert_fusion.4
  128.2 5.6 %all-to-all-start.2 = ((bf16[8,32,1024]{2,1,0:T(8,128)(2,1)}), bf16[8,32,1024]{2,1,0:T(8,128)(2,1)S(1)}, u32[]{:S(2)}, u32[]{:S(2)}) async-start(bf16[8,32,1024]{2,1,0:T(8,128)(2,1)} %bitcast.9), calls=%async_computation.2 | async-start | bytes 1048576 | tf_op jit(solution)/shard_map/all_to_all | solution.py:361
  133.9 5.2 %partial_in.7 = (f32[256,1024]{1,0:T(8,128)}, bf16[256,1024]{1,0:T(8,128)(2,1)}) custom-call(bf16[1024,512]{1,0:T(8,128)(2,1)} %get-tuple-element.58.own.refs_3_, bf16[1024,512]{1,0:T(8,128)(2,1)} %collective-permute-done.9.sibling, bf16[2,256,512]{2,1,0:T(8,128)(2,1)} %pad_maximum_fusion.1.w_own, bf16[2,256,512]{2,1,0:T(8,128)(2,1)} %copy-done, ...), custom_call_target="tpu_custom_call" | custom-call | flops 1073741824 | bytes 3670016 | tf_op jit(solution)/shard_map/partial_in/pallas_call | solution.py:534
  139.1 1.5 collective-permute-start.10
  140.6 10.7 %collective-permute-done.10 = bf16[256,1024]{1,0:T(8,128)(2,1)S(1)} collective-permute-done((bf16[256,1024]{1,0:T(8,128)(2,1)}, bf16[256,1024]{1,0:T(8,128)(2,1)S(1)}, u32[]{:S(2)}, u32[]{:S(2)}) %collective-permute-start.10) | collective-permute-done | bytes 524320 | tf_op jit(solution)/shard_map/ppermute | solution.py:566
  151.3 2.2 add_convert_fusion.1
  153.5 5.7 %all-to-all-start.5 = ((bf16[8,32,1024]{2,1,0:T(8,128)(2,1)}), bf16[8,32,1024]{2,1,0:T(8,128)(2,1)S(1)}, u32[]{:S(2)}, u32[]{:S(2)}) async-start(bf16[8,32,1024]{2,1,0:T(8,128)(2,1)} %bitcast.12), calls=%async_computation.5 | async-start | bytes 1048576 | tf_op jit(solution)/shard_map/all_to_all | solution.py:361
  159.2 1.0 copy-done.7
  160.2 5.2 %partial_in.6 = (f32[256,1024]{1,0:T(8,128)}, bf16[256,1024]{1,0:T(8,128)(2,1)}) custom-call(bf16[1024,512]{1,0:T(8,128)(2,1)} %get-tuple-element.54.own.refs_2_, bf16[1024,512]{1,0:T(8,128)(2,1)} %copy-done.7, bf16[2,256,512]{2,1,0:T(8,128)(2,1)} %pad_maximum_fusion.1.w_own, bf16[2,256,512]{2,1,0:T(8,128)(2,1)} %copy-done, bf16[4,256,1024]{2,1,0:T(8,128)(2,1)} %pick.1.picked), custom_call_target="tpu_custom_call" | custom-call | flops 1073741824 | bytes 3670016 | tf_op jit(solution)/shard_map/partial_in/pallas_call | solution.py:534
  165.4 1.5 collective-permute-start.8
  166.9 13.6 %outer.1 = (bf16[4,800,128]{2,1,0:T(8,128)(2,1)}, bf16[4,800,128]{2,1,0:T(8,128)(2,1)}) custom-call(s32[1,1]{1,0:T(1,128)} %bitcast.13.parity, bf16[4,1024,1024]{2,1,0:T(8,128)(2,1)} %x.4, bf16[4,1024,1024]{2,1,0:T(8,128)(2,1)} %grads.5, bf16[4,1024,256]{2,1,0:T(8,128)(2,1)} %get-tuple-element.62.swished, bf16[1024,512]{1,0:T(8,128)(2,1)} %get-tuple-element.47.own.refs_0_, ...), custom_call_target="tpu_custom_call" | custom-call | flops 6442450944 | bytes 23068672 | tf_op jit(solution)/shard_map/outer/pallas_call | solution.py:572
  180.6 2.0 collective-permute-start.11
  182.6 0.9 add_convert_fusion.2
  183.5 4.5 %all-to-all-start.4 = ((bf16[8,32,1024]{2,1,0:T(8,128)(2,1)}), bf16[8,32,1024]{2,1,0:T(8,128)(2,1)S(1)}, u32[]{:S(2)}, u32[]{:S(2)}) async-start(bf16[8,32,1024]{2,1,0:T(8,128)(2,1)} %bitcast.11), calls=%async_computation.4 | async-start | bytes 1048576 | tf_op jit(solution)/shard_map/all_to_all | solution.py:361
  188.1 14.1 %collective-permute-done.11 = bf16[4,800,128]{2,1,0:T(8,128)(2,1)S(1)} collective-permute-done((bf16[4,800,128]{2,1,0:T(8,128)(2,1)}, bf16[4,800,128]{2,1,0:T(8,128)(2,1)S(1)}, u32[]{:S(2)}, u32[]{:S(2)}) %collective-permute-start.11) | collective-permute-done | bytes 819232 | tf_op jit(solution)/shard_map/ppermute | solution.py:586
  202.2 1.1 add_convert_fusion
  203.4 4.8 %all-to-all-start.6 = ((bf16[4,800,128]{2,1,0:T(8,128)(2,1)}), bf16[4,800,128]{2,1,0:T(8,128)(2,1)S(1)}, u32[]{:S(2)}, u32[]{:S(2)}) async-start(bf16[4,800,128]{2,1,0:T(8,128)(2,1)} %add_convert_fusion), calls=%async_computation.6 | async-start | bytes 1638400 | tf_op jit(solution)/shard_map/all_to_all | solution.py:588
  208.8 64.9 %place.1 = bf16[4,32,8192]{2,1,0:T(8,128)(2,1)} custom-call(bf16[8,32,1024]{2,1,0:T(8,128)(2,1)} %copy-done.3, bf16[8,32,1024]{2,1,0:T(8,128)(2,1)} %copy-done.2, bf16[8,32,1024]{2,1,0:T(8,128)(2,1)} %copy-done.5, bf16[8,32,1024]{2,1,0:T(8,128)(2,1)} %copy-done.4), custom_call_target="tpu_custom_call" | custom-call | bytes 4194304 | tf_op jit(solution)/shard_map/place/pallas_call | solution.py:600
  273.7 0.9 copy-done.1
  274.6 2.0 finish.1
  (68 shorter events, 5.1 us)
Async XLA Ops:
  1.6 15.9 %collective-permute-start = (bf16[4,8,2048]{2,1,0:T(8,128)(2,1)S(1)}, bf16[4,8,2048]{2,1,0:T(8,128)(2,1)S(1)}, u32[]{:S(2)}, u32[]{:S(2)}) collective-permute-start(bf16[4,8,2048]{2,1,0:T(8,128)(2,1)S(1)} %pad_maximum_fusion.3), channel_id=1, source_target_pairs={{0,4},{4,8},{8,12},{12,16},{16,20},{20,24},{24,28},{1,5},{5,9},{9,... | collective-permute-start | bytes 393224 | tf_op jit(solution)/shard_map/ppermute | solution.py:401
  6.5 11.0 %collective-permute-start.1 = (bf16[4,8,2048]{2,1,0:T(8,128)(2,1)S(1)}, bf16[4,8,2048]{2,1,0:T(8,128)(2,1)S(1)}, u32[]{:S(2)}, u32[]{:S(2)}) collective-permute-start(bf16[4,8,2048]{2,1,0:T(8,128)(2,1)S(1)} %pad_maximum_fusion.4), channel_id=1, source_target_pairs={{4,0},{8,4},{12,8},{16,12},{20,16},{24,20},{28,24},{5,1},{9,5},{13... | collective-permute-start | bytes 393224 | tf_op jit(solution)/shard_map/ppermute | solution.py:401
  18.3 23.6 %copy-start.18 = (f32[256]{0:T(256)S(1)}, f32[256]{0:T(256)}, u32[]{:S(2)}) copy-start(f32[256]{0:T(256)} %param.14) | copy-start | bytes 3076
  18.3 23.6 %copy-start.19 = (f32[256]{0:T(256)S(1)}, f32[256]{0:T(256)}, u32[]{:S(2)}) copy-start(f32[256]{0:T(256)} %param.15) | copy-start | bytes 3076
  34.8 13.5 %all-to-all-start = ((f32[8,2,256]{2,1,0:T(2,128)}), f32[8,2,256]{2,1,0:T(2,128)S(1)}, u32[]{:S(2)}, u32[]{:S(2)}) async-start(f32[8,2,256]{2,1,0:T(2,128)} %get-tuple-element.41), calls=%async_computation | async-start | bytes 32768 | tf_op jit(solution)/shard_map/all_to_all | solution.py:361
  48.4 0.6 copy-start.13
  59.2 9.9 %all-to-all-start.1 = ((f32[8,2,256]{2,1,0:T(2,128)}), f32[8,2,256]{2,1,0:T(2,128)S(1)}, u32[]{:S(2)}, u32[]{:S(2)}) async-start(f32[8,2,256]{2,1,0:T(2,128)} %get-tuple-element.43), calls=%async_computation.1 | async-start | bytes 32768 | tf_op jit(solution)/shard_map/all_to_all | solution.py:361
  69.0 0.6 copy-start.14
  69.6 5.2 %copy-start.16 = (bf16[1024,256]{1,0:T(8,128)(2,1)S(1)}, bf16[1024,256]{1,0:T(8,128)(2,1)}, u32[]{:S(2)}) copy-start(bf16[1024,256]{1,0:T(8,128)(2,1)} %wv.1) | copy-start | bytes 1572868
  69.6 5.2 %copy-start.17 = (bf16[1024,256]{1,0:T(8,128)(2,1)S(1)}, bf16[1024,256]{1,0:T(8,128)(2,1)}, u32[]{:S(2)}) copy-start(bf16[1024,256]{1,0:T(8,128)(2,1)} %wg.1) | copy-start | bytes 1572868
  74.7 6.9 %collective-permute-start.5 = (bf16[1024,512]{1,0:T(8,128)(2,1)}, bf16[1024,512]{1,0:T(8,128)(2,1)S(1)}, u32[]{:S(2)}, u32[]{:S(2)}) collective-permute-start(bf16[1024,512]{1,0:T(8,128)(2,1)} %get-tuple-element.50.own.refs_1_), channel_id=1, source_target_pairs={{0,1},{1,0},{2,3},{3,2},{4,5},{5,4},{6,7},{7,6},{8,9},{9,8},{10,11... | collective-permute-start | bytes 3145736 | tf_op jit(solution)/shard_map/ppermute | solution.py:533
  75.1 6.5 %collective-permute-start.3 = (bf16[2,256,512]{2,1,0:T(8,128)(2,1)S(1)}, bf16[2,256,512]{2,1,0:T(8,128)(2,1)S(1)}, u32[]{:S(2)}, u32[]{:S(2)}) collective-permute-start(bf16[2,256,512]{2,1,0:T(8,128)(2,1)S(1)} %pad_maximum_fusion.2), channel_id=1, source_target_pairs={{0,1},{1,0},{2,3},{3,2},{4,5},{5,4},{6,7},{7,6},{8,9},{9,8},{10,11... | collective-permute-start | bytes 1572872 | tf_op jit(solution)/shard_map/ppermute | solution.py:416
  80.6 26.9 %collective-permute-start.2 = (bf16[1024,512]{1,0:T(8,128)(2,1)}, bf16[1024,512]{1,0:T(8,128)(2,1)S(1)}, u32[]{:S(2)}, u32[]{:S(2)}) collective-permute-start(bf16[1024,512]{1,0:T(8,128)(2,1)} %get-tuple-element.47.own.refs_0_), channel_id=1, source_target_pairs={{0,1},{1,0},{2,3},{3,2},{4,5},{5,4},{6,7},{7,6},{8,9},{9,8},{10,11... | collective-permute-start | bytes 3145736 | tf_op jit(solution)/shard_map/ppermute | solution.py:533
  81.6 0.8 copy-start
  82.4 1.0 copy-start.6
  88.5 14.5 %collective-permute-start.6 = (bf16[256,1024]{1,0:T(8,128)(2,1)}, bf16[256,1024]{1,0:T(8,128)(2,1)S(1)}, u32[]{:S(2)}, u32[]{:S(2)}) collective-permute-start(bf16[256,1024]{1,0:T(8,128)(2,1)} %get-tuple-element.52), channel_id=1, source_target_pairs={{0,2},{1,3},{2,0},{3,1},{4,6},{5,7},{6,4},{7,5},{8,10},{9,11},{10,... | collective-permute-start | bytes 1572872 | tf_op jit(solution)/shard_map/ppermute | solution.py:566
  90.0 13.0 %copy-start.11 = (f32[256,1024]{1,0:T(8,128)S(1)}, f32[256,1024]{1,0:T(8,128)}, u32[]{:S(2)}) copy-start(f32[256,1024]{1,0:T(8,128)} %get-tuple-element.51) | copy-start | bytes 3145732
  95.1 38.8 %collective-permute-start.9 = (bf16[1024,512]{1,0:T(8,128)(2,1)}, bf16[1024,512]{1,0:T(8,128)(2,1)}, u32[]{:S(2)}, u32[]{:S(2)}) collective-permute-start(bf16[1024,512]{1,0:T(8,128)(2,1)} %get-tuple-element.58.own.refs_3_), channel_id=1, source_target_pairs={{0,1},{1,0},{2,3},{3,2},{4,5},{5,4},{6,7},{7,6},{8,9},{9,8},{10,11... | collective-permute-start | bytes 3145736 | tf_op jit(solution)/shard_map/ppermute | solution.py:533
  103.9 24.3 %all-to-all-start.3 = ((bf16[8,32,1024]{2,1,0:T(8,128)(2,1)}), bf16[8,32,1024]{2,1,0:T(8,128)(2,1)S(1)}, u32[]{:S(2)}, u32[]{:S(2)}) async-start(bf16[8,32,1024]{2,1,0:T(8,128)(2,1)} %bitcast.10), calls=%async_computation.3 | async-start | bytes 1048576 | tf_op jit(solution)/shard_map/all_to_all | solution.py:361
  107.4 1.0 copy-start.8
  113.5 13.7 %collective-permute-start.4 = (bf16[256,1024]{1,0:T(8,128)(2,1)}, bf16[256,1024]{1,0:T(8,128)(2,1)S(1)}, u32[]{:S(2)}, u32[]{:S(2)}) collective-permute-start(bf16[256,1024]{1,0:T(8,128)(2,1)} %get-tuple-element.49), channel_id=1, source_target_pairs={{0,2},{1,3},{2,0},{3,1},{4,6},{5,7},{6,4},{7,5},{8,10},{9,11},{10,... | collective-permute-start | bytes 1572872 | tf_op jit(solution)/shard_map/ppermute | solution.py:566
  115.0 12.2 %copy-start.10 = (f32[256,1024]{1,0:T(8,128)S(1)}, f32[256,1024]{1,0:T(8,128)}, u32[]{:S(2)}) copy-start(f32[256,1024]{1,0:T(8,128)} %get-tuple-element.48) | copy-start | bytes 3145732
  120.1 39.0 %collective-permute-start.7 = (bf16[1024,512]{1,0:T(8,128)(2,1)}, bf16[1024,512]{1,0:T(8,128)(2,1)S(1)}, u32[]{:S(2)}, u32[]{:S(2)}) collective-permute-start(bf16[1024,512]{1,0:T(8,128)(2,1)} %get-tuple-element.54.own.refs_2_), channel_id=1, source_target_pairs={{0,1},{1,0},{2,3},{3,2},{4,5},{5,4},{6,7},{7,6},{8,9},{9,8},{10,11... | collective-permute-start | bytes 3145736 | tf_op jit(solution)/shard_map/ppermute | solution.py:533
  128.2 10.8 %copy-start.2 = (bf16[8,32,1024]{2,1,0:T(8,128)(2,1)}, bf16[8,32,1024]{2,1,0:T(8,128)(2,1)S(1)}, u32[]{:S(2)}) copy-start(bf16[8,32,1024]{2,1,0:T(8,128)(2,1)S(1)} %all-to-all-done.3.refs_1_) | copy-start | bytes 1572868
  128.2 25.2 %all-to-all-start.2 = ((bf16[8,32,1024]{2,1,0:T(8,128)(2,1)}), bf16[8,32,1024]{2,1,0:T(8,128)(2,1)S(1)}, u32[]{:S(2)}, u32[]{:S(2)}) async-start(bf16[8,32,1024]{2,1,0:T(8,128)(2,1)} %bitcast.9), calls=%async_computation.2 | async-start | bytes 1048576 | tf_op jit(solution)/shard_map/all_to_all | solution.py:361
  139.1 12.2 %collective-permute-start.10 = (bf16[256,1024]{1,0:T(8,128)(2,1)}, bf16[256,1024]{1,0:T(8,128)(2,1)S(1)}, u32[]{:S(2)}, u32[]{:S(2)}) collective-permute-start(bf16[256,1024]{1,0:T(8,128)(2,1)} %get-tuple-element.60), channel_id=1, source_target_pairs={{0,2},{1,3},{2,0},{3,1},{4,6},{5,7},{6,4},{7,5},{8,10},{9,11},{10,... | collective-permute-start | bytes 1572872 | tf_op jit(solution)/shard_map/ppermute | solution.py:566
  153.5 11.9 %copy-start.3 = (bf16[8,32,1024]{2,1,0:T(8,128)(2,1)}, bf16[8,32,1024]{2,1,0:T(8,128)(2,1)S(1)}, u32[]{:S(2)}) copy-start(bf16[8,32,1024]{2,1,0:T(8,128)(2,1)S(1)} %all-to-all-done.2.refs_0_) | copy-start | bytes 1572868
  153.5 30.1 %all-to-all-start.5 = ((bf16[8,32,1024]{2,1,0:T(8,128)(2,1)}), bf16[8,32,1024]{2,1,0:T(8,128)(2,1)S(1)}, u32[]{:S(2)}, u32[]{:S(2)}) async-start(bf16[8,32,1024]{2,1,0:T(8,128)(2,1)} %bitcast.12), calls=%async_computation.5 | async-start | bytes 1048576 | tf_op jit(solution)/shard_map/all_to_all | solution.py:361
  159.2 1.0 copy-start.7
  165.4 17.2 %collective-permute-start.8 = (bf16[256,1024]{1,0:T(8,128)(2,1)}, bf16[256,1024]{1,0:T(8,128)(2,1)S(1)}, u32[]{:S(2)}, u32[]{:S(2)}) collective-permute-start(bf16[256,1024]{1,0:T(8,128)(2,1)} %get-tuple-element.56), channel_id=1, source_target_pairs={{0,2},{1,3},{2,0},{3,1},{4,6},{5,7},{6,4},{7,5},{8,10},{9,11},{10,... | collective-permute-start | bytes 1572872 | tf_op jit(solution)/shard_map/ppermute | solution.py:566
  166.9 15.7 %copy-start.9 = (f32[256,1024]{1,0:T(8,128)S(1)}, f32[256,1024]{1,0:T(8,128)}, u32[]{:S(2)}) copy-start(f32[256,1024]{1,0:T(8,128)} %get-tuple-element.55) | copy-start | bytes 3145732
  180.6 21.7 %copy-start.12 = (bf16[4,800,128]{2,1,0:T(8,128)(2,1)S(1)}, bf16[4,800,128]{2,1,0:T(8,128)(2,1)}, u32[]{:S(2)}) copy-start(bf16[4,800,128]{2,1,0:T(8,128)(2,1)} %get-tuple-element.67) | copy-start | bytes 2457604
  180.6 21.7 %collective-permute-start.11 = (bf16[4,800,128]{2,1,0:T(8,128)(2,1)}, bf16[4,800,128]{2,1,0:T(8,128)(2,1)S(1)}, u32[]{:S(2)}, u32[]{:S(2)}) collective-permute-start(bf16[4,800,128]{2,1,0:T(8,128)(2,1)} %get-tuple-element.68), channel_id=1, source_target_pairs={{0,4},{4,0},{8,12},{12,8},{16,20},{20,16},{24,28},{28,24},{1,5},{5... | collective-permute-start | bytes 2457608 | tf_op jit(solution)/shard_map/ppermute | solution.py:586
  183.5 19.8 %copy-start.4 = (bf16[8,32,1024]{2,1,0:T(8,128)(2,1)}, bf16[8,32,1024]{2,1,0:T(8,128)(2,1)S(1)}, u32[]{:S(2)}) copy-start(bf16[8,32,1024]{2,1,0:T(8,128)(2,1)S(1)} %all-to-all-done.5.refs_3_) | copy-start | bytes 1572868
  183.5 19.8 %all-to-all-start.4 = ((bf16[8,32,1024]{2,1,0:T(8,128)(2,1)}), bf16[8,32,1024]{2,1,0:T(8,128)(2,1)S(1)}, u32[]{:S(2)}, u32[]{:S(2)}) async-start(bf16[8,32,1024]{2,1,0:T(8,128)(2,1)} %bitcast.11), calls=%async_computation.4 | async-start | bytes 1048576 | tf_op jit(solution)/shard_map/all_to_all | solution.py:361
  188.1 20.1 %copy-start.15 = (f32[8,2,256]{2,1,0:T(2,128)S(1)}, f32[8,2,256]{2,1,0:T(2,128)}, u32[]{:S(2)}) copy-start(f32[8,2,256]{2,1,0:T(2,128)} %copy-done.14) | copy-start | bytes 49156
  203.4 5.4 %copy-start.5 = (bf16[8,32,1024]{2,1,0:T(8,128)(2,1)}, bf16[8,32,1024]{2,1,0:T(8,128)(2,1)S(1)}, u32[]{:S(2)}) copy-start(bf16[8,32,1024]{2,1,0:T(8,128)(2,1)S(1)} %all-to-all-done.4.refs_2_) | copy-start | bytes 1572868
  203.4 70.3 %all-to-all-start.6 = ((bf16[4,800,128]{2,1,0:T(8,128)(2,1)}), bf16[4,800,128]{2,1,0:T(8,128)(2,1)S(1)}, u32[]{:S(2)}, u32[]{:S(2)}) async-start(bf16[4,800,128]{2,1,0:T(8,128)(2,1)} %add_convert_fusion), calls=%async_computation.6 | async-start | bytes 1638400 | tf_op jit(solution)/shard_map/all_to_all | solution.py:588
  273.7 0.9 copy-start.1

commit v3 on v2

--- a/solution.py
+++ b/solution.py
@@ -67,7 +67,9 @@
         out[s] = sums
 
 
-def call(kernel, name, grid, in_specs, out_specs, out_shape, scratch, flops, moved, aliases=None):
+def call(
+    kernel, name, grid, in_specs, out_specs, out_shape, scratch, flops, moved, aliases=None, vmem=60
+):
     return pl.pallas_call(
         kernel,
         name=name,
@@ -78,12 +80,8 @@
         scratch_shapes=scratch,
         input_output_aliases=aliases or {},
         cost_estimate=pl.CostEstimate(flops=int(flops), bytes_accessed=int(moved), transcendentals=0),
-        compiler_params=pltpu.CompilerParams(vmem_limit_bytes=60 * 1024 * 1024),
+        compiler_params=pltpu.CompilerParams(vmem_limit_bytes=vmem * 1024 * 1024),
     )
-
-
-def pick_kernel(sel, grads, out):
-    out[0] = dot_nt(sel[...], grads[0]).astype(BF16)
 
 
 def gate_kernel(meta, x, halo, wv, wg, taps, vl_o, sg_o, conv_o, st_o, gp, st):
@@ -108,19 +106,22 @@
     put(EDGE, edge[:EDGE])
     put(2 * EDGE + frames, edge[EDGE:])
     put(3 * EDGE + frames, zero)
-    step = block_rows(frames, 256)
-
-    def project(i, carry):
-        base = pl.multiple_of(i * step, step)
-        xb = x[0, pl.ds(base, step), :]
-        v = dot(xb, wv[...])
-        s = sigmoid(dot(xb, wg[...]))
-        vl_o[0, pl.ds(base, step), :] = v
-        sg_o[0, pl.ds(base, step), :] = s
-        put(2 * EDGE + base, jnp.where(rows_of(step, base) < hi, v * s, 0.0))
+    step = block_rows(frames, 512)
+    small = block_rows(step, 64)
+    for base in range(0, frames, step):
+        xb = x[0, base : base + step, :]
+        vl_o[0, base : base + step, :] = dot(xb, wv[...])
+        sg_o[0, base : base + step, :] = dot(xb, wg[...])
+
+    def gating(i, carry):
+        base = pl.multiple_of(i * small, small)
+        v = vl_o[0, pl.ds(base, small), :]
+        s = sigmoid(sg_o[0, pl.ds(base, small), :])
+        sg_o[0, pl.ds(base, small), :] = s
+        put(2 * EDGE + base, jnp.where(rows_of(small, base) < hi, v * s, 0.0))
         return carry
 
-    lax.fori_loop(0, frames // step, project, 0)
+    lax.fori_loop(0, frames // small, gating, 0)
     span = frames + 2 * EDGE
     cb = block_rows(span, 104)
     kernel = taps.shape[0]
@@ -159,7 +160,8 @@
 
 
 def norm_kernel(
-    meta, count, stats, affine, grads, halo, wo, conv, swished_o, gn_o, st_o, st, ping, pong
+    meta, count, stats, affine, select, grads, halo, wo, conv,
+    swished_o, gn_o, picked_o, st_o, st, ping, pong
 ):
     r = pl.program_id(0)
     hi = meta[0, r]
@@ -183,7 +185,7 @@
     edge = dot(halo[0], wo[...])
     part(0, edge[:EDGE])
     part(frames + EDGE, edge[EDGE:])
-    step = block_rows(frames, 256)
+    step = block_rows(frames, 512)
     small = block_rows(step, 32)
     s1 = jnp.zeros((8, conv.shape[2]), F32)
     s2 = s1
@@ -193,6 +195,9 @@
         now = held[i % 2]
         if (i + 1) * step < frames:
             held[(i + 1) % 2][...] = dot(grads[0, (i + 1) * step : (i + 2) * step, :], wo[...])
+        picked_o[0, :, i * step : (i + 1) * step] = dot_nt(
+            select[...], grads[0, i * step : (i + 1) * step, :]
+        ).astype(BF16)
         for j in range(step // small):
             base = i * step + j * small
             unit, swished, gn = part(base + EDGE, now[j * small : (j + 1) * small, :])
@@ -273,30 +278,41 @@
 
 
 def partial_kernel(own, sibling, w_own, w_sibling, picked, mine, *others):
-    for d in range(w_own.shape[0]):
-        total = dot_nt(w_own[d], own[...]) + dot_nt(w_sibling[d], sibling[...])
-        if d == 0:
-            mine[...] = total + picked[0].astype(F32)
-        else:
-            others[d - 1][...] = total.astype(BF16)
-
-
-def outer_kernel(records, parity, x, grads, swished, *refs):
+    total = dot_nt(w_own[...], own[...]) + dot_nt(w_sibling[...], sibling[...])
+    rows = picked.shape[1]
+    mine[...] = total[:rows] + picked[0].astype(F32)
+    for d, other in enumerate(others):
+        other[...] = total[(d + 1) * rows : (d + 2) * rows].astype(BF16)
+
+
+def first_outer_kernel(grads, swished, out):
+    r = pl.program_id(0)
+    add = dot_tn(swished[0], grads[0])
+
+    @pl.when(r == 0)
+    def _():
+        out[...] = add
+
+    @pl.when(r > 0)
+    def _():
+        out[...] += add
+
+
+def outer_kernel(records, parity, x, w_out, *refs):
     lefts, taps = refs[:records], refs[records : 2 * records]
     keep, send, acc = refs[2 * records :]
-    width = swished.shape[2]
+    width = w_out.shape[0]
     shard = keep.shape[2]
     r = pl.program_id(0)
-
-    def add(rows, value, first):
-        acc[rows, :] = value if first else acc[rows, :] + value
-
     for i, left in enumerate(lefts):
 
         @pl.when(r == i)
         def _(i=i, left=left):
-            add(slice(0, 2 * width), dot_tn(left[...], x[0]), i == 0)
-            add(slice(2 * width, 3 * width), dot_tn(swished[0], grads[0]), i == 0)
+            add = dot_tn(left[...], x[0])
+            if i == 0:
+                acc[...] = add
+            else:
+                acc[...] += add
 
     @pl.when(r == records - 1)
     def _():
@@ -307,7 +323,8 @@
         def write(place, odd):
             for j in range(place.shape[0]):
                 at = (2 * j + odd) * shard
-                place[j, : 3 * width, :] = acc[:, at : at + shard].astype(BF16)
+                place[j, : 2 * width, :] = acc[:, at : at + shard].astype(BF16)
+                place[j, 2 * width : 3 * width, :] = w_out[:, at : at + shard].astype(BF16)
                 for q in range(width // shard):
                     row = 3 * width + 16 * q
                     place[j, row : row + 16, :] = tap_sums[:, q * shard : (q + 1) * shard].astype(
@@ -341,20 +358,11 @@
         taps[:, q * shard : (q + 1) * shard] = total(3 * width + 16 * q, 16)[:kernel]
 
 
-def place_kernel(*refs):
-    parts, out, sem = refs[:-2], refs[-2], refs[-1]
-    frames = parts[0].shape[2]
-    copies = [
-        pltpu.make_async_copy(
-            part.at[s], out.at[r, :, pl.ds(s * frames, frames)], sem.at[r, s]
-        )
-        for r, part in enumerate(parts)
-        for s in range(part.shape[0])
-    ]
-    for copy in copies:
-        copy.start()
-    for copy in copies:
-        copy.wait()
+def place_kernel(moved, *refs):
+    out = refs[-1]
+    frames = moved.shape[2]
+    for s in range(moved.shape[0]):
+        out[0, :, s * frames : (s + 1) * frames] = moved[s]
 
 
 def exchange(copies, axis):
@@ -409,7 +417,7 @@
             lax.dynamic_index_in_dim(both, ((chip_at + d) % chips) * 2 + core, 1, keepdims=False)
             for d in range(chips)
         ]
-        return jnp.stack(picks).reshape(chips, rows, 2 * width)
+        return jnp.stack(picks).reshape(chips * rows, 2 * width)
 
     swap = [(i, i ^ 1) for i in range(tps)]
     w_own = chosen(core_at)
@@ -424,18 +432,6 @@
     array_bytes = recs * frames * width * 4
     input_bytes = recs * frames * model * 2
     matmul = 2 * recs * frames * model * width
-
-    picked = call(
-        pick_kernel,
-        "pick",
-        (recs,),
-        [whole((rows, model)), per_record((frames, model))],
-        per_record((rows, frames)),
-        sds((recs, rows, frames), BF16),
-        [],
-        matmul,
-        input_bytes,
-    )(select, grad_out)
 
     vl, sg, conv, stats = call(
         gate_kernel,
@@ -453,22 +449,23 @@
             per_record((frames, width)),
             per_record((frames, width)),
             per_record((span, width)),
-            whole((seqs, 2, width)),
+            whole((1, 2, width)),
         ],
         [
             sds((recs, frames, width), F32),
             sds((recs, frames, width), F32),
             sds((recs, span, width), F32),
-            sds((seqs, 2, width), F32),
+            sds((1, 2, width), F32),
         ],
         [pltpu.VMEM((halves, frames + 4 * EDGE, LANES), F32), pltpu.VMEM((2, width), F32)],
         2 * matmul,
         input_bytes + 3 * array_bytes,
-    )(meta, normed, after(halo_x, picked), value_weight, gate_weight, depth_taps)
-    stats = exchange(stats, "seq")
+    )(meta, normed, halo_x, value_weight, gate_weight, depth_taps)
+    stats = lax.all_gather(stats, "seq", axis=0, tiled=True)
 
     chunk = block_rows(frames, 256)
-    swished, gn, sums = call(
+    half_rows = block_rows(frames, 512)
+    swished, gn, picked, sums = call(
         norm_kernel,
         "swish_norm",
         (recs,),
@@ -477,25 +474,53 @@
             smem(),
             whole((seqs, 2, width)),
             whole((2, width)),
+            whole((rows, model)),
             per_record((frames, model)),
             per_record((2 * EDGE, model)),
             whole((model, width)),
             per_record((span, width)),
         ],
-        [per_record((frames, width)), per_record((span, width)), whole((seqs, 2, width))],
+        [
+            per_record((frames, width)),
+            per_record((span, width)),
+            per_record((rows, frames)),
+            whole((seqs, 2, width)),
+        ],
         [
             sds((recs, frames, width), BF16),
             sds((recs, span, width), F32),
+            sds((recs, rows, frames), BF16),
             sds((seqs, 2, width), F32),
         ],
         [
             pltpu.VMEM((2, width), F32),
-            pltpu.VMEM((chunk, width), F32),
-            pltpu.VMEM((chunk, width), F32),
+            pltpu.VMEM((block_rows(frames, 512), width), F32),
+            pltpu.VMEM((block_rows(frames, 512), width), F32),
         ],
+        2 * matmul,
+        input_bytes + 3 * array_bytes,
+    )(
+        meta,
+        counts,
+        stats,
+        jnp.stack([norm_gain, norm_shift]),
+        select,
+        grad_out,
+        halo_g,
+        out_weight,
+        conv,
+    )
+    w_out = call(
+        first_outer_kernel,
+        "outer_w_out",
+        (recs,),
+        [per_record((frames, model)), per_record((frames, width))],
+        whole((width, model)),
+        sds((width, model), F32),
+        [],
         matmul,
-        input_bytes + 3 * array_bytes,
-    )(meta, counts, stats, jnp.stack([norm_gain, norm_shift]), grad_out, halo_g, out_weight, conv)
+        input_bytes,
+    )(grad_out, swished)
     sums = exchange(sums, "seq")
     grad_shift, grad_gain = jnp.sum(sums, axis=0)
 
@@ -534,58 +559,67 @@
         return call(
             partial_kernel,
             "partial_in",
-            (frames // chunk,),
+            (frames // half_rows,),
             [
-                pl.BlockSpec((chunk, 2 * width), lambda i: (i, 0)),
-                pl.BlockSpec((chunk, 2 * width), lambda i: (i, 0)),
-                whole((chips, rows, 2 * width)),
-                whole((chips, rows, 2 * width)),
-                pl.BlockSpec((1, rows, chunk), lambda i: (r, 0, i)),
+                pl.BlockSpec((half_rows, 2 * width), lambda i: (i, 0)),
+                pl.BlockSpec((half_rows, 2 * width), lambda i: (i, 0)),
+                whole((chips * rows, 2 * width)),
+                whole((chips * rows, 2 * width)),
+                pl.BlockSpec((1, rows, half_rows), lambda i: (r, 0, i)),
             ],
-            [pl.BlockSpec((rows, chunk), lambda i: (0, i))] * chips,
+            [pl.BlockSpec((rows, half_rows), lambda i: (0, i))] * chips,
             [sds((rows, frames), F32)] + [sds((rows, frames), BF16)] * (chips - 1),
             [],
             2 * matmul // recs,
             8 * frames * width + 6 * rows * frames,
+            vmem=20,
         )(mine, sibling, w_own, w_sibling, picked)
 
-    grads, tap_parts, parts = [], [], []
+    grads, tap_parts, parts, moved = [], [], [], []
+
+    def deliver(r, *earlier):
+        total = after(parts[r][0], *earlier)
+        for d in range(1, chips):
+            send = [(i, ((i // 2 + d) % chips) * 2 + i % 2) for i in range(tps)]
+            total = total + lax.ppermute(parts[r][d], "tp", send).astype(F32)
+        own = total.astype(BF16).reshape(seqs, piece, frames)
+        moved.append(exchange(own, "seq"))
+        return own
+
     for r in range(recs):
         mine, tap_part = back(r, parts[r - 2] if r > 1 else ())
         grads.append(mine)
         tap_parts.append(tap_part)
         if r > 0:
             parts.append(partials(r - 1, grads[r - 1]))
-    parts.append(partials(recs - 1, grads[recs - 1]))
-
-    moved = []
-    for r in range(recs):
-        total = parts[r][0]
-        for d in range(1, chips):
-            send = [(i, ((i // 2 + d) % chips) * 2 + i % 2) for i in range(tps)]
-            total = total + lax.ppermute(parts[r][d], "tp", send).astype(F32)
-        own = total.astype(BF16).reshape(seqs, piece, frames)
-        moved.append(exchange(own, "seq"))
+    owns = [deliver(0, *parts[recs - 2])]
+    parts.append(partials(recs - 1, after(grads[recs - 1], owns[0])))
+    owns.append(deliver(1, *parts[recs - 1]))
 
     slots = 3 * width + 16 * (width // shard)
     half = sds((seqs // 2, slots, shard), BF16)
     keep, send = call(
         functools.partial(outer_kernel, recs),
-        "outer",
+        "outer_w_in",
         (recs,),
-        [smem(), per_record((frames, model)), per_record((frames, model)), per_record((frames, width))]
+        [smem(), per_record((frames, model)), whole((width, model))]
         + [whole((frames, 2 * width))] * recs
         + [whole((16, width))] * recs,
         [whole(half.shape)] * 2,
         [half] * 2,
-        [pltpu.VMEM((3 * width, model), F32)],
-        3 * matmul,
-        2 * input_bytes + 6 * recs * frames * width,
-    )(parity, after(normed, *parts[-1]), grad_out, swished, *grads, *tap_parts)
+        [pltpu.VMEM((2 * width, model), F32)],
+        2 * matmul,
+        input_bytes + 4 * recs * frames * width,
+    )(parity, after(normed, owns[1]), w_out, *grads, *tap_parts)
     pairs = [(i, i ^ 1) for i in range(seqs)]
-    paired = (keep.astype(F32) + lax.ppermute(send, "seq", pairs).astype(F32)).astype(BF16)
+    others = lax.ppermute(send, "seq", pairs)
+    for r in range(2, recs):
+        owns.append(deliver(r, keep, owns[-1]))
+    paired = (after(keep, owns[-2]).astype(F32) + others.astype(F32)).astype(BF16)
     same = [[i for i in range(seqs) if i % 2 == odd] for odd in range(2)]
-    got = lax.all_to_all(paired, "seq", 0, 0, axis_index_groups=same, tiled=True)
+    got = lax.all_to_all(
+        after(paired, owns[-1]), "seq", 0, 0, axis_index_groups=same, tiled=True
+    )
     w_value, w_gate, w_out, grad_taps = call(
         functools.partial(finish_kernel, kernel),
         "finish",
@@ -596,18 +630,26 @@
         [],
         0,
         8 * seqs * slots * shard,
+        vmem=20,
     )(got)
-    grad_in = call(
-        place_kernel,
-        "place",
-        (1,),
-        [anywhere()] * recs,
-        anywhere(),
-        sds((recs, piece, seqs * frames), BF16),
-        [pltpu.SemaphoreType.DMA((recs, seqs))],
-        0,
-        4 * recs * piece * seqs * frames,
-    )(*moved)
+    grad_in = ()
+    for r in range(recs):
+        grad_in = (
+            call(
+                place_kernel,
+                "place",
+                (1,),
+                [whole((seqs, piece, frames))] + [anywhere()] * len(grad_in),
+                pl.BlockSpec((1, piece, seqs * frames), lambda i, r=r: (r, 0, 0)),
+                sds((recs, piece, seqs * frames), BF16),
+                [],
+                0,
+                4 * piece * seqs * frames,
+                {1: 0} if grad_in else None,
+                vmem=20,
+            )(moved[r], *grad_in),
+        )
+    (grad_in,) = grad_in
     return (grad_in, w_value, w_gate, w_out, grad_taps, grad_gain, grad_shift)
 
 

time: 278 us -> 234 us (0.84)
  Pallas kernels: 155 us -> 82.3 us
  blocking collectives: 0 us -> 48.4 us
  starting transfers between devices: 49.7 us -> 34.7 us
  waiting for transfers between devices: 51.4 us -> 42.3 us
    pallas_call x7 -> x10, Pallas kernels: 106 us -> 33.8 us  [the longest x4 12.2 us: partials(): call(partial_kernel, 'partial_in', (frames // half_rows,), [pl.BlockSpec(...]
    all_gather x0 -> x1, blocking collectives: none -> 28.5 us  [per_device(): stats = lax.all_gather(stats, 'seq', axis=0, tiled=True)]
    all_to_all x0 -> x1, blocking collectives: none -> 19.9 us  [exchange(): return lax.all_to_all(copies, axis, 0, 0, tiled=True)]
    ppermute x5, waiting for transfers between devices: 39.5 us -> 20.2 us  [the longest x4 10.5 us: deliver(): total = total + lax.ppermute(parts[r][d], 'tp', send).astype(F32)]
    all_to_all x1, waiting for transfers between devices: 0.01 us -> 13.9 us  [per_device(): lax.all_to_all(after(paired, owns[-1]), 'seq', 0, 0, axis_index_groups=sa...]
    all_to_all x6 -> x4, starting transfers between devices: 29.7 us -> 16.9 us  [exchange(): return lax.all_to_all(copies, axis, 0, 0, tiled=True)]
    all_to_all x6 -> x4, waiting for transfers between devices: 11.8 us -> 7.5 us  [exchange(): return lax.all_to_all(copies, axis, 0, 0, tiled=True)]
    unnamed x41 -> x39, local copies, waits for them, and re-layouts: 5.92 us -> 7.33 us
  transfers between devices with their start and end apart: 19 -> 17, of which waited for: 6 -> 7; matrix products, arithmetic and copies ran while one was open for 4% -> 5% of each run, Pallas kernels for 44% -> 21%
where the time goes in v3:
time: 234 us; the launch traced here: 232 us
  Pallas kernels  82.3 us (35%)
  blocking collectives  48.4 us (21%)
  waiting for transfers between devices  42.3 us (18%)
  starting transfers between devices  34.7 us (15%)
  other arithmetic  12.7 us (5%)
  local copies, waits for them, and re-layouts  10.3 us (4%)
    all_gather x1, blocking collectives, per_device(): stats = lax.all_gather(stats, 'seq', axis=0, tiled=True)  28.5 us
    pallas_call x4, Pallas kernels, back(): call(functools.partial(back_kernel, r), 'back_conv', (frames // chunk,),...  20.3 us
    all_to_all x1, blocking collectives, exchange(): return lax.all_to_all(copies, axis, 0, 0, tiled=True)  19.9 us
    all_to_all x4, starting transfers between devices, exchange(): return lax.all_to_all(copies, axis, 0, 0, tiled=True)  16.9 us
    pallas_call x1, Pallas kernels, per_device(): call(gate_kernel, 'gate_conv', (recs,), [smem(), per_record((frames, mode...  15.2 us
    all_to_all x1, waiting for transfers between devices, per_device(): lax.all_to_all(after(paired, owns[-1]), 'seq', 0, 0, axis_index_groups=sa...  13.9 us
    pallas_call x4, Pallas kernels, partials(): call(partial_kernel, 'partial_in', (frames // half_rows,), [pl.BlockSpec(...  12.2 us
    pallas_call x1, Pallas kernels, per_device(): call(norm_kernel, 'swish_norm', (recs,), [smem(), smem(), whole((seqs, 2,...  12.1 us
  transfers between devices with their start and end apart: 17, of which 7 were waited for; matrix products, arithmetic and copies ran while one was open for 5% of the time, Pallas kernels for 21%

profile of v3, /device:TPU:0, one launch (start us, length us, event | category | flops | bytes accessed | tf_op | source)
XLA Modules:
  0.0 232.3 jit_solution(11647852373882276114)
XLA Ops:
  0.6 1.0 fusion.1
  1.6 4.9 %collective-permute-start = (bf16[4,8,2048]{2,1,0:T(8,128)(2,1)S(1)}, bf16[4,8,2048]{2,1,0:T(8,128)(2,1)S(1)}, u32[]{:S(2)}, u32[]{:S(2)}) collective-permute-start(bf16[4,8,2048]{2,1,0:T(8,128)(2,1)S(1)} %pad_maximum_fusion.3), channel_id=1, source_target_pairs={{0,4},{4,8},{8,12},{12,16},{16,20},{20,24},{24,28},{1,5},{5,9},{9,... | collective-permute-start | bytes 393224 | tf_op jit(solution)/shard_map/ppermute | solution.py:409
  6.5 1.3 collective-permute-start.1
  8.0 1.0 fusion.select
  9.0 1.3 fusion.5
  11.5 1.3 pad_maximum_fusion.5.affine
  14.1 15.2 %gate_conv.1 = (f32[4,1024,256]{2,1,0:T(8,128)}, f32[4,1024,256]{2,1,0:T(8,128)}, f32[4,1040,256]{2,1,0:T(8,128)}, f32[1,2,256]{2,1,0:T(2,128)}) custom-call(s32[2,4]{1,0:T(2,128)} %stack.35.meta, bf16[4,1024,1024]{2,1,0:T(8,128)(2,1)} %x.4, bf16[4,16,1024]{2,1,0:T(8,128)(2,1)} %get-tuple-element.96.halo, bf16[1024,256]{1,0:T(8,128)(2,1)} %wv.1, ...), custom_call_target="tpu_custom_call" | custom-call | flops 4294967296 | bytes 20971520 | tf_op jit(solution)/shard_map/gate_conv/pallas_call | solution.py:436
  29.3 28.5 %all_gather.3.stats = f32[8,2,256]{2,1,0:T(2,128)} all-gather(f32[1,2,256]{2,1,0:T(2,128)} %get-tuple-element.47), channel_id=1, replica_groups=mesh['seq'=8,'tp'=4] {'seq'}, dimensions={0}, use_global_device_ids=true | all-gather | bytes 18432 | tf_op jit(solution)/shard_map/all_gather | solution.py:464
  57.8 12.1 %swish_norm.1 = (bf16[4,1024,256]{2,1,0:T(8,128)(2,1)}, f32[4,1040,256]{2,1,0:T(8,128)}, bf16[4,256,1024]{2,1,0:T(8,128)(2,1)}, f32[8,2,256]{2,1,0:T(2,128)}) custom-call(s32[2,4]{1,0:T(2,128)} %stack.35.meta, f32[1,1]{1,0:T(1,128)} %bitcast.1.count, f32[8,2,256]{2,1,0:T(2,128)} %all_gather.3.stats, f32[2,256]{1,0:T(2,128)} %pad_maximum_fusion.5.affine, ...), custom_call_target="tpu_custom_call" | custom-call | flops 4294967296 | bytes 20971520 | tf_op jit(solution)/shard_map/swish_norm/pallas_call | solution.py:468
  69.9 3.3 %all-to-all-start = ((f32[8,2,256]{2,1,0:T(2,128)}), f32[8,2,256]{2,1,0:T(2,128)S(1)}, u32[]{:S(2)}, u32[]{:S(2)}) async-start(f32[8,2,256]{2,1,0:T(2,128)} %get-tuple-element.49), calls=%async_computation | async-start | bytes 32768 | tf_op jit(solution)/shard_map/all_to_all | solution.py:369
  73.3 6.5 %all-to-all-done.sums = f32[8,2,256]{2,1,0:T(2,128)S(1)} async-done(((f32[8,2,256]{2,1,0:T(2,128)}), f32[8,2,256]{2,1,0:T(2,128)S(1)}, u32[]{:S(2)}, u32[]{:S(2)}) %all-to-all-start) | async-done | bytes 16416 | tf_op jit(solution)/shard_map/all_to_all | solution.py:369
  80.4 5.1 %back_conv.6 = (bf16[1024,512]{1,0:T(8,128)(2,1)}, f32[16,256]{1,0:T(8,128)}) custom-call(s32[2,4]{1,0:T(2,128)} %stack.35.meta, f32[1,1]{1,0:T(1,128)} %bitcast.1.count, f32[8,2,256]{2,1,0:T(2,128)} %all_gather.3.stats, f32[8,2,256]{2,1,0:T(2,128)} %copy-done.15, f32[1,256]{1,0:T(1,128)} %bitcast.32, f32[4,1040,256]{2,1,0:T(8,128)} %get-tuple-element.50.gn, ...), custom_call_target="tpu_custom_call" | custom-call | flops 15728640 | bytes 4194304 | tf_op jit(solution)/shard_map/back_conv/pallas_call | solution.py:531
  86.4 5.2 %back_conv.4 = (bf16[1024,512]{1,0:T(8,128)(2,1)}, f32[16,256]{1,0:T(8,128)}) custom-call(s32[2,4]{1,0:T(2,128)} %stack.35.meta, f32[1,1]{1,0:T(1,128)} %bitcast.1.count, f32[8,2,256]{2,1,0:T(2,128)} %all_gather.3.stats, f32[8,2,256]{2,1,0:T(2,128)} %copy-done.15, f32[1,256]{1,0:T(1,128)} %bitcast.33, f32[4,1040,256]{2,1,0:T(8,128)} %get-tuple-element.50.gn, ...), custom_call_target="tpu_custom_call" | custom-call | flops 15728640 | bytes 4194304 | tf_op jit(solution)/shard_map/back_conv/pallas_call | solution.py:531
  91.8 1.2 copy-done.1
  93.0 2.6 %partial_in.5 = (f32[256,1024]{1,0:T(8,128)S(1)}, bf16[256,1024]{1,0:T(8,128)(2,1)S(1)}) custom-call(bf16[1024,512]{1,0:T(8,128)(2,1)S(1)} %copy-done.1, bf16[1024,512]{1,0:T(8,128)(2,1)} %collective-permute-done.4.sibling, bf16[512,512]{1,0:T(8,128)(2,1)S(1)} %bitcast.23, bf16[512,512]{1,0:T(8,128)(2,1)S(1)} %collective-permute-done.3.w_sibling, ...), custom_call_target="tpu_custom_call" | custom-call | flops 1073741824 | bytes 3670016 | tf_op jit(solution)/shard_map/partial_in/pallas_call | solution.py:559
  95.6 1.0 copy-done.10
  96.6 5.0 %back_conv.7 = (bf16[1024,512]{1,0:T(8,128)(2,1)}, f32[16,256]{1,0:T(8,128)}) custom-call(s32[2,4]{1,0:T(2,128)} %stack.35.meta, f32[1,1]{1,0:T(1,128)} %bitcast.1.count, f32[8,2,256]{2,1,0:T(2,128)} %all_gather.3.stats, f32[8,2,256]{2,1,0:T(2,128)} %copy-done.15, f32[1,256]{1,0:T(1,128)} %bitcast.34, f32[4,1040,256]{2,1,0:T(8,128)} %get-tuple-element.50.gn, ...), custom_call_target="tpu_custom_call" | custom-call | flops 15728640 | bytes 4194304 | tf_op jit(solution)/shard_map/back_conv/pallas_call | solution.py:531
  102.1 1.5 collective-permute-start.6
  103.6 1.2 copy-done.2
  104.8 3.3 %partial_in.4 = (f32[256,1024]{1,0:T(8,128)S(1)}, bf16[256,1024]{1,0:T(8,128)(2,1)}) custom-call(bf16[1024,512]{1,0:T(8,128)(2,1)S(1)} %copy-done.2, bf16[1024,512]{1,0:T(8,128)(2,1)} %collective-permute-done.2.sibling, bf16[512,512]{1,0:T(8,128)(2,1)S(1)} %bitcast.24, bf16[512,512]{1,0:T(8,128)(2,1)S(1)} %collective-permute-done.3.w_sibling, ...), custom_call_target="tpu_custom_call" | custom-call | flops 1073741824 | bytes 3670016 | tf_op jit(solution)/shard_map/partial_in/pallas_call | solution.py:559
  108.1 1.0 copy-done.6
  109.1 5.0 %back_conv.5 = (bf16[1024,512]{1,0:T(8,128)(2,1)}, f32[16,256]{1,0:T(8,128)}) custom-call(s32[2,4]{1,0:T(2,128)} %stack.35.meta, f32[1,1]{1,0:T(1,128)} %bitcast.1.count, f32[8,2,256]{2,1,0:T(2,128)} %all_gather.3.stats, f32[8,2,256]{2,1,0:T(2,128)} %copy-done.15, f32[1,256]{1,0:T(1,128)} %bitcast.35, f32[4,1040,256]{2,1,0:T(8,128)} %get-tuple-element.50.gn, ...), custom_call_target="tpu_custom_call" | custom-call | flops 15728640 | bytes 4194304 | tf_op jit(solution)/shard_map/back_conv/pallas_call | solution.py:531
  114.1 1.2 copy-done.3
  115.4 3.4 %partial_in.6 = (f32[256,1024]{1,0:T(8,128)S(1)}, bf16[256,1024]{1,0:T(8,128)(2,1)}) custom-call(bf16[1024,512]{1,0:T(8,128)(2,1)S(1)} %copy-done.3, bf16[1024,512]{1,0:T(8,128)(2,1)} %collective-permute-done.5.sibling, bf16[512,512]{1,0:T(8,128)(2,1)S(1)} %bitcast.25, bf16[512,512]{1,0:T(8,128)(2,1)S(1)} %collective-permute-done.3.w_sibling, ...), custom_call_target="tpu_custom_call" | custom-call | flops 1073741824 | bytes 3670016 | tf_op jit(solution)/shard_map/partial_in/pallas_call | solution.py:559
  118.8 1.0 copy-done.4
  119.8 2.0 add_convert_fusion.4
  122.3 7.0 %outer_w_out.1.w_out = f32[256,1024]{1,0:T(8,128)} custom-call(bf16[4,1024,1024]{2,1,0:T(8,128)(2,1)} %grads.3, bf16[4,1024,256]{2,1,0:T(8,128)(2,1)} %get-tuple-element.72.swished), custom_call_target="tpu_custom_call" | custom-call | flops 2147483648 | bytes 8388608 | tf_op jit(solution)/shard_map/outer_w_out/pallas_call | solution.py:513
  129.3 1.5 collective-permute-start.9
  130.8 4.3 %all-to-all-start.4 = ((bf16[8,32,1024]{2,1,0:T(8,128)(2,1)}), bf16[8,32,1024]{2,1,0:T(8,128)(2,1)}, u32[]{:S(2)}, u32[]{:S(2)}) async-start(bf16[8,32,1024]{2,1,0:T(8,128)(2,1)} %bitcast.28), calls=%async_computation.4 | async-start | bytes 1048576 | tf_op jit(solution)/shard_map/all_to_all | solution.py:369
  135.1 2.9 %partial_in.7 = (f32[256,1024]{1,0:T(8,128)S(1)}, bf16[256,1024]{1,0:T(8,128)(2,1)S(1)}) custom-call(bf16[1024,512]{1,0:T(8,128)(2,1)} %get-tuple-element.67.own.refs_3_, bf16[1024,512]{1,0:T(8,128)(2,1)} %collective-permute-done.7.sibling, bf16[512,512]{1,0:T(8,128)(2,1)S(1)} %bitcast.26, bf16[512,512]{1,0:T(8,128)(2,1)S(1)} %collective-permute-done.3.w_sibling, ...), custom_call_target="tpu_custom_call" | custom-call | flops 1073741824 | bytes 3670016 | tf_op jit(solution)/shard_map/partial_in/pallas_call | solution.py:559
  138.1 2.4 %add_convert_fusion.3 = bf16[256,1024]{1,0:T(8,128)(2,1)} fusion(f32[256,1024]{1,0:T(8,128)S(1)} %copy-done.7, bf16[256,1024]{1,0:T(8,128)(2,1)} %collective-permute-done.8), kind=kLoop, calls=%fused_computation.4 | loop fusion | flops 786432 | bytes 2097152 | tf_op jit(solution)/shard_map/convert_element_type | solution.py:585
  140.5 10.3 %outer_w_in.1 = (bf16[4,800,128]{2,1,0:T(8,128)(2,1)}, bf16[4,800,128]{2,1,0:T(8,128)(2,1)}) custom-call(s32[1,1]{1,0:T(1,128)} %bitcast.12.parity, bf16[4,1024,1024]{2,1,0:T(8,128)(2,1)} %x.4, f32[256,1024]{1,0:T(8,128)} %outer_w_out.1.w_out, bf16[1024,512]{1,0:T(8,128)(2,1)} %get-tuple-element.59.own.refs_0_, ...), custom_call_target="tpu_custom_call" | custom-call | flops 4294967296 | bytes 12582912 | tf_op jit(solution)/shard_map/outer_w_in/pallas_call | solution.py:601
  150.8 1.3 add_convert_fusion.2
  152.1 19.9 %all_to_all.30.moved = bf16[8,32,1024]{2,1,0:T(8,128)(2,1)S(1)} all-to-all(bf16[8,32,1024]{2,1,0:T(8,128)(2,1)S(1)} %bitcast.29), channel_id=1, replica_groups=mesh['seq'=8,'tp'=4] {'seq'}, dimensions={0} | all-to-all | bytes 1048576 | tf_op jit(solution)/shard_map/all_to_all | solution.py:369
  172.0 3.7 %all-to-all-start.3 = ((bf16[8,32,1024]{2,1,0:T(8,128)(2,1)}), bf16[8,32,1024]{2,1,0:T(8,128)(2,1)S(1)}, u32[]{:S(2)}, u32[]{:S(2)}) async-start(bf16[8,32,1024]{2,1,0:T(8,128)(2,1)} %bitcast.13), calls=%async_computation.3 | async-start | bytes 1048576 | tf_op jit(solution)/shard_map/all_to_all | solution.py:369
  176.3 2.0 collective-permute-start.11
  178.3 10.5 %collective-permute-done.10 = bf16[256,1024]{1,0:T(8,128)(2,1)S(1)} collective-permute-done((bf16[256,1024]{1,0:T(8,128)(2,1)S(1)}, bf16[256,1024]{1,0:T(8,128)(2,1)S(1)}, u32[]{:S(2)}, u32[]{:S(2)}) %collective-permute-start.10) | collective-permute-done | bytes 524320 | tf_op jit(solution)/shard_map/ppermute | solution.py:584
  188.8 0.9 add_convert_fusion.1
  189.9 5.5 %all-to-all-start.1 = ((bf16[8,32,1024]{2,1,0:T(8,128)(2,1)}), bf16[8,32,1024]{2,1,0:T(8,128)(2,1)S(1)}, u32[]{:S(2)}, u32[]{:S(2)}) async-start(bf16[8,32,1024]{2,1,0:T(8,128)(2,1)} %bitcast.15), calls=%async_computation.1 | async-start | bytes 1048576 | tf_op jit(solution)/shard_map/all_to_all | solution.py:369
  195.4 9.7 %collective-permute-done.11 = bf16[4,800,128]{2,1,0:T(8,128)(2,1)} collective-permute-done((bf16[4,800,128]{2,1,0:T(8,128)(2,1)}, bf16[4,800,128]{2,1,0:T(8,128)(2,1)}, u32[]{:S(2)}, u32[]{:S(2)}) %collective-permute-start.11) | collective-permute-done | bytes 819232 | tf_op jit(solution)/shard_map/ppermute | solution.py:615
  205.1 2.2 add_convert_fusion
  207.4 0.8 all-to-all-done.1.moved
  208.2 4.5 %all-to-all-start.5 = ((bf16[4,800,128]{2,1,0:T(8,128)(2,1)}), bf16[4,800,128]{2,1,0:T(8,128)(2,1)S(1)}, u32[]{:S(2)}, u32[]{:S(2)}) async-start(bf16[4,800,128]{2,1,0:T(8,128)(2,1)} %add_convert_fusion), calls=%async_computation.5 | async-start | bytes 1638400 | tf_op jit(solution)/shard_map/all_to_all | solution.py:620
  213.3 1.9 place.4.refs_0_
  215.1 0.8 place.5.refs_0_
  216.0 0.8 place.6.refs_0_
  217.6 13.9 %all-to-all-done.5.got = bf16[4,800,128]{2,1,0:T(8,128)(2,1)S(1)} async-done(((bf16[4,800,128]{2,1,0:T(8,128)(2,1)}), bf16[4,800,128]{2,1,0:T(8,128)(2,1)S(1)}, u32[]{:S(2)}, u32[]{:S(2)}) %all-to-all-start.5) | async-done | bytes 819232 | tf_op jit(solution)/shard_map/all_to_all | solution.py:620
  231.5 0.8 finish.1
  (67 shorter events, 6.9 us)
Async XLA Ops:
  1.6 11.1 %collective-permute-start = (bf16[4,8,2048]{2,1,0:T(8,128)(2,1)S(1)}, bf16[4,8,2048]{2,1,0:T(8,128)(2,1)S(1)}, u32[]{:S(2)}, u32[]{:S(2)}) collective-permute-start(bf16[4,8,2048]{2,1,0:T(8,128)(2,1)S(1)} %pad_maximum_fusion.3), channel_id=1, source_target_pairs={{0,4},{4,8},{8,12},{12,16},{16,20},{20,24},{24,28},{1,5},{5,9},{9,... | collective-permute-start | bytes 393224 | tf_op jit(solution)/shard_map/ppermute | solution.py:409
  6.5 6.9 %collective-permute-start.1 = (bf16[4,8,2048]{2,1,0:T(8,128)(2,1)S(1)}, bf16[4,8,2048]{2,1,0:T(8,128)(2,1)S(1)}, u32[]{:S(2)}, u32[]{:S(2)}) collective-permute-start(bf16[4,8,2048]{2,1,0:T(8,128)(2,1)S(1)} %pad_maximum_fusion.4), channel_id=1, source_target_pairs={{4,0},{8,4},{12,8},{16,12},{20,16},{24,20},{28,24},{5,1},{9,5},{13... | collective-permute-start | bytes 393224 | tf_op jit(solution)/shard_map/ppermute | solution.py:409
  69.9 9.9 %all-to-all-start = ((f32[8,2,256]{2,1,0:T(2,128)}), f32[8,2,256]{2,1,0:T(2,128)S(1)}, u32[]{:S(2)}, u32[]{:S(2)}) async-start(f32[8,2,256]{2,1,0:T(2,128)} %get-tuple-element.49), calls=%async_computation | async-start | bytes 32768 | tf_op jit(solution)/shard_map/all_to_all | solution.py:369
  79.8 0.6 copy-start.15
  80.4 5.3 %copy-start.17 = (bf16[1024,256]{1,0:T(8,128)(2,1)S(1)}, bf16[1024,256]{1,0:T(8,128)(2,1)}, u32[]{:S(2)}) copy-start(bf16[1024,256]{1,0:T(8,128)(2,1)} %wv.1) | copy-start | bytes 1572868
  80.4 5.3 %copy-start.18 = (bf16[1024,256]{1,0:T(8,128)(2,1)S(1)}, bf16[1024,256]{1,0:T(8,128)(2,1)}, u32[]{:S(2)}) copy-start(bf16[1024,256]{1,0:T(8,128)(2,1)} %wg.1) | copy-start | bytes 1572868
  85.5 6.3 %collective-permute-start.4 = (bf16[1024,512]{1,0:T(8,128)(2,1)}, bf16[1024,512]{1,0:T(8,128)(2,1)}, u32[]{:S(2)}, u32[]{:S(2)}) collective-permute-start(bf16[1024,512]{1,0:T(8,128)(2,1)} %get-tuple-element.59.own.refs_0_), channel_id=1, source_target_pairs={{0,1},{1,0},{2,3},{3,2},{4,5},{5,4},{6,7},{7,6},{8,9},{9,8},{10,11... | collective-permute-start | bytes 3145736 | tf_op jit(solution)/shard_map/ppermute | solution.py:558
  85.9 5.9 %collective-permute-start.3 = (bf16[512,512]{1,0:T(8,128)(2,1)S(1)}, bf16[512,512]{1,0:T(8,128)(2,1)S(1)}, u32[]{:S(2)}, u32[]{:S(2)}) collective-permute-start(bf16[512,512]{1,0:T(8,128)(2,1)S(1)} %bitcast.30), channel_id=1, source_target_pairs={{0,1},{1,0},{2,3},{3,2},{4,5},{5,4},{6,7},{7,6},{8,9},{9,8},{10,11... | collective-permute-start | bytes 1572872 | tf_op jit(solution)/shard_map/ppermute | solution.py:424
  86.4 5.3 %copy-start = (bf16[4,256,1024]{2,1,0:T(8,128)(2,1)S(1)}, bf16[4,256,1024]{2,1,0:T(8,128)(2,1)}, u32[]{:S(2)}) copy-start(bf16[4,256,1024]{2,1,0:T(8,128)(2,1)} %get-tuple-element.54.picked) | copy-start | bytes 6291460
  91.6 12.0 %collective-permute-start.2 = (bf16[1024,512]{1,0:T(8,128)(2,1)}, bf16[1024,512]{1,0:T(8,128)(2,1)}, u32[]{:S(2)}, u32[]{:S(2)}) collective-permute-start(bf16[1024,512]{1,0:T(8,128)(2,1)} %get-tuple-element.53.own.refs_1_), channel_id=1, source_target_pairs={{0,1},{1,0},{2,3},{3,2},{4,5},{5,4},{6,7},{7,6},{8,9},{9,8},{10,11... | collective-permute-start | bytes 3145736 | tf_op jit(solution)/shard_map/ppermute | solution.py:558
  91.8 1.2 copy-start.1
  95.6 1.0 copy-start.10
  101.6 12.5 %collective-permute-start.5 = (bf16[1024,512]{1,0:T(8,128)(2,1)}, bf16[1024,512]{1,0:T(8,128)(2,1)}, u32[]{:S(2)}, u32[]{:S(2)}) collective-permute-start(bf16[1024,512]{1,0:T(8,128)(2,1)} %get-tuple-element.63.own.refs_2_), channel_id=1, source_target_pairs={{0,1},{1,0},{2,3},{3,2},{4,5},{5,4},{6,7},{7,6},{8,9},{9,8},{10,11... | collective-permute-start | bytes 3145736 | tf_op jit(solution)/shard_map/ppermute | solution.py:558
  102.1 17.7 %collective-permute-start.6 = (bf16[256,1024]{1,0:T(8,128)(2,1)S(1)}, bf16[256,1024]{1,0:T(8,128)(2,1)}, u32[]{:S(2)}, u32[]{:S(2)}) collective-permute-start(bf16[256,1024]{1,0:T(8,128)(2,1)S(1)} %get-tuple-element.61), channel_id=1, source_target_pairs={{0,2},{1,3},{2,0},{3,1},{4,6},{5,7},{6,4},{7,5},{8,10},{9,11},{10,... | collective-permute-start | bytes 1572872 | tf_op jit(solution)/shard_map/ppermute | solution.py:584
  103.6 1.2 copy-start.2
  108.1 1.0 copy-start.6
  114.1 1.2 copy-start.3
  115.4 4.4 %copy-start.11 = (f32[256,1024]{1,0:T(8,128)S(1)}, f32[256,1024]{1,0:T(8,128)}, u32[]{:S(2)}) copy-start(f32[256,1024]{1,0:T(8,128)} %copy-done.10) | copy-start | bytes 3145732
  118.8 1.0 copy-start.4
  121.8 13.4 %collective-permute-start.7 = (bf16[1024,512]{1,0:T(8,128)(2,1)}, bf16[1024,512]{1,0:T(8,128)(2,1)}, u32[]{:S(2)}, u32[]{:S(2)}) collective-permute-start(bf16[1024,512]{1,0:T(8,128)(2,1)} %get-tuple-element.67.own.refs_3_), channel_id=1, source_target_pairs={{0,1},{1,0},{2,3},{3,2},{4,5},{5,4},{6,7},{7,6},{8,9},{9,8},{10,11... | collective-permute-start | bytes 3145736 | tf_op jit(solution)/shard_map/ppermute | solution.py:558
  121.8 16.3 %collective-permute-start.8 = (bf16[256,1024]{1,0:T(8,128)(2,1)}, bf16[256,1024]{1,0:T(8,128)(2,1)}, u32[]{:S(2)}, u32[]{:S(2)}) collective-permute-start(bf16[256,1024]{1,0:T(8,128)(2,1)} %get-tuple-element.56), channel_id=1, source_target_pairs={{0,2},{1,3},{2,0},{3,1},{4,6},{5,7},{6,4},{7,5},{8,10},{9,11},{10,... | collective-permute-start | bytes 1572872 | tf_op jit(solution)/shard_map/ppermute | solution.py:584
  129.3 21.4 %collective-permute-start.9 = (bf16[256,1024]{1,0:T(8,128)(2,1)}, bf16[256,1024]{1,0:T(8,128)(2,1)}, u32[]{:S(2)}, u32[]{:S(2)}) collective-permute-start(bf16[256,1024]{1,0:T(8,128)(2,1)} %get-tuple-element.65), channel_id=1, source_target_pairs={{0,2},{1,3},{2,0},{3,1},{4,6},{5,7},{6,4},{7,5},{8,10},{9,11},{10,... | collective-permute-start | bytes 1572872 | tf_op jit(solution)/shard_map/ppermute | solution.py:584
  130.8 21.3 %all-to-all-start.4 = ((bf16[8,32,1024]{2,1,0:T(8,128)(2,1)}), bf16[8,32,1024]{2,1,0:T(8,128)(2,1)}, u32[]{:S(2)}, u32[]{:S(2)}) async-start(bf16[8,32,1024]{2,1,0:T(8,128)(2,1)} %bitcast.28), calls=%async_computation.4 | async-start | bytes 1048576 | tf_op jit(solution)/shard_map/all_to_all | solution.py:369
  135.1 2.9 %copy-start.7 = (f32[256,1024]{1,0:T(8,128)S(1)}, f32[256,1024]{1,0:T(8,128)}, u32[]{:S(2)}) copy-start(f32[256,1024]{1,0:T(8,128)} %copy-done.6) | copy-start | bytes 3145732
  138.0 2.4 %copy-start.8 = (f32[256,1024]{1,0:T(8,128)}, f32[256,1024]{1,0:T(8,128)S(1)}, u32[]{:S(2)}) copy-start(f32[256,1024]{1,0:T(8,128)S(1)} %get-tuple-element.79) | copy-start | bytes 3145732
  138.0 2.4 %copy-start.12 = (bf16[256,1024]{1,0:T(8,128)(2,1)}, bf16[256,1024]{1,0:T(8,128)(2,1)S(1)}, u32[]{:S(2)}) copy-start(bf16[256,1024]{1,0:T(8,128)(2,1)S(1)} %get-tuple-element.69) | copy-start | bytes 1572868
  140.5 10.3 %copy-start.5 = (f32[256,1024]{1,0:T(8,128)S(1)}, f32[256,1024]{1,0:T(8,128)}, u32[]{:S(2)}) copy-start(f32[256,1024]{1,0:T(8,128)} %copy-done.4) | copy-start | bytes 3145732
  150.7 25.0 %copy-start.13 = (bf16[256,1024]{1,0:T(8,128)(2,1)S(1)}, bf16[256,1024]{1,0:T(8,128)(2,1)}, u32[]{:S(2)}) copy-start(bf16[256,1024]{1,0:T(8,128)(2,1)} %copy-done.12) | copy-start | bytes 1572868
  150.7 38.1 %copy-start.9 = (f32[256,1024]{1,0:T(8,128)S(1)}, f32[256,1024]{1,0:T(8,128)}, u32[]{:S(2)}) copy-start(f32[256,1024]{1,0:T(8,128)} %copy-done.8) | copy-start | bytes 3145732
  172.0 33.1 %copy-start.14 = (bf16[4,800,128]{2,1,0:T(8,128)(2,1)S(1)}, bf16[4,800,128]{2,1,0:T(8,128)(2,1)}, u32[]{:S(2)}) copy-start(bf16[4,800,128]{2,1,0:T(8,128)(2,1)} %get-tuple-element.80) | copy-start | bytes 2457604
  172.0 17.9 %all-to-all-start.3 = ((bf16[8,32,1024]{2,1,0:T(8,128)(2,1)}), bf16[8,32,1024]{2,1,0:T(8,128)(2,1)S(1)}, u32[]{:S(2)}, u32[]{:S(2)}) async-start(bf16[8,32,1024]{2,1,0:T(8,128)(2,1)} %bitcast.13), calls=%async_computation.3 | async-start | bytes 1048576 | tf_op jit(solution)/shard_map/all_to_all | solution.py:369
  175.7 13.1 %collective-permute-start.10 = (bf16[256,1024]{1,0:T(8,128)(2,1)S(1)}, bf16[256,1024]{1,0:T(8,128)(2,1)S(1)}, u32[]{:S(2)}, u32[]{:S(2)}) collective-permute-start(bf16[256,1024]{1,0:T(8,128)(2,1)S(1)} %copy-done.13), channel_id=1, source_target_pairs={{0,2},{1,3},{2,0},{3,1},{4,6},{5,7},{6,4},{7,5},{8,10},{9,11},{10,... | collective-permute-start | bytes 1572872 | tf_op jit(solution)/shard_map/ppermute | solution.py:584
  176.3 28.8 %collective-permute-start.11 = (bf16[4,800,128]{2,1,0:T(8,128)(2,1)}, bf16[4,800,128]{2,1,0:T(8,128)(2,1)}, u32[]{:S(2)}, u32[]{:S(2)}) collective-permute-start(bf16[4,800,128]{2,1,0:T(8,128)(2,1)} %get-tuple-element.81), channel_id=1, source_target_pairs={{0,4},{4,0},{8,12},{12,8},{16,20},{20,16},{24,28},{28,24},{1,5},{5... | collective-permute-start | bytes 2457608 | tf_op jit(solution)/shard_map/ppermute | solution.py:615
  189.9 18.3 %all-to-all-start.1 = ((bf16[8,32,1024]{2,1,0:T(8,128)(2,1)}), bf16[8,32,1024]{2,1,0:T(8,128)(2,1)S(1)}, u32[]{:S(2)}, u32[]{:S(2)}) async-start(bf16[8,32,1024]{2,1,0:T(8,128)(2,1)} %bitcast.15), calls=%async_computation.1 | async-start | bytes 1048576 | tf_op jit(solution)/shard_map/all_to_all | solution.py:369
  195.4 17.3 %copy-start.16 = (f32[8,2,256]{2,1,0:T(2,128)S(1)}, f32[8,2,256]{2,1,0:T(2,128)}, u32[]{:S(2)}) copy-start(f32[8,2,256]{2,1,0:T(2,128)} %copy-done.15) | copy-start | bytes 49156
  208.2 23.3 %all-to-all-start.5 = ((bf16[4,800,128]{2,1,0:T(8,128)(2,1)}), bf16[4,800,128]{2,1,0:T(8,128)(2,1)S(1)}, u32[]{:S(2)}, u32[]{:S(2)}) async-start(bf16[4,800,128]{2,1,0:T(8,128)(2,1)} %add_convert_fusion), calls=%async_computation.5 | async-start | bytes 1638400 | tf_op jit(solution)/shard_map/all_to_all | solution.py:620

commit v4 on v3

--- a/solution.py
+++ b/solution.py
@@ -449,19 +449,19 @@
             per_record((frames, width)),
             per_record((frames, width)),
             per_record((span, width)),
-            whole((1, 2, width)),
+            whole((seqs, 2, width)),
         ],
         [
             sds((recs, frames, width), F32),
             sds((recs, frames, width), F32),
             sds((recs, span, width), F32),
-            sds((1, 2, width), F32),
+            sds((seqs, 2, width), F32),
         ],
         [pltpu.VMEM((halves, frames + 4 * EDGE, LANES), F32), pltpu.VMEM((2, width), F32)],
         2 * matmul,
         input_bytes + 3 * array_bytes,
     )(meta, normed, halo_x, value_weight, gate_weight, depth_taps)
-    stats = lax.all_gather(stats, "seq", axis=0, tiled=True)
+    stats = exchange(stats, "seq")
 
     chunk = block_rows(frames, 256)
     half_rows = block_rows(frames, 512)
@@ -550,9 +550,9 @@
                 pltpu.VMEM((halves, chunk + 2 * EDGE, LANES), F32),
                 pltpu.VMEM((halves, kernel, 8, LANES), F32),
             ],
-            60 * frames * width,
-            4 * array_bytes // recs,
-        )(meta, counts, stats, sums, norm_gain[None], gn, conv, vl, sg, after(depth_taps, *marker))
+            0,
+            1024,
+        )(meta, counts, stats, sums, norm_gain[None], gn, conv, vl, sg, after(depth_taps, w_out, *marker))
 
     def partials(r, mine):
         sibling = lax.ppermute(mine, "tp", swap)
@@ -570,8 +570,8 @@
             [pl.BlockSpec((rows, half_rows), lambda i: (0, i))] * chips,
             [sds((rows, frames), F32)] + [sds((rows, frames), BF16)] * (chips - 1),
             [],
-            2 * matmul // recs,
-            8 * frames * width + 6 * rows * frames,
+            0,
+            1024,
             vmem=20,
         )(mine, sibling, w_own, w_sibling, picked)
 
@@ -608,8 +608,8 @@
         [whole(half.shape)] * 2,
         [half] * 2,
         [pltpu.VMEM((2 * width, model), F32)],
-        2 * matmul,
-        input_bytes + 4 * recs * frames * width,
+        0,
+        1024,
     )(parity, after(normed, owns[1]), w_out, *grads, *tap_parts)
     pairs = [(i, i ^ 1) for i in range(seqs)]
     others = lax.ppermute(send, "seq", pairs)

time: 234 us -> 216 us (0.923)
  blocking collectives: 48.4 us -> 19.7 us
  starting transfers between devices: 34.7 us -> 42.4 us
  waiting for transfers between devices: 42.3 us -> 46.9 us
    all_gather x1 -> x0, blocking collectives: 28.5 us -> none  [per_device(): stats = lax.all_gather(stats, 'seq', axis=0, tiled=True)]
    all_to_all x4 -> x5, starting transfers between devices: 16.9 us -> 24.3 us  [exchange(): return lax.all_to_all(copies, axis, 0, 0, tiled=True)]
    ppermute x4, waiting for transfers between devices: 10.5 us -> 14.6 us  [deliver(): total = total + lax.ppermute(parts[r][d], 'tp', send).astype(F32)]
    all_to_all x4 -> x5, waiting for transfers between devices: 7.5 us -> 6.15 us  [exchange(): return lax.all_to_all(copies, axis, 0, 0, tiled=True)]
    unnamed x39 -> x47, local copies, waits for them, and re-layouts: 7.33 us -> 7.92 us
  transfers between devices with their start and end apart: 17 -> 18, of which waited for: 7 -> 8; matrix products, arithmetic and copies ran while one was open for 5% -> 5% of each run, Pallas kernels for 21% -> 22%
where the time goes in v4:
time: 216 us; the launch traced here: 215 us
  Pallas kernels  81.6 us (38%)
  waiting for transfers between devices  46.9 us (22%)
  starting transfers between devices  42.4 us (20%)
  blocking collectives  19.7 us (9%)
  other arithmetic  11.8 us (5%)
  local copies, waits for them, and re-layouts  10.9 us (5%)
    all_to_all x5, starting transfers between devices, exchange(): return lax.all_to_all(copies, axis, 0, 0, tiled=True)  24.3 us
    pallas_call x4, Pallas kernels, back(): call(functools.partial(back_kernel, r), 'back_conv', (frames // chunk,),...  20.2 us
    all_to_all x1, blocking collectives, exchange(): return lax.all_to_all(copies, axis, 0, 0, tiled=True)  19.7 us
    pallas_call x1, Pallas kernels, per_device(): call(gate_kernel, 'gate_conv', (recs,), [smem(), per_record((frames, mode...  15.3 us
    ppermute x4, waiting for transfers between devices, deliver(): total = total + lax.ppermute(parts[r][d], 'tp', send).astype(F32)  14.6 us
    all_to_all x1, waiting for transfers between devices, per_device(): lax.all_to_all(after(paired, owns[-1]), 'seq', 0, 0, axis_index_groups=sa...  13.9 us
    pallas_call x1, Pallas kernels, per_device(): call(norm_kernel, 'swish_norm', (recs,), [smem(), smem(), whole((seqs, 2,...  12.1 us
    pallas_call x4, Pallas kernels, partials(): call(partial_kernel, 'partial_in', (frames // half_rows,), [pl.BlockSpec(...  11.5 us
  transfers between devices with their start and end apart: 18, of which 8 were waited for; matrix products, arithmetic and copies ran while one was open for 5% of the time, Pallas kernels for 22%

profile of v4, /device:TPU:0, one launch (start us, length us, event | category | flops | bytes accessed | tf_op | source)
XLA Modules:
  0.0 214.9 jit_solution(10569189128755515385)
XLA Ops:
  0.6 1.0 fusion.1
  1.6 4.9 %collective-permute-start = (bf16[4,8,2048]{2,1,0:T(8,128)(2,1)S(1)}, bf16[4,8,2048]{2,1,0:T(8,128)(2,1)S(1)}, u32[]{:S(2)}, u32[]{:S(2)}) collective-permute-start(bf16[4,8,2048]{2,1,0:T(8,128)(2,1)S(1)} %pad_maximum_fusion.3), channel_id=1, source_target_pairs={{0,4},{4,8},{8,12},{12,16},{16,20},{20,24},{24,28},{1,5},{5,9},{9,... | collective-permute-start | bytes 393224 | tf_op jit(solution)/shard_map/ppermute | solution.py:409
  6.5 1.3 collective-permute-start.1
  7.8 1.3 fusion.5
  9.8 0.9 fusion.select
  10.8 2.6 %collective-permute-done.1 = bf16[4,8,2048]{2,1,0:T(8,128)(2,1)S(1)} collective-permute-done((bf16[4,8,2048]{2,1,0:T(8,128)(2,1)S(1)}, bf16[4,8,2048]{2,1,0:T(8,128)(2,1)S(1)}, u32[]{:S(2)}, u32[]{:S(2)}) %collective-permute-start.1) | collective-permute-done | bytes 131104 | tf_op jit(solution)/shard_map/ppermute | solution.py:409
  14.1 15.3 %gate_conv.1 = (f32[4,1024,256]{2,1,0:T(8,128)}, f32[4,1024,256]{2,1,0:T(8,128)}, f32[4,1040,256]{2,1,0:T(8,128)}, f32[8,2,256]{2,1,0:T(2,128)}) custom-call(s32[2,4]{1,0:T(2,128)} %stack.35.meta, bf16[4,1024,1024]{2,1,0:T(8,128)(2,1)} %x.4, bf16[4,16,1024]{2,1,0:T(8,128)(2,1)} %get-tuple-element.98.halo, bf16[1024,256]{1,0:T(8,128)(2,1)} %wv.1, ...), custom_call_target="tpu_custom_call" | custom-call | flops 4294967296 | bytes 20971520 | tf_op jit(solution)/shard_map/gate_conv/pallas_call | solution.py:436
  29.4 5.7 %all-to-all-start = ((f32[8,2,256]{2,1,0:T(2,128)}), f32[8,2,256]{2,1,0:T(2,128)S(1)}, u32[]{:S(2)}, u32[]{:S(2)}) async-start(f32[8,2,256]{2,1,0:T(2,128)} %get-tuple-element.48), calls=%async_computation | async-start | bytes 32768 | tf_op jit(solution)/shard_map/all_to_all | solution.py:369
  36.4 5.3 %all-to-all-done.stats = f32[8,2,256]{2,1,0:T(2,128)S(1)} async-done(((f32[8,2,256]{2,1,0:T(2,128)}), f32[8,2,256]{2,1,0:T(2,128)S(1)}, u32[]{:S(2)}, u32[]{:S(2)}) %all-to-all-start) | async-done | bytes 16416 | tf_op jit(solution)/shard_map/all_to_all | solution.py:369
  42.3 12.1 %swish_norm.1 = (bf16[4,1024,256]{2,1,0:T(8,128)(2,1)}, f32[4,1040,256]{2,1,0:T(8,128)}, bf16[4,256,1024]{2,1,0:T(8,128)(2,1)}, f32[8,2,256]{2,1,0:T(2,128)}) custom-call(s32[2,4]{1,0:T(2,128)} %stack.35.meta, f32[1,1]{1,0:T(1,128)} %bitcast.1.count, f32[8,2,256]{2,1,0:T(2,128)} %copy-done.20, f32[2,256]{1,0:T(2,128)} %pad_maximum_fusion.5.affine, ...), custom_call_target="tpu_custom_call" | custom-call | flops 4294967296 | bytes 20971520 | tf_op jit(solution)/shard_map/swish_norm/pallas_call | solution.py:468
  54.4 3.3 %all-to-all-start.1 = ((f32[8,2,256]{2,1,0:T(2,128)}), f32[8,2,256]{2,1,0:T(2,128)S(1)}, u32[]{:S(2)}, u32[]{:S(2)}) async-start(f32[8,2,256]{2,1,0:T(2,128)} %get-tuple-element.50), calls=%async_computation.1 | async-start | bytes 32768 | tf_op jit(solution)/shard_map/all_to_all | solution.py:369
  57.7 7.0 %outer_w_out.1.w_out = f32[256,1024]{1,0:T(8,128)} custom-call(bf16[4,1024,1024]{2,1,0:T(8,128)(2,1)} %grads.3, bf16[4,1024,256]{2,1,0:T(8,128)(2,1)} %get-tuple-element.54.swished), custom_call_target="tpu_custom_call" | custom-call | flops 2147483648 | bytes 8388608 | tf_op jit(solution)/shard_map/outer_w_out/pallas_call | solution.py:513
  65.3 5.1 %back_conv.6 = (bf16[1024,512]{1,0:T(8,128)(2,1)}, f32[16,256]{1,0:T(8,128)}) custom-call(s32[2,4]{1,0:T(2,128)} %stack.35.meta, f32[1,1]{1,0:T(1,128)} %bitcast.1.count, f32[8,2,256]{2,1,0:T(2,128)} %copy-done.20, f32[8,2,256]{2,1,0:T(2,128)} %copy-done.16, f32[1,256]{1,0:T(1,128)} %bitcast.31, f32[4,1040,256]{2,1,0:T(8,128)} %get-tuple-element.51.gn, ...), custom_call_target="tpu_custom_call" | custom-call | bytes 1024 | tf_op jit(solution)/shard_map/back_conv/pallas_call | solution.py:531
  71.4 5.2 %back_conv.4 = (bf16[1024,512]{1,0:T(8,128)(2,1)}, f32[16,256]{1,0:T(8,128)}) custom-call(s32[2,4]{1,0:T(2,128)} %stack.35.meta, f32[1,1]{1,0:T(1,128)} %bitcast.1.count, f32[8,2,256]{2,1,0:T(2,128)} %copy-done.20, f32[8,2,256]{2,1,0:T(2,128)} %copy-done.16, f32[1,256]{1,0:T(1,128)} %bitcast.32, f32[4,1040,256]{2,1,0:T(8,128)} %get-tuple-element.51.gn, ...), custom_call_target="tpu_custom_call" | custom-call | bytes 1024 | tf_op jit(solution)/shard_map/back_conv/pallas_call | solution.py:531
  76.8 1.2 copy-done.1
  78.0 2.6 %partial_in.5 = (f32[256,1024]{1,0:T(8,128)S(1)}, bf16[256,1024]{1,0:T(8,128)(2,1)S(1)}) custom-call(bf16[1024,512]{1,0:T(8,128)(2,1)S(1)} %copy-done.1, bf16[1024,512]{1,0:T(8,128)(2,1)} %collective-permute-done.4.sibling, bf16[512,512]{1,0:T(8,128)(2,1)S(1)} %bitcast.23, bf16[512,512]{1,0:T(8,128)(2,1)S(1)} %collective-permute-done.3.w_sibling, ...), custom_call_target="tpu_custom_call" | custom-call | bytes 1024 | tf_op jit(solution)/shard_map/partial_in/pallas_call | solution.py:559
  80.6 1.0 copy-done.10
  81.6 5.0 %back_conv.7 = (bf16[1024,512]{1,0:T(8,128)(2,1)}, f32[16,256]{1,0:T(8,128)}) custom-call(s32[2,4]{1,0:T(2,128)} %stack.35.meta, f32[1,1]{1,0:T(1,128)} %bitcast.1.count, f32[8,2,256]{2,1,0:T(2,128)} %copy-done.20, f32[8,2,256]{2,1,0:T(2,128)} %copy-done.16, f32[1,256]{1,0:T(1,128)} %bitcast.33, f32[4,1040,256]{2,1,0:T(8,128)} %get-tuple-element.51.gn, ...), custom_call_target="tpu_custom_call" | custom-call | bytes 1024 | tf_op jit(solution)/shard_map/back_conv/pallas_call | solution.py:531
  87.0 1.5 collective-permute-start.6
  88.5 1.2 copy-done.2
  89.8 3.3 %partial_in.4 = (f32[256,1024]{1,0:T(8,128)S(1)}, bf16[256,1024]{1,0:T(8,128)(2,1)}) custom-call(bf16[1024,512]{1,0:T(8,128)(2,1)S(1)} %copy-done.2, bf16[1024,512]{1,0:T(8,128)(2,1)} %collective-permute-done.2.sibling, bf16[512,512]{1,0:T(8,128)(2,1)S(1)} %bitcast.24, bf16[512,512]{1,0:T(8,128)(2,1)S(1)} %collective-permute-done.3.w_sibling, ...), custom_call_target="tpu_custom_call" | custom-call | bytes 1024 | tf_op jit(solution)/shard_map/partial_in/pallas_call | solution.py:559
  93.1 1.0 copy-done.6
  94.1 5.0 %back_conv.5 = (bf16[1024,512]{1,0:T(8,128)(2,1)}, f32[16,256]{1,0:T(8,128)}) custom-call(s32[2,4]{1,0:T(2,128)} %stack.35.meta, f32[1,1]{1,0:T(1,128)} %bitcast.1.count, f32[8,2,256]{2,1,0:T(2,128)} %copy-done.20, f32[8,2,256]{2,1,0:T(2,128)} %copy-done.16, f32[1,256]{1,0:T(1,128)} %bitcast.34, f32[4,1040,256]{2,1,0:T(8,128)} %get-tuple-element.51.gn, ...), custom_call_target="tpu_custom_call" | custom-call | bytes 1024 | tf_op jit(solution)/shard_map/back_conv/pallas_call | solution.py:531
  99.1 1.2 copy-done.3
  100.3 2.7 %partial_in.6 = (f32[256,1024]{1,0:T(8,128)S(1)}, bf16[256,1024]{1,0:T(8,128)(2,1)S(1)}) custom-call(bf16[1024,512]{1,0:T(8,128)(2,1)S(1)} %copy-done.3, bf16[1024,512]{1,0:T(8,128)(2,1)} %collective-permute-done.5.sibling, bf16[512,512]{1,0:T(8,128)(2,1)S(1)} %bitcast.25, bf16[512,512]{1,0:T(8,128)(2,1)S(1)} %collective-permute-done.3.w_sibling, ...), custom_call_target="tpu_custom_call" | custom-call | bytes 1024 | tf_op jit(solution)/shard_map/partial_in/pallas_call | solution.py:559
  103.0 1.0 copy-done.4
  104.0 2.2 %add_convert_fusion.4 = bf16[256,1024]{1,0:T(8,128)(2,1)} fusion(f32[256,1024]{1,0:T(8,128)S(1)} %copy-done.11, bf16[256,1024]{1,0:T(8,128)(2,1)} %collective-permute-done.6), kind=kLoop, calls=%fused_computation.5 | loop fusion | flops 786432 | bytes 2097152 | tf_op jit(solution)/shard_map/convert_element_type | solution.py:585
  106.8 5.9 %all-to-all-start.5 = ((bf16[8,32,1024]{2,1,0:T(8,128)(2,1)}), bf16[8,32,1024]{2,1,0:T(8,128)(2,1)}, u32[]{:S(2)}, u32[]{:S(2)}) async-start(bf16[8,32,1024]{2,1,0:T(8,128)(2,1)} %bitcast.28), calls=%async_computation.5 | async-start | bytes 1048576 | tf_op jit(solution)/shard_map/all_to_all | solution.py:369
  112.7 1.5 collective-permute-start.9
  114.2 2.9 %partial_in.7 = (f32[256,1024]{1,0:T(8,128)S(1)}, bf16[256,1024]{1,0:T(8,128)(2,1)S(1)}) custom-call(bf16[1024,512]{1,0:T(8,128)(2,1)} %get-tuple-element.70.own.refs_3_, bf16[1024,512]{1,0:T(8,128)(2,1)} %collective-permute-done.7.sibling, bf16[512,512]{1,0:T(8,128)(2,1)S(1)} %bitcast.26, bf16[512,512]{1,0:T(8,128)(2,1)S(1)} %collective-permute-done.3.w_sibling, ...), custom_call_target="tpu_custom_call" | custom-call | bytes 1024 | tf_op jit(solution)/shard_map/partial_in/pallas_call | solution.py:559
  117.1 4.2 %collective-permute-done.8 = bf16[256,1024]{1,0:T(8,128)(2,1)} collective-permute-done((bf16[256,1024]{1,0:T(8,128)(2,1)}, bf16[256,1024]{1,0:T(8,128)(2,1)}, u32[]{:S(2)}, u32[]{:S(2)}) %collective-permute-start.8) | collective-permute-done | bytes 524320 | tf_op jit(solution)/shard_map/ppermute | solution.py:584
  121.3 2.0 add_convert_fusion.3
  123.3 10.3 %outer_w_in.1 = (bf16[4,800,128]{2,1,0:T(8,128)(2,1)}, bf16[4,800,128]{2,1,0:T(8,128)(2,1)}) custom-call(s32[1,1]{1,0:T(1,128)} %bitcast.12.parity, bf16[4,1024,1024]{2,1,0:T(8,128)(2,1)} %x.4, f32[256,1024]{1,0:T(8,128)} %outer_w_out.1.w_out, bf16[1024,512]{1,0:T(8,128)(2,1)} %get-tuple-element.62.own.refs_0_, ...), custom_call_target="tpu_custom_call" | custom-call | bytes 1024 | tf_op jit(solution)/shard_map/outer_w_in/pallas_call | solution.py:601
  133.6 1.3 add_convert_fusion.2
  134.9 19.7 %all_to_all.35.moved = bf16[8,32,1024]{2,1,0:T(8,128)(2,1)S(1)} all-to-all(bf16[8,32,1024]{2,1,0:T(8,128)(2,1)S(1)} %bitcast.29), channel_id=1, replica_groups=mesh['seq'=8,'tp'=4] {'seq'}, dimensions={0} | all-to-all | bytes 1048576 | tf_op jit(solution)/shard_map/all_to_all | solution.py:369
  154.6 3.8 %all-to-all-start.4 = ((bf16[8,32,1024]{2,1,0:T(8,128)(2,1)}), bf16[8,32,1024]{2,1,0:T(8,128)(2,1)S(1)}, u32[]{:S(2)}, u32[]{:S(2)}) async-start(bf16[8,32,1024]{2,1,0:T(8,128)(2,1)} %bitcast.13), calls=%async_computation.4 | async-start | bytes 1048576 | tf_op jit(solution)/shard_map/all_to_all | solution.py:369
  159.0 2.0 collective-permute-start.11
  160.9 10.4 %collective-permute-done.10 = bf16[256,1024]{1,0:T(8,128)(2,1)S(1)} collective-permute-done((bf16[256,1024]{1,0:T(8,128)(2,1)S(1)}, bf16[256,1024]{1,0:T(8,128)(2,1)S(1)}, u32[]{:S(2)}, u32[]{:S(2)}) %collective-permute-start.10) | collective-permute-done | bytes 524320 | tf_op jit(solution)/shard_map/ppermute | solution.py:584
  171.3 0.9 add_convert_fusion.1
  172.4 5.5 %all-to-all-start.2 = ((bf16[8,32,1024]{2,1,0:T(8,128)(2,1)}), bf16[8,32,1024]{2,1,0:T(8,128)(2,1)S(1)}, u32[]{:S(2)}, u32[]{:S(2)}) async-start(bf16[8,32,1024]{2,1,0:T(8,128)(2,1)} %bitcast.15), calls=%async_computation.2 | async-start | bytes 1048576 | tf_op jit(solution)/shard_map/all_to_all | solution.py:369
  177.9 9.7 %collective-permute-done.11 = bf16[4,800,128]{2,1,0:T(8,128)(2,1)} collective-permute-done((bf16[4,800,128]{2,1,0:T(8,128)(2,1)}, bf16[4,800,128]{2,1,0:T(8,128)(2,1)}, u32[]{:S(2)}, u32[]{:S(2)}) %collective-permute-start.11) | collective-permute-done | bytes 819232 | tf_op jit(solution)/shard_map/ppermute | solution.py:615
  187.6 2.3 %add_convert_fusion = bf16[4,800,128]{2,1,0:T(8,128)(2,1)} fusion(bf16[4,800,128]{2,1,0:T(8,128)(2,1)} %collective-permute-done.11, bf16[4,800,128]{2,1,0:T(8,128)(2,1)S(1)} %copy-done.15), kind=kLoop, calls=%fused_computation | loop fusion | flops 1638400 | bytes 2457600 | tf_op jit(solution)/shard_map/convert_element_type | solution.py:618
  190.6 4.6 %all-to-all-start.6 = ((bf16[4,800,128]{2,1,0:T(8,128)(2,1)}), bf16[4,800,128]{2,1,0:T(8,128)(2,1)S(1)}, u32[]{:S(2)}, u32[]{:S(2)}) async-start(bf16[4,800,128]{2,1,0:T(8,128)(2,1)} %add_convert_fusion), calls=%async_computation.6 | async-start | bytes 1638400 | tf_op jit(solution)/shard_map/all_to_all | solution.py:620
  195.8 1.9 place.4.refs_0_
  197.7 0.8 place.5.refs_0_
  198.5 0.8 place.6.refs_0_
  200.2 13.9 %all-to-all-done.6.got = bf16[4,800,128]{2,1,0:T(8,128)(2,1)S(1)} async-done(((bf16[4,800,128]{2,1,0:T(8,128)(2,1)}), bf16[4,800,128]{2,1,0:T(8,128)(2,1)S(1)}, u32[]{:S(2)}, u32[]{:S(2)}) %all-to-all-start.6) | async-done | bytes 819232 | tf_op jit(solution)/shard_map/all_to_all | solution.py:620
  214.1 0.8 finish.1
  (76 shorter events, 8.2 us)
Async XLA Ops:
  1.6 9.2 %collective-permute-start = (bf16[4,8,2048]{2,1,0:T(8,128)(2,1)S(1)}, bf16[4,8,2048]{2,1,0:T(8,128)(2,1)S(1)}, u32[]{:S(2)}, u32[]{:S(2)}) collective-permute-start(bf16[4,8,2048]{2,1,0:T(8,128)(2,1)S(1)} %pad_maximum_fusion.3), channel_id=1, source_target_pairs={{0,4},{4,8},{8,12},{12,16},{16,20},{20,24},{24,28},{1,5},{5,9},{9,... | collective-permute-start | bytes 393224 | tf_op jit(solution)/shard_map/ppermute | solution.py:409
  6.5 6.9 %collective-permute-start.1 = (bf16[4,8,2048]{2,1,0:T(8,128)(2,1)S(1)}, bf16[4,8,2048]{2,1,0:T(8,128)(2,1)S(1)}, u32[]{:S(2)}, u32[]{:S(2)}) collective-permute-start(bf16[4,8,2048]{2,1,0:T(8,128)(2,1)S(1)} %pad_maximum_fusion.4), channel_id=1, source_target_pairs={{4,0},{8,4},{12,8},{16,12},{20,16},{24,20},{28,24},{5,1},{9,5},{13... | collective-permute-start | bytes 393224 | tf_op jit(solution)/shard_map/ppermute | solution.py:409
  14.1 21.0 %copy-start.21 = (f32[256]{0:T(256)S(1)}, f32[256]{0:T(256)}, u32[]{:S(2)}) copy-start(f32[256]{0:T(256)} %param.14) | copy-start | bytes 3076
  14.1 21.0 %copy-start.22 = (f32[256]{0:T(256)S(1)}, f32[256]{0:T(256)}, u32[]{:S(2)}) copy-start(f32[256]{0:T(256)} %param.15) | copy-start | bytes 3076
  29.4 12.3 %all-to-all-start = ((f32[8,2,256]{2,1,0:T(2,128)}), f32[8,2,256]{2,1,0:T(2,128)S(1)}, u32[]{:S(2)}, u32[]{:S(2)}) async-start(f32[8,2,256]{2,1,0:T(2,128)} %get-tuple-element.48), calls=%async_computation | async-start | bytes 32768 | tf_op jit(solution)/shard_map/all_to_all | solution.py:369
  41.7 0.6 copy-start.20
  54.4 10.4 %all-to-all-start.1 = ((f32[8,2,256]{2,1,0:T(2,128)}), f32[8,2,256]{2,1,0:T(2,128)S(1)}, u32[]{:S(2)}, u32[]{:S(2)}) async-start(f32[8,2,256]{2,1,0:T(2,128)} %get-tuple-element.50), calls=%async_computation.1 | async-start | bytes 32768 | tf_op jit(solution)/shard_map/all_to_all | solution.py:369
  64.7 0.6 copy-start.16
  65.3 5.3 %copy-start.18 = (bf16[1024,256]{1,0:T(8,128)(2,1)S(1)}, bf16[1024,256]{1,0:T(8,128)(2,1)}, u32[]{:S(2)}) copy-start(bf16[1024,256]{1,0:T(8,128)(2,1)} %wv.1) | copy-start | bytes 1572868
  65.3 5.3 %copy-start.19 = (bf16[1024,256]{1,0:T(8,128)(2,1)S(1)}, bf16[1024,256]{1,0:T(8,128)(2,1)}, u32[]{:S(2)}) copy-start(bf16[1024,256]{1,0:T(8,128)(2,1)} %wg.1) | copy-start | bytes 1572868
  70.4 6.3 %collective-permute-start.4 = (bf16[1024,512]{1,0:T(8,128)(2,1)}, bf16[1024,512]{1,0:T(8,128)(2,1)}, u32[]{:S(2)}, u32[]{:S(2)}) collective-permute-start(bf16[1024,512]{1,0:T(8,128)(2,1)} %get-tuple-element.62.own.refs_0_), channel_id=1, source_target_pairs={{0,1},{1,0},{2,3},{3,2},{4,5},{5,4},{6,7},{7,6},{8,9},{9,8},{10,11... | collective-permute-start | bytes 3145736 | tf_op jit(solution)/shard_map/ppermute | solution.py:558
  70.8 5.9 %collective-permute-start.3 = (bf16[512,512]{1,0:T(8,128)(2,1)S(1)}, bf16[512,512]{1,0:T(8,128)(2,1)S(1)}, u32[]{:S(2)}, u32[]{:S(2)}) collective-permute-start(bf16[512,512]{1,0:T(8,128)(2,1)S(1)} %bitcast.30), channel_id=1, source_target_pairs={{0,1},{1,0},{2,3},{3,2},{4,5},{5,4},{6,7},{7,6},{8,9},{9,8},{10,11... | collective-permute-start | bytes 1572872 | tf_op jit(solution)/shard_map/ppermute | solution.py:424
  71.4 5.4 %copy-start = (bf16[4,256,1024]{2,1,0:T(8,128)(2,1)S(1)}, bf16[4,256,1024]{2,1,0:T(8,128)(2,1)}, u32[]{:S(2)}) copy-start(bf16[4,256,1024]{2,1,0:T(8,128)(2,1)} %get-tuple-element.57.picked) | copy-start | bytes 6291460
  76.6 12.0 %collective-permute-start.2 = (bf16[1024,512]{1,0:T(8,128)(2,1)}, bf16[1024,512]{1,0:T(8,128)(2,1)}, u32[]{:S(2)}, u32[]{:S(2)}) collective-permute-start(bf16[1024,512]{1,0:T(8,128)(2,1)} %get-tuple-element.56.own.refs_1_), channel_id=1, source_target_pairs={{0,1},{1,0},{2,3},{3,2},{4,5},{5,4},{6,7},{7,6},{8,9},{9,8},{10,11... | collective-permute-start | bytes 3145736 | tf_op jit(solution)/shard_map/ppermute | solution.py:558
  76.7 1.2 copy-start.1
  80.6 1.0 copy-start.10
  86.6 12.5 %collective-permute-start.5 = (bf16[1024,512]{1,0:T(8,128)(2,1)}, bf16[1024,512]{1,0:T(8,128)(2,1)}, u32[]{:S(2)}, u32[]{:S(2)}) collective-permute-start(bf16[1024,512]{1,0:T(8,128)(2,1)} %get-tuple-element.66.own.refs_2_), channel_id=1, source_target_pairs={{0,1},{1,0},{2,3},{3,2},{4,5},{5,4},{6,7},{7,6},{8,9},{9,8},{10,11... | collective-permute-start | bytes 3145736 | tf_op jit(solution)/shard_map/ppermute | solution.py:558
  87.0 17.0 %collective-permute-start.6 = (bf16[256,1024]{1,0:T(8,128)(2,1)S(1)}, bf16[256,1024]{1,0:T(8,128)(2,1)}, u32[]{:S(2)}, u32[]{:S(2)}) collective-permute-start(bf16[256,1024]{1,0:T(8,128)(2,1)S(1)} %get-tuple-element.64), channel_id=1, source_target_pairs={{0,2},{1,3},{2,0},{3,1},{4,6},{5,7},{6,4},{7,5},{8,10},{9,11},{10,... | collective-permute-start | bytes 1572872 | tf_op jit(solution)/shard_map/ppermute | solution.py:584
  88.5 1.2 copy-start.2
  93.1 1.0 copy-start.6
  99.1 1.2 copy-start.3
  100.3 3.7 %copy-start.11 = (f32[256,1024]{1,0:T(8,128)S(1)}, f32[256,1024]{1,0:T(8,128)}, u32[]{:S(2)}) copy-start(f32[256,1024]{1,0:T(8,128)} %copy-done.10) | copy-start | bytes 3145732
  103.0 1.0 copy-start.4
  104.0 2.2 %copy-start.12 = (bf16[256,1024]{1,0:T(8,128)(2,1)}, bf16[256,1024]{1,0:T(8,128)(2,1)S(1)}, u32[]{:S(2)}) copy-start(bf16[256,1024]{1,0:T(8,128)(2,1)S(1)} %get-tuple-element.68) | copy-start | bytes 1572868
  106.2 8.0 %collective-permute-start.7 = (bf16[1024,512]{1,0:T(8,128)(2,1)}, bf16[1024,512]{1,0:T(8,128)(2,1)}, u32[]{:S(2)}, u32[]{:S(2)}) collective-permute-start(bf16[1024,512]{1,0:T(8,128)(2,1)} %get-tuple-element.70.own.refs_3_), channel_id=1, source_target_pairs={{0,1},{1,0},{2,3},{3,2},{4,5},{5,4},{6,7},{7,6},{8,9},{9,8},{10,11... | collective-permute-start | bytes 3145736 | tf_op jit(solution)/shard_map/ppermute | solution.py:558
  106.2 15.0 %collective-permute-start.8 = (bf16[256,1024]{1,0:T(8,128)(2,1)}, bf16[256,1024]{1,0:T(8,128)(2,1)}, u32[]{:S(2)}, u32[]{:S(2)}) collective-permute-start(bf16[256,1024]{1,0:T(8,128)(2,1)} %get-tuple-element.59), channel_id=1, source_target_pairs={{0,2},{1,3},{2,0},{3,1},{4,6},{5,7},{6,4},{7,5},{8,10},{9,11},{10,... | collective-permute-start | bytes 1572872 | tf_op jit(solution)/shard_map/ppermute | solution.py:584
  106.8 28.1 %all-to-all-start.5 = ((bf16[8,32,1024]{2,1,0:T(8,128)(2,1)}), bf16[8,32,1024]{2,1,0:T(8,128)(2,1)}, u32[]{:S(2)}, u32[]{:S(2)}) async-start(bf16[8,32,1024]{2,1,0:T(8,128)(2,1)} %bitcast.28), calls=%async_computation.5 | async-start | bytes 1048576 | tf_op jit(solution)/shard_map/all_to_all | solution.py:369
  112.7 20.9 %collective-permute-start.9 = (bf16[256,1024]{1,0:T(8,128)(2,1)}, bf16[256,1024]{1,0:T(8,128)(2,1)}, u32[]{:S(2)}, u32[]{:S(2)}) collective-permute-start(bf16[256,1024]{1,0:T(8,128)(2,1)} %copy-done.12), channel_id=1, source_target_pairs={{0,2},{1,3},{2,0},{3,1},{4,6},{5,7},{6,4},{7,5},{8,10},{9,11},{10,... | collective-permute-start | bytes 1572872 | tf_op jit(solution)/shard_map/ppermute | solution.py:584
  114.2 7.1 %copy-start.7 = (f32[256,1024]{1,0:T(8,128)S(1)}, f32[256,1024]{1,0:T(8,128)}, u32[]{:S(2)}) copy-start(f32[256,1024]{1,0:T(8,128)} %copy-done.6) | copy-start | bytes 3145732
  117.1 6.2 %copy-start.8 = (f32[256,1024]{1,0:T(8,128)}, f32[256,1024]{1,0:T(8,128)S(1)}, u32[]{:S(2)}) copy-start(f32[256,1024]{1,0:T(8,128)S(1)} %get-tuple-element.81) | copy-start | bytes 3145732
  117.1 6.2 %copy-start.13 = (bf16[256,1024]{1,0:T(8,128)(2,1)}, bf16[256,1024]{1,0:T(8,128)(2,1)S(1)}, u32[]{:S(2)}) copy-start(bf16[256,1024]{1,0:T(8,128)(2,1)S(1)} %get-tuple-element.72) | copy-start | bytes 1572868
  123.3 10.3 %copy-start.5 = (f32[256,1024]{1,0:T(8,128)S(1)}, f32[256,1024]{1,0:T(8,128)}, u32[]{:S(2)}) copy-start(f32[256,1024]{1,0:T(8,128)} %copy-done.4) | copy-start | bytes 3145732
  133.5 24.8 %copy-start.14 = (bf16[256,1024]{1,0:T(8,128)(2,1)S(1)}, bf16[256,1024]{1,0:T(8,128)(2,1)}, u32[]{:S(2)}) copy-start(bf16[256,1024]{1,0:T(8,128)(2,1)} %copy-done.13) | copy-start | bytes 1572868
  133.5 37.8 %copy-start.9 = (f32[256,1024]{1,0:T(8,128)S(1)}, f32[256,1024]{1,0:T(8,128)}, u32[]{:S(2)}) copy-start(f32[256,1024]{1,0:T(8,128)} %copy-done.8) | copy-start | bytes 3145732
  154.6 33.0 %copy-start.15 = (bf16[4,800,128]{2,1,0:T(8,128)(2,1)S(1)}, bf16[4,800,128]{2,1,0:T(8,128)(2,1)}, u32[]{:S(2)}) copy-start(bf16[4,800,128]{2,1,0:T(8,128)(2,1)} %get-tuple-element.82) | copy-start | bytes 2457604
  154.6 17.8 %all-to-all-start.4 = ((bf16[8,32,1024]{2,1,0:T(8,128)(2,1)}), bf16[8,32,1024]{2,1,0:T(8,128)(2,1)S(1)}, u32[]{:S(2)}, u32[]{:S(2)}) async-start(bf16[8,32,1024]{2,1,0:T(8,128)(2,1)} %bitcast.13), calls=%async_computation.4 | async-start | bytes 1048576 | tf_op jit(solution)/shard_map/all_to_all | solution.py:369
  158.4 13.0 %collective-permute-start.10 = (bf16[256,1024]{1,0:T(8,128)(2,1)S(1)}, bf16[256,1024]{1,0:T(8,128)(2,1)S(1)}, u32[]{:S(2)}, u32[]{:S(2)}) collective-permute-start(bf16[256,1024]{1,0:T(8,128)(2,1)S(1)} %copy-done.14), channel_id=1, source_target_pairs={{0,2},{1,3},{2,0},{3,1},{4,6},{5,7},{6,4},{7,5},{8,10},{9,11},{10,... | collective-permute-start | bytes 1572872 | tf_op jit(solution)/shard_map/ppermute | solution.py:584
  159.0 28.7 %collective-permute-start.11 = (bf16[4,800,128]{2,1,0:T(8,128)(2,1)}, bf16[4,800,128]{2,1,0:T(8,128)(2,1)}, u32[]{:S(2)}, u32[]{:S(2)}) collective-permute-start(bf16[4,800,128]{2,1,0:T(8,128)(2,1)} %get-tuple-element.83), channel_id=1, source_target_pairs={{0,4},{4,0},{8,12},{12,8},{16,20},{20,16},{24,28},{28,24},{1,5},{5... | collective-permute-start | bytes 2457608 | tf_op jit(solution)/shard_map/ppermute | solution.py:615
  172.4 18.2 %all-to-all-start.2 = ((bf16[8,32,1024]{2,1,0:T(8,128)(2,1)}), bf16[8,32,1024]{2,1,0:T(8,128)(2,1)S(1)}, u32[]{:S(2)}, u32[]{:S(2)}) async-start(bf16[8,32,1024]{2,1,0:T(8,128)(2,1)} %bitcast.15), calls=%async_computation.2 | async-start | bytes 1048576 | tf_op jit(solution)/shard_map/all_to_all | solution.py:369
  177.9 17.3 %copy-start.17 = (f32[8,2,256]{2,1,0:T(2,128)S(1)}, f32[8,2,256]{2,1,0:T(2,128)}, u32[]{:S(2)}) copy-start(f32[8,2,256]{2,1,0:T(2,128)} %copy-done.16) | copy-start | bytes 49156
  190.6 23.5 %all-to-all-start.6 = ((bf16[4,800,128]{2,1,0:T(8,128)(2,1)}), bf16[4,800,128]{2,1,0:T(8,128)(2,1)S(1)}, u32[]{:S(2)}, u32[]{:S(2)}) async-start(bf16[4,800,128]{2,1,0:T(8,128)(2,1)} %add_convert_fusion), calls=%async_computation.6 | async-start | bytes 1638400 | tf_op jit(solution)/shard_map/all_to_all | solution.py:620

commit v5 on v4

--- a/solution.py
+++ b/solution.py
@@ -215,12 +215,12 @@
 
 
 def back_kernel(
-    record, meta, count, stats, sums, gain, gn, conv, vl, sg, taps, out, taps_o, gc, acc
+    record, blocks, meta, count, stats, sums, gain, gn, conv, vl, sg, taps, out, taps_o, gc, acc
 ):
     i = pl.program_id(0)
-    hi = meta[0, record]
-    lo = meta[1, record]
     frames, width = vl.shape[1:]
+    hi = meta[0, record + i // blocks]
+    lo = meta[1, record + i // blocks]
     halves = width // LANES
     span = frames + 2 * EDGE
     kernel = taps.shape[0]
@@ -233,7 +233,7 @@
     scale = gain[...] * inv
     offset = scale * grad_sums[0:1] / total_frames
     slope = scale * inv * grad_sums[1:2] / total_frames
-    first = i * frames
+    first = i % blocks * frames
 
     @pl.when(i == 0)
     def _():
@@ -280,9 +280,14 @@
 def partial_kernel(own, sibling, w_own, w_sibling, picked, mine, *others):
     total = dot_nt(w_own[...], own[...]) + dot_nt(w_sibling[...], sibling[...])
     rows = picked.shape[1]
-    mine[...] = total[:rows] + picked[0].astype(F32)
+    seqs, _, piece, frames = mine.shape
+    mine[...] = (
+        (total[:rows] + picked[0].astype(F32)).astype(BF16).reshape(seqs, 1, piece, frames)
+    )
     for d, other in enumerate(others):
-        other[...] = total[(d + 1) * rows : (d + 2) * rows].astype(BF16)
+        other[...] = (
+            total[(d + 1) * rows : (d + 2) * rows].astype(BF16).reshape(seqs, 1, piece, frames)
+        )
 
 
 def first_outer_kernel(grads, swished, out):
@@ -298,21 +303,19 @@
         out[...] += add
 
 
-def outer_kernel(records, parity, x, w_out, *refs):
-    lefts, taps = refs[:records], refs[records : 2 * records]
-    keep, send, acc = refs[2 * records :]
+def outer_kernel(groups, parity, x, w_out, *refs):
+    lefts, taps = refs[: len(groups)], refs[len(groups) : 2 * len(groups)]
+    keep, send, acc = refs[2 * len(groups) :]
+    records = groups[-1][0] + groups[-1][1]
     width = w_out.shape[0]
     shard = keep.shape[2]
     r = pl.program_id(0)
-    for i, left in enumerate(lefts):
-
-        @pl.when(r == i)
-        def _(i=i, left=left):
+    for (first, size), left in zip(groups, lefts):
+
+        @pl.when((r >= first) & (r < first + size))
+        def _(left=left):
             add = dot_tn(left[...], x[0])
-            if i == 0:
-                acc[...] = add
-            else:
-                acc[...] += add
+            acc[...] = add + jnp.where(r == 0, 0.0, acc[...])
 
     @pl.when(r == records - 1)
     def _():
@@ -360,9 +363,9 @@
 
 def place_kernel(moved, *refs):
     out = refs[-1]
-    frames = moved.shape[2]
+    frames = moved.shape[3]
     for s in range(moved.shape[0]):
-        out[0, :, s * frames : (s + 1) * frames] = moved[s]
+        out[0, :, s * frames : (s + 1) * frames] = moved[s, 0]
 
 
 def exchange(copies, axis):
@@ -524,14 +527,20 @@
     sums = exchange(sums, "seq")
     grad_shift, grad_gain = jnp.sum(sums, axis=0)
 
-    def back(r, marker):
+    blocks = frames // chunk
+    parts_in = frames // half_rows
+
+    def back(first, size, *earlier):
         def window(i):
-            return (r, pl.multiple_of(i * chunk, chunk), 0)
+            return (first + i // blocks, pl.multiple_of(i % blocks * chunk, chunk), 0)
+
+        def block(i):
+            return (first + i // blocks, i % blocks, 0)
 
         return call(
-            functools.partial(back_kernel, r),
+            functools.partial(back_kernel, first, blocks),
             "back_conv",
-            (frames // chunk,),
+            (size * blocks,),
             [
                 smem(),
                 smem(),
@@ -540,86 +549,99 @@
                 whole((1, width)),
                 pl.BlockSpec((pl.Element(1), pl.Element(chunk + 2 * EDGE), pl.Element(width)), window),
                 pl.BlockSpec((pl.Element(1), pl.Element(chunk + 2 * EDGE), pl.Element(width)), window),
-                pl.BlockSpec((1, chunk, width), lambda i: (r, i, 0)),
-                pl.BlockSpec((1, chunk, width), lambda i: (r, i, 0)),
+                pl.BlockSpec((1, chunk, width), block),
+                pl.BlockSpec((1, chunk, width), block),
                 whole((kernel, width)),
             ],
             [pl.BlockSpec((chunk, 2 * width), lambda i: (i, 0)), whole((16, width))],
-            [sds((frames, 2 * width), BF16), sds((16, width), F32)],
+            [sds((size * frames, 2 * width), BF16), sds((16, width), F32)],
             [
                 pltpu.VMEM((halves, chunk + 2 * EDGE, LANES), F32),
                 pltpu.VMEM((halves, kernel, 8, LANES), F32),
             ],
             0,
             1024,
-        )(meta, counts, stats, sums, norm_gain[None], gn, conv, vl, sg, after(depth_taps, w_out, *marker))
-
-    def partials(r, mine):
+        )(meta, counts, stats, sums, norm_gain[None], gn, conv, vl, sg, after(depth_taps, *earlier))
+
+    def partials(first, size, mine, *earlier):
         sibling = lax.ppermute(mine, "tp", swap)
+        out = sds((seqs, size, piece, frames), BF16)
         return call(
             partial_kernel,
             "partial_in",
-            (frames // half_rows,),
+            (size * parts_in,),
             [
                 pl.BlockSpec((half_rows, 2 * width), lambda i: (i, 0)),
                 pl.BlockSpec((half_rows, 2 * width), lambda i: (i, 0)),
                 whole((chips * rows, 2 * width)),
                 whole((chips * rows, 2 * width)),
-                pl.BlockSpec((1, rows, half_rows), lambda i: (r, 0, i)),
+                pl.BlockSpec(
+                    (1, rows, half_rows), lambda i: (first + i // parts_in, 0, i % parts_in)
+                ),
             ],
-            [pl.BlockSpec((rows, half_rows), lambda i: (0, i))] * chips,
-            [sds((rows, frames), F32)] + [sds((rows, frames), BF16)] * (chips - 1),
+            [
+                pl.BlockSpec(
+                    (seqs, 1, piece, half_rows), lambda i: (0, i // parts_in, 0, i % parts_in)
+                )
+            ]
+            * chips,
+            [out] * chips,
             [],
             0,
             1024,
             vmem=20,
-        )(mine, sibling, w_own, w_sibling, picked)
-
-    grads, tap_parts, parts, moved = [], [], [], []
-
-    def deliver(r, *earlier):
-        total = after(parts[r][0], *earlier)
+        )(mine, sibling, after(w_own, *earlier), w_sibling, picked)
+
+    def deliver(part, *earlier):
+        total = after(part[0], *earlier).astype(F32)
         for d in range(1, chips):
             send = [(i, ((i // 2 + d) % chips) * 2 + i % 2) for i in range(tps)]
-            total = total + lax.ppermute(parts[r][d], "tp", send).astype(F32)
-        own = total.astype(BF16).reshape(seqs, piece, frames)
-        moved.append(exchange(own, "seq"))
-        return own
-
-    for r in range(recs):
-        mine, tap_part = back(r, parts[r - 2] if r > 1 else ())
-        grads.append(mine)
-        tap_parts.append(tap_part)
-        if r > 0:
-            parts.append(partials(r - 1, grads[r - 1]))
-    owns = [deliver(0, *parts[recs - 2])]
-    parts.append(partials(recs - 1, after(grads[recs - 1], owns[0])))
-    owns.append(deliver(1, *parts[recs - 1]))
+            total = total + lax.ppermute(part[d], "tp", send).astype(F32)
+        own = total.astype(BF16)
+        return own, exchange(own, "seq")
+
+    groups = ((0, 1), (1, 1), (2, recs - 2))
+    grads = [None] * 3
+    taps = [None] * 3
+    parts = [None] * 3
+    owns = [None] * 3
+    moved = [None] * 3
+    grads[0], taps[0] = back(*groups[0], w_out)
+    grads[1], taps[1] = back(*groups[1], grads[0])
+    parts[0] = partials(*groups[0], grads[0], grads[1])
+    grads[2], taps[2] = back(*groups[2], *parts[0])
+    parts[1] = partials(*groups[1], grads[1], grads[2])
+    parts[2] = partials(*groups[2], grads[2], *parts[1])
+    owns[0], moved[0] = deliver(parts[0], *parts[2])
 
     slots = 3 * width + 16 * (width // shard)
     half = sds((seqs // 2, slots, shard), BF16)
     keep, send = call(
-        functools.partial(outer_kernel, recs),
+        functools.partial(outer_kernel, groups),
         "outer_w_in",
         (recs,),
         [smem(), per_record((frames, model)), whole((width, model))]
-        + [whole((frames, 2 * width))] * recs
-        + [whole((16, width))] * recs,
+        + [
+            pl.BlockSpec(
+                (frames, 2 * width),
+                lambda r, first=first, size=size: (jnp.clip(r - first, 0, size - 1), 0),
+            )
+            for first, size in groups
+        ]
+        + [whole((16, width))] * len(groups),
         [whole(half.shape)] * 2,
         [half] * 2,
         [pltpu.VMEM((2 * width, model), F32)],
         0,
         1024,
-    )(parity, after(normed, owns[1]), w_out, *grads, *tap_parts)
+    )(parity, after(normed, owns[0]), w_out, *grads, *taps)
     pairs = [(i, i ^ 1) for i in range(seqs)]
     others = lax.ppermute(send, "seq", pairs)
-    for r in range(2, recs):
-        owns.append(deliver(r, keep, owns[-1]))
-    paired = (after(keep, owns[-2]).astype(F32) + others.astype(F32)).astype(BF16)
+    owns[1], moved[1] = deliver(parts[1], keep)
+    paired = (after(keep, owns[1]).astype(F32) + others.astype(F32)).astype(BF16)
     same = [[i for i in range(seqs) if i % 2 == odd] for odd in range(2)]
-    got = lax.all_to_all(
-        after(paired, owns[-1]), "seq", 0, 0, axis_index_groups=same, tiled=True
-    )
+    got = lax.all_to_all(paired, "seq", 0, 0, axis_index_groups=same, tiled=True)
+    owns[2], moved[2] = deliver(parts[2], paired)
     w_value, w_gate, w_out, grad_taps = call(
         functools.partial(finish_kernel, kernel),
         "finish",
@@ -633,21 +655,22 @@
         vmem=20,
     )(got)
     grad_in = ()
-    for r in range(recs):
+    for (first, size), part in zip(groups, moved):
         grad_in = (
             call(
                 place_kernel,
                 "place",
-                (1,),
-                [whole((seqs, piece, frames))] + [anywhere()] * len(grad_in),
-                pl.BlockSpec((1, piece, seqs * frames), lambda i, r=r: (r, 0, 0)),
+                (size,),
+                [pl.BlockSpec((seqs, 1, piece, frames), lambda i: (0, i, 0, 0))]
+                + [anywhere()] * len(grad_in),
+                pl.BlockSpec((1, piece, seqs * frames), lambda i, first=first: (first + i, 0, 0)),
                 sds((recs, piece, seqs * frames), BF16),
                 [],
                 0,
-                4 * piece * seqs * frames,
+                4 * size * piece * seqs * frames,
                 {1: 0} if grad_in else None,
                 vmem=20,
-            )(moved[r], *grad_in),
+            )(part, *grad_in),
         )
     (grad_in,) = grad_in
     return (grad_in, w_value, w_gate, w_out, grad_taps, grad_gain, grad_shift)

time: 216 us -> 219 us (1.014)
  waiting for transfers between devices: 46.9 us -> 75 us
  blocking collectives: 19.7 us -> 0 us
  Pallas kernels: 81.6 us -> 77.8 us
  starting transfers between devices: 42.4 us -> 39.6 us
    all_to_all x5, waiting for transfers between devices: 6.15 us -> 41 us  [exchange(): return lax.all_to_all(copies, axis, 0, 0, tiled=True)]
    all_to_all x1 -> x0, blocking collectives: 19.7 us -> none  [exchange(): return lax.all_to_all(copies, axis, 0, 0, tiled=True)]
    ppermute x4 -> x3, waiting for transfers between devices: 14.6 us -> 6.02 us  [deliver(): total = total + lax.ppermute(part[d], 'tp', send).astype(F32)]
    pallas_call x13 -> x10, Pallas kernels: 46.4 us -> 42.6 us  [the longest x3 19.3 us: back(): call(functools.partial(back_kernel, first, blocks), 'back_conv', (size *...]
    ppermute x4 -> x3, waiting for transfers between devices: 0.01 us -> 3.6 us  [partials(): sibling = lax.ppermute(mine, 'tp', swap)]
    all_to_all x1, waiting for transfers between devices: 13.9 us -> 10.7 us  [per_device(): lax.all_to_all(paired, 'seq', 0, 0, axis_index_groups=same, tiled=True)]
    convert_element_type x5 -> x4, other arithmetic: 8.7 us -> 9.4 us  [the longest x3 7.15 us: deliver(): own = total.astype(BF16)]
    unnamed x47 -> x39, local copies, waits for them, and re-layouts: 7.92 us -> 7.9 us
  transfers between devices with their start and end apart: 18 -> 16, of which waited for: 8 -> 9; matrix products, arithmetic and copies ran while one was open for 5% -> 5% of each run, Pallas kernels for 22% -> 15%
where the time goes in v5:
time: 219 us; the launch traced here: 218 us
  Pallas kernels  77.8 us (36%)
  waiting for transfers between devices  75 us (34%)
  starting transfers between devices  39.6 us (18%)
  other arithmetic  12.5 us (6%)
  local copies, waits for them, and re-layouts  10.9 us (5%)
    all_to_all x5, waiting for transfers between devices, exchange(): return lax.all_to_all(copies, axis, 0, 0, tiled=True)  41 us
    all_to_all x5, starting transfers between devices, exchange(): return lax.all_to_all(copies, axis, 0, 0, tiled=True)  22.2 us
    pallas_call x3, Pallas kernels, back(): call(functools.partial(back_kernel, first, blocks), 'back_conv', (size *...  19.3 us
    pallas_call x1, Pallas kernels, per_device(): call(gate_kernel, 'gate_conv', (recs,), [smem(), per_record((frames, mode...  15.3 us
    pallas_call x1, Pallas kernels, per_device(): call(norm_kernel, 'swish_norm', (recs,), [smem(), smem(), whole((seqs, 2,...  12.1 us
    ppermute x1, waiting for transfers between devices, per_device(): others = lax.ppermute(send, 'seq', pairs)  11.1 us
    all_to_all x1, waiting for transfers between devices, per_device(): lax.all_to_all(paired, 'seq', 0, 0, axis_index_groups=same, tiled=True)  10.7 us
    pallas_call x3, Pallas kernels, partials(): call(partial_kernel, 'partial_in', (size * parts_in,), [pl.BlockSpec((hal...  10.4 us
  transfers between devices with their start and end apart: 16, of which 9 were waited for; matrix products, arithmetic and copies ran while one was open for 5% of the time, Pallas kernels for 15%

profile of v5, /device:TPU:0, one launch (start us, length us, event | category | flops | bytes accessed | tf_op | source)
XLA Modules:
  0.0 217.5 jit_solution(4381284277932405052)
XLA Ops:
  0.6 1.0 fusion.1
  1.6 4.9 %collective-permute-start = (bf16[4,8,2048]{2,1,0:T(8,128)(2,1)S(1)}, bf16[4,8,2048]{2,1,0:T(8,128)(2,1)S(1)}, u32[]{:S(2)}, u32[]{:S(2)}) collective-permute-start(bf16[4,8,2048]{2,1,0:T(8,128)(2,1)S(1)} %pad_maximum_fusion.3), channel_id=1, source_target_pairs={{0,4},{4,8},{8,12},{12,16},{16,20},{20,24},{24,28},{1,5},{5,9},{9,... | collective-permute-start | bytes 393224 | tf_op jit(solution)/shard_map/ppermute | solution.py:412
  6.5 1.3 collective-permute-start.1
  7.8 1.3 fusion.5
  9.8 0.9 fusion.select
  10.8 2.6 %collective-permute-done.1 = bf16[4,8,2048]{2,1,0:T(8,128)(2,1)S(1)} collective-permute-done((bf16[4,8,2048]{2,1,0:T(8,128)(2,1)S(1)}, bf16[4,8,2048]{2,1,0:T(8,128)(2,1)S(1)}, u32[]{:S(2)}, u32[]{:S(2)}) %collective-permute-start.1) | collective-permute-done | bytes 131104 | tf_op jit(solution)/shard_map/ppermute | solution.py:412
  13.4 0.7 fusion.3
  14.1 15.3 %gate_conv.1 = (f32[4,1024,256]{2,1,0:T(8,128)}, f32[4,1024,256]{2,1,0:T(8,128)}, f32[4,1040,256]{2,1,0:T(8,128)}, f32[8,2,256]{2,1,0:T(2,128)}) custom-call(s32[2,4]{1,0:T(2,128)} %stack.35.meta, bf16[4,1024,1024]{2,1,0:T(8,128)(2,1)} %x.4, bf16[4,16,1024]{2,1,0:T(8,128)(2,1)} %get-tuple-element.90.halo, bf16[1024,256]{1,0:T(8,128)(2,1)} %wv.1, ...), custom_call_target="tpu_custom_call" | custom-call | flops 4294967296 | bytes 20971520 | tf_op jit(solution)/shard_map/gate_conv/pallas_call | solution.py:439
  29.4 5.7 %all-to-all-start = ((f32[8,2,256]{2,1,0:T(2,128)}), f32[8,2,256]{2,1,0:T(2,128)S(1)}, u32[]{:S(2)}, u32[]{:S(2)}) async-start(f32[8,2,256]{2,1,0:T(2,128)} %get-tuple-element.44), calls=%async_computation | async-start | bytes 32768 | tf_op jit(solution)/shard_map/all_to_all | solution.py:372
  36.4 5.3 %all-to-all-done.stats = f32[8,2,256]{2,1,0:T(2,128)S(1)} async-done(((f32[8,2,256]{2,1,0:T(2,128)}), f32[8,2,256]{2,1,0:T(2,128)S(1)}, u32[]{:S(2)}, u32[]{:S(2)}) %all-to-all-start) | async-done | bytes 16416 | tf_op jit(solution)/shard_map/all_to_all | solution.py:372
  42.3 12.1 %swish_norm.1 = (bf16[4,1024,256]{2,1,0:T(8,128)(2,1)}, f32[4,1040,256]{2,1,0:T(8,128)}, bf16[4,256,1024]{2,1,0:T(8,128)(2,1)}, f32[8,2,256]{2,1,0:T(2,128)}) custom-call(s32[2,4]{1,0:T(2,128)} %stack.35.meta, f32[1,1]{1,0:T(1,128)} %bitcast.1.count, f32[8,2,256]{2,1,0:T(2,128)} %copy-done.16, f32[2,256]{1,0:T(2,128)} %pad_maximum_fusion.5.affine, ...), custom_call_target="tpu_custom_call" | custom-call | flops 4294967296 | bytes 20971520 | tf_op jit(solution)/shard_map/swish_norm/pallas_call | solution.py:471
  54.4 3.5 %all-to-all-start.1 = ((f32[8,2,256]{2,1,0:T(2,128)}), f32[8,2,256]{2,1,0:T(2,128)S(1)}, u32[]{:S(2)}, u32[]{:S(2)}) async-start(f32[8,2,256]{2,1,0:T(2,128)} %get-tuple-element.46), calls=%async_computation.1 | async-start | bytes 32768 | tf_op jit(solution)/shard_map/all_to_all | solution.py:372
  57.9 7.0 %outer_w_out.1.w_out = f32[256,1024]{1,0:T(8,128)} custom-call(bf16[4,1024,1024]{2,1,0:T(8,128)(2,1)} %grads.3, bf16[4,1024,256]{2,1,0:T(8,128)(2,1)} %get-tuple-element.50.swished), custom_call_target="tpu_custom_call" | custom-call | flops 2147483648 | bytes 8388608 | tf_op jit(solution)/shard_map/outer_w_out/pallas_call | solution.py:516
  65.5 5.2 %back_conv.3 = (bf16[1024,512]{1,0:T(8,128)(2,1)}, f32[16,256]{1,0:T(8,128)}) custom-call(s32[2,4]{1,0:T(2,128)} %stack.35.meta, f32[1,1]{1,0:T(1,128)} %bitcast.1.count, f32[8,2,256]{2,1,0:T(2,128)} %copy-done.16, f32[8,2,256]{2,1,0:T(2,128)} %copy-done.14, f32[1,256]{1,0:T(1,128)} %bitcast.24, f32[4,1040,256]{2,1,0:T(8,128)} %get-tuple-element.47.gn, ...), custom_call_target="tpu_custom_call" | custom-call | bytes 1024 | tf_op jit(solution)/shard_map/back_conv/pallas_call | solution.py:540
  71.6 5.2 %back_conv.4 = (bf16[1024,512]{1,0:T(8,128)(2,1)}, f32[16,256]{1,0:T(8,128)}) custom-call(s32[2,4]{1,0:T(2,128)} %stack.35.meta, f32[1,1]{1,0:T(1,128)} %bitcast.1.count, f32[8,2,256]{2,1,0:T(2,128)} %copy-done.16, f32[8,2,256]{2,1,0:T(2,128)} %copy-done.14, f32[1,256]{1,0:T(1,128)} %bitcast.25, f32[4,1040,256]{2,1,0:T(8,128)} %get-tuple-element.47.gn, ...), custom_call_target="tpu_custom_call" | custom-call | bytes 1024 | tf_op jit(solution)/shard_map/back_conv/pallas_call | solution.py:540
  76.9 1.2 copy-done.2
  78.1 3.4 %partial_in.3 = (bf16[8,1,32,1024]{3,2,1,0:T(8,128)(2,1)S(1)}, bf16[8,1,32,1024]{3,2,1,0:T(8,128)(2,1)}) custom-call(bf16[1024,512]{1,0:T(8,128)(2,1)S(1)} %copy-done.2, bf16[1024,512]{1,0:T(8,128)(2,1)} %collective-permute-done.2.sibling, bf16[512,512]{1,0:T(8,128)(2,1)S(1)} %bitcast.19, bf16[512,512]{1,0:T(8,128)(2,1)S(1)} %collective-permute-done.3.w_sibling, ...), custom_call_target="tpu_custom_call" | custom-call | bytes 1024 | tf_op jit(solution)/shard_map/partial_in/pallas_call | solution.py:569
  81.5 0.8 copy-done.6
  82.3 8.9 %back_conv.5 = (bf16[2048,512]{1,0:T(8,128)(2,1)}, f32[16,256]{1,0:T(8,128)}) custom-call(s32[2,4]{1,0:T(2,128)} %stack.35.meta, f32[1,1]{1,0:T(1,128)} %bitcast.1.count, f32[8,2,256]{2,1,0:T(2,128)} %copy-done.16, f32[8,2,256]{2,1,0:T(2,128)} %copy-done.14, f32[1,256]{1,0:T(1,128)} %bitcast.26, f32[4,1040,256]{2,1,0:T(8,128)} %get-tuple-element.47.gn, ...), custom_call_target="tpu_custom_call" | custom-call | bytes 1024 | tf_op jit(solution)/shard_map/back_conv/pallas_call | solution.py:540
  91.8 1.5 collective-permute-start.6
  93.3 3.6 %collective-permute-done.5.sibling = bf16[1024,512]{1,0:T(8,128)(2,1)S(1)} collective-permute-done((bf16[1024,512]{1,0:T(8,128)(2,1)}, bf16[1024,512]{1,0:T(8,128)(2,1)S(1)}, u32[]{:S(2)}, u32[]{:S(2)}) %collective-permute-start.5) | collective-permute-done | bytes 1048608 | tf_op jit(solution)/shard_map/ppermute | solution.py:567
  96.9 1.2 copy-done.3
  98.1 2.4 %partial_in.4 = (bf16[8,1,32,1024]{3,2,1,0:T(8,128)(2,1)S(1)}, bf16[8,1,32,1024]{3,2,1,0:T(8,128)(2,1)}) custom-call(bf16[1024,512]{1,0:T(8,128)(2,1)S(1)} %copy-done.3, bf16[1024,512]{1,0:T(8,128)(2,1)S(1)} %collective-permute-done.5.sibling, bf16[512,512]{1,0:T(8,128)(2,1)S(1)} %bitcast.20, bf16[512,512]{1,0:T(8,128)(2,1)S(1)} %collective-permute-done.3.w_sibling, ...), custom_call_target="tpu_custom_call" | custom-call | bytes 1024 | tf_op jit(solution)/shard_map/partial_in/pallas_call | solution.py:569
  100.4 0.8 copy-done.8
  101.2 1.5 collective-permute-start.7
  102.8 1.6 copy-done.1
  104.3 4.7 %partial_in.5 = (bf16[8,2,32,1024]{3,2,1,0:T(8,128)(2,1)S(1)}, bf16[8,2,32,1024]{3,2,1,0:T(8,128)(2,1)S(1)}) custom-call(bf16[2048,512]{1,0:T(8,128)(2,1)S(1)} %copy-done.1, bf16[2048,512]{1,0:T(8,128)(2,1)} %collective-permute-done.4.sibling, bf16[512,512]{1,0:T(8,128)(2,1)S(1)} %bitcast.21, bf16[512,512]{1,0:T(8,128)(2,1)S(1)} %collective-permute-done.3.w_sibling, ...), custom_call_target="tpu_custom_call" | custom-call | bytes 1024 | tf_op jit(solution)/shard_map/partial_in/pallas_call | solution.py:569
  109.0 1.0 copy-done.4
  110.0 2.4 %add_convert_fusion.3 = bf16[8,1,32,1024]{3,2,1,0:T(8,128)(2,1)} fusion(bf16[8,1,32,1024]{3,2,1,0:T(8,128)(2,1)} %collective-permute-done.6, bf16[8,1,32,1024]{3,2,1,0:T(8,128)(2,1)S(1)} %copy-done.7), kind=kLoop, calls=%fused_computation.4 | loop fusion | flops 1048576 | bytes 1572864 | tf_op jit(solution)/shard_map/convert_element_type | solution.py:600
  112.4 10.2 %outer_w_in.1 = (bf16[4,800,128]{2,1,0:T(8,128)(2,1)}, bf16[4,800,128]{2,1,0:T(8,128)(2,1)}) custom-call(s32[1,1]{1,0:T(1,128)} %bitcast.11.parity, bf16[4,1024,1024]{2,1,0:T(8,128)(2,1)} %x.4, f32[256,1024]{1,0:T(8,128)} %outer_w_out.1.w_out, bf16[1024,512]{1,0:T(8,128)(2,1)} %get-tuple-element.52.own.refs_0_, ...), custom_call_target="tpu_custom_call" | custom-call | bytes 1024 | tf_op jit(solution)/shard_map/outer_w_in/pallas_call | solution.py:619
  122.7 2.1 add_convert_fusion.2
  124.8 5.7 %all-to-all-start.3 = ((bf16[8,1,32,1024]{3,2,1,0:T(8,128)(2,1)}), bf16[8,1,32,1024]{3,2,1,0:T(8,128)(2,1)S(1)}, u32[]{:S(2)}, u32[]{:S(2)}) async-start(bf16[8,1,32,1024]{3,2,1,0:T(8,128)(2,1)} %add_convert_fusion.2), calls=%async_computation.3 | async-start | bytes 1048576 | tf_op jit(solution)/shard_map/all_to_all | solution.py:372
  130.5 2.0 collective-permute-start.8
  132.5 12.7 %all-to-all-done.3.moved = bf16[8,1,32,1024]{3,2,1,0:T(8,128)(2,1)S(1)} async-done(((bf16[8,1,32,1024]{3,2,1,0:T(8,128)(2,1)}), bf16[8,1,32,1024]{3,2,1,0:T(8,128)(2,1)S(1)}, u32[]{:S(2)}, u32[]{:S(2)}) %all-to-all-start.3) | async-done | bytes 524320 | tf_op jit(solution)/shard_map/all_to_all | solution.py:372
  145.3 3.7 %all-to-all-start.4 = ((bf16[8,1,32,1024]{3,2,1,0:T(8,128)(2,1)}), bf16[8,1,32,1024]{3,2,1,0:T(8,128)(2,1)S(1)}, u32[]{:S(2)}, u32[]{:S(2)}) async-start(bf16[8,1,32,1024]{3,2,1,0:T(8,128)(2,1)} %add_convert_fusion.3), calls=%async_computation.4 | async-start | bytes 1048576 | tf_op jit(solution)/shard_map/all_to_all | solution.py:372
  149.5 11.1 %collective-permute-done.8 = bf16[4,800,128]{2,1,0:T(8,128)(2,1)} collective-permute-done((bf16[4,800,128]{2,1,0:T(8,128)(2,1)}, bf16[4,800,128]{2,1,0:T(8,128)(2,1)}, u32[]{:S(2)}, u32[]{:S(2)}) %collective-permute-start.8) | collective-permute-done | bytes 819232 | tf_op jit(solution)/shard_map/ppermute | solution.py:639
  160.6 2.2 %add_convert_fusion.1 = bf16[4,800,128]{2,1,0:T(8,128)(2,1)} fusion(bf16[4,800,128]{2,1,0:T(8,128)(2,1)} %collective-permute-done.8, bf16[4,800,128]{2,1,0:T(8,128)(2,1)S(1)} %copy-done.11), kind=kLoop, calls=%fused_computation.1 | loop fusion | flops 1638400 | bytes 2457600 | tf_op jit(solution)/shard_map/convert_element_type | solution.py:641
  162.9 0.7 all-to-all-done.4.moved
  163.6 4.5 %all-to-all-start.5 = ((bf16[4,800,128]{2,1,0:T(8,128)(2,1)}), bf16[4,800,128]{2,1,0:T(8,128)(2,1)S(1)}, u32[]{:S(2)}, u32[]{:S(2)}) async-start(bf16[4,800,128]{2,1,0:T(8,128)(2,1)} %add_convert_fusion.1), calls=%async_computation.5 | async-start | bytes 1638400 | tf_op jit(solution)/shard_map/all_to_all | solution.py:643
  168.1 6.0 %collective-permute-done.9 = bf16[8,2,32,1024]{3,2,1,0:T(8,128)(2,1)} collective-permute-done((bf16[8,2,32,1024]{3,2,1,0:T(8,128)(2,1)}, bf16[8,2,32,1024]{3,2,1,0:T(8,128)(2,1)}, u32[]{:S(2)}, u32[]{:S(2)}) %collective-permute-start.9) | collective-permute-done | bytes 1048608 | tf_op jit(solution)/shard_map/ppermute | solution.py:599
  174.1 2.6 %add_convert_fusion = bf16[8,2,32,1024]{3,2,1,0:T(8,128)(2,1)} fusion(bf16[8,2,32,1024]{3,2,1,0:T(8,128)(2,1)} %collective-permute-done.9, bf16[8,2,32,1024]{3,2,1,0:T(8,128)(2,1)S(1)} %copy-done.5), kind=kLoop, calls=%fused_computation | loop fusion | flops 2097152 | bytes 3145728 | tf_op jit(solution)/shard_map/convert_element_type | solution.py:600
  176.7 10.7 %all-to-all-done.5.got = bf16[4,800,128]{2,1,0:T(8,128)(2,1)S(1)} async-done(((bf16[4,800,128]{2,1,0:T(8,128)(2,1)}), bf16[4,800,128]{2,1,0:T(8,128)(2,1)S(1)}, u32[]{:S(2)}, u32[]{:S(2)}) %all-to-all-start.5) | async-done | bytes 819232 | tf_op jit(solution)/shard_map/all_to_all | solution.py:643
  187.5 3.6 %all-to-all-start.2 = ((bf16[8,2,32,1024]{3,2,1,0:T(8,128)(2,1)}), bf16[8,2,32,1024]{3,2,1,0:T(8,128)(2,1)S(1)}, u32[]{:S(2)}, u32[]{:S(2)}) async-start(bf16[8,2,32,1024]{3,2,1,0:T(8,128)(2,1)} %add_convert_fusion), calls=%async_computation.2 | async-start | bytes 2097152 | tf_op jit(solution)/shard_map/all_to_all | solution.py:372
  191.7 0.8 place.3.refs_0_
  192.5 0.8 place.4.refs_0_
  193.3 0.8 finish.1
  194.2 22.3 %all-to-all-done.2.moved = bf16[8,2,32,1024]{3,2,1,0:T(8,128)(2,1)S(1)} async-done(((bf16[8,2,32,1024]{3,2,1,0:T(8,128)(2,1)}), bf16[8,2,32,1024]{3,2,1,0:T(8,128)(2,1)S(1)}, u32[]{:S(2)}, u32[]{:S(2)}) %all-to-all-start.2) | async-done | bytes 1048608 | tf_op jit(solution)/shard_map/all_to_all | solution.py:372
  216.4 1.1 place.5
  (59 shorter events, 5.2 us)
Async XLA Ops:
  1.6 9.2 %collective-permute-start = (bf16[4,8,2048]{2,1,0:T(8,128)(2,1)S(1)}, bf16[4,8,2048]{2,1,0:T(8,128)(2,1)S(1)}, u32[]{:S(2)}, u32[]{:S(2)}) collective-permute-start(bf16[4,8,2048]{2,1,0:T(8,128)(2,1)S(1)} %pad_maximum_fusion.3), channel_id=1, source_target_pairs={{0,4},{4,8},{8,12},{12,16},{16,20},{20,24},{24,28},{1,5},{5,9},{9,... | collective-permute-start | bytes 393224 | tf_op jit(solution)/shard_map/ppermute | solution.py:412
  6.5 6.9 %collective-permute-start.1 = (bf16[4,8,2048]{2,1,0:T(8,128)(2,1)S(1)}, bf16[4,8,2048]{2,1,0:T(8,128)(2,1)S(1)}, u32[]{:S(2)}, u32[]{:S(2)}) collective-permute-start(bf16[4,8,2048]{2,1,0:T(8,128)(2,1)S(1)} %pad_maximum_fusion.4), channel_id=1, source_target_pairs={{4,0},{8,4},{12,8},{16,12},{20,16},{24,20},{28,24},{5,1},{9,5},{13... | collective-permute-start | bytes 393224 | tf_op jit(solution)/shard_map/ppermute | solution.py:412
  14.1 21.0 %copy-start.17 = (f32[256]{0:T(256)S(1)}, f32[256]{0:T(256)}, u32[]{:S(2)}) copy-start(f32[256]{0:T(256)} %param.14) | copy-start | bytes 3076
  14.1 21.0 %copy-start.18 = (f32[256]{0:T(256)S(1)}, f32[256]{0:T(256)}, u32[]{:S(2)}) copy-start(f32[256]{0:T(256)} %param.15) | copy-start | bytes 3076
  29.4 12.3 %all-to-all-start = ((f32[8,2,256]{2,1,0:T(2,128)}), f32[8,2,256]{2,1,0:T(2,128)S(1)}, u32[]{:S(2)}, u32[]{:S(2)}) async-start(f32[8,2,256]{2,1,0:T(2,128)} %get-tuple-element.44), calls=%async_computation | async-start | bytes 32768 | tf_op jit(solution)/shard_map/all_to_all | solution.py:372
  41.7 0.6 copy-start.16
  54.4 10.6 %all-to-all-start.1 = ((f32[8,2,256]{2,1,0:T(2,128)}), f32[8,2,256]{2,1,0:T(2,128)S(1)}, u32[]{:S(2)}, u32[]{:S(2)}) async-start(f32[8,2,256]{2,1,0:T(2,128)} %get-tuple-element.46), calls=%async_computation.1 | async-start | bytes 32768 | tf_op jit(solution)/shard_map/all_to_all | solution.py:372
  64.9 0.6 copy-start.14
  65.5 5.3 %copy-start.12 = (bf16[1024,256]{1,0:T(8,128)(2,1)S(1)}, bf16[1024,256]{1,0:T(8,128)(2,1)}, u32[]{:S(2)}) copy-start(bf16[1024,256]{1,0:T(8,128)(2,1)} %wv.1) | copy-start | bytes 1572868
  65.5 5.3 %copy-start.13 = (bf16[1024,256]{1,0:T(8,128)(2,1)S(1)}, bf16[1024,256]{1,0:T(8,128)(2,1)}, u32[]{:S(2)}) copy-start(bf16[1024,256]{1,0:T(8,128)(2,1)} %wg.1) | copy-start | bytes 1572868
  70.7 6.2 %collective-permute-start.2 = (bf16[1024,512]{1,0:T(8,128)(2,1)}, bf16[1024,512]{1,0:T(8,128)(2,1)}, u32[]{:S(2)}, u32[]{:S(2)}) collective-permute-start(bf16[1024,512]{1,0:T(8,128)(2,1)} %get-tuple-element.52.own.refs_0_), channel_id=1, source_target_pairs={{0,1},{1,0},{2,3},{3,2},{4,5},{5,4},{6,7},{7,6},{8,9},{9,8},{10,11... | collective-permute-start | bytes 3145736 | tf_op jit(solution)/shard_map/ppermute | solution.py:567
  71.1 5.8 %collective-permute-start.3 = (bf16[512,512]{1,0:T(8,128)(2,1)S(1)}, bf16[512,512]{1,0:T(8,128)(2,1)S(1)}, u32[]{:S(2)}, u32[]{:S(2)}) collective-permute-start(bf16[512,512]{1,0:T(8,128)(2,1)S(1)} %bitcast.23), channel_id=1, source_target_pairs={{0,1},{1,0},{2,3},{3,2},{4,5},{5,4},{6,7},{7,6},{8,9},{9,8},{10,11... | collective-permute-start | bytes 1572872 | tf_op jit(solution)/shard_map/ppermute | solution.py:427
  71.6 5.2 %copy-start = (bf16[4,256,1024]{2,1,0:T(8,128)(2,1)S(1)}, bf16[4,256,1024]{2,1,0:T(8,128)(2,1)}, u32[]{:S(2)}) copy-start(bf16[4,256,1024]{2,1,0:T(8,128)(2,1)} %get-tuple-element.56.picked) | copy-start | bytes 6291460
  76.9 1.2 copy-start.2
  81.5 0.8 copy-start.6
  91.2 11.6 %collective-permute-start.4 = (bf16[2048,512]{1,0:T(8,128)(2,1)}, bf16[2048,512]{1,0:T(8,128)(2,1)}, u32[]{:S(2)}, u32[]{:S(2)}) collective-permute-start(bf16[2048,512]{1,0:T(8,128)(2,1)} %get-tuple-element.60.own.refs_2_), channel_id=1, source_target_pairs={{0,1},{1,0},{2,3},{3,2},{4,5},{5,4},{6,7},{7,6},{8,9},{9,8},{10,11... | collective-permute-start | bytes 6291464 | tf_op jit(solution)/shard_map/ppermute | solution.py:567
  91.4 5.5 %collective-permute-start.5 = (bf16[1024,512]{1,0:T(8,128)(2,1)}, bf16[1024,512]{1,0:T(8,128)(2,1)S(1)}, u32[]{:S(2)}, u32[]{:S(2)}) collective-permute-start(bf16[1024,512]{1,0:T(8,128)(2,1)} %get-tuple-element.54.own.refs_1_), channel_id=1, source_target_pairs={{0,1},{1,0},{2,3},{3,2},{4,5},{5,4},{6,7},{7,6},{8,9},{9,8},{10,11... | collective-permute-start | bytes 3145736 | tf_op jit(solution)/shard_map/ppermute | solution.py:567
  91.8 18.2 %collective-permute-start.6 = (bf16[8,1,32,1024]{3,2,1,0:T(8,128)(2,1)}, bf16[8,1,32,1024]{3,2,1,0:T(8,128)(2,1)}, u32[]{:S(2)}, u32[]{:S(2)}) collective-permute-start(bf16[8,1,32,1024]{3,2,1,0:T(8,128)(2,1)} %get-tuple-element.58), channel_id=1, source_target_pairs={{0,2},{1,3},{2,0},{3,1},{4,6},{5,7},{6,4},{7,5},{8,10},{9,11},{10,... | collective-permute-start | bytes 1572872 | tf_op jit(solution)/shard_map/ppermute | solution.py:599
  96.9 1.2 copy-start.3
  100.4 0.8 copy-start.8
  101.2 21.4 %collective-permute-start.7 = (bf16[8,1,32,1024]{3,2,1,0:T(8,128)(2,1)}, bf16[8,1,32,1024]{3,2,1,0:T(8,128)(2,1)}, u32[]{:S(2)}, u32[]{:S(2)}) collective-permute-start(bf16[8,1,32,1024]{3,2,1,0:T(8,128)(2,1)} %get-tuple-element.63), channel_id=1, source_target_pairs={{0,2},{1,3},{2,0},{3,1},{4,6},{5,7},{6,4},{7,5},{8,10},{9,11},{10,... | collective-permute-start | bytes 1572872 | tf_op jit(solution)/shard_map/ppermute | solution.py:599
  102.7 1.6 copy-start.1
  104.3 5.7 %copy-start.7 = (bf16[8,1,32,1024]{3,2,1,0:T(8,128)(2,1)S(1)}, bf16[8,1,32,1024]{3,2,1,0:T(8,128)(2,1)}, u32[]{:S(2)}) copy-start(bf16[8,1,32,1024]{3,2,1,0:T(8,128)(2,1)} %copy-done.6) | copy-start | bytes 1572868
  109.0 1.0 copy-start.4
  110.0 2.4 %copy-start.10 = (bf16[8,2,32,1024]{3,2,1,0:T(8,128)(2,1)}, bf16[8,2,32,1024]{3,2,1,0:T(8,128)(2,1)S(1)}, u32[]{:S(2)}) copy-start(bf16[8,2,32,1024]{3,2,1,0:T(8,128)(2,1)S(1)} %get-tuple-element.66) | copy-start | bytes 3145732
  112.4 10.2 %copy-start.9 = (bf16[8,1,32,1024]{3,2,1,0:T(8,128)(2,1)S(1)}, bf16[8,1,32,1024]{3,2,1,0:T(8,128)(2,1)}, u32[]{:S(2)}) copy-start(bf16[8,1,32,1024]{3,2,1,0:T(8,128)(2,1)} %copy-done.8) | copy-start | bytes 1572868
  122.7 37.9 %copy-start.11 = (bf16[4,800,128]{2,1,0:T(8,128)(2,1)S(1)}, bf16[4,800,128]{2,1,0:T(8,128)(2,1)}, u32[]{:S(2)}) copy-start(bf16[4,800,128]{2,1,0:T(8,128)(2,1)} %get-tuple-element.74) | copy-start | bytes 2457604
  124.8 20.5 %all-to-all-start.3 = ((bf16[8,1,32,1024]{3,2,1,0:T(8,128)(2,1)}), bf16[8,1,32,1024]{3,2,1,0:T(8,128)(2,1)S(1)}, u32[]{:S(2)}, u32[]{:S(2)}) async-start(bf16[8,1,32,1024]{3,2,1,0:T(8,128)(2,1)} %add_convert_fusion.2), calls=%async_computation.3 | async-start | bytes 1048576 | tf_op jit(solution)/shard_map/all_to_all | solution.py:372
  130.5 30.1 %collective-permute-start.8 = (bf16[4,800,128]{2,1,0:T(8,128)(2,1)}, bf16[4,800,128]{2,1,0:T(8,128)(2,1)}, u32[]{:S(2)}, u32[]{:S(2)}) collective-permute-start(bf16[4,800,128]{2,1,0:T(8,128)(2,1)} %get-tuple-element.75), channel_id=1, source_target_pairs={{0,4},{4,0},{8,12},{12,8},{16,20},{20,16},{24,28},{28,24},{1,5},{5... | collective-permute-start | bytes 2457608 | tf_op jit(solution)/shard_map/ppermute | solution.py:639
  145.3 18.3 %all-to-all-start.4 = ((bf16[8,1,32,1024]{3,2,1,0:T(8,128)(2,1)}), bf16[8,1,32,1024]{3,2,1,0:T(8,128)(2,1)S(1)}, u32[]{:S(2)}, u32[]{:S(2)}) async-start(bf16[8,1,32,1024]{3,2,1,0:T(8,128)(2,1)} %add_convert_fusion.3), calls=%async_computation.4 | async-start | bytes 1048576 | tf_op jit(solution)/shard_map/all_to_all | solution.py:372
  148.9 25.2 %copy-start.5 = (bf16[8,2,32,1024]{3,2,1,0:T(8,128)(2,1)S(1)}, bf16[8,2,32,1024]{3,2,1,0:T(8,128)(2,1)}, u32[]{:S(2)}) copy-start(bf16[8,2,32,1024]{3,2,1,0:T(8,128)(2,1)} %copy-done.4) | copy-start | bytes 3145732
  148.9 25.2 %collective-permute-start.9 = (bf16[8,2,32,1024]{3,2,1,0:T(8,128)(2,1)}, bf16[8,2,32,1024]{3,2,1,0:T(8,128)(2,1)}, u32[]{:S(2)}, u32[]{:S(2)}) collective-permute-start(bf16[8,2,32,1024]{3,2,1,0:T(8,128)(2,1)} %copy-done.10), channel_id=1, source_target_pairs={{0,2},{1,3},{2,0},{3,1},{4,6},{5,7},{6,4},{7,5},{8,10},{9,11},{10,... | collective-permute-start | bytes 3145736 | tf_op jit(solution)/shard_map/ppermute | solution.py:599
  163.6 23.9 %all-to-all-start.5 = ((bf16[4,800,128]{2,1,0:T(8,128)(2,1)}), bf16[4,800,128]{2,1,0:T(8,128)(2,1)S(1)}, u32[]{:S(2)}, u32[]{:S(2)}) async-start(bf16[4,800,128]{2,1,0:T(8,128)(2,1)} %add_convert_fusion.1), calls=%async_computation.5 | async-start | bytes 1638400 | tf_op jit(solution)/shard_map/all_to_all | solution.py:643
  168.1 23.0 %copy-start.15 = (f32[8,2,256]{2,1,0:T(2,128)S(1)}, f32[8,2,256]{2,1,0:T(2,128)}, u32[]{:S(2)}) copy-start(f32[8,2,256]{2,1,0:T(2,128)} %copy-done.14) | copy-start | bytes 49156
  187.5 28.9 %all-to-all-start.2 = ((bf16[8,2,32,1024]{3,2,1,0:T(8,128)(2,1)}), bf16[8,2,32,1024]{3,2,1,0:T(8,128)(2,1)S(1)}, u32[]{:S(2)}, u32[]{:S(2)}) async-start(bf16[8,2,32,1024]{3,2,1,0:T(8,128)(2,1)} %add_convert_fusion), calls=%async_computation.2 | async-start | bytes 2097152 | tf_op jit(solution)/shard_map/all_to_all | solution.py:372

commit v6 on v5

--- a/solution.py
+++ b/solution.py
@@ -587,7 +587,7 @@
             * chips,
             [out] * chips,
             [],
-            0,
+            50_000_000_000,
             1024,
             vmem=20,
         )(mine, sibling, after(w_own, *earlier), w_sibling, picked)
@@ -610,9 +610,10 @@
     grads[1], taps[1] = back(*groups[1], grads[0])
     parts[0] = partials(*groups[0], grads[0], grads[1])
     grads[2], taps[2] = back(*groups[2], *parts[0])
-    parts[1] = partials(*groups[1], grads[1], grads[2])
+    owns[0], moved[0] = deliver(parts[0], grads[2])
+    parts[1] = partials(*groups[1], grads[1], owns[0])
     parts[2] = partials(*groups[2], grads[2], *parts[1])
-    owns[0], moved[0] = deliver(parts[0], *parts[2])
+    owns[1], moved[1] = deliver(parts[1], *parts[2])
 
     slots = 3 * width + 16 * (width // shard)
     half = sds((seqs // 2, slots, shard), BF16)
@@ -632,16 +633,15 @@
         [whole(half.shape)] * 2,
         [half] * 2,
         [pltpu.VMEM((2 * width, model), F32)],
-        0,
+        50_000_000_000,
         1024,
-    )(parity, after(normed, owns[0]), w_out, *grads, *taps)
+    )(parity, after(normed, owns[1]), w_out, *grads, *taps)
     pairs = [(i, i ^ 1) for i in range(seqs)]
     others = lax.ppermute(send, "seq", pairs)
-    owns[1], moved[1] = deliver(parts[1], keep)
-    paired = (after(keep, owns[1]).astype(F32) + others.astype(F32)).astype(BF16)
+    owns[2], moved[2] = deliver(parts[2], keep)
+    paired = (after(keep, owns[2]).astype(F32) + others.astype(F32)).astype(BF16)
     same = [[i for i in range(seqs) if i % 2 == odd] for odd in range(2)]
     got = lax.all_to_all(paired, "seq", 0, 0, axis_index_groups=same, tiled=True)
-    owns[2], moved[2] = deliver(parts[2], paired)
     w_value, w_gate, w_out, grad_taps = call(
         functools.partial(finish_kernel, kernel),
         "finish",

time: 219 us -> 211 us (0.963)
  waiting for transfers between devices: 75 us -> 51 us
  blocking collectives: 0 us -> 19.9 us
  starting transfers between devices: 39.6 us -> 36.3 us
    all_to_all x0 -> x1, blocking collectives: none -> 19.9 us  [per_device(): lax.all_to_all(paired, 'seq', 0, 0, axis_index_groups=same, tiled=True)]
    all_to_all x5, waiting for transfers between devices: 41 us -> 25 us  [exchange(): return lax.all_to_all(copies, axis, 0, 0, tiled=True)]
    all_to_all x1 -> x0, waiting for transfers between devices: 10.7 us -> none  [per_device(): lax.all_to_all(paired, 'seq', 0, 0, axis_index_groups=same, tiled=True)]
    ppermute x3, waiting for transfers between devices: 6.02 us -> 13.6 us  [deliver(): total = total + lax.ppermute(part[d], 'tp', send).astype(F32)]
    all_to_all x1 -> x0, starting transfers between devices: 4.5 us -> none  [per_device(): lax.all_to_all(paired, 'seq', 0, 0, axis_index_groups=same, tiled=True)]
    ppermute x3, waiting for transfers between devices: 3.6 us -> 0.01 us  [partials(): sibling = lax.ppermute(mine, 'tp', swap)]
    unnamed x39 -> x35, local copies, waits for them, and re-layouts: 7.9 us -> 9.96 us
  transfers between devices with their start and end apart: 16 -> 15, of which waited for: 9 -> 7; matrix products, arithmetic and copies ran while one was open for 5% -> 6% of each run, Pallas kernels for 15% -> 21%
where the time goes in v6:
time: 211 us; the launch traced here: 209 us
  Pallas kernels  76.8 us (36%)
  waiting for transfers between devices  51 us (24%)
  starting transfers between devices  36.3 us (17%)
  blocking collectives  19.9 us (9%)
  local copies, waits for them, and re-layouts  12.9 us (6%)
  other arithmetic  10.9 us (5%)
    all_to_all x5, waiting for transfers between devices, exchange(): return lax.all_to_all(copies, axis, 0, 0, tiled=True)  25 us
    all_to_all x5, starting transfers between devices, exchange(): return lax.all_to_all(copies, axis, 0, 0, tiled=True)  23.6 us
    all_to_all x1, blocking collectives, per_device(): lax.all_to_all(paired, 'seq', 0, 0, axis_index_groups=same, tiled=True)  19.9 us
    pallas_call x3, Pallas kernels, back(): call(functools.partial(back_kernel, first, blocks), 'back_conv', (size *...  19.2 us
    pallas_call x1, Pallas kernels, per_device(): call(gate_kernel, 'gate_conv', (recs,), [smem(), per_record((frames, mode...  15.3 us
    ppermute x3, waiting for transfers between devices, deliver(): total = total + lax.ppermute(part[d], 'tp', send).astype(F32)  13.6 us
    pallas_call x1, Pallas kernels, per_device(): call(norm_kernel, 'swish_norm', (recs,), [smem(), smem(), whole((seqs, 2,...  12.1 us
    pallas_call x1, Pallas kernels, per_device(): call(functools.partial(outer_kernel, groups), 'outer_w_in', (recs,), [sme...  10.2 us
  transfers between devices with their start and end apart: 15, of which 7 were waited for; matrix products, arithmetic and copies ran while one was open for 6% of the time, Pallas kernels for 21%

profile of v6, /device:TPU:0, one launch (start us, length us, event | category | flops | bytes accessed | tf_op | source)
XLA Modules:
  0.0 209.4 jit_solution(1043350372829151862)
XLA Ops:
  0.6 1.0 fusion.1
  1.6 4.9 %collective-permute-start = (bf16[4,8,2048]{2,1,0:T(8,128)(2,1)S(1)}, bf16[4,8,2048]{2,1,0:T(8,128)(2,1)S(1)}, u32[]{:S(2)}, u32[]{:S(2)}) collective-permute-start(bf16[4,8,2048]{2,1,0:T(8,128)(2,1)S(1)} %pad_maximum_fusion.3), channel_id=1, source_target_pairs={{0,4},{4,8},{8,12},{12,16},{16,20},{20,24},{24,28},{1,5},{5,9},{9,... | collective-permute-start | bytes 393224 | tf_op jit(solution)/shard_map/ppermute | solution.py:412
  6.5 1.3 collective-permute-start.1
  7.8 1.3 fusion.5
  9.8 0.9 fusion.select
  10.8 2.6 %collective-permute-done.1 = bf16[4,8,2048]{2,1,0:T(8,128)(2,1)S(1)} collective-permute-done((bf16[4,8,2048]{2,1,0:T(8,128)(2,1)S(1)}, bf16[4,8,2048]{2,1,0:T(8,128)(2,1)S(1)}, u32[]{:S(2)}, u32[]{:S(2)}) %collective-permute-start.1) | collective-permute-done | bytes 131104 | tf_op jit(solution)/shard_map/ppermute | solution.py:412
  13.4 0.7 fusion.3
  14.1 15.3 %gate_conv.1 = (f32[4,1024,256]{2,1,0:T(8,128)}, f32[4,1024,256]{2,1,0:T(8,128)}, f32[4,1040,256]{2,1,0:T(8,128)}, f32[8,2,256]{2,1,0:T(2,128)}) custom-call(s32[2,4]{1,0:T(2,128)} %stack.35.meta, bf16[4,1024,1024]{2,1,0:T(8,128)(2,1)} %x.4, bf16[4,16,1024]{2,1,0:T(8,128)(2,1)} %get-tuple-element.90.halo, bf16[1024,256]{1,0:T(8,128)(2,1)} %wv.1, ...), custom_call_target="tpu_custom_call" | custom-call | flops 4294967296 | bytes 20971520 | tf_op jit(solution)/shard_map/gate_conv/pallas_call | solution.py:439
  29.4 5.7 %all-to-all-start = ((f32[8,2,256]{2,1,0:T(2,128)}), f32[8,2,256]{2,1,0:T(2,128)S(1)}, u32[]{:S(2)}, u32[]{:S(2)}) async-start(f32[8,2,256]{2,1,0:T(2,128)} %get-tuple-element.44), calls=%async_computation | async-start | bytes 32768 | tf_op jit(solution)/shard_map/all_to_all | solution.py:372
  36.4 5.3 %all-to-all-done.stats = f32[8,2,256]{2,1,0:T(2,128)S(1)} async-done(((f32[8,2,256]{2,1,0:T(2,128)}), f32[8,2,256]{2,1,0:T(2,128)S(1)}, u32[]{:S(2)}, u32[]{:S(2)}) %all-to-all-start) | async-done | bytes 16416 | tf_op jit(solution)/shard_map/all_to_all | solution.py:372
  42.3 12.1 %swish_norm.1 = (bf16[4,1024,256]{2,1,0:T(8,128)(2,1)}, f32[4,1040,256]{2,1,0:T(8,128)}, bf16[4,256,1024]{2,1,0:T(8,128)(2,1)}, f32[8,2,256]{2,1,0:T(2,128)}) custom-call(s32[2,4]{1,0:T(2,128)} %stack.35.meta, f32[1,1]{1,0:T(1,128)} %bitcast.1.count, f32[8,2,256]{2,1,0:T(2,128)} %copy-done.14, f32[2,256]{1,0:T(2,128)} %pad_maximum_fusion.5.affine, ...), custom_call_target="tpu_custom_call" | custom-call | flops 4294967296 | bytes 20971520 | tf_op jit(solution)/shard_map/swish_norm/pallas_call | solution.py:471
  54.4 3.3 %all-to-all-start.1 = ((f32[8,2,256]{2,1,0:T(2,128)}), f32[8,2,256]{2,1,0:T(2,128)S(1)}, u32[]{:S(2)}, u32[]{:S(2)}) async-start(f32[8,2,256]{2,1,0:T(2,128)} %get-tuple-element.46), calls=%async_computation.1 | async-start | bytes 32768 | tf_op jit(solution)/shard_map/all_to_all | solution.py:372
  57.7 7.0 %outer_w_out.1.w_out = f32[256,1024]{1,0:T(8,128)} custom-call(bf16[4,1024,1024]{2,1,0:T(8,128)(2,1)} %grads.3, bf16[4,1024,256]{2,1,0:T(8,128)(2,1)} %get-tuple-element.50.swished), custom_call_target="tpu_custom_call" | custom-call | flops 2147483648 | bytes 8388608 | tf_op jit(solution)/shard_map/outer_w_out/pallas_call | solution.py:516
  64.7 0.6 copy-done.12
  65.3 5.2 %back_conv.3 = (bf16[1024,512]{1,0:T(8,128)(2,1)}, f32[16,256]{1,0:T(8,128)}) custom-call(s32[2,4]{1,0:T(2,128)} %stack.35.meta, f32[1,1]{1,0:T(1,128)} %bitcast.1.count, f32[8,2,256]{2,1,0:T(2,128)} %copy-done.14, f32[8,2,256]{2,1,0:T(2,128)} %copy-done.12, f32[1,256]{1,0:T(1,128)} %bitcast.23, f32[4,1040,256]{2,1,0:T(8,128)} %get-tuple-element.47.gn, ...), custom_call_target="tpu_custom_call" | custom-call | bytes 1024 | tf_op jit(solution)/shard_map/back_conv/pallas_call | solution.py:540
  70.9 0.8 pad_maximum_fusion.2
  72.2 5.1 %back_conv.4 = (bf16[1024,512]{1,0:T(8,128)(2,1)}, f32[16,256]{1,0:T(8,128)}) custom-call(s32[2,4]{1,0:T(2,128)} %stack.35.meta, f32[1,1]{1,0:T(1,128)} %bitcast.1.count, f32[8,2,256]{2,1,0:T(2,128)} %copy-done.14, f32[8,2,256]{2,1,0:T(2,128)} %copy-done.12, f32[1,256]{1,0:T(1,128)} %bitcast.24, f32[4,1040,256]{2,1,0:T(8,128)} %get-tuple-element.47.gn, ...), custom_call_target="tpu_custom_call" | custom-call | bytes 1024 | tf_op jit(solution)/shard_map/back_conv/pallas_call | solution.py:540
  77.5 1.8 copy-done.7
  79.3 2.4 %partial_in.3 = (bf16[8,1,32,1024]{3,2,1,0:T(8,128)(2,1)S(1)}, bf16[8,1,32,1024]{3,2,1,0:T(8,128)(2,1)}) custom-call(bf16[1024,512]{1,0:T(8,128)(2,1)S(1)} %copy-done.3, bf16[1024,512]{1,0:T(8,128)(2,1)S(1)} %collective-permute-done.2.sibling, bf16[512,512]{1,0:T(8,128)(2,1)S(1)} %bitcast.19, bf16[512,512]{1,0:T(8,128)(2,1)S(1)} %collective-permute-done.3.w_sibling, ...), custom_call_target="tpu_custom_call" | custom-call | flops 49999998976 | bytes 1024 | tf_op jit(solution)/shard_map/partial_in/pallas_call | solution.py:569
  81.7 1.5 collective-permute-start.6
  83.2 8.9 %back_conv.5 = (bf16[2048,512]{1,0:T(8,128)(2,1)}, f32[16,256]{1,0:T(8,128)}) custom-call(s32[2,4]{1,0:T(2,128)} %stack.35.meta, f32[1,1]{1,0:T(1,128)} %bitcast.1.count, f32[8,2,256]{2,1,0:T(2,128)} %copy-done.14, f32[8,2,256]{2,1,0:T(2,128)} %copy-done.12, f32[1,256]{1,0:T(1,128)} %bitcast.25, f32[4,1040,256]{2,1,0:T(8,128)} %get-tuple-element.47.gn, ...), custom_call_target="tpu_custom_call" | custom-call | bytes 1024 | tf_op jit(solution)/shard_map/back_conv/pallas_call | solution.py:540
  92.2 4.0 %collective-permute-done.6 = bf16[8,1,32,1024]{3,2,1,0:T(8,128)(2,1)} collective-permute-done((bf16[8,1,32,1024]{3,2,1,0:T(8,128)(2,1)}, bf16[8,1,32,1024]{3,2,1,0:T(8,128)(2,1)}, u32[]{:S(2)}, u32[]{:S(2)}) %collective-permute-start.6) | collective-permute-done | bytes 524320 | tf_op jit(solution)/shard_map/ppermute | solution.py:599
  96.2 2.0 add_convert_fusion.3
  98.3 5.9 %all-to-all-start.4 = ((bf16[8,1,32,1024]{3,2,1,0:T(8,128)(2,1)}), bf16[8,1,32,1024]{3,2,1,0:T(8,128)(2,1)}, u32[]{:S(2)}, u32[]{:S(2)}) async-start(bf16[8,1,32,1024]{3,2,1,0:T(8,128)(2,1)} %add_convert_fusion.3), calls=%async_computation.4 | async-start | bytes 1048576 | tf_op jit(solution)/shard_map/all_to_all | solution.py:372
  104.2 1.4 copy-done.4
  105.6 1.0 copy-done.6
  106.6 1.6 copy-done.8
  108.2 2.7 %partial_in.4 = (bf16[8,1,32,1024]{3,2,1,0:T(8,128)(2,1)S(1)}, bf16[8,1,32,1024]{3,2,1,0:T(8,128)(2,1)S(1)}) custom-call(bf16[1024,512]{1,0:T(8,128)(2,1)S(1)} %copy-done.4, bf16[1024,512]{1,0:T(8,128)(2,1)} %collective-permute-done.5.sibling, bf16[512,512]{1,0:T(8,128)(2,1)S(1)} %bitcast.20, bf16[512,512]{1,0:T(8,128)(2,1)S(1)} %copy-done.6, ...), custom_call_target="tpu_custom_call" | custom-call | flops 49999998976 | bytes 1024 | tf_op jit(solution)/shard_map/partial_in/pallas_call | solution.py:569
  110.9 1.6 collective-permute-start.7
  112.5 1.3 copy-done.1
  113.8 1.6 copy-done.2
  115.4 3.4 %partial_in.5 = (bf16[8,2,32,1024]{3,2,1,0:T(8,128)(2,1)S(1)}, bf16[8,2,32,1024]{3,2,1,0:T(8,128)(2,1)S(1)}) custom-call(bf16[2048,512]{1,0:T(8,128)(2,1)S(1)} %copy-done, bf16[2048,512]{1,0:T(8,128)(2,1)S(1)} %copy-done.2, bf16[512,512]{1,0:T(8,128)(2,1)S(1)} %bitcast.21, bf16[512,512]{1,0:T(8,128)(2,1)S(1)} %copy-done.6, bf16[4,256,1024]{2,1,0:T(8,128)(2,1)S(1)} %copy-done.8), custom_call_target="tpu_custom_call" | custom-call | flops 49999998976 | bytes 1024 | tf_op jit(solution)/shard_map/partial_in/pallas_call | solution.py:569
  119.4 6.4 %collective-permute-done.7 = bf16[8,1,32,1024]{3,2,1,0:T(8,128)(2,1)S(1)} collective-permute-done((bf16[8,1,32,1024]{3,2,1,0:T(8,128)(2,1)S(1)}, bf16[8,1,32,1024]{3,2,1,0:T(8,128)(2,1)S(1)}, u32[]{:S(2)}, u32[]{:S(2)}) %collective-permute-start.7) | collective-permute-done | bytes 524320 | tf_op jit(solution)/shard_map/ppermute | solution.py:599
  125.9 1.0 add_convert_fusion.2
  126.9 10.2 %outer_w_in.1 = (bf16[4,800,128]{2,1,0:T(8,128)(2,1)}, bf16[4,800,128]{2,1,0:T(8,128)(2,1)}) custom-call(s32[1,1]{1,0:T(1,128)} %bitcast.11.parity, bf16[4,1024,1024]{2,1,0:T(8,128)(2,1)} %x.4, f32[256,1024]{1,0:T(8,128)} %outer_w_out.1.w_out, bf16[1024,512]{1,0:T(8,128)(2,1)} %get-tuple-element.52.own.refs_0_, ...), custom_call_target="tpu_custom_call" | custom-call | flops 49999998976 | bytes 1024 | tf_op jit(solution)/shard_map/outer_w_in/pallas_call | solution.py:620
  137.0 2.0 collective-permute-start.9
  139.0 4.6 %all-to-all-start.3 = ((bf16[8,1,32,1024]{3,2,1,0:T(8,128)(2,1)}), bf16[8,1,32,1024]{3,2,1,0:T(8,128)(2,1)S(1)}, u32[]{:S(2)}, u32[]{:S(2)}) async-start(bf16[8,1,32,1024]{3,2,1,0:T(8,128)(2,1)} %add_convert_fusion.2), calls=%async_computation.3 | async-start | bytes 1048576 | tf_op jit(solution)/shard_map/all_to_all | solution.py:372
  143.6 3.1 %collective-permute-done.8 = bf16[8,2,32,1024]{3,2,1,0:T(8,128)(2,1)} collective-permute-done((bf16[8,2,32,1024]{3,2,1,0:T(8,128)(2,1)S(1)}, bf16[8,2,32,1024]{3,2,1,0:T(8,128)(2,1)}, u32[]{:S(2)}, u32[]{:S(2)}) %collective-permute-start.8) | collective-permute-done | bytes 1048608 | tf_op jit(solution)/shard_map/ppermute | solution.py:599
  146.7 2.6 %add_convert_fusion = bf16[8,2,32,1024]{3,2,1,0:T(8,128)(2,1)} fusion(bf16[8,2,32,1024]{3,2,1,0:T(8,128)(2,1)} %collective-permute-done.8, bf16[8,2,32,1024]{3,2,1,0:T(8,128)(2,1)S(1)} %get-tuple-element.74), kind=kLoop, calls=%fused_computation | loop fusion | flops 2097152 | bytes 3145728 | tf_op jit(solution)/shard_map/convert_element_type | solution.py:600
  149.3 9.8 %collective-permute-done.9 = bf16[4,800,128]{2,1,0:T(8,128)(2,1)} collective-permute-done((bf16[4,800,128]{2,1,0:T(8,128)(2,1)}, bf16[4,800,128]{2,1,0:T(8,128)(2,1)}, u32[]{:S(2)}, u32[]{:S(2)}) %collective-permute-start.9) | collective-permute-done | bytes 819232 | tf_op jit(solution)/shard_map/ppermute | solution.py:640
  159.2 1.4 add_convert_fusion.1
  160.6 19.9 %all_to_all.30.got = bf16[4,800,128]{2,1,0:T(8,128)(2,1)S(1)} all-to-all(bf16[4,800,128]{2,1,0:T(8,128)(2,1)S(1)} %add_convert_fusion.1), channel_id=1, replica_groups={{0,8,16,24},{4,12,20,28},{1,9,17,25},{5,13,21,29},{2,10,18,26},{6,14,22..., dimensions={0} | all-to-all | bytes 1638400 | tf_op jit(solution)/shard_map/all_to_all | solution.py:644
  180.4 4.1 %all-to-all-start.2 = ((bf16[8,2,32,1024]{3,2,1,0:T(8,128)(2,1)}), bf16[8,2,32,1024]{3,2,1,0:T(8,128)(2,1)S(1)}, u32[]{:S(2)}, u32[]{:S(2)}) async-start(bf16[8,2,32,1024]{3,2,1,0:T(8,128)(2,1)} %add_convert_fusion), calls=%async_computation.2 | async-start | bytes 2097152 | tf_op jit(solution)/shard_map/all_to_all | solution.py:372
  185.1 1.9 place.3.refs_0_
  186.9 0.8 place.4.refs_0_
  187.8 0.8 finish.1
  188.6 19.7 %all-to-all-done.2.moved = bf16[8,2,32,1024]{3,2,1,0:T(8,128)(2,1)S(1)} async-done(((bf16[8,2,32,1024]{3,2,1,0:T(8,128)(2,1)}), bf16[8,2,32,1024]{3,2,1,0:T(8,128)(2,1)S(1)}, u32[]{:S(2)}, u32[]{:S(2)}) %all-to-all-start.2) | async-done | bytes 1048608 | tf_op jit(solution)/shard_map/all_to_all | solution.py:372
  208.3 1.1 place.5
  (54 shorter events, 4.3 us)
Async XLA Ops:
  1.6 9.2 %collective-permute-start = (bf16[4,8,2048]{2,1,0:T(8,128)(2,1)S(1)}, bf16[4,8,2048]{2,1,0:T(8,128)(2,1)S(1)}, u32[]{:S(2)}, u32[]{:S(2)}) collective-permute-start(bf16[4,8,2048]{2,1,0:T(8,128)(2,1)S(1)} %pad_maximum_fusion.3), channel_id=1, source_target_pairs={{0,4},{4,8},{8,12},{12,16},{16,20},{20,24},{24,28},{1,5},{5,9},{9,... | collective-permute-start | bytes 393224 | tf_op jit(solution)/shard_map/ppermute | solution.py:412
  6.5 6.9 %collective-permute-start.1 = (bf16[4,8,2048]{2,1,0:T(8,128)(2,1)S(1)}, bf16[4,8,2048]{2,1,0:T(8,128)(2,1)S(1)}, u32[]{:S(2)}, u32[]{:S(2)}) collective-permute-start(bf16[4,8,2048]{2,1,0:T(8,128)(2,1)S(1)} %pad_maximum_fusion.4), channel_id=1, source_target_pairs={{4,0},{8,4},{12,8},{16,12},{20,16},{24,20},{28,24},{5,1},{9,5},{13... | collective-permute-start | bytes 393224 | tf_op jit(solution)/shard_map/ppermute | solution.py:412
  14.1 21.0 %copy-start.15 = (f32[256]{0:T(256)S(1)}, f32[256]{0:T(256)}, u32[]{:S(2)}) copy-start(f32[256]{0:T(256)} %param.14) | copy-start | bytes 3076
  14.1 21.0 %copy-start.16 = (f32[256]{0:T(256)S(1)}, f32[256]{0:T(256)}, u32[]{:S(2)}) copy-start(f32[256]{0:T(256)} %param.15) | copy-start | bytes 3076
  29.4 12.3 %all-to-all-start = ((f32[8,2,256]{2,1,0:T(2,128)}), f32[8,2,256]{2,1,0:T(2,128)S(1)}, u32[]{:S(2)}, u32[]{:S(2)}) async-start(f32[8,2,256]{2,1,0:T(2,128)} %get-tuple-element.44), calls=%async_computation | async-start | bytes 32768 | tf_op jit(solution)/shard_map/all_to_all | solution.py:372
  41.7 0.6 copy-start.14
  54.4 10.4 %all-to-all-start.1 = ((f32[8,2,256]{2,1,0:T(2,128)}), f32[8,2,256]{2,1,0:T(2,128)S(1)}, u32[]{:S(2)}, u32[]{:S(2)}) async-start(f32[8,2,256]{2,1,0:T(2,128)} %get-tuple-element.46), calls=%async_computation.1 | async-start | bytes 32768 | tf_op jit(solution)/shard_map/all_to_all | solution.py:372
  64.7 0.6 copy-start.12
  65.3 5.3 %copy-start.10 = (bf16[1024,256]{1,0:T(8,128)(2,1)S(1)}, bf16[1024,256]{1,0:T(8,128)(2,1)}, u32[]{:S(2)}) copy-start(bf16[1024,256]{1,0:T(8,128)(2,1)} %wv.1) | copy-start | bytes 1572868
  65.3 5.4 %copy-start.11 = (bf16[1024,256]{1,0:T(8,128)(2,1)S(1)}, bf16[1024,256]{1,0:T(8,128)(2,1)}, u32[]{:S(2)}) copy-start(bf16[1024,256]{1,0:T(8,128)(2,1)} %wg.1) | copy-start | bytes 1572868
  70.5 7.0 %collective-permute-start.2 = (bf16[1024,512]{1,0:T(8,128)(2,1)}, bf16[1024,512]{1,0:T(8,128)(2,1)S(1)}, u32[]{:S(2)}, u32[]{:S(2)}) collective-permute-start(bf16[1024,512]{1,0:T(8,128)(2,1)} %get-tuple-element.52.own.refs_0_), channel_id=1, source_target_pairs={{0,1},{1,0},{2,3},{3,2},{4,5},{5,4},{6,7},{7,6},{8,9},{9,8},{10,11... | collective-permute-start | bytes 3145736 | tf_op jit(solution)/shard_map/ppermute | solution.py:567
  71.7 5.8 %collective-permute-start.3 = (bf16[512,512]{1,0:T(8,128)(2,1)}, bf16[512,512]{1,0:T(8,128)(2,1)S(1)}, u32[]{:S(2)}, u32[]{:S(2)}) collective-permute-start(bf16[512,512]{1,0:T(8,128)(2,1)} %bitcast.10), channel_id=1, source_target_pairs={{0,1},{1,0},{2,3},{3,2},{4,5},{5,4},{6,7},{7,6},{8,9},{9,8},{10,11... | collective-permute-start | bytes 1572872 | tf_op jit(solution)/shard_map/ppermute | solution.py:427
  72.2 5.3 %copy-start.3 = (bf16[1024,512]{1,0:T(8,128)(2,1)S(1)}, bf16[1024,512]{1,0:T(8,128)(2,1)}, u32[]{:S(2)}) copy-start(bf16[1024,512]{1,0:T(8,128)(2,1)} %get-tuple-element.52.own.refs_0_) | copy-start | bytes 3145732
  77.3 26.9 %collective-permute-start.5 = (bf16[1024,512]{1,0:T(8,128)(2,1)}, bf16[1024,512]{1,0:T(8,128)(2,1)}, u32[]{:S(2)}, u32[]{:S(2)}) collective-permute-start(bf16[1024,512]{1,0:T(8,128)(2,1)} %get-tuple-element.54.own.refs_1_), channel_id=1, source_target_pairs={{0,1},{1,0},{2,3},{3,2},{4,5},{5,4},{6,7},{7,6},{8,9},{9,8},{10,11... | collective-permute-start | bytes 3145736 | tf_op jit(solution)/shard_map/ppermute | solution.py:567
  77.5 4.2 %copy-start.5 = (bf16[512,512]{1,0:T(8,128)(2,1)}, bf16[512,512]{1,0:T(8,128)(2,1)S(1)}, u32[]{:S(2)}) copy-start(bf16[512,512]{1,0:T(8,128)(2,1)S(1)} %collective-permute-done.3.w_sibling) | copy-start | bytes 1572868
  77.5 1.8 copy-start.7
  81.7 14.6 %collective-permute-start.6 = (bf16[8,1,32,1024]{3,2,1,0:T(8,128)(2,1)}, bf16[8,1,32,1024]{3,2,1,0:T(8,128)(2,1)}, u32[]{:S(2)}, u32[]{:S(2)}) collective-permute-start(bf16[8,1,32,1024]{3,2,1,0:T(8,128)(2,1)} %get-tuple-element.58), channel_id=1, source_target_pairs={{0,2},{1,3},{2,0},{3,1},{4,6},{5,7},{6,4},{7,5},{8,10},{9,11},{10,... | collective-permute-start | bytes 1572872 | tf_op jit(solution)/shard_map/ppermute | solution.py:599
  92.0 20.4 %collective-permute-start.4 = (bf16[2048,512]{1,0:T(8,128)(2,1)}, bf16[2048,512]{1,0:T(8,128)(2,1)S(1)}, u32[]{:S(2)}, u32[]{:S(2)}) collective-permute-start(bf16[2048,512]{1,0:T(8,128)(2,1)} %get-tuple-element.60.own.refs_2_), channel_id=1, source_target_pairs={{0,1},{1,0},{2,3},{3,2},{4,5},{5,4},{6,7},{7,6},{8,9},{9,8},{10,11... | collective-permute-start | bytes 6291464 | tf_op jit(solution)/shard_map/ppermute | solution.py:567
  98.3 40.8 %all-to-all-start.4 = ((bf16[8,1,32,1024]{3,2,1,0:T(8,128)(2,1)}), bf16[8,1,32,1024]{3,2,1,0:T(8,128)(2,1)}, u32[]{:S(2)}, u32[]{:S(2)}) async-start(bf16[8,1,32,1024]{3,2,1,0:T(8,128)(2,1)} %add_convert_fusion.3), calls=%async_computation.4 | async-start | bytes 1048576 | tf_op jit(solution)/shard_map/all_to_all | solution.py:372
  104.2 9.6 %copy-start = (bf16[2048,512]{1,0:T(8,128)(2,1)S(1)}, bf16[2048,512]{1,0:T(8,128)(2,1)}, u32[]{:S(2)}) copy-start(bf16[2048,512]{1,0:T(8,128)(2,1)} %get-tuple-element.60.own.refs_2_) | copy-start | bytes 6291460
  104.2 1.4 copy-start.4
  105.6 1.0 copy-start.6
  106.6 1.6 copy-start.8
  110.9 14.9 %collective-permute-start.7 = (bf16[8,1,32,1024]{3,2,1,0:T(8,128)(2,1)S(1)}, bf16[8,1,32,1024]{3,2,1,0:T(8,128)(2,1)S(1)}, u32[]{:S(2)}, u32[]{:S(2)}) collective-permute-start(bf16[8,1,32,1024]{3,2,1,0:T(8,128)(2,1)S(1)} %get-tuple-element.64), channel_id=1, source_target_pairs={{0,2},{1,3},{2,0},{3,1},{4,6},{5,7},{6,4},{7,5},{8,10},{9,11},{10,... | collective-permute-start | bytes 1572872 | tf_op jit(solution)/shard_map/ppermute | solution.py:599
  112.5 1.3 copy-start.1
  113.8 1.6 copy-start.2
  118.8 27.9 %collective-permute-start.8 = (bf16[8,2,32,1024]{3,2,1,0:T(8,128)(2,1)S(1)}, bf16[8,2,32,1024]{3,2,1,0:T(8,128)(2,1)}, u32[]{:S(2)}, u32[]{:S(2)}) collective-permute-start(bf16[8,2,32,1024]{3,2,1,0:T(8,128)(2,1)S(1)} %get-tuple-element.67), channel_id=1, source_target_pairs={{0,2},{1,3},{2,0},{3,1},{4,6},{5,7},{6,4},{7,5},{8,10},{9,11},{10,... | collective-permute-start | bytes 3145736 | tf_op jit(solution)/shard_map/ppermute | solution.py:599
  137.0 22.1 %copy-start.9 = (bf16[4,800,128]{2,1,0:T(8,128)(2,1)S(1)}, bf16[4,800,128]{2,1,0:T(8,128)(2,1)}, u32[]{:S(2)}) copy-start(bf16[4,800,128]{2,1,0:T(8,128)(2,1)} %get-tuple-element.75) | copy-start | bytes 2457604
  137.0 22.1 %collective-permute-start.9 = (bf16[4,800,128]{2,1,0:T(8,128)(2,1)}, bf16[4,800,128]{2,1,0:T(8,128)(2,1)}, u32[]{:S(2)}, u32[]{:S(2)}) collective-permute-start(bf16[4,800,128]{2,1,0:T(8,128)(2,1)} %get-tuple-element.76), channel_id=1, source_target_pairs={{0,4},{4,0},{8,12},{12,8},{16,20},{20,16},{24,28},{28,24},{1,5},{5... | collective-permute-start | bytes 2457608 | tf_op jit(solution)/shard_map/ppermute | solution.py:640
  139.0 21.5 %all-to-all-start.3 = ((bf16[8,1,32,1024]{3,2,1,0:T(8,128)(2,1)}), bf16[8,1,32,1024]{3,2,1,0:T(8,128)(2,1)S(1)}, u32[]{:S(2)}, u32[]{:S(2)}) async-start(bf16[8,1,32,1024]{3,2,1,0:T(8,128)(2,1)} %add_convert_fusion.2), calls=%async_computation.3 | async-start | bytes 1048576 | tf_op jit(solution)/shard_map/all_to_all | solution.py:372
  160.5 23.9 %copy-start.13 = (f32[8,2,256]{2,1,0:T(2,128)S(1)}, f32[8,2,256]{2,1,0:T(2,128)}, u32[]{:S(2)}) copy-start(f32[8,2,256]{2,1,0:T(2,128)} %copy-done.12) | copy-start | bytes 49156
  180.4 27.9 %all-to-all-start.2 = ((bf16[8,2,32,1024]{3,2,1,0:T(8,128)(2,1)}), bf16[8,2,32,1024]{3,2,1,0:T(8,128)(2,1)S(1)}, u32[]{:S(2)}, u32[]{:S(2)}) async-start(bf16[8,2,32,1024]{3,2,1,0:T(8,128)(2,1)} %add_convert_fusion), calls=%async_computation.2 | async-start | bytes 2097152 | tf_op jit(solution)/shard_map/all_to_all | solution.py:372

commit v7 on v6

--- a/solution.py
+++ b/solution.py
@@ -68,7 +68,7 @@
 
 
 def call(
-    kernel, name, grid, in_specs, out_specs, out_shape, scratch, flops, moved, aliases=None, vmem=60
+    kernel, name, grid, in_specs, out_specs, out_shape, scratch, flops, moved, aliases=None, vmem=63
 ):
     return pl.pallas_call(
         kernel,
@@ -288,6 +288,13 @@
         other[...] = (
             total[(d + 1) * rows : (d + 2) * rows].astype(BF16).reshape(seqs, 1, piece, frames)
         )
+
+
+def add_kernel(*refs):
+    total = refs[0][...].astype(F32)
+    for other in refs[1:-1]:
+        total = total + other[...].astype(F32)
+    refs[-1][...] = total.astype(BF16)
 
 
 def first_outer_kernel(grads, swished, out):
@@ -587,17 +594,30 @@
             * chips,
             [out] * chips,
             [],
+            0,
+            1024,
+        )(mine, sibling, after(w_own, *earlier), w_sibling, picked)
+
+    def deliver(part, *earlier):
+        arrived = []
+        for d in range(1, chips):
+            send = [(i, ((i // 2 + d) % chips) * 2 + i % 2) for i in range(tps)]
+            arrived.append(lax.ppermute(part[d], "tp", send))
+        size = part[0].shape[1]
+        block = pl.BlockSpec(
+            (seqs, 1, piece, half_rows), lambda i: (0, i // parts_in, 0, i % parts_in)
+        )
+        own = call(
+            add_kernel,
+            "add",
+            (size * parts_in,),
+            [block] * chips,
+            block,
+            sds(part[0].shape, BF16),
+            [],
             50_000_000_000,
             1024,
-            vmem=20,
-        )(mine, sibling, after(w_own, *earlier), w_sibling, picked)
-
-    def deliver(part, *earlier):
-        total = after(part[0], *earlier).astype(F32)
-        for d in range(1, chips):
-            send = [(i, ((i // 2 + d) % chips) * 2 + i % 2) for i in range(tps)]
-            total = total + lax.ppermute(part[d], "tp", send).astype(F32)
-        own = total.astype(BF16)
+        )(after(part[0], *earlier), *arrived)
         return own, exchange(own, "seq")
 
     groups = ((0, 1), (1, 1), (2, recs - 2))
@@ -610,9 +630,9 @@
     grads[1], taps[1] = back(*groups[1], grads[0])
     parts[0] = partials(*groups[0], grads[0], grads[1])
     grads[2], taps[2] = back(*groups[2], *parts[0])
-    owns[0], moved[0] = deliver(parts[0], grads[2])
-    parts[1] = partials(*groups[1], grads[1], owns[0])
-    parts[2] = partials(*groups[2], grads[2], *parts[1])
+    parts[1] = partials(*groups[1], grads[1], grads[2])
+    owns[0], moved[0] = deliver(parts[0], *parts[1])
+    parts[2] = partials(*groups[2], grads[2], owns[0])
     owns[1], moved[1] = deliver(parts[1], *parts[2])
 
     slots = 3 * width + 16 * (width // shard)
@@ -641,7 +661,7 @@
     owns[2], moved[2] = deliver(parts[2], keep)
     paired = (after(keep, owns[2]).astype(F32) + others.astype(F32)).astype(BF16)
     same = [[i for i in range(seqs) if i % 2 == odd] for odd in range(2)]
-    got = lax.all_to_all(paired, "seq", 0, 0, axis_index_groups=same, tiled=True)
+    got = lax.all_to_all(after(paired, moved[2]), "seq", 0, 0, axis_index_groups=same, tiled=True)
     w_value, w_gate, w_out, grad_taps = call(
         functools.partial(finish_kernel, kernel),
         "finish",

time: 211 us -> 221 us (1.047)
  waiting for transfers between devices: 51 us -> 72.5 us
  blocking collectives: 19.9 us -> 0 us
  Pallas kernels: 76.8 us -> 90.8 us
  local copies, waits for them, and re-layouts: 12.9 us -> 6.56 us
  starting transfers between devices: 36.3 us -> 40.3 us
  other arithmetic: 10.9 us -> 7.9 us
    all_to_all x1 -> x0, blocking collectives: 19.9 us -> none  [per_device(): lax.all_to_all(paired, 'seq', 0, 0, axis_index_groups=same, tiled=True)]
    all_to_all x0 -> x1, waiting for transfers between devices: none -> 15.4 us  [per_device(): lax.all_to_all(after(paired, moved[2]), 'seq', 0, 0, axis_index_groups=sa...]
    all_to_all x5, waiting for transfers between devices: 25 us -> 40 us  [exchange(): return lax.all_to_all(copies, axis, 0, 0, tiled=True)]
    ppermute x1, waiting for transfers between devices: 9.82 us -> 1.64 us  [per_device(): others = lax.ppermute(send, 'seq', pairs)]
    pallas_call x0 -> x3, Pallas kernels: none -> 7.63 us  [deliver(): call(add_kernel, 'add', (size * parts_in,), [block] * chips, block, sds(p...]
    unnamed x35 -> x19, local copies, waits for them, and re-layouts: 9.96 us -> 2.87 us
    pallas_call x3, Pallas kernels: 8.43 us -> 15 us  [partials(): call(partial_kernel, 'partial_in', (size * parts_in,), [pl.BlockSpec((hal...]
    convert_element_type x3 -> x0, other arithmetic: 5.65 us -> none  [deliver(): own = total.astype(BF16)]
  transfers between devices with their start and end apart: 15 -> 16, of which waited for: 7 -> 8; matrix products, arithmetic and copies ran while one was open for 6% -> 5% of each run, Pallas kernels for 21% -> 26%
where the time goes in v7:
time: 221 us; the launch traced here: 220 us
  Pallas kernels  90.8 us (41%)
  waiting for transfers between devices  72.5 us (33%)
  starting transfers between devices  40.3 us (18%)
  other arithmetic  7.9 us (4%)
  local copies, waits for them, and re-layouts  6.56 us (3%)
    all_to_all x5, waiting for transfers between devices, exchange(): return lax.all_to_all(copies, axis, 0, 0, tiled=True)  40 us
    all_to_all x5, starting transfers between devices, exchange(): return lax.all_to_all(copies, axis, 0, 0, tiled=True)  24.3 us
    pallas_call x3, Pallas kernels, back(): call(functools.partial(back_kernel, first, blocks), 'back_conv', (size *...  19 us
    all_to_all x1, waiting for transfers between devices, per_device(): lax.all_to_all(after(paired, moved[2]), 'seq', 0, 0, axis_index_groups=sa...  15.4 us
    pallas_call x1, Pallas kernels, per_device(): call(gate_kernel, 'gate_conv', (recs,), [smem(), per_record((frames, mode...  15.3 us
    pallas_call x3, Pallas kernels, partials(): call(partial_kernel, 'partial_in', (size * parts_in,), [pl.BlockSpec((hal...  15 us
    pallas_call x1, Pallas kernels, per_device(): call(norm_kernel, 'swish_norm', (recs,), [smem(), smem(), whole((seqs, 2,...  12.1 us
    ppermute x3, waiting for transfers between devices, deliver(): arrived.append(lax.ppermute(part[d], 'tp', send))  11.6 us
  transfers between devices with their start and end apart: 16, of which 8 were waited for; matrix products, arithmetic and copies ran while one was open for 5% of the time, Pallas kernels for 26%

profile of v7, /device:TPU:0, one launch (start us, length us, event | category | flops | bytes accessed | tf_op | source)
XLA Modules:
  0.0 219.6 jit_solution(7778865539207917357)
XLA Ops:
  0.6 1.0 fusion.1
  1.6 4.9 %collective-permute-start = (bf16[4,8,2048]{2,1,0:T(8,128)(2,1)S(1)}, bf16[4,8,2048]{2,1,0:T(8,128)(2,1)S(1)}, u32[]{:S(2)}, u32[]{:S(2)}) collective-permute-start(bf16[4,8,2048]{2,1,0:T(8,128)(2,1)S(1)} %pad_maximum_fusion.3), channel_id=1, source_target_pairs={{0,4},{4,8},{8,12},{12,16},{16,20},{20,24},{24,28},{1,5},{5,9},{9,... | collective-permute-start | bytes 393224 | tf_op jit(solution)/shard_map/ppermute | solution.py:419
  6.5 1.3 collective-permute-start.1
  7.8 1.3 fusion.5
  9.8 1.0 fusion.select
  10.8 2.6 %collective-permute-done.1 = bf16[4,8,2048]{2,1,0:T(8,128)(2,1)S(1)} collective-permute-done((bf16[4,8,2048]{2,1,0:T(8,128)(2,1)S(1)}, bf16[4,8,2048]{2,1,0:T(8,128)(2,1)S(1)}, u32[]{:S(2)}, u32[]{:S(2)}) %collective-permute-start.1) | collective-permute-done | bytes 131104 | tf_op jit(solution)/shard_map/ppermute | solution.py:419
  13.4 0.7 fusion.3
  14.1 15.3 %gate_conv.1 = (f32[4,1024,256]{2,1,0:T(8,128)}, f32[4,1024,256]{2,1,0:T(8,128)}, f32[4,1040,256]{2,1,0:T(8,128)}, f32[8,2,256]{2,1,0:T(2,128)}) custom-call(s32[2,4]{1,0:T(2,128)} %stack.35.meta, bf16[4,1024,1024]{2,1,0:T(8,128)(2,1)} %x.4, bf16[4,16,1024]{2,1,0:T(8,128)(2,1)} %get-tuple-element.92.halo, bf16[1024,256]{1,0:T(8,128)(2,1)} %wv.1, ...), custom_call_target="tpu_custom_call" | custom-call | flops 4294967296 | bytes 20971520 | tf_op jit(solution)/shard_map/gate_conv/pallas_call | solution.py:446
  29.4 5.7 %all-to-all-start = ((f32[8,2,256]{2,1,0:T(2,128)}), f32[8,2,256]{2,1,0:T(2,128)S(1)}, u32[]{:S(2)}, u32[]{:S(2)}) async-start(f32[8,2,256]{2,1,0:T(2,128)} %get-tuple-element.45), calls=%async_computation | async-start | bytes 32768 | tf_op jit(solution)/shard_map/all_to_all | solution.py:379
  36.4 5.3 %all-to-all-done.stats = f32[8,2,256]{2,1,0:T(2,128)S(1)} async-done(((f32[8,2,256]{2,1,0:T(2,128)}), f32[8,2,256]{2,1,0:T(2,128)S(1)}, u32[]{:S(2)}, u32[]{:S(2)}) %all-to-all-start) | async-done | bytes 16416 | tf_op jit(solution)/shard_map/all_to_all | solution.py:379
  42.3 12.1 %swish_norm.1 = (bf16[4,1024,256]{2,1,0:T(8,128)(2,1)}, f32[4,1040,256]{2,1,0:T(8,128)}, bf16[4,256,1024]{2,1,0:T(8,128)(2,1)}, f32[8,2,256]{2,1,0:T(2,128)}) custom-call(s32[2,4]{1,0:T(2,128)} %stack.35.meta, f32[1,1]{1,0:T(1,128)} %bitcast.1.count, f32[8,2,256]{2,1,0:T(2,128)} %copy-done.5, f32[2,256]{1,0:T(2,128)} %pad_maximum_fusion.5.affine, ...), custom_call_target="tpu_custom_call" | custom-call | flops 4294967296 | bytes 20971520 | tf_op jit(solution)/shard_map/swish_norm/pallas_call | solution.py:478
  54.4 3.3 %all-to-all-start.1 = ((f32[8,2,256]{2,1,0:T(2,128)}), f32[8,2,256]{2,1,0:T(2,128)S(1)}, u32[]{:S(2)}, u32[]{:S(2)}) async-start(f32[8,2,256]{2,1,0:T(2,128)} %get-tuple-element.47), calls=%async_computation.1 | async-start | bytes 32768 | tf_op jit(solution)/shard_map/all_to_all | solution.py:379
  57.7 7.0 %outer_w_out.1.w_out = f32[256,1024]{1,0:T(8,128)} custom-call(bf16[4,1024,1024]{2,1,0:T(8,128)(2,1)} %grads.3, bf16[4,1024,256]{2,1,0:T(8,128)(2,1)} %get-tuple-element.51.swished), custom_call_target="tpu_custom_call" | custom-call | flops 2147483648 | bytes 8388608 | tf_op jit(solution)/shard_map/outer_w_out/pallas_call | solution.py:523
  64.7 0.6 copy-done.3
  65.3 5.1 %back_conv.3 = (bf16[1024,512]{1,0:T(8,128)(2,1)}, f32[16,256]{1,0:T(8,128)}) custom-call(s32[2,4]{1,0:T(2,128)} %stack.35.meta, f32[1,1]{1,0:T(1,128)} %bitcast.1.count, f32[8,2,256]{2,1,0:T(2,128)} %copy-done.5, f32[8,2,256]{2,1,0:T(2,128)} %copy-done.3, f32[1,256]{1,0:T(1,128)} %bitcast.24, f32[4,1040,256]{2,1,0:T(8,128)} %get-tuple-element.48.gn, ...), custom_call_target="tpu_custom_call" | custom-call | bytes 1024 | tf_op jit(solution)/shard_map/back_conv/pallas_call | solution.py:547
  70.6 1.1 pad_maximum_fusion
  71.7 0.8 dynamic-slice_bitcast_fusion.1
  72.5 0.8 pad_maximum_fusion.2
  73.4 5.0 %back_conv.4 = (bf16[1024,512]{1,0:T(8,128)(2,1)}, f32[16,256]{1,0:T(8,128)}) custom-call(s32[2,4]{1,0:T(2,128)} %stack.35.meta, f32[1,1]{1,0:T(1,128)} %bitcast.1.count, f32[8,2,256]{2,1,0:T(2,128)} %copy-done.5, f32[8,2,256]{2,1,0:T(2,128)} %copy-done.3, f32[1,256]{1,0:T(1,128)} %bitcast.25, f32[4,1040,256]{2,1,0:T(8,128)} %get-tuple-element.48.gn, ...), custom_call_target="tpu_custom_call" | custom-call | bytes 1024 | tf_op jit(solution)/shard_map/back_conv/pallas_call | solution.py:547
  79.0 1.9 pad_maximum_fusion.1
  80.8 1.3 collective-permute-done.3.w_sibling
  82.1 0.8 copy-done
  83.0 4.2 %partial_in.3 = (bf16[8,1,32,1024]{3,2,1,0:T(8,128)(2,1)}, bf16[8,1,32,1024]{3,2,1,0:T(8,128)(2,1)}) custom-call(bf16[1024,512]{1,0:T(8,128)(2,1)} %get-tuple-element.53.own.refs_0_, bf16[1024,512]{1,0:T(8,128)(2,1)} %collective-permute-done.2.sibling, bf16[512,512]{1,0:T(8,128)(2,1)} %bitcast.19, bf16[512,512]{1,0:T(8,128)(2,1)} %copy-done, ...), custom_call_target="tpu_custom_call" | custom-call | bytes 1024 | tf_op jit(solution)/shard_map/partial_in/pallas_call | solution.py:576
  87.2 1.5 collective-permute-start.6
  88.7 8.9 %back_conv.5 = (bf16[2048,512]{1,0:T(8,128)(2,1)}, f32[16,256]{1,0:T(8,128)}) custom-call(s32[2,4]{1,0:T(2,128)} %stack.35.meta, f32[1,1]{1,0:T(1,128)} %bitcast.1.count, f32[8,2,256]{2,1,0:T(2,128)} %copy-done.5, f32[8,2,256]{2,1,0:T(2,128)} %copy-done.3, f32[1,256]{1,0:T(1,128)} %bitcast.26, f32[4,1040,256]{2,1,0:T(8,128)} %get-tuple-element.48.gn, ...), custom_call_target="tpu_custom_call" | custom-call | bytes 1024 | tf_op jit(solution)/shard_map/back_conv/pallas_call | solution.py:547
  97.7 4.3 %partial_in.4 = (bf16[8,1,32,1024]{3,2,1,0:T(8,128)(2,1)}, bf16[8,1,32,1024]{3,2,1,0:T(8,128)(2,1)}) custom-call(bf16[1024,512]{1,0:T(8,128)(2,1)} %get-tuple-element.55.own.refs_1_, bf16[1024,512]{1,0:T(8,128)(2,1)} %collective-permute-done.5.sibling, bf16[512,512]{1,0:T(8,128)(2,1)} %bitcast.20, bf16[512,512]{1,0:T(8,128)(2,1)} %copy-done, ...), custom_call_target="tpu_custom_call" | custom-call | bytes 1024 | tf_op jit(solution)/shard_map/partial_in/pallas_call | solution.py:576
  102.5 0.8 copy-done.8
  103.3 2.0 add.110
  105.3 5.9 %all-to-all-start.4 = ((bf16[8,1,32,1024]{3,2,1,0:T(8,128)(2,1)}), bf16[8,1,32,1024]{3,2,1,0:T(8,128)(2,1)}, u32[]{:S(2)}, u32[]{:S(2)}) async-start(bf16[8,1,32,1024]{3,2,1,0:T(8,128)(2,1)} %add.110), calls=%async_computation.4 | async-start | bytes 1048576 | tf_op jit(solution)/shard_map/all_to_all | solution.py:379
  111.2 6.5 %partial_in.5 = (bf16[8,2,32,1024]{3,2,1,0:T(8,128)(2,1)}, bf16[8,2,32,1024]{3,2,1,0:T(8,128)(2,1)}) custom-call(bf16[2048,512]{1,0:T(8,128)(2,1)} %get-tuple-element.61.own.refs_2_, bf16[2048,512]{1,0:T(8,128)(2,1)} %collective-permute-done.4.sibling, bf16[512,512]{1,0:T(8,128)(2,1)} %bitcast.21, bf16[512,512]{1,0:T(8,128)(2,1)} %copy-done, ...), custom_call_target="tpu_custom_call" | custom-call | bytes 1024 | tf_op jit(solution)/shard_map/partial_in/pallas_call | solution.py:576
  117.7 1.5 collective-permute-start.8
  119.2 2.0 add.111
  121.2 10.2 %outer_w_in.1 = (bf16[4,800,128]{2,1,0:T(8,128)(2,1)}, bf16[4,800,128]{2,1,0:T(8,128)(2,1)}) custom-call(s32[1,1]{1,0:T(1,128)} %bitcast.11.parity, bf16[4,1024,1024]{2,1,0:T(8,128)(2,1)} %x.4, f32[256,1024]{1,0:T(8,128)} %outer_w_out.1.w_out, bf16[1024,512]{1,0:T(8,128)(2,1)} %get-tuple-element.53.own.refs_0_, ...), custom_call_target="tpu_custom_call" | custom-call | flops 49999998976 | bytes 1024 | tf_op jit(solution)/shard_map/outer_w_in/pallas_call | solution.py:640
  131.4 11.6 %collective-permute-done.8.refs_1_ = bf16[8,2,32,1024]{3,2,1,0:T(8,128)(2,1)} collective-permute-done((bf16[8,2,32,1024]{3,2,1,0:T(8,128)(2,1)}, bf16[8,2,32,1024]{3,2,1,0:T(8,128)(2,1)}, u32[]{:S(2)}, u32[]{:S(2)}) %collective-permute-start.8) | collective-permute-done | bytes 1048608 | tf_op jit(solution)/shard_map/ppermute | solution.py:605
  143.0 3.6 %add.112 = bf16[8,2,32,1024]{3,2,1,0:T(8,128)(2,1)} custom-call(bf16[8,2,32,1024]{3,2,1,0:T(8,128)(2,1)} %get-tuple-element.75.refs_0_, bf16[8,2,32,1024]{3,2,1,0:T(8,128)(2,1)} %collective-permute-done.8.refs_1_), custom_call_target="tpu_custom_call" | custom-call | flops 49999998976 | bytes 1024 | tf_op jit(solution)/shard_map/add/pallas_call | solution.py:610
  146.7 5.8 %all-to-all-start.2 = ((bf16[8,2,32,1024]{3,2,1,0:T(8,128)(2,1)}), bf16[8,2,32,1024]{3,2,1,0:T(8,128)(2,1)S(1)}, u32[]{:S(2)}, u32[]{:S(2)}) async-start(bf16[8,2,32,1024]{3,2,1,0:T(8,128)(2,1)} %add.112), calls=%async_computation.2 | async-start | bytes 2097152 | tf_op jit(solution)/shard_map/all_to_all | solution.py:379
  152.5 2.0 collective-permute-start.9
  154.5 22.8 %all-to-all-done.2.moved = bf16[8,2,32,1024]{3,2,1,0:T(8,128)(2,1)S(1)} async-done(((bf16[8,2,32,1024]{3,2,1,0:T(8,128)(2,1)}), bf16[8,2,32,1024]{3,2,1,0:T(8,128)(2,1)S(1)}, u32[]{:S(2)}, u32[]{:S(2)}) %all-to-all-start.2) | async-done | bytes 1048608 | tf_op jit(solution)/shard_map/all_to_all | solution.py:379
  177.4 3.5 %all-to-all-start.3 = ((bf16[8,1,32,1024]{3,2,1,0:T(8,128)(2,1)}), bf16[8,1,32,1024]{3,2,1,0:T(8,128)(2,1)S(1)}, u32[]{:S(2)}, u32[]{:S(2)}) async-start(bf16[8,1,32,1024]{3,2,1,0:T(8,128)(2,1)} %add.111), calls=%async_computation.3 | async-start | bytes 1048576 | tf_op jit(solution)/shard_map/all_to_all | solution.py:379
  180.9 1.6 collective-permute-done.9
  182.5 1.1 add_convert_fusion
  183.6 11.8 %all-to-all-done.3.moved = bf16[8,1,32,1024]{3,2,1,0:T(8,128)(2,1)S(1)} async-done(((bf16[8,1,32,1024]{3,2,1,0:T(8,128)(2,1)}), bf16[8,1,32,1024]{3,2,1,0:T(8,128)(2,1)S(1)}, u32[]{:S(2)}, u32[]{:S(2)}) %all-to-all-start.3) | async-done | bytes 524320 | tf_op jit(solution)/shard_map/all_to_all | solution.py:379
  195.5 3.5 %all-to-all-start.5 = ((bf16[4,800,128]{2,1,0:T(8,128)(2,1)}), bf16[4,800,128]{2,1,0:T(8,128)(2,1)S(1)}, u32[]{:S(2)}, u32[]{:S(2)}) async-start(bf16[4,800,128]{2,1,0:T(8,128)(2,1)} %add_convert_fusion), calls=%async_computation.5 | async-start | bytes 1638400 | tf_op jit(solution)/shard_map/all_to_all | solution.py:664
  199.6 1.9 place.3.refs_0_
  201.5 0.8 place.4.refs_0_
  202.3 1.1 place.5
  203.4 15.4 %all-to-all-done.5.got = bf16[4,800,128]{2,1,0:T(8,128)(2,1)S(1)} async-done(((bf16[4,800,128]{2,1,0:T(8,128)(2,1)}), bf16[4,800,128]{2,1,0:T(8,128)(2,1)S(1)}, u32[]{:S(2)}, u32[]{:S(2)}) %all-to-all-start.5) | async-done | bytes 819232 | tf_op jit(solution)/shard_map/all_to_all | solution.py:664
  218.8 0.8 finish.1
  (39 shorter events, 3.9 us)
Async XLA Ops:
  1.6 9.2 %collective-permute-start = (bf16[4,8,2048]{2,1,0:T(8,128)(2,1)S(1)}, bf16[4,8,2048]{2,1,0:T(8,128)(2,1)S(1)}, u32[]{:S(2)}, u32[]{:S(2)}) collective-permute-start(bf16[4,8,2048]{2,1,0:T(8,128)(2,1)S(1)} %pad_maximum_fusion.3), channel_id=1, source_target_pairs={{0,4},{4,8},{8,12},{12,16},{16,20},{20,24},{24,28},{1,5},{5,9},{9,... | collective-permute-start | bytes 393224 | tf_op jit(solution)/shard_map/ppermute | solution.py:419
  6.5 6.9 %collective-permute-start.1 = (bf16[4,8,2048]{2,1,0:T(8,128)(2,1)S(1)}, bf16[4,8,2048]{2,1,0:T(8,128)(2,1)S(1)}, u32[]{:S(2)}, u32[]{:S(2)}) collective-permute-start(bf16[4,8,2048]{2,1,0:T(8,128)(2,1)S(1)} %pad_maximum_fusion.4), channel_id=1, source_target_pairs={{4,0},{8,4},{12,8},{16,12},{20,16},{24,20},{28,24},{5,1},{9,5},{13... | collective-permute-start | bytes 393224 | tf_op jit(solution)/shard_map/ppermute | solution.py:419
  14.1 21.0 %copy-start.6 = (f32[256]{0:T(256)S(1)}, f32[256]{0:T(256)}, u32[]{:S(2)}) copy-start(f32[256]{0:T(256)} %param.14) | copy-start | bytes 3076
  14.1 21.0 %copy-start.7 = (f32[256]{0:T(256)S(1)}, f32[256]{0:T(256)}, u32[]{:S(2)}) copy-start(f32[256]{0:T(256)} %param.15) | copy-start | bytes 3076
  29.4 12.3 %all-to-all-start = ((f32[8,2,256]{2,1,0:T(2,128)}), f32[8,2,256]{2,1,0:T(2,128)S(1)}, u32[]{:S(2)}, u32[]{:S(2)}) async-start(f32[8,2,256]{2,1,0:T(2,128)} %get-tuple-element.45), calls=%async_computation | async-start | bytes 32768 | tf_op jit(solution)/shard_map/all_to_all | solution.py:379
  41.7 0.6 copy-start.5
  54.4 10.3 %all-to-all-start.1 = ((f32[8,2,256]{2,1,0:T(2,128)}), f32[8,2,256]{2,1,0:T(2,128)S(1)}, u32[]{:S(2)}, u32[]{:S(2)}) async-start(f32[8,2,256]{2,1,0:T(2,128)} %get-tuple-element.47), calls=%async_computation.1 | async-start | bytes 32768 | tf_op jit(solution)/shard_map/all_to_all | solution.py:379
  64.7 0.6 copy-start.3
  65.3 5.3 %copy-start.2 = (bf16[1024,256]{1,0:T(8,128)(2,1)S(1)}, bf16[1024,256]{1,0:T(8,128)(2,1)}, u32[]{:S(2)}) copy-start(bf16[1024,256]{1,0:T(8,128)(2,1)} %wv.1) | copy-start | bytes 1572868
  70.5 11.7 %collective-permute-start.2 = (bf16[1024,512]{1,0:T(8,128)(2,1)}, bf16[1024,512]{1,0:T(8,128)(2,1)}, u32[]{:S(2)}, u32[]{:S(2)}) collective-permute-start(bf16[1024,512]{1,0:T(8,128)(2,1)} %get-tuple-element.53.own.refs_0_), channel_id=1, source_target_pairs={{0,1},{1,0},{2,3},{3,2},{4,5},{5,4},{6,7},{7,6},{8,9},{9,8},{10,11... | collective-permute-start | bytes 3145736 | tf_op jit(solution)/shard_map/ppermute | solution.py:574
  78.4 19.3 %collective-permute-start.5 = (bf16[1024,512]{1,0:T(8,128)(2,1)}, bf16[1024,512]{1,0:T(8,128)(2,1)}, u32[]{:S(2)}, u32[]{:S(2)}) collective-permute-start(bf16[1024,512]{1,0:T(8,128)(2,1)} %get-tuple-element.55.own.refs_1_), channel_id=1, source_target_pairs={{0,1},{1,0},{2,3},{3,2},{4,5},{5,4},{6,7},{7,6},{8,9},{9,8},{10,11... | collective-permute-start | bytes 3145736 | tf_op jit(solution)/shard_map/ppermute | solution.py:574
  78.9 3.2 %collective-permute-start.3 = (bf16[512,512]{1,0:T(8,128)(2,1)}, bf16[512,512]{1,0:T(8,128)(2,1)S(1)}, u32[]{:S(2)}, u32[]{:S(2)}) collective-permute-start(bf16[512,512]{1,0:T(8,128)(2,1)} %bitcast.23), channel_id=1, source_target_pairs={{0,1},{1,0},{2,3},{3,2},{4,5},{5,4},{6,7},{7,6},{8,9},{9,8},{10,11... | collective-permute-start | bytes 1572872 | tf_op jit(solution)/shard_map/ppermute | solution.py:434
  82.1 0.8 copy-start
  87.2 15.3 %collective-permute-start.6 = (bf16[8,1,32,1024]{3,2,1,0:T(8,128)(2,1)}, bf16[8,1,32,1024]{3,2,1,0:T(8,128)(2,1)S(1)}, u32[]{:S(2)}, u32[]{:S(2)}) collective-permute-start(bf16[8,1,32,1024]{3,2,1,0:T(8,128)(2,1)} %get-tuple-element.59), channel_id=1, source_target_pairs={{0,2},{1,3},{2,0},{3,1},{4,6},{5,7},{6,4},{7,5},{8,10},{9,11},{10,... | collective-permute-start | bytes 1572872 | tf_op jit(solution)/shard_map/ppermute | solution.py:605
  97.6 13.7 %collective-permute-start.4 = (bf16[2048,512]{1,0:T(8,128)(2,1)}, bf16[2048,512]{1,0:T(8,128)(2,1)}, u32[]{:S(2)}, u32[]{:S(2)}) collective-permute-start(bf16[2048,512]{1,0:T(8,128)(2,1)} %get-tuple-element.61.own.refs_2_), channel_id=1, source_target_pairs={{0,1},{1,0},{2,3},{3,2},{4,5},{5,4},{6,7},{7,6},{8,9},{9,8},{10,11... | collective-permute-start | bytes 6291464 | tf_op jit(solution)/shard_map/ppermute | solution.py:574
  102.0 17.3 %collective-permute-start.7 = (bf16[8,1,32,1024]{3,2,1,0:T(8,128)(2,1)}, bf16[8,1,32,1024]{3,2,1,0:T(8,128)(2,1)}, u32[]{:S(2)}, u32[]{:S(2)}) collective-permute-start(bf16[8,1,32,1024]{3,2,1,0:T(8,128)(2,1)} %get-tuple-element.64), channel_id=1, source_target_pairs={{0,2},{1,3},{2,0},{3,1},{4,6},{5,7},{6,4},{7,5},{8,10},{9,11},{10,... | collective-permute-start | bytes 1572872 | tf_op jit(solution)/shard_map/ppermute | solution.py:605
  102.5 0.8 copy-start.8
  105.3 41.4 %all-to-all-start.4 = ((bf16[8,1,32,1024]{3,2,1,0:T(8,128)(2,1)}), bf16[8,1,32,1024]{3,2,1,0:T(8,128)(2,1)}, u32[]{:S(2)}, u32[]{:S(2)}) async-start(bf16[8,1,32,1024]{3,2,1,0:T(8,128)(2,1)} %add.110), calls=%async_computation.4 | async-start | bytes 1048576 | tf_op jit(solution)/shard_map/all_to_all | solution.py:379
  117.7 25.3 %collective-permute-start.8 = (bf16[8,2,32,1024]{3,2,1,0:T(8,128)(2,1)}, bf16[8,2,32,1024]{3,2,1,0:T(8,128)(2,1)}, u32[]{:S(2)}, u32[]{:S(2)}) collective-permute-start(bf16[8,2,32,1024]{3,2,1,0:T(8,128)(2,1)} %get-tuple-element.68), channel_id=1, source_target_pairs={{0,2},{1,3},{2,0},{3,1},{4,6},{5,7},{6,4},{7,5},{8,10},{9,11},{10,... | collective-permute-start | bytes 3145736 | tf_op jit(solution)/shard_map/ppermute | solution.py:605
  146.7 35.9 %copy-start.1 = (bf16[4,800,128]{2,1,0:T(8,128)(2,1)S(1)}, bf16[4,800,128]{2,1,0:T(8,128)(2,1)}, u32[]{:S(2)}) copy-start(bf16[4,800,128]{2,1,0:T(8,128)(2,1)} %get-tuple-element.76) | copy-start | bytes 2457604
  146.7 30.7 %all-to-all-start.2 = ((bf16[8,2,32,1024]{3,2,1,0:T(8,128)(2,1)}), bf16[8,2,32,1024]{3,2,1,0:T(8,128)(2,1)S(1)}, u32[]{:S(2)}, u32[]{:S(2)}) async-start(bf16[8,2,32,1024]{3,2,1,0:T(8,128)(2,1)} %add.112), calls=%async_computation.2 | async-start | bytes 2097152 | tf_op jit(solution)/shard_map/all_to_all | solution.py:379
  152.5 30.0 %collective-permute-start.9 = (bf16[4,800,128]{2,1,0:T(8,128)(2,1)}, bf16[4,800,128]{2,1,0:T(8,128)(2,1)S(1)}, u32[]{:S(2)}, u32[]{:S(2)}) collective-permute-start(bf16[4,800,128]{2,1,0:T(8,128)(2,1)} %get-tuple-element.77), channel_id=1, source_target_pairs={{0,4},{4,0},{8,12},{12,8},{16,20},{20,16},{24,28},{28,24},{1,5},{5... | collective-permute-start | bytes 2457608 | tf_op jit(solution)/shard_map/ppermute | solution.py:660
  177.4 18.1 %all-to-all-start.3 = ((bf16[8,1,32,1024]{3,2,1,0:T(8,128)(2,1)}), bf16[8,1,32,1024]{3,2,1,0:T(8,128)(2,1)S(1)}, u32[]{:S(2)}, u32[]{:S(2)}) async-start(bf16[8,1,32,1024]{3,2,1,0:T(8,128)(2,1)} %add.111), calls=%async_computation.3 | async-start | bytes 1048576 | tf_op jit(solution)/shard_map/all_to_all | solution.py:379
  180.9 18.1 %copy-start.4 = (f32[8,2,256]{2,1,0:T(2,128)S(1)}, f32[8,2,256]{2,1,0:T(2,128)}, u32[]{:S(2)}) copy-start(f32[8,2,256]{2,1,0:T(2,128)} %copy-done.3) | copy-start | bytes 49156
  195.5 23.3 %all-to-all-start.5 = ((bf16[4,800,128]{2,1,0:T(8,128)(2,1)}), bf16[4,800,128]{2,1,0:T(8,128)(2,1)S(1)}, u32[]{:S(2)}, u32[]{:S(2)}) async-start(bf16[4,800,128]{2,1,0:T(8,128)(2,1)} %add_convert_fusion), calls=%async_computation.5 | async-start | bytes 1638400 | tf_op jit(solution)/shard_map/all_to_all | solution.py:664

commit v8 on v7

--- a/solution.py
+++ b/solution.py
@@ -352,15 +352,29 @@
             write(send, 0)
 
 
-def finish_kernel(kernel, got, value, gate, out, taps):
+def fold_kernel(parity, own, other, keep, send):
+    def write(place, odd):
+        for j in range(place.shape[0]):
+            total = own[2 * j + odd].astype(F32) + other[2 * j + odd].astype(F32)
+            place[j] = total.astype(BF16)
+
+    @pl.when(parity[0, 0] == 0)
+    def _():
+        write(keep, 0)
+        write(send, 1)
+
+    @pl.when(parity[0, 0] != 0)
+    def _():
+        write(keep, 1)
+        write(send, 0)
+
+
+def finish_kernel(kernel, own, other, value, gate, out, taps):
     width = value.shape[1]
     shard = value.shape[0]
 
     def total(row, size):
-        sums = got[0, row : row + size, :].astype(F32)
-        for j in range(1, got.shape[0]):
-            sums = sums + got[j, row : row + size, :].astype(F32)
-        return sums
+        return own[0, row : row + size, :].astype(F32) + other[0, row : row + size, :].astype(F32)
 
     for i, place in enumerate((value, gate, out)):
         place[...] = total(i * width, width).T
@@ -420,19 +434,6 @@
     )
     halo_x, halo_g = halo[:, :, :model], halo[:, :, model:]
 
-    both = jnp.concatenate([value_weight, gate_weight], axis=1).reshape(seqs, tps, piece, 2 * width)
-
-    def chosen(core):
-        picks = [
-            lax.dynamic_index_in_dim(both, ((chip_at + d) % chips) * 2 + core, 1, keepdims=False)
-            for d in range(chips)
-        ]
-        return jnp.stack(picks).reshape(chips * rows, 2 * width)
-
-    swap = [(i, i ^ 1) for i in range(tps)]
-    w_own = chosen(core_at)
-    w_sibling = lax.ppermute(chosen(1 - core_at), "tp", swap)
-
     channel = (
         jnp.arange(seqs, dtype=jnp.int32)[:, None] * (tps * piece)
         + tp_at * piece
@@ -471,6 +472,19 @@
         2 * matmul,
         input_bytes + 3 * array_bytes,
     )(meta, normed, halo_x, value_weight, gate_weight, depth_taps)
+    both = jnp.concatenate([after(value_weight, stats), gate_weight], axis=1).reshape(seqs, tps, piece, 2 * width)
+
+    def chosen(core):
+        picks = [
+            lax.dynamic_index_in_dim(both, ((chip_at + d) % chips) * 2 + core, 1, keepdims=False)
+            for d in range(chips)
+        ]
+        return jnp.stack(picks).reshape(chips * rows, 2 * width)
+
+    swap = [(i, i ^ 1) for i in range(tps)]
+    w_own = chosen(core_at)
+    w_sibling = lax.ppermute(chosen(1 - core_at), "tp", swap)
+
     stats = exchange(stats, "seq")
 
     chunk = block_rows(frames, 256)
@@ -514,7 +528,7 @@
         counts,
         stats,
         jnp.stack([norm_gain, norm_shift]),
-        select,
+        after(select, w_own, w_sibling),
         grad_out,
         halo_g,
         out_weight,
@@ -656,24 +670,39 @@
         50_000_000_000,
         1024,
     )(parity, after(normed, owns[1]), w_out, *grads, *taps)
-    pairs = [(i, i ^ 1) for i in range(seqs)]
-    others = lax.ppermute(send, "seq", pairs)
-    owns[2], moved[2] = deliver(parts[2], keep)
-    paired = (after(keep, owns[2]).astype(F32) + others.astype(F32)).astype(BF16)
-    same = [[i for i in range(seqs) if i % 2 == odd] for odd in range(2)]
-    got = lax.all_to_all(after(paired, moved[2]), "seq", 0, 0, axis_index_groups=same, tiled=True)
+    owns[2], moved[2] = deliver(parts[2], keep, moved[1])
+    bit = 1
+    while True:
+        others = lax.ppermute(send, "seq", [(i, i ^ bit) for i in range(seqs)])
+        bit *= 2
+        if bit == seqs:
+            break
+        shape = (keep.shape[0] // 2,) + keep.shape[1:]
+        side = ((seq_at // bit) % 2).astype(jnp.int32).reshape(1, 1)
+        keep, send = call(
+            fold_kernel,
+            "fold",
+            (1,),
+            [smem()] + [whole(keep.shape)] * 2,
+            [whole(shape)] * 2,
+            [sds(shape, BF16)] * 2,
+            [],
+            0,
+            1024,
+            vmem=20,
+        )(side, keep, others)
     w_value, w_gate, w_out, grad_taps = call(
         functools.partial(finish_kernel, kernel),
         "finish",
         (1,),
-        [whole(half.shape)],
+        [whole(keep.shape)] * 2,
         [whole((shard, width))] * 3 + [whole((kernel, width))],
         [sds((shard, width), F32)] * 3 + [sds((kernel, width), F32)],
         [],
         0,
-        8 * seqs * slots * shard,
+        1024,
         vmem=20,
-    )(got)
+    )(keep, others)
     grad_in = ()
     for (first, size), part in zip(groups, moved):
         grad_in = (

time: 221 us -> 216 us (0.977)
  other arithmetic: 7.9 us -> 5 us
    ppermute x1 -> x3, waiting for transfers between devices: 1.64 us -> 42.3 us  [per_device(): others = lax.ppermute(send, 'seq', [(i, i ^ bit) for i in range(seqs)])]
    all_to_all x5, waiting for transfers between devices: 40 us -> 13.5 us  [exchange(): return lax.all_to_all(copies, axis, 0, 0, tiled=True)]
    all_to_all x1 -> x0, waiting for transfers between devices: 15.4 us -> none  [per_device(): lax.all_to_all(after(paired, moved[2]), 'seq', 0, 0, axis_index_groups=sa...]
    ppermute x1 -> x3, starting transfers between devices: 2.02 us -> 7.56 us  [per_device(): others = lax.ppermute(send, 'seq', [(i, i ^ bit) for i in range(seqs)])]
    all_to_all x1 -> x0, starting transfers between devices: 3.5 us -> none  [per_device(): lax.all_to_all(after(paired, moved[2]), 'seq', 0, 0, axis_index_groups=sa...]
  transfers between devices with their start and end apart: 16 -> 17, of which waited for: 8 -> 9; matrix products, arithmetic and copies ran while one was open for 5% -> 2% of each run, Pallas kernels for 26% -> 27%
where the time goes in v8:
time: 216 us; the launch traced here: 214 us
  Pallas kernels  92.3 us (43%)
  waiting for transfers between devices  70.6 us (33%)
  starting transfers between devices  39.7 us (18%)
  local copies, waits for them, and re-layouts  5.03 us (2%)
  other arithmetic  5 us (2%)
    ppermute x3, waiting for transfers between devices, per_device(): others = lax.ppermute(send, 'seq', [(i, i ^ bit) for i in range(seqs)])  42.3 us
    all_to_all x5, starting transfers between devices, exchange(): return lax.all_to_all(copies, axis, 0, 0, tiled=True)  22.7 us
    pallas_call x3, Pallas kernels, back(): call(functools.partial(back_kernel, first, blocks), 'back_conv', (size *...  19 us
    pallas_call x1, Pallas kernels, per_device(): call(gate_kernel, 'gate_conv', (recs,), [smem(), per_record((frames, mode...  15.3 us
    pallas_call x3, Pallas kernels, partials(): call(partial_kernel, 'partial_in', (size * parts_in,), [pl.BlockSpec((hal...  15 us
    all_to_all x5, waiting for transfers between devices, exchange(): return lax.all_to_all(copies, axis, 0, 0, tiled=True)  13.5 us
    pallas_call x1, Pallas kernels, per_device(): call(norm_kernel, 'swish_norm', (recs,), [smem(), smem(), whole((seqs, 2,...  12.1 us
    ppermute x3, waiting for transfers between devices, deliver(): arrived.append(lax.ppermute(part[d], 'tp', send))  11.1 us
  transfers between devices with their start and end apart: 17, of which 9 were waited for; matrix products, arithmetic and copies ran while one was open for 2% of the time, Pallas kernels for 27%

profile of v8, /device:TPU:0, one launch (start us, length us, event | category | flops | bytes accessed | tf_op | source)
XLA Modules:
  0.0 214.2 jit_solution(18328089457055387244)
XLA Ops:
  0.6 1.0 fusion.1
  1.6 4.9 %collective-permute-start = (bf16[4,8,2048]{2,1,0:T(8,128)(2,1)S(1)}, bf16[4,8,2048]{2,1,0:T(8,128)(2,1)S(1)}, u32[]{:S(2)}, u32[]{:S(2)}) collective-permute-start(bf16[4,8,2048]{2,1,0:T(8,128)(2,1)S(1)} %pad_maximum_fusion.3), channel_id=1, source_target_pairs={{0,4},{4,8},{8,12},{12,16},{16,20},{20,24},{24,28},{1,5},{5,9},{9,... | collective-permute-start | bytes 393224 | tf_op jit(solution)/shard_map/ppermute | solution.py:433
  6.5 1.3 collective-permute-start.1
  7.8 1.3 fusion.5
  9.7 3.7 %collective-permute-done.1 = bf16[4,8,2048]{2,1,0:T(8,128)(2,1)S(1)} collective-permute-done((bf16[4,8,2048]{2,1,0:T(8,128)(2,1)S(1)}, bf16[4,8,2048]{2,1,0:T(8,128)(2,1)S(1)}, u32[]{:S(2)}, u32[]{:S(2)}) %collective-permute-start.1) | collective-permute-done | bytes 131104 | tf_op jit(solution)/shard_map/ppermute | solution.py:433
  13.4 0.7 fusion.3
  14.1 15.3 %gate_conv.1 = (f32[4,1024,256]{2,1,0:T(8,128)}, f32[4,1024,256]{2,1,0:T(8,128)}, f32[4,1040,256]{2,1,0:T(8,128)}, f32[8,2,256]{2,1,0:T(2,128)}) custom-call(s32[2,4]{1,0:T(2,128)} %stack.35.meta, bf16[4,1024,1024]{2,1,0:T(8,128)(2,1)} %x.4, bf16[4,16,1024]{2,1,0:T(8,128)(2,1)} %get-tuple-element.100.halo, bf16[1024,256]{1,0:T(8,128)(2,1)} %wv.1, ...), custom_call_target="tpu_custom_call" | custom-call | flops 4294967296 | bytes 20971520 | tf_op jit(solution)/shard_map/gate_conv/pallas_call | solution.py:447
  29.4 1.1 pad_maximum_fusion
  31.6 0.6 pad_maximum_fusion.5.affine
  32.2 1.0 fusion.select
  33.2 5.7 %all-to-all-start = ((f32[8,2,256]{2,1,0:T(2,128)}), f32[8,2,256]{2,1,0:T(2,128)S(1)}, u32[]{:S(2)}, u32[]{:S(2)}) async-start(f32[8,2,256]{2,1,0:T(2,128)} %get-tuple-element.49), calls=%async_computation | async-start | bytes 32768 | tf_op jit(solution)/shard_map/all_to_all | solution.py:393
  38.9 0.9 pad_maximum_fusion.1
  39.8 5.7 %all-to-all-done.stats = f32[8,2,256]{2,1,0:T(2,128)S(1)} async-done(((f32[8,2,256]{2,1,0:T(2,128)}), f32[8,2,256]{2,1,0:T(2,128)S(1)}, u32[]{:S(2)}, u32[]{:S(2)}) %all-to-all-start) | async-done | bytes 16416 | tf_op jit(solution)/shard_map/all_to_all | solution.py:393
  45.5 0.6 copy-done.5
  46.1 12.1 %swish_norm.1 = (bf16[4,1024,256]{2,1,0:T(8,128)(2,1)}, f32[4,1040,256]{2,1,0:T(8,128)}, bf16[4,256,1024]{2,1,0:T(8,128)(2,1)}, f32[8,2,256]{2,1,0:T(2,128)}) custom-call(s32[2,4]{1,0:T(2,128)} %stack.35.meta, f32[1,1]{1,0:T(1,128)} %bitcast.1.count, f32[8,2,256]{2,1,0:T(2,128)} %copy-done.5, f32[2,256]{1,0:T(2,128)} %pad_maximum_fusion.5.affine, ...), custom_call_target="tpu_custom_call" | custom-call | flops 4294967296 | bytes 20971520 | tf_op jit(solution)/shard_map/swish_norm/pallas_call | solution.py:492
  58.2 3.3 %all-to-all-start.1 = ((f32[8,2,256]{2,1,0:T(2,128)}), f32[8,2,256]{2,1,0:T(2,128)S(1)}, u32[]{:S(2)}, u32[]{:S(2)}) async-start(f32[8,2,256]{2,1,0:T(2,128)} %get-tuple-element.53), calls=%async_computation.1 | async-start | bytes 32768 | tf_op jit(solution)/shard_map/all_to_all | solution.py:393
  61.5 7.0 %outer_w_out.1.w_out = f32[256,1024]{1,0:T(8,128)} custom-call(bf16[4,1024,1024]{2,1,0:T(8,128)(2,1)} %grads.3, bf16[4,1024,256]{2,1,0:T(8,128)(2,1)} %get-tuple-element.57.swished), custom_call_target="tpu_custom_call" | custom-call | flops 2147483648 | bytes 8388608 | tf_op jit(solution)/shard_map/outer_w_out/pallas_call | solution.py:537
  68.5 0.6 copy-done.3
  69.1 5.0 %back_conv.3 = (bf16[1024,512]{1,0:T(8,128)(2,1)}, f32[16,256]{1,0:T(8,128)}) custom-call(s32[2,4]{1,0:T(2,128)} %stack.35.meta, f32[1,1]{1,0:T(1,128)} %bitcast.1.count, f32[8,2,256]{2,1,0:T(2,128)} %copy-done.5, f32[8,2,256]{2,1,0:T(2,128)} %copy-done.3, f32[1,256]{1,0:T(1,128)} %bitcast.26, f32[4,1040,256]{2,1,0:T(8,128)} %get-tuple-element.54.gn, ...), custom_call_target="tpu_custom_call" | custom-call | bytes 1024 | tf_op jit(solution)/shard_map/back_conv/pallas_call | solution.py:561
  74.2 5.1 %back_conv.4 = (bf16[1024,512]{1,0:T(8,128)(2,1)}, f32[16,256]{1,0:T(8,128)}) custom-call(s32[2,4]{1,0:T(2,128)} %stack.35.meta, f32[1,1]{1,0:T(1,128)} %bitcast.1.count, f32[8,2,256]{2,1,0:T(2,128)} %copy-done.5, f32[8,2,256]{2,1,0:T(2,128)} %copy-done.3, f32[1,256]{1,0:T(1,128)} %bitcast.27, f32[4,1040,256]{2,1,0:T(8,128)} %get-tuple-element.54.gn, ...), custom_call_target="tpu_custom_call" | custom-call | bytes 1024 | tf_op jit(solution)/shard_map/back_conv/pallas_call | solution.py:561
  79.8 4.2 %partial_in.3 = (bf16[8,1,32,1024]{3,2,1,0:T(8,128)(2,1)}, bf16[8,1,32,1024]{3,2,1,0:T(8,128)(2,1)}) custom-call(bf16[1024,512]{1,0:T(8,128)(2,1)} %get-tuple-element.59.own.refs_0_, bf16[1024,512]{1,0:T(8,128)(2,1)} %collective-permute-done.3.sibling, bf16[512,512]{1,0:T(8,128)(2,1)} %bitcast.21, bf16[512,512]{1,0:T(8,128)(2,1)} %copy-done.1, ...), custom_call_target="tpu_custom_call" | custom-call | bytes 1024 | tf_op jit(solution)/shard_map/partial_in/pallas_call | solution.py:590
  84.1 1.5 collective-permute-start.6
  85.6 8.9 %back_conv.5 = (bf16[2048,512]{1,0:T(8,128)(2,1)}, f32[16,256]{1,0:T(8,128)}) custom-call(s32[2,4]{1,0:T(2,128)} %stack.35.meta, f32[1,1]{1,0:T(1,128)} %bitcast.1.count, f32[8,2,256]{2,1,0:T(2,128)} %copy-done.5, f32[8,2,256]{2,1,0:T(2,128)} %copy-done.3, f32[1,256]{1,0:T(1,128)} %bitcast.28, f32[4,1040,256]{2,1,0:T(8,128)} %get-tuple-element.54.gn, ...), custom_call_target="tpu_custom_call" | custom-call | bytes 1024 | tf_op jit(solution)/shard_map/back_conv/pallas_call | solution.py:561
  94.5 4.3 %partial_in.4 = (bf16[8,1,32,1024]{3,2,1,0:T(8,128)(2,1)}, bf16[8,1,32,1024]{3,2,1,0:T(8,128)(2,1)}) custom-call(bf16[1024,512]{1,0:T(8,128)(2,1)} %get-tuple-element.61.own.refs_1_, bf16[1024,512]{1,0:T(8,128)(2,1)} %collective-permute-done.5.sibling, bf16[512,512]{1,0:T(8,128)(2,1)} %bitcast.22, bf16[512,512]{1,0:T(8,128)(2,1)} %copy-done.1, ...), custom_call_target="tpu_custom_call" | custom-call | bytes 1024 | tf_op jit(solution)/shard_map/partial_in/pallas_call | solution.py:590
  99.4 0.8 copy-done.8
  100.1 2.0 add.115
  102.2 6.5 %partial_in.5 = (bf16[8,2,32,1024]{3,2,1,0:T(8,128)(2,1)}, bf16[8,2,32,1024]{3,2,1,0:T(8,128)(2,1)}) custom-call(bf16[2048,512]{1,0:T(8,128)(2,1)} %get-tuple-element.67.own.refs_2_, bf16[2048,512]{1,0:T(8,128)(2,1)} %collective-permute-done.4.sibling, bf16[512,512]{1,0:T(8,128)(2,1)} %bitcast.23, bf16[512,512]{1,0:T(8,128)(2,1)} %copy-done.1, ...), custom_call_target="tpu_custom_call" | custom-call | bytes 1024 | tf_op jit(solution)/shard_map/partial_in/pallas_call | solution.py:590
  108.6 4.8 %collective-permute-done.7.refs_1_ = bf16[8,1,32,1024]{3,2,1,0:T(8,128)(2,1)} collective-permute-done((bf16[8,1,32,1024]{3,2,1,0:T(8,128)(2,1)}, bf16[8,1,32,1024]{3,2,1,0:T(8,128)(2,1)}, u32[]{:S(2)}, u32[]{:S(2)}) %collective-permute-start.7) | collective-permute-done | bytes 524320 | tf_op jit(solution)/shard_map/ppermute | solution.py:619
  113.4 2.0 add.116
  115.4 5.9 %all-to-all-start.2 = ((bf16[8,1,32,1024]{3,2,1,0:T(8,128)(2,1)}), bf16[8,1,32,1024]{3,2,1,0:T(8,128)(2,1)S(1)}, u32[]{:S(2)}, u32[]{:S(2)}) async-start(bf16[8,1,32,1024]{3,2,1,0:T(8,128)(2,1)} %add.116), calls=%async_computation.2 | async-start | bytes 1048576 | tf_op jit(solution)/shard_map/all_to_all | solution.py:393
  121.9 10.2 %outer_w_in.1 = (bf16[4,800,128]{2,1,0:T(8,128)(2,1)}, bf16[4,800,128]{2,1,0:T(8,128)(2,1)}) custom-call(s32[1,1]{1,0:T(1,128)} %bitcast.11.parity, bf16[4,1024,1024]{2,1,0:T(8,128)(2,1)} %x.4, f32[256,1024]{1,0:T(8,128)} %outer_w_out.1.w_out, bf16[1024,512]{1,0:T(8,128)(2,1)} %get-tuple-element.59.own.refs_0_, ...), custom_call_target="tpu_custom_call" | custom-call | flops 49999998976 | bytes 1024 | tf_op jit(solution)/shard_map/outer_w_in/pallas_call | solution.py:654
  132.1 3.6 %all-to-all-done.2.moved = bf16[8,1,32,1024]{3,2,1,0:T(8,128)(2,1)S(1)} async-done(((bf16[8,1,32,1024]{3,2,1,0:T(8,128)(2,1)}), bf16[8,1,32,1024]{3,2,1,0:T(8,128)(2,1)S(1)}, u32[]{:S(2)}, u32[]{:S(2)}) %all-to-all-start.2) | async-done | bytes 524320 | tf_op jit(solution)/shard_map/all_to_all | solution.py:393
  135.7 4.1 %all-to-all-start.4 = ((bf16[8,1,32,1024]{3,2,1,0:T(8,128)(2,1)}), bf16[8,1,32,1024]{3,2,1,0:T(8,128)(2,1)}, u32[]{:S(2)}, u32[]{:S(2)}) async-start(bf16[8,1,32,1024]{3,2,1,0:T(8,128)(2,1)} %add.115), calls=%async_computation.4 | async-start | bytes 1048576 | tf_op jit(solution)/shard_map/all_to_all | solution.py:393
  139.8 6.3 %collective-permute-done.8.refs_1_ = bf16[8,2,32,1024]{3,2,1,0:T(8,128)(2,1)} collective-permute-done((bf16[8,2,32,1024]{3,2,1,0:T(8,128)(2,1)}, bf16[8,2,32,1024]{3,2,1,0:T(8,128)(2,1)}, u32[]{:S(2)}, u32[]{:S(2)}) %collective-permute-start.8) | collective-permute-done | bytes 1048608 | tf_op jit(solution)/shard_map/ppermute | solution.py:619
  146.1 3.7 %add.117 = bf16[8,2,32,1024]{3,2,1,0:T(8,128)(2,1)} custom-call(bf16[8,2,32,1024]{3,2,1,0:T(8,128)(2,1)} %get-tuple-element.81.refs_0_, bf16[8,2,32,1024]{3,2,1,0:T(8,128)(2,1)} %collective-permute-done.8.refs_1_), custom_call_target="tpu_custom_call" | custom-call | flops 49999998976 | bytes 1024 | tf_op jit(solution)/shard_map/add/pallas_call | solution.py:624
  149.8 4.2 %all-to-all-done.4.moved = bf16[8,1,32,1024]{3,2,1,0:T(8,128)(2,1)} async-done(((bf16[8,1,32,1024]{3,2,1,0:T(8,128)(2,1)}), bf16[8,1,32,1024]{3,2,1,0:T(8,128)(2,1)}, u32[]{:S(2)}, u32[]{:S(2)}) %all-to-all-start.4) | async-done | bytes 524320 | tf_op jit(solution)/shard_map/all_to_all | solution.py:393
  154.1 3.6 %all-to-all-start.3 = ((bf16[8,2,32,1024]{3,2,1,0:T(8,128)(2,1)}), bf16[8,2,32,1024]{3,2,1,0:T(8,128)(2,1)S(1)}, u32[]{:S(2)}, u32[]{:S(2)}) async-start(bf16[8,2,32,1024]{3,2,1,0:T(8,128)(2,1)} %add.117), calls=%async_computation.3 | async-start | bytes 2097152 | tf_op jit(solution)/shard_map/all_to_all | solution.py:393
  157.7 2.0 collective-permute-start.9
  159.7 29.2 %collective-permute-done.9.other = bf16[4,800,128]{2,1,0:T(8,128)(2,1)} collective-permute-done((bf16[4,800,128]{2,1,0:T(8,128)(2,1)}, bf16[4,800,128]{2,1,0:T(8,128)(2,1)}, u32[]{:S(2)}, u32[]{:S(2)}) %collective-permute-start.9) | collective-permute-done | bytes 819232 | tf_op jit(solution)/shard_map/ppermute | solution.py:676
  188.9 1.3 fold.2
  190.2 1.5 collective-permute-start.10
  191.8 8.5 %collective-permute-done.10.other = bf16[2,800,128]{2,1,0:T(8,128)(2,1)S(1)} collective-permute-done((bf16[2,800,128]{2,1,0:T(8,128)(2,1)S(1)}, bf16[2,800,128]{2,1,0:T(8,128)(2,1)S(1)}, u32[]{:S(2)}, u32[]{:S(2)}) %collective-permute-start.10) | collective-permute-done | bytes 409632 | tf_op jit(solution)/shard_map/ppermute | solution.py:676
  200.4 4.0 %collective-permute-start.11 = (bf16[1,800,128]{2,1,0:T(8,128)(2,1)S(1)}, bf16[1,800,128]{2,1,0:T(8,128)(2,1)S(1)}, u32[]{:S(2)}, u32[]{:S(2)}) collective-permute-start(bf16[1,800,128]{2,1,0:T(8,128)(2,1)S(1)} %get-tuple-element.86), channel_id=1, source_target_pairs={{0,16},{4,20},{8,24},{12,28},{16,0},{20,4},{24,8},{28,12},{1,17},{... | collective-permute-start | bytes 614408 | tf_op jit(solution)/shard_map/ppermute | solution.py:676
  205.0 1.9 place.3.refs_0_
  206.9 0.8 place.4.refs_0_
  207.7 4.5 %collective-permute-done.11.other = bf16[1,800,128]{2,1,0:T(8,128)(2,1)S(1)} collective-permute-done((bf16[1,800,128]{2,1,0:T(8,128)(2,1)S(1)}, bf16[1,800,128]{2,1,0:T(8,128)(2,1)S(1)}, u32[]{:S(2)}, u32[]{:S(2)}) %collective-permute-start.11) | collective-permute-done | bytes 204832 | tf_op jit(solution)/shard_map/ppermute | solution.py:676
  212.2 0.9 finish.1
  213.1 1.1 place.5
  (42 shorter events, 3.4 us)
Async XLA Ops:
  1.6 8.1 %collective-permute-start = (bf16[4,8,2048]{2,1,0:T(8,128)(2,1)S(1)}, bf16[4,8,2048]{2,1,0:T(8,128)(2,1)S(1)}, u32[]{:S(2)}, u32[]{:S(2)}) collective-permute-start(bf16[4,8,2048]{2,1,0:T(8,128)(2,1)S(1)} %pad_maximum_fusion.3), channel_id=1, source_target_pairs={{0,4},{4,8},{8,12},{12,16},{16,20},{20,24},{24,28},{1,5},{5,9},{9,... | collective-permute-start | bytes 393224 | tf_op jit(solution)/shard_map/ppermute | solution.py:433
  6.5 6.9 %collective-permute-start.1 = (bf16[4,8,2048]{2,1,0:T(8,128)(2,1)S(1)}, bf16[4,8,2048]{2,1,0:T(8,128)(2,1)S(1)}, u32[]{:S(2)}, u32[]{:S(2)}) collective-permute-start(bf16[4,8,2048]{2,1,0:T(8,128)(2,1)S(1)} %pad_maximum_fusion.4), channel_id=1, source_target_pairs={{4,0},{8,4},{12,8},{16,12},{20,16},{24,20},{28,24},{5,1},{9,5},{13... | collective-permute-start | bytes 393224 | tf_op jit(solution)/shard_map/ppermute | solution.py:433
  14.1 15.3 %copy-start.2 = (bf16[1024,256]{1,0:T(8,128)(2,1)S(1)}, bf16[1024,256]{1,0:T(8,128)(2,1)}, u32[]{:S(2)}) copy-start(bf16[1024,256]{1,0:T(8,128)(2,1)} %wv.1) | copy-start | bytes 1572868
  30.6 1.1 copy-start.6
  30.6 1.1 copy-start.7
  30.7 9.1 %collective-permute-start.2 = (bf16[512,512]{1,0:T(8,128)(2,1)S(1)}, bf16[512,512]{1,0:T(8,128)(2,1)S(1)}, u32[]{:S(2)}, u32[]{:S(2)}) collective-permute-start(bf16[512,512]{1,0:T(8,128)(2,1)S(1)} %bitcast.25), channel_id=1, source_target_pairs={{0,1},{1,0},{2,3},{3,2},{4,5},{5,4},{6,7},{7,6},{8,9},{9,8},{10,11... | collective-permute-start | bytes 1572872 | tf_op jit(solution)/shard_map/ppermute | solution.py:486
  33.2 12.3 %all-to-all-start = ((f32[8,2,256]{2,1,0:T(2,128)}), f32[8,2,256]{2,1,0:T(2,128)S(1)}, u32[]{:S(2)}, u32[]{:S(2)}) async-start(f32[8,2,256]{2,1,0:T(2,128)} %get-tuple-element.49), calls=%async_computation | async-start | bytes 32768 | tf_op jit(solution)/shard_map/all_to_all | solution.py:393
  39.8 18.4 %copy-start.1 = (bf16[512,512]{1,0:T(8,128)(2,1)}, bf16[512,512]{1,0:T(8,128)(2,1)S(1)}, u32[]{:S(2)}) copy-start(bf16[512,512]{1,0:T(8,128)(2,1)S(1)} %collective-permute-done.2.w_sibling) | copy-start | bytes 1572868
  45.5 0.6 copy-start.5
  58.2 10.4 %all-to-all-start.1 = ((f32[8,2,256]{2,1,0:T(2,128)}), f32[8,2,256]{2,1,0:T(2,128)S(1)}, u32[]{:S(2)}, u32[]{:S(2)}) async-start(f32[8,2,256]{2,1,0:T(2,128)} %get-tuple-element.53), calls=%async_computation.1 | async-start | bytes 32768 | tf_op jit(solution)/shard_map/all_to_all | solution.py:393
  68.5 0.6 copy-start.3
  74.2 5.7 %collective-permute-start.3 = (bf16[1024,512]{1,0:T(8,128)(2,1)}, bf16[1024,512]{1,0:T(8,128)(2,1)}, u32[]{:S(2)}, u32[]{:S(2)}) collective-permute-start(bf16[1024,512]{1,0:T(8,128)(2,1)} %get-tuple-element.59.own.refs_0_), channel_id=1, source_target_pairs={{0,1},{1,0},{2,3},{3,2},{4,5},{5,4},{6,7},{7,6},{8,9},{9,8},{10,11... | collective-permute-start | bytes 3145736 | tf_op jit(solution)/shard_map/ppermute | solution.py:588
  79.3 15.2 %collective-permute-start.5 = (bf16[1024,512]{1,0:T(8,128)(2,1)}, bf16[1024,512]{1,0:T(8,128)(2,1)}, u32[]{:S(2)}, u32[]{:S(2)}) collective-permute-start(bf16[1024,512]{1,0:T(8,128)(2,1)} %get-tuple-element.61.own.refs_1_), channel_id=1, source_target_pairs={{0,1},{1,0},{2,3},{3,2},{4,5},{5,4},{6,7},{7,6},{8,9},{9,8},{10,11... | collective-permute-start | bytes 3145736 | tf_op jit(solution)/shard_map/ppermute | solution.py:588
  84.1 15.3 %collective-permute-start.6 = (bf16[8,1,32,1024]{3,2,1,0:T(8,128)(2,1)}, bf16[8,1,32,1024]{3,2,1,0:T(8,128)(2,1)S(1)}, u32[]{:S(2)}, u32[]{:S(2)}) collective-permute-start(bf16[8,1,32,1024]{3,2,1,0:T(8,128)(2,1)} %get-tuple-element.65), channel_id=1, source_target_pairs={{0,2},{1,3},{2,0},{3,1},{4,6},{5,7},{6,4},{7,5},{8,10},{9,11},{10,... | collective-permute-start | bytes 1572872 | tf_op jit(solution)/shard_map/ppermute | solution.py:619
  94.5 7.7 %collective-permute-start.4 = (bf16[2048,512]{1,0:T(8,128)(2,1)}, bf16[2048,512]{1,0:T(8,128)(2,1)}, u32[]{:S(2)}, u32[]{:S(2)}) collective-permute-start(bf16[2048,512]{1,0:T(8,128)(2,1)} %get-tuple-element.67.own.refs_2_), channel_id=1, source_target_pairs={{0,1},{1,0},{2,3},{3,2},{4,5},{5,4},{6,7},{7,6},{8,9},{9,8},{10,11... | collective-permute-start | bytes 6291464 | tf_op jit(solution)/shard_map/ppermute | solution.py:588
  98.8 14.6 %collective-permute-start.7 = (bf16[8,1,32,1024]{3,2,1,0:T(8,128)(2,1)}, bf16[8,1,32,1024]{3,2,1,0:T(8,128)(2,1)}, u32[]{:S(2)}, u32[]{:S(2)}) collective-permute-start(bf16[8,1,32,1024]{3,2,1,0:T(8,128)(2,1)} %get-tuple-element.70), channel_id=1, source_target_pairs={{0,2},{1,3},{2,0},{3,1},{4,6},{5,7},{6,4},{7,5},{8,10},{9,11},{10,... | collective-permute-start | bytes 1572872 | tf_op jit(solution)/shard_map/ppermute | solution.py:619
  99.3 0.8 copy-start.8
  115.4 20.3 %all-to-all-start.2 = ((bf16[8,1,32,1024]{3,2,1,0:T(8,128)(2,1)}), bf16[8,1,32,1024]{3,2,1,0:T(8,128)(2,1)S(1)}, u32[]{:S(2)}, u32[]{:S(2)}) async-start(bf16[8,1,32,1024]{3,2,1,0:T(8,128)(2,1)} %add.116), calls=%async_computation.2 | async-start | bytes 1048576 | tf_op jit(solution)/shard_map/all_to_all | solution.py:393
  121.3 24.8 %collective-permute-start.8 = (bf16[8,2,32,1024]{3,2,1,0:T(8,128)(2,1)}, bf16[8,2,32,1024]{3,2,1,0:T(8,128)(2,1)}, u32[]{:S(2)}, u32[]{:S(2)}) collective-permute-start(bf16[8,2,32,1024]{3,2,1,0:T(8,128)(2,1)} %get-tuple-element.74), channel_id=1, source_target_pairs={{0,2},{1,3},{2,0},{3,1},{4,6},{5,7},{6,4},{7,5},{8,10},{9,11},{10,... | collective-permute-start | bytes 3145736 | tf_op jit(solution)/shard_map/ppermute | solution.py:619
  135.7 18.4 %all-to-all-start.4 = ((bf16[8,1,32,1024]{3,2,1,0:T(8,128)(2,1)}), bf16[8,1,32,1024]{3,2,1,0:T(8,128)(2,1)}, u32[]{:S(2)}, u32[]{:S(2)}) async-start(bf16[8,1,32,1024]{3,2,1,0:T(8,128)(2,1)} %add.115), calls=%async_computation.4 | async-start | bytes 1048576 | tf_op jit(solution)/shard_map/all_to_all | solution.py:393
  149.8 39.1 %copy-start = (bf16[4,800,128]{2,1,0:T(8,128)(2,1)S(1)}, bf16[4,800,128]{2,1,0:T(8,128)(2,1)}, u32[]{:S(2)}) copy-start(bf16[4,800,128]{2,1,0:T(8,128)(2,1)} %get-tuple-element.80.own) | copy-start | bytes 2457604
  149.8 42.0 %copy-start.4 = (f32[8,2,256]{2,1,0:T(2,128)S(1)}, f32[8,2,256]{2,1,0:T(2,128)}, u32[]{:S(2)}) copy-start(f32[8,2,256]{2,1,0:T(2,128)} %copy-done.3) | copy-start | bytes 49156
  154.1 59.0 %all-to-all-start.3 = ((bf16[8,2,32,1024]{3,2,1,0:T(8,128)(2,1)}), bf16[8,2,32,1024]{3,2,1,0:T(8,128)(2,1)S(1)}, u32[]{:S(2)}, u32[]{:S(2)}) async-start(bf16[8,2,32,1024]{3,2,1,0:T(8,128)(2,1)} %add.117), calls=%async_computation.3 | async-start | bytes 2097152 | tf_op jit(solution)/shard_map/all_to_all | solution.py:393
  157.7 31.2 %collective-permute-start.9 = (bf16[4,800,128]{2,1,0:T(8,128)(2,1)}, bf16[4,800,128]{2,1,0:T(8,128)(2,1)}, u32[]{:S(2)}, u32[]{:S(2)}) collective-permute-start(bf16[4,800,128]{2,1,0:T(8,128)(2,1)} %get-tuple-element.82), channel_id=1, source_target_pairs={{0,4},{4,0},{8,12},{12,8},{16,20},{20,16},{24,28},{28,24},{1,5},{5... | collective-permute-start | bytes 2457608 | tf_op jit(solution)/shard_map/ppermute | solution.py:676
  190.2 10.1 %collective-permute-start.10 = (bf16[2,800,128]{2,1,0:T(8,128)(2,1)S(1)}, bf16[2,800,128]{2,1,0:T(8,128)(2,1)S(1)}, u32[]{:S(2)}, u32[]{:S(2)}) collective-permute-start(bf16[2,800,128]{2,1,0:T(8,128)(2,1)S(1)} %get-tuple-element.84), channel_id=1, source_target_pairs={{0,8},{4,12},{8,0},{12,4},{16,24},{20,28},{24,16},{28,20},{1,9},{5... | collective-permute-start | bytes 1228808 | tf_op jit(solution)/shard_map/ppermute | solution.py:676
  200.4 11.8 %collective-permute-start.11 = (bf16[1,800,128]{2,1,0:T(8,128)(2,1)S(1)}, bf16[1,800,128]{2,1,0:T(8,128)(2,1)S(1)}, u32[]{:S(2)}, u32[]{:S(2)}) collective-permute-start(bf16[1,800,128]{2,1,0:T(8,128)(2,1)S(1)} %get-tuple-element.86), channel_id=1, source_target_pairs={{0,16},{4,20},{8,24},{12,28},{16,0},{20,4},{24,8},{28,12},{1,17},{... | collective-permute-start | bytes 614408 | tf_op jit(solution)/shard_map/ppermute | solution.py:676

commit v9 on v8

--- a/solution.py
+++ b/solution.py
@@ -632,7 +632,7 @@
             50_000_000_000,
             1024,
         )(after(part[0], *earlier), *arrived)
-        return own, exchange(own, "seq")
+        return own
 
     groups = ((0, 1), (1, 1), (2, recs - 2))
     grads = [None] * 3
@@ -645,9 +645,10 @@
     parts[0] = partials(*groups[0], grads[0], grads[1])
     grads[2], taps[2] = back(*groups[2], *parts[0])
     parts[1] = partials(*groups[1], grads[1], grads[2])
-    owns[0], moved[0] = deliver(parts[0], *parts[1])
-    parts[2] = partials(*groups[2], grads[2], owns[0])
-    owns[1], moved[1] = deliver(parts[1], *parts[2])
+    owns[0] = deliver(parts[0], *parts[1])
+    moved[0] = exchange(owns[0], "seq")
+    owns[1] = deliver(parts[1], owns[0])
+    parts[2] = partials(*groups[2], grads[2], owns[1])
 
     slots = 3 * width + 16 * (width // shard)
     half = sds((seqs // 2, slots, shard), BF16)
@@ -669,11 +670,14 @@
         [pltpu.VMEM((2 * width, model), F32)],
         50_000_000_000,
         1024,
-    )(parity, after(normed, owns[1]), w_out, *grads, *taps)
-    owns[2], moved[2] = deliver(parts[2], keep, moved[1])
+    )(parity, after(normed, *parts[2]), w_out, *grads, *taps)
+    moved[1] = exchange(after(owns[1], keep, moved[0]), "seq")
     bit = 1
     while True:
         others = lax.ppermute(send, "seq", [(i, i ^ bit) for i in range(seqs)])
+        if bit == 1:
+            owns[2] = deliver(parts[2], others)
+            moved[2] = exchange(after(owns[2], moved[1]), "seq")
         bit *= 2
         if bit == seqs:
             break

time: 216 us -> 206 us (0.954)
  waiting for transfers between devices: 70.6 us -> 58.2 us
  starting transfers between devices: 39.7 us -> 42.3 us
    all_to_all x5, waiting for transfers between devices: 13.5 us -> 5.7 us  [exchange(): return lax.all_to_all(copies, axis, 0, 0, tiled=True)]
    ppermute x3, waiting for transfers between devices: 11.1 us -> 5.38 us  [deliver(): arrived.append(lax.ppermute(part[d], 'tp', send))]
    all_to_all x5, starting transfers between devices: 22.7 us -> 25.5 us  [exchange(): return lax.all_to_all(copies, axis, 0, 0, tiled=True)]
  transfers between devices with their start and end apart: 17 -> 17, of which waited for: 9 -> 6; matrix products, arithmetic and copies ran while one was open for 2% -> 2% of each run, Pallas kernels for 27% -> 28%
where the time goes in v9:
time: 206 us; the launch traced here: 205 us
  Pallas kernels  91.1 us (44%)
  waiting for transfers between devices  58.2 us (28%)
  starting transfers between devices  42.3 us (21%)
  local copies, waits for them, and re-layouts  7.06 us (3%)
  other arithmetic  4.99 us (2%)
    ppermute x3, waiting for transfers between devices, per_device(): others = lax.ppermute(send, 'seq', [(i, i ^ bit) for i in range(seqs)])  43.4 us
    all_to_all x5, starting transfers between devices, exchange(): return lax.all_to_all(copies, axis, 0, 0, tiled=True)  25.5 us
    pallas_call x3, Pallas kernels, back(): call(functools.partial(back_kernel, first, blocks), 'back_conv', (size *...  19 us
    pallas_call x1, Pallas kernels, per_device(): call(gate_kernel, 'gate_conv', (recs,), [smem(), per_record((frames, mode...  15.3 us
    pallas_call x3, Pallas kernels, partials(): call(partial_kernel, 'partial_in', (size * parts_in,), [pl.BlockSpec((hal...  15 us
    pallas_call x1, Pallas kernels, per_device(): call(norm_kernel, 'swish_norm', (recs,), [smem(), smem(), whole((seqs, 2,...  12.1 us
    pallas_call x1, Pallas kernels, per_device(): call(functools.partial(outer_kernel, groups), 'outer_w_in', (recs,), [sme...  10.2 us
    pallas_call x3, Pallas kernels, deliver(): call(add_kernel, 'add', (size * parts_in,), [block] * chips, block, sds(p...  7.68 us
  transfers between devices with their start and end apart: 17, of which 6 were waited for; matrix products, arithmetic and copies ran while one was open for 2% of the time, Pallas kernels for 28%

profile of v9, /device:TPU:0, one launch (start us, length us, event | category | flops | bytes accessed | tf_op | source)
XLA Modules:
  0.0 205.1 jit_solution(1187645716470361875)
XLA Ops:
  0.6 1.0 fusion.1
  1.6 4.9 %collective-permute-start = (bf16[4,8,2048]{2,1,0:T(8,128)(2,1)S(1)}, bf16[4,8,2048]{2,1,0:T(8,128)(2,1)S(1)}, u32[]{:S(2)}, u32[]{:S(2)}) collective-permute-start(bf16[4,8,2048]{2,1,0:T(8,128)(2,1)S(1)} %pad_maximum_fusion.3), channel_id=1, source_target_pairs={{0,4},{4,8},{8,12},{12,16},{16,20},{20,24},{24,28},{1,5},{5,9},{9,... | collective-permute-start | bytes 393224 | tf_op jit(solution)/shard_map/ppermute | solution.py:433
  6.5 1.3 collective-permute-start.1
  7.8 1.3 fusion.5
  9.1 0.6 stack.35.meta
  9.7 3.7 %collective-permute-done.1 = bf16[4,8,2048]{2,1,0:T(8,128)(2,1)S(1)} collective-permute-done((bf16[4,8,2048]{2,1,0:T(8,128)(2,1)S(1)}, bf16[4,8,2048]{2,1,0:T(8,128)(2,1)S(1)}, u32[]{:S(2)}, u32[]{:S(2)}) %collective-permute-start.1) | collective-permute-done | bytes 131104 | tf_op jit(solution)/shard_map/ppermute | solution.py:433
  13.4 0.7 fusion.3
  14.1 15.3 %gate_conv.1 = (f32[4,1024,256]{2,1,0:T(8,128)}, f32[4,1024,256]{2,1,0:T(8,128)}, f32[4,1040,256]{2,1,0:T(8,128)}, f32[8,2,256]{2,1,0:T(2,128)}) custom-call(s32[2,4]{1,0:T(2,128)} %stack.35.meta, bf16[4,1024,1024]{2,1,0:T(8,128)(2,1)} %x.4, bf16[4,16,1024]{2,1,0:T(8,128)(2,1)} %get-tuple-element.104.halo, bf16[1024,256]{1,0:T(8,128)(2,1)} %wv.1, ...), custom_call_target="tpu_custom_call" | custom-call | flops 4294967296 | bytes 20971520 | tf_op jit(solution)/shard_map/gate_conv/pallas_call | solution.py:447
  29.4 1.1 pad_maximum_fusion
  31.6 0.6 pad_maximum_fusion.5.affine
  32.2 0.9 fusion.select
  33.2 5.7 %all-to-all-start = ((f32[8,2,256]{2,1,0:T(2,128)}), f32[8,2,256]{2,1,0:T(2,128)S(1)}, u32[]{:S(2)}, u32[]{:S(2)}) async-start(f32[8,2,256]{2,1,0:T(2,128)} %get-tuple-element.51), calls=%async_computation | async-start | bytes 32768 | tf_op jit(solution)/shard_map/all_to_all | solution.py:393
  38.9 0.9 pad_maximum_fusion.1
  39.8 5.7 %all-to-all-done.stats = f32[8,2,256]{2,1,0:T(2,128)S(1)} async-done(((f32[8,2,256]{2,1,0:T(2,128)}), f32[8,2,256]{2,1,0:T(2,128)S(1)}, u32[]{:S(2)}, u32[]{:S(2)}) %all-to-all-start) | async-done | bytes 16416 | tf_op jit(solution)/shard_map/all_to_all | solution.py:393
  45.5 0.6 copy-done.7
  46.1 12.1 %swish_norm.1 = (bf16[4,1024,256]{2,1,0:T(8,128)(2,1)}, f32[4,1040,256]{2,1,0:T(8,128)}, bf16[4,256,1024]{2,1,0:T(8,128)(2,1)}, f32[8,2,256]{2,1,0:T(2,128)}) custom-call(s32[2,4]{1,0:T(2,128)} %stack.35.meta, f32[1,1]{1,0:T(1,128)} %bitcast.1.count, f32[8,2,256]{2,1,0:T(2,128)} %copy-done.7, f32[2,256]{1,0:T(2,128)} %pad_maximum_fusion.5.affine, ...), custom_call_target="tpu_custom_call" | custom-call | flops 4294967296 | bytes 20971520 | tf_op jit(solution)/shard_map/swish_norm/pallas_call | solution.py:492
  58.1 3.3 %all-to-all-start.1 = ((f32[8,2,256]{2,1,0:T(2,128)}), f32[8,2,256]{2,1,0:T(2,128)S(1)}, u32[]{:S(2)}, u32[]{:S(2)}) async-start(f32[8,2,256]{2,1,0:T(2,128)} %get-tuple-element.55), calls=%async_computation.1 | async-start | bytes 32768 | tf_op jit(solution)/shard_map/all_to_all | solution.py:393
  61.5 7.0 %outer_w_out.1.w_out = f32[256,1024]{1,0:T(8,128)} custom-call(bf16[4,1024,1024]{2,1,0:T(8,128)(2,1)} %grads.3, bf16[4,1024,256]{2,1,0:T(8,128)(2,1)} %get-tuple-element.59.swished), custom_call_target="tpu_custom_call" | custom-call | flops 2147483648 | bytes 8388608 | tf_op jit(solution)/shard_map/outer_w_out/pallas_call | solution.py:537
  68.5 0.6 copy-done.5
  69.1 5.0 %back_conv.3 = (bf16[1024,512]{1,0:T(8,128)(2,1)}, f32[16,256]{1,0:T(8,128)}) custom-call(s32[2,4]{1,0:T(2,128)} %stack.35.meta, f32[1,1]{1,0:T(1,128)} %bitcast.1.count, f32[8,2,256]{2,1,0:T(2,128)} %copy-done.7, f32[8,2,256]{2,1,0:T(2,128)} %copy-done.5, f32[1,256]{1,0:T(1,128)} %bitcast.26, f32[4,1040,256]{2,1,0:T(8,128)} %get-tuple-element.56.gn, ...), custom_call_target="tpu_custom_call" | custom-call | bytes 1024 | tf_op jit(solution)/shard_map/back_conv/pallas_call | solution.py:561
  74.2 5.1 %back_conv.4 = (bf16[1024,512]{1,0:T(8,128)(2,1)}, f32[16,256]{1,0:T(8,128)}) custom-call(s32[2,4]{1,0:T(2,128)} %stack.35.meta, f32[1,1]{1,0:T(1,128)} %bitcast.1.count, f32[8,2,256]{2,1,0:T(2,128)} %copy-done.7, f32[8,2,256]{2,1,0:T(2,128)} %copy-done.5, f32[1,256]{1,0:T(1,128)} %bitcast.27, f32[4,1040,256]{2,1,0:T(8,128)} %get-tuple-element.56.gn, ...), custom_call_target="tpu_custom_call" | custom-call | bytes 1024 | tf_op jit(solution)/shard_map/back_conv/pallas_call | solution.py:561
  79.8 4.2 %partial_in.3 = (bf16[8,1,32,1024]{3,2,1,0:T(8,128)(2,1)}, bf16[8,1,32,1024]{3,2,1,0:T(8,128)(2,1)}) custom-call(bf16[1024,512]{1,0:T(8,128)(2,1)} %get-tuple-element.61.own.refs_0_, bf16[1024,512]{1,0:T(8,128)(2,1)} %collective-permute-done.3.sibling, bf16[512,512]{1,0:T(8,128)(2,1)} %bitcast.21, bf16[512,512]{1,0:T(8,128)(2,1)} %copy-done.3, ...), custom_call_target="tpu_custom_call" | custom-call | bytes 1024 | tf_op jit(solution)/shard_map/partial_in/pallas_call | solution.py:590
  84.1 1.5 collective-permute-start.6
  85.5 8.9 %back_conv.5 = (bf16[2048,512]{1,0:T(8,128)(2,1)}, f32[16,256]{1,0:T(8,128)}) custom-call(s32[2,4]{1,0:T(2,128)} %stack.35.meta, f32[1,1]{1,0:T(1,128)} %bitcast.1.count, f32[8,2,256]{2,1,0:T(2,128)} %copy-done.7, f32[8,2,256]{2,1,0:T(2,128)} %copy-done.5, f32[1,256]{1,0:T(1,128)} %bitcast.28, f32[4,1040,256]{2,1,0:T(8,128)} %get-tuple-element.56.gn, ...), custom_call_target="tpu_custom_call" | custom-call | bytes 1024 | tf_op jit(solution)/shard_map/back_conv/pallas_call | solution.py:561
  94.5 4.3 %partial_in.4 = (bf16[8,1,32,1024]{3,2,1,0:T(8,128)(2,1)}, bf16[8,1,32,1024]{3,2,1,0:T(8,128)(2,1)}) custom-call(bf16[1024,512]{1,0:T(8,128)(2,1)} %get-tuple-element.63.own.refs_1_, bf16[1024,512]{1,0:T(8,128)(2,1)} %collective-permute-done.5.sibling, bf16[512,512]{1,0:T(8,128)(2,1)} %bitcast.22, bf16[512,512]{1,0:T(8,128)(2,1)} %copy-done.3, ...), custom_call_target="tpu_custom_call" | custom-call | bytes 1024 | tf_op jit(solution)/shard_map/partial_in/pallas_call | solution.py:590
  99.3 0.8 copy-done.10
  100.1 2.0 add.115
  102.1 5.9 %all-to-all-start.2 = ((bf16[8,1,32,1024]{3,2,1,0:T(8,128)(2,1)}), bf16[8,1,32,1024]{3,2,1,0:T(8,128)(2,1)S(1)}, u32[]{:S(2)}, u32[]{:S(2)}) async-start(bf16[8,1,32,1024]{3,2,1,0:T(8,128)(2,1)} %add.115), calls=%async_computation.2 | async-start | bytes 1048576 | tf_op jit(solution)/shard_map/all_to_all | solution.py:393
  108.0 5.4 %collective-permute-done.7.refs_1_ = bf16[8,1,32,1024]{3,2,1,0:T(8,128)(2,1)} collective-permute-done((bf16[8,1,32,1024]{3,2,1,0:T(8,128)(2,1)}, bf16[8,1,32,1024]{3,2,1,0:T(8,128)(2,1)}, u32[]{:S(2)}, u32[]{:S(2)}) %collective-permute-start.7) | collective-permute-done | bytes 524320 | tf_op jit(solution)/shard_map/ppermute | solution.py:619
  113.4 2.0 add.116
  115.4 6.5 %partial_in.5 = (bf16[8,2,32,1024]{3,2,1,0:T(8,128)(2,1)}, bf16[8,2,32,1024]{3,2,1,0:T(8,128)(2,1)}) custom-call(bf16[2048,512]{1,0:T(8,128)(2,1)} %get-tuple-element.69.own.refs_2_, bf16[2048,512]{1,0:T(8,128)(2,1)} %collective-permute-done.4.sibling, bf16[512,512]{1,0:T(8,128)(2,1)} %bitcast.23, bf16[512,512]{1,0:T(8,128)(2,1)} %copy-done.3, ...), custom_call_target="tpu_custom_call" | custom-call | bytes 1024 | tf_op jit(solution)/shard_map/partial_in/pallas_call | solution.py:590
  122.4 10.2 %outer_w_in.1 = (bf16[4,800,128]{2,1,0:T(8,128)(2,1)}, bf16[4,800,128]{2,1,0:T(8,128)(2,1)}) custom-call(s32[1,1]{1,0:T(1,128)} %bitcast.11.parity, bf16[4,1024,1024]{2,1,0:T(8,128)(2,1)} %x.4, f32[256,1024]{1,0:T(8,128)} %outer_w_out.1.w_out, bf16[1024,512]{1,0:T(8,128)(2,1)} %get-tuple-element.61.own.refs_0_, ...), custom_call_target="tpu_custom_call" | custom-call | flops 49999998976 | bytes 1024 | tf_op jit(solution)/shard_map/outer_w_in/pallas_call | solution.py:655
  132.6 1.9 collective-permute-start.8
  134.5 4.6 %all-to-all-start.3 = ((bf16[8,1,32,1024]{3,2,1,0:T(8,128)(2,1)}), bf16[8,1,32,1024]{3,2,1,0:T(8,128)(2,1)}, u32[]{:S(2)}, u32[]{:S(2)}) async-start(bf16[8,1,32,1024]{3,2,1,0:T(8,128)(2,1)} %add.116), calls=%async_computation.3 | async-start | bytes 1048576 | tf_op jit(solution)/shard_map/all_to_all | solution.py:393
  139.1 18.4 %collective-permute-done.8.other = bf16[4,800,128]{2,1,0:T(8,128)(2,1)S(1)} collective-permute-done((bf16[4,800,128]{2,1,0:T(8,128)(2,1)}, bf16[4,800,128]{2,1,0:T(8,128)(2,1)S(1)}, u32[]{:S(2)}, u32[]{:S(2)}) %collective-permute-start.8) | collective-permute-done | bytes 819232 | tf_op jit(solution)/shard_map/ppermute | solution.py:677
  157.4 0.9 copy-done.1
  158.3 3.7 %add.117 = bf16[8,2,32,1024]{3,2,1,0:T(8,128)(2,1)} custom-call(bf16[8,2,32,1024]{3,2,1,0:T(8,128)(2,1)} %get-tuple-element.83.refs_0_, bf16[8,2,32,1024]{3,2,1,0:T(8,128)(2,1)} %collective-permute-done.9.refs_1_), custom_call_target="tpu_custom_call" | custom-call | flops 49999998976 | bytes 1024 | tf_op jit(solution)/shard_map/add/pallas_call | solution.py:624
  162.0 5.9 %all-to-all-start.4 = ((bf16[8,2,32,1024]{3,2,1,0:T(8,128)(2,1)}), bf16[8,2,32,1024]{3,2,1,0:T(8,128)(2,1)S(1)}, u32[]{:S(2)}, u32[]{:S(2)}) async-start(bf16[8,2,32,1024]{3,2,1,0:T(8,128)(2,1)} %add.117), calls=%async_computation.4 | async-start | bytes 2097152 | tf_op jit(solution)/shard_map/all_to_all | solution.py:393
  167.9 1.1 copy-done.2
  169.3 2.1 %collective-permute-start.10 = (bf16[2,800,128]{2,1,0:T(8,128)(2,1)S(1)}, bf16[2,800,128]{2,1,0:T(8,128)(2,1)S(1)}, u32[]{:S(2)}, u32[]{:S(2)}) collective-permute-start(bf16[2,800,128]{2,1,0:T(8,128)(2,1)S(1)} %get-tuple-element.88), channel_id=1, source_target_pairs={{0,8},{4,12},{8,0},{12,4},{16,24},{20,28},{24,16},{28,20},{1,9},{5... | collective-permute-start | bytes 1228808 | tf_op jit(solution)/shard_map/ppermute | solution.py:677
  171.4 22.5 %collective-permute-done.10.other = bf16[2,800,128]{2,1,0:T(8,128)(2,1)S(1)} collective-permute-done((bf16[2,800,128]{2,1,0:T(8,128)(2,1)S(1)}, bf16[2,800,128]{2,1,0:T(8,128)(2,1)S(1)}, u32[]{:S(2)}, u32[]{:S(2)}) %collective-permute-start.10) | collective-permute-done | bytes 409632 | tf_op jit(solution)/shard_map/ppermute | solution.py:677
  194.0 3.4 %collective-permute-start.11 = (bf16[1,800,128]{2,1,0:T(8,128)(2,1)S(1)}, bf16[1,800,128]{2,1,0:T(8,128)(2,1)S(1)}, u32[]{:S(2)}, u32[]{:S(2)}) collective-permute-start(bf16[1,800,128]{2,1,0:T(8,128)(2,1)S(1)} %get-tuple-element.90), channel_id=1, source_target_pairs={{0,16},{4,20},{8,24},{12,28},{16,0},{20,4},{24,8},{28,12},{1,17},{... | collective-permute-start | bytes 614408 | tf_op jit(solution)/shard_map/ppermute | solution.py:677
  197.4 0.6 fusion.4
  198.0 0.8 place.3.refs_0_
  198.8 1.9 place.4.refs_0_
  200.7 2.5 %collective-permute-done.11.other = bf16[1,800,128]{2,1,0:T(8,128)(2,1)S(1)} collective-permute-done((bf16[1,800,128]{2,1,0:T(8,128)(2,1)S(1)}, bf16[1,800,128]{2,1,0:T(8,128)(2,1)S(1)}, u32[]{:S(2)}, u32[]{:S(2)}) %collective-permute-start.11) | collective-permute-done | bytes 204832 | tf_op jit(solution)/shard_map/ppermute | solution.py:677
  203.2 0.8 finish.1
  204.0 1.1 place.5
  (46 shorter events, 2.5 us)
Async XLA Ops:
  1.6 8.1 %collective-permute-start = (bf16[4,8,2048]{2,1,0:T(8,128)(2,1)S(1)}, bf16[4,8,2048]{2,1,0:T(8,128)(2,1)S(1)}, u32[]{:S(2)}, u32[]{:S(2)}) collective-permute-start(bf16[4,8,2048]{2,1,0:T(8,128)(2,1)S(1)} %pad_maximum_fusion.3), channel_id=1, source_target_pairs={{0,4},{4,8},{8,12},{12,16},{16,20},{20,24},{24,28},{1,5},{5,9},{9,... | collective-permute-start | bytes 393224 | tf_op jit(solution)/shard_map/ppermute | solution.py:433
  6.5 6.9 %collective-permute-start.1 = (bf16[4,8,2048]{2,1,0:T(8,128)(2,1)S(1)}, bf16[4,8,2048]{2,1,0:T(8,128)(2,1)S(1)}, u32[]{:S(2)}, u32[]{:S(2)}) collective-permute-start(bf16[4,8,2048]{2,1,0:T(8,128)(2,1)S(1)} %pad_maximum_fusion.4), channel_id=1, source_target_pairs={{4,0},{8,4},{12,8},{16,12},{20,16},{24,20},{28,24},{5,1},{9,5},{13... | collective-permute-start | bytes 393224 | tf_op jit(solution)/shard_map/ppermute | solution.py:433
  14.1 15.3 %copy-start.4 = (bf16[1024,256]{1,0:T(8,128)(2,1)S(1)}, bf16[1024,256]{1,0:T(8,128)(2,1)}, u32[]{:S(2)}) copy-start(bf16[1024,256]{1,0:T(8,128)(2,1)} %wv.1) | copy-start | bytes 1572868
  30.6 1.1 copy-start.8
  30.6 1.1 copy-start.9
  30.7 9.0 %collective-permute-start.2 = (bf16[512,512]{1,0:T(8,128)(2,1)S(1)}, bf16[512,512]{1,0:T(8,128)(2,1)S(1)}, u32[]{:S(2)}, u32[]{:S(2)}) collective-permute-start(bf16[512,512]{1,0:T(8,128)(2,1)S(1)} %bitcast.25), channel_id=1, source_target_pairs={{0,1},{1,0},{2,3},{3,2},{4,5},{5,4},{6,7},{7,6},{8,9},{9,8},{10,11... | collective-permute-start | bytes 1572872 | tf_op jit(solution)/shard_map/ppermute | solution.py:486
  33.2 12.3 %all-to-all-start = ((f32[8,2,256]{2,1,0:T(2,128)}), f32[8,2,256]{2,1,0:T(2,128)S(1)}, u32[]{:S(2)}, u32[]{:S(2)}) async-start(f32[8,2,256]{2,1,0:T(2,128)} %get-tuple-element.51), calls=%async_computation | async-start | bytes 32768 | tf_op jit(solution)/shard_map/all_to_all | solution.py:393
  39.8 18.4 %copy-start.3 = (bf16[512,512]{1,0:T(8,128)(2,1)}, bf16[512,512]{1,0:T(8,128)(2,1)S(1)}, u32[]{:S(2)}) copy-start(bf16[512,512]{1,0:T(8,128)(2,1)S(1)} %collective-permute-done.2.w_sibling) | copy-start | bytes 1572868
  45.5 0.6 copy-start.7
  58.1 10.4 %all-to-all-start.1 = ((f32[8,2,256]{2,1,0:T(2,128)}), f32[8,2,256]{2,1,0:T(2,128)S(1)}, u32[]{:S(2)}, u32[]{:S(2)}) async-start(f32[8,2,256]{2,1,0:T(2,128)} %get-tuple-element.55), calls=%async_computation.1 | async-start | bytes 32768 | tf_op jit(solution)/shard_map/all_to_all | solution.py:393
  68.5 0.6 copy-start.5
  74.1 5.7 %collective-permute-start.3 = (bf16[1024,512]{1,0:T(8,128)(2,1)}, bf16[1024,512]{1,0:T(8,128)(2,1)}, u32[]{:S(2)}, u32[]{:S(2)}) collective-permute-start(bf16[1024,512]{1,0:T(8,128)(2,1)} %get-tuple-element.61.own.refs_0_), channel_id=1, source_target_pairs={{0,1},{1,0},{2,3},{3,2},{4,5},{5,4},{6,7},{7,6},{8,9},{9,8},{10,11... | collective-permute-start | bytes 3145736 | tf_op jit(solution)/shard_map/ppermute | solution.py:588
  79.3 15.2 %collective-permute-start.5 = (bf16[1024,512]{1,0:T(8,128)(2,1)}, bf16[1024,512]{1,0:T(8,128)(2,1)}, u32[]{:S(2)}, u32[]{:S(2)}) collective-permute-start(bf16[1024,512]{1,0:T(8,128)(2,1)} %get-tuple-element.63.own.refs_1_), channel_id=1, source_target_pairs={{0,1},{1,0},{2,3},{3,2},{4,5},{5,4},{6,7},{7,6},{8,9},{9,8},{10,11... | collective-permute-start | bytes 3145736 | tf_op jit(solution)/shard_map/ppermute | solution.py:588
  84.1 15.3 %collective-permute-start.6 = (bf16[8,1,32,1024]{3,2,1,0:T(8,128)(2,1)}, bf16[8,1,32,1024]{3,2,1,0:T(8,128)(2,1)S(1)}, u32[]{:S(2)}, u32[]{:S(2)}) collective-permute-start(bf16[8,1,32,1024]{3,2,1,0:T(8,128)(2,1)} %get-tuple-element.67), channel_id=1, source_target_pairs={{0,2},{1,3},{2,0},{3,1},{4,6},{5,7},{6,4},{7,5},{8,10},{9,11},{10,... | collective-permute-start | bytes 1572872 | tf_op jit(solution)/shard_map/ppermute | solution.py:619
  94.4 21.0 %collective-permute-start.4 = (bf16[2048,512]{1,0:T(8,128)(2,1)}, bf16[2048,512]{1,0:T(8,128)(2,1)}, u32[]{:S(2)}, u32[]{:S(2)}) collective-permute-start(bf16[2048,512]{1,0:T(8,128)(2,1)} %get-tuple-element.69.own.refs_2_), channel_id=1, source_target_pairs={{0,1},{1,0},{2,3},{3,2},{4,5},{5,4},{6,7},{7,6},{8,9},{9,8},{10,11... | collective-permute-start | bytes 6291464 | tf_op jit(solution)/shard_map/ppermute | solution.py:588
  98.8 14.6 %collective-permute-start.7 = (bf16[8,1,32,1024]{3,2,1,0:T(8,128)(2,1)}, bf16[8,1,32,1024]{3,2,1,0:T(8,128)(2,1)}, u32[]{:S(2)}, u32[]{:S(2)}) collective-permute-start(bf16[8,1,32,1024]{3,2,1,0:T(8,128)(2,1)} %get-tuple-element.72), channel_id=1, source_target_pairs={{0,2},{1,3},{2,0},{3,1},{4,6},{5,7},{6,4},{7,5},{8,10},{9,11},{10,... | collective-permute-start | bytes 1572872 | tf_op jit(solution)/shard_map/ppermute | solution.py:619
  99.3 0.8 copy-start.10
  102.1 32.4 %all-to-all-start.2 = ((bf16[8,1,32,1024]{3,2,1,0:T(8,128)(2,1)}), bf16[8,1,32,1024]{3,2,1,0:T(8,128)(2,1)S(1)}, u32[]{:S(2)}, u32[]{:S(2)}) async-start(bf16[8,1,32,1024]{3,2,1,0:T(8,128)(2,1)} %add.115), calls=%async_computation.2 | async-start | bytes 1048576 | tf_op jit(solution)/shard_map/all_to_all | solution.py:393
  121.9 36.4 %collective-permute-start.9 = (bf16[8,2,32,1024]{3,2,1,0:T(8,128)(2,1)}, bf16[8,2,32,1024]{3,2,1,0:T(8,128)(2,1)}, u32[]{:S(2)}, u32[]{:S(2)}) collective-permute-start(bf16[8,2,32,1024]{3,2,1,0:T(8,128)(2,1)} %get-tuple-element.77), channel_id=1, source_target_pairs={{0,2},{1,3},{2,0},{3,1},{4,6},{5,7},{6,4},{7,5},{8,10},{9,11},{10,... | collective-permute-start | bytes 3145736 | tf_op jit(solution)/shard_map/ppermute | solution.py:619
  132.6 24.9 %collective-permute-start.8 = (bf16[4,800,128]{2,1,0:T(8,128)(2,1)}, bf16[4,800,128]{2,1,0:T(8,128)(2,1)S(1)}, u32[]{:S(2)}, u32[]{:S(2)}) collective-permute-start(bf16[4,800,128]{2,1,0:T(8,128)(2,1)} %get-tuple-element.82), channel_id=1, source_target_pairs={{0,4},{4,0},{8,12},{12,8},{16,20},{20,16},{24,28},{28,24},{1,5},{5... | collective-permute-start | bytes 2457608 | tf_op jit(solution)/shard_map/ppermute | solution.py:677
  134.5 27.5 %all-to-all-start.3 = ((bf16[8,1,32,1024]{3,2,1,0:T(8,128)(2,1)}), bf16[8,1,32,1024]{3,2,1,0:T(8,128)(2,1)}, u32[]{:S(2)}, u32[]{:S(2)}) async-start(bf16[8,1,32,1024]{3,2,1,0:T(8,128)(2,1)} %add.116), calls=%async_computation.3 | async-start | bytes 1048576 | tf_op jit(solution)/shard_map/all_to_all | solution.py:393
  157.4 0.9 copy-start.1
  162.0 5.9 %copy-start = (bf16[4,800,128]{2,1,0:T(8,128)(2,1)S(1)}, bf16[4,800,128]{2,1,0:T(8,128)(2,1)}, u32[]{:S(2)}) copy-start(bf16[4,800,128]{2,1,0:T(8,128)(2,1)} %get-tuple-element.84.own) | copy-start | bytes 2457604
  162.0 9.3 %copy-start.6 = (f32[8,2,256]{2,1,0:T(2,128)S(1)}, f32[8,2,256]{2,1,0:T(2,128)}, u32[]{:S(2)}) copy-start(f32[8,2,256]{2,1,0:T(2,128)} %copy-done.5) | copy-start | bytes 49156
  162.0 42.0 %all-to-all-start.4 = ((bf16[8,2,32,1024]{3,2,1,0:T(8,128)(2,1)}), bf16[8,2,32,1024]{3,2,1,0:T(8,128)(2,1)S(1)}, u32[]{:S(2)}, u32[]{:S(2)}) async-start(bf16[8,2,32,1024]{3,2,1,0:T(8,128)(2,1)} %add.117), calls=%async_computation.4 | async-start | bytes 2097152 | tf_op jit(solution)/shard_map/all_to_all | solution.py:393
  167.9 1.1 copy-start.2
  169.3 24.6 %collective-permute-start.10 = (bf16[2,800,128]{2,1,0:T(8,128)(2,1)S(1)}, bf16[2,800,128]{2,1,0:T(8,128)(2,1)S(1)}, u32[]{:S(2)}, u32[]{:S(2)}) collective-permute-start(bf16[2,800,128]{2,1,0:T(8,128)(2,1)S(1)} %get-tuple-element.88), channel_id=1, source_target_pairs={{0,8},{4,12},{8,0},{12,4},{16,24},{20,28},{24,16},{28,20},{1,9},{5... | collective-permute-start | bytes 1228808 | tf_op jit(solution)/shard_map/ppermute | solution.py:677
  194.0 9.2 %collective-permute-start.11 = (bf16[1,800,128]{2,1,0:T(8,128)(2,1)S(1)}, bf16[1,800,128]{2,1,0:T(8,128)(2,1)S(1)}, u32[]{:S(2)}, u32[]{:S(2)}) collective-permute-start(bf16[1,800,128]{2,1,0:T(8,128)(2,1)S(1)} %get-tuple-element.90), channel_id=1, source_target_pairs={{0,16},{4,20},{8,24},{12,28},{16,0},{20,4},{24,8},{28,12},{1,17},{... | collective-permute-start | bytes 614408 | tf_op jit(solution)/shard_map/ppermute | solution.py:677

commit v10 on v9

--- a/solution.py
+++ b/solution.py
@@ -297,24 +297,23 @@
     refs[-1][...] = total.astype(BF16)
 
 
-def first_outer_kernel(grads, swished, out):
+def first_outer_kernel(grads, swished, out, acc):
     r = pl.program_id(0)
     add = dot_tn(swished[0], grads[0])
-
-    @pl.when(r == 0)
+    acc[...] = add + jnp.where(r == 0, 0.0, acc[...])
+
+    @pl.when(r == pl.num_programs(0) - 1)
     def _():
-        out[...] = add
-
-    @pl.when(r > 0)
-    def _():
-        out[...] += add
-
-
-def outer_kernel(groups, parity, x, w_out, *refs):
+        shard = out.shape[2]
+        for s in range(out.shape[0]):
+            out[s] = acc[:, s * shard : (s + 1) * shard].astype(BF16)
+
+
+def outer_kernel(groups, parity, x, *refs):
     lefts, taps = refs[: len(groups)], refs[len(groups) : 2 * len(groups)]
     keep, send, acc = refs[2 * len(groups) :]
     records = groups[-1][0] + groups[-1][1]
-    width = w_out.shape[0]
+    width = acc.shape[0] // 2
     shard = keep.shape[2]
     r = pl.program_id(0)
     for (first, size), left in zip(groups, lefts):
@@ -334,9 +333,8 @@
             for j in range(place.shape[0]):
                 at = (2 * j + odd) * shard
                 place[j, : 2 * width, :] = acc[:, at : at + shard].astype(BF16)
-                place[j, 2 * width : 3 * width, :] = w_out[:, at : at + shard].astype(BF16)
                 for q in range(width // shard):
-                    row = 3 * width + 16 * q
+                    row = 2 * width + 16 * q
                     place[j, row : row + 16, :] = tap_sums[:, q * shard : (q + 1) * shard].astype(
                         BF16
                     )
@@ -369,17 +367,18 @@
         write(send, 0)
 
 
-def finish_kernel(kernel, own, other, value, gate, out, taps):
+def finish_kernel(kernel, own, other, ready, value, gate, out, taps):
     width = value.shape[1]
     shard = value.shape[0]
 
     def total(row, size):
         return own[0, row : row + size, :].astype(F32) + other[0, row : row + size, :].astype(F32)
 
-    for i, place in enumerate((value, gate, out)):
-        place[...] = total(i * width, width).T
+    value[...] = total(0, width).T
+    gate[...] = total(width, width).T
+    out[...] = ready[0].astype(F32).T
     for q in range(width // shard):
-        taps[:, q * shard : (q + 1) * shard] = total(3 * width + 16 * q, 16)[:kernel]
+        taps[:, q * shard : (q + 1) * shard] = total(2 * width + 16 * q, 16)[:kernel]
 
 
 def place_kernel(moved, *refs):
@@ -539,9 +538,9 @@
         "outer_w_out",
         (recs,),
         [per_record((frames, model)), per_record((frames, width))],
-        whole((width, model)),
-        sds((width, model), F32),
-        [],
+        whole((seqs, width, shard)),
+        sds((seqs, width, shard), BF16),
+        [pltpu.VMEM((width, model), F32)],
         matmul,
         input_bytes,
     )(grad_out, swished)
@@ -640,6 +639,7 @@
     parts = [None] * 3
     owns = [None] * 3
     moved = [None] * 3
+    w_out_sum = lax.psum_scatter(w_out, "seq", scatter_dimension=0, tiled=True)
     grads[0], taps[0] = back(*groups[0], w_out)
     grads[1], taps[1] = back(*groups[1], grads[0])
     parts[0] = partials(*groups[0], grads[0], grads[1])
@@ -650,13 +650,13 @@
     owns[1] = deliver(parts[1], owns[0])
     parts[2] = partials(*groups[2], grads[2], owns[1])
 
-    slots = 3 * width + 16 * (width // shard)
+    slots = 2 * width + 16 * (width // shard)
     half = sds((seqs // 2, slots, shard), BF16)
     keep, send = call(
         functools.partial(outer_kernel, groups),
         "outer_w_in",
         (recs,),
-        [smem(), per_record((frames, model)), whole((width, model))]
+        [smem(), per_record((frames, model))]
         + [
             pl.BlockSpec(
                 (frames, 2 * width),
@@ -670,7 +670,7 @@
         [pltpu.VMEM((2 * width, model), F32)],
         50_000_000_000,
         1024,
-    )(parity, after(normed, *parts[2]), w_out, *grads, *taps)
+    )(parity, after(normed, *parts[2]), *grads, *taps)
     moved[1] = exchange(after(owns[1], keep, moved[0]), "seq")
     bit = 1
     while True:
@@ -699,14 +699,14 @@
         functools.partial(finish_kernel, kernel),
         "finish",
         (1,),
-        [whole(keep.shape)] * 2,
+        [whole(keep.shape)] * 2 + [whole((1, width, shard))],
         [whole((shard, width))] * 3 + [whole((kernel, width))],
         [sds((shard, width), F32)] * 3 + [sds((kernel, width), F32)],
         [],
         0,
         1024,
         vmem=20,
-    )(keep, others)
+    )(keep, others, w_out_sum)
     grad_in = ()
     for (first, size), part in zip(groups, moved):
         grad_in = (

time: 206 us -> 248 us (1.20)
  waiting for transfers between devices: 58.2 us -> 84.6 us
  between operations: 1.51 us -> 14.9 us
  starting transfers between devices: 42.3 us -> 45.3 us
    reduce_scatter x0 -> x1, waiting for transfers between devices: none -> 35.9 us  [per_device(): w_out_sum = lax.psum_scatter(w_out, 'seq', scatter_dimension=0, tiled=True)]
    ppermute x3, waiting for transfers between devices: 43.4 us -> 33.1 us  [per_device(): others = lax.ppermute(send, 'seq', [(i, i ^ bit) for i in range(seqs)])]
    ppermute x3, starting transfers between devices: 7.38 us -> 10.4 us  [per_device(): others = lax.ppermute(send, 'seq', [(i, i ^ bit) for i in range(seqs)])]
  transfers between devices with their start and end apart: 17 -> 18, of which waited for: 6 -> 6; matrix products, arithmetic and copies ran while one was open for 2% -> 2% of each run, Pallas kernels for 28% -> 23%
where the time goes in v10:
time: 248 us; the launch traced here: 247 us
  Pallas kernels  90.1 us (36%)
  waiting for transfers between devices  84.6 us (34%)
  starting transfers between devices  45.3 us (18%)
  between operations  14.9 us (6%)
  local copies, waits for them, and re-layouts  6.65 us (3%)
  other arithmetic  4.95 us (2%)
    reduce_scatter x1, waiting for transfers between devices, per_device(): w_out_sum = lax.psum_scatter(w_out, 'seq', scatter_dimension=0, tiled=True)  35.9 us
    ppermute x3, waiting for transfers between devices, per_device(): others = lax.ppermute(send, 'seq', [(i, i ^ bit) for i in range(seqs)])  33.1 us
    all_to_all x5, starting transfers between devices, exchange(): return lax.all_to_all(copies, axis, 0, 0, tiled=True)  25.5 us
    pallas_call x3, Pallas kernels, back(): call(functools.partial(back_kernel, first, blocks), 'back_conv', (size *...  19 us
    pallas_call x1, Pallas kernels, per_device(): call(gate_kernel, 'gate_conv', (recs,), [smem(), per_record((frames, mode...  15.3 us
    pallas_call x3, Pallas kernels, partials(): call(partial_kernel, 'partial_in', (size * parts_in,), [pl.BlockSpec((hal...  15 us
    pallas_call x1, Pallas kernels, per_device(): call(norm_kernel, 'swish_norm', (recs,), [smem(), smem(), whole((seqs, 2,...  12.1 us
    ppermute x3, starting transfers between devices, per_device(): others = lax.ppermute(send, 'seq', [(i, i ^ bit) for i in range(seqs)])  10.4 us
  transfers between devices with their start and end apart: 18, of which 6 were waited for; matrix products, arithmetic and copies ran while one was open for 2% of the time, Pallas kernels for 23%

profile of v10, /device:TPU:0, one launch (start us, length us, event | category | flops | bytes accessed | tf_op | source)
XLA Modules:
  0.0 246.5 jit_solution(15490837284929371352)
XLA Ops:
  7.2 1.0 fusion.1
  8.1 4.9 %collective-permute-start = (bf16[4,8,2048]{2,1,0:T(8,128)(2,1)S(1)}, bf16[4,8,2048]{2,1,0:T(8,128)(2,1)S(1)}, u32[]{:S(2)}, u32[]{:S(2)}) collective-permute-start(bf16[4,8,2048]{2,1,0:T(8,128)(2,1)S(1)} %pad_maximum_fusion.3), channel_id=1, source_target_pairs={{0,4},{4,8},{8,12},{12,16},{16,20},{20,24},{24,28},{1,5},{5,9},{9,... | collective-permute-start | bytes 393224 | tf_op jit(solution)/shard_map/ppermute | solution.py:432
  13.1 1.3 collective-permute-start.1
  14.4 1.3 fusion.5
  16.2 3.7 %collective-permute-done.1 = bf16[4,8,2048]{2,1,0:T(8,128)(2,1)S(1)} collective-permute-done((bf16[4,8,2048]{2,1,0:T(8,128)(2,1)S(1)}, bf16[4,8,2048]{2,1,0:T(8,128)(2,1)S(1)}, u32[]{:S(2)}, u32[]{:S(2)}) %collective-permute-start.1) | collective-permute-done | bytes 131104 | tf_op jit(solution)/shard_map/ppermute | solution.py:432
  19.9 0.7 fusion.3
  20.6 15.3 %gate_conv.1 = (f32[4,1024,256]{2,1,0:T(8,128)}, f32[4,1024,256]{2,1,0:T(8,128)}, f32[4,1040,256]{2,1,0:T(8,128)}, f32[8,2,256]{2,1,0:T(2,128)}) custom-call(s32[2,4]{1,0:T(2,128)} %stack.35.meta, bf16[4,1024,1024]{2,1,0:T(8,128)(2,1)} %x.4, bf16[4,16,1024]{2,1,0:T(8,128)(2,1)} %get-tuple-element.104.halo, bf16[1024,256]{1,0:T(8,128)(2,1)} %wv.1, ...), custom_call_target="tpu_custom_call" | custom-call | flops 4294967296 | bytes 20971520 | tf_op jit(solution)/shard_map/gate_conv/pallas_call | solution.py:446
  36.0 1.1 pad_maximum_fusion
  38.2 0.6 pad_maximum_fusion.5.affine
  38.7 0.9 fusion.select
  39.7 5.7 %all-to-all-start = ((f32[8,2,256]{2,1,0:T(2,128)}), f32[8,2,256]{2,1,0:T(2,128)S(1)}, u32[]{:S(2)}, u32[]{:S(2)}) async-start(f32[8,2,256]{2,1,0:T(2,128)} %get-tuple-element.51), calls=%async_computation | async-start | bytes 32768 | tf_op jit(solution)/shard_map/all_to_all | solution.py:392
  45.4 0.8 pad_maximum_fusion.1
  46.3 5.7 %all-to-all-done.stats = f32[8,2,256]{2,1,0:T(2,128)S(1)} async-done(((f32[8,2,256]{2,1,0:T(2,128)}), f32[8,2,256]{2,1,0:T(2,128)S(1)}, u32[]{:S(2)}, u32[]{:S(2)}) %all-to-all-start) | async-done | bytes 16416 | tf_op jit(solution)/shard_map/all_to_all | solution.py:392
  52.0 0.6 copy-done.8
  52.6 12.1 %swish_norm.1 = (bf16[4,1024,256]{2,1,0:T(8,128)(2,1)}, f32[4,1040,256]{2,1,0:T(8,128)}, bf16[4,256,1024]{2,1,0:T(8,128)(2,1)}, f32[8,2,256]{2,1,0:T(2,128)}) custom-call(s32[2,4]{1,0:T(2,128)} %stack.35.meta, f32[1,1]{1,0:T(1,128)} %bitcast.1.count, f32[8,2,256]{2,1,0:T(2,128)} %copy-done.8, f32[2,256]{1,0:T(2,128)} %pad_maximum_fusion.5.affine, ...), custom_call_target="tpu_custom_call" | custom-call | flops 4294967296 | bytes 20971520 | tf_op jit(solution)/shard_map/swish_norm/pallas_call | solution.py:491
  64.7 3.3 %all-to-all-start.1 = ((f32[8,2,256]{2,1,0:T(2,128)}), f32[8,2,256]{2,1,0:T(2,128)S(1)}, u32[]{:S(2)}, u32[]{:S(2)}) async-start(f32[8,2,256]{2,1,0:T(2,128)} %get-tuple-element.55), calls=%async_computation.1 | async-start | bytes 32768 | tf_op jit(solution)/shard_map/all_to_all | solution.py:392
  68.0 6.7 %outer_w_out.1 = bf16[8,256,128]{2,1,0:T(8,128)(2,1)} custom-call(bf16[4,1024,1024]{2,1,0:T(8,128)(2,1)} %grads.3, bf16[4,1024,256]{2,1,0:T(8,128)(2,1)} %get-tuple-element.59.swished), custom_call_target="tpu_custom_call" | custom-call | flops 2147483648 | bytes 8388608 | tf_op jit(solution)/shard_map/outer_w_out/pallas_call | solution.py:536
  74.7 0.6 copy-done.6
  75.3 5.0 %back_conv.3 = (bf16[1024,512]{1,0:T(8,128)(2,1)}, f32[16,256]{1,0:T(8,128)}) custom-call(s32[2,4]{1,0:T(2,128)} %stack.35.meta, f32[1,1]{1,0:T(1,128)} %bitcast.1.count, f32[8,2,256]{2,1,0:T(2,128)} %copy-done.8, f32[8,2,256]{2,1,0:T(2,128)} %copy-done.6, f32[1,256]{1,0:T(1,128)} %bitcast.26, f32[4,1040,256]{2,1,0:T(8,128)} %get-tuple-element.56.gn, ...), custom_call_target="tpu_custom_call" | custom-call | bytes 1024 | tf_op jit(solution)/shard_map/back_conv/pallas_call | solution.py:560
  80.4 5.1 %back_conv.4 = (bf16[1024,512]{1,0:T(8,128)(2,1)}, f32[16,256]{1,0:T(8,128)}) custom-call(s32[2,4]{1,0:T(2,128)} %stack.35.meta, f32[1,1]{1,0:T(1,128)} %bitcast.1.count, f32[8,2,256]{2,1,0:T(2,128)} %copy-done.8, f32[8,2,256]{2,1,0:T(2,128)} %copy-done.6, f32[1,256]{1,0:T(1,128)} %bitcast.27, f32[4,1040,256]{2,1,0:T(8,128)} %get-tuple-element.56.gn, ...), custom_call_target="tpu_custom_call" | custom-call | bytes 1024 | tf_op jit(solution)/shard_map/back_conv/pallas_call | solution.py:560
  86.0 4.2 %partial_in.3 = (bf16[8,1,32,1024]{3,2,1,0:T(8,128)(2,1)}, bf16[8,1,32,1024]{3,2,1,0:T(8,128)(2,1)}) custom-call(bf16[1024,512]{1,0:T(8,128)(2,1)} %get-tuple-element.61.own.refs_0_, bf16[1024,512]{1,0:T(8,128)(2,1)} %collective-permute-done.3.sibling, bf16[512,512]{1,0:T(8,128)(2,1)} %bitcast.21, bf16[512,512]{1,0:T(8,128)(2,1)} %copy-done.4, ...), custom_call_target="tpu_custom_call" | custom-call | bytes 1024 | tf_op jit(solution)/shard_map/partial_in/pallas_call | solution.py:589
  90.3 1.5 collective-permute-start.6
  91.8 8.9 %back_conv.5 = (bf16[2048,512]{1,0:T(8,128)(2,1)}, f32[16,256]{1,0:T(8,128)}) custom-call(s32[2,4]{1,0:T(2,128)} %stack.35.meta, f32[1,1]{1,0:T(1,128)} %bitcast.1.count, f32[8,2,256]{2,1,0:T(2,128)} %copy-done.8, f32[8,2,256]{2,1,0:T(2,128)} %copy-done.6, f32[1,256]{1,0:T(1,128)} %bitcast.28, f32[4,1040,256]{2,1,0:T(8,128)} %get-tuple-element.56.gn, ...), custom_call_target="tpu_custom_call" | custom-call | bytes 1024 | tf_op jit(solution)/shard_map/back_conv/pallas_call | solution.py:560
  100.7 4.3 %partial_in.4 = (bf16[8,1,32,1024]{3,2,1,0:T(8,128)(2,1)}, bf16[8,1,32,1024]{3,2,1,0:T(8,128)(2,1)}) custom-call(bf16[1024,512]{1,0:T(8,128)(2,1)} %get-tuple-element.63.own.refs_1_, bf16[1024,512]{1,0:T(8,128)(2,1)} %collective-permute-done.5.sibling, bf16[512,512]{1,0:T(8,128)(2,1)} %bitcast.22, bf16[512,512]{1,0:T(8,128)(2,1)} %copy-done.4, ...), custom_call_target="tpu_custom_call" | custom-call | bytes 1024 | tf_op jit(solution)/shard_map/partial_in/pallas_call | solution.py:589
  105.6 0.8 copy-done.11
  106.4 2.0 add.118
  108.3 5.9 %all-to-all-start.2 = ((bf16[8,1,32,1024]{3,2,1,0:T(8,128)(2,1)}), bf16[8,1,32,1024]{3,2,1,0:T(8,128)(2,1)S(1)}, u32[]{:S(2)}, u32[]{:S(2)}) async-start(bf16[8,1,32,1024]{3,2,1,0:T(8,128)(2,1)} %add.118), calls=%async_computation.2 | async-start | bytes 1048576 | tf_op jit(solution)/shard_map/all_to_all | solution.py:392
  114.2 5.4 %collective-permute-done.7.refs_1_ = bf16[8,1,32,1024]{3,2,1,0:T(8,128)(2,1)} collective-permute-done((bf16[8,1,32,1024]{3,2,1,0:T(8,128)(2,1)}, bf16[8,1,32,1024]{3,2,1,0:T(8,128)(2,1)}, u32[]{:S(2)}, u32[]{:S(2)}) %collective-permute-start.7) | collective-permute-done | bytes 524320 | tf_op jit(solution)/shard_map/ppermute | solution.py:618
  119.7 2.0 add.119
  121.7 6.5 %partial_in.5 = (bf16[8,2,32,1024]{3,2,1,0:T(8,128)(2,1)}, bf16[8,2,32,1024]{3,2,1,0:T(8,128)(2,1)}) custom-call(bf16[2048,512]{1,0:T(8,128)(2,1)} %get-tuple-element.69.own.refs_2_, bf16[2048,512]{1,0:T(8,128)(2,1)} %collective-permute-done.4.sibling, bf16[512,512]{1,0:T(8,128)(2,1)} %bitcast.23, bf16[512,512]{1,0:T(8,128)(2,1)} %copy-done.4, ...), custom_call_target="tpu_custom_call" | custom-call | bytes 1024 | tf_op jit(solution)/shard_map/partial_in/pallas_call | solution.py:589
  128.7 9.5 %outer_w_in.1 = (bf16[4,544,128]{2,1,0:T(8,128)(2,1)}, bf16[4,544,128]{2,1,0:T(8,128)(2,1)}) custom-call(s32[1,1]{1,0:T(1,128)} %bitcast.11.parity, bf16[4,1024,1024]{2,1,0:T(8,128)(2,1)} %x.4, bf16[1024,512]{1,0:T(8,128)(2,1)} %get-tuple-element.61.own.refs_0_, bf16[1024,512]{1,0:T(8,128)(2,1)} %get-tuple-element.63.own.refs_1_, ...), custom_call_target="tpu_custom_call" | custom-call | flops 49999998976 | bytes 1024 | tf_op jit(solution)/shard_map/outer_w_in/pallas_call | solution.py:655
  138.2 1.9 collective-permute-start.8
  140.1 4.6 %all-to-all-start.3 = ((bf16[8,1,32,1024]{3,2,1,0:T(8,128)(2,1)}), bf16[8,1,32,1024]{3,2,1,0:T(8,128)(2,1)}, u32[]{:S(2)}, u32[]{:S(2)}) async-start(bf16[8,1,32,1024]{3,2,1,0:T(8,128)(2,1)} %add.119), calls=%async_computation.3 | async-start | bytes 1048576 | tf_op jit(solution)/shard_map/all_to_all | solution.py:392
  144.7 12.8 %collective-permute-done.8.other = bf16[4,544,128]{2,1,0:T(8,128)(2,1)S(1)} collective-permute-done((bf16[4,544,128]{2,1,0:T(8,128)(2,1)}, bf16[4,544,128]{2,1,0:T(8,128)(2,1)S(1)}, u32[]{:S(2)}, u32[]{:S(2)}) %collective-permute-start.8) | collective-permute-done | bytes 557088 | tf_op jit(solution)/shard_map/ppermute | solution.py:677
  157.4 0.8 copy-done.1
  158.2 3.7 %add.120 = bf16[8,2,32,1024]{3,2,1,0:T(8,128)(2,1)} custom-call(bf16[8,2,32,1024]{3,2,1,0:T(8,128)(2,1)} %get-tuple-element.83.refs_0_, bf16[8,2,32,1024]{3,2,1,0:T(8,128)(2,1)} %collective-permute-done.9.refs_1_), custom_call_target="tpu_custom_call" | custom-call | flops 49999998976 | bytes 1024 | tf_op jit(solution)/shard_map/add/pallas_call | solution.py:623
  161.9 5.9 %all-to-all-start.4 = ((bf16[8,2,32,1024]{3,2,1,0:T(8,128)(2,1)}), bf16[8,2,32,1024]{3,2,1,0:T(8,128)(2,1)S(1)}, u32[]{:S(2)}, u32[]{:S(2)}) async-start(bf16[8,2,32,1024]{3,2,1,0:T(8,128)(2,1)} %add.120), calls=%async_computation.4 | async-start | bytes 2097152 | tf_op jit(solution)/shard_map/all_to_all | solution.py:392
  167.9 0.7 reduce-scatter.2.cloned.1.call-update
  168.8 2.1 collective-permute-start.10
  170.9 20.4 %collective-permute-done.10.other = bf16[2,544,128]{2,1,0:T(8,128)(2,1)S(1)} collective-permute-done((bf16[2,544,128]{2,1,0:T(8,128)(2,1)S(1)}, bf16[2,544,128]{2,1,0:T(8,128)(2,1)S(1)}, u32[]{:S(2)}, u32[]{:S(2)}) %collective-permute-start.10) | collective-permute-done | bytes 278560 | tf_op jit(solution)/shard_map/ppermute | solution.py:677
  191.3 6.4 %collective-permute-start.11 = (bf16[1,544,128]{2,1,0:T(8,128)(2,1)S(1)}, bf16[1,544,128]{2,1,0:T(8,128)(2,1)S(1)}, u32[]{:S(2)}, u32[]{:S(2)}) collective-permute-start(bf16[1,544,128]{2,1,0:T(8,128)(2,1)S(1)} %get-tuple-element.90), channel_id=1, source_target_pairs={{0,16},{4,20},{8,24},{12,28},{16,0},{20,4},{24,8},{28,12},{1,17},{... | collective-permute-start | bytes 417800 | tf_op jit(solution)/shard_map/ppermute | solution.py:677
  197.7 0.6 fusion.4
  198.3 0.8 place.3.refs_0_
  199.1 1.9 place.4.refs_0_
  201.0 35.9 %reduce-scatter.2.cloned.1.call-done.ready = bf16[1,256,128]{2,1,0:T(8,128)(2,1)} async-done(((bf16[8,256,128]{2,1,0:T(8,128)(2,1)}), bf16[1,256,128]{2,1,0:T(8,128)(2,1)}) %reduce-scatter.2.cloned.1.call-update) | async-done | bytes 65552 | tf_op jit(solution)/shard_map/reduce_scatter | solution.py:642
  236.9 0.8 copy-done.3
  237.7 0.9 finish.1
  238.6 1.1 place.5
  (51 shorter events, 3.0 us)
Async XLA Ops:
  8.1 8.1 %collective-permute-start = (bf16[4,8,2048]{2,1,0:T(8,128)(2,1)S(1)}, bf16[4,8,2048]{2,1,0:T(8,128)(2,1)S(1)}, u32[]{:S(2)}, u32[]{:S(2)}) collective-permute-start(bf16[4,8,2048]{2,1,0:T(8,128)(2,1)S(1)} %pad_maximum_fusion.3), channel_id=1, source_target_pairs={{0,4},{4,8},{8,12},{12,16},{16,20},{20,24},{24,28},{1,5},{5,9},{9,... | collective-permute-start | bytes 393224 | tf_op jit(solution)/shard_map/ppermute | solution.py:432
  13.1 6.9 %collective-permute-start.1 = (bf16[4,8,2048]{2,1,0:T(8,128)(2,1)S(1)}, bf16[4,8,2048]{2,1,0:T(8,128)(2,1)S(1)}, u32[]{:S(2)}, u32[]{:S(2)}) collective-permute-start(bf16[4,8,2048]{2,1,0:T(8,128)(2,1)S(1)} %pad_maximum_fusion.4), channel_id=1, source_target_pairs={{4,0},{8,4},{12,8},{16,12},{20,16},{24,20},{28,24},{5,1},{9,5},{13... | collective-permute-start | bytes 393224 | tf_op jit(solution)/shard_map/ppermute | solution.py:432
  20.6 15.3 %copy-start.5 = (bf16[1024,256]{1,0:T(8,128)(2,1)S(1)}, bf16[1024,256]{1,0:T(8,128)(2,1)}, u32[]{:S(2)}) copy-start(bf16[1024,256]{1,0:T(8,128)(2,1)} %wv.1) | copy-start | bytes 1572868
  37.1 1.1 copy-start.9
  37.1 1.0 copy-start.10
  37.3 9.0 %collective-permute-start.2 = (bf16[512,512]{1,0:T(8,128)(2,1)S(1)}, bf16[512,512]{1,0:T(8,128)(2,1)S(1)}, u32[]{:S(2)}, u32[]{:S(2)}) collective-permute-start(bf16[512,512]{1,0:T(8,128)(2,1)S(1)} %bitcast.25), channel_id=1, source_target_pairs={{0,1},{1,0},{2,3},{3,2},{4,5},{5,4},{6,7},{7,6},{8,9},{9,8},{10,11... | collective-permute-start | bytes 1572872 | tf_op jit(solution)/shard_map/ppermute | solution.py:485
  39.7 12.3 %all-to-all-start = ((f32[8,2,256]{2,1,0:T(2,128)}), f32[8,2,256]{2,1,0:T(2,128)S(1)}, u32[]{:S(2)}, u32[]{:S(2)}) async-start(f32[8,2,256]{2,1,0:T(2,128)} %get-tuple-element.51), calls=%async_computation | async-start | bytes 32768 | tf_op jit(solution)/shard_map/all_to_all | solution.py:392
  46.3 18.4 %copy-start.4 = (bf16[512,512]{1,0:T(8,128)(2,1)}, bf16[512,512]{1,0:T(8,128)(2,1)S(1)}, u32[]{:S(2)}) copy-start(bf16[512,512]{1,0:T(8,128)(2,1)S(1)} %collective-permute-done.2.w_sibling) | copy-start | bytes 1572868
  52.0 0.6 copy-start.8
  64.7 10.1 %all-to-all-start.1 = ((f32[8,2,256]{2,1,0:T(2,128)}), f32[8,2,256]{2,1,0:T(2,128)S(1)}, u32[]{:S(2)}, u32[]{:S(2)}) async-start(f32[8,2,256]{2,1,0:T(2,128)} %get-tuple-element.55), calls=%async_computation.1 | async-start | bytes 32768 | tf_op jit(solution)/shard_map/all_to_all | solution.py:392
  74.7 0.6 copy-start.6
  80.3 5.7 %collective-permute-start.3 = (bf16[1024,512]{1,0:T(8,128)(2,1)}, bf16[1024,512]{1,0:T(8,128)(2,1)}, u32[]{:S(2)}, u32[]{:S(2)}) collective-permute-start(bf16[1024,512]{1,0:T(8,128)(2,1)} %get-tuple-element.61.own.refs_0_), channel_id=1, source_target_pairs={{0,1},{1,0},{2,3},{3,2},{4,5},{5,4},{6,7},{7,6},{8,9},{9,8},{10,11... | collective-permute-start | bytes 3145736 | tf_op jit(solution)/shard_map/ppermute | solution.py:587
  85.5 15.2 %collective-permute-start.5 = (bf16[1024,512]{1,0:T(8,128)(2,1)}, bf16[1024,512]{1,0:T(8,128)(2,1)}, u32[]{:S(2)}, u32[]{:S(2)}) collective-permute-start(bf16[1024,512]{1,0:T(8,128)(2,1)} %get-tuple-element.63.own.refs_1_), channel_id=1, source_target_pairs={{0,1},{1,0},{2,3},{3,2},{4,5},{5,4},{6,7},{7,6},{8,9},{9,8},{10,11... | collective-permute-start | bytes 3145736 | tf_op jit(solution)/shard_map/ppermute | solution.py:587
  90.3 15.3 %collective-permute-start.6 = (bf16[8,1,32,1024]{3,2,1,0:T(8,128)(2,1)}, bf16[8,1,32,1024]{3,2,1,0:T(8,128)(2,1)S(1)}, u32[]{:S(2)}, u32[]{:S(2)}) collective-permute-start(bf16[8,1,32,1024]{3,2,1,0:T(8,128)(2,1)} %get-tuple-element.67), channel_id=1, source_target_pairs={{0,2},{1,3},{2,0},{3,1},{4,6},{5,7},{6,4},{7,5},{8,10},{9,11},{10,... | collective-permute-start | bytes 1572872 | tf_op jit(solution)/shard_map/ppermute | solution.py:618
  100.6 21.0 %collective-permute-start.4 = (bf16[2048,512]{1,0:T(8,128)(2,1)}, bf16[2048,512]{1,0:T(8,128)(2,1)}, u32[]{:S(2)}, u32[]{:S(2)}) collective-permute-start(bf16[2048,512]{1,0:T(8,128)(2,1)} %get-tuple-element.69.own.refs_2_), channel_id=1, source_target_pairs={{0,1},{1,0},{2,3},{3,2},{4,5},{5,4},{6,7},{7,6},{8,9},{9,8},{10,11... | collective-permute-start | bytes 6291464 | tf_op jit(solution)/shard_map/ppermute | solution.py:587
  105.0 14.6 %collective-permute-start.7 = (bf16[8,1,32,1024]{3,2,1,0:T(8,128)(2,1)}, bf16[8,1,32,1024]{3,2,1,0:T(8,128)(2,1)}, u32[]{:S(2)}, u32[]{:S(2)}) collective-permute-start(bf16[8,1,32,1024]{3,2,1,0:T(8,128)(2,1)} %get-tuple-element.72), channel_id=1, source_target_pairs={{0,2},{1,3},{2,0},{3,1},{4,6},{5,7},{6,4},{7,5},{8,10},{9,11},{10,... | collective-permute-start | bytes 1572872 | tf_op jit(solution)/shard_map/ppermute | solution.py:618
  105.6 0.8 copy-start.11
  108.3 31.8 %all-to-all-start.2 = ((bf16[8,1,32,1024]{3,2,1,0:T(8,128)(2,1)}), bf16[8,1,32,1024]{3,2,1,0:T(8,128)(2,1)S(1)}, u32[]{:S(2)}, u32[]{:S(2)}) async-start(bf16[8,1,32,1024]{3,2,1,0:T(8,128)(2,1)} %add.118), calls=%async_computation.2 | async-start | bytes 1048576 | tf_op jit(solution)/shard_map/all_to_all | solution.py:392
  128.1 30.1 %collective-permute-start.9 = (bf16[8,2,32,1024]{3,2,1,0:T(8,128)(2,1)}, bf16[8,2,32,1024]{3,2,1,0:T(8,128)(2,1)}, u32[]{:S(2)}, u32[]{:S(2)}) collective-permute-start(bf16[8,2,32,1024]{3,2,1,0:T(8,128)(2,1)} %get-tuple-element.77), channel_id=1, source_target_pairs={{0,2},{1,3},{2,0},{3,1},{4,6},{5,7},{6,4},{7,5},{8,10},{9,11},{10,... | collective-permute-start | bytes 3145736 | tf_op jit(solution)/shard_map/ppermute | solution.py:618
  138.2 19.2 %collective-permute-start.8 = (bf16[4,544,128]{2,1,0:T(8,128)(2,1)}, bf16[4,544,128]{2,1,0:T(8,128)(2,1)S(1)}, u32[]{:S(2)}, u32[]{:S(2)}) collective-permute-start(bf16[4,544,128]{2,1,0:T(8,128)(2,1)} %get-tuple-element.82), channel_id=1, source_target_pairs={{0,4},{4,0},{8,12},{12,8},{16,20},{20,16},{24,28},{28,24},{1,5},{5... | collective-permute-start | bytes 1671176 | tf_op jit(solution)/shard_map/ppermute | solution.py:677
  140.1 21.8 %all-to-all-start.3 = ((bf16[8,1,32,1024]{3,2,1,0:T(8,128)(2,1)}), bf16[8,1,32,1024]{3,2,1,0:T(8,128)(2,1)}, u32[]{:S(2)}, u32[]{:S(2)}) async-start(bf16[8,1,32,1024]{3,2,1,0:T(8,128)(2,1)} %add.119), calls=%async_computation.3 | async-start | bytes 1048576 | tf_op jit(solution)/shard_map/all_to_all | solution.py:392
  157.4 0.8 copy-start.1
  161.9 6.7 %copy-start = (bf16[4,544,128]{2,1,0:T(8,128)(2,1)S(1)}, bf16[4,544,128]{2,1,0:T(8,128)(2,1)}, u32[]{:S(2)}) copy-start(bf16[4,544,128]{2,1,0:T(8,128)(2,1)} %get-tuple-element.84.own) | copy-start | bytes 1671172
  161.9 6.7 %copy-start.2 = (bf16[4,544,128]{2,1,0:T(8,128)(2,1)S(1)}, bf16[4,544,128]{2,1,0:T(8,128)(2,1)}, u32[]{:S(2)}) copy-start(bf16[4,544,128]{2,1,0:T(8,128)(2,1)} %copy-done.1) | copy-start | bytes 1671172
  161.9 8.9 %copy-start.7 = (f32[8,2,256]{2,1,0:T(2,128)S(1)}, f32[8,2,256]{2,1,0:T(2,128)}, u32[]{:S(2)}) copy-start(f32[8,2,256]{2,1,0:T(2,128)} %copy-done.6) | copy-start | bytes 49156
  161.9 76.7 %all-to-all-start.4 = ((bf16[8,2,32,1024]{3,2,1,0:T(8,128)(2,1)}), bf16[8,2,32,1024]{3,2,1,0:T(8,128)(2,1)S(1)}, u32[]{:S(2)}, u32[]{:S(2)}) async-start(bf16[8,2,32,1024]{3,2,1,0:T(8,128)(2,1)} %add.120), calls=%async_computation.4 | async-start | bytes 2097152 | tf_op jit(solution)/shard_map/all_to_all | solution.py:392
  167.8 69.1 %reduce-scatter.2.cloned.1.call-start = ((), (), s32[]{:S(2)}) async-start(), calls=%async_computation.6 | async-start | bytes 589824 | tf_op jit(solution)/shard_map/reduce_scatter | solution.py:642
  168.8 22.5 %collective-permute-start.10 = (bf16[2,544,128]{2,1,0:T(8,128)(2,1)S(1)}, bf16[2,544,128]{2,1,0:T(8,128)(2,1)S(1)}, u32[]{:S(2)}, u32[]{:S(2)}) collective-permute-start(bf16[2,544,128]{2,1,0:T(8,128)(2,1)S(1)} %get-tuple-element.88), channel_id=1, source_target_pairs={{0,8},{4,12},{8,0},{12,4},{16,24},{20,28},{24,16},{28,20},{1,9},{5... | collective-permute-start | bytes 835592 | tf_op jit(solution)/shard_map/ppermute | solution.py:677
  191.3 45.6 %collective-permute-start.11 = (bf16[1,544,128]{2,1,0:T(8,128)(2,1)S(1)}, bf16[1,544,128]{2,1,0:T(8,128)(2,1)S(1)}, u32[]{:S(2)}, u32[]{:S(2)}) collective-permute-start(bf16[1,544,128]{2,1,0:T(8,128)(2,1)S(1)} %get-tuple-element.90), channel_id=1, source_target_pairs={{0,16},{4,20},{8,24},{12,28},{16,0},{20,4},{24,8},{28,12},{1,17},{... | collective-permute-start | bytes 417800 | tf_op jit(solution)/shard_map/ppermute | solution.py:677
  236.9 0.8 copy-start.3
Sparse Core Ops, SparseCore 0:
  172.0 64.8 reduce-scatter.1

commit v11 on v9

--- a/solution.py
+++ b/solution.py
@@ -10,6 +10,7 @@
 EPSILON = 1e-05
 EDGE = 8
 LANES = 128
+LONG = 50_000_000_000
 F32 = jnp.float32
 BF16 = jnp.bfloat16
 
@@ -612,7 +613,7 @@
             1024,
         )(mine, sibling, after(w_own, *earlier), w_sibling, picked)
 
-    def deliver(part, *earlier):
+    def deliver(part, weight, *earlier):
         arrived = []
         for d in range(1, chips):
             send = [(i, ((i // 2 + d) % chips) * 2 + i % 2) for i in range(tps)]
@@ -629,7 +630,7 @@
             block,
             sds(part[0].shape, BF16),
             [],
-            50_000_000_000,
+            weight,
             1024,
         )(after(part[0], *earlier), *arrived)
         return own
@@ -645,10 +646,8 @@
     parts[0] = partials(*groups[0], grads[0], grads[1])
     grads[2], taps[2] = back(*groups[2], *parts[0])
     parts[1] = partials(*groups[1], grads[1], grads[2])
-    owns[0] = deliver(parts[0], *parts[1])
+    owns[0] = deliver(parts[0], LONG, *parts[1])
     moved[0] = exchange(owns[0], "seq")
-    owns[1] = deliver(parts[1], owns[0])
-    parts[2] = partials(*groups[2], grads[2], owns[1])
 
     slots = 3 * width + 16 * (width // shard)
     half = sds((seqs // 2, slots, shard), BF16)
@@ -668,19 +667,20 @@
         [whole(half.shape)] * 2,
         [half] * 2,
         [pltpu.VMEM((2 * width, model), F32)],
-        50_000_000_000,
+        LONG,
         1024,
-    )(parity, after(normed, *parts[2]), w_out, *grads, *taps)
-    moved[1] = exchange(after(owns[1], keep, moved[0]), "seq")
+    )(parity, after(normed, owns[0]), w_out, *grads, *taps)
+    owns[1] = deliver(parts[1], LONG, keep)
+    moved[1] = exchange(after(owns[1], moved[0]), "seq")
+    parts[2] = partials(*groups[2], grads[2], owns[1])
     bit = 1
     while True:
         others = lax.ppermute(send, "seq", [(i, i ^ bit) for i in range(seqs)])
-        if bit == 1:
-            owns[2] = deliver(parts[2], others)
-            moved[2] = exchange(after(owns[2], moved[1]), "seq")
         bit *= 2
         if bit == seqs:
             break
+        if bit == 2:
+            keep = after(keep, *parts[2])
         shape = (keep.shape[0] // 2,) + keep.shape[1:]
         side = ((seq_at // bit) % 2).astype(jnp.int32).reshape(1, 1)
         keep, send = call(
@@ -691,10 +691,13 @@
             [whole(shape)] * 2,
             [sds(shape, BF16)] * 2,
             [],
-            0,
+            LONG if bit == 2 else 0,
             1024,
             vmem=20,
         )(side, keep, others)
+        if bit == min(4, seqs // 2):
+            owns[2] = deliver(parts[2], 0, keep, moved[1])
+            moved[2] = exchange(owns[2], "seq")
     w_value, w_gate, w_out, grad_taps = call(
         functools.partial(finish_kernel, kernel),
         "finish",

time: 206 us -> 204 us (level)
  waiting for transfers between devices: 58.2 us -> 55.1 us
    ppermute x3, waiting for transfers between devices: 5.38 us -> 1.27 us  [deliver(): arrived.append(lax.ppermute(part[d], 'tp', send))]
  transfers between devices with their start and end apart: 17 -> 17, of which waited for: 6 -> 7; matrix products, arithmetic and copies ran while one was open for 2% -> 2% of each run, Pallas kernels for 28% -> 27%
where the time goes in v11:
time: 204 us; the launch traced here: 203 us
  Pallas kernels  92.3 us (45%)
  waiting for transfers between devices  55.1 us (27%)
  starting transfers between devices  42.4 us (21%)
  local copies, waits for them, and re-layouts  6.16 us (3%)
  other arithmetic  5 us (2%)
    ppermute x3, waiting for transfers between devices, per_device(): others = lax.ppermute(send, 'seq', [(i, i ^ bit) for i in range(seqs)])  43.8 us
    all_to_all x5, starting transfers between devices, exchange(): return lax.all_to_all(copies, axis, 0, 0, tiled=True)  24.8 us
    pallas_call x3, Pallas kernels, back(): call(functools.partial(back_kernel, first, blocks), 'back_conv', (size *...  19 us
    pallas_call x1, Pallas kernels, per_device(): call(gate_kernel, 'gate_conv', (recs,), [smem(), per_record((frames, mode...  15.3 us
    pallas_call x3, Pallas kernels, partials(): call(partial_kernel, 'partial_in', (size * parts_in,), [pl.BlockSpec((hal...  15 us
    pallas_call x1, Pallas kernels, per_device(): call(norm_kernel, 'swish_norm', (recs,), [smem(), smem(), whole((seqs, 2,...  12.1 us
    pallas_call x1, Pallas kernels, per_device(): call(functools.partial(outer_kernel, groups), 'outer_w_in', (recs,), [sme...  10.2 us
    pallas_call x3, Pallas kernels, deliver(): call(add_kernel, 'add', (size * parts_in,), [block] * chips, block, sds(p...  7.66 us
  transfers between devices with their start and end apart: 17, of which 7 were waited for; matrix products, arithmetic and copies ran while one was open for 2% of the time, Pallas kernels for 27%

profile of v11, /device:TPU:0, one launch (start us, length us, event | category | flops | bytes accessed | tf_op | source)
XLA Modules:
  0.0 202.6 jit_solution(15340954397740109283)
XLA Ops:
  0.6 1.0 fusion.1
  1.6 4.9 %collective-permute-start = (bf16[4,8,2048]{2,1,0:T(8,128)(2,1)S(1)}, bf16[4,8,2048]{2,1,0:T(8,128)(2,1)S(1)}, u32[]{:S(2)}, u32[]{:S(2)}) collective-permute-start(bf16[4,8,2048]{2,1,0:T(8,128)(2,1)S(1)} %pad_maximum_fusion.3), channel_id=1, source_target_pairs={{0,4},{4,8},{8,12},{12,16},{16,20},{20,24},{24,28},{1,5},{5,9},{9,... | collective-permute-start | bytes 393224 | tf_op jit(solution)/shard_map/ppermute | solution.py:434
  6.5 1.3 collective-permute-start.1
  7.8 1.3 fusion.5
  9.7 3.7 %collective-permute-done.1 = bf16[4,8,2048]{2,1,0:T(8,128)(2,1)S(1)} collective-permute-done((bf16[4,8,2048]{2,1,0:T(8,128)(2,1)S(1)}, bf16[4,8,2048]{2,1,0:T(8,128)(2,1)S(1)}, u32[]{:S(2)}, u32[]{:S(2)}) %collective-permute-start.1) | collective-permute-done | bytes 131104 | tf_op jit(solution)/shard_map/ppermute | solution.py:434
  13.4 0.7 fusion.3
  14.1 15.3 %gate_conv.1 = (f32[4,1024,256]{2,1,0:T(8,128)}, f32[4,1024,256]{2,1,0:T(8,128)}, f32[4,1040,256]{2,1,0:T(8,128)}, f32[8,2,256]{2,1,0:T(2,128)}) custom-call(s32[2,4]{1,0:T(2,128)} %stack.35.meta, bf16[4,1024,1024]{2,1,0:T(8,128)(2,1)} %x.4, bf16[4,16,1024]{2,1,0:T(8,128)(2,1)} %get-tuple-element.104.halo, bf16[1024,256]{1,0:T(8,128)(2,1)} %wv.1, ...), custom_call_target="tpu_custom_call" | custom-call | flops 4294967296 | bytes 20971520 | tf_op jit(solution)/shard_map/gate_conv/pallas_call | solution.py:448
  29.4 1.1 pad_maximum_fusion
  31.6 0.6 pad_maximum_fusion.5.affine
  32.2 1.0 fusion.select
  33.2 5.7 %all-to-all-start = ((f32[8,2,256]{2,1,0:T(2,128)}), f32[8,2,256]{2,1,0:T(2,128)S(1)}, u32[]{:S(2)}, u32[]{:S(2)}) async-start(f32[8,2,256]{2,1,0:T(2,128)} %get-tuple-element.51), calls=%async_computation | async-start | bytes 32768 | tf_op jit(solution)/shard_map/all_to_all | solution.py:394
  38.9 0.9 pad_maximum_fusion.1
  39.8 5.7 %all-to-all-done.stats = f32[8,2,256]{2,1,0:T(2,128)S(1)} async-done(((f32[8,2,256]{2,1,0:T(2,128)}), f32[8,2,256]{2,1,0:T(2,128)S(1)}, u32[]{:S(2)}, u32[]{:S(2)}) %all-to-all-start) | async-done | bytes 16416 | tf_op jit(solution)/shard_map/all_to_all | solution.py:394
  45.5 0.6 copy-done.5
  46.1 12.1 %swish_norm.1 = (bf16[4,1024,256]{2,1,0:T(8,128)(2,1)}, f32[4,1040,256]{2,1,0:T(8,128)}, bf16[4,256,1024]{2,1,0:T(8,128)(2,1)}, f32[8,2,256]{2,1,0:T(2,128)}) custom-call(s32[2,4]{1,0:T(2,128)} %stack.35.meta, f32[1,1]{1,0:T(1,128)} %bitcast.1.count, f32[8,2,256]{2,1,0:T(2,128)} %copy-done.5, f32[2,256]{1,0:T(2,128)} %pad_maximum_fusion.5.affine, ...), custom_call_target="tpu_custom_call" | custom-call | flops 4294967296 | bytes 20971520 | tf_op jit(solution)/shard_map/swish_norm/pallas_call | solution.py:493
  58.2 3.3 %all-to-all-start.1 = ((f32[8,2,256]{2,1,0:T(2,128)}), f32[8,2,256]{2,1,0:T(2,128)S(1)}, u32[]{:S(2)}, u32[]{:S(2)}) async-start(f32[8,2,256]{2,1,0:T(2,128)} %get-tuple-element.55), calls=%async_computation.1 | async-start | bytes 32768 | tf_op jit(solution)/shard_map/all_to_all | solution.py:394
  61.5 7.0 %outer_w_out.1.w_out = f32[256,1024]{1,0:T(8,128)} custom-call(bf16[4,1024,1024]{2,1,0:T(8,128)(2,1)} %grads.3, bf16[4,1024,256]{2,1,0:T(8,128)(2,1)} %get-tuple-element.59.swished), custom_call_target="tpu_custom_call" | custom-call | flops 2147483648 | bytes 8388608 | tf_op jit(solution)/shard_map/outer_w_out/pallas_call | solution.py:538
  68.5 0.6 copy-done.3
  69.1 5.0 %back_conv.3 = (bf16[1024,512]{1,0:T(8,128)(2,1)}, f32[16,256]{1,0:T(8,128)}) custom-call(s32[2,4]{1,0:T(2,128)} %stack.35.meta, f32[1,1]{1,0:T(1,128)} %bitcast.1.count, f32[8,2,256]{2,1,0:T(2,128)} %copy-done.5, f32[8,2,256]{2,1,0:T(2,128)} %copy-done.3, f32[1,256]{1,0:T(1,128)} %bitcast.26, f32[4,1040,256]{2,1,0:T(8,128)} %get-tuple-element.56.gn, ...), custom_call_target="tpu_custom_call" | custom-call | bytes 1024 | tf_op jit(solution)/shard_map/back_conv/pallas_call | solution.py:562
  74.2 5.1 %back_conv.4 = (bf16[1024,512]{1,0:T(8,128)(2,1)}, f32[16,256]{1,0:T(8,128)}) custom-call(s32[2,4]{1,0:T(2,128)} %stack.35.meta, f32[1,1]{1,0:T(1,128)} %bitcast.1.count, f32[8,2,256]{2,1,0:T(2,128)} %copy-done.5, f32[8,2,256]{2,1,0:T(2,128)} %copy-done.3, f32[1,256]{1,0:T(1,128)} %bitcast.27, f32[4,1040,256]{2,1,0:T(8,128)} %get-tuple-element.56.gn, ...), custom_call_target="tpu_custom_call" | custom-call | bytes 1024 | tf_op jit(solution)/shard_map/back_conv/pallas_call | solution.py:562
  79.8 4.2 %partial_in.3 = (bf16[8,1,32,1024]{3,2,1,0:T(8,128)(2,1)}, bf16[8,1,32,1024]{3,2,1,0:T(8,128)(2,1)}) custom-call(bf16[1024,512]{1,0:T(8,128)(2,1)} %get-tuple-element.61.own.refs_0_, bf16[1024,512]{1,0:T(8,128)(2,1)} %collective-permute-done.3.sibling, bf16[512,512]{1,0:T(8,128)(2,1)} %bitcast.21, bf16[512,512]{1,0:T(8,128)(2,1)} %copy-done.1, ...), custom_call_target="tpu_custom_call" | custom-call | bytes 1024 | tf_op jit(solution)/shard_map/partial_in/pallas_call | solution.py:591
  84.1 1.5 collective-permute-start.6
  85.6 8.9 %back_conv.5 = (bf16[2048,512]{1,0:T(8,128)(2,1)}, f32[16,256]{1,0:T(8,128)}) custom-call(s32[2,4]{1,0:T(2,128)} %stack.35.meta, f32[1,1]{1,0:T(1,128)} %bitcast.1.count, f32[8,2,256]{2,1,0:T(2,128)} %copy-done.5, f32[8,2,256]{2,1,0:T(2,128)} %copy-done.3, f32[1,256]{1,0:T(1,128)} %bitcast.28, f32[4,1040,256]{2,1,0:T(8,128)} %get-tuple-element.56.gn, ...), custom_call_target="tpu_custom_call" | custom-call | bytes 1024 | tf_op jit(solution)/shard_map/back_conv/pallas_call | solution.py:562
  94.5 4.3 %partial_in.4 = (bf16[8,1,32,1024]{3,2,1,0:T(8,128)(2,1)}, bf16[8,1,32,1024]{3,2,1,0:T(8,128)(2,1)}) custom-call(bf16[1024,512]{1,0:T(8,128)(2,1)} %get-tuple-element.63.own.refs_1_, bf16[1024,512]{1,0:T(8,128)(2,1)} %collective-permute-done.5.sibling, bf16[512,512]{1,0:T(8,128)(2,1)} %bitcast.22, bf16[512,512]{1,0:T(8,128)(2,1)} %copy-done.1, ...), custom_call_target="tpu_custom_call" | custom-call | bytes 1024 | tf_op jit(solution)/shard_map/partial_in/pallas_call | solution.py:591
  99.4 0.8 copy-done.8
  100.1 2.0 add.115
  102.1 5.9 %all-to-all-start.2 = ((bf16[8,1,32,1024]{3,2,1,0:T(8,128)(2,1)}), bf16[8,1,32,1024]{3,2,1,0:T(8,128)(2,1)S(1)}, u32[]{:S(2)}, u32[]{:S(2)}) async-start(bf16[8,1,32,1024]{3,2,1,0:T(8,128)(2,1)} %add.115), calls=%async_computation.2 | async-start | bytes 1048576 | tf_op jit(solution)/shard_map/all_to_all | solution.py:394
  108.0 10.2 %outer_w_in.1 = (bf16[4,800,128]{2,1,0:T(8,128)(2,1)}, bf16[4,800,128]{2,1,0:T(8,128)(2,1)}) custom-call(s32[1,1]{1,0:T(1,128)} %bitcast.11.parity, bf16[4,1024,1024]{2,1,0:T(8,128)(2,1)} %x.4, f32[256,1024]{1,0:T(8,128)} %outer_w_out.1.w_out, bf16[1024,512]{1,0:T(8,128)(2,1)} %get-tuple-element.61.own.refs_0_, ...), custom_call_target="tpu_custom_call" | custom-call | flops 49999998976 | bytes 1024 | tf_op jit(solution)/shard_map/outer_w_in/pallas_call | solution.py:654
  118.2 2.0 collective-permute-start.8
  120.3 2.0 add.116
  122.3 0.6 all-to-all-done.2.moved
  122.9 4.1 %all-to-all-start.3 = ((bf16[8,1,32,1024]{3,2,1,0:T(8,128)(2,1)}), bf16[8,1,32,1024]{3,2,1,0:T(8,128)(2,1)}, u32[]{:S(2)}, u32[]{:S(2)}) async-start(bf16[8,1,32,1024]{3,2,1,0:T(8,128)(2,1)} %add.116), calls=%async_computation.3 | async-start | bytes 1048576 | tf_op jit(solution)/shard_map/all_to_all | solution.py:394
  127.1 6.5 %partial_in.5 = (bf16[8,2,32,1024]{3,2,1,0:T(8,128)(2,1)}, bf16[8,2,32,1024]{3,2,1,0:T(8,128)(2,1)}) custom-call(bf16[2048,512]{1,0:T(8,128)(2,1)} %get-tuple-element.69.refs_2_.own, bf16[2048,512]{1,0:T(8,128)(2,1)} %collective-permute-done.4.sibling, bf16[512,512]{1,0:T(8,128)(2,1)} %bitcast.23, bf16[512,512]{1,0:T(8,128)(2,1)} %copy-done.1, ...), custom_call_target="tpu_custom_call" | custom-call | bytes 1024 | tf_op jit(solution)/shard_map/partial_in/pallas_call | solution.py:591
  133.6 1.5 collective-permute-start.10
  135.0 8.7 %collective-permute-done.8.other = bf16[4,800,128]{2,1,0:T(8,128)(2,1)} collective-permute-done((bf16[4,800,128]{2,1,0:T(8,128)(2,1)}, bf16[4,800,128]{2,1,0:T(8,128)(2,1)}, u32[]{:S(2)}, u32[]{:S(2)}) %collective-permute-start.8) | collective-permute-done | bytes 819232 | tf_op jit(solution)/shard_map/ppermute | solution.py:678
  143.8 1.1 copy-done
  144.9 1.3 fold.2
  146.3 2.2 %collective-permute-start.9 = (bf16[2,800,128]{2,1,0:T(8,128)(2,1)S(1)}, bf16[2,800,128]{2,1,0:T(8,128)(2,1)S(1)}, u32[]{:S(2)}, u32[]{:S(2)}) collective-permute-start(bf16[2,800,128]{2,1,0:T(8,128)(2,1)S(1)} %get-tuple-element.86), channel_id=1, source_target_pairs={{0,8},{4,12},{8,0},{12,4},{16,24},{20,28},{24,16},{28,20},{1,9},{5... | collective-permute-start | bytes 1228808 | tf_op jit(solution)/shard_map/ppermute | solution.py:678
  148.5 8.3 %collective-permute-done.9.other = bf16[2,800,128]{2,1,0:T(8,128)(2,1)S(1)} collective-permute-done((bf16[2,800,128]{2,1,0:T(8,128)(2,1)S(1)}, bf16[2,800,128]{2,1,0:T(8,128)(2,1)S(1)}, u32[]{:S(2)}, u32[]{:S(2)}) %collective-permute-start.9) | collective-permute-done | bytes 409632 | tf_op jit(solution)/shard_map/ppermute | solution.py:678
  156.9 1.3 collective-permute-done.10.refs_1_
  158.2 3.7 %add.117 = bf16[8,2,32,1024]{3,2,1,0:T(8,128)(2,1)} custom-call(bf16[8,2,32,1024]{3,2,1,0:T(8,128)(2,1)} %get-tuple-element.89.refs_0_, bf16[8,2,32,1024]{3,2,1,0:T(8,128)(2,1)} %collective-permute-done.10.refs_1_), custom_call_target="tpu_custom_call" | custom-call | bytes 1024 | tf_op jit(solution)/shard_map/add/pallas_call | solution.py:625
  161.9 5.7 %all-to-all-start.4 = ((bf16[8,2,32,1024]{3,2,1,0:T(8,128)(2,1)}), bf16[8,2,32,1024]{3,2,1,0:T(8,128)(2,1)S(1)}, u32[]{:S(2)}, u32[]{:S(2)}) async-start(bf16[8,2,32,1024]{3,2,1,0:T(8,128)(2,1)} %add.117), calls=%async_computation.4 | async-start | bytes 2097152 | tf_op jit(solution)/shard_map/all_to_all | solution.py:394
  167.6 3.0 %collective-permute-start.11 = (bf16[1,800,128]{2,1,0:T(8,128)(2,1)S(1)}, bf16[1,800,128]{2,1,0:T(8,128)(2,1)S(1)}, u32[]{:S(2)}, u32[]{:S(2)}) collective-permute-start(bf16[1,800,128]{2,1,0:T(8,128)(2,1)S(1)} %get-tuple-element.90), channel_id=1, source_target_pairs={{0,16},{4,20},{8,24},{12,28},{16,0},{20,4},{24,8},{28,12},{1,17},{... | collective-permute-start | bytes 614408 | tf_op jit(solution)/shard_map/ppermute | solution.py:678
  171.1 0.8 place.3.refs_0_
  172.0 1.9 place.4.refs_0_
  173.8 26.8 %collective-permute-done.11.other = bf16[1,800,128]{2,1,0:T(8,128)(2,1)S(1)} collective-permute-done((bf16[1,800,128]{2,1,0:T(8,128)(2,1)S(1)}, bf16[1,800,128]{2,1,0:T(8,128)(2,1)S(1)}, u32[]{:S(2)}, u32[]{:S(2)}) %collective-permute-start.11) | collective-permute-done | bytes 204832 | tf_op jit(solution)/shard_map/ppermute | solution.py:678
  200.6 0.8 finish.1
  201.5 1.1 place.5
  (42 shorter events, 2.9 us)
Async XLA Ops:
  1.6 8.1 %collective-permute-start = (bf16[4,8,2048]{2,1,0:T(8,128)(2,1)S(1)}, bf16[4,8,2048]{2,1,0:T(8,128)(2,1)S(1)}, u32[]{:S(2)}, u32[]{:S(2)}) collective-permute-start(bf16[4,8,2048]{2,1,0:T(8,128)(2,1)S(1)} %pad_maximum_fusion.3), channel_id=1, source_target_pairs={{0,4},{4,8},{8,12},{12,16},{16,20},{20,24},{24,28},{1,5},{5,9},{9,... | collective-permute-start | bytes 393224 | tf_op jit(solution)/shard_map/ppermute | solution.py:434
  6.5 6.9 %collective-permute-start.1 = (bf16[4,8,2048]{2,1,0:T(8,128)(2,1)S(1)}, bf16[4,8,2048]{2,1,0:T(8,128)(2,1)S(1)}, u32[]{:S(2)}, u32[]{:S(2)}) collective-permute-start(bf16[4,8,2048]{2,1,0:T(8,128)(2,1)S(1)} %pad_maximum_fusion.4), channel_id=1, source_target_pairs={{4,0},{8,4},{12,8},{16,12},{20,16},{24,20},{28,24},{5,1},{9,5},{13... | collective-permute-start | bytes 393224 | tf_op jit(solution)/shard_map/ppermute | solution.py:434
  14.1 15.3 %copy-start.2 = (bf16[1024,256]{1,0:T(8,128)(2,1)S(1)}, bf16[1024,256]{1,0:T(8,128)(2,1)}, u32[]{:S(2)}) copy-start(bf16[1024,256]{1,0:T(8,128)(2,1)} %wv.1) | copy-start | bytes 1572868
  30.6 1.1 copy-start.6
  30.6 1.1 copy-start.7
  30.7 9.1 %collective-permute-start.2 = (bf16[512,512]{1,0:T(8,128)(2,1)S(1)}, bf16[512,512]{1,0:T(8,128)(2,1)S(1)}, u32[]{:S(2)}, u32[]{:S(2)}) collective-permute-start(bf16[512,512]{1,0:T(8,128)(2,1)S(1)} %bitcast.25), channel_id=1, source_target_pairs={{0,1},{1,0},{2,3},{3,2},{4,5},{5,4},{6,7},{7,6},{8,9},{9,8},{10,11... | collective-permute-start | bytes 1572872 | tf_op jit(solution)/shard_map/ppermute | solution.py:487
  33.2 12.3 %all-to-all-start = ((f32[8,2,256]{2,1,0:T(2,128)}), f32[8,2,256]{2,1,0:T(2,128)S(1)}, u32[]{:S(2)}, u32[]{:S(2)}) async-start(f32[8,2,256]{2,1,0:T(2,128)} %get-tuple-element.51), calls=%async_computation | async-start | bytes 32768 | tf_op jit(solution)/shard_map/all_to_all | solution.py:394
  39.8 18.4 %copy-start.1 = (bf16[512,512]{1,0:T(8,128)(2,1)}, bf16[512,512]{1,0:T(8,128)(2,1)S(1)}, u32[]{:S(2)}) copy-start(bf16[512,512]{1,0:T(8,128)(2,1)S(1)} %collective-permute-done.2.w_sibling) | copy-start | bytes 1572868
  45.5 0.6 copy-start.5
  58.2 10.4 %all-to-all-start.1 = ((f32[8,2,256]{2,1,0:T(2,128)}), f32[8,2,256]{2,1,0:T(2,128)S(1)}, u32[]{:S(2)}, u32[]{:S(2)}) async-start(f32[8,2,256]{2,1,0:T(2,128)} %get-tuple-element.55), calls=%async_computation.1 | async-start | bytes 32768 | tf_op jit(solution)/shard_map/all_to_all | solution.py:394
  68.5 0.6 copy-start.3
  74.2 5.7 %collective-permute-start.3 = (bf16[1024,512]{1,0:T(8,128)(2,1)}, bf16[1024,512]{1,0:T(8,128)(2,1)}, u32[]{:S(2)}, u32[]{:S(2)}) collective-permute-start(bf16[1024,512]{1,0:T(8,128)(2,1)} %get-tuple-element.61.own.refs_0_), channel_id=1, source_target_pairs={{0,1},{1,0},{2,3},{3,2},{4,5},{5,4},{6,7},{7,6},{8,9},{9,8},{10,11... | collective-permute-start | bytes 3145736 | tf_op jit(solution)/shard_map/ppermute | solution.py:589
  79.3 15.2 %collective-permute-start.5 = (bf16[1024,512]{1,0:T(8,128)(2,1)}, bf16[1024,512]{1,0:T(8,128)(2,1)}, u32[]{:S(2)}, u32[]{:S(2)}) collective-permute-start(bf16[1024,512]{1,0:T(8,128)(2,1)} %get-tuple-element.63.own.refs_1_), channel_id=1, source_target_pairs={{0,1},{1,0},{2,3},{3,2},{4,5},{5,4},{6,7},{7,6},{8,9},{9,8},{10,11... | collective-permute-start | bytes 3145736 | tf_op jit(solution)/shard_map/ppermute | solution.py:589
  84.1 15.3 %collective-permute-start.6 = (bf16[8,1,32,1024]{3,2,1,0:T(8,128)(2,1)}, bf16[8,1,32,1024]{3,2,1,0:T(8,128)(2,1)S(1)}, u32[]{:S(2)}, u32[]{:S(2)}) collective-permute-start(bf16[8,1,32,1024]{3,2,1,0:T(8,128)(2,1)} %get-tuple-element.67), channel_id=1, source_target_pairs={{0,2},{1,3},{2,0},{3,1},{4,6},{5,7},{6,4},{7,5},{8,10},{9,11},{10,... | collective-permute-start | bytes 1572872 | tf_op jit(solution)/shard_map/ppermute | solution.py:620
  94.5 32.6 %collective-permute-start.4 = (bf16[2048,512]{1,0:T(8,128)(2,1)}, bf16[2048,512]{1,0:T(8,128)(2,1)}, u32[]{:S(2)}, u32[]{:S(2)}) collective-permute-start(bf16[2048,512]{1,0:T(8,128)(2,1)} %get-tuple-element.69.refs_2_.own), channel_id=1, source_target_pairs={{0,1},{1,0},{2,3},{3,2},{4,5},{5,4},{6,7},{7,6},{8,9},{9,8},{10,11... | collective-permute-start | bytes 6291464 | tf_op jit(solution)/shard_map/ppermute | solution.py:589
  98.8 21.5 %collective-permute-start.7 = (bf16[8,1,32,1024]{3,2,1,0:T(8,128)(2,1)}, bf16[8,1,32,1024]{3,2,1,0:T(8,128)(2,1)}, u32[]{:S(2)}, u32[]{:S(2)}) collective-permute-start(bf16[8,1,32,1024]{3,2,1,0:T(8,128)(2,1)} %get-tuple-element.72), channel_id=1, source_target_pairs={{0,2},{1,3},{2,0},{3,1},{4,6},{5,7},{6,4},{7,5},{8,10},{9,11},{10,... | collective-permute-start | bytes 1572872 | tf_op jit(solution)/shard_map/ppermute | solution.py:620
  99.3 0.8 copy-start.8
  102.1 20.8 %all-to-all-start.2 = ((bf16[8,1,32,1024]{3,2,1,0:T(8,128)(2,1)}), bf16[8,1,32,1024]{3,2,1,0:T(8,128)(2,1)S(1)}, u32[]{:S(2)}, u32[]{:S(2)}) async-start(bf16[8,1,32,1024]{3,2,1,0:T(8,128)(2,1)} %add.115), calls=%async_computation.2 | async-start | bytes 1048576 | tf_op jit(solution)/shard_map/all_to_all | solution.py:394
  118.2 25.5 %collective-permute-start.8 = (bf16[4,800,128]{2,1,0:T(8,128)(2,1)}, bf16[4,800,128]{2,1,0:T(8,128)(2,1)}, u32[]{:S(2)}, u32[]{:S(2)}) collective-permute-start(bf16[4,800,128]{2,1,0:T(8,128)(2,1)} %get-tuple-element.84), channel_id=1, source_target_pairs={{0,4},{4,0},{8,12},{12,8},{16,20},{20,16},{24,28},{28,24},{1,5},{5... | collective-permute-start | bytes 2457608 | tf_op jit(solution)/shard_map/ppermute | solution.py:678
  122.9 34.0 %all-to-all-start.3 = ((bf16[8,1,32,1024]{3,2,1,0:T(8,128)(2,1)}), bf16[8,1,32,1024]{3,2,1,0:T(8,128)(2,1)}, u32[]{:S(2)}, u32[]{:S(2)}) async-start(bf16[8,1,32,1024]{3,2,1,0:T(8,128)(2,1)} %add.116), calls=%async_computation.3 | async-start | bytes 1048576 | tf_op jit(solution)/shard_map/all_to_all | solution.py:394
  133.6 24.6 %collective-permute-start.10 = (bf16[8,2,32,1024]{3,2,1,0:T(8,128)(2,1)}, bf16[8,2,32,1024]{3,2,1,0:T(8,128)(2,1)}, u32[]{:S(2)}, u32[]{:S(2)}) collective-permute-start(bf16[8,2,32,1024]{3,2,1,0:T(8,128)(2,1)} %get-tuple-element.82), channel_id=1, source_target_pairs={{0,2},{1,3},{2,0},{3,1},{4,6},{5,7},{6,4},{7,5},{8,10},{9,11},{10,... | collective-permute-start | bytes 3145736 | tf_op jit(solution)/shard_map/ppermute | solution.py:620
  143.8 1.1 copy-start
  146.3 10.5 %collective-permute-start.9 = (bf16[2,800,128]{2,1,0:T(8,128)(2,1)S(1)}, bf16[2,800,128]{2,1,0:T(8,128)(2,1)S(1)}, u32[]{:S(2)}, u32[]{:S(2)}) collective-permute-start(bf16[2,800,128]{2,1,0:T(8,128)(2,1)S(1)} %get-tuple-element.86), channel_id=1, source_target_pairs={{0,8},{4,12},{8,0},{12,4},{16,24},{20,28},{24,16},{28,20},{1,9},{5... | collective-permute-start | bytes 1228808 | tf_op jit(solution)/shard_map/ppermute | solution.py:678
  156.9 10.7 %copy-start.4 = (f32[8,2,256]{2,1,0:T(2,128)S(1)}, f32[8,2,256]{2,1,0:T(2,128)}, u32[]{:S(2)}) copy-start(f32[8,2,256]{2,1,0:T(2,128)} %copy-done.3) | copy-start | bytes 49156
  161.9 39.6 %all-to-all-start.4 = ((bf16[8,2,32,1024]{3,2,1,0:T(8,128)(2,1)}), bf16[8,2,32,1024]{3,2,1,0:T(8,128)(2,1)S(1)}, u32[]{:S(2)}, u32[]{:S(2)}) async-start(bf16[8,2,32,1024]{3,2,1,0:T(8,128)(2,1)} %add.117), calls=%async_computation.4 | async-start | bytes 2097152 | tf_op jit(solution)/shard_map/all_to_all | solution.py:394
  167.6 33.0 %collective-permute-start.11 = (bf16[1,800,128]{2,1,0:T(8,128)(2,1)S(1)}, bf16[1,800,128]{2,1,0:T(8,128)(2,1)S(1)}, u32[]{:S(2)}, u32[]{:S(2)}) collective-permute-start(bf16[1,800,128]{2,1,0:T(8,128)(2,1)S(1)} %get-tuple-element.90), channel_id=1, source_target_pairs={{0,16},{4,20},{8,24},{12,28},{16,0},{20,4},{24,8},{28,12},{1,17},{... | collective-permute-start | bytes 614408 | tf_op jit(solution)/shard_map/ppermute | solution.py:678

commit v12 on v11

--- a/solution.py
+++ b/solution.py
@@ -647,7 +647,9 @@
     grads[2], taps[2] = back(*groups[2], *parts[0])
     parts[1] = partials(*groups[1], grads[1], grads[2])
     owns[0] = deliver(parts[0], LONG, *parts[1])
-    moved[0] = exchange(owns[0], "seq")
+    parts[2] = partials(*groups[2], grads[2], owns[0])
+    moved[0] = exchange(after(owns[0], *parts[2]), "seq")
+    owns[1] = deliver(parts[1], 0, *parts[2])
 
     slots = 3 * width + 16 * (width // shard)
     half = sds((seqs // 2, slots, shard), BF16)
@@ -669,10 +671,10 @@
         [pltpu.VMEM((2 * width, model), F32)],
         LONG,
         1024,
-    )(parity, after(normed, owns[0]), w_out, *grads, *taps)
-    owns[1] = deliver(parts[1], LONG, keep)
-    moved[1] = exchange(after(owns[1], moved[0]), "seq")
-    parts[2] = partials(*groups[2], grads[2], owns[1])
+    )(parity, after(normed, owns[1]), w_out, *grads, *taps)
+    moved[1] = exchange(after(owns[1], keep, moved[0]), "seq")
+    owns[2] = deliver(parts[2], 0, keep)
+    moved[2] = exchange(after(owns[2], moved[1]), "seq")
     bit = 1
     while True:
         others = lax.ppermute(send, "seq", [(i, i ^ bit) for i in range(seqs)])
@@ -680,7 +682,7 @@
         if bit == seqs:
             break
         if bit == 2:
-            keep = after(keep, *parts[2])
+            keep = after(keep, owns[2])
         shape = (keep.shape[0] // 2,) + keep.shape[1:]
         side = ((seq_at // bit) % 2).astype(jnp.int32).reshape(1, 1)
         keep, send = call(
@@ -691,13 +693,10 @@
             [whole(shape)] * 2,
             [sds(shape, BF16)] * 2,
             [],
-            LONG if bit == 2 else 0,
+            0,
             1024,
             vmem=20,
         )(side, keep, others)
-        if bit == min(4, seqs // 2):
-            owns[2] = deliver(parts[2], 0, keep, moved[1])
-            moved[2] = exchange(owns[2], "seq")
     w_value, w_gate, w_out, grad_taps = call(
         functools.partial(finish_kernel, kernel),
         "finish",

time: 204 us -> 216 us (1.059)
  waiting for transfers between devices: 55.1 us -> 69.3 us
    all_to_all x5, waiting for transfers between devices: 6.33 us -> 19.6 us  [exchange(): return lax.all_to_all(copies, axis, 0, 0, tiled=True)]
    ppermute x3, waiting for transfers between devices: 1.27 us -> 4.47 us  [deliver(): arrived.append(lax.ppermute(part[d], 'tp', send))]
    ppermute x3, waiting for transfers between devices: 43.8 us -> 41.6 us  [per_device(): others = lax.ppermute(send, 'seq', [(i, i ^ bit) for i in range(seqs)])]
  transfers between devices with their start and end apart: 17 -> 17, of which waited for: 7 -> 8; matrix products, arithmetic and copies ran while one was open for 2% -> 2% of each run, Pallas kernels for 27% -> 27%
where the time goes in v12:
time: 216 us; the launch traced here: 214 us
  Pallas kernels  92.3 us (43%)
  waiting for transfers between devices  69.3 us (32%)
  starting transfers between devices  41.3 us (19%)
  local copies, waits for them, and re-layouts  5.06 us (2%)
  other arithmetic  4.94 us (2%)
    ppermute x3, waiting for transfers between devices, per_device(): others = lax.ppermute(send, 'seq', [(i, i ^ bit) for i in range(seqs)])  41.6 us
    all_to_all x5, starting transfers between devices, exchange(): return lax.all_to_all(copies, axis, 0, 0, tiled=True)  22.8 us
    all_to_all x5, waiting for transfers between devices, exchange(): return lax.all_to_all(copies, axis, 0, 0, tiled=True)  19.6 us
    pallas_call x3, Pallas kernels, back(): call(functools.partial(back_kernel, first, blocks), 'back_conv', (size *...  19 us
    pallas_call x1, Pallas kernels, per_device(): call(gate_kernel, 'gate_conv', (recs,), [smem(), per_record((frames, mode...  15.3 us
    pallas_call x3, Pallas kernels, partials(): call(partial_kernel, 'partial_in', (size * parts_in,), [pl.BlockSpec((hal...  14.9 us
    pallas_call x1, Pallas kernels, per_device(): call(norm_kernel, 'swish_norm', (recs,), [smem(), smem(), whole((seqs, 2,...  12.1 us
    pallas_call x1, Pallas kernels, per_device(): call(functools.partial(outer_kernel, groups), 'outer_w_in', (recs,), [sme...  10.2 us
  transfers between devices with their start and end apart: 17, of which 8 were waited for; matrix products, arithmetic and copies ran while one was open for 2% of the time, Pallas kernels for 27%

profile of v12, /device:TPU:0, one launch (start us, length us, event | category | flops | bytes accessed | tf_op | source)
XLA Modules:
  0.0 214.5 jit_solution(10766135908234678425)
XLA Ops:
  0.6 1.0 fusion.1
  1.6 4.9 %collective-permute-start = (bf16[4,8,2048]{2,1,0:T(8,128)(2,1)S(1)}, bf16[4,8,2048]{2,1,0:T(8,128)(2,1)S(1)}, u32[]{:S(2)}, u32[]{:S(2)}) collective-permute-start(bf16[4,8,2048]{2,1,0:T(8,128)(2,1)S(1)} %pad_maximum_fusion.3), channel_id=1, source_target_pairs={{0,4},{4,8},{8,12},{12,16},{16,20},{20,24},{24,28},{1,5},{5,9},{9,... | collective-permute-start | bytes 393224 | tf_op jit(solution)/shard_map/ppermute | solution.py:434
  6.5 1.3 collective-permute-start.1
  7.8 1.3 fusion.5
  9.7 3.7 %collective-permute-done.1 = bf16[4,8,2048]{2,1,0:T(8,128)(2,1)S(1)} collective-permute-done((bf16[4,8,2048]{2,1,0:T(8,128)(2,1)S(1)}, bf16[4,8,2048]{2,1,0:T(8,128)(2,1)S(1)}, u32[]{:S(2)}, u32[]{:S(2)}) %collective-permute-start.1) | collective-permute-done | bytes 131104 | tf_op jit(solution)/shard_map/ppermute | solution.py:434
  13.4 0.7 fusion.3
  14.1 15.3 %gate_conv.1 = (f32[4,1024,256]{2,1,0:T(8,128)}, f32[4,1024,256]{2,1,0:T(8,128)}, f32[4,1040,256]{2,1,0:T(8,128)}, f32[8,2,256]{2,1,0:T(2,128)}) custom-call(s32[2,4]{1,0:T(2,128)} %stack.35.meta, bf16[4,1024,1024]{2,1,0:T(8,128)(2,1)} %x.4, bf16[4,16,1024]{2,1,0:T(8,128)(2,1)} %get-tuple-element.108.halo, bf16[1024,256]{1,0:T(8,128)(2,1)} %wv.1, ...), custom_call_target="tpu_custom_call" | custom-call | flops 4294967296 | bytes 20971520 | tf_op jit(solution)/shard_map/gate_conv/pallas_call | solution.py:448
  29.4 1.1 pad_maximum_fusion
  31.6 0.6 pad_maximum_fusion.5.affine
  32.2 0.9 fusion.select
  33.2 5.7 %all-to-all-start = ((f32[8,2,256]{2,1,0:T(2,128)}), f32[8,2,256]{2,1,0:T(2,128)S(1)}, u32[]{:S(2)}, u32[]{:S(2)}) async-start(f32[8,2,256]{2,1,0:T(2,128)} %get-tuple-element.53), calls=%async_computation | async-start | bytes 32768 | tf_op jit(solution)/shard_map/all_to_all | solution.py:394
  38.9 0.8 pad_maximum_fusion.1
  39.7 5.7 %all-to-all-done.stats = f32[8,2,256]{2,1,0:T(2,128)S(1)} async-done(((f32[8,2,256]{2,1,0:T(2,128)}), f32[8,2,256]{2,1,0:T(2,128)S(1)}, u32[]{:S(2)}, u32[]{:S(2)}) %all-to-all-start) | async-done | bytes 16416 | tf_op jit(solution)/shard_map/all_to_all | solution.py:394
  45.5 0.6 copy-done.6
  46.1 12.1 %swish_norm.1 = (bf16[4,1024,256]{2,1,0:T(8,128)(2,1)}, f32[4,1040,256]{2,1,0:T(8,128)}, bf16[4,256,1024]{2,1,0:T(8,128)(2,1)}, f32[8,2,256]{2,1,0:T(2,128)}) custom-call(s32[2,4]{1,0:T(2,128)} %stack.35.meta, f32[1,1]{1,0:T(1,128)} %bitcast.1.count, f32[8,2,256]{2,1,0:T(2,128)} %copy-done.6, f32[2,256]{1,0:T(2,128)} %pad_maximum_fusion.5.affine, ...), custom_call_target="tpu_custom_call" | custom-call | flops 4294967296 | bytes 20971520 | tf_op jit(solution)/shard_map/swish_norm/pallas_call | solution.py:493
  58.1 3.3 %all-to-all-start.1 = ((f32[8,2,256]{2,1,0:T(2,128)}), f32[8,2,256]{2,1,0:T(2,128)S(1)}, u32[]{:S(2)}, u32[]{:S(2)}) async-start(f32[8,2,256]{2,1,0:T(2,128)} %get-tuple-element.57), calls=%async_computation.1 | async-start | bytes 32768 | tf_op jit(solution)/shard_map/all_to_all | solution.py:394
  61.5 7.0 %outer_w_out.1.w_out = f32[256,1024]{1,0:T(8,128)} custom-call(bf16[4,1024,1024]{2,1,0:T(8,128)(2,1)} %grads.3, bf16[4,1024,256]{2,1,0:T(8,128)(2,1)} %get-tuple-element.61.swished), custom_call_target="tpu_custom_call" | custom-call | flops 2147483648 | bytes 8388608 | tf_op jit(solution)/shard_map/outer_w_out/pallas_call | solution.py:538
  68.5 0.6 copy-done.4
  69.1 5.0 %back_conv.3 = (bf16[1024,512]{1,0:T(8,128)(2,1)}, f32[16,256]{1,0:T(8,128)}) custom-call(s32[2,4]{1,0:T(2,128)} %stack.35.meta, f32[1,1]{1,0:T(1,128)} %bitcast.1.count, f32[8,2,256]{2,1,0:T(2,128)} %copy-done.6, f32[8,2,256]{2,1,0:T(2,128)} %copy-done.4, f32[1,256]{1,0:T(1,128)} %bitcast.26, f32[4,1040,256]{2,1,0:T(8,128)} %get-tuple-element.58.gn, ...), custom_call_target="tpu_custom_call" | custom-call | bytes 1024 | tf_op jit(solution)/shard_map/back_conv/pallas_call | solution.py:562
  74.2 5.1 %back_conv.4 = (bf16[1024,512]{1,0:T(8,128)(2,1)}, f32[16,256]{1,0:T(8,128)}) custom-call(s32[2,4]{1,0:T(2,128)} %stack.35.meta, f32[1,1]{1,0:T(1,128)} %bitcast.1.count, f32[8,2,256]{2,1,0:T(2,128)} %copy-done.6, f32[8,2,256]{2,1,0:T(2,128)} %copy-done.4, f32[1,256]{1,0:T(1,128)} %bitcast.27, f32[4,1040,256]{2,1,0:T(8,128)} %get-tuple-element.58.gn, ...), custom_call_target="tpu_custom_call" | custom-call | bytes 1024 | tf_op jit(solution)/shard_map/back_conv/pallas_call | solution.py:562
  79.8 4.2 %partial_in.3 = (bf16[8,1,32,1024]{3,2,1,0:T(8,128)(2,1)}, bf16[8,1,32,1024]{3,2,1,0:T(8,128)(2,1)}) custom-call(bf16[1024,512]{1,0:T(8,128)(2,1)} %get-tuple-element.63.own.refs_0_, bf16[1024,512]{1,0:T(8,128)(2,1)} %collective-permute-done.3.sibling, bf16[512,512]{1,0:T(8,128)(2,1)} %bitcast.21, bf16[512,512]{1,0:T(8,128)(2,1)} %copy-done.1, ...), custom_call_target="tpu_custom_call" | custom-call | bytes 1024 | tf_op jit(solution)/shard_map/partial_in/pallas_call | solution.py:591
  84.1 1.5 collective-permute-start.6
  85.6 8.9 %back_conv.5 = (bf16[2048,512]{1,0:T(8,128)(2,1)}, f32[16,256]{1,0:T(8,128)}) custom-call(s32[2,4]{1,0:T(2,128)} %stack.35.meta, f32[1,1]{1,0:T(1,128)} %bitcast.1.count, f32[8,2,256]{2,1,0:T(2,128)} %copy-done.6, f32[8,2,256]{2,1,0:T(2,128)} %copy-done.4, f32[1,256]{1,0:T(1,128)} %bitcast.28, f32[4,1040,256]{2,1,0:T(8,128)} %get-tuple-element.58.gn, ...), custom_call_target="tpu_custom_call" | custom-call | bytes 1024 | tf_op jit(solution)/shard_map/back_conv/pallas_call | solution.py:562
  94.5 4.2 %partial_in.4 = (bf16[8,1,32,1024]{3,2,1,0:T(8,128)(2,1)}, bf16[8,1,32,1024]{3,2,1,0:T(8,128)(2,1)}) custom-call(bf16[1024,512]{1,0:T(8,128)(2,1)} %get-tuple-element.65.own.refs_1_, bf16[1024,512]{1,0:T(8,128)(2,1)} %collective-permute-done.5.sibling, bf16[512,512]{1,0:T(8,128)(2,1)} %bitcast.22, bf16[512,512]{1,0:T(8,128)(2,1)} %copy-done.1, ...), custom_call_target="tpu_custom_call" | custom-call | bytes 1024 | tf_op jit(solution)/shard_map/partial_in/pallas_call | solution.py:591
  99.3 2.0 add.115
  101.3 6.5 %partial_in.5 = (bf16[8,2,32,1024]{3,2,1,0:T(8,128)(2,1)}, bf16[8,2,32,1024]{3,2,1,0:T(8,128)(2,1)}) custom-call(bf16[2048,512]{1,0:T(8,128)(2,1)} %get-tuple-element.71.own.refs_2_, bf16[2048,512]{1,0:T(8,128)(2,1)} %collective-permute-done.4.sibling, bf16[512,512]{1,0:T(8,128)(2,1)} %bitcast.23, bf16[512,512]{1,0:T(8,128)(2,1)} %copy-done.1, ...), custom_call_target="tpu_custom_call" | custom-call | bytes 1024 | tf_op jit(solution)/shard_map/partial_in/pallas_call | solution.py:591
  107.8 1.5 collective-permute-start.8
  109.2 4.5 %collective-permute-done.7.refs_1_ = bf16[8,1,32,1024]{3,2,1,0:T(8,128)(2,1)S(1)} collective-permute-done((bf16[8,1,32,1024]{3,2,1,0:T(8,128)(2,1)}, bf16[8,1,32,1024]{3,2,1,0:T(8,128)(2,1)S(1)}, u32[]{:S(2)}, u32[]{:S(2)}) %collective-permute-start.7) | collective-permute-done | bytes 524320 | tf_op jit(solution)/shard_map/ppermute | solution.py:620
  113.7 0.8 copy-done.2
  114.5 2.0 add.116
  116.5 5.9 %all-to-all-start.2 = ((bf16[8,1,32,1024]{3,2,1,0:T(8,128)(2,1)}), bf16[8,1,32,1024]{3,2,1,0:T(8,128)(2,1)S(1)}, u32[]{:S(2)}, u32[]{:S(2)}) async-start(bf16[8,1,32,1024]{3,2,1,0:T(8,128)(2,1)} %add.115), calls=%async_computation.2 | async-start | bytes 1048576 | tf_op jit(solution)/shard_map/all_to_all | solution.py:394
  122.4 10.2 %outer_w_in.1 = (bf16[4,800,128]{2,1,0:T(8,128)(2,1)}, bf16[4,800,128]{2,1,0:T(8,128)(2,1)}) custom-call(s32[1,1]{1,0:T(1,128)} %bitcast.11.parity, bf16[4,1024,1024]{2,1,0:T(8,128)(2,1)} %x.4, f32[256,1024]{1,0:T(8,128)} %outer_w_out.1.w_out, bf16[1024,512]{1,0:T(8,128)(2,1)} %get-tuple-element.63.own.refs_0_, ...), custom_call_target="tpu_custom_call" | custom-call | flops 49999998976 | bytes 1024 | tf_op jit(solution)/shard_map/outer_w_in/pallas_call | solution.py:656
  132.7 3.7 %all-to-all-done.2.moved = bf16[8,1,32,1024]{3,2,1,0:T(8,128)(2,1)S(1)} async-done(((bf16[8,1,32,1024]{3,2,1,0:T(8,128)(2,1)}), bf16[8,1,32,1024]{3,2,1,0:T(8,128)(2,1)S(1)}, u32[]{:S(2)}, u32[]{:S(2)}) %all-to-all-start.2) | async-done | bytes 524320 | tf_op jit(solution)/shard_map/all_to_all | solution.py:394
  136.4 4.1 %all-to-all-start.3 = ((bf16[8,1,32,1024]{3,2,1,0:T(8,128)(2,1)}), bf16[8,1,32,1024]{3,2,1,0:T(8,128)(2,1)}, u32[]{:S(2)}, u32[]{:S(2)}) async-start(bf16[8,1,32,1024]{3,2,1,0:T(8,128)(2,1)} %add.116), calls=%async_computation.3 | async-start | bytes 1048576 | tf_op jit(solution)/shard_map/all_to_all | solution.py:394
  140.6 3.7 %add.117 = bf16[8,2,32,1024]{3,2,1,0:T(8,128)(2,1)} custom-call(bf16[8,2,32,1024]{3,2,1,0:T(8,128)(2,1)} %get-tuple-element.85.refs_0_, bf16[8,2,32,1024]{3,2,1,0:T(8,128)(2,1)} %collective-permute-done.8.refs_1_), custom_call_target="tpu_custom_call" | custom-call | bytes 1024 | tf_op jit(solution)/shard_map/add/pallas_call | solution.py:625
  144.3 10.1 %all-to-all-done.3.moved = bf16[8,1,32,1024]{3,2,1,0:T(8,128)(2,1)} async-done(((bf16[8,1,32,1024]{3,2,1,0:T(8,128)(2,1)}), bf16[8,1,32,1024]{3,2,1,0:T(8,128)(2,1)}, u32[]{:S(2)}, u32[]{:S(2)}) %all-to-all-start.3) | async-done | bytes 524320 | tf_op jit(solution)/shard_map/all_to_all | solution.py:394
  154.4 3.6 %all-to-all-start.4 = ((bf16[8,2,32,1024]{3,2,1,0:T(8,128)(2,1)}), bf16[8,2,32,1024]{3,2,1,0:T(8,128)(2,1)S(1)}, u32[]{:S(2)}, u32[]{:S(2)}) async-start(bf16[8,2,32,1024]{3,2,1,0:T(8,128)(2,1)} %add.117), calls=%async_computation.4 | async-start | bytes 2097152 | tf_op jit(solution)/shard_map/all_to_all | solution.py:394
  158.0 2.0 collective-permute-start.9
  160.0 28.5 %collective-permute-done.9.other = bf16[4,800,128]{2,1,0:T(8,128)(2,1)} collective-permute-done((bf16[4,800,128]{2,1,0:T(8,128)(2,1)}, bf16[4,800,128]{2,1,0:T(8,128)(2,1)}, u32[]{:S(2)}, u32[]{:S(2)}) %collective-permute-start.9) | collective-permute-done | bytes 819232 | tf_op jit(solution)/shard_map/ppermute | solution.py:680
  188.5 1.3 fold.2
  189.9 1.5 collective-permute-start.10
  191.4 8.0 %collective-permute-done.10.other = bf16[2,800,128]{2,1,0:T(8,128)(2,1)S(1)} collective-permute-done((bf16[2,800,128]{2,1,0:T(8,128)(2,1)S(1)}, bf16[2,800,128]{2,1,0:T(8,128)(2,1)S(1)}, u32[]{:S(2)}, u32[]{:S(2)}) %collective-permute-start.10) | collective-permute-done | bytes 409632 | tf_op jit(solution)/shard_map/ppermute | solution.py:680
  199.5 4.6 %collective-permute-start.11 = (bf16[1,800,128]{2,1,0:T(8,128)(2,1)S(1)}, bf16[1,800,128]{2,1,0:T(8,128)(2,1)S(1)}, u32[]{:S(2)}, u32[]{:S(2)}) collective-permute-start(bf16[1,800,128]{2,1,0:T(8,128)(2,1)S(1)} %get-tuple-element.94), channel_id=1, source_target_pairs={{0,16},{4,20},{8,24},{12,28},{16,0},{20,4},{24,8},{28,12},{1,17},{... | collective-permute-start | bytes 614408 | tf_op jit(solution)/shard_map/ppermute | solution.py:680
  204.7 0.8 place.3.refs_0_
  205.5 5.1 %collective-permute-done.11.other = bf16[1,800,128]{2,1,0:T(8,128)(2,1)S(1)} collective-permute-done((bf16[1,800,128]{2,1,0:T(8,128)(2,1)S(1)}, bf16[1,800,128]{2,1,0:T(8,128)(2,1)S(1)}, u32[]{:S(2)}, u32[]{:S(2)}) %collective-permute-start.11) | collective-permute-done | bytes 204832 | tf_op jit(solution)/shard_map/ppermute | solution.py:680
  210.6 0.9 finish.1
  211.5 1.9 place.4.refs_0_
  213.4 1.1 place.5
  (42 shorter events, 2.9 us)
Async XLA Ops:
  1.6 8.1 %collective-permute-start = (bf16[4,8,2048]{2,1,0:T(8,128)(2,1)S(1)}, bf16[4,8,2048]{2,1,0:T(8,128)(2,1)S(1)}, u32[]{:S(2)}, u32[]{:S(2)}) collective-permute-start(bf16[4,8,2048]{2,1,0:T(8,128)(2,1)S(1)} %pad_maximum_fusion.3), channel_id=1, source_target_pairs={{0,4},{4,8},{8,12},{12,16},{16,20},{20,24},{24,28},{1,5},{5,9},{9,... | collective-permute-start | bytes 393224 | tf_op jit(solution)/shard_map/ppermute | solution.py:434
  6.5 6.9 %collective-permute-start.1 = (bf16[4,8,2048]{2,1,0:T(8,128)(2,1)S(1)}, bf16[4,8,2048]{2,1,0:T(8,128)(2,1)S(1)}, u32[]{:S(2)}, u32[]{:S(2)}) collective-permute-start(bf16[4,8,2048]{2,1,0:T(8,128)(2,1)S(1)} %pad_maximum_fusion.4), channel_id=1, source_target_pairs={{4,0},{8,4},{12,8},{16,12},{20,16},{24,20},{28,24},{5,1},{9,5},{13... | collective-permute-start | bytes 393224 | tf_op jit(solution)/shard_map/ppermute | solution.py:434
  14.1 15.3 %copy-start.3 = (bf16[1024,256]{1,0:T(8,128)(2,1)S(1)}, bf16[1024,256]{1,0:T(8,128)(2,1)}, u32[]{:S(2)}) copy-start(bf16[1024,256]{1,0:T(8,128)(2,1)} %wv.1) | copy-start | bytes 1572868
  30.6 1.1 copy-start.7
  30.6 1.1 copy-start.8
  30.7 9.0 %collective-permute-start.2 = (bf16[512,512]{1,0:T(8,128)(2,1)S(1)}, bf16[512,512]{1,0:T(8,128)(2,1)S(1)}, u32[]{:S(2)}, u32[]{:S(2)}) collective-permute-start(bf16[512,512]{1,0:T(8,128)(2,1)S(1)} %bitcast.25), channel_id=1, source_target_pairs={{0,1},{1,0},{2,3},{3,2},{4,5},{5,4},{6,7},{7,6},{8,9},{9,8},{10,11... | collective-permute-start | bytes 1572872 | tf_op jit(solution)/shard_map/ppermute | solution.py:487
  33.2 12.3 %all-to-all-start = ((f32[8,2,256]{2,1,0:T(2,128)}), f32[8,2,256]{2,1,0:T(2,128)S(1)}, u32[]{:S(2)}, u32[]{:S(2)}) async-start(f32[8,2,256]{2,1,0:T(2,128)} %get-tuple-element.53), calls=%async_computation | async-start | bytes 32768 | tf_op jit(solution)/shard_map/all_to_all | solution.py:394
  39.7 18.4 %copy-start.1 = (bf16[512,512]{1,0:T(8,128)(2,1)}, bf16[512,512]{1,0:T(8,128)(2,1)S(1)}, u32[]{:S(2)}) copy-start(bf16[512,512]{1,0:T(8,128)(2,1)S(1)} %collective-permute-done.2.w_sibling) | copy-start | bytes 1572868
  45.5 0.6 copy-start.6
  58.1 10.4 %all-to-all-start.1 = ((f32[8,2,256]{2,1,0:T(2,128)}), f32[8,2,256]{2,1,0:T(2,128)S(1)}, u32[]{:S(2)}, u32[]{:S(2)}) async-start(f32[8,2,256]{2,1,0:T(2,128)} %get-tuple-element.57), calls=%async_computation.1 | async-start | bytes 32768 | tf_op jit(solution)/shard_map/all_to_all | solution.py:394
  68.5 0.6 copy-start.4
  74.2 5.7 %collective-permute-start.3 = (bf16[1024,512]{1,0:T(8,128)(2,1)}, bf16[1024,512]{1,0:T(8,128)(2,1)}, u32[]{:S(2)}, u32[]{:S(2)}) collective-permute-start(bf16[1024,512]{1,0:T(8,128)(2,1)} %get-tuple-element.63.own.refs_0_), channel_id=1, source_target_pairs={{0,1},{1,0},{2,3},{3,2},{4,5},{5,4},{6,7},{7,6},{8,9},{9,8},{10,11... | collective-permute-start | bytes 3145736 | tf_op jit(solution)/shard_map/ppermute | solution.py:589
  79.3 15.2 %collective-permute-start.5 = (bf16[1024,512]{1,0:T(8,128)(2,1)}, bf16[1024,512]{1,0:T(8,128)(2,1)}, u32[]{:S(2)}, u32[]{:S(2)}) collective-permute-start(bf16[1024,512]{1,0:T(8,128)(2,1)} %get-tuple-element.65.own.refs_1_), channel_id=1, source_target_pairs={{0,1},{1,0},{2,3},{3,2},{4,5},{5,4},{6,7},{7,6},{8,9},{9,8},{10,11... | collective-permute-start | bytes 3145736 | tf_op jit(solution)/shard_map/ppermute | solution.py:589
  84.1 15.2 %collective-permute-start.6 = (bf16[8,1,32,1024]{3,2,1,0:T(8,128)(2,1)}, bf16[8,1,32,1024]{3,2,1,0:T(8,128)(2,1)}, u32[]{:S(2)}, u32[]{:S(2)}) collective-permute-start(bf16[8,1,32,1024]{3,2,1,0:T(8,128)(2,1)} %get-tuple-element.69), channel_id=1, source_target_pairs={{0,2},{1,3},{2,0},{3,1},{4,6},{5,7},{6,4},{7,5},{8,10},{9,11},{10,... | collective-permute-start | bytes 1572872 | tf_op jit(solution)/shard_map/ppermute | solution.py:620
  94.5 6.8 %collective-permute-start.4 = (bf16[2048,512]{1,0:T(8,128)(2,1)}, bf16[2048,512]{1,0:T(8,128)(2,1)}, u32[]{:S(2)}, u32[]{:S(2)}) collective-permute-start(bf16[2048,512]{1,0:T(8,128)(2,1)} %get-tuple-element.71.own.refs_2_), channel_id=1, source_target_pairs={{0,1},{1,0},{2,3},{3,2},{4,5},{5,4},{6,7},{7,6},{8,9},{9,8},{10,11... | collective-permute-start | bytes 6291464 | tf_op jit(solution)/shard_map/ppermute | solution.py:589
  98.8 14.9 %collective-permute-start.7 = (bf16[8,1,32,1024]{3,2,1,0:T(8,128)(2,1)}, bf16[8,1,32,1024]{3,2,1,0:T(8,128)(2,1)S(1)}, u32[]{:S(2)}, u32[]{:S(2)}) collective-permute-start(bf16[8,1,32,1024]{3,2,1,0:T(8,128)(2,1)} %get-tuple-element.74), channel_id=1, source_target_pairs={{0,2},{1,3},{2,0},{3,1},{4,6},{5,7},{6,4},{7,5},{8,10},{9,11},{10,... | collective-permute-start | bytes 1572872 | tf_op jit(solution)/shard_map/ppermute | solution.py:620
  107.8 32.8 %collective-permute-start.8 = (bf16[8,2,32,1024]{3,2,1,0:T(8,128)(2,1)}, bf16[8,2,32,1024]{3,2,1,0:T(8,128)(2,1)}, u32[]{:S(2)}, u32[]{:S(2)}) collective-permute-start(bf16[8,2,32,1024]{3,2,1,0:T(8,128)(2,1)} %get-tuple-element.78), channel_id=1, source_target_pairs={{0,2},{1,3},{2,0},{3,1},{4,6},{5,7},{6,4},{7,5},{8,10},{9,11},{10,... | collective-permute-start | bytes 3145736 | tf_op jit(solution)/shard_map/ppermute | solution.py:620
  113.7 0.8 copy-start.2
  116.5 19.9 %all-to-all-start.2 = ((bf16[8,1,32,1024]{3,2,1,0:T(8,128)(2,1)}), bf16[8,1,32,1024]{3,2,1,0:T(8,128)(2,1)S(1)}, u32[]{:S(2)}, u32[]{:S(2)}) async-start(bf16[8,1,32,1024]{3,2,1,0:T(8,128)(2,1)} %add.115), calls=%async_computation.2 | async-start | bytes 1048576 | tf_op jit(solution)/shard_map/all_to_all | solution.py:394
  136.4 18.0 %all-to-all-start.3 = ((bf16[8,1,32,1024]{3,2,1,0:T(8,128)(2,1)}), bf16[8,1,32,1024]{3,2,1,0:T(8,128)(2,1)}, u32[]{:S(2)}, u32[]{:S(2)}) async-start(bf16[8,1,32,1024]{3,2,1,0:T(8,128)(2,1)} %add.116), calls=%async_computation.3 | async-start | bytes 1048576 | tf_op jit(solution)/shard_map/all_to_all | solution.py:394
  144.3 44.2 %copy-start = (bf16[4,800,128]{2,1,0:T(8,128)(2,1)S(1)}, bf16[4,800,128]{2,1,0:T(8,128)(2,1)}, u32[]{:S(2)}) copy-start(bf16[4,800,128]{2,1,0:T(8,128)(2,1)} %get-tuple-element.89.own) | copy-start | bytes 2457604
  144.3 47.1 %copy-start.5 = (f32[8,2,256]{2,1,0:T(2,128)S(1)}, f32[8,2,256]{2,1,0:T(2,128)}, u32[]{:S(2)}) copy-start(f32[8,2,256]{2,1,0:T(2,128)} %copy-done.4) | copy-start | bytes 49156
  154.4 59.0 %all-to-all-start.4 = ((bf16[8,2,32,1024]{3,2,1,0:T(8,128)(2,1)}), bf16[8,2,32,1024]{3,2,1,0:T(8,128)(2,1)S(1)}, u32[]{:S(2)}, u32[]{:S(2)}) async-start(bf16[8,2,32,1024]{3,2,1,0:T(8,128)(2,1)} %add.117), calls=%async_computation.4 | async-start | bytes 2097152 | tf_op jit(solution)/shard_map/all_to_all | solution.py:394
  158.0 30.5 %collective-permute-start.9 = (bf16[4,800,128]{2,1,0:T(8,128)(2,1)}, bf16[4,800,128]{2,1,0:T(8,128)(2,1)}, u32[]{:S(2)}, u32[]{:S(2)}) collective-permute-start(bf16[4,800,128]{2,1,0:T(8,128)(2,1)} %get-tuple-element.90), channel_id=1, source_target_pairs={{0,4},{4,0},{8,12},{12,8},{16,20},{20,16},{24,28},{28,24},{1,5},{5... | collective-permute-start | bytes 2457608 | tf_op jit(solution)/shard_map/ppermute | solution.py:680
  189.9 9.6 %collective-permute-start.10 = (bf16[2,800,128]{2,1,0:T(8,128)(2,1)S(1)}, bf16[2,800,128]{2,1,0:T(8,128)(2,1)S(1)}, u32[]{:S(2)}, u32[]{:S(2)}) collective-permute-start(bf16[2,800,128]{2,1,0:T(8,128)(2,1)S(1)} %get-tuple-element.92), channel_id=1, source_target_pairs={{0,8},{4,12},{8,0},{12,4},{16,24},{20,28},{24,16},{28,20},{1,9},{5... | collective-permute-start | bytes 1228808 | tf_op jit(solution)/shard_map/ppermute | solution.py:680
  199.5 11.1 %collective-permute-start.11 = (bf16[1,800,128]{2,1,0:T(8,128)(2,1)S(1)}, bf16[1,800,128]{2,1,0:T(8,128)(2,1)S(1)}, u32[]{:S(2)}, u32[]{:S(2)}) collective-permute-start(bf16[1,800,128]{2,1,0:T(8,128)(2,1)S(1)} %get-tuple-element.94), channel_id=1, source_target_pairs={{0,16},{4,20},{8,24},{12,28},{16,0},{20,4},{24,8},{28,12},{1,17},{... | collective-permute-start | bytes 614408 | tf_op jit(solution)/shard_map/ppermute | solution.py:680

commit v13 on v10

--- a/solution.py
+++ b/solution.py
@@ -10,6 +10,7 @@
 EPSILON = 1e-05
 EDGE = 8
 LANES = 128
+LONG = 50_000_000_000
 F32 = jnp.float32
 BF16 = jnp.bfloat16
 
@@ -367,7 +368,7 @@
         write(send, 0)
 
 
-def finish_kernel(kernel, own, other, ready, value, gate, out, taps):
+def finish_kernel(kernel, own, other, pieces, value, gate, out, taps):
     width = value.shape[1]
     shard = value.shape[0]
 
@@ -376,7 +377,7 @@
 
     value[...] = total(0, width).T
     gate[...] = total(width, width).T
-    out[...] = ready[0].astype(F32).T
+    out[...] = jnp.sum(pieces[...].astype(F32), axis=0).T
     for q in range(width // shard):
         taps[:, q * shard : (q + 1) * shard] = total(2 * width + 16 * q, 16)[:kernel]
 
@@ -611,7 +612,7 @@
             1024,
         )(mine, sibling, after(w_own, *earlier), w_sibling, picked)
 
-    def deliver(part, *earlier):
+    def deliver(part, weight, *earlier):
         arrived = []
         for d in range(1, chips):
             send = [(i, ((i // 2 + d) % chips) * 2 + i % 2) for i in range(tps)]
@@ -628,7 +629,7 @@
             block,
             sds(part[0].shape, BF16),
             [],
-            50_000_000_000,
+            weight,
             1024,
         )(after(part[0], *earlier), *arrived)
         return own
@@ -639,16 +640,16 @@
     parts = [None] * 3
     owns = [None] * 3
     moved = [None] * 3
-    w_out_sum = lax.psum_scatter(w_out, "seq", scatter_dimension=0, tiled=True)
+    w_out_pieces = exchange(w_out, "seq")
     grads[0], taps[0] = back(*groups[0], w_out)
     grads[1], taps[1] = back(*groups[1], grads[0])
     parts[0] = partials(*groups[0], grads[0], grads[1])
     grads[2], taps[2] = back(*groups[2], *parts[0])
     parts[1] = partials(*groups[1], grads[1], grads[2])
-    owns[0] = deliver(parts[0], *parts[1])
-    moved[0] = exchange(owns[0], "seq")
-    owns[1] = deliver(parts[1], owns[0])
-    parts[2] = partials(*groups[2], grads[2], owns[1])
+    owns[0] = deliver(parts[0], LONG, w_out_pieces, *parts[1])
+    parts[2] = partials(*groups[2], grads[2], owns[0])
+    moved[0] = exchange(after(owns[0], *parts[2]), "seq")
+    owns[1] = deliver(parts[1], 0, *parts[2])
 
     slots = 2 * width + 16 * (width // shard)
     half = sds((seqs // 2, slots, shard), BF16)
@@ -668,19 +669,21 @@
         [whole(half.shape)] * 2,
         [half] * 2,
         [pltpu.VMEM((2 * width, model), F32)],
-        50_000_000_000,
+        LONG,
         1024,
-    )(parity, after(normed, *parts[2]), *grads, *taps)
+    )(parity, after(normed, owns[1]), *grads, *taps)
     moved[1] = exchange(after(owns[1], keep, moved[0]), "seq")
     bit = 1
     while True:
         others = lax.ppermute(send, "seq", [(i, i ^ bit) for i in range(seqs)])
         if bit == 1:
-            owns[2] = deliver(parts[2], others)
+            owns[2] = deliver(parts[2], 0, others)
             moved[2] = exchange(after(owns[2], moved[1]), "seq")
         bit *= 2
         if bit == seqs:
             break
+        if bit == 2:
+            keep = after(keep, owns[2])
         shape = (keep.shape[0] // 2,) + keep.shape[1:]
         side = ((seq_at // bit) % 2).astype(jnp.int32).reshape(1, 1)
         keep, send = call(
@@ -699,14 +702,14 @@
         functools.partial(finish_kernel, kernel),
         "finish",
         (1,),
-        [whole(keep.shape)] * 2 + [whole((1, width, shard))],
+        [whole(keep.shape)] * 2 + [whole((seqs, width, shard))],
         [whole((shard, width))] * 3 + [whole((kernel, width))],
         [sds((shard, width), F32)] * 3 + [sds((kernel, width), F32)],
         [],
         0,
         1024,
         vmem=20,
-    )(keep, others, w_out_sum)
+    )(keep, others, w_out_pieces)
     grad_in = ()
     for (first, size), part in zip(groups, moved):
         grad_in = (

time: 248 us -> 211 us (0.85)
  waiting for transfers between devices: 84.6 us -> 56.9 us
  between operations: 14.9 us -> 1.52 us
  starting transfers between devices: 45.3 us -> 49.5 us
    reduce_scatter x1 -> x0, waiting for transfers between devices: 35.9 us -> none  [per_device(): w_out_sum = lax.psum_scatter(w_out, 'seq', scatter_dimension=0, tiled=True)]
    ppermute x3, waiting for transfers between devices: 33.1 us -> 38.7 us  [per_device(): others = lax.ppermute(send, 'seq', [(i, i ^ bit) for i in range(seqs)])]
    all_to_all x5 -> x6, waiting for transfers between devices: 5.74 us -> 10.2 us  [exchange(): return lax.all_to_all(copies, axis, 0, 0, tiled=True)]
    all_to_all x5 -> x6, starting transfers between devices: 25.5 us -> 29.8 us  [exchange(): return lax.all_to_all(copies, axis, 0, 0, tiled=True)]
  transfers between devices with their start and end apart: 18 -> 18, of which waited for: 6 -> 7; matrix products, arithmetic and copies ran while one was open for 2% -> 2% of each run, Pallas kernels for 23% -> 27%
where the time goes in v13:
time: 211 us; the launch traced here: 209 us
  Pallas kernels  90.4 us (43%)
  waiting for transfers between devices  56.9 us (27%)
  starting transfers between devices  49.5 us (23%)
  local copies, waits for them, and re-layouts  6.08 us (3%)
  other arithmetic  4.94 us (2%)
    ppermute x3, waiting for transfers between devices, per_device(): others = lax.ppermute(send, 'seq', [(i, i ^ bit) for i in range(seqs)])  38.7 us
    all_to_all x6, starting transfers between devices, exchange(): return lax.all_to_all(copies, axis, 0, 0, tiled=True)  29.8 us
    pallas_call x3, Pallas kernels, back(): call(functools.partial(back_kernel, first, blocks), 'back_conv', (size *...  19 us
    pallas_call x1, Pallas kernels, per_device(): call(gate_kernel, 'gate_conv', (recs,), [smem(), per_record((frames, mode...  15.3 us
    pallas_call x3, Pallas kernels, partials(): call(partial_kernel, 'partial_in', (size * parts_in,), [pl.BlockSpec((hal...  15.1 us
    pallas_call x1, Pallas kernels, per_device(): call(norm_kernel, 'swish_norm', (recs,), [smem(), smem(), whole((seqs, 2,...  12.1 us
    all_to_all x6, waiting for transfers between devices, exchange(): return lax.all_to_all(copies, axis, 0, 0, tiled=True)  10.2 us
    pallas_call x1, Pallas kernels, per_device(): call(functools.partial(outer_kernel, groups), 'outer_w_in', (recs,), [sme...  9.54 us
  transfers between devices with their start and end apart: 18, of which 7 were waited for; matrix products, arithmetic and copies ran while one was open for 2% of the time, Pallas kernels for 27%

profile of v13, /device:TPU:0, one launch (start us, length us, event | category | flops | bytes accessed | tf_op | source)
XLA Modules:
  0.0 209.3 jit_solution(8026029972801388212)
XLA Ops:
  0.6 1.0 fusion.1
  1.6 4.9 %collective-permute-start = (bf16[4,8,2048]{2,1,0:T(8,128)(2,1)S(1)}, bf16[4,8,2048]{2,1,0:T(8,128)(2,1)S(1)}, u32[]{:S(2)}, u32[]{:S(2)}) collective-permute-start(bf16[4,8,2048]{2,1,0:T(8,128)(2,1)S(1)} %pad_maximum_fusion.3), channel_id=1, source_target_pairs={{0,4},{4,8},{8,12},{12,16},{16,20},{20,24},{24,28},{1,5},{5,9},{9,... | collective-permute-start | bytes 393224 | tf_op jit(solution)/shard_map/ppermute | solution.py:433
  6.5 1.3 collective-permute-start.1
  7.8 1.3 fusion.5
  9.7 3.7 %collective-permute-done.1 = bf16[4,8,2048]{2,1,0:T(8,128)(2,1)S(1)} collective-permute-done((bf16[4,8,2048]{2,1,0:T(8,128)(2,1)S(1)}, bf16[4,8,2048]{2,1,0:T(8,128)(2,1)S(1)}, u32[]{:S(2)}, u32[]{:S(2)}) %collective-permute-start.1) | collective-permute-done | bytes 131104 | tf_op jit(solution)/shard_map/ppermute | solution.py:433
  13.4 0.7 fusion.3
  14.1 15.3 %gate_conv.1 = (f32[4,1024,256]{2,1,0:T(8,128)}, f32[4,1024,256]{2,1,0:T(8,128)}, f32[4,1040,256]{2,1,0:T(8,128)}, f32[8,2,256]{2,1,0:T(2,128)}) custom-call(s32[2,4]{1,0:T(2,128)} %stack.35.meta, bf16[4,1024,1024]{2,1,0:T(8,128)(2,1)} %x.4, bf16[4,16,1024]{2,1,0:T(8,128)(2,1)} %get-tuple-element.108.halo, bf16[1024,256]{1,0:T(8,128)(2,1)} %wv.1, ...), custom_call_target="tpu_custom_call" | custom-call | flops 4294967296 | bytes 20971520 | tf_op jit(solution)/shard_map/gate_conv/pallas_call | solution.py:447
  29.4 1.1 pad_maximum_fusion
  31.6 0.6 pad_maximum_fusion.5.affine
  32.2 0.9 fusion.select
  33.2 5.7 %all-to-all-start = ((f32[8,2,256]{2,1,0:T(2,128)}), f32[8,2,256]{2,1,0:T(2,128)S(1)}, u32[]{:S(2)}, u32[]{:S(2)}) async-start(f32[8,2,256]{2,1,0:T(2,128)} %get-tuple-element.53), calls=%async_computation | async-start | bytes 32768 | tf_op jit(solution)/shard_map/all_to_all | solution.py:393
  38.9 0.8 pad_maximum_fusion.1
  39.7 5.7 %all-to-all-done.stats = f32[8,2,256]{2,1,0:T(2,128)S(1)} async-done(((f32[8,2,256]{2,1,0:T(2,128)}), f32[8,2,256]{2,1,0:T(2,128)S(1)}, u32[]{:S(2)}, u32[]{:S(2)}) %all-to-all-start) | async-done | bytes 16416 | tf_op jit(solution)/shard_map/all_to_all | solution.py:393
  45.5 0.6 copy-done.8
  46.1 12.1 %swish_norm.1 = (bf16[4,1024,256]{2,1,0:T(8,128)(2,1)}, f32[4,1040,256]{2,1,0:T(8,128)}, bf16[4,256,1024]{2,1,0:T(8,128)(2,1)}, f32[8,2,256]{2,1,0:T(2,128)}) custom-call(s32[2,4]{1,0:T(2,128)} %stack.35.meta, f32[1,1]{1,0:T(1,128)} %bitcast.1.count, f32[8,2,256]{2,1,0:T(2,128)} %copy-done.8, f32[2,256]{1,0:T(2,128)} %pad_maximum_fusion.5.affine, ...), custom_call_target="tpu_custom_call" | custom-call | flops 4294967296 | bytes 20971520 | tf_op jit(solution)/shard_map/swish_norm/pallas_call | solution.py:492
  58.1 3.3 %all-to-all-start.1 = ((f32[8,2,256]{2,1,0:T(2,128)}), f32[8,2,256]{2,1,0:T(2,128)S(1)}, u32[]{:S(2)}, u32[]{:S(2)}) async-start(f32[8,2,256]{2,1,0:T(2,128)} %get-tuple-element.57), calls=%async_computation.1 | async-start | bytes 32768 | tf_op jit(solution)/shard_map/all_to_all | solution.py:393
  61.5 6.7 %outer_w_out.1 = bf16[8,256,128]{2,1,0:T(8,128)(2,1)} custom-call(bf16[4,1024,1024]{2,1,0:T(8,128)(2,1)} %grads.3, bf16[4,1024,256]{2,1,0:T(8,128)(2,1)} %get-tuple-element.61.swished), custom_call_target="tpu_custom_call" | custom-call | flops 2147483648 | bytes 8388608 | tf_op jit(solution)/shard_map/outer_w_out/pallas_call | solution.py:537
  68.2 0.6 copy-done.6
  68.8 5.0 %back_conv.3 = (bf16[1024,512]{1,0:T(8,128)(2,1)}, f32[16,256]{1,0:T(8,128)}) custom-call(s32[2,4]{1,0:T(2,128)} %stack.35.meta, f32[1,1]{1,0:T(1,128)} %bitcast.1.count, f32[8,2,256]{2,1,0:T(2,128)} %copy-done.8, f32[8,2,256]{2,1,0:T(2,128)} %copy-done.6, f32[1,256]{1,0:T(1,128)} %bitcast.26, f32[4,1040,256]{2,1,0:T(8,128)} %get-tuple-element.58.gn, ...), custom_call_target="tpu_custom_call" | custom-call | bytes 1024 | tf_op jit(solution)/shard_map/back_conv/pallas_call | solution.py:561
  73.9 5.1 %back_conv.4 = (bf16[1024,512]{1,0:T(8,128)(2,1)}, f32[16,256]{1,0:T(8,128)}) custom-call(s32[2,4]{1,0:T(2,128)} %stack.35.meta, f32[1,1]{1,0:T(1,128)} %bitcast.1.count, f32[8,2,256]{2,1,0:T(2,128)} %copy-done.8, f32[8,2,256]{2,1,0:T(2,128)} %copy-done.6, f32[1,256]{1,0:T(1,128)} %bitcast.27, f32[4,1040,256]{2,1,0:T(8,128)} %get-tuple-element.58.gn, ...), custom_call_target="tpu_custom_call" | custom-call | bytes 1024 | tf_op jit(solution)/shard_map/back_conv/pallas_call | solution.py:561
  79.5 5.9 %all-to-all-start.2 = ((bf16[8,256,128]{2,1,0:T(8,128)(2,1)}), bf16[8,256,128]{2,1,0:T(8,128)(2,1)S(1)}, u32[]{:S(2)}, u32[]{:S(2)}) async-start(bf16[8,256,128]{2,1,0:T(8,128)(2,1)} %outer_w_out.1), calls=%async_computation.2 | async-start | bytes 1048576 | tf_op jit(solution)/shard_map/all_to_all | solution.py:393
  85.4 4.3 %partial_in.3 = (bf16[8,1,32,1024]{3,2,1,0:T(8,128)(2,1)}, bf16[8,1,32,1024]{3,2,1,0:T(8,128)(2,1)}) custom-call(bf16[1024,512]{1,0:T(8,128)(2,1)} %get-tuple-element.63.own.refs_0_, bf16[1024,512]{1,0:T(8,128)(2,1)} %collective-permute-done.3.sibling, bf16[512,512]{1,0:T(8,128)(2,1)} %bitcast.21, bf16[512,512]{1,0:T(8,128)(2,1)} %collective-permute-done.2.w_sibling, ...), custom_call_target="tpu_custom_call" | custom-call | bytes 1024 | tf_op jit(solution)/shard_map/partial_in/pallas_call | solution.py:590
  89.7 1.5 collective-permute-start.6
  91.2 8.9 %back_conv.5 = (bf16[2048,512]{1,0:T(8,128)(2,1)}, f32[16,256]{1,0:T(8,128)}) custom-call(s32[2,4]{1,0:T(2,128)} %stack.35.meta, f32[1,1]{1,0:T(1,128)} %bitcast.1.count, f32[8,2,256]{2,1,0:T(2,128)} %copy-done.8, f32[8,2,256]{2,1,0:T(2,128)} %copy-done.6, f32[1,256]{1,0:T(1,128)} %bitcast.28, f32[4,1040,256]{2,1,0:T(8,128)} %get-tuple-element.58.gn, ...), custom_call_target="tpu_custom_call" | custom-call | bytes 1024 | tf_op jit(solution)/shard_map/back_conv/pallas_call | solution.py:561
  100.2 4.3 %partial_in.4 = (bf16[8,1,32,1024]{3,2,1,0:T(8,128)(2,1)}, bf16[8,1,32,1024]{3,2,1,0:T(8,128)(2,1)}) custom-call(bf16[1024,512]{1,0:T(8,128)(2,1)} %get-tuple-element.65.own.refs_1_, bf16[1024,512]{1,0:T(8,128)(2,1)} %collective-permute-done.5.sibling, bf16[512,512]{1,0:T(8,128)(2,1)} %bitcast.22, bf16[512,512]{1,0:T(8,128)(2,1)} %collective-permute-done.2.w_sibling, ...), custom_call_target="tpu_custom_call" | custom-call | bytes 1024 | tf_op jit(solution)/shard_map/partial_in/pallas_call | solution.py:590
  105.0 2.2 %add.115 = bf16[8,1,32,1024]{3,2,1,0:T(8,128)(2,1)} custom-call(bf16[8,1,32,1024]{3,2,1,0:T(8,128)(2,1)} %get-tuple-element.75.refs_0_, bf16[8,1,32,1024]{3,2,1,0:T(8,128)(2,1)} %collective-permute-done.6.refs_1_), custom_call_target="tpu_custom_call" | custom-call | flops 49999998976 | bytes 1024 | tf_op jit(solution)/shard_map/add/pallas_call | solution.py:624
  107.2 6.5 %partial_in.5 = (bf16[8,2,32,1024]{3,2,1,0:T(8,128)(2,1)}, bf16[8,2,32,1024]{3,2,1,0:T(8,128)(2,1)}) custom-call(bf16[2048,512]{1,0:T(8,128)(2,1)} %get-tuple-element.71.own.refs_2_, bf16[2048,512]{1,0:T(8,128)(2,1)} %collective-permute-done.4.sibling, bf16[512,512]{1,0:T(8,128)(2,1)} %bitcast.23, bf16[512,512]{1,0:T(8,128)(2,1)} %collective-permute-done.2.w_sibling, ...), custom_call_target="tpu_custom_call" | custom-call | bytes 1024 | tf_op jit(solution)/shard_map/partial_in/pallas_call | solution.py:590
  113.7 1.5 collective-permute-start.9
  115.2 4.3 %collective-permute-done.7.refs_1_ = bf16[8,1,32,1024]{3,2,1,0:T(8,128)(2,1)} collective-permute-done((bf16[8,1,32,1024]{3,2,1,0:T(8,128)(2,1)}, bf16[8,1,32,1024]{3,2,1,0:T(8,128)(2,1)}, u32[]{:S(2)}, u32[]{:S(2)}) %collective-permute-start.7) | collective-permute-done | bytes 524320 | tf_op jit(solution)/shard_map/ppermute | solution.py:619
  119.5 2.0 add.116
  121.5 6.0 %all-to-all-start.3 = ((bf16[8,1,32,1024]{3,2,1,0:T(8,128)(2,1)}), bf16[8,1,32,1024]{3,2,1,0:T(8,128)(2,1)S(1)}, u32[]{:S(2)}, u32[]{:S(2)}) async-start(bf16[8,1,32,1024]{3,2,1,0:T(8,128)(2,1)} %add.115), calls=%async_computation.3 | async-start | bytes 1048576 | tf_op jit(solution)/shard_map/all_to_all | solution.py:393
  127.5 9.5 %outer_w_in.1 = (bf16[4,544,128]{2,1,0:T(8,128)(2,1)}, bf16[4,544,128]{2,1,0:T(8,128)(2,1)}) custom-call(s32[1,1]{1,0:T(1,128)} %bitcast.11.parity, bf16[4,1024,1024]{2,1,0:T(8,128)(2,1)} %x.4, bf16[1024,512]{1,0:T(8,128)(2,1)} %get-tuple-element.63.own.refs_0_, bf16[1024,512]{1,0:T(8,128)(2,1)} %get-tuple-element.65.own.refs_1_, ...), custom_call_target="tpu_custom_call" | custom-call | flops 49999998976 | bytes 1024 | tf_op jit(solution)/shard_map/outer_w_in/pallas_call | solution.py:656
  137.0 4.4 %all-to-all-done.3.moved = bf16[8,1,32,1024]{3,2,1,0:T(8,128)(2,1)S(1)} async-done(((bf16[8,1,32,1024]{3,2,1,0:T(8,128)(2,1)}), bf16[8,1,32,1024]{3,2,1,0:T(8,128)(2,1)S(1)}, u32[]{:S(2)}, u32[]{:S(2)}) %all-to-all-start.3) | async-done | bytes 524320 | tf_op jit(solution)/shard_map/all_to_all | solution.py:393
  141.5 4.2 %all-to-all-start.4 = ((bf16[8,1,32,1024]{3,2,1,0:T(8,128)(2,1)}), bf16[8,1,32,1024]{3,2,1,0:T(8,128)(2,1)}, u32[]{:S(2)}, u32[]{:S(2)}) async-start(bf16[8,1,32,1024]{3,2,1,0:T(8,128)(2,1)} %add.116), calls=%async_computation.4 | async-start | bytes 1048576 | tf_op jit(solution)/shard_map/all_to_all | solution.py:393
  145.6 1.9 collective-permute-start.8
  147.5 17.2 %collective-permute-done.8.other = bf16[4,544,128]{2,1,0:T(8,128)(2,1)S(1)} collective-permute-done((bf16[4,544,128]{2,1,0:T(8,128)(2,1)}, bf16[4,544,128]{2,1,0:T(8,128)(2,1)S(1)}, u32[]{:S(2)}, u32[]{:S(2)}) %collective-permute-start.8) | collective-permute-done | bytes 557088 | tf_op jit(solution)/shard_map/ppermute | solution.py:678
  164.7 0.8 copy-done.3
  165.5 3.7 %add.117 = bf16[8,2,32,1024]{3,2,1,0:T(8,128)(2,1)} custom-call(bf16[8,2,32,1024]{3,2,1,0:T(8,128)(2,1)} %get-tuple-element.85.refs_0_, bf16[8,2,32,1024]{3,2,1,0:T(8,128)(2,1)} %collective-permute-done.9.refs_1_), custom_call_target="tpu_custom_call" | custom-call | bytes 1024 | tf_op jit(solution)/shard_map/add/pallas_call | solution.py:624
  169.2 4.7 %all-to-all-start.5 = ((bf16[8,2,32,1024]{3,2,1,0:T(8,128)(2,1)}), bf16[8,2,32,1024]{3,2,1,0:T(8,128)(2,1)S(1)}, u32[]{:S(2)}, u32[]{:S(2)}) async-start(bf16[8,2,32,1024]{3,2,1,0:T(8,128)(2,1)} %add.117), calls=%async_computation.5 | async-start | bytes 2097152 | tf_op jit(solution)/shard_map/all_to_all | solution.py:393
  173.9 1.0 copy-done.4
  175.1 2.1 collective-permute-start.10
  177.2 18.8 %collective-permute-done.10.other = bf16[2,544,128]{2,1,0:T(8,128)(2,1)S(1)} collective-permute-done((bf16[2,544,128]{2,1,0:T(8,128)(2,1)S(1)}, bf16[2,544,128]{2,1,0:T(8,128)(2,1)S(1)}, u32[]{:S(2)}, u32[]{:S(2)}) %collective-permute-start.10) | collective-permute-done | bytes 278560 | tf_op jit(solution)/shard_map/ppermute | solution.py:678
  196.1 5.3 %collective-permute-start.11 = (bf16[1,544,128]{2,1,0:T(8,128)(2,1)S(1)}, bf16[1,544,128]{2,1,0:T(8,128)(2,1)S(1)}, u32[]{:S(2)}, u32[]{:S(2)}) collective-permute-start(bf16[1,544,128]{2,1,0:T(8,128)(2,1)S(1)} %get-tuple-element.94), channel_id=1, source_target_pairs={{0,16},{4,20},{8,24},{12,28},{16,0},{20,4},{24,8},{28,12},{1,17},{... | collective-permute-start | bytes 417800 | tf_op jit(solution)/shard_map/ppermute | solution.py:678
  202.0 0.8 place.3.refs_0_
  202.8 2.7 %collective-permute-done.11.other = bf16[1,544,128]{2,1,0:T(8,128)(2,1)S(1)} collective-permute-done((bf16[1,544,128]{2,1,0:T(8,128)(2,1)S(1)}, bf16[1,544,128]{2,1,0:T(8,128)(2,1)S(1)}, u32[]{:S(2)}, u32[]{:S(2)}) %collective-permute-start.11) | collective-permute-done | bytes 139296 | tf_op jit(solution)/shard_map/ppermute | solution.py:678
  205.5 0.8 finish.1
  206.4 1.9 place.4.refs_0_
  208.3 1.1 place.5
  (48 shorter events, 3.0 us)
Async XLA Ops:
  1.6 8.1 %collective-permute-start = (bf16[4,8,2048]{2,1,0:T(8,128)(2,1)S(1)}, bf16[4,8,2048]{2,1,0:T(8,128)(2,1)S(1)}, u32[]{:S(2)}, u32[]{:S(2)}) collective-permute-start(bf16[4,8,2048]{2,1,0:T(8,128)(2,1)S(1)} %pad_maximum_fusion.3), channel_id=1, source_target_pairs={{0,4},{4,8},{8,12},{12,16},{16,20},{20,24},{24,28},{1,5},{5,9},{9,... | collective-permute-start | bytes 393224 | tf_op jit(solution)/shard_map/ppermute | solution.py:433
  6.5 6.9 %collective-permute-start.1 = (bf16[4,8,2048]{2,1,0:T(8,128)(2,1)S(1)}, bf16[4,8,2048]{2,1,0:T(8,128)(2,1)S(1)}, u32[]{:S(2)}, u32[]{:S(2)}) collective-permute-start(bf16[4,8,2048]{2,1,0:T(8,128)(2,1)S(1)} %pad_maximum_fusion.4), channel_id=1, source_target_pairs={{4,0},{8,4},{12,8},{16,12},{20,16},{24,20},{28,24},{5,1},{9,5},{13... | collective-permute-start | bytes 393224 | tf_op jit(solution)/shard_map/ppermute | solution.py:433
  14.1 15.3 %copy-start.5 = (bf16[1024,256]{1,0:T(8,128)(2,1)S(1)}, bf16[1024,256]{1,0:T(8,128)(2,1)}, u32[]{:S(2)}) copy-start(bf16[1024,256]{1,0:T(8,128)(2,1)} %wv.1) | copy-start | bytes 1572868
  30.6 1.1 copy-start.9
  30.6 1.1 copy-start.10
  30.7 9.0 %collective-permute-start.2 = (bf16[512,512]{1,0:T(8,128)(2,1)S(1)}, bf16[512,512]{1,0:T(8,128)(2,1)}, u32[]{:S(2)}, u32[]{:S(2)}) collective-permute-start(bf16[512,512]{1,0:T(8,128)(2,1)S(1)} %bitcast.25), channel_id=1, source_target_pairs={{0,1},{1,0},{2,3},{3,2},{4,5},{5,4},{6,7},{7,6},{8,9},{9,8},{10,11... | collective-permute-start | bytes 1572872 | tf_op jit(solution)/shard_map/ppermute | solution.py:486
  33.2 12.3 %all-to-all-start = ((f32[8,2,256]{2,1,0:T(2,128)}), f32[8,2,256]{2,1,0:T(2,128)S(1)}, u32[]{:S(2)}, u32[]{:S(2)}) async-start(f32[8,2,256]{2,1,0:T(2,128)} %get-tuple-element.53), calls=%async_computation | async-start | bytes 32768 | tf_op jit(solution)/shard_map/all_to_all | solution.py:393
  45.5 0.6 copy-start.8
  58.1 10.1 %all-to-all-start.1 = ((f32[8,2,256]{2,1,0:T(2,128)}), f32[8,2,256]{2,1,0:T(2,128)S(1)}, u32[]{:S(2)}, u32[]{:S(2)}) async-start(f32[8,2,256]{2,1,0:T(2,128)} %get-tuple-element.57), calls=%async_computation.1 | async-start | bytes 32768 | tf_op jit(solution)/shard_map/all_to_all | solution.py:393
  68.2 0.6 copy-start.6
  73.8 11.6 %collective-permute-start.3 = (bf16[1024,512]{1,0:T(8,128)(2,1)}, bf16[1024,512]{1,0:T(8,128)(2,1)}, u32[]{:S(2)}, u32[]{:S(2)}) collective-permute-start(bf16[1024,512]{1,0:T(8,128)(2,1)} %get-tuple-element.63.own.refs_0_), channel_id=1, source_target_pairs={{0,1},{1,0},{2,3},{3,2},{4,5},{5,4},{6,7},{7,6},{8,9},{9,8},{10,11... | collective-permute-start | bytes 3145736 | tf_op jit(solution)/shard_map/ppermute | solution.py:588
  79.0 21.1 %collective-permute-start.5 = (bf16[1024,512]{1,0:T(8,128)(2,1)}, bf16[1024,512]{1,0:T(8,128)(2,1)}, u32[]{:S(2)}, u32[]{:S(2)}) collective-permute-start(bf16[1024,512]{1,0:T(8,128)(2,1)} %get-tuple-element.65.own.refs_1_), channel_id=1, source_target_pairs={{0,1},{1,0},{2,3},{3,2},{4,5},{5,4},{6,7},{7,6},{8,9},{9,8},{10,11... | collective-permute-start | bytes 3145736 | tf_op jit(solution)/shard_map/ppermute | solution.py:588
  79.5 25.5 %all-to-all-start.2 = ((bf16[8,256,128]{2,1,0:T(8,128)(2,1)}), bf16[8,256,128]{2,1,0:T(8,128)(2,1)S(1)}, u32[]{:S(2)}, u32[]{:S(2)}) async-start(bf16[8,256,128]{2,1,0:T(8,128)(2,1)} %outer_w_out.1), calls=%async_computation.2 | async-start | bytes 1048576 | tf_op jit(solution)/shard_map/all_to_all | solution.py:393
  89.7 15.3 %collective-permute-start.6 = (bf16[8,1,32,1024]{3,2,1,0:T(8,128)(2,1)}, bf16[8,1,32,1024]{3,2,1,0:T(8,128)(2,1)}, u32[]{:S(2)}, u32[]{:S(2)}) collective-permute-start(bf16[8,1,32,1024]{3,2,1,0:T(8,128)(2,1)} %get-tuple-element.69), channel_id=1, source_target_pairs={{0,2},{1,3},{2,0},{3,1},{4,6},{5,7},{6,4},{7,5},{8,10},{9,11},{10,... | collective-permute-start | bytes 1572872 | tf_op jit(solution)/shard_map/ppermute | solution.py:619
  100.1 7.1 %collective-permute-start.4 = (bf16[2048,512]{1,0:T(8,128)(2,1)}, bf16[2048,512]{1,0:T(8,128)(2,1)}, u32[]{:S(2)}, u32[]{:S(2)}) collective-permute-start(bf16[2048,512]{1,0:T(8,128)(2,1)} %get-tuple-element.71.own.refs_2_), channel_id=1, source_target_pairs={{0,1},{1,0},{2,3},{3,2},{4,5},{5,4},{6,7},{7,6},{8,9},{9,8},{10,11... | collective-permute-start | bytes 6291464 | tf_op jit(solution)/shard_map/ppermute | solution.py:588
  104.5 15.0 %collective-permute-start.7 = (bf16[8,1,32,1024]{3,2,1,0:T(8,128)(2,1)}, bf16[8,1,32,1024]{3,2,1,0:T(8,128)(2,1)}, u32[]{:S(2)}, u32[]{:S(2)}) collective-permute-start(bf16[8,1,32,1024]{3,2,1,0:T(8,128)(2,1)} %get-tuple-element.74), channel_id=1, source_target_pairs={{0,2},{1,3},{2,0},{3,1},{4,6},{5,7},{6,4},{7,5},{8,10},{9,11},{10,... | collective-permute-start | bytes 1572872 | tf_op jit(solution)/shard_map/ppermute | solution.py:619
  105.0 2.2 %copy-start = (bf16[8,256,128]{2,1,0:T(8,128)(2,1)}, bf16[8,256,128]{2,1,0:T(8,128)(2,1)S(1)}, u32[]{:S(2)}) copy-start(bf16[8,256,128]{2,1,0:T(8,128)(2,1)S(1)} %all-to-all-done.2.pieces) | copy-start | bytes 1572868
  113.7 51.8 %collective-permute-start.9 = (bf16[8,2,32,1024]{3,2,1,0:T(8,128)(2,1)}, bf16[8,2,32,1024]{3,2,1,0:T(8,128)(2,1)}, u32[]{:S(2)}, u32[]{:S(2)}) collective-permute-start(bf16[8,2,32,1024]{3,2,1,0:T(8,128)(2,1)} %get-tuple-element.78), channel_id=1, source_target_pairs={{0,2},{1,3},{2,0},{3,1},{4,6},{5,7},{6,4},{7,5},{8,10},{9,11},{10,... | collective-permute-start | bytes 3145736 | tf_op jit(solution)/shard_map/ppermute | solution.py:619
  121.5 20.0 %all-to-all-start.3 = ((bf16[8,1,32,1024]{3,2,1,0:T(8,128)(2,1)}), bf16[8,1,32,1024]{3,2,1,0:T(8,128)(2,1)S(1)}, u32[]{:S(2)}, u32[]{:S(2)}) async-start(bf16[8,1,32,1024]{3,2,1,0:T(8,128)(2,1)} %add.115), calls=%async_computation.3 | async-start | bytes 1048576 | tf_op jit(solution)/shard_map/all_to_all | solution.py:393
  141.5 27.8 %all-to-all-start.4 = ((bf16[8,1,32,1024]{3,2,1,0:T(8,128)(2,1)}), bf16[8,1,32,1024]{3,2,1,0:T(8,128)(2,1)}, u32[]{:S(2)}, u32[]{:S(2)}) async-start(bf16[8,1,32,1024]{3,2,1,0:T(8,128)(2,1)} %add.116), calls=%async_computation.4 | async-start | bytes 1048576 | tf_op jit(solution)/shard_map/all_to_all | solution.py:393
  145.6 19.1 %collective-permute-start.8 = (bf16[4,544,128]{2,1,0:T(8,128)(2,1)}, bf16[4,544,128]{2,1,0:T(8,128)(2,1)S(1)}, u32[]{:S(2)}, u32[]{:S(2)}) collective-permute-start(bf16[4,544,128]{2,1,0:T(8,128)(2,1)} %get-tuple-element.84), channel_id=1, source_target_pairs={{0,4},{4,0},{8,12},{12,8},{16,20},{20,16},{24,28},{28,24},{1,5},{5... | collective-permute-start | bytes 1671176 | tf_op jit(solution)/shard_map/ppermute | solution.py:678
  164.7 0.8 copy-start.3
  169.2 4.7 %copy-start.2 = (bf16[4,544,128]{2,1,0:T(8,128)(2,1)S(1)}, bf16[4,544,128]{2,1,0:T(8,128)(2,1)}, u32[]{:S(2)}) copy-start(bf16[4,544,128]{2,1,0:T(8,128)(2,1)} %get-tuple-element.90.own) | copy-start | bytes 1671172
  169.2 8.0 %copy-start.7 = (f32[8,2,256]{2,1,0:T(2,128)S(1)}, f32[8,2,256]{2,1,0:T(2,128)}, u32[]{:S(2)}) copy-start(f32[8,2,256]{2,1,0:T(2,128)} %copy-done.6) | copy-start | bytes 49156
  169.2 39.0 %all-to-all-start.5 = ((bf16[8,2,32,1024]{3,2,1,0:T(8,128)(2,1)}), bf16[8,2,32,1024]{3,2,1,0:T(8,128)(2,1)S(1)}, u32[]{:S(2)}, u32[]{:S(2)}) async-start(bf16[8,2,32,1024]{3,2,1,0:T(8,128)(2,1)} %add.117), calls=%async_computation.5 | async-start | bytes 2097152 | tf_op jit(solution)/shard_map/all_to_all | solution.py:393
  173.9 1.1 copy-start.4
  175.0 30.6 %copy-start.1 = (bf16[8,256,128]{2,1,0:T(8,128)(2,1)S(1)}, bf16[8,256,128]{2,1,0:T(8,128)(2,1)}, u32[]{:S(2)}) copy-start(bf16[8,256,128]{2,1,0:T(8,128)(2,1)} %copy-done) | copy-start | bytes 1572868
  175.1 20.9 %collective-permute-start.10 = (bf16[2,544,128]{2,1,0:T(8,128)(2,1)S(1)}, bf16[2,544,128]{2,1,0:T(8,128)(2,1)S(1)}, u32[]{:S(2)}, u32[]{:S(2)}) collective-permute-start(bf16[2,544,128]{2,1,0:T(8,128)(2,1)S(1)} %get-tuple-element.92), channel_id=1, source_target_pairs={{0,8},{4,12},{8,0},{12,4},{16,24},{20,28},{24,16},{28,20},{1,9},{5... | collective-permute-start | bytes 835592 | tf_op jit(solution)/shard_map/ppermute | solution.py:678
  196.1 9.4 %collective-permute-start.11 = (bf16[1,544,128]{2,1,0:T(8,128)(2,1)S(1)}, bf16[1,544,128]{2,1,0:T(8,128)(2,1)S(1)}, u32[]{:S(2)}, u32[]{:S(2)}) collective-permute-start(bf16[1,544,128]{2,1,0:T(8,128)(2,1)S(1)} %get-tuple-element.94), channel_id=1, source_target_pairs={{0,16},{4,20},{8,24},{12,28},{16,0},{20,4},{24,8},{28,12},{1,17},{... | collective-permute-start | bytes 417800 | tf_op jit(solution)/shard_map/ppermute | solution.py:678

commit v14 on v12

--- a/solution.py
+++ b/solution.py
@@ -635,21 +635,12 @@
         )(after(part[0], *earlier), *arrived)
         return own
 
-    groups = ((0, 1), (1, 1), (2, recs - 2))
-    grads = [None] * 3
-    taps = [None] * 3
-    parts = [None] * 3
-    owns = [None] * 3
-    moved = [None] * 3
+    groups = ((0, recs // 2), (recs // 2, recs - recs // 2))
+    grads, taps, parts, owns, moved = ([None] * 2 for _ in range(5))
     grads[0], taps[0] = back(*groups[0], w_out)
     grads[1], taps[1] = back(*groups[1], grads[0])
     parts[0] = partials(*groups[0], grads[0], grads[1])
-    grads[2], taps[2] = back(*groups[2], *parts[0])
-    parts[1] = partials(*groups[1], grads[1], grads[2])
-    owns[0] = deliver(parts[0], LONG, *parts[1])
-    parts[2] = partials(*groups[2], grads[2], owns[0])
-    moved[0] = exchange(after(owns[0], *parts[2]), "seq")
-    owns[1] = deliver(parts[1], 0, *parts[2])
+    parts[1] = partials(*groups[1], grads[1], *parts[0])
 
     slots = 3 * width + 16 * (width // shard)
     half = sds((seqs // 2, slots, shard), BF16)
@@ -669,12 +660,11 @@
         [whole(half.shape)] * 2,
         [half] * 2,
         [pltpu.VMEM((2 * width, model), F32)],
-        LONG,
+        0,
         1024,
-    )(parity, after(normed, owns[1]), w_out, *grads, *taps)
-    moved[1] = exchange(after(owns[1], keep, moved[0]), "seq")
-    owns[2] = deliver(parts[2], 0, keep)
-    moved[2] = exchange(after(owns[2], moved[1]), "seq")
+    )(parity, after(normed, *parts[1]), w_out, *grads, *taps)
+    owns[0] = deliver(parts[0], LONG, keep)
+    moved[0] = exchange(owns[0], "seq")
     bit = 1
     while True:
         others = lax.ppermute(send, "seq", [(i, i ^ bit) for i in range(seqs)])
@@ -682,7 +672,7 @@
         if bit == seqs:
             break
         if bit == 2:
-            keep = after(keep, owns[2])
+            keep = after(keep, owns[0])
         shape = (keep.shape[0] // 2,) + keep.shape[1:]
         side = ((seq_at // bit) % 2).astype(jnp.int32).reshape(1, 1)
         keep, send = call(
@@ -697,6 +687,10 @@
             1024,
             vmem=20,
         )(side, keep, others)
+        if bit == 2:
+            owns[1] = deliver(parts[1], 0, keep)
+        if bit == min(4, seqs // 2):
+            moved[1] = exchange(after(owns[1], moved[0], keep), "seq")
     w_value, w_gate, w_out, grad_taps = call(
         functools.partial(finish_kernel, kernel),
         "finish",

time: 216 us -> 216 us (level)
  waiting for transfers between devices: 69.3 us -> 78.8 us
  Pallas kernels: 92.3 us -> 87.9 us
  starting transfers between devices: 41.3 us -> 37.5 us
    ppermute x3, waiting for transfers between devices: 41.6 us -> 62.1 us  [per_device(): others = lax.ppermute(send, 'seq', [(i, i ^ bit) for i in range(seqs)])]
    all_to_all x5 -> x4, waiting for transfers between devices: 19.6 us -> 5.68 us  [exchange(): return lax.all_to_all(copies, axis, 0, 0, tiled=True)]
    ppermute x3 -> x2, waiting for transfers between devices: 4.47 us -> 7.3 us  [deliver(): arrived.append(lax.ppermute(part[d], 'tp', send))]
    pallas_call x3 -> x2, Pallas kernels: 14.9 us -> 13.2 us  [partials(): call(partial_kernel, 'partial_in', (size * parts_in,), [pl.BlockSpec((hal...]
    all_to_all x5 -> x4, starting transfers between devices: 22.8 us -> 21.3 us  [exchange(): return lax.all_to_all(copies, axis, 0, 0, tiled=True)]
    pallas_call x3 -> x2, Pallas kernels: 19 us -> 17.8 us  [back(): call(functools.partial(back_kernel, first, blocks), 'back_conv', (size *...]
    pallas_call x3 -> x2, Pallas kernels: 7.67 us -> 7.32 us  [deliver(): call(add_kernel, 'add', (size * parts_in,), [block] * chips, block, sds(p...]
  transfers between devices with their start and end apart: 17 -> 14, of which waited for: 8 -> 6; matrix products, arithmetic and copies ran while one was open for 2% -> 2% of each run, Pallas kernels for 27% -> 22%
where the time goes in v14:
time: 216 us; the launch traced here: 215 us
  Pallas kernels  87.9 us (41%)
  waiting for transfers between devices  78.8 us (36%)
  starting transfers between devices  37.5 us (17%)
  other arithmetic  5.01 us (2%)
  local copies, waits for them, and re-layouts  4.23 us (2%)
    ppermute x3, waiting for transfers between devices, per_device(): others = lax.ppermute(send, 'seq', [(i, i ^ bit) for i in range(seqs)])  62.1 us
    all_to_all x4, starting transfers between devices, exchange(): return lax.all_to_all(copies, axis, 0, 0, tiled=True)  21.3 us
    pallas_call x2, Pallas kernels, back(): call(functools.partial(back_kernel, first, blocks), 'back_conv', (size *...  17.8 us
    pallas_call x1, Pallas kernels, per_device(): call(gate_kernel, 'gate_conv', (recs,), [smem(), per_record((frames, mode...  15.3 us
    pallas_call x2, Pallas kernels, partials(): call(partial_kernel, 'partial_in', (size * parts_in,), [pl.BlockSpec((hal...  13.2 us
    pallas_call x1, Pallas kernels, per_device(): call(norm_kernel, 'swish_norm', (recs,), [smem(), smem(), whole((seqs, 2,...  12.1 us
    pallas_call x1, Pallas kernels, per_device(): call(functools.partial(outer_kernel, groups), 'outer_w_in', (recs,), [sme...  10.1 us
    pallas_call x2, Pallas kernels, deliver(): call(add_kernel, 'add', (size * parts_in,), [block] * chips, block, sds(p...  7.32 us
  transfers between devices with their start and end apart: 14, of which 6 were waited for; matrix products, arithmetic and copies ran while one was open for 2% of the time, Pallas kernels for 22%

profile of v14, /device:TPU:0, one launch (start us, length us, event | category | flops | bytes accessed | tf_op | source)
XLA Modules:
  0.0 214.9 jit_solution(7451592385069158112)
XLA Ops:
  0.6 1.0 fusion.1
  1.6 4.9 %collective-permute-start = (bf16[4,8,2048]{2,1,0:T(8,128)(2,1)S(1)}, bf16[4,8,2048]{2,1,0:T(8,128)(2,1)S(1)}, u32[]{:S(2)}, u32[]{:S(2)}) collective-permute-start(bf16[4,8,2048]{2,1,0:T(8,128)(2,1)S(1)} %pad_maximum_fusion.3), channel_id=1, source_target_pairs={{0,4},{4,8},{8,12},{12,16},{16,20},{20,24},{24,28},{1,5},{5,9},{9,... | collective-permute-start | bytes 393224 | tf_op jit(solution)/shard_map/ppermute | solution.py:434
  6.5 1.3 collective-permute-start.1
  7.8 1.3 fusion.5
  9.1 0.6 stack.35.meta
  9.7 3.7 %collective-permute-done.1 = bf16[4,8,2048]{2,1,0:T(8,128)(2,1)S(1)} collective-permute-done((bf16[4,8,2048]{2,1,0:T(8,128)(2,1)S(1)}, bf16[4,8,2048]{2,1,0:T(8,128)(2,1)S(1)}, u32[]{:S(2)}, u32[]{:S(2)}) %collective-permute-start.1) | collective-permute-done | bytes 131104 | tf_op jit(solution)/shard_map/ppermute | solution.py:434
  13.4 0.7 fusion.3
  14.1 15.3 %gate_conv.1 = (f32[4,1024,256]{2,1,0:T(8,128)}, f32[4,1024,256]{2,1,0:T(8,128)}, f32[4,1040,256]{2,1,0:T(8,128)}, f32[8,2,256]{2,1,0:T(2,128)}) custom-call(s32[2,4]{1,0:T(2,128)} %stack.35.meta, bf16[4,1024,1024]{2,1,0:T(8,128)(2,1)} %x.4, bf16[4,16,1024]{2,1,0:T(8,128)(2,1)} %get-tuple-element.90.halo, bf16[1024,256]{1,0:T(8,128)(2,1)} %wv.1, ...), custom_call_target="tpu_custom_call" | custom-call | flops 4294967296 | bytes 20971520 | tf_op jit(solution)/shard_map/gate_conv/pallas_call | solution.py:448
  29.4 1.1 pad_maximum_fusion
  30.6 0.1 dynamic-slice_bitcast_fusion.1
  30.7 0.1 collective-permute-start.2
  30.8 0.1 iota_add_fusion
  30.9 0.1 add.93
  31.6 0.6 pad_maximum_fusion.5.affine
  32.2 0.9 fusion.select
  33.2 5.7 %all-to-all-start = ((f32[8,2,256]{2,1,0:T(2,128)}), f32[8,2,256]{2,1,0:T(2,128)S(1)}, u32[]{:S(2)}, u32[]{:S(2)}) async-start(f32[8,2,256]{2,1,0:T(2,128)} %get-tuple-element.44), calls=%async_computation | async-start | bytes 32768 | tf_op jit(solution)/shard_map/all_to_all | solution.py:394
  38.9 0.9 pad_maximum_fusion.1
  39.8 5.7 %all-to-all-done.stats = f32[8,2,256]{2,1,0:T(2,128)S(1)} async-done(((f32[8,2,256]{2,1,0:T(2,128)}), f32[8,2,256]{2,1,0:T(2,128)S(1)}, u32[]{:S(2)}, u32[]{:S(2)}) %all-to-all-start) | async-done | bytes 16416 | tf_op jit(solution)/shard_map/all_to_all | solution.py:394
  45.5 0.6 copy-done.5
  46.1 12.1 %swish_norm.1 = (bf16[4,1024,256]{2,1,0:T(8,128)(2,1)}, f32[4,1040,256]{2,1,0:T(8,128)}, bf16[4,256,1024]{2,1,0:T(8,128)(2,1)}, f32[8,2,256]{2,1,0:T(2,128)}) custom-call(s32[2,4]{1,0:T(2,128)} %stack.35.meta, f32[1,1]{1,0:T(1,128)} %bitcast.1.count, f32[8,2,256]{2,1,0:T(2,128)} %copy-done.5, f32[2,256]{1,0:T(2,128)} %pad_maximum_fusion.5.affine, ...), custom_call_target="tpu_custom_call" | custom-call | flops 4294967296 | bytes 20971520 | tf_op jit(solution)/shard_map/swish_norm/pallas_call | solution.py:493
  58.1 3.3 %all-to-all-start.1 = ((f32[8,2,256]{2,1,0:T(2,128)}), f32[8,2,256]{2,1,0:T(2,128)S(1)}, u32[]{:S(2)}, u32[]{:S(2)}) async-start(f32[8,2,256]{2,1,0:T(2,128)} %get-tuple-element.48), calls=%async_computation.1 | async-start | bytes 32768 | tf_op jit(solution)/shard_map/all_to_all | solution.py:394
  61.5 7.0 %outer_w_out.1.w_out = f32[256,1024]{1,0:T(8,128)} custom-call(bf16[4,1024,1024]{2,1,0:T(8,128)(2,1)} %grads.3, bf16[4,1024,256]{2,1,0:T(8,128)(2,1)} %get-tuple-element.52.swished), custom_call_target="tpu_custom_call" | custom-call | flops 2147483648 | bytes 8388608 | tf_op jit(solution)/shard_map/outer_w_out/pallas_call | solution.py:538
  68.5 0.6 copy-done.3
  69.1 8.9 %back_conv.2 = (bf16[2048,512]{1,0:T(8,128)(2,1)}, f32[16,256]{1,0:T(8,128)}) custom-call(s32[2,4]{1,0:T(2,128)} %stack.35.meta, f32[1,1]{1,0:T(1,128)} %bitcast.1.count, f32[8,2,256]{2,1,0:T(2,128)} %copy-done.5, f32[8,2,256]{2,1,0:T(2,128)} %copy-done.3, f32[1,256]{1,0:T(1,128)} %bitcast.25, f32[4,1040,256]{2,1,0:T(8,128)} %get-tuple-element.49.gn, ...), custom_call_target="tpu_custom_call" | custom-call | bytes 1024 | tf_op jit(solution)/shard_map/back_conv/pallas_call | solution.py:562
  78.1 8.9 %back_conv.3 = (bf16[2048,512]{1,0:T(8,128)(2,1)}, f32[16,256]{1,0:T(8,128)}) custom-call(s32[2,4]{1,0:T(2,128)} %stack.35.meta, f32[1,1]{1,0:T(1,128)} %bitcast.1.count, f32[8,2,256]{2,1,0:T(2,128)} %copy-done.5, f32[8,2,256]{2,1,0:T(2,128)} %copy-done.3, f32[1,256]{1,0:T(1,128)} %bitcast.26, f32[4,1040,256]{2,1,0:T(8,128)} %get-tuple-element.49.gn, ...), custom_call_target="tpu_custom_call" | custom-call | bytes 1024 | tf_op jit(solution)/shard_map/back_conv/pallas_call | solution.py:562
  87.0 0.5 collective-permute-start.3
  87.5 6.6 %partial_in.2 = (bf16[8,2,32,1024]{3,2,1,0:T(8,128)(2,1)}, bf16[8,2,32,1024]{3,2,1,0:T(8,128)(2,1)}) custom-call(bf16[2048,512]{1,0:T(8,128)(2,1)} %get-tuple-element.54.own.refs_0_, bf16[2048,512]{1,0:T(8,128)(2,1)} %collective-permute-done.4.sibling, bf16[512,512]{1,0:T(8,128)(2,1)} %bitcast.21, bf16[512,512]{1,0:T(8,128)(2,1)} %copy-done.1, ...), custom_call_target="tpu_custom_call" | custom-call | bytes 1024 | tf_op jit(solution)/shard_map/partial_in/pallas_call | solution.py:591
  94.2 1.5 collective-permute-start.5
  95.7 6.5 %partial_in.3 = (bf16[8,2,32,1024]{3,2,1,0:T(8,128)(2,1)}, bf16[8,2,32,1024]{3,2,1,0:T(8,128)(2,1)}) custom-call(bf16[2048,512]{1,0:T(8,128)(2,1)} %get-tuple-element.56.own.refs_1_, bf16[2048,512]{1,0:T(8,128)(2,1)} %collective-permute-done.3.sibling, bf16[512,512]{1,0:T(8,128)(2,1)} %bitcast.22, bf16[512,512]{1,0:T(8,128)(2,1)} %copy-done.1, ...), custom_call_target="tpu_custom_call" | custom-call | bytes 1024 | tf_op jit(solution)/shard_map/partial_in/pallas_call | solution.py:591
  102.2 10.1 %outer_w_in.1 = (bf16[4,800,128]{2,1,0:T(8,128)(2,1)}, bf16[4,800,128]{2,1,0:T(8,128)(2,1)}) custom-call(s32[1,1]{1,0:T(1,128)} %bitcast.12.parity, bf16[4,1024,1024]{2,1,0:T(8,128)(2,1)} %x.4, f32[256,1024]{1,0:T(8,128)} %outer_w_out.1.w_out, bf16[2048,512]{1,0:T(8,128)(2,1)} %get-tuple-element.54.own.refs_0_, ...), custom_call_target="tpu_custom_call" | custom-call | bytes 1024 | tf_op jit(solution)/shard_map/outer_w_in/pallas_call | solution.py:647
  112.3 7.3 %collective-permute-done.5.refs_1_ = bf16[8,2,32,1024]{3,2,1,0:T(8,128)(2,1)} collective-permute-done((bf16[8,2,32,1024]{3,2,1,0:T(8,128)(2,1)}, bf16[8,2,32,1024]{3,2,1,0:T(8,128)(2,1)}, u32[]{:S(2)}, u32[]{:S(2)}) %collective-permute-start.5) | collective-permute-done | bytes 1048608 | tf_op jit(solution)/shard_map/ppermute | solution.py:620
  119.6 3.6 %add.114 = bf16[8,2,32,1024]{3,2,1,0:T(8,128)(2,1)} custom-call(bf16[8,2,32,1024]{3,2,1,0:T(8,128)(2,1)} %get-tuple-element.68.refs_0_, bf16[8,2,32,1024]{3,2,1,0:T(8,128)(2,1)} %collective-permute-done.5.refs_1_), custom_call_target="tpu_custom_call" | custom-call | flops 49999998976 | bytes 1024 | tf_op jit(solution)/shard_map/add/pallas_call | solution.py:625
  123.3 6.1 %all-to-all-start.2 = ((bf16[8,2,32,1024]{3,2,1,0:T(8,128)(2,1)}), bf16[8,2,32,1024]{3,2,1,0:T(8,128)(2,1)}, u32[]{:S(2)}, u32[]{:S(2)}) async-start(bf16[8,2,32,1024]{3,2,1,0:T(8,128)(2,1)} %add.114), calls=%async_computation.2 | async-start | bytes 2097152 | tf_op jit(solution)/shard_map/all_to_all | solution.py:394
  129.3 2.0 collective-permute-start.6
  131.4 1.5 collective-permute-start.7
  132.8 27.0 %collective-permute-done.6.other = bf16[4,800,128]{2,1,0:T(8,128)(2,1)S(1)} collective-permute-done((bf16[4,800,128]{2,1,0:T(8,128)(2,1)S(1)}, bf16[4,800,128]{2,1,0:T(8,128)(2,1)S(1)}, u32[]{:S(2)}, u32[]{:S(2)}) %collective-permute-start.6) | collective-permute-done | bytes 819232 | tf_op jit(solution)/shard_map/ppermute | solution.py:670
  159.9 1.0 fold.2
  160.8 1.5 collective-permute-start.8
  162.3 3.7 %add.115 = bf16[8,2,32,1024]{3,2,1,0:T(8,128)(2,1)} custom-call(bf16[8,2,32,1024]{3,2,1,0:T(8,128)(2,1)} %get-tuple-element.72.refs_0_, bf16[8,2,32,1024]{3,2,1,0:T(8,128)(2,1)} %collective-permute-done.7.refs_1_), custom_call_target="tpu_custom_call" | custom-call | bytes 1024 | tf_op jit(solution)/shard_map/add/pallas_call | solution.py:625
  166.0 4.6 %collective-permute-done.8.other = bf16[2,800,128]{2,1,0:T(8,128)(2,1)S(1)} collective-permute-done((bf16[2,800,128]{2,1,0:T(8,128)(2,1)}, bf16[2,800,128]{2,1,0:T(8,128)(2,1)S(1)}, u32[]{:S(2)}, u32[]{:S(2)}) %collective-permute-start.8) | collective-permute-done | bytes 409632 | tf_op jit(solution)/shard_map/ppermute | solution.py:670
  170.5 0.1 fold.3
  170.7 6.1 %all-to-all-start.3 = ((bf16[8,2,32,1024]{3,2,1,0:T(8,128)(2,1)}), bf16[8,2,32,1024]{3,2,1,0:T(8,128)(2,1)S(1)}, u32[]{:S(2)}, u32[]{:S(2)}) async-start(bf16[8,2,32,1024]{3,2,1,0:T(8,128)(2,1)} %add.115), calls=%async_computation.3 | async-start | bytes 2097152 | tf_op jit(solution)/shard_map/all_to_all | solution.py:394
  176.8 3.0 %collective-permute-start.9 = (bf16[1,800,128]{2,1,0:T(8,128)(2,1)S(1)}, bf16[1,800,128]{2,1,0:T(8,128)(2,1)S(1)}, u32[]{:S(2)}, u32[]{:S(2)}) collective-permute-start(bf16[1,800,128]{2,1,0:T(8,128)(2,1)S(1)} %get-tuple-element.76), channel_id=1, source_target_pairs={{0,16},{4,20},{8,24},{12,28},{16,0},{20,4},{24,8},{28,12},{1,17},{... | collective-permute-start | bytes 614408 | tf_op jit(solution)/shard_map/ppermute | solution.py:670
  179.8 0.6 fusion.4
  180.4 30.5 %collective-permute-done.9.other = bf16[1,800,128]{2,1,0:T(8,128)(2,1)S(1)} collective-permute-done((bf16[1,800,128]{2,1,0:T(8,128)(2,1)S(1)}, bf16[1,800,128]{2,1,0:T(8,128)(2,1)S(1)}, u32[]{:S(2)}, u32[]{:S(2)}) %collective-permute-start.9) | collective-permute-done | bytes 204832 | tf_op jit(solution)/shard_map/ppermute | solution.py:670
  210.9 0.8 finish.1
  211.8 2.0 place.2.refs_0_
  213.8 1.1 place.3
  (32 shorter events, 0.2 us)
Async XLA Ops:
  1.6 8.1 %collective-permute-start = (bf16[4,8,2048]{2,1,0:T(8,128)(2,1)S(1)}, bf16[4,8,2048]{2,1,0:T(8,128)(2,1)S(1)}, u32[]{:S(2)}, u32[]{:S(2)}) collective-permute-start(bf16[4,8,2048]{2,1,0:T(8,128)(2,1)S(1)} %pad_maximum_fusion.3), channel_id=1, source_target_pairs={{0,4},{4,8},{8,12},{12,16},{16,20},{20,24},{24,28},{1,5},{5,9},{9,... | collective-permute-start | bytes 393224 | tf_op jit(solution)/shard_map/ppermute | solution.py:434
  6.5 6.9 %collective-permute-start.1 = (bf16[4,8,2048]{2,1,0:T(8,128)(2,1)S(1)}, bf16[4,8,2048]{2,1,0:T(8,128)(2,1)S(1)}, u32[]{:S(2)}, u32[]{:S(2)}) collective-permute-start(bf16[4,8,2048]{2,1,0:T(8,128)(2,1)S(1)} %pad_maximum_fusion.4), channel_id=1, source_target_pairs={{4,0},{8,4},{12,8},{16,12},{20,16},{24,20},{28,24},{5,1},{9,5},{13... | collective-permute-start | bytes 393224 | tf_op jit(solution)/shard_map/ppermute | solution.py:434
  14.1 15.3 %copy-start.2 = (bf16[1024,256]{1,0:T(8,128)(2,1)S(1)}, bf16[1024,256]{1,0:T(8,128)(2,1)}, u32[]{:S(2)}) copy-start(bf16[1024,256]{1,0:T(8,128)(2,1)} %wv.1) | copy-start | bytes 1572868
  30.6 1.1 copy-start.6
  30.6 1.1 copy-start.7
  30.7 9.1 %collective-permute-start.2 = (bf16[512,512]{1,0:T(8,128)(2,1)S(1)}, bf16[512,512]{1,0:T(8,128)(2,1)S(1)}, u32[]{:S(2)}, u32[]{:S(2)}) collective-permute-start(bf16[512,512]{1,0:T(8,128)(2,1)S(1)} %bitcast.24), channel_id=1, source_target_pairs={{0,1},{1,0},{2,3},{3,2},{4,5},{5,4},{6,7},{7,6},{8,9},{9,8},{10,11... | collective-permute-start | bytes 1572872 | tf_op jit(solution)/shard_map/ppermute | solution.py:487
  33.2 12.3 %all-to-all-start = ((f32[8,2,256]{2,1,0:T(2,128)}), f32[8,2,256]{2,1,0:T(2,128)S(1)}, u32[]{:S(2)}, u32[]{:S(2)}) async-start(f32[8,2,256]{2,1,0:T(2,128)} %get-tuple-element.44), calls=%async_computation | async-start | bytes 32768 | tf_op jit(solution)/shard_map/all_to_all | solution.py:394
  39.8 18.3 %copy-start.1 = (bf16[512,512]{1,0:T(8,128)(2,1)}, bf16[512,512]{1,0:T(8,128)(2,1)S(1)}, u32[]{:S(2)}) copy-start(bf16[512,512]{1,0:T(8,128)(2,1)S(1)} %collective-permute-done.2.w_sibling) | copy-start | bytes 1572868
  45.5 0.6 copy-start.5
  58.1 10.4 %all-to-all-start.1 = ((f32[8,2,256]{2,1,0:T(2,128)}), f32[8,2,256]{2,1,0:T(2,128)S(1)}, u32[]{:S(2)}, u32[]{:S(2)}) async-start(f32[8,2,256]{2,1,0:T(2,128)} %get-tuple-element.48), calls=%async_computation.1 | async-start | bytes 32768 | tf_op jit(solution)/shard_map/all_to_all | solution.py:394
  68.5 0.6 copy-start.3
  78.0 9.5 %collective-permute-start.4 = (bf16[2048,512]{1,0:T(8,128)(2,1)}, bf16[2048,512]{1,0:T(8,128)(2,1)}, u32[]{:S(2)}, u32[]{:S(2)}) collective-permute-start(bf16[2048,512]{1,0:T(8,128)(2,1)} %get-tuple-element.54.own.refs_0_), channel_id=1, source_target_pairs={{0,1},{1,0},{2,3},{3,2},{4,5},{5,4},{6,7},{7,6},{8,9},{9,8},{10,11... | collective-permute-start | bytes 6291464 | tf_op jit(solution)/shard_map/ppermute | solution.py:589
  87.0 8.6 %collective-permute-start.3 = (bf16[2048,512]{1,0:T(8,128)(2,1)}, bf16[2048,512]{1,0:T(8,128)(2,1)}, u32[]{:S(2)}, u32[]{:S(2)}) collective-permute-start(bf16[2048,512]{1,0:T(8,128)(2,1)} %get-tuple-element.56.own.refs_1_), channel_id=1, source_target_pairs={{0,1},{1,0},{2,3},{3,2},{4,5},{5,4},{6,7},{7,6},{8,9},{9,8},{10,11... | collective-permute-start | bytes 6291464 | tf_op jit(solution)/shard_map/ppermute | solution.py:589
  94.2 25.4 %collective-permute-start.5 = (bf16[8,2,32,1024]{3,2,1,0:T(8,128)(2,1)}, bf16[8,2,32,1024]{3,2,1,0:T(8,128)(2,1)}, u32[]{:S(2)}, u32[]{:S(2)}) collective-permute-start(bf16[8,2,32,1024]{3,2,1,0:T(8,128)(2,1)} %get-tuple-element.60), channel_id=1, source_target_pairs={{0,2},{1,3},{2,0},{3,1},{4,6},{5,7},{6,4},{7,5},{8,10},{9,11},{10,... | collective-permute-start | bytes 3145736 | tf_op jit(solution)/shard_map/ppermute | solution.py:620
  123.3 6.1 %copy-start.8 = (bf16[4,800,128]{2,1,0:T(8,128)(2,1)S(1)}, bf16[4,800,128]{2,1,0:T(8,128)(2,1)}, u32[]{:S(2)}) copy-start(bf16[4,800,128]{2,1,0:T(8,128)(2,1)} %get-tuple-element.70) | copy-start | bytes 2457604
  123.3 36.6 %copy-start = (bf16[4,800,128]{2,1,0:T(8,128)(2,1)S(1)}, bf16[4,800,128]{2,1,0:T(8,128)(2,1)}, u32[]{:S(2)}) copy-start(bf16[4,800,128]{2,1,0:T(8,128)(2,1)} %get-tuple-element.69.own) | copy-start | bytes 2457604
  123.3 47.4 %all-to-all-start.2 = ((bf16[8,2,32,1024]{3,2,1,0:T(8,128)(2,1)}), bf16[8,2,32,1024]{3,2,1,0:T(8,128)(2,1)}, u32[]{:S(2)}, u32[]{:S(2)}) async-start(bf16[8,2,32,1024]{3,2,1,0:T(8,128)(2,1)} %add.114), calls=%async_computation.2 | async-start | bytes 2097152 | tf_op jit(solution)/shard_map/all_to_all | solution.py:394
  129.3 30.5 %collective-permute-start.6 = (bf16[4,800,128]{2,1,0:T(8,128)(2,1)S(1)}, bf16[4,800,128]{2,1,0:T(8,128)(2,1)S(1)}, u32[]{:S(2)}, u32[]{:S(2)}) collective-permute-start(bf16[4,800,128]{2,1,0:T(8,128)(2,1)S(1)} %copy-done.8), channel_id=1, source_target_pairs={{0,4},{4,0},{8,12},{12,8},{16,20},{20,16},{24,28},{28,24},{1,5},{5... | collective-permute-start | bytes 2457608 | tf_op jit(solution)/shard_map/ppermute | solution.py:670
  131.4 30.9 %collective-permute-start.7 = (bf16[8,2,32,1024]{3,2,1,0:T(8,128)(2,1)}, bf16[8,2,32,1024]{3,2,1,0:T(8,128)(2,1)}, u32[]{:S(2)}, u32[]{:S(2)}) collective-permute-start(bf16[8,2,32,1024]{3,2,1,0:T(8,128)(2,1)} %get-tuple-element.63), channel_id=1, source_target_pairs={{0,2},{1,3},{2,0},{3,1},{4,6},{5,7},{6,4},{7,5},{8,10},{9,11},{10,... | collective-permute-start | bytes 3145736 | tf_op jit(solution)/shard_map/ppermute | solution.py:620
  160.8 9.7 %collective-permute-start.8 = (bf16[2,800,128]{2,1,0:T(8,128)(2,1)}, bf16[2,800,128]{2,1,0:T(8,128)(2,1)S(1)}, u32[]{:S(2)}, u32[]{:S(2)}) collective-permute-start(bf16[2,800,128]{2,1,0:T(8,128)(2,1)} %get-tuple-element.73), channel_id=1, source_target_pairs={{0,8},{4,12},{8,0},{12,4},{16,24},{20,28},{24,16},{28,20},{1,9},{5... | collective-permute-start | bytes 1228808 | tf_op jit(solution)/shard_map/ppermute | solution.py:670
  166.0 10.8 %copy-start.4 = (f32[8,2,256]{2,1,0:T(2,128)S(1)}, f32[8,2,256]{2,1,0:T(2,128)}, u32[]{:S(2)}) copy-start(f32[8,2,256]{2,1,0:T(2,128)} %copy-done.3) | copy-start | bytes 49156
  170.7 43.1 %all-to-all-start.3 = ((bf16[8,2,32,1024]{3,2,1,0:T(8,128)(2,1)}), bf16[8,2,32,1024]{3,2,1,0:T(8,128)(2,1)S(1)}, u32[]{:S(2)}, u32[]{:S(2)}) async-start(bf16[8,2,32,1024]{3,2,1,0:T(8,128)(2,1)} %add.115), calls=%async_computation.3 | async-start | bytes 2097152 | tf_op jit(solution)/shard_map/all_to_all | solution.py:394
  176.8 34.1 %collective-permute-start.9 = (bf16[1,800,128]{2,1,0:T(8,128)(2,1)S(1)}, bf16[1,800,128]{2,1,0:T(8,128)(2,1)S(1)}, u32[]{:S(2)}, u32[]{:S(2)}) collective-permute-start(bf16[1,800,128]{2,1,0:T(8,128)(2,1)S(1)} %get-tuple-element.76), channel_id=1, source_target_pairs={{0,16},{4,20},{8,24},{12,28},{16,0},{20,4},{24,8},{28,12},{1,17},{... | collective-permute-start | bytes 614408 | tf_op jit(solution)/shard_map/ppermute | solution.py:670

commit v15 on v11

--- a/solution.py
+++ b/solution.py
@@ -153,6 +153,16 @@
         spread_sums(st_o, st[...])
 
 
+def swish_kernel(grads, halo, wo, sw_o):
+    frames = grads.shape[1]
+    edge = dot(halo[0], wo[...])
+    sw_o[0, :EDGE, :] = edge[:EDGE]
+    sw_o[0, EDGE + frames :, :] = edge[EDGE:]
+    step = block_rows(frames, 512)
+    for base in range(0, frames, step):
+        sw_o[0, EDGE + base : EDGE + base + step, :] = dot(grads[0, base : base + step, :], wo[...])
+
+
 def batch_norm(stats, count):
     sums = jnp.sum(stats[...], axis=0)
     centre = sums[0:1] / count
@@ -161,8 +171,7 @@
 
 
 def norm_kernel(
-    meta, count, stats, affine, select, grads, halo, wo, conv,
-    swished_o, gn_o, picked_o, st_o, st, ping, pong
+    meta, count, stats, affine, select, grads, sw, conv, swished_o, gn_o, picked_o, st_o, st
 ):
     r = pl.program_id(0)
     hi = meta[0, r]
@@ -171,37 +180,31 @@
     centre, inv = batch_norm(stats, count[0, 0])
     gain, shift = affine[0:1, :], affine[1:2, :]
 
-    def part(row, swish_grad):
-        size = swish_grad.shape[0]
+    def part(row, size):
         unit = (conv[0, pl.ds(row, size), :] - centre) * inv
         normalized = unit * gain + shift
         s = sigmoid(normalized)
         pos = rows_of(size, row - EDGE)
         keep = (pos >= lo) & (pos < hi)
         swished = jnp.where(keep, normalized * s, 0.0)
+        swish_grad = sw[0, pl.ds(row, size), :]
         gn = jnp.where(keep, swish_grad, 0.0) * (s + normalized * (s - s * s))
         gn_o[0, pl.ds(row, size), :] = gn
         return unit, swished, gn
 
-    edge = dot(halo[0], wo[...])
-    part(0, edge[:EDGE])
-    part(frames + EDGE, edge[EDGE:])
+    part(0, EDGE)
+    part(frames + EDGE, EDGE)
     step = block_rows(frames, 512)
     small = block_rows(step, 32)
     s1 = jnp.zeros((8, conv.shape[2]), F32)
     s2 = s1
-    held = (ping, pong)
-    ping[...] = dot(grads[0, :step, :], wo[...])
     for i in range(frames // step):
-        now = held[i % 2]
-        if (i + 1) * step < frames:
-            held[(i + 1) % 2][...] = dot(grads[0, (i + 1) * step : (i + 2) * step, :], wo[...])
         picked_o[0, :, i * step : (i + 1) * step] = dot_nt(
             select[...], grads[0, i * step : (i + 1) * step, :]
         ).astype(BF16)
         for j in range(step // small):
             base = i * step + j * small
-            unit, swished, gn = part(base + EDGE, now[j * small : (j + 1) * small, :])
+            unit, swished, gn = part(base + EDGE, small)
             swished_o[0, base : base + small, :] = swished.astype(BF16)
             s1 = s1 + fold_rows(gn)
             s2 = s2 + fold_rows(gn * unit)
@@ -490,9 +493,21 @@
 
     chunk = block_rows(frames, 256)
     half_rows = block_rows(frames, 512)
+    sw = call(
+        swish_kernel,
+        "swish_grad",
+        (recs,),
+        [per_record((frames, model)), per_record((2 * EDGE, model)), whole((model, width))],
+        per_record((span, width)),
+        sds((recs, span, width), F32),
+        [],
+        matmul,
+        input_bytes + array_bytes,
+    )(grad_out, halo_g, after(out_weight, w_own))
+
     swished, gn, picked, sums = call(
         norm_kernel,
-        "swish_norm",
+        "norm",
         (recs,),
         [
             smem(),
@@ -501,8 +516,7 @@
             whole((2, width)),
             whole((rows, model)),
             per_record((frames, model)),
-            per_record((2 * EDGE, model)),
-            whole((model, width)),
+            per_record((span, width)),
             per_record((span, width)),
         ],
         [
@@ -517,12 +531,8 @@
             sds((recs, rows, frames), BF16),
             sds((seqs, 2, width), F32),
         ],
-        [
-            pltpu.VMEM((2, width), F32),
-            pltpu.VMEM((block_rows(frames, 512), width), F32),
-            pltpu.VMEM((block_rows(frames, 512), width), F32),
-        ],
-        2 * matmul,
+        [pltpu.VMEM((2, width), F32)],
+        matmul,
         input_bytes + 3 * array_bytes,
     )(
         meta,
@@ -531,8 +541,7 @@
         jnp.stack([norm_gain, norm_shift]),
         after(select, w_own, w_sibling),
         grad_out,
-        halo_g,
-        out_weight,
+        sw,
         conv,
     )
     w_out = call(
@@ -648,6 +657,7 @@
     parts[1] = partials(*groups[1], grads[1], grads[2])
     owns[0] = deliver(parts[0], LONG, *parts[1])
     moved[0] = exchange(owns[0], "seq")
+    parts[2] = partials(*groups[2], grads[2], owns[0])
 
     slots = 3 * width + 16 * (width // shard)
     half = sds((seqs // 2, slots, shard), BF16)
@@ -669,10 +679,9 @@
         [pltpu.VMEM((2 * width, model), F32)],
         LONG,
         1024,
-    )(parity, after(normed, owns[0]), w_out, *grads, *taps)
+    )(parity, after(normed, *parts[2]), w_out, *grads, *taps)
     owns[1] = deliver(parts[1], LONG, keep)
     moved[1] = exchange(after(owns[1], moved[0]), "seq")
-    parts[2] = partials(*groups[2], grads[2], owns[1])
     bit = 1
     while True:
         others = lax.ppermute(send, "seq", [(i, i ^ bit) for i in range(seqs)])
@@ -680,7 +689,7 @@
         if bit == seqs:
             break
         if bit == 2:
-            keep = after(keep, *parts[2])
+            keep = after(keep, owns[1])
         shape = (keep.shape[0] // 2,) + keep.shape[1:]
         side = ((seq_at // bit) % 2).astype(jnp.int32).reshape(1, 1)
         keep, send = call(
@@ -691,13 +700,14 @@
             [whole(shape)] * 2,
             [sds(shape, BF16)] * 2,
             [],
-            LONG if bit == 2 else 0,
+            0,
             1024,
             vmem=20,
         )(side, keep, others)
+        if bit == 2:
+            owns[2] = deliver(parts[2], 0, keep)
         if bit == min(4, seqs // 2):
-            owns[2] = deliver(parts[2], 0, keep, moved[1])
-            moved[2] = exchange(owns[2], "seq")
+            moved[2] = exchange(after(owns[2], moved[1], keep), "seq")
     w_value, w_gate, w_out, grad_taps = call(
         functools.partial(finish_kernel, kernel),
         "finish",

time: 204 us -> 210 us (1.029)
  Pallas kernels: 92.3 us -> 102 us
  waiting for transfers between devices: 55.1 us -> 47.9 us
  starting transfers between devices: 42.4 us -> 44.7 us
    pallas_call x1 -> x2, Pallas kernels: 12.1 us -> 20.1 us  [the longest x1 12.7 us: per_device(): call(norm_kernel, 'norm', (recs,), [smem(), smem(), whole((seqs, 2, width...]
    all_to_all x5, waiting for transfers between devices: 6.33 us -> 0.01 us  [exchange(): return lax.all_to_all(copies, axis, 0, 0, tiled=True)]
    all_to_all x5, starting transfers between devices: 24.8 us -> 27.7 us  [exchange(): return lax.all_to_all(copies, axis, 0, 0, tiled=True)]
    ppermute x3, waiting for transfers between devices: 43.8 us -> 46.3 us  [per_device(): others = lax.ppermute(send, 'seq', [(i, i ^ bit) for i in range(seqs)])]
    ppermute x1, waiting for transfers between devices: 3.67 us -> 1.56 us  [per_device(): lax.ppermute(high_edge, 'seq', down)]
  transfers between devices with their start and end apart: 17 -> 17, of which waited for: 7 -> 4; matrix products, arithmetic and copies ran while one was open for 2% -> 3% of each run, Pallas kernels for 27% -> 33%
where the time goes in v15:
time: 210 us; the launch traced here: 209 us
  Pallas kernels  102 us (49%)
  waiting for transfers between devices  47.9 us (23%)
  starting transfers between devices  44.7 us (21%)
  other arithmetic  6.49 us (3%)
  local copies, waits for them, and re-layouts  6.2 us (3%)
    ppermute x3, waiting for transfers between devices, per_device(): others = lax.ppermute(send, 'seq', [(i, i ^ bit) for i in range(seqs)])  46.3 us
    all_to_all x5, starting transfers between devices, exchange(): return lax.all_to_all(copies, axis, 0, 0, tiled=True)  27.7 us
    pallas_call x3, Pallas kernels, back(): call(functools.partial(back_kernel, first, blocks), 'back_conv', (size *...  19 us
    pallas_call x1, Pallas kernels, per_device(): call(gate_kernel, 'gate_conv', (recs,), [smem(), per_record((frames, mode...  15.3 us
    pallas_call x3, Pallas kernels, partials(): call(partial_kernel, 'partial_in', (size * parts_in,), [pl.BlockSpec((hal...  15 us
    pallas_call x1, Pallas kernels, per_device(): call(norm_kernel, 'norm', (recs,), [smem(), smem(), whole((seqs, 2, width...  12.7 us
    pallas_call x1, Pallas kernels, per_device(): call(functools.partial(outer_kernel, groups), 'outer_w_in', (recs,), [sme...  10.2 us
    pallas_call x3, Pallas kernels, deliver(): call(add_kernel, 'add', (size * parts_in,), [block] * chips, block, sds(p...  7.64 us
  transfers between devices with their start and end apart: 17, of which 4 were waited for; matrix products, arithmetic and copies ran while one was open for 3% of the time, Pallas kernels for 33%

profile of v15, /device:TPU:0, one launch (start us, length us, event | category | flops | bytes accessed | tf_op | source)
XLA Modules:
  0.0 208.8 jit_solution(10104076964347893722)
XLA Ops:
  0.6 1.0 fusion.1
  1.6 4.9 %collective-permute-start = (bf16[4,8,2048]{2,1,0:T(8,128)(2,1)S(1)}, bf16[4,8,2048]{2,1,0:T(8,128)(2,1)S(1)}, u32[]{:S(2)}, u32[]{:S(2)}) collective-permute-start(bf16[4,8,2048]{2,1,0:T(8,128)(2,1)S(1)} %pad_maximum_fusion.3), channel_id=1, source_target_pairs={{0,4},{4,8},{8,12},{12,16},{16,20},{20,24},{24,28},{1,5},{5,9},{9,... | collective-permute-start | bytes 393224 | tf_op jit(solution)/shard_map/ppermute | solution.py:437
  6.5 1.3 collective-permute-start.1
  7.9 1.3 fusion.5
  10.5 1.3 pad_maximum_fusion.5.affine
  11.8 1.6 collective-permute-done.1
  13.4 0.7 fusion.3
  14.1 15.3 %gate_conv.1 = (f32[4,1024,256]{2,1,0:T(8,128)}, f32[4,1024,256]{2,1,0:T(8,128)}, f32[4,1040,256]{2,1,0:T(8,128)}, f32[8,2,256]{2,1,0:T(2,128)}) custom-call(s32[2,4]{1,0:T(2,128)} %stack.35.meta, bf16[4,1024,1024]{2,1,0:T(8,128)(2,1)} %x.4, bf16[4,16,1024]{2,1,0:T(8,128)(2,1)} %get-tuple-element.108.halo, bf16[1024,256]{1,0:T(8,128)(2,1)} %wv.1, ...), custom_call_target="tpu_custom_call" | custom-call | flops 4294967296 | bytes 20971520 | tf_op jit(solution)/shard_map/gate_conv/pallas_call | solution.py:451
  29.4 1.1 pad_maximum_fusion
  30.7 0.8 pad_maximum_fusion.2
  31.5 1.0 fusion.select
  32.5 5.7 %all-to-all-start = ((f32[8,2,256]{2,1,0:T(2,128)}), f32[8,2,256]{2,1,0:T(2,128)S(1)}, u32[]{:S(2)}, u32[]{:S(2)}) async-start(f32[8,2,256]{2,1,0:T(2,128)} %get-tuple-element.53), calls=%async_computation | async-start | bytes 32768 | tf_op jit(solution)/shard_map/all_to_all | solution.py:397
  38.2 0.9 pad_maximum_fusion.1
  39.1 7.4 %swish_grad.1.sw = f32[4,1040,256]{2,1,0:T(8,128)} custom-call(bf16[4,1024,1024]{2,1,0:T(8,128)(2,1)} %grads.5, bf16[4,16,1024]{2,1,0:T(8,128)(2,1)} %get-tuple-element.107.halo, bf16[1024,256]{1,0:T(8,128)(2,1)} %wo), custom_call_target="tpu_custom_call" | custom-call | flops 2147483648 | bytes 12582912 | tf_op jit(solution)/shard_map/swish_grad/pallas_call | solution.py:496
  46.5 0.7 copy-done.3
  47.2 12.7 %norm.1 = (bf16[4,1024,256]{2,1,0:T(8,128)(2,1)}, f32[4,1040,256]{2,1,0:T(8,128)}, bf16[4,256,1024]{2,1,0:T(8,128)(2,1)}, f32[8,2,256]{2,1,0:T(2,128)}) custom-call(s32[2,4]{1,0:T(2,128)} %stack.35.meta, f32[1,1]{1,0:T(1,128)} %bitcast.1.count, f32[8,2,256]{2,1,0:T(2,128)} %copy-done.3, f32[2,256]{1,0:T(2,128)} %pad_maximum_fusion.5.affine, ...), custom_call_target="tpu_custom_call" | custom-call | flops 2147483648 | bytes 20971520 | tf_op jit(solution)/shard_map/norm/pallas_call | solution.py:508
  59.8 6.0 %all-to-all-start.1 = ((f32[8,2,256]{2,1,0:T(2,128)}), f32[8,2,256]{2,1,0:T(2,128)S(1)}, u32[]{:S(2)}, u32[]{:S(2)}) async-start(f32[8,2,256]{2,1,0:T(2,128)} %get-tuple-element.58), calls=%async_computation.1 | async-start | bytes 32768 | tf_op jit(solution)/shard_map/all_to_all | solution.py:397
  65.9 7.0 %outer_w_out.1.w_out = f32[256,1024]{1,0:T(8,128)} custom-call(bf16[4,1024,1024]{2,1,0:T(8,128)(2,1)} %grads.5, bf16[4,1024,256]{2,1,0:T(8,128)(2,1)} %get-tuple-element.62.swished), custom_call_target="tpu_custom_call" | custom-call | flops 2147483648 | bytes 8388608 | tf_op jit(solution)/shard_map/outer_w_out/pallas_call | solution.py:547
  72.9 0.6 copy-done.4
  73.5 5.0 %back_conv.3 = (bf16[1024,512]{1,0:T(8,128)(2,1)}, f32[16,256]{1,0:T(8,128)}) custom-call(s32[2,4]{1,0:T(2,128)} %stack.35.meta, f32[1,1]{1,0:T(1,128)} %bitcast.1.count, f32[8,2,256]{2,1,0:T(2,128)} %copy-done.3, f32[8,2,256]{2,1,0:T(2,128)} %copy-done.4, f32[1,256]{1,0:T(1,128)} %bitcast.26, f32[4,1040,256]{2,1,0:T(8,128)} %get-tuple-element.59.gn, ...), custom_call_target="tpu_custom_call" | custom-call | bytes 1024 | tf_op jit(solution)/shard_map/back_conv/pallas_call | solution.py:571
  78.6 5.1 %back_conv.4 = (bf16[1024,512]{1,0:T(8,128)(2,1)}, f32[16,256]{1,0:T(8,128)}) custom-call(s32[2,4]{1,0:T(2,128)} %stack.35.meta, f32[1,1]{1,0:T(1,128)} %bitcast.1.count, f32[8,2,256]{2,1,0:T(2,128)} %copy-done.3, f32[8,2,256]{2,1,0:T(2,128)} %copy-done.4, f32[1,256]{1,0:T(1,128)} %bitcast.27, f32[4,1040,256]{2,1,0:T(8,128)} %get-tuple-element.59.gn, ...), custom_call_target="tpu_custom_call" | custom-call | bytes 1024 | tf_op jit(solution)/shard_map/back_conv/pallas_call | solution.py:571
  84.1 4.2 %partial_in.3 = (bf16[8,1,32,1024]{3,2,1,0:T(8,128)(2,1)}, bf16[8,1,32,1024]{3,2,1,0:T(8,128)(2,1)}) custom-call(bf16[1024,512]{1,0:T(8,128)(2,1)} %get-tuple-element.64.own.refs_0_, bf16[1024,512]{1,0:T(8,128)(2,1)} %collective-permute-done.3.sibling, bf16[512,512]{1,0:T(8,128)(2,1)} %bitcast.21, bf16[512,512]{1,0:T(8,128)(2,1)} %copy-done.1, ...), custom_call_target="tpu_custom_call" | custom-call | bytes 1024 | tf_op jit(solution)/shard_map/partial_in/pallas_call | solution.py:600
  88.4 1.5 collective-permute-start.6
  89.9 8.9 %back_conv.5 = (bf16[2048,512]{1,0:T(8,128)(2,1)}, f32[16,256]{1,0:T(8,128)}) custom-call(s32[2,4]{1,0:T(2,128)} %stack.35.meta, f32[1,1]{1,0:T(1,128)} %bitcast.1.count, f32[8,2,256]{2,1,0:T(2,128)} %copy-done.3, f32[8,2,256]{2,1,0:T(2,128)} %copy-done.4, f32[1,256]{1,0:T(1,128)} %bitcast.28, f32[4,1040,256]{2,1,0:T(8,128)} %get-tuple-element.59.gn, ...), custom_call_target="tpu_custom_call" | custom-call | bytes 1024 | tf_op jit(solution)/shard_map/back_conv/pallas_call | solution.py:571
  98.9 4.3 %partial_in.4 = (bf16[8,1,32,1024]{3,2,1,0:T(8,128)(2,1)}, bf16[8,1,32,1024]{3,2,1,0:T(8,128)(2,1)}) custom-call(bf16[1024,512]{1,0:T(8,128)(2,1)} %get-tuple-element.66.own.refs_1_, bf16[1024,512]{1,0:T(8,128)(2,1)} %collective-permute-done.5.sibling, bf16[512,512]{1,0:T(8,128)(2,1)} %bitcast.22, bf16[512,512]{1,0:T(8,128)(2,1)} %copy-done.1, ...), custom_call_target="tpu_custom_call" | custom-call | bytes 1024 | tf_op jit(solution)/shard_map/partial_in/pallas_call | solution.py:600
  103.6 0.8 copy-done.6
  104.4 2.0 add.115
  106.4 6.0 %all-to-all-start.2 = ((bf16[8,1,32,1024]{3,2,1,0:T(8,128)(2,1)}), bf16[8,1,32,1024]{3,2,1,0:T(8,128)(2,1)S(1)}, u32[]{:S(2)}, u32[]{:S(2)}) async-start(bf16[8,1,32,1024]{3,2,1,0:T(8,128)(2,1)} %add.115), calls=%async_computation.2 | async-start | bytes 1048576 | tf_op jit(solution)/shard_map/all_to_all | solution.py:397
  112.4 6.5 %partial_in.5 = (bf16[8,2,32,1024]{3,2,1,0:T(8,128)(2,1)}, bf16[8,2,32,1024]{3,2,1,0:T(8,128)(2,1)}) custom-call(bf16[2048,512]{1,0:T(8,128)(2,1)} %get-tuple-element.72.own.refs_2_, bf16[2048,512]{1,0:T(8,128)(2,1)} %collective-permute-done.4.sibling, bf16[512,512]{1,0:T(8,128)(2,1)} %bitcast.23, bf16[512,512]{1,0:T(8,128)(2,1)} %copy-done.1, ...), custom_call_target="tpu_custom_call" | custom-call | bytes 1024 | tf_op jit(solution)/shard_map/partial_in/pallas_call | solution.py:600
  118.9 1.5 collective-permute-start.9
  120.4 10.2 %outer_w_in.1 = (bf16[4,800,128]{2,1,0:T(8,128)(2,1)}, bf16[4,800,128]{2,1,0:T(8,128)(2,1)}) custom-call(s32[1,1]{1,0:T(1,128)} %bitcast.12.parity, bf16[4,1024,1024]{2,1,0:T(8,128)(2,1)} %x.4, f32[256,1024]{1,0:T(8,128)} %outer_w_out.1.w_out, bf16[1024,512]{1,0:T(8,128)(2,1)} %get-tuple-element.64.own.refs_0_, ...), custom_call_target="tpu_custom_call" | custom-call | flops 49999998976 | bytes 1024 | tf_op jit(solution)/shard_map/outer_w_in/pallas_call | solution.py:664
  130.6 2.0 collective-permute-start.8
  132.6 2.0 add.116
  134.6 4.5 %all-to-all-start.3 = ((bf16[8,1,32,1024]{3,2,1,0:T(8,128)(2,1)}), bf16[8,1,32,1024]{3,2,1,0:T(8,128)(2,1)}, u32[]{:S(2)}, u32[]{:S(2)}) async-start(bf16[8,1,32,1024]{3,2,1,0:T(8,128)(2,1)} %add.116), calls=%async_computation.3 | async-start | bytes 1048576 | tf_op jit(solution)/shard_map/all_to_all | solution.py:397
  139.1 16.5 %collective-permute-done.8.other = bf16[4,800,128]{2,1,0:T(8,128)(2,1)} collective-permute-done((bf16[4,800,128]{2,1,0:T(8,128)(2,1)}, bf16[4,800,128]{2,1,0:T(8,128)(2,1)}, u32[]{:S(2)}, u32[]{:S(2)}) %collective-permute-start.8) | collective-permute-done | bytes 819232 | tf_op jit(solution)/shard_map/ppermute | solution.py:687
  155.6 1.1 copy-done
  156.8 2.1 %fold.2 = (bf16[2,800,128]{2,1,0:T(8,128)(2,1)S(1)}, bf16[2,800,128]{2,1,0:T(8,128)(2,1)}) custom-call(s32[1,1]{1,0:T(1,128)} %bitcast.11.parity, bf16[4,800,128]{2,1,0:T(8,128)(2,1)S(1)} %copy-done, bf16[4,800,128]{2,1,0:T(8,128)(2,1)} %collective-permute-done.8.other), custom_call_target="tpu_custom_call" | custom-call | bytes 1024 | tf_op jit(solution)/shard_map/fold/pallas_call | solution.py:695
  158.9 1.7 collective-permute-start.10
  160.6 3.7 %add.117 = bf16[8,2,32,1024]{3,2,1,0:T(8,128)(2,1)} custom-call(bf16[8,2,32,1024]{3,2,1,0:T(8,128)(2,1)} %get-tuple-element.89.refs_0_, bf16[8,2,32,1024]{3,2,1,0:T(8,128)(2,1)} %collective-permute-done.9.refs_1_), custom_call_target="tpu_custom_call" | custom-call | bytes 1024 | tf_op jit(solution)/shard_map/add/pallas_call | solution.py:634
  164.3 4.3 %collective-permute-done.10.other = bf16[2,800,128]{2,1,0:T(8,128)(2,1)} collective-permute-done((bf16[2,800,128]{2,1,0:T(8,128)(2,1)}, bf16[2,800,128]{2,1,0:T(8,128)(2,1)}, u32[]{:S(2)}, u32[]{:S(2)}) %collective-permute-start.10) | collective-permute-done | bytes 409632 | tf_op jit(solution)/shard_map/ppermute | solution.py:687
  168.6 1.1 fold.3
  169.7 5.4 %all-to-all-start.4 = ((bf16[8,2,32,1024]{3,2,1,0:T(8,128)(2,1)}), bf16[8,2,32,1024]{3,2,1,0:T(8,128)(2,1)S(1)}, u32[]{:S(2)}, u32[]{:S(2)}) async-start(bf16[8,2,32,1024]{3,2,1,0:T(8,128)(2,1)} %add.117), calls=%async_computation.4 | async-start | bytes 2097152 | tf_op jit(solution)/shard_map/all_to_all | solution.py:397
  175.1 3.0 %collective-permute-start.11 = (bf16[1,800,128]{2,1,0:T(8,128)(2,1)S(1)}, bf16[1,800,128]{2,1,0:T(8,128)(2,1)S(1)}, u32[]{:S(2)}, u32[]{:S(2)}) collective-permute-start(bf16[1,800,128]{2,1,0:T(8,128)(2,1)S(1)} %get-tuple-element.94), channel_id=1, source_target_pairs={{0,16},{4,20},{8,24},{12,28},{16,0},{20,4},{24,8},{28,12},{1,17},{... | collective-permute-start | bytes 614408 | tf_op jit(solution)/shard_map/ppermute | solution.py:687
  178.7 0.8 place.3.refs_0_
  179.5 1.9 place.4.refs_0_
  181.4 25.5 %collective-permute-done.11.other = bf16[1,800,128]{2,1,0:T(8,128)(2,1)S(1)} collective-permute-done((bf16[1,800,128]{2,1,0:T(8,128)(2,1)S(1)}, bf16[1,800,128]{2,1,0:T(8,128)(2,1)S(1)}, u32[]{:S(2)}, u32[]{:S(2)}) %collective-permute-start.11) | collective-permute-done | bytes 204832 | tf_op jit(solution)/shard_map/ppermute | solution.py:687
  206.9 0.8 finish.1
  207.7 1.1 place.5
  (39 shorter events, 2.7 us)
Async XLA Ops:
  1.6 10.2 %collective-permute-start = (bf16[4,8,2048]{2,1,0:T(8,128)(2,1)S(1)}, bf16[4,8,2048]{2,1,0:T(8,128)(2,1)S(1)}, u32[]{:S(2)}, u32[]{:S(2)}) collective-permute-start(bf16[4,8,2048]{2,1,0:T(8,128)(2,1)S(1)} %pad_maximum_fusion.3), channel_id=1, source_target_pairs={{0,4},{4,8},{8,12},{12,16},{16,20},{20,24},{24,28},{1,5},{5,9},{9,... | collective-permute-start | bytes 393224 | tf_op jit(solution)/shard_map/ppermute | solution.py:437
  6.5 6.9 %collective-permute-start.1 = (bf16[4,8,2048]{2,1,0:T(8,128)(2,1)S(1)}, bf16[4,8,2048]{2,1,0:T(8,128)(2,1)S(1)}, u32[]{:S(2)}, u32[]{:S(2)}) collective-permute-start(bf16[4,8,2048]{2,1,0:T(8,128)(2,1)S(1)} %pad_maximum_fusion.4), channel_id=1, source_target_pairs={{4,0},{8,4},{12,8},{16,12},{20,16},{24,20},{28,24},{5,1},{9,5},{13... | collective-permute-start | bytes 393224 | tf_op jit(solution)/shard_map/ppermute | solution.py:437
  14.1 15.3 %copy-start.2 = (bf16[1024,256]{1,0:T(8,128)(2,1)S(1)}, bf16[1024,256]{1,0:T(8,128)(2,1)}, u32[]{:S(2)}) copy-start(bf16[1024,256]{1,0:T(8,128)(2,1)} %wv.1) | copy-start | bytes 1572868
  31.5 15.0 %collective-permute-start.2 = (bf16[512,512]{1,0:T(8,128)(2,1)}, bf16[512,512]{1,0:T(8,128)(2,1)S(1)}, u32[]{:S(2)}, u32[]{:S(2)}) collective-permute-start(bf16[512,512]{1,0:T(8,128)(2,1)} %bitcast.10), channel_id=1, source_target_pairs={{0,1},{1,0},{2,3},{3,2},{4,5},{5,4},{6,7},{7,6},{8,9},{9,8},{10,11... | collective-permute-start | bytes 1572872 | tf_op jit(solution)/shard_map/ppermute | solution.py:490
  32.5 14.0 %all-to-all-start = ((f32[8,2,256]{2,1,0:T(2,128)}), f32[8,2,256]{2,1,0:T(2,128)S(1)}, u32[]{:S(2)}, u32[]{:S(2)}) async-start(f32[8,2,256]{2,1,0:T(2,128)} %get-tuple-element.53), calls=%async_computation | async-start | bytes 32768 | tf_op jit(solution)/shard_map/all_to_all | solution.py:397
  46.5 13.3 %copy-start.1 = (bf16[512,512]{1,0:T(8,128)(2,1)}, bf16[512,512]{1,0:T(8,128)(2,1)S(1)}, u32[]{:S(2)}) copy-start(bf16[512,512]{1,0:T(8,128)(2,1)S(1)} %collective-permute-done.2.w_sibling) | copy-start | bytes 1572868
  46.5 0.7 copy-start.3
  59.8 13.0 %all-to-all-start.1 = ((f32[8,2,256]{2,1,0:T(2,128)}), f32[8,2,256]{2,1,0:T(2,128)S(1)}, u32[]{:S(2)}, u32[]{:S(2)}) async-start(f32[8,2,256]{2,1,0:T(2,128)} %get-tuple-element.58), calls=%async_computation.1 | async-start | bytes 32768 | tf_op jit(solution)/shard_map/all_to_all | solution.py:397
  72.9 0.6 copy-start.4
  78.5 5.7 %collective-permute-start.3 = (bf16[1024,512]{1,0:T(8,128)(2,1)}, bf16[1024,512]{1,0:T(8,128)(2,1)}, u32[]{:S(2)}, u32[]{:S(2)}) collective-permute-start(bf16[1024,512]{1,0:T(8,128)(2,1)} %get-tuple-element.64.own.refs_0_), channel_id=1, source_target_pairs={{0,1},{1,0},{2,3},{3,2},{4,5},{5,4},{6,7},{7,6},{8,9},{9,8},{10,11... | collective-permute-start | bytes 3145736 | tf_op jit(solution)/shard_map/ppermute | solution.py:598
  83.6 15.2 %collective-permute-start.5 = (bf16[1024,512]{1,0:T(8,128)(2,1)}, bf16[1024,512]{1,0:T(8,128)(2,1)}, u32[]{:S(2)}, u32[]{:S(2)}) collective-permute-start(bf16[1024,512]{1,0:T(8,128)(2,1)} %get-tuple-element.66.own.refs_1_), channel_id=1, source_target_pairs={{0,1},{1,0},{2,3},{3,2},{4,5},{5,4},{6,7},{7,6},{8,9},{9,8},{10,11... | collective-permute-start | bytes 3145736 | tf_op jit(solution)/shard_map/ppermute | solution.py:598
  88.4 15.3 %collective-permute-start.6 = (bf16[8,1,32,1024]{3,2,1,0:T(8,128)(2,1)}, bf16[8,1,32,1024]{3,2,1,0:T(8,128)(2,1)S(1)}, u32[]{:S(2)}, u32[]{:S(2)}) collective-permute-start(bf16[8,1,32,1024]{3,2,1,0:T(8,128)(2,1)} %get-tuple-element.70), channel_id=1, source_target_pairs={{0,2},{1,3},{2,0},{3,1},{4,6},{5,7},{6,4},{7,5},{8,10},{9,11},{10,... | collective-permute-start | bytes 1572872 | tf_op jit(solution)/shard_map/ppermute | solution.py:629
  98.8 13.6 %collective-permute-start.4 = (bf16[2048,512]{1,0:T(8,128)(2,1)}, bf16[2048,512]{1,0:T(8,128)(2,1)}, u32[]{:S(2)}, u32[]{:S(2)}) collective-permute-start(bf16[2048,512]{1,0:T(8,128)(2,1)} %get-tuple-element.72.own.refs_2_), channel_id=1, source_target_pairs={{0,1},{1,0},{2,3},{3,2},{4,5},{5,4},{6,7},{7,6},{8,9},{9,8},{10,11... | collective-permute-start | bytes 6291464 | tf_op jit(solution)/shard_map/ppermute | solution.py:598
  103.1 29.5 %collective-permute-start.7 = (bf16[8,1,32,1024]{3,2,1,0:T(8,128)(2,1)}, bf16[8,1,32,1024]{3,2,1,0:T(8,128)(2,1)}, u32[]{:S(2)}, u32[]{:S(2)}) collective-permute-start(bf16[8,1,32,1024]{3,2,1,0:T(8,128)(2,1)} %get-tuple-element.75), channel_id=1, source_target_pairs={{0,2},{1,3},{2,0},{3,1},{4,6},{5,7},{6,4},{7,5},{8,10},{9,11},{10,... | collective-permute-start | bytes 1572872 | tf_op jit(solution)/shard_map/ppermute | solution.py:629
  103.6 0.8 copy-start.6
  106.4 28.1 %all-to-all-start.2 = ((bf16[8,1,32,1024]{3,2,1,0:T(8,128)(2,1)}), bf16[8,1,32,1024]{3,2,1,0:T(8,128)(2,1)S(1)}, u32[]{:S(2)}, u32[]{:S(2)}) async-start(bf16[8,1,32,1024]{3,2,1,0:T(8,128)(2,1)} %add.115), calls=%async_computation.2 | async-start | bytes 1048576 | tf_op jit(solution)/shard_map/all_to_all | solution.py:397
  118.9 41.7 %collective-permute-start.9 = (bf16[8,2,32,1024]{3,2,1,0:T(8,128)(2,1)}, bf16[8,2,32,1024]{3,2,1,0:T(8,128)(2,1)}, u32[]{:S(2)}, u32[]{:S(2)}) collective-permute-start(bf16[8,2,32,1024]{3,2,1,0:T(8,128)(2,1)} %get-tuple-element.79), channel_id=1, source_target_pairs={{0,2},{1,3},{2,0},{3,1},{4,6},{5,7},{6,4},{7,5},{8,10},{9,11},{10,... | collective-permute-start | bytes 3145736 | tf_op jit(solution)/shard_map/ppermute | solution.py:629
  130.6 25.0 %collective-permute-start.8 = (bf16[4,800,128]{2,1,0:T(8,128)(2,1)}, bf16[4,800,128]{2,1,0:T(8,128)(2,1)}, u32[]{:S(2)}, u32[]{:S(2)}) collective-permute-start(bf16[4,800,128]{2,1,0:T(8,128)(2,1)} %get-tuple-element.87), channel_id=1, source_target_pairs={{0,4},{4,0},{8,12},{12,8},{16,20},{20,16},{24,28},{28,24},{1,5},{5... | collective-permute-start | bytes 2457608 | tf_op jit(solution)/shard_map/ppermute | solution.py:687
  134.6 35.1 %all-to-all-start.3 = ((bf16[8,1,32,1024]{3,2,1,0:T(8,128)(2,1)}), bf16[8,1,32,1024]{3,2,1,0:T(8,128)(2,1)}, u32[]{:S(2)}, u32[]{:S(2)}) async-start(bf16[8,1,32,1024]{3,2,1,0:T(8,128)(2,1)} %add.116), calls=%async_computation.3 | async-start | bytes 1048576 | tf_op jit(solution)/shard_map/all_to_all | solution.py:397
  155.6 1.1 copy-start
  158.9 9.7 %collective-permute-start.10 = (bf16[2,800,128]{2,1,0:T(8,128)(2,1)}, bf16[2,800,128]{2,1,0:T(8,128)(2,1)}, u32[]{:S(2)}, u32[]{:S(2)}) collective-permute-start(bf16[2,800,128]{2,1,0:T(8,128)(2,1)} %get-tuple-element.91), channel_id=1, source_target_pairs={{0,8},{4,12},{8,0},{12,4},{16,24},{20,28},{24,16},{28,20},{1,9},{5... | collective-permute-start | bytes 1228808 | tf_op jit(solution)/shard_map/ppermute | solution.py:687
  164.3 10.8 %copy-start.5 = (f32[8,2,256]{2,1,0:T(2,128)S(1)}, f32[8,2,256]{2,1,0:T(2,128)}, u32[]{:S(2)}) copy-start(f32[8,2,256]{2,1,0:T(2,128)} %copy-done.4) | copy-start | bytes 49156
  169.7 38.0 %all-to-all-start.4 = ((bf16[8,2,32,1024]{3,2,1,0:T(8,128)(2,1)}), bf16[8,2,32,1024]{3,2,1,0:T(8,128)(2,1)S(1)}, u32[]{:S(2)}, u32[]{:S(2)}) async-start(bf16[8,2,32,1024]{3,2,1,0:T(8,128)(2,1)} %add.117), calls=%async_computation.4 | async-start | bytes 2097152 | tf_op jit(solution)/shard_map/all_to_all | solution.py:397
  175.1 31.7 %collective-permute-start.11 = (bf16[1,800,128]{2,1,0:T(8,128)(2,1)S(1)}, bf16[1,800,128]{2,1,0:T(8,128)(2,1)S(1)}, u32[]{:S(2)}, u32[]{:S(2)}) collective-permute-start(bf16[1,800,128]{2,1,0:T(8,128)(2,1)S(1)} %get-tuple-element.94), channel_id=1, source_target_pairs={{0,16},{4,20},{8,24},{12,28},{16,0},{20,4},{24,8},{28,12},{1,17},{... | collective-permute-start | bytes 614408 | tf_op jit(solution)/shard_map/ppermute | solution.py:687

commit v16 on v12

--- a/solution.py
+++ b/solution.py
@@ -647,9 +647,8 @@
     grads[2], taps[2] = back(*groups[2], *parts[0])
     parts[1] = partials(*groups[1], grads[1], grads[2])
     owns[0] = deliver(parts[0], LONG, *parts[1])
+    moved[0] = exchange(owns[0], "seq")
     parts[2] = partials(*groups[2], grads[2], owns[0])
-    moved[0] = exchange(after(owns[0], *parts[2]), "seq")
-    owns[1] = deliver(parts[1], 0, *parts[2])
 
     slots = 3 * width + 16 * (width // shard)
     half = sds((seqs // 2, slots, shard), BF16)
@@ -671,9 +670,10 @@
         [pltpu.VMEM((2 * width, model), F32)],
         LONG,
         1024,
-    )(parity, after(normed, owns[1]), w_out, *grads, *taps)
-    moved[1] = exchange(after(owns[1], keep, moved[0]), "seq")
-    owns[2] = deliver(parts[2], 0, keep)
+    )(parity, after(normed, *parts[2]), w_out, *grads, *taps)
+    owns[1] = deliver(parts[1], LONG, keep)
+    moved[1] = exchange(after(owns[1], moved[0]), "seq")
+    owns[2] = deliver(parts[2], 0, owns[1])
     moved[2] = exchange(after(owns[2], moved[1]), "seq")
     bit = 1
     while True:

time: 216 us -> 209 us (0.968)
  waiting for transfers between devices: 69.3 us -> 61.5 us
    all_to_all x5, waiting for transfers between devices: 19.6 us -> 10.5 us  [exchange(): return lax.all_to_all(copies, axis, 0, 0, tiled=True)]
  transfers between devices with their start and end apart: 17 -> 17, of which waited for: 8 -> 7; matrix products, arithmetic and copies ran while one was open for 2% -> 2% of each run, Pallas kernels for 27% -> 28%
where the time goes in v16:
time: 209 us; the launch traced here: 208 us
  Pallas kernels  92.3 us (44%)
  waiting for transfers between devices  61.5 us (29%)
  starting transfers between devices  42.8 us (20%)
  local copies, waits for them, and re-layouts  5.03 us (2%)
  other arithmetic  5 us (2%)
    ppermute x3, waiting for transfers between devices, per_device(): others = lax.ppermute(send, 'seq', [(i, i ^ bit) for i in range(seqs)])  41.7 us
    all_to_all x5, starting transfers between devices, exchange(): return lax.all_to_all(copies, axis, 0, 0, tiled=True)  24.6 us
    pallas_call x3, Pallas kernels, back(): call(functools.partial(back_kernel, first, blocks), 'back_conv', (size *...  19 us
    pallas_call x1, Pallas kernels, per_device(): call(gate_kernel, 'gate_conv', (recs,), [smem(), per_record((frames, mode...  15.3 us
    pallas_call x3, Pallas kernels, partials(): call(partial_kernel, 'partial_in', (size * parts_in,), [pl.BlockSpec((hal...  15 us
    pallas_call x1, Pallas kernels, per_device(): call(norm_kernel, 'swish_norm', (recs,), [smem(), smem(), whole((seqs, 2,...  12.1 us
    all_to_all x5, waiting for transfers between devices, exchange(): return lax.all_to_all(copies, axis, 0, 0, tiled=True)  10.5 us
    pallas_call x1, Pallas kernels, per_device(): call(functools.partial(outer_kernel, groups), 'outer_w_in', (recs,), [sme...  10.2 us
  transfers between devices with their start and end apart: 17, of which 7 were waited for; matrix products, arithmetic and copies ran while one was open for 2% of the time, Pallas kernels for 28%

profile of v16, /device:TPU:0, one launch (start us, length us, event | category | flops | bytes accessed | tf_op | source)
XLA Modules:
  0.0 208.2 jit_solution(402288551475937837)
XLA Ops:
  0.6 1.0 fusion.1
  1.6 4.9 %collective-permute-start = (bf16[4,8,2048]{2,1,0:T(8,128)(2,1)S(1)}, bf16[4,8,2048]{2,1,0:T(8,128)(2,1)S(1)}, u32[]{:S(2)}, u32[]{:S(2)}) collective-permute-start(bf16[4,8,2048]{2,1,0:T(8,128)(2,1)S(1)} %pad_maximum_fusion.3), channel_id=1, source_target_pairs={{0,4},{4,8},{8,12},{12,16},{16,20},{20,24},{24,28},{1,5},{5,9},{9,... | collective-permute-start | bytes 393224 | tf_op jit(solution)/shard_map/ppermute | solution.py:434
  6.5 1.3 collective-permute-start.1
  7.8 1.3 fusion.5
  9.7 3.7 %collective-permute-done.1 = bf16[4,8,2048]{2,1,0:T(8,128)(2,1)S(1)} collective-permute-done((bf16[4,8,2048]{2,1,0:T(8,128)(2,1)S(1)}, bf16[4,8,2048]{2,1,0:T(8,128)(2,1)S(1)}, u32[]{:S(2)}, u32[]{:S(2)}) %collective-permute-start.1) | collective-permute-done | bytes 131104 | tf_op jit(solution)/shard_map/ppermute | solution.py:434
  13.4 0.7 fusion.3
  14.1 15.3 %gate_conv.1 = (f32[4,1024,256]{2,1,0:T(8,128)}, f32[4,1024,256]{2,1,0:T(8,128)}, f32[4,1040,256]{2,1,0:T(8,128)}, f32[8,2,256]{2,1,0:T(2,128)}) custom-call(s32[2,4]{1,0:T(2,128)} %stack.35.meta, bf16[4,1024,1024]{2,1,0:T(8,128)(2,1)} %x.4, bf16[4,16,1024]{2,1,0:T(8,128)(2,1)} %get-tuple-element.106.halo, bf16[1024,256]{1,0:T(8,128)(2,1)} %wv.1, ...), custom_call_target="tpu_custom_call" | custom-call | flops 4294967296 | bytes 20971520 | tf_op jit(solution)/shard_map/gate_conv/pallas_call | solution.py:448
  29.4 1.1 pad_maximum_fusion
  31.6 0.6 pad_maximum_fusion.5.affine
  32.2 1.0 fusion.select
  33.2 5.7 %all-to-all-start = ((f32[8,2,256]{2,1,0:T(2,128)}), f32[8,2,256]{2,1,0:T(2,128)S(1)}, u32[]{:S(2)}, u32[]{:S(2)}) async-start(f32[8,2,256]{2,1,0:T(2,128)} %get-tuple-element.52), calls=%async_computation | async-start | bytes 32768 | tf_op jit(solution)/shard_map/all_to_all | solution.py:394
  38.9 0.9 pad_maximum_fusion.1
  39.8 5.7 %all-to-all-done.stats = f32[8,2,256]{2,1,0:T(2,128)S(1)} async-done(((f32[8,2,256]{2,1,0:T(2,128)}), f32[8,2,256]{2,1,0:T(2,128)S(1)}, u32[]{:S(2)}, u32[]{:S(2)}) %all-to-all-start) | async-done | bytes 16416 | tf_op jit(solution)/shard_map/all_to_all | solution.py:394
  45.5 0.6 copy-done.5
  46.1 12.1 %swish_norm.1 = (bf16[4,1024,256]{2,1,0:T(8,128)(2,1)}, f32[4,1040,256]{2,1,0:T(8,128)}, bf16[4,256,1024]{2,1,0:T(8,128)(2,1)}, f32[8,2,256]{2,1,0:T(2,128)}) custom-call(s32[2,4]{1,0:T(2,128)} %stack.35.meta, f32[1,1]{1,0:T(1,128)} %bitcast.1.count, f32[8,2,256]{2,1,0:T(2,128)} %copy-done.5, f32[2,256]{1,0:T(2,128)} %pad_maximum_fusion.5.affine, ...), custom_call_target="tpu_custom_call" | custom-call | flops 4294967296 | bytes 20971520 | tf_op jit(solution)/shard_map/swish_norm/pallas_call | solution.py:493
  58.2 3.3 %all-to-all-start.1 = ((f32[8,2,256]{2,1,0:T(2,128)}), f32[8,2,256]{2,1,0:T(2,128)S(1)}, u32[]{:S(2)}, u32[]{:S(2)}) async-start(f32[8,2,256]{2,1,0:T(2,128)} %get-tuple-element.56), calls=%async_computation.1 | async-start | bytes 32768 | tf_op jit(solution)/shard_map/all_to_all | solution.py:394
  61.5 7.0 %outer_w_out.1.w_out = f32[256,1024]{1,0:T(8,128)} custom-call(bf16[4,1024,1024]{2,1,0:T(8,128)(2,1)} %grads.3, bf16[4,1024,256]{2,1,0:T(8,128)(2,1)} %get-tuple-element.60.swished), custom_call_target="tpu_custom_call" | custom-call | flops 2147483648 | bytes 8388608 | tf_op jit(solution)/shard_map/outer_w_out/pallas_call | solution.py:538
  68.5 0.6 copy-done.3
  69.1 5.0 %back_conv.3 = (bf16[1024,512]{1,0:T(8,128)(2,1)}, f32[16,256]{1,0:T(8,128)}) custom-call(s32[2,4]{1,0:T(2,128)} %stack.35.meta, f32[1,1]{1,0:T(1,128)} %bitcast.1.count, f32[8,2,256]{2,1,0:T(2,128)} %copy-done.5, f32[8,2,256]{2,1,0:T(2,128)} %copy-done.3, f32[1,256]{1,0:T(1,128)} %bitcast.26, f32[4,1040,256]{2,1,0:T(8,128)} %get-tuple-element.57.gn, ...), custom_call_target="tpu_custom_call" | custom-call | bytes 1024 | tf_op jit(solution)/shard_map/back_conv/pallas_call | solution.py:562
  74.2 5.1 %back_conv.4 = (bf16[1024,512]{1,0:T(8,128)(2,1)}, f32[16,256]{1,0:T(8,128)}) custom-call(s32[2,4]{1,0:T(2,128)} %stack.35.meta, f32[1,1]{1,0:T(1,128)} %bitcast.1.count, f32[8,2,256]{2,1,0:T(2,128)} %copy-done.5, f32[8,2,256]{2,1,0:T(2,128)} %copy-done.3, f32[1,256]{1,0:T(1,128)} %bitcast.27, f32[4,1040,256]{2,1,0:T(8,128)} %get-tuple-element.57.gn, ...), custom_call_target="tpu_custom_call" | custom-call | bytes 1024 | tf_op jit(solution)/shard_map/back_conv/pallas_call | solution.py:562
  79.8 4.2 %partial_in.3 = (bf16[8,1,32,1024]{3,2,1,0:T(8,128)(2,1)}, bf16[8,1,32,1024]{3,2,1,0:T(8,128)(2,1)}) custom-call(bf16[1024,512]{1,0:T(8,128)(2,1)} %get-tuple-element.62.own.refs_0_, bf16[1024,512]{1,0:T(8,128)(2,1)} %collective-permute-done.3.sibling, bf16[512,512]{1,0:T(8,128)(2,1)} %bitcast.21, bf16[512,512]{1,0:T(8,128)(2,1)} %copy-done.1, ...), custom_call_target="tpu_custom_call" | custom-call | bytes 1024 | tf_op jit(solution)/shard_map/partial_in/pallas_call | solution.py:591
  84.1 1.5 collective-permute-start.6
  85.6 8.9 %back_conv.5 = (bf16[2048,512]{1,0:T(8,128)(2,1)}, f32[16,256]{1,0:T(8,128)}) custom-call(s32[2,4]{1,0:T(2,128)} %stack.35.meta, f32[1,1]{1,0:T(1,128)} %bitcast.1.count, f32[8,2,256]{2,1,0:T(2,128)} %copy-done.5, f32[8,2,256]{2,1,0:T(2,128)} %copy-done.3, f32[1,256]{1,0:T(1,128)} %bitcast.28, f32[4,1040,256]{2,1,0:T(8,128)} %get-tuple-element.57.gn, ...), custom_call_target="tpu_custom_call" | custom-call | bytes 1024 | tf_op jit(solution)/shard_map/back_conv/pallas_call | solution.py:562
  94.5 4.3 %partial_in.4 = (bf16[8,1,32,1024]{3,2,1,0:T(8,128)(2,1)}, bf16[8,1,32,1024]{3,2,1,0:T(8,128)(2,1)}) custom-call(bf16[1024,512]{1,0:T(8,128)(2,1)} %get-tuple-element.64.own.refs_1_, bf16[1024,512]{1,0:T(8,128)(2,1)} %collective-permute-done.5.sibling, bf16[512,512]{1,0:T(8,128)(2,1)} %bitcast.22, bf16[512,512]{1,0:T(8,128)(2,1)} %copy-done.1, ...), custom_call_target="tpu_custom_call" | custom-call | bytes 1024 | tf_op jit(solution)/shard_map/partial_in/pallas_call | solution.py:591
  99.4 0.8 copy-done.8
  100.1 2.0 add.115
  102.1 5.9 %all-to-all-start.2 = ((bf16[8,1,32,1024]{3,2,1,0:T(8,128)(2,1)}), bf16[8,1,32,1024]{3,2,1,0:T(8,128)(2,1)S(1)}, u32[]{:S(2)}, u32[]{:S(2)}) async-start(bf16[8,1,32,1024]{3,2,1,0:T(8,128)(2,1)} %add.115), calls=%async_computation.2 | async-start | bytes 1048576 | tf_op jit(solution)/shard_map/all_to_all | solution.py:394
  108.1 6.5 %partial_in.5 = (bf16[8,2,32,1024]{3,2,1,0:T(8,128)(2,1)}, bf16[8,2,32,1024]{3,2,1,0:T(8,128)(2,1)}) custom-call(bf16[2048,512]{1,0:T(8,128)(2,1)} %get-tuple-element.70.own.refs_2_, bf16[2048,512]{1,0:T(8,128)(2,1)} %collective-permute-done.4.sibling, bf16[512,512]{1,0:T(8,128)(2,1)} %bitcast.23, bf16[512,512]{1,0:T(8,128)(2,1)} %copy-done.1, ...), custom_call_target="tpu_custom_call" | custom-call | bytes 1024 | tf_op jit(solution)/shard_map/partial_in/pallas_call | solution.py:591
  114.6 1.5 collective-permute-start.8
  116.0 10.2 %outer_w_in.1 = (bf16[4,800,128]{2,1,0:T(8,128)(2,1)}, bf16[4,800,128]{2,1,0:T(8,128)(2,1)}) custom-call(s32[1,1]{1,0:T(1,128)} %bitcast.11.parity, bf16[4,1024,1024]{2,1,0:T(8,128)(2,1)} %x.4, f32[256,1024]{1,0:T(8,128)} %outer_w_out.1.w_out, bf16[1024,512]{1,0:T(8,128)(2,1)} %get-tuple-element.62.own.refs_0_, ...), custom_call_target="tpu_custom_call" | custom-call | flops 49999998976 | bytes 1024 | tf_op jit(solution)/shard_map/outer_w_in/pallas_call | solution.py:655
  126.2 2.0 add.116
  128.2 6.0 %all-to-all-start.3 = ((bf16[8,1,32,1024]{3,2,1,0:T(8,128)(2,1)}), bf16[8,1,32,1024]{3,2,1,0:T(8,128)(2,1)}, u32[]{:S(2)}, u32[]{:S(2)}) async-start(bf16[8,1,32,1024]{3,2,1,0:T(8,128)(2,1)} %add.116), calls=%async_computation.3 | async-start | bytes 1048576 | tf_op jit(solution)/shard_map/all_to_all | solution.py:394
  134.2 5.7 %collective-permute-done.8.refs_1_ = bf16[8,2,32,1024]{3,2,1,0:T(8,128)(2,1)} collective-permute-done((bf16[8,2,32,1024]{3,2,1,0:T(8,128)(2,1)}, bf16[8,2,32,1024]{3,2,1,0:T(8,128)(2,1)}, u32[]{:S(2)}, u32[]{:S(2)}) %collective-permute-start.8) | collective-permute-done | bytes 1048608 | tf_op jit(solution)/shard_map/ppermute | solution.py:620
  139.9 3.7 %add.117 = bf16[8,2,32,1024]{3,2,1,0:T(8,128)(2,1)} custom-call(bf16[8,2,32,1024]{3,2,1,0:T(8,128)(2,1)} %get-tuple-element.84.refs_0_, bf16[8,2,32,1024]{3,2,1,0:T(8,128)(2,1)} %collective-permute-done.8.refs_1_), custom_call_target="tpu_custom_call" | custom-call | bytes 1024 | tf_op jit(solution)/shard_map/add/pallas_call | solution.py:625
  143.6 4.8 %all-to-all-done.3.moved = bf16[8,1,32,1024]{3,2,1,0:T(8,128)(2,1)} async-done(((bf16[8,1,32,1024]{3,2,1,0:T(8,128)(2,1)}), bf16[8,1,32,1024]{3,2,1,0:T(8,128)(2,1)}, u32[]{:S(2)}, u32[]{:S(2)}) %all-to-all-start.3) | async-done | bytes 524320 | tf_op jit(solution)/shard_map/all_to_all | solution.py:394
  148.3 3.6 %all-to-all-start.4 = ((bf16[8,2,32,1024]{3,2,1,0:T(8,128)(2,1)}), bf16[8,2,32,1024]{3,2,1,0:T(8,128)(2,1)S(1)}, u32[]{:S(2)}, u32[]{:S(2)}) async-start(bf16[8,2,32,1024]{3,2,1,0:T(8,128)(2,1)} %add.117), calls=%async_computation.4 | async-start | bytes 2097152 | tf_op jit(solution)/shard_map/all_to_all | solution.py:394
  152.0 2.0 collective-permute-start.9
  154.0 29.0 %collective-permute-done.9.other = bf16[4,800,128]{2,1,0:T(8,128)(2,1)} collective-permute-done((bf16[4,800,128]{2,1,0:T(8,128)(2,1)}, bf16[4,800,128]{2,1,0:T(8,128)(2,1)}, u32[]{:S(2)}, u32[]{:S(2)}) %collective-permute-start.9) | collective-permute-done | bytes 819232 | tf_op jit(solution)/shard_map/ppermute | solution.py:680
  183.0 1.3 fold.2
  184.3 1.5 collective-permute-start.10
  185.9 8.3 %collective-permute-done.10.other = bf16[2,800,128]{2,1,0:T(8,128)(2,1)S(1)} collective-permute-done((bf16[2,800,128]{2,1,0:T(8,128)(2,1)S(1)}, bf16[2,800,128]{2,1,0:T(8,128)(2,1)S(1)}, u32[]{:S(2)}, u32[]{:S(2)}) %collective-permute-start.10) | collective-permute-done | bytes 409632 | tf_op jit(solution)/shard_map/ppermute | solution.py:680
  194.3 4.3 %collective-permute-start.11 = (bf16[1,800,128]{2,1,0:T(8,128)(2,1)S(1)}, bf16[1,800,128]{2,1,0:T(8,128)(2,1)S(1)}, u32[]{:S(2)}, u32[]{:S(2)}) collective-permute-start(bf16[1,800,128]{2,1,0:T(8,128)(2,1)S(1)} %get-tuple-element.92), channel_id=1, source_target_pairs={{0,16},{4,20},{8,24},{12,28},{16,0},{20,4},{24,8},{28,12},{1,17},{... | collective-permute-start | bytes 614408 | tf_op jit(solution)/shard_map/ppermute | solution.py:680
  198.5 0.6 fusion.4
  199.1 0.8 place.3.refs_0_
  199.9 1.9 place.4.refs_0_
  201.8 4.4 %collective-permute-done.11.other = bf16[1,800,128]{2,1,0:T(8,128)(2,1)S(1)} collective-permute-done((bf16[1,800,128]{2,1,0:T(8,128)(2,1)S(1)}, bf16[1,800,128]{2,1,0:T(8,128)(2,1)S(1)}, u32[]{:S(2)}, u32[]{:S(2)}) %collective-permute-start.11) | collective-permute-done | bytes 204832 | tf_op jit(solution)/shard_map/ppermute | solution.py:680
  206.2 0.9 finish.1
  207.1 1.1 place.5
  (42 shorter events, 2.3 us)
Async XLA Ops:
  1.6 8.1 %collective-permute-start = (bf16[4,8,2048]{2,1,0:T(8,128)(2,1)S(1)}, bf16[4,8,2048]{2,1,0:T(8,128)(2,1)S(1)}, u32[]{:S(2)}, u32[]{:S(2)}) collective-permute-start(bf16[4,8,2048]{2,1,0:T(8,128)(2,1)S(1)} %pad_maximum_fusion.3), channel_id=1, source_target_pairs={{0,4},{4,8},{8,12},{12,16},{16,20},{20,24},{24,28},{1,5},{5,9},{9,... | collective-permute-start | bytes 393224 | tf_op jit(solution)/shard_map/ppermute | solution.py:434
  6.5 6.9 %collective-permute-start.1 = (bf16[4,8,2048]{2,1,0:T(8,128)(2,1)S(1)}, bf16[4,8,2048]{2,1,0:T(8,128)(2,1)S(1)}, u32[]{:S(2)}, u32[]{:S(2)}) collective-permute-start(bf16[4,8,2048]{2,1,0:T(8,128)(2,1)S(1)} %pad_maximum_fusion.4), channel_id=1, source_target_pairs={{4,0},{8,4},{12,8},{16,12},{20,16},{24,20},{28,24},{5,1},{9,5},{13... | collective-permute-start | bytes 393224 | tf_op jit(solution)/shard_map/ppermute | solution.py:434
  14.1 15.3 %copy-start.2 = (bf16[1024,256]{1,0:T(8,128)(2,1)S(1)}, bf16[1024,256]{1,0:T(8,128)(2,1)}, u32[]{:S(2)}) copy-start(bf16[1024,256]{1,0:T(8,128)(2,1)} %wv.1) | copy-start | bytes 1572868
  30.6 1.1 copy-start.6
  30.6 1.1 copy-start.7
  30.7 9.1 %collective-permute-start.2 = (bf16[512,512]{1,0:T(8,128)(2,1)S(1)}, bf16[512,512]{1,0:T(8,128)(2,1)S(1)}, u32[]{:S(2)}, u32[]{:S(2)}) collective-permute-start(bf16[512,512]{1,0:T(8,128)(2,1)S(1)} %bitcast.25), channel_id=1, source_target_pairs={{0,1},{1,0},{2,3},{3,2},{4,5},{5,4},{6,7},{7,6},{8,9},{9,8},{10,11... | collective-permute-start | bytes 1572872 | tf_op jit(solution)/shard_map/ppermute | solution.py:487
  33.2 12.3 %all-to-all-start = ((f32[8,2,256]{2,1,0:T(2,128)}), f32[8,2,256]{2,1,0:T(2,128)S(1)}, u32[]{:S(2)}, u32[]{:S(2)}) async-start(f32[8,2,256]{2,1,0:T(2,128)} %get-tuple-element.52), calls=%async_computation | async-start | bytes 32768 | tf_op jit(solution)/shard_map/all_to_all | solution.py:394
  39.8 18.4 %copy-start.1 = (bf16[512,512]{1,0:T(8,128)(2,1)}, bf16[512,512]{1,0:T(8,128)(2,1)S(1)}, u32[]{:S(2)}) copy-start(bf16[512,512]{1,0:T(8,128)(2,1)S(1)} %collective-permute-done.2.w_sibling) | copy-start | bytes 1572868
  45.5 0.6 copy-start.5
  58.2 10.4 %all-to-all-start.1 = ((f32[8,2,256]{2,1,0:T(2,128)}), f32[8,2,256]{2,1,0:T(2,128)S(1)}, u32[]{:S(2)}, u32[]{:S(2)}) async-start(f32[8,2,256]{2,1,0:T(2,128)} %get-tuple-element.56), calls=%async_computation.1 | async-start | bytes 32768 | tf_op jit(solution)/shard_map/all_to_all | solution.py:394
  68.5 0.6 copy-start.3
  74.2 5.7 %collective-permute-start.3 = (bf16[1024,512]{1,0:T(8,128)(2,1)}, bf16[1024,512]{1,0:T(8,128)(2,1)}, u32[]{:S(2)}, u32[]{:S(2)}) collective-permute-start(bf16[1024,512]{1,0:T(8,128)(2,1)} %get-tuple-element.62.own.refs_0_), channel_id=1, source_target_pairs={{0,1},{1,0},{2,3},{3,2},{4,5},{5,4},{6,7},{7,6},{8,9},{9,8},{10,11... | collective-permute-start | bytes 3145736 | tf_op jit(solution)/shard_map/ppermute | solution.py:589
  79.3 15.2 %collective-permute-start.5 = (bf16[1024,512]{1,0:T(8,128)(2,1)}, bf16[1024,512]{1,0:T(8,128)(2,1)}, u32[]{:S(2)}, u32[]{:S(2)}) collective-permute-start(bf16[1024,512]{1,0:T(8,128)(2,1)} %get-tuple-element.64.own.refs_1_), channel_id=1, source_target_pairs={{0,1},{1,0},{2,3},{3,2},{4,5},{5,4},{6,7},{7,6},{8,9},{9,8},{10,11... | collective-permute-start | bytes 3145736 | tf_op jit(solution)/shard_map/ppermute | solution.py:589
  84.1 15.3 %collective-permute-start.6 = (bf16[8,1,32,1024]{3,2,1,0:T(8,128)(2,1)}, bf16[8,1,32,1024]{3,2,1,0:T(8,128)(2,1)S(1)}, u32[]{:S(2)}, u32[]{:S(2)}) collective-permute-start(bf16[8,1,32,1024]{3,2,1,0:T(8,128)(2,1)} %get-tuple-element.68), channel_id=1, source_target_pairs={{0,2},{1,3},{2,0},{3,1},{4,6},{5,7},{6,4},{7,5},{8,10},{9,11},{10,... | collective-permute-start | bytes 1572872 | tf_op jit(solution)/shard_map/ppermute | solution.py:620
  94.5 13.6 %collective-permute-start.4 = (bf16[2048,512]{1,0:T(8,128)(2,1)}, bf16[2048,512]{1,0:T(8,128)(2,1)}, u32[]{:S(2)}, u32[]{:S(2)}) collective-permute-start(bf16[2048,512]{1,0:T(8,128)(2,1)} %get-tuple-element.70.own.refs_2_), channel_id=1, source_target_pairs={{0,1},{1,0},{2,3},{3,2},{4,5},{5,4},{6,7},{7,6},{8,9},{9,8},{10,11... | collective-permute-start | bytes 6291464 | tf_op jit(solution)/shard_map/ppermute | solution.py:589
  98.8 27.4 %collective-permute-start.7 = (bf16[8,1,32,1024]{3,2,1,0:T(8,128)(2,1)}, bf16[8,1,32,1024]{3,2,1,0:T(8,128)(2,1)}, u32[]{:S(2)}, u32[]{:S(2)}) collective-permute-start(bf16[8,1,32,1024]{3,2,1,0:T(8,128)(2,1)} %get-tuple-element.73), channel_id=1, source_target_pairs={{0,2},{1,3},{2,0},{3,1},{4,6},{5,7},{6,4},{7,5},{8,10},{9,11},{10,... | collective-permute-start | bytes 1572872 | tf_op jit(solution)/shard_map/ppermute | solution.py:620
  99.3 0.8 copy-start.8
  102.1 26.1 %all-to-all-start.2 = ((bf16[8,1,32,1024]{3,2,1,0:T(8,128)(2,1)}), bf16[8,1,32,1024]{3,2,1,0:T(8,128)(2,1)S(1)}, u32[]{:S(2)}, u32[]{:S(2)}) async-start(bf16[8,1,32,1024]{3,2,1,0:T(8,128)(2,1)} %add.115), calls=%async_computation.2 | async-start | bytes 1048576 | tf_op jit(solution)/shard_map/all_to_all | solution.py:394
  114.6 25.3 %collective-permute-start.8 = (bf16[8,2,32,1024]{3,2,1,0:T(8,128)(2,1)}, bf16[8,2,32,1024]{3,2,1,0:T(8,128)(2,1)}, u32[]{:S(2)}, u32[]{:S(2)}) collective-permute-start(bf16[8,2,32,1024]{3,2,1,0:T(8,128)(2,1)} %get-tuple-element.77), channel_id=1, source_target_pairs={{0,2},{1,3},{2,0},{3,1},{4,6},{5,7},{6,4},{7,5},{8,10},{9,11},{10,... | collective-permute-start | bytes 3145736 | tf_op jit(solution)/shard_map/ppermute | solution.py:620
  128.2 20.1 %all-to-all-start.3 = ((bf16[8,1,32,1024]{3,2,1,0:T(8,128)(2,1)}), bf16[8,1,32,1024]{3,2,1,0:T(8,128)(2,1)}, u32[]{:S(2)}, u32[]{:S(2)}) async-start(bf16[8,1,32,1024]{3,2,1,0:T(8,128)(2,1)} %add.116), calls=%async_computation.3 | async-start | bytes 1048576 | tf_op jit(solution)/shard_map/all_to_all | solution.py:394
  143.6 39.4 %copy-start = (bf16[4,800,128]{2,1,0:T(8,128)(2,1)S(1)}, bf16[4,800,128]{2,1,0:T(8,128)(2,1)}, u32[]{:S(2)}) copy-start(bf16[4,800,128]{2,1,0:T(8,128)(2,1)} %get-tuple-element.87.own) | copy-start | bytes 2457604
  143.6 42.3 %copy-start.4 = (f32[8,2,256]{2,1,0:T(2,128)S(1)}, f32[8,2,256]{2,1,0:T(2,128)}, u32[]{:S(2)}) copy-start(f32[8,2,256]{2,1,0:T(2,128)} %copy-done.3) | copy-start | bytes 49156
  148.3 58.7 %all-to-all-start.4 = ((bf16[8,2,32,1024]{3,2,1,0:T(8,128)(2,1)}), bf16[8,2,32,1024]{3,2,1,0:T(8,128)(2,1)S(1)}, u32[]{:S(2)}, u32[]{:S(2)}) async-start(bf16[8,2,32,1024]{3,2,1,0:T(8,128)(2,1)} %add.117), calls=%async_computation.4 | async-start | bytes 2097152 | tf_op jit(solution)/shard_map/all_to_all | solution.py:394
  152.0 31.0 %collective-permute-start.9 = (bf16[4,800,128]{2,1,0:T(8,128)(2,1)}, bf16[4,800,128]{2,1,0:T(8,128)(2,1)}, u32[]{:S(2)}, u32[]{:S(2)}) collective-permute-start(bf16[4,800,128]{2,1,0:T(8,128)(2,1)} %get-tuple-element.88), channel_id=1, source_target_pairs={{0,4},{4,0},{8,12},{12,8},{16,20},{20,16},{24,28},{28,24},{1,5},{5... | collective-permute-start | bytes 2457608 | tf_op jit(solution)/shard_map/ppermute | solution.py:680
  184.3 9.8 %collective-permute-start.10 = (bf16[2,800,128]{2,1,0:T(8,128)(2,1)S(1)}, bf16[2,800,128]{2,1,0:T(8,128)(2,1)S(1)}, u32[]{:S(2)}, u32[]{:S(2)}) collective-permute-start(bf16[2,800,128]{2,1,0:T(8,128)(2,1)S(1)} %get-tuple-element.90), channel_id=1, source_target_pairs={{0,8},{4,12},{8,0},{12,4},{16,24},{20,28},{24,16},{28,20},{1,9},{5... | collective-permute-start | bytes 1228808 | tf_op jit(solution)/shard_map/ppermute | solution.py:680
  194.3 11.9 %collective-permute-start.11 = (bf16[1,800,128]{2,1,0:T(8,128)(2,1)S(1)}, bf16[1,800,128]{2,1,0:T(8,128)(2,1)S(1)}, u32[]{:S(2)}, u32[]{:S(2)}) collective-permute-start(bf16[1,800,128]{2,1,0:T(8,128)(2,1)S(1)} %get-tuple-element.92), channel_id=1, source_target_pairs={{0,16},{4,20},{8,24},{12,28},{16,0},{20,4},{24,8},{28,12},{1,17},{... | collective-permute-start | bytes 614408 | tf_op jit(solution)/shard_map/ppermute | solution.py:680

commit v17 on v16

--- a/solution.py
+++ b/solution.py
@@ -674,10 +674,11 @@
     owns[1] = deliver(parts[1], LONG, keep)
     moved[1] = exchange(after(owns[1], moved[0]), "seq")
     owns[2] = deliver(parts[2], 0, owns[1])
-    moved[2] = exchange(after(owns[2], moved[1]), "seq")
     bit = 1
     while True:
         others = lax.ppermute(send, "seq", [(i, i ^ bit) for i in range(seqs)])
+        if bit == 1:
+            moved[2] = exchange(after(owns[2], moved[1], others), "seq")
         bit *= 2
         if bit == seqs:
             break

time: 209 us -> 205 us (0.981)
  waiting for transfers between devices: 61.5 us -> 57.2 us
    all_to_all x5, waiting for transfers between devices: 10.5 us -> 5.69 us  [exchange(): return lax.all_to_all(copies, axis, 0, 0, tiled=True)]
    ppermute x3, waiting for transfers between devices: 41.7 us -> 44.2 us  [per_device(): others = lax.ppermute(send, 'seq', [(i, i ^ bit) for i in range(seqs)])]
  transfers between devices with their start and end apart: 17 -> 17, of which waited for: 7 -> 6; matrix products, arithmetic and copies ran while one was open for 2% -> 2% of each run, Pallas kernels for 28% -> 29%
where the time goes in v17:
time: 205 us; the launch traced here: 204 us
  Pallas kernels  92.3 us (45%)
  waiting for transfers between devices  57.2 us (28%)
  starting transfers between devices  42.6 us (21%)
  local copies, waits for them, and re-layouts  5.03 us (2%)
  other arithmetic  5 us (2%)
    ppermute x3, waiting for transfers between devices, per_device(): others = lax.ppermute(send, 'seq', [(i, i ^ bit) for i in range(seqs)])  44.2 us
    all_to_all x5, starting transfers between devices, exchange(): return lax.all_to_all(copies, axis, 0, 0, tiled=True)  25.5 us
    pallas_call x3, Pallas kernels, back(): call(functools.partial(back_kernel, first, blocks), 'back_conv', (size *...  19 us
    pallas_call x1, Pallas kernels, per_device(): call(gate_kernel, 'gate_conv', (recs,), [smem(), per_record((frames, mode...  15.3 us
    pallas_call x3, Pallas kernels, partials(): call(partial_kernel, 'partial_in', (size * parts_in,), [pl.BlockSpec((hal...  15 us
    pallas_call x1, Pallas kernels, per_device(): call(norm_kernel, 'swish_norm', (recs,), [smem(), smem(), whole((seqs, 2,...  12.1 us
    pallas_call x1, Pallas kernels, per_device(): call(functools.partial(outer_kernel, groups), 'outer_w_in', (recs,), [sme...  10.2 us
    pallas_call x3, Pallas kernels, deliver(): call(add_kernel, 'add', (size * parts_in,), [block] * chips, block, sds(p...  7.66 us
  transfers between devices with their start and end apart: 17, of which 6 were waited for; matrix products, arithmetic and copies ran while one was open for 2% of the time, Pallas kernels for 29%

profile of v17, /device:TPU:0, one launch (start us, length us, event | category | flops | bytes accessed | tf_op | source)
XLA Modules:
  0.0 203.7 jit_solution(630577470080837335)
XLA Ops:
  0.6 1.0 fusion.1
  1.6 4.9 %collective-permute-start = (bf16[4,8,2048]{2,1,0:T(8,128)(2,1)S(1)}, bf16[4,8,2048]{2,1,0:T(8,128)(2,1)S(1)}, u32[]{:S(2)}, u32[]{:S(2)}) collective-permute-start(bf16[4,8,2048]{2,1,0:T(8,128)(2,1)S(1)} %pad_maximum_fusion.3), channel_id=1, source_target_pairs={{0,4},{4,8},{8,12},{12,16},{16,20},{20,24},{24,28},{1,5},{5,9},{9,... | collective-permute-start | bytes 393224 | tf_op jit(solution)/shard_map/ppermute | solution.py:434
  6.5 1.3 collective-permute-start.1
  7.8 1.3 fusion.5
  9.1 0.6 stack.35.meta
  9.7 3.7 %collective-permute-done.1 = bf16[4,8,2048]{2,1,0:T(8,128)(2,1)S(1)} collective-permute-done((bf16[4,8,2048]{2,1,0:T(8,128)(2,1)S(1)}, bf16[4,8,2048]{2,1,0:T(8,128)(2,1)S(1)}, u32[]{:S(2)}, u32[]{:S(2)}) %collective-permute-start.1) | collective-permute-done | bytes 131104 | tf_op jit(solution)/shard_map/ppermute | solution.py:434
  13.4 0.7 fusion.3
  14.1 15.3 %gate_conv.1 = (f32[4,1024,256]{2,1,0:T(8,128)}, f32[4,1024,256]{2,1,0:T(8,128)}, f32[4,1040,256]{2,1,0:T(8,128)}, f32[8,2,256]{2,1,0:T(2,128)}) custom-call(s32[2,4]{1,0:T(2,128)} %stack.35.meta, bf16[4,1024,1024]{2,1,0:T(8,128)(2,1)} %x.4, bf16[4,16,1024]{2,1,0:T(8,128)(2,1)} %get-tuple-element.106.halo, bf16[1024,256]{1,0:T(8,128)(2,1)} %wv.1, ...), custom_call_target="tpu_custom_call" | custom-call | flops 4294967296 | bytes 20971520 | tf_op jit(solution)/shard_map/gate_conv/pallas_call | solution.py:448
  29.4 1.1 pad_maximum_fusion
  31.6 0.6 pad_maximum_fusion.5.affine
  32.2 1.0 fusion.select
  33.2 5.7 %all-to-all-start = ((f32[8,2,256]{2,1,0:T(2,128)}), f32[8,2,256]{2,1,0:T(2,128)S(1)}, u32[]{:S(2)}, u32[]{:S(2)}) async-start(f32[8,2,256]{2,1,0:T(2,128)} %get-tuple-element.52), calls=%async_computation | async-start | bytes 32768 | tf_op jit(solution)/shard_map/all_to_all | solution.py:394
  38.9 0.9 pad_maximum_fusion.1
  39.8 5.7 %all-to-all-done.stats = f32[8,2,256]{2,1,0:T(2,128)S(1)} async-done(((f32[8,2,256]{2,1,0:T(2,128)}), f32[8,2,256]{2,1,0:T(2,128)S(1)}, u32[]{:S(2)}, u32[]{:S(2)}) %all-to-all-start) | async-done | bytes 16416 | tf_op jit(solution)/shard_map/all_to_all | solution.py:394
  45.5 0.6 copy-done.5
  46.1 12.1 %swish_norm.1 = (bf16[4,1024,256]{2,1,0:T(8,128)(2,1)}, f32[4,1040,256]{2,1,0:T(8,128)}, bf16[4,256,1024]{2,1,0:T(8,128)(2,1)}, f32[8,2,256]{2,1,0:T(2,128)}) custom-call(s32[2,4]{1,0:T(2,128)} %stack.35.meta, f32[1,1]{1,0:T(1,128)} %bitcast.1.count, f32[8,2,256]{2,1,0:T(2,128)} %copy-done.5, f32[2,256]{1,0:T(2,128)} %pad_maximum_fusion.5.affine, ...), custom_call_target="tpu_custom_call" | custom-call | flops 4294967296 | bytes 20971520 | tf_op jit(solution)/shard_map/swish_norm/pallas_call | solution.py:493
  58.2 3.3 %all-to-all-start.1 = ((f32[8,2,256]{2,1,0:T(2,128)}), f32[8,2,256]{2,1,0:T(2,128)S(1)}, u32[]{:S(2)}, u32[]{:S(2)}) async-start(f32[8,2,256]{2,1,0:T(2,128)} %get-tuple-element.56), calls=%async_computation.1 | async-start | bytes 32768 | tf_op jit(solution)/shard_map/all_to_all | solution.py:394
  61.5 7.0 %outer_w_out.1.w_out = f32[256,1024]{1,0:T(8,128)} custom-call(bf16[4,1024,1024]{2,1,0:T(8,128)(2,1)} %grads.3, bf16[4,1024,256]{2,1,0:T(8,128)(2,1)} %get-tuple-element.60.swished), custom_call_target="tpu_custom_call" | custom-call | flops 2147483648 | bytes 8388608 | tf_op jit(solution)/shard_map/outer_w_out/pallas_call | solution.py:538
  68.5 0.6 copy-done.3
  69.1 5.0 %back_conv.3 = (bf16[1024,512]{1,0:T(8,128)(2,1)}, f32[16,256]{1,0:T(8,128)}) custom-call(s32[2,4]{1,0:T(2,128)} %stack.35.meta, f32[1,1]{1,0:T(1,128)} %bitcast.1.count, f32[8,2,256]{2,1,0:T(2,128)} %copy-done.5, f32[8,2,256]{2,1,0:T(2,128)} %copy-done.3, f32[1,256]{1,0:T(1,128)} %bitcast.26, f32[4,1040,256]{2,1,0:T(8,128)} %get-tuple-element.57.gn, ...), custom_call_target="tpu_custom_call" | custom-call | bytes 1024 | tf_op jit(solution)/shard_map/back_conv/pallas_call | solution.py:562
  74.2 5.1 %back_conv.4 = (bf16[1024,512]{1,0:T(8,128)(2,1)}, f32[16,256]{1,0:T(8,128)}) custom-call(s32[2,4]{1,0:T(2,128)} %stack.35.meta, f32[1,1]{1,0:T(1,128)} %bitcast.1.count, f32[8,2,256]{2,1,0:T(2,128)} %copy-done.5, f32[8,2,256]{2,1,0:T(2,128)} %copy-done.3, f32[1,256]{1,0:T(1,128)} %bitcast.27, f32[4,1040,256]{2,1,0:T(8,128)} %get-tuple-element.57.gn, ...), custom_call_target="tpu_custom_call" | custom-call | bytes 1024 | tf_op jit(solution)/shard_map/back_conv/pallas_call | solution.py:562
  79.8 4.2 %partial_in.3 = (bf16[8,1,32,1024]{3,2,1,0:T(8,128)(2,1)}, bf16[8,1,32,1024]{3,2,1,0:T(8,128)(2,1)}) custom-call(bf16[1024,512]{1,0:T(8,128)(2,1)} %get-tuple-element.62.own.refs_0_, bf16[1024,512]{1,0:T(8,128)(2,1)} %collective-permute-done.3.sibling, bf16[512,512]{1,0:T(8,128)(2,1)} %bitcast.21, bf16[512,512]{1,0:T(8,128)(2,1)} %copy-done.1, ...), custom_call_target="tpu_custom_call" | custom-call | bytes 1024 | tf_op jit(solution)/shard_map/partial_in/pallas_call | solution.py:591
  84.1 1.5 collective-permute-start.6
  85.6 8.9 %back_conv.5 = (bf16[2048,512]{1,0:T(8,128)(2,1)}, f32[16,256]{1,0:T(8,128)}) custom-call(s32[2,4]{1,0:T(2,128)} %stack.35.meta, f32[1,1]{1,0:T(1,128)} %bitcast.1.count, f32[8,2,256]{2,1,0:T(2,128)} %copy-done.5, f32[8,2,256]{2,1,0:T(2,128)} %copy-done.3, f32[1,256]{1,0:T(1,128)} %bitcast.28, f32[4,1040,256]{2,1,0:T(8,128)} %get-tuple-element.57.gn, ...), custom_call_target="tpu_custom_call" | custom-call | bytes 1024 | tf_op jit(solution)/shard_map/back_conv/pallas_call | solution.py:562
  94.5 4.3 %partial_in.4 = (bf16[8,1,32,1024]{3,2,1,0:T(8,128)(2,1)}, bf16[8,1,32,1024]{3,2,1,0:T(8,128)(2,1)}) custom-call(bf16[1024,512]{1,0:T(8,128)(2,1)} %get-tuple-element.64.own.refs_1_, bf16[1024,512]{1,0:T(8,128)(2,1)} %collective-permute-done.5.sibling, bf16[512,512]{1,0:T(8,128)(2,1)} %bitcast.22, bf16[512,512]{1,0:T(8,128)(2,1)} %copy-done.1, ...), custom_call_target="tpu_custom_call" | custom-call | bytes 1024 | tf_op jit(solution)/shard_map/partial_in/pallas_call | solution.py:591
  99.4 0.8 copy-done.8
  100.1 2.0 add.115
  102.1 5.9 %all-to-all-start.2 = ((bf16[8,1,32,1024]{3,2,1,0:T(8,128)(2,1)}), bf16[8,1,32,1024]{3,2,1,0:T(8,128)(2,1)S(1)}, u32[]{:S(2)}, u32[]{:S(2)}) async-start(bf16[8,1,32,1024]{3,2,1,0:T(8,128)(2,1)} %add.115), calls=%async_computation.2 | async-start | bytes 1048576 | tf_op jit(solution)/shard_map/all_to_all | solution.py:394
  108.1 6.5 %partial_in.5 = (bf16[8,2,32,1024]{3,2,1,0:T(8,128)(2,1)}, bf16[8,2,32,1024]{3,2,1,0:T(8,128)(2,1)}) custom-call(bf16[2048,512]{1,0:T(8,128)(2,1)} %get-tuple-element.70.own.refs_2_, bf16[2048,512]{1,0:T(8,128)(2,1)} %collective-permute-done.4.sibling, bf16[512,512]{1,0:T(8,128)(2,1)} %bitcast.23, bf16[512,512]{1,0:T(8,128)(2,1)} %copy-done.1, ...), custom_call_target="tpu_custom_call" | custom-call | bytes 1024 | tf_op jit(solution)/shard_map/partial_in/pallas_call | solution.py:591
  114.6 1.5 collective-permute-start.8
  116.0 10.2 %outer_w_in.1 = (bf16[4,800,128]{2,1,0:T(8,128)(2,1)}, bf16[4,800,128]{2,1,0:T(8,128)(2,1)}) custom-call(s32[1,1]{1,0:T(1,128)} %bitcast.11.parity, bf16[4,1024,1024]{2,1,0:T(8,128)(2,1)} %x.4, f32[256,1024]{1,0:T(8,128)} %outer_w_out.1.w_out, bf16[1024,512]{1,0:T(8,128)(2,1)} %get-tuple-element.62.own.refs_0_, ...), custom_call_target="tpu_custom_call" | custom-call | flops 49999998976 | bytes 1024 | tf_op jit(solution)/shard_map/outer_w_in/pallas_call | solution.py:655
  126.2 2.0 add.116
  128.2 6.0 %all-to-all-start.3 = ((bf16[8,1,32,1024]{3,2,1,0:T(8,128)(2,1)}), bf16[8,1,32,1024]{3,2,1,0:T(8,128)(2,1)}, u32[]{:S(2)}, u32[]{:S(2)}) async-start(bf16[8,1,32,1024]{3,2,1,0:T(8,128)(2,1)} %add.116), calls=%async_computation.3 | async-start | bytes 1048576 | tf_op jit(solution)/shard_map/all_to_all | solution.py:394
  134.2 2.0 collective-permute-start.9
  136.2 3.6 %collective-permute-done.8.refs_1_ = bf16[8,2,32,1024]{3,2,1,0:T(8,128)(2,1)} collective-permute-done((bf16[8,2,32,1024]{3,2,1,0:T(8,128)(2,1)}, bf16[8,2,32,1024]{3,2,1,0:T(8,128)(2,1)}, u32[]{:S(2)}, u32[]{:S(2)}) %collective-permute-start.8) | collective-permute-done | bytes 1048608 | tf_op jit(solution)/shard_map/ppermute | solution.py:620
  139.9 3.7 %add.117 = bf16[8,2,32,1024]{3,2,1,0:T(8,128)(2,1)} custom-call(bf16[8,2,32,1024]{3,2,1,0:T(8,128)(2,1)} %get-tuple-element.84.refs_0_, bf16[8,2,32,1024]{3,2,1,0:T(8,128)(2,1)} %collective-permute-done.8.refs_1_), custom_call_target="tpu_custom_call" | custom-call | bytes 1024 | tf_op jit(solution)/shard_map/add/pallas_call | solution.py:625
  143.6 15.8 %collective-permute-done.9.other = bf16[4,800,128]{2,1,0:T(8,128)(2,1)} collective-permute-done((bf16[4,800,128]{2,1,0:T(8,128)(2,1)}, bf16[4,800,128]{2,1,0:T(8,128)(2,1)}, u32[]{:S(2)}, u32[]{:S(2)}) %collective-permute-start.9) | collective-permute-done | bytes 819232 | tf_op jit(solution)/shard_map/ppermute | solution.py:679
  159.3 4.5 %all-to-all-start.4 = ((bf16[8,2,32,1024]{3,2,1,0:T(8,128)(2,1)}), bf16[8,2,32,1024]{3,2,1,0:T(8,128)(2,1)S(1)}, u32[]{:S(2)}, u32[]{:S(2)}) async-start(bf16[8,2,32,1024]{3,2,1,0:T(8,128)(2,1)} %add.117), calls=%async_computation.4 | async-start | bytes 2097152 | tf_op jit(solution)/shard_map/all_to_all | solution.py:394
  163.9 1.3 fold.2
  165.2 2.1 %collective-permute-start.10 = (bf16[2,800,128]{2,1,0:T(8,128)(2,1)S(1)}, bf16[2,800,128]{2,1,0:T(8,128)(2,1)S(1)}, u32[]{:S(2)}, u32[]{:S(2)}) collective-permute-start(bf16[2,800,128]{2,1,0:T(8,128)(2,1)S(1)} %get-tuple-element.90), channel_id=1, source_target_pairs={{0,8},{4,12},{8,0},{12,4},{16,24},{20,28},{24,16},{28,20},{1,9},{5... | collective-permute-start | bytes 1228808 | tf_op jit(solution)/shard_map/ppermute | solution.py:679
  167.3 23.9 %collective-permute-done.10.other = bf16[2,800,128]{2,1,0:T(8,128)(2,1)S(1)} collective-permute-done((bf16[2,800,128]{2,1,0:T(8,128)(2,1)S(1)}, bf16[2,800,128]{2,1,0:T(8,128)(2,1)S(1)}, u32[]{:S(2)}, u32[]{:S(2)}) %collective-permute-start.10) | collective-permute-done | bytes 409632 | tf_op jit(solution)/shard_map/ppermute | solution.py:679
  191.3 2.6 %collective-permute-start.11 = (bf16[1,800,128]{2,1,0:T(8,128)(2,1)S(1)}, bf16[1,800,128]{2,1,0:T(8,128)(2,1)S(1)}, u32[]{:S(2)}, u32[]{:S(2)}) collective-permute-start(bf16[1,800,128]{2,1,0:T(8,128)(2,1)S(1)} %get-tuple-element.92), channel_id=1, source_target_pairs={{0,16},{4,20},{8,24},{12,28},{16,0},{20,4},{24,8},{28,12},{1,17},{... | collective-permute-start | bytes 614408 | tf_op jit(solution)/shard_map/ppermute | solution.py:679
  193.9 0.6 fusion.4
  194.5 0.8 place.3.refs_0_
  195.3 1.9 place.4.refs_0_
  197.2 4.5 %collective-permute-done.11.other = bf16[1,800,128]{2,1,0:T(8,128)(2,1)S(1)} collective-permute-done((bf16[1,800,128]{2,1,0:T(8,128)(2,1)S(1)}, bf16[1,800,128]{2,1,0:T(8,128)(2,1)S(1)}, u32[]{:S(2)}, u32[]{:S(2)}) %collective-permute-start.11) | collective-permute-done | bytes 204832 | tf_op jit(solution)/shard_map/ppermute | solution.py:679
  201.7 0.9 finish.1
  202.6 1.1 place.5
  (42 shorter events, 1.7 us)
Async XLA Ops:
  1.6 8.1 %collective-permute-start = (bf16[4,8,2048]{2,1,0:T(8,128)(2,1)S(1)}, bf16[4,8,2048]{2,1,0:T(8,128)(2,1)S(1)}, u32[]{:S(2)}, u32[]{:S(2)}) collective-permute-start(bf16[4,8,2048]{2,1,0:T(8,128)(2,1)S(1)} %pad_maximum_fusion.3), channel_id=1, source_target_pairs={{0,4},{4,8},{8,12},{12,16},{16,20},{20,24},{24,28},{1,5},{5,9},{9,... | collective-permute-start | bytes 393224 | tf_op jit(solution)/shard_map/ppermute | solution.py:434
  6.5 6.9 %collective-permute-start.1 = (bf16[4,8,2048]{2,1,0:T(8,128)(2,1)S(1)}, bf16[4,8,2048]{2,1,0:T(8,128)(2,1)S(1)}, u32[]{:S(2)}, u32[]{:S(2)}) collective-permute-start(bf16[4,8,2048]{2,1,0:T(8,128)(2,1)S(1)} %pad_maximum_fusion.4), channel_id=1, source_target_pairs={{4,0},{8,4},{12,8},{16,12},{20,16},{24,20},{28,24},{5,1},{9,5},{13... | collective-permute-start | bytes 393224 | tf_op jit(solution)/shard_map/ppermute | solution.py:434
  14.1 15.3 %copy-start.2 = (bf16[1024,256]{1,0:T(8,128)(2,1)S(1)}, bf16[1024,256]{1,0:T(8,128)(2,1)}, u32[]{:S(2)}) copy-start(bf16[1024,256]{1,0:T(8,128)(2,1)} %wv.1) | copy-start | bytes 1572868
  30.6 1.1 copy-start.6
  30.6 1.1 copy-start.7
  30.7 9.1 %collective-permute-start.2 = (bf16[512,512]{1,0:T(8,128)(2,1)S(1)}, bf16[512,512]{1,0:T(8,128)(2,1)S(1)}, u32[]{:S(2)}, u32[]{:S(2)}) collective-permute-start(bf16[512,512]{1,0:T(8,128)(2,1)S(1)} %bitcast.25), channel_id=1, source_target_pairs={{0,1},{1,0},{2,3},{3,2},{4,5},{5,4},{6,7},{7,6},{8,9},{9,8},{10,11... | collective-permute-start | bytes 1572872 | tf_op jit(solution)/shard_map/ppermute | solution.py:487
  33.2 12.3 %all-to-all-start = ((f32[8,2,256]{2,1,0:T(2,128)}), f32[8,2,256]{2,1,0:T(2,128)S(1)}, u32[]{:S(2)}, u32[]{:S(2)}) async-start(f32[8,2,256]{2,1,0:T(2,128)} %get-tuple-element.52), calls=%async_computation | async-start | bytes 32768 | tf_op jit(solution)/shard_map/all_to_all | solution.py:394
  39.8 18.4 %copy-start.1 = (bf16[512,512]{1,0:T(8,128)(2,1)}, bf16[512,512]{1,0:T(8,128)(2,1)S(1)}, u32[]{:S(2)}) copy-start(bf16[512,512]{1,0:T(8,128)(2,1)S(1)} %collective-permute-done.2.w_sibling) | copy-start | bytes 1572868
  45.5 0.6 copy-start.5
  58.2 10.4 %all-to-all-start.1 = ((f32[8,2,256]{2,1,0:T(2,128)}), f32[8,2,256]{2,1,0:T(2,128)S(1)}, u32[]{:S(2)}, u32[]{:S(2)}) async-start(f32[8,2,256]{2,1,0:T(2,128)} %get-tuple-element.56), calls=%async_computation.1 | async-start | bytes 32768 | tf_op jit(solution)/shard_map/all_to_all | solution.py:394
  68.5 0.6 copy-start.3
  74.2 5.7 %collective-permute-start.3 = (bf16[1024,512]{1,0:T(8,128)(2,1)}, bf16[1024,512]{1,0:T(8,128)(2,1)}, u32[]{:S(2)}, u32[]{:S(2)}) collective-permute-start(bf16[1024,512]{1,0:T(8,128)(2,1)} %get-tuple-element.62.own.refs_0_), channel_id=1, source_target_pairs={{0,1},{1,0},{2,3},{3,2},{4,5},{5,4},{6,7},{7,6},{8,9},{9,8},{10,11... | collective-permute-start | bytes 3145736 | tf_op jit(solution)/shard_map/ppermute | solution.py:589
  79.3 15.2 %collective-permute-start.5 = (bf16[1024,512]{1,0:T(8,128)(2,1)}, bf16[1024,512]{1,0:T(8,128)(2,1)}, u32[]{:S(2)}, u32[]{:S(2)}) collective-permute-start(bf16[1024,512]{1,0:T(8,128)(2,1)} %get-tuple-element.64.own.refs_1_), channel_id=1, source_target_pairs={{0,1},{1,0},{2,3},{3,2},{4,5},{5,4},{6,7},{7,6},{8,9},{9,8},{10,11... | collective-permute-start | bytes 3145736 | tf_op jit(solution)/shard_map/ppermute | solution.py:589
  84.1 15.3 %collective-permute-start.6 = (bf16[8,1,32,1024]{3,2,1,0:T(8,128)(2,1)}, bf16[8,1,32,1024]{3,2,1,0:T(8,128)(2,1)S(1)}, u32[]{:S(2)}, u32[]{:S(2)}) collective-permute-start(bf16[8,1,32,1024]{3,2,1,0:T(8,128)(2,1)} %get-tuple-element.68), channel_id=1, source_target_pairs={{0,2},{1,3},{2,0},{3,1},{4,6},{5,7},{6,4},{7,5},{8,10},{9,11},{10,... | collective-permute-start | bytes 1572872 | tf_op jit(solution)/shard_map/ppermute | solution.py:620
  94.5 13.6 %collective-permute-start.4 = (bf16[2048,512]{1,0:T(8,128)(2,1)}, bf16[2048,512]{1,0:T(8,128)(2,1)}, u32[]{:S(2)}, u32[]{:S(2)}) collective-permute-start(bf16[2048,512]{1,0:T(8,128)(2,1)} %get-tuple-element.70.own.refs_2_), channel_id=1, source_target_pairs={{0,1},{1,0},{2,3},{3,2},{4,5},{5,4},{6,7},{7,6},{8,9},{9,8},{10,11... | collective-permute-start | bytes 6291464 | tf_op jit(solution)/shard_map/ppermute | solution.py:589
  98.8 27.4 %collective-permute-start.7 = (bf16[8,1,32,1024]{3,2,1,0:T(8,128)(2,1)}, bf16[8,1,32,1024]{3,2,1,0:T(8,128)(2,1)}, u32[]{:S(2)}, u32[]{:S(2)}) collective-permute-start(bf16[8,1,32,1024]{3,2,1,0:T(8,128)(2,1)} %get-tuple-element.73), channel_id=1, source_target_pairs={{0,2},{1,3},{2,0},{3,1},{4,6},{5,7},{6,4},{7,5},{8,10},{9,11},{10,... | collective-permute-start | bytes 1572872 | tf_op jit(solution)/shard_map/ppermute | solution.py:620
  99.3 0.8 copy-start.8
  102.1 26.1 %all-to-all-start.2 = ((bf16[8,1,32,1024]{3,2,1,0:T(8,128)(2,1)}), bf16[8,1,32,1024]{3,2,1,0:T(8,128)(2,1)S(1)}, u32[]{:S(2)}, u32[]{:S(2)}) async-start(bf16[8,1,32,1024]{3,2,1,0:T(8,128)(2,1)} %add.115), calls=%async_computation.2 | async-start | bytes 1048576 | tf_op jit(solution)/shard_map/all_to_all | solution.py:394
  114.6 25.3 %collective-permute-start.8 = (bf16[8,2,32,1024]{3,2,1,0:T(8,128)(2,1)}, bf16[8,2,32,1024]{3,2,1,0:T(8,128)(2,1)}, u32[]{:S(2)}, u32[]{:S(2)}) collective-permute-start(bf16[8,2,32,1024]{3,2,1,0:T(8,128)(2,1)} %get-tuple-element.77), channel_id=1, source_target_pairs={{0,2},{1,3},{2,0},{3,1},{4,6},{5,7},{6,4},{7,5},{8,10},{9,11},{10,... | collective-permute-start | bytes 3145736 | tf_op jit(solution)/shard_map/ppermute | solution.py:620
  128.2 31.1 %all-to-all-start.3 = ((bf16[8,1,32,1024]{3,2,1,0:T(8,128)(2,1)}), bf16[8,1,32,1024]{3,2,1,0:T(8,128)(2,1)}, u32[]{:S(2)}, u32[]{:S(2)}) async-start(bf16[8,1,32,1024]{3,2,1,0:T(8,128)(2,1)} %add.116), calls=%async_computation.3 | async-start | bytes 1048576 | tf_op jit(solution)/shard_map/all_to_all | solution.py:394
  134.2 25.1 %collective-permute-start.9 = (bf16[4,800,128]{2,1,0:T(8,128)(2,1)}, bf16[4,800,128]{2,1,0:T(8,128)(2,1)}, u32[]{:S(2)}, u32[]{:S(2)}) collective-permute-start(bf16[4,800,128]{2,1,0:T(8,128)(2,1)} %get-tuple-element.86), channel_id=1, source_target_pairs={{0,4},{4,0},{8,12},{12,8},{16,20},{20,16},{24,28},{28,24},{1,5},{5... | collective-permute-start | bytes 2457608 | tf_op jit(solution)/shard_map/ppermute | solution.py:679
  143.6 20.3 %copy-start = (bf16[4,800,128]{2,1,0:T(8,128)(2,1)S(1)}, bf16[4,800,128]{2,1,0:T(8,128)(2,1)}, u32[]{:S(2)}) copy-start(bf16[4,800,128]{2,1,0:T(8,128)(2,1)} %get-tuple-element.88.own) | copy-start | bytes 2457604
  143.6 23.7 %copy-start.4 = (f32[8,2,256]{2,1,0:T(2,128)S(1)}, f32[8,2,256]{2,1,0:T(2,128)}, u32[]{:S(2)}) copy-start(f32[8,2,256]{2,1,0:T(2,128)} %copy-done.3) | copy-start | bytes 49156
  159.3 43.2 %all-to-all-start.4 = ((bf16[8,2,32,1024]{3,2,1,0:T(8,128)(2,1)}), bf16[8,2,32,1024]{3,2,1,0:T(8,128)(2,1)S(1)}, u32[]{:S(2)}, u32[]{:S(2)}) async-start(bf16[8,2,32,1024]{3,2,1,0:T(8,128)(2,1)} %add.117), calls=%async_computation.4 | async-start | bytes 2097152 | tf_op jit(solution)/shard_map/all_to_all | solution.py:394
  165.2 26.0 %collective-permute-start.10 = (bf16[2,800,128]{2,1,0:T(8,128)(2,1)S(1)}, bf16[2,800,128]{2,1,0:T(8,128)(2,1)S(1)}, u32[]{:S(2)}, u32[]{:S(2)}) collective-permute-start(bf16[2,800,128]{2,1,0:T(8,128)(2,1)S(1)} %get-tuple-element.90), channel_id=1, source_target_pairs={{0,8},{4,12},{8,0},{12,4},{16,24},{20,28},{24,16},{28,20},{1,9},{5... | collective-permute-start | bytes 1228808 | tf_op jit(solution)/shard_map/ppermute | solution.py:679
  191.3 10.4 %collective-permute-start.11 = (bf16[1,800,128]{2,1,0:T(8,128)(2,1)S(1)}, bf16[1,800,128]{2,1,0:T(8,128)(2,1)S(1)}, u32[]{:S(2)}, u32[]{:S(2)}) collective-permute-start(bf16[1,800,128]{2,1,0:T(8,128)(2,1)S(1)} %get-tuple-element.92), channel_id=1, source_target_pairs={{0,16},{4,20},{8,24},{12,28},{16,0},{20,4},{24,8},{28,12},{1,17},{... | collective-permute-start | bytes 614408 | tf_op jit(solution)/shard_map/ppermute | solution.py:679

commit v18 on v13

--- a/solution.py
+++ b/solution.py
@@ -647,9 +647,8 @@
     grads[2], taps[2] = back(*groups[2], *parts[0])
     parts[1] = partials(*groups[1], grads[1], grads[2])
     owns[0] = deliver(parts[0], LONG, w_out_pieces, *parts[1])
+    moved[0] = exchange(owns[0], "seq")
     parts[2] = partials(*groups[2], grads[2], owns[0])
-    moved[0] = exchange(after(owns[0], *parts[2]), "seq")
-    owns[1] = deliver(parts[1], 0, *parts[2])
 
     slots = 2 * width + 16 * (width // shard)
     half = sds((seqs // 2, slots, shard), BF16)
@@ -671,14 +670,15 @@
         [pltpu.VMEM((2 * width, model), F32)],
         LONG,
         1024,
-    )(parity, after(normed, owns[1]), *grads, *taps)
-    moved[1] = exchange(after(owns[1], keep, moved[0]), "seq")
+    )(parity, after(normed, *parts[2]), *grads, *taps)
+    owns[1] = deliver(parts[1], LONG, keep)
+    moved[1] = exchange(after(owns[1], moved[0]), "seq")
+    owns[2] = deliver(parts[2], 0, owns[1])
     bit = 1
     while True:
         others = lax.ppermute(send, "seq", [(i, i ^ bit) for i in range(seqs)])
         if bit == 1:
-            owns[2] = deliver(parts[2], 0, others)
-            moved[2] = exchange(after(owns[2], moved[1]), "seq")
+            moved[2] = exchange(after(owns[2], moved[1], others), "seq")
         bit *= 2
         if bit == seqs:
             break

time: 211 us -> 198 us (0.938)
  waiting for transfers between devices: 56.9 us -> 43.5 us
    ppermute x3, waiting for transfers between devices: 38.7 us -> 29.8 us  [per_device(): others = lax.ppermute(send, 'seq', [(i, i ^ bit) for i in range(seqs)])]
    all_to_all x6, waiting for transfers between devices: 10.2 us -> 5.73 us  [exchange(): return lax.all_to_all(copies, axis, 0, 0, tiled=True)]
  transfers between devices with their start and end apart: 18 -> 18, of which waited for: 7 -> 6; matrix products, arithmetic and copies ran while one was open for 2% -> 3% of each run, Pallas kernels for 27% -> 29%
where the time goes in v18:
time: 198 us; the launch traced here: 197 us
  Pallas kernels  91.5 us (46%)
  starting transfers between devices  51.1 us (26%)
  waiting for transfers between devices  43.5 us (22%)
  other arithmetic  4.97 us (3%)
  local copies, waits for them, and re-layouts  4.23 us (2%)
    all_to_all x6, starting transfers between devices, exchange(): return lax.all_to_all(copies, axis, 0, 0, tiled=True)  31.5 us
    ppermute x3, waiting for transfers between devices, per_device(): others = lax.ppermute(send, 'seq', [(i, i ^ bit) for i in range(seqs)])  29.8 us
    pallas_call x3, Pallas kernels, back(): call(functools.partial(back_kernel, first, blocks), 'back_conv', (size *...  19 us
    pallas_call x1, Pallas kernels, per_device(): call(gate_kernel, 'gate_conv', (recs,), [smem(), per_record((frames, mode...  15.3 us
    pallas_call x3, Pallas kernels, partials(): call(partial_kernel, 'partial_in', (size * parts_in,), [pl.BlockSpec((hal...  15.1 us
    pallas_call x1, Pallas kernels, per_device(): call(norm_kernel, 'swish_norm', (recs,), [smem(), smem(), whole((seqs, 2,...  12.1 us
    pallas_call x1, Pallas kernels, per_device(): call(functools.partial(outer_kernel, groups), 'outer_w_in', (recs,), [sme...  9.54 us
    ppermute x3, starting transfers between devices, per_device(): others = lax.ppermute(send, 'seq', [(i, i ^ bit) for i in range(seqs)])  9.28 us
  transfers between devices with their start and end apart: 18, of which 6 were waited for; matrix products, arithmetic and copies ran while one was open for 3% of the time, Pallas kernels for 29%

profile of v18, /device:TPU:0, one launch (start us, length us, event | category | flops | bytes accessed | tf_op | source)
XLA Modules:
  0.0 196.9 jit_solution(1817521465084434799)
XLA Ops:
  0.6 1.0 fusion.1
  1.6 4.9 %collective-permute-start = (bf16[4,8,2048]{2,1,0:T(8,128)(2,1)S(1)}, bf16[4,8,2048]{2,1,0:T(8,128)(2,1)S(1)}, u32[]{:S(2)}, u32[]{:S(2)}) collective-permute-start(bf16[4,8,2048]{2,1,0:T(8,128)(2,1)S(1)} %pad_maximum_fusion.3), channel_id=1, source_target_pairs={{0,4},{4,8},{8,12},{12,16},{16,20},{20,24},{24,28},{1,5},{5,9},{9,... | collective-permute-start | bytes 393224 | tf_op jit(solution)/shard_map/ppermute | solution.py:433
  6.5 1.3 collective-permute-start.1
  7.8 1.3 fusion.5
  9.1 0.6 stack.35.meta
  9.7 3.7 %collective-permute-done.1 = bf16[4,8,2048]{2,1,0:T(8,128)(2,1)S(1)} collective-permute-done((bf16[4,8,2048]{2,1,0:T(8,128)(2,1)S(1)}, bf16[4,8,2048]{2,1,0:T(8,128)(2,1)S(1)}, u32[]{:S(2)}, u32[]{:S(2)}) %collective-permute-start.1) | collective-permute-done | bytes 131104 | tf_op jit(solution)/shard_map/ppermute | solution.py:433
  13.4 0.7 fusion.3
  14.1 15.3 %gate_conv.1 = (f32[4,1024,256]{2,1,0:T(8,128)}, f32[4,1024,256]{2,1,0:T(8,128)}, f32[4,1040,256]{2,1,0:T(8,128)}, f32[8,2,256]{2,1,0:T(2,128)}) custom-call(s32[2,4]{1,0:T(2,128)} %stack.35.meta, bf16[4,1024,1024]{2,1,0:T(8,128)(2,1)} %x.4, bf16[4,16,1024]{2,1,0:T(8,128)(2,1)} %get-tuple-element.106.halo, bf16[1024,256]{1,0:T(8,128)(2,1)} %wv.1, ...), custom_call_target="tpu_custom_call" | custom-call | flops 4294967296 | bytes 20971520 | tf_op jit(solution)/shard_map/gate_conv/pallas_call | solution.py:447
  29.4 1.1 pad_maximum_fusion
  31.6 0.6 pad_maximum_fusion.5.affine
  32.2 0.9 fusion.select
  33.2 5.7 %all-to-all-start = ((f32[8,2,256]{2,1,0:T(2,128)}), f32[8,2,256]{2,1,0:T(2,128)S(1)}, u32[]{:S(2)}, u32[]{:S(2)}) async-start(f32[8,2,256]{2,1,0:T(2,128)} %get-tuple-element.52), calls=%async_computation | async-start | bytes 32768 | tf_op jit(solution)/shard_map/all_to_all | solution.py:393
  38.9 0.9 pad_maximum_fusion.1
  39.8 5.7 %all-to-all-done.stats = f32[8,2,256]{2,1,0:T(2,128)S(1)} async-done(((f32[8,2,256]{2,1,0:T(2,128)}), f32[8,2,256]{2,1,0:T(2,128)S(1)}, u32[]{:S(2)}, u32[]{:S(2)}) %all-to-all-start) | async-done | bytes 16416 | tf_op jit(solution)/shard_map/all_to_all | solution.py:393
  45.5 0.6 copy-done.6
  46.1 12.1 %swish_norm.1 = (bf16[4,1024,256]{2,1,0:T(8,128)(2,1)}, f32[4,1040,256]{2,1,0:T(8,128)}, bf16[4,256,1024]{2,1,0:T(8,128)(2,1)}, f32[8,2,256]{2,1,0:T(2,128)}) custom-call(s32[2,4]{1,0:T(2,128)} %stack.35.meta, f32[1,1]{1,0:T(1,128)} %bitcast.1.count, f32[8,2,256]{2,1,0:T(2,128)} %copy-done.6, f32[2,256]{1,0:T(2,128)} %pad_maximum_fusion.5.affine, ...), custom_call_target="tpu_custom_call" | custom-call | flops 4294967296 | bytes 20971520 | tf_op jit(solution)/shard_map/swish_norm/pallas_call | solution.py:492
  58.1 3.3 %all-to-all-start.1 = ((f32[8,2,256]{2,1,0:T(2,128)}), f32[8,2,256]{2,1,0:T(2,128)S(1)}, u32[]{:S(2)}, u32[]{:S(2)}) async-start(f32[8,2,256]{2,1,0:T(2,128)} %get-tuple-element.56), calls=%async_computation.1 | async-start | bytes 32768 | tf_op jit(solution)/shard_map/all_to_all | solution.py:393
  61.5 6.7 %outer_w_out.1 = bf16[8,256,128]{2,1,0:T(8,128)(2,1)} custom-call(bf16[4,1024,1024]{2,1,0:T(8,128)(2,1)} %grads.3, bf16[4,1024,256]{2,1,0:T(8,128)(2,1)} %get-tuple-element.60.swished), custom_call_target="tpu_custom_call" | custom-call | flops 2147483648 | bytes 8388608 | tf_op jit(solution)/shard_map/outer_w_out/pallas_call | solution.py:537
  68.2 0.6 copy-done.4
  68.8 5.0 %back_conv.3 = (bf16[1024,512]{1,0:T(8,128)(2,1)}, f32[16,256]{1,0:T(8,128)}) custom-call(s32[2,4]{1,0:T(2,128)} %stack.35.meta, f32[1,1]{1,0:T(1,128)} %bitcast.1.count, f32[8,2,256]{2,1,0:T(2,128)} %copy-done.6, f32[8,2,256]{2,1,0:T(2,128)} %copy-done.4, f32[1,256]{1,0:T(1,128)} %bitcast.26, f32[4,1040,256]{2,1,0:T(8,128)} %get-tuple-element.57.gn, ...), custom_call_target="tpu_custom_call" | custom-call | bytes 1024 | tf_op jit(solution)/shard_map/back_conv/pallas_call | solution.py:561
  73.9 5.1 %back_conv.4 = (bf16[1024,512]{1,0:T(8,128)(2,1)}, f32[16,256]{1,0:T(8,128)}) custom-call(s32[2,4]{1,0:T(2,128)} %stack.35.meta, f32[1,1]{1,0:T(1,128)} %bitcast.1.count, f32[8,2,256]{2,1,0:T(2,128)} %copy-done.6, f32[8,2,256]{2,1,0:T(2,128)} %copy-done.4, f32[1,256]{1,0:T(1,128)} %bitcast.27, f32[4,1040,256]{2,1,0:T(8,128)} %get-tuple-element.57.gn, ...), custom_call_target="tpu_custom_call" | custom-call | bytes 1024 | tf_op jit(solution)/shard_map/back_conv/pallas_call | solution.py:561
  79.5 5.9 %all-to-all-start.2 = ((bf16[8,256,128]{2,1,0:T(8,128)(2,1)}), bf16[8,256,128]{2,1,0:T(8,128)(2,1)S(1)}, u32[]{:S(2)}, u32[]{:S(2)}) async-start(bf16[8,256,128]{2,1,0:T(8,128)(2,1)} %outer_w_out.1), calls=%async_computation.2 | async-start | bytes 1048576 | tf_op jit(solution)/shard_map/all_to_all | solution.py:393
  85.5 4.3 %partial_in.3 = (bf16[8,1,32,1024]{3,2,1,0:T(8,128)(2,1)}, bf16[8,1,32,1024]{3,2,1,0:T(8,128)(2,1)}) custom-call(bf16[1024,512]{1,0:T(8,128)(2,1)} %get-tuple-element.62.own.refs_0_, bf16[1024,512]{1,0:T(8,128)(2,1)} %collective-permute-done.3.sibling, bf16[512,512]{1,0:T(8,128)(2,1)} %bitcast.21, bf16[512,512]{1,0:T(8,128)(2,1)} %collective-permute-done.2.w_sibling, ...), custom_call_target="tpu_custom_call" | custom-call | bytes 1024 | tf_op jit(solution)/shard_map/partial_in/pallas_call | solution.py:590
  89.7 1.5 collective-permute-start.6
  91.2 8.9 %back_conv.5 = (bf16[2048,512]{1,0:T(8,128)(2,1)}, f32[16,256]{1,0:T(8,128)}) custom-call(s32[2,4]{1,0:T(2,128)} %stack.35.meta, f32[1,1]{1,0:T(1,128)} %bitcast.1.count, f32[8,2,256]{2,1,0:T(2,128)} %copy-done.6, f32[8,2,256]{2,1,0:T(2,128)} %copy-done.4, f32[1,256]{1,0:T(1,128)} %bitcast.28, f32[4,1040,256]{2,1,0:T(8,128)} %get-tuple-element.57.gn, ...), custom_call_target="tpu_custom_call" | custom-call | bytes 1024 | tf_op jit(solution)/shard_map/back_conv/pallas_call | solution.py:561
  100.2 4.3 %partial_in.4 = (bf16[8,1,32,1024]{3,2,1,0:T(8,128)(2,1)}, bf16[8,1,32,1024]{3,2,1,0:T(8,128)(2,1)}) custom-call(bf16[1024,512]{1,0:T(8,128)(2,1)} %get-tuple-element.64.own.refs_1_, bf16[1024,512]{1,0:T(8,128)(2,1)} %collective-permute-done.5.sibling, bf16[512,512]{1,0:T(8,128)(2,1)} %bitcast.22, bf16[512,512]{1,0:T(8,128)(2,1)} %collective-permute-done.2.w_sibling, ...), custom_call_target="tpu_custom_call" | custom-call | bytes 1024 | tf_op jit(solution)/shard_map/partial_in/pallas_call | solution.py:590
  105.0 2.2 %add.115 = bf16[8,1,32,1024]{3,2,1,0:T(8,128)(2,1)} custom-call(bf16[8,1,32,1024]{3,2,1,0:T(8,128)(2,1)} %get-tuple-element.74.refs_0_, bf16[8,1,32,1024]{3,2,1,0:T(8,128)(2,1)} %collective-permute-done.6.refs_1_), custom_call_target="tpu_custom_call" | custom-call | flops 49999998976 | bytes 1024 | tf_op jit(solution)/shard_map/add/pallas_call | solution.py:624
  107.2 6.0 %all-to-all-start.3 = ((bf16[8,1,32,1024]{3,2,1,0:T(8,128)(2,1)}), bf16[8,1,32,1024]{3,2,1,0:T(8,128)(2,1)S(1)}, u32[]{:S(2)}, u32[]{:S(2)}) async-start(bf16[8,1,32,1024]{3,2,1,0:T(8,128)(2,1)} %add.115), calls=%async_computation.3 | async-start | bytes 1048576 | tf_op jit(solution)/shard_map/all_to_all | solution.py:393
  113.2 6.5 %partial_in.5 = (bf16[8,2,32,1024]{3,2,1,0:T(8,128)(2,1)}, bf16[8,2,32,1024]{3,2,1,0:T(8,128)(2,1)}) custom-call(bf16[2048,512]{1,0:T(8,128)(2,1)} %get-tuple-element.70.own.refs_2_, bf16[2048,512]{1,0:T(8,128)(2,1)} %collective-permute-done.4.sibling, bf16[512,512]{1,0:T(8,128)(2,1)} %bitcast.23, bf16[512,512]{1,0:T(8,128)(2,1)} %collective-permute-done.2.w_sibling, ...), custom_call_target="tpu_custom_call" | custom-call | bytes 1024 | tf_op jit(solution)/shard_map/partial_in/pallas_call | solution.py:590
  119.7 1.5 collective-permute-start.8
  121.2 9.5 %outer_w_in.1 = (bf16[4,544,128]{2,1,0:T(8,128)(2,1)}, bf16[4,544,128]{2,1,0:T(8,128)(2,1)}) custom-call(s32[1,1]{1,0:T(1,128)} %bitcast.11.parity, bf16[4,1024,1024]{2,1,0:T(8,128)(2,1)} %x.4, bf16[1024,512]{1,0:T(8,128)(2,1)} %get-tuple-element.62.own.refs_0_, bf16[1024,512]{1,0:T(8,128)(2,1)} %get-tuple-element.64.own.refs_1_, ...), custom_call_target="tpu_custom_call" | custom-call | flops 49999998976 | bytes 1024 | tf_op jit(solution)/shard_map/outer_w_in/pallas_call | solution.py:655
  130.7 2.0 %add.116 = bf16[8,1,32,1024]{3,2,1,0:T(8,128)(2,1)} custom-call(bf16[8,1,32,1024]{3,2,1,0:T(8,128)(2,1)} %get-tuple-element.83.refs_0_, bf16[8,1,32,1024]{3,2,1,0:T(8,128)(2,1)} %collective-permute-done.7.refs_1_), custom_call_target="tpu_custom_call" | custom-call | flops 49999998976 | bytes 1024 | tf_op jit(solution)/shard_map/add/pallas_call | solution.py:624
  132.7 6.0 %all-to-all-start.4 = ((bf16[8,1,32,1024]{3,2,1,0:T(8,128)(2,1)}), bf16[8,1,32,1024]{3,2,1,0:T(8,128)(2,1)}, u32[]{:S(2)}, u32[]{:S(2)}) async-start(bf16[8,1,32,1024]{3,2,1,0:T(8,128)(2,1)} %add.116), calls=%async_computation.4 | async-start | bytes 1048576 | tf_op jit(solution)/shard_map/all_to_all | solution.py:393
  138.7 2.0 %collective-permute-start.9 = (bf16[4,544,128]{2,1,0:T(8,128)(2,1)}, bf16[4,544,128]{2,1,0:T(8,128)(2,1)}, u32[]{:S(2)}, u32[]{:S(2)}) collective-permute-start(bf16[4,544,128]{2,1,0:T(8,128)(2,1)} %get-tuple-element.86), channel_id=1, source_target_pairs={{0,4},{4,0},{8,12},{12,8},{16,20},{20,16},{24,28},{28,24},{1,5},{5... | collective-permute-start | bytes 1671176 | tf_op jit(solution)/shard_map/ppermute | solution.py:679
  140.7 4.3 %collective-permute-done.8.refs_1_ = bf16[8,2,32,1024]{3,2,1,0:T(8,128)(2,1)} collective-permute-done((bf16[8,2,32,1024]{3,2,1,0:T(8,128)(2,1)}, bf16[8,2,32,1024]{3,2,1,0:T(8,128)(2,1)}, u32[]{:S(2)}, u32[]{:S(2)}) %collective-permute-start.8) | collective-permute-done | bytes 1048608 | tf_op jit(solution)/shard_map/ppermute | solution.py:619
  145.0 3.7 %add.117 = bf16[8,2,32,1024]{3,2,1,0:T(8,128)(2,1)} custom-call(bf16[8,2,32,1024]{3,2,1,0:T(8,128)(2,1)} %get-tuple-element.84.refs_0_, bf16[8,2,32,1024]{3,2,1,0:T(8,128)(2,1)} %collective-permute-done.8.refs_1_), custom_call_target="tpu_custom_call" | custom-call | bytes 1024 | tf_op jit(solution)/shard_map/add/pallas_call | solution.py:624
  148.7 9.5 %collective-permute-done.9.other = bf16[4,544,128]{2,1,0:T(8,128)(2,1)} collective-permute-done((bf16[4,544,128]{2,1,0:T(8,128)(2,1)}, bf16[4,544,128]{2,1,0:T(8,128)(2,1)}, u32[]{:S(2)}, u32[]{:S(2)}) %collective-permute-start.9) | collective-permute-done | bytes 557088 | tf_op jit(solution)/shard_map/ppermute | solution.py:679
  158.2 4.5 %all-to-all-start.5 = ((bf16[8,2,32,1024]{3,2,1,0:T(8,128)(2,1)}), bf16[8,2,32,1024]{3,2,1,0:T(8,128)(2,1)S(1)}, u32[]{:S(2)}, u32[]{:S(2)}) async-start(bf16[8,2,32,1024]{3,2,1,0:T(8,128)(2,1)} %add.117), calls=%async_computation.5 | async-start | bytes 2097152 | tf_op jit(solution)/shard_map/all_to_all | solution.py:393
  162.8 1.2 fold.2
  164.0 2.1 %collective-permute-start.10 = (bf16[2,544,128]{2,1,0:T(8,128)(2,1)S(1)}, bf16[2,544,128]{2,1,0:T(8,128)(2,1)S(1)}, u32[]{:S(2)}, u32[]{:S(2)}) collective-permute-start(bf16[2,544,128]{2,1,0:T(8,128)(2,1)S(1)} %get-tuple-element.90), channel_id=1, source_target_pairs={{0,8},{4,12},{8,0},{12,4},{16,24},{20,28},{24,16},{28,20},{1,9},{5... | collective-permute-start | bytes 835592 | tf_op jit(solution)/shard_map/ppermute | solution.py:679
  166.1 19.0 %collective-permute-done.10.other = bf16[2,544,128]{2,1,0:T(8,128)(2,1)S(1)} collective-permute-done((bf16[2,544,128]{2,1,0:T(8,128)(2,1)S(1)}, bf16[2,544,128]{2,1,0:T(8,128)(2,1)S(1)}, u32[]{:S(2)}, u32[]{:S(2)}) %collective-permute-start.10) | collective-permute-done | bytes 278560 | tf_op jit(solution)/shard_map/ppermute | solution.py:679
  185.2 5.2 %collective-permute-start.11 = (bf16[1,544,128]{2,1,0:T(8,128)(2,1)S(1)}, bf16[1,544,128]{2,1,0:T(8,128)(2,1)S(1)}, u32[]{:S(2)}, u32[]{:S(2)}) collective-permute-start(bf16[1,544,128]{2,1,0:T(8,128)(2,1)S(1)} %get-tuple-element.92), channel_id=1, source_target_pairs={{0,16},{4,20},{8,24},{12,28},{16,0},{20,4},{24,8},{28,12},{1,17},{... | collective-permute-start | bytes 417800 | tf_op jit(solution)/shard_map/ppermute | solution.py:679
  190.3 0.6 fusion.4
  190.9 0.8 place.3.refs_0_
  191.7 1.9 place.4.refs_0_
  193.7 1.3 collective-permute-done.11.other
  194.9 0.8 finish.1
  195.8 1.1 place.5
  (44 shorter events, 1.7 us)
Async XLA Ops:
  1.6 8.1 %collective-permute-start = (bf16[4,8,2048]{2,1,0:T(8,128)(2,1)S(1)}, bf16[4,8,2048]{2,1,0:T(8,128)(2,1)S(1)}, u32[]{:S(2)}, u32[]{:S(2)}) collective-permute-start(bf16[4,8,2048]{2,1,0:T(8,128)(2,1)S(1)} %pad_maximum_fusion.3), channel_id=1, source_target_pairs={{0,4},{4,8},{8,12},{12,16},{16,20},{20,24},{24,28},{1,5},{5,9},{9,... | collective-permute-start | bytes 393224 | tf_op jit(solution)/shard_map/ppermute | solution.py:433
  6.5 6.9 %collective-permute-start.1 = (bf16[4,8,2048]{2,1,0:T(8,128)(2,1)S(1)}, bf16[4,8,2048]{2,1,0:T(8,128)(2,1)S(1)}, u32[]{:S(2)}, u32[]{:S(2)}) collective-permute-start(bf16[4,8,2048]{2,1,0:T(8,128)(2,1)S(1)} %pad_maximum_fusion.4), channel_id=1, source_target_pairs={{4,0},{8,4},{12,8},{16,12},{20,16},{24,20},{28,24},{5,1},{9,5},{13... | collective-permute-start | bytes 393224 | tf_op jit(solution)/shard_map/ppermute | solution.py:433
  14.1 15.3 %copy-start.3 = (bf16[1024,256]{1,0:T(8,128)(2,1)S(1)}, bf16[1024,256]{1,0:T(8,128)(2,1)}, u32[]{:S(2)}) copy-start(bf16[1024,256]{1,0:T(8,128)(2,1)} %wv.1) | copy-start | bytes 1572868
  30.6 1.1 copy-start.7
  30.6 1.1 copy-start.8
  30.7 9.0 %collective-permute-start.2 = (bf16[512,512]{1,0:T(8,128)(2,1)S(1)}, bf16[512,512]{1,0:T(8,128)(2,1)}, u32[]{:S(2)}, u32[]{:S(2)}) collective-permute-start(bf16[512,512]{1,0:T(8,128)(2,1)S(1)} %bitcast.25), channel_id=1, source_target_pairs={{0,1},{1,0},{2,3},{3,2},{4,5},{5,4},{6,7},{7,6},{8,9},{9,8},{10,11... | collective-permute-start | bytes 1572872 | tf_op jit(solution)/shard_map/ppermute | solution.py:486
  33.2 12.3 %all-to-all-start = ((f32[8,2,256]{2,1,0:T(2,128)}), f32[8,2,256]{2,1,0:T(2,128)S(1)}, u32[]{:S(2)}, u32[]{:S(2)}) async-start(f32[8,2,256]{2,1,0:T(2,128)} %get-tuple-element.52), calls=%async_computation | async-start | bytes 32768 | tf_op jit(solution)/shard_map/all_to_all | solution.py:393
  45.5 0.6 copy-start.6
  58.1 10.1 %all-to-all-start.1 = ((f32[8,2,256]{2,1,0:T(2,128)}), f32[8,2,256]{2,1,0:T(2,128)S(1)}, u32[]{:S(2)}, u32[]{:S(2)}) async-start(f32[8,2,256]{2,1,0:T(2,128)} %get-tuple-element.56), calls=%async_computation.1 | async-start | bytes 32768 | tf_op jit(solution)/shard_map/all_to_all | solution.py:393
  68.2 0.6 copy-start.4
  73.9 11.6 %collective-permute-start.3 = (bf16[1024,512]{1,0:T(8,128)(2,1)}, bf16[1024,512]{1,0:T(8,128)(2,1)}, u32[]{:S(2)}, u32[]{:S(2)}) collective-permute-start(bf16[1024,512]{1,0:T(8,128)(2,1)} %get-tuple-element.62.own.refs_0_), channel_id=1, source_target_pairs={{0,1},{1,0},{2,3},{3,2},{4,5},{5,4},{6,7},{7,6},{8,9},{9,8},{10,11... | collective-permute-start | bytes 3145736 | tf_op jit(solution)/shard_map/ppermute | solution.py:588
  79.0 21.1 %collective-permute-start.5 = (bf16[1024,512]{1,0:T(8,128)(2,1)}, bf16[1024,512]{1,0:T(8,128)(2,1)}, u32[]{:S(2)}, u32[]{:S(2)}) collective-permute-start(bf16[1024,512]{1,0:T(8,128)(2,1)} %get-tuple-element.64.own.refs_1_), channel_id=1, source_target_pairs={{0,1},{1,0},{2,3},{3,2},{4,5},{5,4},{6,7},{7,6},{8,9},{9,8},{10,11... | collective-permute-start | bytes 3145736 | tf_op jit(solution)/shard_map/ppermute | solution.py:588
  79.5 25.5 %all-to-all-start.2 = ((bf16[8,256,128]{2,1,0:T(8,128)(2,1)}), bf16[8,256,128]{2,1,0:T(8,128)(2,1)S(1)}, u32[]{:S(2)}, u32[]{:S(2)}) async-start(bf16[8,256,128]{2,1,0:T(8,128)(2,1)} %outer_w_out.1), calls=%async_computation.2 | async-start | bytes 1048576 | tf_op jit(solution)/shard_map/all_to_all | solution.py:393
  89.7 15.3 %collective-permute-start.6 = (bf16[8,1,32,1024]{3,2,1,0:T(8,128)(2,1)}, bf16[8,1,32,1024]{3,2,1,0:T(8,128)(2,1)}, u32[]{:S(2)}, u32[]{:S(2)}) collective-permute-start(bf16[8,1,32,1024]{3,2,1,0:T(8,128)(2,1)} %get-tuple-element.68), channel_id=1, source_target_pairs={{0,2},{1,3},{2,0},{3,1},{4,6},{5,7},{6,4},{7,5},{8,10},{9,11},{10,... | collective-permute-start | bytes 1572872 | tf_op jit(solution)/shard_map/ppermute | solution.py:619
  100.1 13.1 %collective-permute-start.4 = (bf16[2048,512]{1,0:T(8,128)(2,1)}, bf16[2048,512]{1,0:T(8,128)(2,1)}, u32[]{:S(2)}, u32[]{:S(2)}) collective-permute-start(bf16[2048,512]{1,0:T(8,128)(2,1)} %get-tuple-element.70.own.refs_2_), channel_id=1, source_target_pairs={{0,1},{1,0},{2,3},{3,2},{4,5},{5,4},{6,7},{7,6},{8,9},{9,8},{10,11... | collective-permute-start | bytes 6291464 | tf_op jit(solution)/shard_map/ppermute | solution.py:588
  104.5 26.2 %collective-permute-start.7 = (bf16[8,1,32,1024]{3,2,1,0:T(8,128)(2,1)}, bf16[8,1,32,1024]{3,2,1,0:T(8,128)(2,1)}, u32[]{:S(2)}, u32[]{:S(2)}) collective-permute-start(bf16[8,1,32,1024]{3,2,1,0:T(8,128)(2,1)} %get-tuple-element.73), channel_id=1, source_target_pairs={{0,2},{1,3},{2,0},{3,1},{4,6},{5,7},{6,4},{7,5},{8,10},{9,11},{10,... | collective-permute-start | bytes 1572872 | tf_op jit(solution)/shard_map/ppermute | solution.py:619
  105.0 2.2 %copy-start = (bf16[8,256,128]{2,1,0:T(8,128)(2,1)}, bf16[8,256,128]{2,1,0:T(8,128)(2,1)S(1)}, u32[]{:S(2)}) copy-start(bf16[8,256,128]{2,1,0:T(8,128)(2,1)S(1)} %all-to-all-done.2.pieces) | copy-start | bytes 1572868
  107.2 25.5 %all-to-all-start.3 = ((bf16[8,1,32,1024]{3,2,1,0:T(8,128)(2,1)}), bf16[8,1,32,1024]{3,2,1,0:T(8,128)(2,1)S(1)}, u32[]{:S(2)}, u32[]{:S(2)}) async-start(bf16[8,1,32,1024]{3,2,1,0:T(8,128)(2,1)} %add.115), calls=%async_computation.3 | async-start | bytes 1048576 | tf_op jit(solution)/shard_map/all_to_all | solution.py:393
  119.7 25.3 %collective-permute-start.8 = (bf16[8,2,32,1024]{3,2,1,0:T(8,128)(2,1)}, bf16[8,2,32,1024]{3,2,1,0:T(8,128)(2,1)}, u32[]{:S(2)}, u32[]{:S(2)}) collective-permute-start(bf16[8,2,32,1024]{3,2,1,0:T(8,128)(2,1)} %get-tuple-element.77), channel_id=1, source_target_pairs={{0,2},{1,3},{2,0},{3,1},{4,6},{5,7},{6,4},{7,5},{8,10},{9,11},{10,... | collective-permute-start | bytes 3145736 | tf_op jit(solution)/shard_map/ppermute | solution.py:619
  132.7 25.5 %all-to-all-start.4 = ((bf16[8,1,32,1024]{3,2,1,0:T(8,128)(2,1)}), bf16[8,1,32,1024]{3,2,1,0:T(8,128)(2,1)}, u32[]{:S(2)}, u32[]{:S(2)}) async-start(bf16[8,1,32,1024]{3,2,1,0:T(8,128)(2,1)} %add.116), calls=%async_computation.4 | async-start | bytes 1048576 | tf_op jit(solution)/shard_map/all_to_all | solution.py:393
  138.7 19.5 %collective-permute-start.9 = (bf16[4,544,128]{2,1,0:T(8,128)(2,1)}, bf16[4,544,128]{2,1,0:T(8,128)(2,1)}, u32[]{:S(2)}, u32[]{:S(2)}) collective-permute-start(bf16[4,544,128]{2,1,0:T(8,128)(2,1)} %get-tuple-element.86), channel_id=1, source_target_pairs={{0,4},{4,0},{8,12},{12,8},{16,20},{20,16},{24,28},{28,24},{1,5},{5... | collective-permute-start | bytes 1671176 | tf_op jit(solution)/shard_map/ppermute | solution.py:679
  148.7 14.1 %copy-start.2 = (bf16[4,544,128]{2,1,0:T(8,128)(2,1)S(1)}, bf16[4,544,128]{2,1,0:T(8,128)(2,1)}, u32[]{:S(2)}) copy-start(bf16[4,544,128]{2,1,0:T(8,128)(2,1)} %get-tuple-element.88.own) | copy-start | bytes 1671172
  148.7 17.3 %copy-start.5 = (f32[8,2,256]{2,1,0:T(2,128)S(1)}, f32[8,2,256]{2,1,0:T(2,128)}, u32[]{:S(2)}) copy-start(f32[8,2,256]{2,1,0:T(2,128)} %copy-done.4) | copy-start | bytes 49156
  158.2 37.6 %all-to-all-start.5 = ((bf16[8,2,32,1024]{3,2,1,0:T(8,128)(2,1)}), bf16[8,2,32,1024]{3,2,1,0:T(8,128)(2,1)S(1)}, u32[]{:S(2)}, u32[]{:S(2)}) async-start(bf16[8,2,32,1024]{3,2,1,0:T(8,128)(2,1)} %add.117), calls=%async_computation.5 | async-start | bytes 2097152 | tf_op jit(solution)/shard_map/all_to_all | solution.py:393
  164.0 21.1 %collective-permute-start.10 = (bf16[2,544,128]{2,1,0:T(8,128)(2,1)S(1)}, bf16[2,544,128]{2,1,0:T(8,128)(2,1)S(1)}, u32[]{:S(2)}, u32[]{:S(2)}) collective-permute-start(bf16[2,544,128]{2,1,0:T(8,128)(2,1)S(1)} %get-tuple-element.90), channel_id=1, source_target_pairs={{0,8},{4,12},{8,0},{12,4},{16,24},{20,28},{24,16},{28,20},{1,9},{5... | collective-permute-start | bytes 835592 | tf_op jit(solution)/shard_map/ppermute | solution.py:679
  185.2 9.8 %collective-permute-start.11 = (bf16[1,544,128]{2,1,0:T(8,128)(2,1)S(1)}, bf16[1,544,128]{2,1,0:T(8,128)(2,1)S(1)}, u32[]{:S(2)}, u32[]{:S(2)}) collective-permute-start(bf16[1,544,128]{2,1,0:T(8,128)(2,1)S(1)} %get-tuple-element.92), channel_id=1, source_target_pairs={{0,16},{4,20},{8,24},{12,28},{16,0},{20,4},{24,8},{28,12},{1,17},{... | collective-permute-start | bytes 417800 | tf_op jit(solution)/shard_map/ppermute | solution.py:679
  191.7 3.2 %copy-start.1 = (bf16[8,256,128]{2,1,0:T(8,128)(2,1)S(1)}, bf16[8,256,128]{2,1,0:T(8,128)(2,1)}, u32[]{:S(2)}) copy-start(bf16[8,256,128]{2,1,0:T(8,128)(2,1)} %copy-done) | copy-start | bytes 1572868

commit v19 on v18

--- a/solution.py
+++ b/solution.py
@@ -227,7 +227,7 @@
     kernel = taps.shape[0]
     margin = (kernel - 1) // 2
     cb = block_rows(span, 144)
-    step = block_rows(frames, 64)
+    step = block_rows(frames, 32)
     total_frames = count[0, 0]
     centre, inv = batch_norm(stats, total_frames)
     grad_sums = jnp.sum(sums[...], axis=0)
@@ -291,6 +291,18 @@
         )
 
 
+def join_kernel(half, *refs):
+    i = pl.program_id(0)
+
+    @pl.when(i < half)
+    def _():
+        add_kernel(*refs[:-2], refs[-1])
+
+    @pl.when(i >= half)
+    def _():
+        refs[-1][...] = refs[-2][...]
+
+
 def add_kernel(*refs):
     total = refs[0][...].astype(F32)
     for other in refs[1:-1]:
@@ -305,9 +317,13 @@
 
     @pl.when(r == pl.num_programs(0) - 1)
     def _():
-        shard = out.shape[2]
-        for s in range(out.shape[0]):
-            out[s] = acc[:, s * shard : (s + 1) * shard].astype(BF16)
+        seqs, _, piece, frames = out.shape
+        shard = acc.shape[1] // seqs
+        for s in range(seqs):
+            for q in range(frames // shard):
+                out[s, 0, :, q * shard : (q + 1) * shard] = acc[
+                    q * piece : (q + 1) * piece, s * shard : (s + 1) * shard
+                ].astype(BF16)
 
 
 def outer_kernel(groups, parity, x, *refs):
@@ -377,7 +393,11 @@
 
     value[...] = total(0, width).T
     gate[...] = total(width, width).T
-    out[...] = jnp.sum(pieces[...].astype(F32), axis=0).T
+    ready = pieces[0, 0].astype(F32)
+    for s in range(1, pieces.shape[0]):
+        ready = ready + pieces[s, 0].astype(F32)
+    blocks = [ready[:, q * shard : (q + 1) * shard] for q in range(ready.shape[1] // shard)]
+    out[...] = jnp.concatenate(blocks, axis=0).T
     for q in range(width // shard):
         taps[:, q * shard : (q + 1) * shard] = total(2 * width + 16 * q, 16)[:kernel]
 
@@ -539,8 +559,8 @@
         "outer_w_out",
         (recs,),
         [per_record((frames, model)), per_record((frames, width))],
-        whole((seqs, width, shard)),
-        sds((seqs, width, shard), BF16),
+        whole((seqs, 1, piece, frames)),
+        sds((seqs, 1, piece, frames), BF16),
         [pltpu.VMEM((width, model), F32)],
         matmul,
         input_bytes,
@@ -612,7 +632,7 @@
             1024,
         )(mine, sibling, after(w_own, *earlier), w_sibling, picked)
 
-    def deliver(part, weight, *earlier):
+    def deliver(part, weight, *earlier, extra=None):
         arrived = []
         for d in range(1, chips):
             send = [(i, ((i // 2 + d) % chips) * 2 + i % 2) for i in range(tps)]
@@ -621,18 +641,30 @@
         block = pl.BlockSpec(
             (seqs, 1, piece, half_rows), lambda i: (0, i // parts_in, 0, i % parts_in)
         )
-        own = call(
-            add_kernel,
-            "add",
-            (size * parts_in,),
-            [block] * chips,
+        if extra is None:
+            return call(
+                add_kernel,
+                "add",
+                (size * parts_in,),
+                [block] * chips,
+                block,
+                sds(part[0].shape, BF16),
+                [],
+                weight,
+                1024,
+            )(after(part[0], *earlier), *arrived)
+        one = pl.BlockSpec((seqs, 1, piece, half_rows), lambda i: (0, 0, 0, i % parts_in))
+        return call(
+            functools.partial(join_kernel, parts_in),
+            "add_join",
+            (2 * parts_in,),
+            [one] * (chips + 1),
             block,
-            sds(part[0].shape, BF16),
+            sds((seqs, 2, piece, frames), BF16),
             [],
             weight,
             1024,
-        )(after(part[0], *earlier), *arrived)
-        return own
+        )(after(part[0], *earlier), *arrived, extra)
 
     groups = ((0, 1), (1, 1), (2, recs - 2))
     grads = [None] * 3
@@ -640,13 +672,12 @@
     parts = [None] * 3
     owns = [None] * 3
     moved = [None] * 3
-    w_out_pieces = exchange(w_out, "seq")
     grads[0], taps[0] = back(*groups[0], w_out)
     grads[1], taps[1] = back(*groups[1], grads[0])
     parts[0] = partials(*groups[0], grads[0], grads[1])
     grads[2], taps[2] = back(*groups[2], *parts[0])
     parts[1] = partials(*groups[1], grads[1], grads[2])
-    owns[0] = deliver(parts[0], LONG, w_out_pieces, *parts[1])
+    owns[0] = deliver(parts[0], LONG, *parts[1], extra=w_out)
     moved[0] = exchange(owns[0], "seq")
     parts[2] = partials(*groups[2], grads[2], owns[0])
 
@@ -702,14 +733,15 @@
         functools.partial(finish_kernel, kernel),
         "finish",
         (1,),
-        [whole(keep.shape)] * 2 + [whole((seqs, width, shard))],
+        [whole(keep.shape)] * 2
+        + [pl.BlockSpec((seqs, 1, piece, frames), lambda i: (0, 1, 0, 0))],
         [whole((shard, width))] * 3 + [whole((kernel, width))],
         [sds((shard, width), F32)] * 3 + [sds((kernel, width), F32)],
         [],
         0,
         1024,
         vmem=20,
-    )(keep, others, w_out_pieces)
+    )(keep, others, moved[0])
     grad_in = ()
     for (first, size), part in zip(groups, moved):
         grad_in = (

time: 198 us -> 202 us (1.020)
  starting transfers between devices: 51.1 us -> 42.3 us
  waiting for transfers between devices: 43.5 us -> 52.3 us
  Pallas kernels: 91.5 us -> 94.1 us
    all_to_all x6 -> x5, starting transfers between devices: 31.5 us -> 23.2 us  [exchange(): return lax.all_to_all(copies, axis, 0, 0, tiled=True)]
    all_to_all x6 -> x5, waiting for transfers between devices: 5.73 us -> 12.5 us  [exchange(): return lax.all_to_all(copies, axis, 0, 0, tiled=True)]
    ppermute x3, waiting for transfers between devices: 29.8 us -> 36.2 us  [per_device(): others = lax.ppermute(send, 'seq', [(i, i ^ bit) for i in range(seqs)])]
    ppermute x3, waiting for transfers between devices: 4.28 us -> 0.01 us  [deliver(): arrived.append(lax.ppermute(part[d], 'tp', send))]
    pallas_call x0 -> x1, Pallas kernels: none -> 3.82 us  [deliver(): call(functools.partial(join_kernel, parts_in), 'add_join', (2 * parts_in,...]
    pallas_call x3 -> x2, Pallas kernels: 7.86 us -> 5.67 us  [deliver(): call(add_kernel, 'add', (size * parts_in,), [block] * chips, block, sds(p...]
  transfers between devices with their start and end apart: 18 -> 17, of which waited for: 6 -> 6; matrix products, arithmetic and copies ran while one was open for 3% -> 2% of each run, Pallas kernels for 29% -> 30%
where the time goes in v19:
time: 202 us; the launch traced here: 200 us
  Pallas kernels  94.1 us (47%)
  waiting for transfers between devices  52.3 us (26%)
  starting transfers between devices  42.3 us (21%)
  local copies, waits for them, and re-layouts  5.06 us (3%)
  other arithmetic  4.95 us (2%)
    ppermute x3, waiting for transfers between devices, per_device(): others = lax.ppermute(send, 'seq', [(i, i ^ bit) for i in range(seqs)])  36.2 us
    all_to_all x5, starting transfers between devices, exchange(): return lax.all_to_all(copies, axis, 0, 0, tiled=True)  23.2 us
    pallas_call x3, Pallas kernels, back(): call(functools.partial(back_kernel, first, blocks), 'back_conv', (size *...  18.9 us
    pallas_call x1, Pallas kernels, per_device(): call(gate_kernel, 'gate_conv', (recs,), [smem(), per_record((frames, mode...  15.3 us
    pallas_call x3, Pallas kernels, partials(): call(partial_kernel, 'partial_in', (size * parts_in,), [pl.BlockSpec((hal...  15.1 us
    all_to_all x5, waiting for transfers between devices, exchange(): return lax.all_to_all(copies, axis, 0, 0, tiled=True)  12.5 us
    pallas_call x1, Pallas kernels, per_device(): call(norm_kernel, 'swish_norm', (recs,), [smem(), smem(), whole((seqs, 2,...  12.1 us
    pallas_call x1, Pallas kernels, per_device(): call(functools.partial(outer_kernel, groups), 'outer_w_in', (recs,), [sme...  9.51 us
  transfers between devices with their start and end apart: 17, of which 6 were waited for; matrix products, arithmetic and copies ran while one was open for 2% of the time, Pallas kernels for 30%

profile of v19, /device:TPU:0, one launch (start us, length us, event | category | flops | bytes accessed | tf_op | source)
XLA Modules:
  0.0 200.2 jit_solution(13120822232605521576)
XLA Ops:
  0.6 1.0 fusion.1
  1.6 4.9 %collective-permute-start = (bf16[4,8,2048]{2,1,0:T(8,128)(2,1)S(1)}, bf16[4,8,2048]{2,1,0:T(8,128)(2,1)S(1)}, u32[]{:S(2)}, u32[]{:S(2)}) collective-permute-start(bf16[4,8,2048]{2,1,0:T(8,128)(2,1)S(1)} %pad_maximum_fusion.3), channel_id=1, source_target_pairs={{0,4},{4,8},{8,12},{12,16},{16,20},{20,24},{24,28},{1,5},{5,9},{9,... | collective-permute-start | bytes 393224 | tf_op jit(solution)/shard_map/ppermute | solution.py:453
  6.5 1.3 collective-permute-start.1
  7.8 1.3 fusion.5
  9.1 0.6 stack.35.meta
  9.7 3.7 %collective-permute-done.1 = bf16[4,8,2048]{2,1,0:T(8,128)(2,1)S(1)} collective-permute-done((bf16[4,8,2048]{2,1,0:T(8,128)(2,1)S(1)}, bf16[4,8,2048]{2,1,0:T(8,128)(2,1)S(1)}, u32[]{:S(2)}, u32[]{:S(2)}) %collective-permute-start.1) | collective-permute-done | bytes 131104 | tf_op jit(solution)/shard_map/ppermute | solution.py:453
  13.4 0.7 fusion.3
  14.1 15.3 %gate_conv.1 = (f32[4,1024,256]{2,1,0:T(8,128)}, f32[4,1024,256]{2,1,0:T(8,128)}, f32[4,1040,256]{2,1,0:T(8,128)}, f32[8,2,256]{2,1,0:T(2,128)}) custom-call(s32[2,4]{1,0:T(2,128)} %stack.35.meta, bf16[4,1024,1024]{2,1,0:T(8,128)(2,1)} %x.4, bf16[4,16,1024]{2,1,0:T(8,128)(2,1)} %get-tuple-element.106.halo, bf16[1024,256]{1,0:T(8,128)(2,1)} %wv.1, ...), custom_call_target="tpu_custom_call" | custom-call | flops 4294967296 | bytes 20971520 | tf_op jit(solution)/shard_map/gate_conv/pallas_call | solution.py:467
  29.4 1.1 pad_maximum_fusion
  31.6 0.6 pad_maximum_fusion.5.affine
  32.2 1.0 fusion.select
  33.2 5.7 %all-to-all-start = ((f32[8,2,256]{2,1,0:T(2,128)}), f32[8,2,256]{2,1,0:T(2,128)S(1)}, u32[]{:S(2)}, u32[]{:S(2)}) async-start(f32[8,2,256]{2,1,0:T(2,128)} %get-tuple-element.52), calls=%async_computation | async-start | bytes 32768 | tf_op jit(solution)/shard_map/all_to_all | solution.py:413
  38.9 0.8 pad_maximum_fusion.1
  39.7 5.7 %all-to-all-done.stats = f32[8,2,256]{2,1,0:T(2,128)S(1)} async-done(((f32[8,2,256]{2,1,0:T(2,128)}), f32[8,2,256]{2,1,0:T(2,128)S(1)}, u32[]{:S(2)}, u32[]{:S(2)}) %all-to-all-start) | async-done | bytes 16416 | tf_op jit(solution)/shard_map/all_to_all | solution.py:413
  45.5 0.6 copy-done.5
  46.1 12.1 %swish_norm.1 = (bf16[4,1024,256]{2,1,0:T(8,128)(2,1)}, f32[4,1040,256]{2,1,0:T(8,128)}, bf16[4,256,1024]{2,1,0:T(8,128)(2,1)}, f32[8,2,256]{2,1,0:T(2,128)}) custom-call(s32[2,4]{1,0:T(2,128)} %stack.35.meta, f32[1,1]{1,0:T(1,128)} %bitcast.1.count, f32[8,2,256]{2,1,0:T(2,128)} %copy-done.5, f32[2,256]{1,0:T(2,128)} %pad_maximum_fusion.5.affine, ...), custom_call_target="tpu_custom_call" | custom-call | flops 4294967296 | bytes 20971520 | tf_op jit(solution)/shard_map/swish_norm/pallas_call | solution.py:512
  58.2 3.3 %all-to-all-start.1 = ((f32[8,2,256]{2,1,0:T(2,128)}), f32[8,2,256]{2,1,0:T(2,128)S(1)}, u32[]{:S(2)}, u32[]{:S(2)}) async-start(f32[8,2,256]{2,1,0:T(2,128)} %get-tuple-element.56), calls=%async_computation.1 | async-start | bytes 32768 | tf_op jit(solution)/shard_map/all_to_all | solution.py:413
  61.5 6.7 %outer_w_out.1.refs_2_ = bf16[8,1,32,1024]{3,2,1,0:T(8,128)(2,1)} custom-call(bf16[4,1024,1024]{2,1,0:T(8,128)(2,1)} %grads.3, bf16[4,1024,256]{2,1,0:T(8,128)(2,1)} %get-tuple-element.60.swished), custom_call_target="tpu_custom_call" | custom-call | flops 2147483648 | bytes 8388608 | tf_op jit(solution)/shard_map/outer_w_out/pallas_call | solution.py:557
  68.3 0.6 copy-done.3
  68.9 5.0 %back_conv.3 = (bf16[1024,512]{1,0:T(8,128)(2,1)}, f32[16,256]{1,0:T(8,128)}) custom-call(s32[2,4]{1,0:T(2,128)} %stack.35.meta, f32[1,1]{1,0:T(1,128)} %bitcast.1.count, f32[8,2,256]{2,1,0:T(2,128)} %copy-done.5, f32[8,2,256]{2,1,0:T(2,128)} %copy-done.3, f32[1,256]{1,0:T(1,128)} %bitcast.26, f32[4,1040,256]{2,1,0:T(8,128)} %get-tuple-element.57.gn, ...), custom_call_target="tpu_custom_call" | custom-call | bytes 1024 | tf_op jit(solution)/shard_map/back_conv/pallas_call | solution.py:581
  74.0 5.0 %back_conv.4 = (bf16[1024,512]{1,0:T(8,128)(2,1)}, f32[16,256]{1,0:T(8,128)}) custom-call(s32[2,4]{1,0:T(2,128)} %stack.35.meta, f32[1,1]{1,0:T(1,128)} %bitcast.1.count, f32[8,2,256]{2,1,0:T(2,128)} %copy-done.5, f32[8,2,256]{2,1,0:T(2,128)} %copy-done.3, f32[1,256]{1,0:T(1,128)} %bitcast.27, f32[4,1040,256]{2,1,0:T(8,128)} %get-tuple-element.57.gn, ...), custom_call_target="tpu_custom_call" | custom-call | bytes 1024 | tf_op jit(solution)/shard_map/back_conv/pallas_call | solution.py:581
  79.5 4.3 %partial_in.3 = (bf16[8,1,32,1024]{3,2,1,0:T(8,128)(2,1)}, bf16[8,1,32,1024]{3,2,1,0:T(8,128)(2,1)}) custom-call(bf16[1024,512]{1,0:T(8,128)(2,1)} %get-tuple-element.62.own.refs_0_, bf16[1024,512]{1,0:T(8,128)(2,1)} %collective-permute-done.3.sibling, bf16[512,512]{1,0:T(8,128)(2,1)} %bitcast.21, bf16[512,512]{1,0:T(8,128)(2,1)} %copy-done.1, ...), custom_call_target="tpu_custom_call" | custom-call | bytes 1024 | tf_op jit(solution)/shard_map/partial_in/pallas_call | solution.py:610
  83.8 1.5 collective-permute-start.6
  85.3 8.8 %back_conv.5 = (bf16[2048,512]{1,0:T(8,128)(2,1)}, f32[16,256]{1,0:T(8,128)}) custom-call(s32[2,4]{1,0:T(2,128)} %stack.35.meta, f32[1,1]{1,0:T(1,128)} %bitcast.1.count, f32[8,2,256]{2,1,0:T(2,128)} %copy-done.5, f32[8,2,256]{2,1,0:T(2,128)} %copy-done.3, f32[1,256]{1,0:T(1,128)} %bitcast.28, f32[4,1040,256]{2,1,0:T(8,128)} %get-tuple-element.57.gn, ...), custom_call_target="tpu_custom_call" | custom-call | bytes 1024 | tf_op jit(solution)/shard_map/back_conv/pallas_call | solution.py:581
  94.2 4.3 %partial_in.4 = (bf16[8,1,32,1024]{3,2,1,0:T(8,128)(2,1)}, bf16[8,1,32,1024]{3,2,1,0:T(8,128)(2,1)}) custom-call(bf16[1024,512]{1,0:T(8,128)(2,1)} %get-tuple-element.64.own.refs_1_, bf16[1024,512]{1,0:T(8,128)(2,1)} %collective-permute-done.5.sibling, bf16[512,512]{1,0:T(8,128)(2,1)} %bitcast.22, bf16[512,512]{1,0:T(8,128)(2,1)} %copy-done.1, ...), custom_call_target="tpu_custom_call" | custom-call | bytes 1024 | tf_op jit(solution)/shard_map/partial_in/pallas_call | solution.py:610
  99.0 0.8 copy-done.8
  99.9 3.8 %add_join.1 = bf16[8,2,32,1024]{3,2,1,0:T(8,128)(2,1)} custom-call(bf16[8,1,32,1024]{3,2,1,0:T(8,128)(2,1)} %get-tuple-element.74.refs_0_, bf16[8,1,32,1024]{3,2,1,0:T(8,128)(2,1)} %copy-done.8, bf16[8,1,32,1024]{3,2,1,0:T(8,128)(2,1)} %outer_w_out.1.refs_2_), custom_call_target="tpu_custom_call" | custom-call | flops 49999998976 | bytes 1024 | tf_op jit(solution)/shard_map/add_join/pallas_call | solution.py:657
  103.7 5.9 %all-to-all-start.2 = ((bf16[8,2,32,1024]{3,2,1,0:T(8,128)(2,1)}), bf16[8,2,32,1024]{3,2,1,0:T(8,128)(2,1)}, u32[]{:S(2)}, u32[]{:S(2)}) async-start(bf16[8,2,32,1024]{3,2,1,0:T(8,128)(2,1)} %add_join.1), calls=%async_computation.2 | async-start | bytes 2097152 | tf_op jit(solution)/shard_map/all_to_all | solution.py:413
  109.6 6.5 %partial_in.5 = (bf16[8,2,32,1024]{3,2,1,0:T(8,128)(2,1)}, bf16[8,2,32,1024]{3,2,1,0:T(8,128)(2,1)}) custom-call(bf16[2048,512]{1,0:T(8,128)(2,1)} %get-tuple-element.70.own.refs_2_, bf16[2048,512]{1,0:T(8,128)(2,1)} %collective-permute-done.4.sibling, bf16[512,512]{1,0:T(8,128)(2,1)} %bitcast.23, bf16[512,512]{1,0:T(8,128)(2,1)} %copy-done.1, ...), custom_call_target="tpu_custom_call" | custom-call | bytes 1024 | tf_op jit(solution)/shard_map/partial_in/pallas_call | solution.py:610
  116.1 1.5 collective-permute-start.8
  117.6 9.5 %outer_w_in.1 = (bf16[4,544,128]{2,1,0:T(8,128)(2,1)}, bf16[4,544,128]{2,1,0:T(8,128)(2,1)}) custom-call(s32[1,1]{1,0:T(1,128)} %bitcast.11.parity, bf16[4,1024,1024]{2,1,0:T(8,128)(2,1)} %x.4, bf16[1024,512]{1,0:T(8,128)(2,1)} %get-tuple-element.62.own.refs_0_, bf16[1024,512]{1,0:T(8,128)(2,1)} %get-tuple-element.64.own.refs_1_, ...), custom_call_target="tpu_custom_call" | custom-call | flops 49999998976 | bytes 1024 | tf_op jit(solution)/shard_map/outer_w_in/pallas_call | solution.py:686
  127.2 2.0 add.114
  129.1 6.7 %all-to-all-done.2.moved.pieces = bf16[8,2,32,1024]{3,2,1,0:T(8,128)(2,1)} async-done(((bf16[8,2,32,1024]{3,2,1,0:T(8,128)(2,1)}), bf16[8,2,32,1024]{3,2,1,0:T(8,128)(2,1)}, u32[]{:S(2)}, u32[]{:S(2)}) %all-to-all-start.2) | async-done | bytes 1048608 | tf_op jit(solution)/shard_map/all_to_all | solution.py:413
  135.8 3.6 %all-to-all-start.3 = ((bf16[8,1,32,1024]{3,2,1,0:T(8,128)(2,1)}), bf16[8,1,32,1024]{3,2,1,0:T(8,128)(2,1)S(1)}, u32[]{:S(2)}, u32[]{:S(2)}) async-start(bf16[8,1,32,1024]{3,2,1,0:T(8,128)(2,1)} %add.114), calls=%async_computation.3 | async-start | bytes 1048576 | tf_op jit(solution)/shard_map/all_to_all | solution.py:413
  139.5 2.0 %collective-permute-start.9 = (bf16[4,544,128]{2,1,0:T(8,128)(2,1)}, bf16[4,544,128]{2,1,0:T(8,128)(2,1)}, u32[]{:S(2)}, u32[]{:S(2)}) collective-permute-start(bf16[4,544,128]{2,1,0:T(8,128)(2,1)} %get-tuple-element.86), channel_id=1, source_target_pairs={{0,4},{4,0},{8,12},{12,8},{16,20},{20,16},{24,28},{28,24},{1,5},{5... | collective-permute-start | bytes 1671176 | tf_op jit(solution)/shard_map/ppermute | solution.py:710
  141.5 3.7 %add.115 = bf16[8,2,32,1024]{3,2,1,0:T(8,128)(2,1)} custom-call(bf16[8,2,32,1024]{3,2,1,0:T(8,128)(2,1)} %get-tuple-element.84.refs_0_, bf16[8,2,32,1024]{3,2,1,0:T(8,128)(2,1)} %collective-permute-done.8.refs_1_), custom_call_target="tpu_custom_call" | custom-call | bytes 1024 | tf_op jit(solution)/shard_map/add/pallas_call | solution.py:645
  145.2 14.5 %collective-permute-done.9.other = bf16[4,544,128]{2,1,0:T(8,128)(2,1)} collective-permute-done((bf16[4,544,128]{2,1,0:T(8,128)(2,1)}, bf16[4,544,128]{2,1,0:T(8,128)(2,1)}, u32[]{:S(2)}, u32[]{:S(2)}) %collective-permute-start.9) | collective-permute-done | bytes 557088 | tf_op jit(solution)/shard_map/ppermute | solution.py:710
  159.7 4.5 %all-to-all-start.4 = ((bf16[8,2,32,1024]{3,2,1,0:T(8,128)(2,1)}), bf16[8,2,32,1024]{3,2,1,0:T(8,128)(2,1)S(1)}, u32[]{:S(2)}, u32[]{:S(2)}) async-start(bf16[8,2,32,1024]{3,2,1,0:T(8,128)(2,1)} %add.115), calls=%async_computation.4 | async-start | bytes 2097152 | tf_op jit(solution)/shard_map/all_to_all | solution.py:413
  164.2 1.2 fold.2
  165.4 2.1 %collective-permute-start.10 = (bf16[2,544,128]{2,1,0:T(8,128)(2,1)S(1)}, bf16[2,544,128]{2,1,0:T(8,128)(2,1)S(1)}, u32[]{:S(2)}, u32[]{:S(2)}) collective-permute-start(bf16[2,544,128]{2,1,0:T(8,128)(2,1)S(1)} %get-tuple-element.90), channel_id=1, source_target_pairs={{0,8},{4,12},{8,0},{12,4},{16,24},{20,28},{24,16},{28,20},{1,9},{5... | collective-permute-start | bytes 835592 | tf_op jit(solution)/shard_map/ppermute | solution.py:710
  167.5 19.6 %collective-permute-done.10.other = bf16[2,544,128]{2,1,0:T(8,128)(2,1)S(1)} collective-permute-done((bf16[2,544,128]{2,1,0:T(8,128)(2,1)S(1)}, bf16[2,544,128]{2,1,0:T(8,128)(2,1)S(1)}, u32[]{:S(2)}, u32[]{:S(2)}) %collective-permute-start.10) | collective-permute-done | bytes 278560 | tf_op jit(solution)/shard_map/ppermute | solution.py:710
  187.2 4.7 %collective-permute-start.11 = (bf16[1,544,128]{2,1,0:T(8,128)(2,1)S(1)}, bf16[1,544,128]{2,1,0:T(8,128)(2,1)S(1)}, u32[]{:S(2)}, u32[]{:S(2)}) collective-permute-start(bf16[1,544,128]{2,1,0:T(8,128)(2,1)S(1)} %get-tuple-element.92), channel_id=1, source_target_pairs={{0,16},{4,20},{8,24},{12,28},{16,0},{20,4},{24,8},{28,12},{1,17},{... | collective-permute-start | bytes 417800 | tf_op jit(solution)/shard_map/ppermute | solution.py:710
  191.9 0.6 fusion.4
  192.4 1.9 place.3.refs_0_
  194.3 0.8 place.4.refs_0_
  195.1 2.1 %collective-permute-done.11.other = bf16[1,544,128]{2,1,0:T(8,128)(2,1)S(1)} collective-permute-done((bf16[1,544,128]{2,1,0:T(8,128)(2,1)S(1)}, bf16[1,544,128]{2,1,0:T(8,128)(2,1)S(1)}, u32[]{:S(2)}, u32[]{:S(2)}) %collective-permute-start.11) | collective-permute-done | bytes 139296 | tf_op jit(solution)/shard_map/ppermute | solution.py:710
  197.3 1.9 finish.1
  199.2 1.1 place.5
  (42 shorter events, 1.7 us)
Async XLA Ops:
  1.6 8.1 %collective-permute-start = (bf16[4,8,2048]{2,1,0:T(8,128)(2,1)S(1)}, bf16[4,8,2048]{2,1,0:T(8,128)(2,1)S(1)}, u32[]{:S(2)}, u32[]{:S(2)}) collective-permute-start(bf16[4,8,2048]{2,1,0:T(8,128)(2,1)S(1)} %pad_maximum_fusion.3), channel_id=1, source_target_pairs={{0,4},{4,8},{8,12},{12,16},{16,20},{20,24},{24,28},{1,5},{5,9},{9,... | collective-permute-start | bytes 393224 | tf_op jit(solution)/shard_map/ppermute | solution.py:453
  6.5 6.9 %collective-permute-start.1 = (bf16[4,8,2048]{2,1,0:T(8,128)(2,1)S(1)}, bf16[4,8,2048]{2,1,0:T(8,128)(2,1)S(1)}, u32[]{:S(2)}, u32[]{:S(2)}) collective-permute-start(bf16[4,8,2048]{2,1,0:T(8,128)(2,1)S(1)} %pad_maximum_fusion.4), channel_id=1, source_target_pairs={{4,0},{8,4},{12,8},{16,12},{20,16},{24,20},{28,24},{5,1},{9,5},{13... | collective-permute-start | bytes 393224 | tf_op jit(solution)/shard_map/ppermute | solution.py:453
  14.1 15.3 %copy-start.2 = (bf16[1024,256]{1,0:T(8,128)(2,1)S(1)}, bf16[1024,256]{1,0:T(8,128)(2,1)}, u32[]{:S(2)}) copy-start(bf16[1024,256]{1,0:T(8,128)(2,1)} %wv.1) | copy-start | bytes 1572868
  30.6 1.1 copy-start.6
  30.6 1.1 copy-start.7
  30.7 9.0 %collective-permute-start.2 = (bf16[512,512]{1,0:T(8,128)(2,1)S(1)}, bf16[512,512]{1,0:T(8,128)(2,1)S(1)}, u32[]{:S(2)}, u32[]{:S(2)}) collective-permute-start(bf16[512,512]{1,0:T(8,128)(2,1)S(1)} %bitcast.25), channel_id=1, source_target_pairs={{0,1},{1,0},{2,3},{3,2},{4,5},{5,4},{6,7},{7,6},{8,9},{9,8},{10,11... | collective-permute-start | bytes 1572872 | tf_op jit(solution)/shard_map/ppermute | solution.py:506
  33.2 12.3 %all-to-all-start = ((f32[8,2,256]{2,1,0:T(2,128)}), f32[8,2,256]{2,1,0:T(2,128)S(1)}, u32[]{:S(2)}, u32[]{:S(2)}) async-start(f32[8,2,256]{2,1,0:T(2,128)} %get-tuple-element.52), calls=%async_computation | async-start | bytes 32768 | tf_op jit(solution)/shard_map/all_to_all | solution.py:413
  39.7 18.4 %copy-start.1 = (bf16[512,512]{1,0:T(8,128)(2,1)}, bf16[512,512]{1,0:T(8,128)(2,1)S(1)}, u32[]{:S(2)}) copy-start(bf16[512,512]{1,0:T(8,128)(2,1)S(1)} %collective-permute-done.2.w_sibling) | copy-start | bytes 1572868
  45.5 0.6 copy-start.5
  58.2 10.1 %all-to-all-start.1 = ((f32[8,2,256]{2,1,0:T(2,128)}), f32[8,2,256]{2,1,0:T(2,128)S(1)}, u32[]{:S(2)}, u32[]{:S(2)}) async-start(f32[8,2,256]{2,1,0:T(2,128)} %get-tuple-element.56), calls=%async_computation.1 | async-start | bytes 32768 | tf_op jit(solution)/shard_map/all_to_all | solution.py:413
  68.3 0.6 copy-start.3
  73.9 5.6 %collective-permute-start.3 = (bf16[1024,512]{1,0:T(8,128)(2,1)}, bf16[1024,512]{1,0:T(8,128)(2,1)}, u32[]{:S(2)}, u32[]{:S(2)}) collective-permute-start(bf16[1024,512]{1,0:T(8,128)(2,1)} %get-tuple-element.62.own.refs_0_), channel_id=1, source_target_pairs={{0,1},{1,0},{2,3},{3,2},{4,5},{5,4},{6,7},{7,6},{8,9},{9,8},{10,11... | collective-permute-start | bytes 3145736 | tf_op jit(solution)/shard_map/ppermute | solution.py:608
  79.0 15.2 %collective-permute-start.5 = (bf16[1024,512]{1,0:T(8,128)(2,1)}, bf16[1024,512]{1,0:T(8,128)(2,1)}, u32[]{:S(2)}, u32[]{:S(2)}) collective-permute-start(bf16[1024,512]{1,0:T(8,128)(2,1)} %get-tuple-element.64.own.refs_1_), channel_id=1, source_target_pairs={{0,1},{1,0},{2,3},{3,2},{4,5},{5,4},{6,7},{7,6},{8,9},{9,8},{10,11... | collective-permute-start | bytes 3145736 | tf_op jit(solution)/shard_map/ppermute | solution.py:608
  83.8 15.3 %collective-permute-start.6 = (bf16[8,1,32,1024]{3,2,1,0:T(8,128)(2,1)}, bf16[8,1,32,1024]{3,2,1,0:T(8,128)(2,1)S(1)}, u32[]{:S(2)}, u32[]{:S(2)}) collective-permute-start(bf16[8,1,32,1024]{3,2,1,0:T(8,128)(2,1)} %get-tuple-element.68), channel_id=1, source_target_pairs={{0,2},{1,3},{2,0},{3,1},{4,6},{5,7},{6,4},{7,5},{8,10},{9,11},{10,... | collective-permute-start | bytes 1572872 | tf_op jit(solution)/shard_map/ppermute | solution.py:639
  94.1 15.5 %collective-permute-start.4 = (bf16[2048,512]{1,0:T(8,128)(2,1)}, bf16[2048,512]{1,0:T(8,128)(2,1)}, u32[]{:S(2)}, u32[]{:S(2)}) collective-permute-start(bf16[2048,512]{1,0:T(8,128)(2,1)} %get-tuple-element.70.own.refs_2_), channel_id=1, source_target_pairs={{0,1},{1,0},{2,3},{3,2},{4,5},{5,4},{6,7},{7,6},{8,9},{9,8},{10,11... | collective-permute-start | bytes 6291464 | tf_op jit(solution)/shard_map/ppermute | solution.py:608
  98.5 28.7 %collective-permute-start.7 = (bf16[8,1,32,1024]{3,2,1,0:T(8,128)(2,1)}, bf16[8,1,32,1024]{3,2,1,0:T(8,128)(2,1)}, u32[]{:S(2)}, u32[]{:S(2)}) collective-permute-start(bf16[8,1,32,1024]{3,2,1,0:T(8,128)(2,1)} %get-tuple-element.73), channel_id=1, source_target_pairs={{0,2},{1,3},{2,0},{3,1},{4,6},{5,7},{6,4},{7,5},{8,10},{9,11},{10,... | collective-permute-start | bytes 1572872 | tf_op jit(solution)/shard_map/ppermute | solution.py:639
  99.0 0.8 copy-start.8
  103.7 32.2 %all-to-all-start.2 = ((bf16[8,2,32,1024]{3,2,1,0:T(8,128)(2,1)}), bf16[8,2,32,1024]{3,2,1,0:T(8,128)(2,1)}, u32[]{:S(2)}, u32[]{:S(2)}) async-start(bf16[8,2,32,1024]{3,2,1,0:T(8,128)(2,1)} %add_join.1), calls=%async_computation.2 | async-start | bytes 2097152 | tf_op jit(solution)/shard_map/all_to_all | solution.py:413
  116.1 25.4 %collective-permute-start.8 = (bf16[8,2,32,1024]{3,2,1,0:T(8,128)(2,1)}, bf16[8,2,32,1024]{3,2,1,0:T(8,128)(2,1)}, u32[]{:S(2)}, u32[]{:S(2)}) collective-permute-start(bf16[8,2,32,1024]{3,2,1,0:T(8,128)(2,1)} %get-tuple-element.77), channel_id=1, source_target_pairs={{0,2},{1,3},{2,0},{3,1},{4,6},{5,7},{6,4},{7,5},{8,10},{9,11},{10,... | collective-permute-start | bytes 3145736 | tf_op jit(solution)/shard_map/ppermute | solution.py:639
  135.8 23.8 %all-to-all-start.3 = ((bf16[8,1,32,1024]{3,2,1,0:T(8,128)(2,1)}), bf16[8,1,32,1024]{3,2,1,0:T(8,128)(2,1)S(1)}, u32[]{:S(2)}, u32[]{:S(2)}) async-start(bf16[8,1,32,1024]{3,2,1,0:T(8,128)(2,1)} %add.114), calls=%async_computation.3 | async-start | bytes 1048576 | tf_op jit(solution)/shard_map/all_to_all | solution.py:413
  139.5 20.2 %collective-permute-start.9 = (bf16[4,544,128]{2,1,0:T(8,128)(2,1)}, bf16[4,544,128]{2,1,0:T(8,128)(2,1)}, u32[]{:S(2)}, u32[]{:S(2)}) collective-permute-start(bf16[4,544,128]{2,1,0:T(8,128)(2,1)} %get-tuple-element.86), channel_id=1, source_target_pairs={{0,4},{4,0},{8,12},{12,8},{16,20},{20,16},{24,28},{28,24},{1,5},{5... | collective-permute-start | bytes 1671176 | tf_op jit(solution)/shard_map/ppermute | solution.py:710
  145.2 19.0 %copy-start = (bf16[4,544,128]{2,1,0:T(8,128)(2,1)S(1)}, bf16[4,544,128]{2,1,0:T(8,128)(2,1)}, u32[]{:S(2)}) copy-start(bf16[4,544,128]{2,1,0:T(8,128)(2,1)} %get-tuple-element.88.own) | copy-start | bytes 1671172
  145.2 22.3 %copy-start.4 = (f32[8,2,256]{2,1,0:T(2,128)S(1)}, f32[8,2,256]{2,1,0:T(2,128)}, u32[]{:S(2)}) copy-start(f32[8,2,256]{2,1,0:T(2,128)} %copy-done.3) | copy-start | bytes 49156
  159.7 39.5 %all-to-all-start.4 = ((bf16[8,2,32,1024]{3,2,1,0:T(8,128)(2,1)}), bf16[8,2,32,1024]{3,2,1,0:T(8,128)(2,1)S(1)}, u32[]{:S(2)}, u32[]{:S(2)}) async-start(bf16[8,2,32,1024]{3,2,1,0:T(8,128)(2,1)} %add.115), calls=%async_computation.4 | async-start | bytes 2097152 | tf_op jit(solution)/shard_map/all_to_all | solution.py:413
  165.4 21.7 %collective-permute-start.10 = (bf16[2,544,128]{2,1,0:T(8,128)(2,1)S(1)}, bf16[2,544,128]{2,1,0:T(8,128)(2,1)S(1)}, u32[]{:S(2)}, u32[]{:S(2)}) collective-permute-start(bf16[2,544,128]{2,1,0:T(8,128)(2,1)S(1)} %get-tuple-element.90), channel_id=1, source_target_pairs={{0,8},{4,12},{8,0},{12,4},{16,24},{20,28},{24,16},{28,20},{1,9},{5... | collective-permute-start | bytes 835592 | tf_op jit(solution)/shard_map/ppermute | solution.py:710
  187.2 10.1 %collective-permute-start.11 = (bf16[1,544,128]{2,1,0:T(8,128)(2,1)S(1)}, bf16[1,544,128]{2,1,0:T(8,128)(2,1)S(1)}, u32[]{:S(2)}, u32[]{:S(2)}) collective-permute-start(bf16[1,544,128]{2,1,0:T(8,128)(2,1)S(1)} %get-tuple-element.92), channel_id=1, source_target_pairs={{0,16},{4,20},{8,24},{12,28},{16,0},{20,4},{24,8},{28,12},{1,17},{... | collective-permute-start | bytes 417800 | tf_op jit(solution)/shard_map/ppermute | solution.py:710

commit v20 on v19

--- a/solution.py
+++ b/solution.py
@@ -704,17 +704,14 @@
     )(parity, after(normed, *parts[2]), *grads, *taps)
     owns[1] = deliver(parts[1], LONG, keep)
     moved[1] = exchange(after(owns[1], moved[0]), "seq")
-    owns[2] = deliver(parts[2], 0, owns[1])
     bit = 1
     while True:
         others = lax.ppermute(send, "seq", [(i, i ^ bit) for i in range(seqs)])
-        if bit == 1:
-            moved[2] = exchange(after(owns[2], moved[1], others), "seq")
         bit *= 2
         if bit == seqs:
             break
         if bit == 2:
-            keep = after(keep, owns[2])
+            keep = after(keep, owns[1])
         shape = (keep.shape[0] // 2,) + keep.shape[1:]
         side = ((seq_at // bit) % 2).astype(jnp.int32).reshape(1, 1)
         keep, send = call(
@@ -729,6 +726,10 @@
             1024,
             vmem=20,
         )(side, keep, others)
+        if bit == 2:
+            owns[2] = deliver(parts[2], 0, keep)
+        if bit == min(4, seqs // 2):
+            moved[2] = exchange(after(owns[2], moved[1], keep), "seq")
     w_value, w_gate, w_out, grad_taps = call(
         functools.partial(finish_kernel, kernel),
         "finish",

time: 202 us -> 214 us (1.059)
  waiting for transfers between devices: 52.3 us -> 66 us
    ppermute x3, waiting for transfers between devices: 36.2 us -> 49.9 us  [per_device(): others = lax.ppermute(send, 'seq', [(i, i ^ bit) for i in range(seqs)])]
    ppermute x3, starting transfers between devices: 8.77 us -> 6.52 us  [per_device(): others = lax.ppermute(send, 'seq', [(i, i ^ bit) for i in range(seqs)])]
  transfers between devices with their start and end apart: 17 -> 17, of which waited for: 6 -> 6; matrix products, arithmetic and copies ran while one was open for 2% -> 2% of each run, Pallas kernels for 30% -> 28%
where the time goes in v20:
time: 214 us; the launch traced here: 213 us
  Pallas kernels  93.1 us (44%)
  waiting for transfers between devices  66 us (31%)
  starting transfers between devices  41 us (19%)
  local copies, waits for them, and re-layouts  6.11 us (3%)
  other arithmetic  4.95 us (2%)
    ppermute x3, waiting for transfers between devices, per_device(): others = lax.ppermute(send, 'seq', [(i, i ^ bit) for i in range(seqs)])  49.9 us
    all_to_all x5, starting transfers between devices, exchange(): return lax.all_to_all(copies, axis, 0, 0, tiled=True)  24 us
    pallas_call x3, Pallas kernels, back(): call(functools.partial(back_kernel, first, blocks), 'back_conv', (size *...  18.9 us
    pallas_call x1, Pallas kernels, per_device(): call(gate_kernel, 'gate_conv', (recs,), [smem(), per_record((frames, mode...  15.3 us
    pallas_call x3, Pallas kernels, partials(): call(partial_kernel, 'partial_in', (size * parts_in,), [pl.BlockSpec((hal...  15.1 us
    all_to_all x5, waiting for transfers between devices, exchange(): return lax.all_to_all(copies, axis, 0, 0, tiled=True)  12.4 us
    pallas_call x1, Pallas kernels, per_device(): call(norm_kernel, 'swish_norm', (recs,), [smem(), smem(), whole((seqs, 2,...  12.1 us
    pallas_call x1, Pallas kernels, per_device(): call(functools.partial(outer_kernel, groups), 'outer_w_in', (recs,), [sme...  9.55 us
  transfers between devices with their start and end apart: 17, of which 6 were waited for; matrix products, arithmetic and copies ran while one was open for 2% of the time, Pallas kernels for 28%

profile of v20, /device:TPU:0, one launch (start us, length us, event | category | flops | bytes accessed | tf_op | source)
XLA Modules:
  0.0 212.6 jit_solution(17710849204703854049)
XLA Ops:
  0.6 1.0 fusion.1
  1.6 4.9 %collective-permute-start = (bf16[4,8,2048]{2,1,0:T(8,128)(2,1)S(1)}, bf16[4,8,2048]{2,1,0:T(8,128)(2,1)S(1)}, u32[]{:S(2)}, u32[]{:S(2)}) collective-permute-start(bf16[4,8,2048]{2,1,0:T(8,128)(2,1)S(1)} %pad_maximum_fusion.3), channel_id=1, source_target_pairs={{0,4},{4,8},{8,12},{12,16},{16,20},{20,24},{24,28},{1,5},{5,9},{9,... | collective-permute-start | bytes 393224 | tf_op jit(solution)/shard_map/ppermute | solution.py:453
  6.5 1.3 collective-permute-start.1
  7.8 1.3 fusion.5
  9.1 0.6 stack.35.meta
  9.7 3.7 %collective-permute-done.1 = bf16[4,8,2048]{2,1,0:T(8,128)(2,1)S(1)} collective-permute-done((bf16[4,8,2048]{2,1,0:T(8,128)(2,1)S(1)}, bf16[4,8,2048]{2,1,0:T(8,128)(2,1)S(1)}, u32[]{:S(2)}, u32[]{:S(2)}) %collective-permute-start.1) | collective-permute-done | bytes 131104 | tf_op jit(solution)/shard_map/ppermute | solution.py:453
  13.4 0.7 fusion.3
  14.1 15.3 %gate_conv.1 = (f32[4,1024,256]{2,1,0:T(8,128)}, f32[4,1024,256]{2,1,0:T(8,128)}, f32[4,1040,256]{2,1,0:T(8,128)}, f32[8,2,256]{2,1,0:T(2,128)}) custom-call(s32[2,4]{1,0:T(2,128)} %stack.35.meta, bf16[4,1024,1024]{2,1,0:T(8,128)(2,1)} %x.4, bf16[4,16,1024]{2,1,0:T(8,128)(2,1)} %get-tuple-element.106.halo, bf16[1024,256]{1,0:T(8,128)(2,1)} %wv.1, ...), custom_call_target="tpu_custom_call" | custom-call | flops 4294967296 | bytes 20971520 | tf_op jit(solution)/shard_map/gate_conv/pallas_call | solution.py:467
  29.4 1.1 pad_maximum_fusion
  31.6 0.6 pad_maximum_fusion.5.affine
  32.2 1.0 fusion.select
  33.2 5.7 %all-to-all-start = ((f32[8,2,256]{2,1,0:T(2,128)}), f32[8,2,256]{2,1,0:T(2,128)S(1)}, u32[]{:S(2)}, u32[]{:S(2)}) async-start(f32[8,2,256]{2,1,0:T(2,128)} %get-tuple-element.52), calls=%async_computation | async-start | bytes 32768 | tf_op jit(solution)/shard_map/all_to_all | solution.py:413
  38.9 0.8 pad_maximum_fusion.1
  39.7 5.7 %all-to-all-done.stats = f32[8,2,256]{2,1,0:T(2,128)S(1)} async-done(((f32[8,2,256]{2,1,0:T(2,128)}), f32[8,2,256]{2,1,0:T(2,128)S(1)}, u32[]{:S(2)}, u32[]{:S(2)}) %all-to-all-start) | async-done | bytes 16416 | tf_op jit(solution)/shard_map/all_to_all | solution.py:413
  45.5 0.6 copy-done.5
  46.1 12.1 %swish_norm.1 = (bf16[4,1024,256]{2,1,0:T(8,128)(2,1)}, f32[4,1040,256]{2,1,0:T(8,128)}, bf16[4,256,1024]{2,1,0:T(8,128)(2,1)}, f32[8,2,256]{2,1,0:T(2,128)}) custom-call(s32[2,4]{1,0:T(2,128)} %stack.35.meta, f32[1,1]{1,0:T(1,128)} %bitcast.1.count, f32[8,2,256]{2,1,0:T(2,128)} %copy-done.5, f32[2,256]{1,0:T(2,128)} %pad_maximum_fusion.5.affine, ...), custom_call_target="tpu_custom_call" | custom-call | flops 4294967296 | bytes 20971520 | tf_op jit(solution)/shard_map/swish_norm/pallas_call | solution.py:512
  58.2 3.3 %all-to-all-start.1 = ((f32[8,2,256]{2,1,0:T(2,128)}), f32[8,2,256]{2,1,0:T(2,128)S(1)}, u32[]{:S(2)}, u32[]{:S(2)}) async-start(f32[8,2,256]{2,1,0:T(2,128)} %get-tuple-element.56), calls=%async_computation.1 | async-start | bytes 32768 | tf_op jit(solution)/shard_map/all_to_all | solution.py:413
  61.5 6.7 %outer_w_out.1.refs_2_ = bf16[8,1,32,1024]{3,2,1,0:T(8,128)(2,1)} custom-call(bf16[4,1024,1024]{2,1,0:T(8,128)(2,1)} %grads.3, bf16[4,1024,256]{2,1,0:T(8,128)(2,1)} %get-tuple-element.60.swished), custom_call_target="tpu_custom_call" | custom-call | flops 2147483648 | bytes 8388608 | tf_op jit(solution)/shard_map/outer_w_out/pallas_call | solution.py:557
  68.3 0.6 copy-done.3
  68.9 5.0 %back_conv.3 = (bf16[1024,512]{1,0:T(8,128)(2,1)}, f32[16,256]{1,0:T(8,128)}) custom-call(s32[2,4]{1,0:T(2,128)} %stack.35.meta, f32[1,1]{1,0:T(1,128)} %bitcast.1.count, f32[8,2,256]{2,1,0:T(2,128)} %copy-done.5, f32[8,2,256]{2,1,0:T(2,128)} %copy-done.3, f32[1,256]{1,0:T(1,128)} %bitcast.26, f32[4,1040,256]{2,1,0:T(8,128)} %get-tuple-element.57.gn, ...), custom_call_target="tpu_custom_call" | custom-call | bytes 1024 | tf_op jit(solution)/shard_map/back_conv/pallas_call | solution.py:581
  74.0 5.0 %back_conv.4 = (bf16[1024,512]{1,0:T(8,128)(2,1)}, f32[16,256]{1,0:T(8,128)}) custom-call(s32[2,4]{1,0:T(2,128)} %stack.35.meta, f32[1,1]{1,0:T(1,128)} %bitcast.1.count, f32[8,2,256]{2,1,0:T(2,128)} %copy-done.5, f32[8,2,256]{2,1,0:T(2,128)} %copy-done.3, f32[1,256]{1,0:T(1,128)} %bitcast.27, f32[4,1040,256]{2,1,0:T(8,128)} %get-tuple-element.57.gn, ...), custom_call_target="tpu_custom_call" | custom-call | bytes 1024 | tf_op jit(solution)/shard_map/back_conv/pallas_call | solution.py:581
  79.5 4.3 %partial_in.3 = (bf16[8,1,32,1024]{3,2,1,0:T(8,128)(2,1)}, bf16[8,1,32,1024]{3,2,1,0:T(8,128)(2,1)}) custom-call(bf16[1024,512]{1,0:T(8,128)(2,1)} %get-tuple-element.62.own.refs_0_, bf16[1024,512]{1,0:T(8,128)(2,1)} %collective-permute-done.3.sibling, bf16[512,512]{1,0:T(8,128)(2,1)} %bitcast.21, bf16[512,512]{1,0:T(8,128)(2,1)} %copy-done.1, ...), custom_call_target="tpu_custom_call" | custom-call | bytes 1024 | tf_op jit(solution)/shard_map/partial_in/pallas_call | solution.py:610
  83.8 1.5 collective-permute-start.6
  85.3 8.8 %back_conv.5 = (bf16[2048,512]{1,0:T(8,128)(2,1)}, f32[16,256]{1,0:T(8,128)}) custom-call(s32[2,4]{1,0:T(2,128)} %stack.35.meta, f32[1,1]{1,0:T(1,128)} %bitcast.1.count, f32[8,2,256]{2,1,0:T(2,128)} %copy-done.5, f32[8,2,256]{2,1,0:T(2,128)} %copy-done.3, f32[1,256]{1,0:T(1,128)} %bitcast.28, f32[4,1040,256]{2,1,0:T(8,128)} %get-tuple-element.57.gn, ...), custom_call_target="tpu_custom_call" | custom-call | bytes 1024 | tf_op jit(solution)/shard_map/back_conv/pallas_call | solution.py:581
  94.2 4.3 %partial_in.4 = (bf16[8,1,32,1024]{3,2,1,0:T(8,128)(2,1)}, bf16[8,1,32,1024]{3,2,1,0:T(8,128)(2,1)}) custom-call(bf16[1024,512]{1,0:T(8,128)(2,1)} %get-tuple-element.64.own.refs_1_, bf16[1024,512]{1,0:T(8,128)(2,1)} %collective-permute-done.5.sibling, bf16[512,512]{1,0:T(8,128)(2,1)} %bitcast.22, bf16[512,512]{1,0:T(8,128)(2,1)} %copy-done.1, ...), custom_call_target="tpu_custom_call" | custom-call | bytes 1024 | tf_op jit(solution)/shard_map/partial_in/pallas_call | solution.py:610
  99.0 0.8 copy-done.8
  99.9 3.8 %add_join.1 = bf16[8,2,32,1024]{3,2,1,0:T(8,128)(2,1)} custom-call(bf16[8,1,32,1024]{3,2,1,0:T(8,128)(2,1)} %get-tuple-element.74.refs_0_, bf16[8,1,32,1024]{3,2,1,0:T(8,128)(2,1)} %copy-done.8, bf16[8,1,32,1024]{3,2,1,0:T(8,128)(2,1)} %outer_w_out.1.refs_2_), custom_call_target="tpu_custom_call" | custom-call | flops 49999998976 | bytes 1024 | tf_op jit(solution)/shard_map/add_join/pallas_call | solution.py:657
  103.7 5.9 %all-to-all-start.2 = ((bf16[8,2,32,1024]{3,2,1,0:T(8,128)(2,1)}), bf16[8,2,32,1024]{3,2,1,0:T(8,128)(2,1)}, u32[]{:S(2)}, u32[]{:S(2)}) async-start(bf16[8,2,32,1024]{3,2,1,0:T(8,128)(2,1)} %add_join.1), calls=%async_computation.2 | async-start | bytes 2097152 | tf_op jit(solution)/shard_map/all_to_all | solution.py:413
  109.6 6.5 %partial_in.5 = (bf16[8,2,32,1024]{3,2,1,0:T(8,128)(2,1)}, bf16[8,2,32,1024]{3,2,1,0:T(8,128)(2,1)}) custom-call(bf16[2048,512]{1,0:T(8,128)(2,1)} %get-tuple-element.70.own.refs_2_, bf16[2048,512]{1,0:T(8,128)(2,1)} %collective-permute-done.4.sibling, bf16[512,512]{1,0:T(8,128)(2,1)} %bitcast.23, bf16[512,512]{1,0:T(8,128)(2,1)} %copy-done.1, ...), custom_call_target="tpu_custom_call" | custom-call | bytes 1024 | tf_op jit(solution)/shard_map/partial_in/pallas_call | solution.py:610
  116.1 1.5 collective-permute-start.9
  117.6 9.5 %outer_w_in.1 = (bf16[4,544,128]{2,1,0:T(8,128)(2,1)}, bf16[4,544,128]{2,1,0:T(8,128)(2,1)}) custom-call(s32[1,1]{1,0:T(1,128)} %bitcast.12.parity, bf16[4,1024,1024]{2,1,0:T(8,128)(2,1)} %x.4, bf16[1024,512]{1,0:T(8,128)(2,1)} %get-tuple-element.62.own.refs_0_, bf16[1024,512]{1,0:T(8,128)(2,1)} %get-tuple-element.64.own.refs_1_, ...), custom_call_target="tpu_custom_call" | custom-call | flops 49999998976 | bytes 1024 | tf_op jit(solution)/shard_map/outer_w_in/pallas_call | solution.py:686
  127.2 2.0 add.114
  129.2 6.7 %all-to-all-done.2.moved.pieces = bf16[8,2,32,1024]{3,2,1,0:T(8,128)(2,1)} async-done(((bf16[8,2,32,1024]{3,2,1,0:T(8,128)(2,1)}), bf16[8,2,32,1024]{3,2,1,0:T(8,128)(2,1)}, u32[]{:S(2)}, u32[]{:S(2)}) %all-to-all-start.2) | async-done | bytes 1048608 | tf_op jit(solution)/shard_map/all_to_all | solution.py:413
  135.8 3.6 %all-to-all-start.3 = ((bf16[8,1,32,1024]{3,2,1,0:T(8,128)(2,1)}), bf16[8,1,32,1024]{3,2,1,0:T(8,128)(2,1)S(1)}, u32[]{:S(2)}, u32[]{:S(2)}) async-start(bf16[8,1,32,1024]{3,2,1,0:T(8,128)(2,1)} %add.114), calls=%async_computation.3 | async-start | bytes 1048576 | tf_op jit(solution)/shard_map/all_to_all | solution.py:413
  139.5 2.0 collective-permute-start.8
  141.5 18.1 %collective-permute-done.8.other = bf16[4,544,128]{2,1,0:T(8,128)(2,1)S(1)} collective-permute-done((bf16[4,544,128]{2,1,0:T(8,128)(2,1)}, bf16[4,544,128]{2,1,0:T(8,128)(2,1)S(1)}, u32[]{:S(2)}, u32[]{:S(2)}) %collective-permute-start.8) | collective-permute-done | bytes 557088 | tf_op jit(solution)/shard_map/ppermute | solution.py:709
  159.6 1.1 copy-done
  160.8 1.5 collective-permute-start.10
  162.3 6.0 %collective-permute-done.10.other = bf16[2,544,128]{2,1,0:T(8,128)(2,1)S(1)} collective-permute-done((bf16[2,544,128]{2,1,0:T(8,128)(2,1)S(1)}, bf16[2,544,128]{2,1,0:T(8,128)(2,1)S(1)}, u32[]{:S(2)}, u32[]{:S(2)}) %collective-permute-start.10) | collective-permute-done | bytes 278560 | tf_op jit(solution)/shard_map/ppermute | solution.py:709
  168.3 3.7 %add.115 = bf16[8,2,32,1024]{3,2,1,0:T(8,128)(2,1)} custom-call(bf16[8,2,32,1024]{3,2,1,0:T(8,128)(2,1)} %get-tuple-element.87.refs_0_, bf16[8,2,32,1024]{3,2,1,0:T(8,128)(2,1)} %collective-permute-done.9.refs_1_), custom_call_target="tpu_custom_call" | custom-call | bytes 1024 | tf_op jit(solution)/shard_map/add/pallas_call | solution.py:645
  172.1 5.4 %all-to-all-start.4 = ((bf16[8,2,32,1024]{3,2,1,0:T(8,128)(2,1)}), bf16[8,2,32,1024]{3,2,1,0:T(8,128)(2,1)S(1)}, u32[]{:S(2)}, u32[]{:S(2)}) async-start(bf16[8,2,32,1024]{3,2,1,0:T(8,128)(2,1)} %add.115), calls=%async_computation.4 | async-start | bytes 2097152 | tf_op jit(solution)/shard_map/all_to_all | solution.py:413
  177.5 3.0 %collective-permute-start.11 = (bf16[1,544,128]{2,1,0:T(8,128)(2,1)S(1)}, bf16[1,544,128]{2,1,0:T(8,128)(2,1)S(1)}, u32[]{:S(2)}, u32[]{:S(2)}) collective-permute-start(bf16[1,544,128]{2,1,0:T(8,128)(2,1)S(1)} %get-tuple-element.92), channel_id=1, source_target_pairs={{0,16},{4,20},{8,24},{12,28},{16,0},{20,4},{24,8},{28,12},{1,17},{... | collective-permute-start | bytes 417800 | tf_op jit(solution)/shard_map/ppermute | solution.py:709
  180.5 0.6 fusion.4
  181.1 1.9 place.3.refs_0_
  182.9 25.8 %collective-permute-done.11.other = bf16[1,544,128]{2,1,0:T(8,128)(2,1)S(1)} collective-permute-done((bf16[1,544,128]{2,1,0:T(8,128)(2,1)S(1)}, bf16[1,544,128]{2,1,0:T(8,128)(2,1)S(1)}, u32[]{:S(2)}, u32[]{:S(2)}) %collective-permute-start.11) | collective-permute-done | bytes 139296 | tf_op jit(solution)/shard_map/ppermute | solution.py:709
  208.8 1.9 finish.1
  210.7 0.8 place.4.refs_0_
  211.5 1.1 place.5
  (42 shorter events, 1.9 us)
Async XLA Ops:
  1.6 8.1 %collective-permute-start = (bf16[4,8,2048]{2,1,0:T(8,128)(2,1)S(1)}, bf16[4,8,2048]{2,1,0:T(8,128)(2,1)S(1)}, u32[]{:S(2)}, u32[]{:S(2)}) collective-permute-start(bf16[4,8,2048]{2,1,0:T(8,128)(2,1)S(1)} %pad_maximum_fusion.3), channel_id=1, source_target_pairs={{0,4},{4,8},{8,12},{12,16},{16,20},{20,24},{24,28},{1,5},{5,9},{9,... | collective-permute-start | bytes 393224 | tf_op jit(solution)/shard_map/ppermute | solution.py:453
  6.5 6.9 %collective-permute-start.1 = (bf16[4,8,2048]{2,1,0:T(8,128)(2,1)S(1)}, bf16[4,8,2048]{2,1,0:T(8,128)(2,1)S(1)}, u32[]{:S(2)}, u32[]{:S(2)}) collective-permute-start(bf16[4,8,2048]{2,1,0:T(8,128)(2,1)S(1)} %pad_maximum_fusion.4), channel_id=1, source_target_pairs={{4,0},{8,4},{12,8},{16,12},{20,16},{24,20},{28,24},{5,1},{9,5},{13... | collective-permute-start | bytes 393224 | tf_op jit(solution)/shard_map/ppermute | solution.py:453
  14.1 15.3 %copy-start.2 = (bf16[1024,256]{1,0:T(8,128)(2,1)S(1)}, bf16[1024,256]{1,0:T(8,128)(2,1)}, u32[]{:S(2)}) copy-start(bf16[1024,256]{1,0:T(8,128)(2,1)} %wv.1) | copy-start | bytes 1572868
  30.6 1.1 copy-start.6
  30.6 1.1 copy-start.7
  30.7 9.0 %collective-permute-start.2 = (bf16[512,512]{1,0:T(8,128)(2,1)S(1)}, bf16[512,512]{1,0:T(8,128)(2,1)S(1)}, u32[]{:S(2)}, u32[]{:S(2)}) collective-permute-start(bf16[512,512]{1,0:T(8,128)(2,1)S(1)} %bitcast.25), channel_id=1, source_target_pairs={{0,1},{1,0},{2,3},{3,2},{4,5},{5,4},{6,7},{7,6},{8,9},{9,8},{10,11... | collective-permute-start | bytes 1572872 | tf_op jit(solution)/shard_map/ppermute | solution.py:506
  33.2 12.3 %all-to-all-start = ((f32[8,2,256]{2,1,0:T(2,128)}), f32[8,2,256]{2,1,0:T(2,128)S(1)}, u32[]{:S(2)}, u32[]{:S(2)}) async-start(f32[8,2,256]{2,1,0:T(2,128)} %get-tuple-element.52), calls=%async_computation | async-start | bytes 32768 | tf_op jit(solution)/shard_map/all_to_all | solution.py:413
  39.7 18.4 %copy-start.1 = (bf16[512,512]{1,0:T(8,128)(2,1)}, bf16[512,512]{1,0:T(8,128)(2,1)S(1)}, u32[]{:S(2)}) copy-start(bf16[512,512]{1,0:T(8,128)(2,1)S(1)} %collective-permute-done.2.w_sibling) | copy-start | bytes 1572868
  45.5 0.6 copy-start.5
  58.2 10.1 %all-to-all-start.1 = ((f32[8,2,256]{2,1,0:T(2,128)}), f32[8,2,256]{2,1,0:T(2,128)S(1)}, u32[]{:S(2)}, u32[]{:S(2)}) async-start(f32[8,2,256]{2,1,0:T(2,128)} %get-tuple-element.56), calls=%async_computation.1 | async-start | bytes 32768 | tf_op jit(solution)/shard_map/all_to_all | solution.py:413
  68.3 0.6 copy-start.3
  73.9 5.6 %collective-permute-start.3 = (bf16[1024,512]{1,0:T(8,128)(2,1)}, bf16[1024,512]{1,0:T(8,128)(2,1)}, u32[]{:S(2)}, u32[]{:S(2)}) collective-permute-start(bf16[1024,512]{1,0:T(8,128)(2,1)} %get-tuple-element.62.own.refs_0_), channel_id=1, source_target_pairs={{0,1},{1,0},{2,3},{3,2},{4,5},{5,4},{6,7},{7,6},{8,9},{9,8},{10,11... | collective-permute-start | bytes 3145736 | tf_op jit(solution)/shard_map/ppermute | solution.py:608
  79.0 15.2 %collective-permute-start.5 = (bf16[1024,512]{1,0:T(8,128)(2,1)}, bf16[1024,512]{1,0:T(8,128)(2,1)}, u32[]{:S(2)}, u32[]{:S(2)}) collective-permute-start(bf16[1024,512]{1,0:T(8,128)(2,1)} %get-tuple-element.64.own.refs_1_), channel_id=1, source_target_pairs={{0,1},{1,0},{2,3},{3,2},{4,5},{5,4},{6,7},{7,6},{8,9},{9,8},{10,11... | collective-permute-start | bytes 3145736 | tf_op jit(solution)/shard_map/ppermute | solution.py:608
  83.8 15.3 %collective-permute-start.6 = (bf16[8,1,32,1024]{3,2,1,0:T(8,128)(2,1)}, bf16[8,1,32,1024]{3,2,1,0:T(8,128)(2,1)S(1)}, u32[]{:S(2)}, u32[]{:S(2)}) collective-permute-start(bf16[8,1,32,1024]{3,2,1,0:T(8,128)(2,1)} %get-tuple-element.68), channel_id=1, source_target_pairs={{0,2},{1,3},{2,0},{3,1},{4,6},{5,7},{6,4},{7,5},{8,10},{9,11},{10,... | collective-permute-start | bytes 1572872 | tf_op jit(solution)/shard_map/ppermute | solution.py:639
  94.1 15.5 %collective-permute-start.4 = (bf16[2048,512]{1,0:T(8,128)(2,1)}, bf16[2048,512]{1,0:T(8,128)(2,1)}, u32[]{:S(2)}, u32[]{:S(2)}) collective-permute-start(bf16[2048,512]{1,0:T(8,128)(2,1)} %get-tuple-element.70.own.refs_2_), channel_id=1, source_target_pairs={{0,1},{1,0},{2,3},{3,2},{4,5},{5,4},{6,7},{7,6},{8,9},{9,8},{10,11... | collective-permute-start | bytes 6291464 | tf_op jit(solution)/shard_map/ppermute | solution.py:608
  98.5 28.7 %collective-permute-start.7 = (bf16[8,1,32,1024]{3,2,1,0:T(8,128)(2,1)}, bf16[8,1,32,1024]{3,2,1,0:T(8,128)(2,1)}, u32[]{:S(2)}, u32[]{:S(2)}) collective-permute-start(bf16[8,1,32,1024]{3,2,1,0:T(8,128)(2,1)} %get-tuple-element.73), channel_id=1, source_target_pairs={{0,2},{1,3},{2,0},{3,1},{4,6},{5,7},{6,4},{7,5},{8,10},{9,11},{10,... | collective-permute-start | bytes 1572872 | tf_op jit(solution)/shard_map/ppermute | solution.py:639
  99.0 0.8 copy-start.8
  103.7 32.2 %all-to-all-start.2 = ((bf16[8,2,32,1024]{3,2,1,0:T(8,128)(2,1)}), bf16[8,2,32,1024]{3,2,1,0:T(8,128)(2,1)}, u32[]{:S(2)}, u32[]{:S(2)}) async-start(bf16[8,2,32,1024]{3,2,1,0:T(8,128)(2,1)} %add_join.1), calls=%async_computation.2 | async-start | bytes 2097152 | tf_op jit(solution)/shard_map/all_to_all | solution.py:413
  116.1 52.2 %collective-permute-start.9 = (bf16[8,2,32,1024]{3,2,1,0:T(8,128)(2,1)}, bf16[8,2,32,1024]{3,2,1,0:T(8,128)(2,1)}, u32[]{:S(2)}, u32[]{:S(2)}) collective-permute-start(bf16[8,2,32,1024]{3,2,1,0:T(8,128)(2,1)} %get-tuple-element.77), channel_id=1, source_target_pairs={{0,2},{1,3},{2,0},{3,1},{4,6},{5,7},{6,4},{7,5},{8,10},{9,11},{10,... | collective-permute-start | bytes 3145736 | tf_op jit(solution)/shard_map/ppermute | solution.py:639
  135.8 36.2 %all-to-all-start.3 = ((bf16[8,1,32,1024]{3,2,1,0:T(8,128)(2,1)}), bf16[8,1,32,1024]{3,2,1,0:T(8,128)(2,1)S(1)}, u32[]{:S(2)}, u32[]{:S(2)}) async-start(bf16[8,1,32,1024]{3,2,1,0:T(8,128)(2,1)} %add.114), calls=%async_computation.3 | async-start | bytes 1048576 | tf_op jit(solution)/shard_map/all_to_all | solution.py:413
  139.5 20.1 %collective-permute-start.8 = (bf16[4,544,128]{2,1,0:T(8,128)(2,1)}, bf16[4,544,128]{2,1,0:T(8,128)(2,1)S(1)}, u32[]{:S(2)}, u32[]{:S(2)}) collective-permute-start(bf16[4,544,128]{2,1,0:T(8,128)(2,1)} %get-tuple-element.85), channel_id=1, source_target_pairs={{0,4},{4,0},{8,12},{12,8},{16,20},{20,16},{24,28},{28,24},{1,5},{5... | collective-permute-start | bytes 1671176 | tf_op jit(solution)/shard_map/ppermute | solution.py:709
  159.6 1.1 copy-start
  160.8 7.5 %collective-permute-start.10 = (bf16[2,544,128]{2,1,0:T(8,128)(2,1)S(1)}, bf16[2,544,128]{2,1,0:T(8,128)(2,1)S(1)}, u32[]{:S(2)}, u32[]{:S(2)}) collective-permute-start(bf16[2,544,128]{2,1,0:T(8,128)(2,1)S(1)} %get-tuple-element.89), channel_id=1, source_target_pairs={{0,8},{4,12},{8,0},{12,4},{16,24},{20,28},{24,16},{28,20},{1,9},{5... | collective-permute-start | bytes 835592 | tf_op jit(solution)/shard_map/ppermute | solution.py:709
  168.3 9.2 %copy-start.4 = (f32[8,2,256]{2,1,0:T(2,128)S(1)}, f32[8,2,256]{2,1,0:T(2,128)}, u32[]{:S(2)}) copy-start(f32[8,2,256]{2,1,0:T(2,128)} %copy-done.3) | copy-start | bytes 49156
  172.1 39.4 %all-to-all-start.4 = ((bf16[8,2,32,1024]{3,2,1,0:T(8,128)(2,1)}), bf16[8,2,32,1024]{3,2,1,0:T(8,128)(2,1)S(1)}, u32[]{:S(2)}, u32[]{:S(2)}) async-start(bf16[8,2,32,1024]{3,2,1,0:T(8,128)(2,1)} %add.115), calls=%async_computation.4 | async-start | bytes 2097152 | tf_op jit(solution)/shard_map/all_to_all | solution.py:413
  177.5 31.3 %collective-permute-start.11 = (bf16[1,544,128]{2,1,0:T(8,128)(2,1)S(1)}, bf16[1,544,128]{2,1,0:T(8,128)(2,1)S(1)}, u32[]{:S(2)}, u32[]{:S(2)}) collective-permute-start(bf16[1,544,128]{2,1,0:T(8,128)(2,1)S(1)} %get-tuple-element.92), channel_id=1, source_target_pairs={{0,16},{4,20},{8,24},{12,28},{16,0},{20,4},{24,8},{28,12},{1,17},{... | collective-permute-start | bytes 417800 | tf_op jit(solution)/shard_map/ppermute | solution.py:709

commit v21 on v19

--- a/solution.py
+++ b/solution.py
@@ -704,12 +704,12 @@
     )(parity, after(normed, *parts[2]), *grads, *taps)
     owns[1] = deliver(parts[1], LONG, keep)
     moved[1] = exchange(after(owns[1], moved[0]), "seq")
-    owns[2] = deliver(parts[2], 0, owns[1])
     bit = 1
     while True:
         others = lax.ppermute(send, "seq", [(i, i ^ bit) for i in range(seqs)])
         if bit == 1:
-            moved[2] = exchange(after(owns[2], moved[1], others), "seq")
+            owns[2] = deliver(parts[2], LONG, others, owns[1])
+            moved[2] = exchange(after(owns[2], moved[1]), "seq")
         bit *= 2
         if bit == seqs:
             break

time: 202 us -> 195 us (0.965)
  waiting for transfers between devices: 52.3 us -> 47.1 us
    ppermute x3, waiting for transfers between devices: 36.2 us -> 29.8 us  [per_device(): others = lax.ppermute(send, 'seq', [(i, i ^ bit) for i in range(seqs)])]
  transfers between devices with their start and end apart: 17 -> 17, of which waited for: 6 -> 7; matrix products, arithmetic and copies ran while one was open for 2% -> 3% of each run, Pallas kernels for 30% -> 31%
where the time goes in v21:
time: 195 us; the launch traced here: 194 us
  Pallas kernels  94 us (48%)
  waiting for transfers between devices  47.1 us (24%)
  starting transfers between devices  41 us (21%)
  local copies, waits for them, and re-layouts  5.02 us (3%)
  other arithmetic  4.95 us (3%)
    ppermute x3, waiting for transfers between devices, per_device(): others = lax.ppermute(send, 'seq', [(i, i ^ bit) for i in range(seqs)])  29.8 us
    all_to_all x5, starting transfers between devices, exchange(): return lax.all_to_all(copies, axis, 0, 0, tiled=True)  22.3 us
    pallas_call x3, Pallas kernels, back(): call(functools.partial(back_kernel, first, blocks), 'back_conv', (size *...  18.9 us
    pallas_call x1, Pallas kernels, per_device(): call(gate_kernel, 'gate_conv', (recs,), [smem(), per_record((frames, mode...  15.3 us
    pallas_call x3, Pallas kernels, partials(): call(partial_kernel, 'partial_in', (size * parts_in,), [pl.BlockSpec((hal...  15.1 us
    all_to_all x5, waiting for transfers between devices, exchange(): return lax.all_to_all(copies, axis, 0, 0, tiled=True)  13.6 us
    pallas_call x1, Pallas kernels, per_device(): call(norm_kernel, 'swish_norm', (recs,), [smem(), smem(), whole((seqs, 2,...  12.1 us
    pallas_call x1, Pallas kernels, per_device(): call(functools.partial(outer_kernel, groups), 'outer_w_in', (recs,), [sme...  9.53 us
  transfers between devices with their start and end apart: 17, of which 7 were waited for; matrix products, arithmetic and copies ran while one was open for 3% of the time, Pallas kernels for 31%

profile of v21, /device:TPU:0, one launch (start us, length us, event | category | flops | bytes accessed | tf_op | source)
XLA Modules:
  0.0 193.6 jit_solution(10312411390651507459)
XLA Ops:
  0.6 1.0 fusion.1
  1.6 4.9 %collective-permute-start = (bf16[4,8,2048]{2,1,0:T(8,128)(2,1)S(1)}, bf16[4,8,2048]{2,1,0:T(8,128)(2,1)S(1)}, u32[]{:S(2)}, u32[]{:S(2)}) collective-permute-start(bf16[4,8,2048]{2,1,0:T(8,128)(2,1)S(1)} %pad_maximum_fusion.3), channel_id=1, source_target_pairs={{0,4},{4,8},{8,12},{12,16},{16,20},{20,24},{24,28},{1,5},{5,9},{9,... | collective-permute-start | bytes 393224 | tf_op jit(solution)/shard_map/ppermute | solution.py:453
  6.5 1.3 collective-permute-start.1
  7.8 1.3 fusion.5
  9.7 3.7 %collective-permute-done.1 = bf16[4,8,2048]{2,1,0:T(8,128)(2,1)S(1)} collective-permute-done((bf16[4,8,2048]{2,1,0:T(8,128)(2,1)S(1)}, bf16[4,8,2048]{2,1,0:T(8,128)(2,1)S(1)}, u32[]{:S(2)}, u32[]{:S(2)}) %collective-permute-start.1) | collective-permute-done | bytes 131104 | tf_op jit(solution)/shard_map/ppermute | solution.py:453
  13.4 0.7 fusion.3
  14.1 15.3 %gate_conv.1 = (f32[4,1024,256]{2,1,0:T(8,128)}, f32[4,1024,256]{2,1,0:T(8,128)}, f32[4,1040,256]{2,1,0:T(8,128)}, f32[8,2,256]{2,1,0:T(2,128)}) custom-call(s32[2,4]{1,0:T(2,128)} %stack.35.meta, bf16[4,1024,1024]{2,1,0:T(8,128)(2,1)} %x.4, bf16[4,16,1024]{2,1,0:T(8,128)(2,1)} %get-tuple-element.106.halo, bf16[1024,256]{1,0:T(8,128)(2,1)} %wv.1, ...), custom_call_target="tpu_custom_call" | custom-call | flops 4294967296 | bytes 20971520 | tf_op jit(solution)/shard_map/gate_conv/pallas_call | solution.py:467
  29.4 1.1 pad_maximum_fusion
  31.6 0.6 pad_maximum_fusion.5.affine
  32.2 1.0 fusion.select
  33.2 5.7 %all-to-all-start = ((f32[8,2,256]{2,1,0:T(2,128)}), f32[8,2,256]{2,1,0:T(2,128)S(1)}, u32[]{:S(2)}, u32[]{:S(2)}) async-start(f32[8,2,256]{2,1,0:T(2,128)} %get-tuple-element.52), calls=%async_computation | async-start | bytes 32768 | tf_op jit(solution)/shard_map/all_to_all | solution.py:413
  38.9 0.8 pad_maximum_fusion.1
  39.7 5.7 %all-to-all-done.stats = f32[8,2,256]{2,1,0:T(2,128)S(1)} async-done(((f32[8,2,256]{2,1,0:T(2,128)}), f32[8,2,256]{2,1,0:T(2,128)S(1)}, u32[]{:S(2)}, u32[]{:S(2)}) %all-to-all-start) | async-done | bytes 16416 | tf_op jit(solution)/shard_map/all_to_all | solution.py:413
  45.5 0.6 copy-done.5
  46.1 12.1 %swish_norm.1 = (bf16[4,1024,256]{2,1,0:T(8,128)(2,1)}, f32[4,1040,256]{2,1,0:T(8,128)}, bf16[4,256,1024]{2,1,0:T(8,128)(2,1)}, f32[8,2,256]{2,1,0:T(2,128)}) custom-call(s32[2,4]{1,0:T(2,128)} %stack.35.meta, f32[1,1]{1,0:T(1,128)} %bitcast.1.count, f32[8,2,256]{2,1,0:T(2,128)} %copy-done.5, f32[2,256]{1,0:T(2,128)} %pad_maximum_fusion.5.affine, ...), custom_call_target="tpu_custom_call" | custom-call | flops 4294967296 | bytes 20971520 | tf_op jit(solution)/shard_map/swish_norm/pallas_call | solution.py:512
  58.2 3.3 %all-to-all-start.1 = ((f32[8,2,256]{2,1,0:T(2,128)}), f32[8,2,256]{2,1,0:T(2,128)S(1)}, u32[]{:S(2)}, u32[]{:S(2)}) async-start(f32[8,2,256]{2,1,0:T(2,128)} %get-tuple-element.56), calls=%async_computation.1 | async-start | bytes 32768 | tf_op jit(solution)/shard_map/all_to_all | solution.py:413
  61.5 6.7 %outer_w_out.1.refs_2_ = bf16[8,1,32,1024]{3,2,1,0:T(8,128)(2,1)} custom-call(bf16[4,1024,1024]{2,1,0:T(8,128)(2,1)} %grads.3, bf16[4,1024,256]{2,1,0:T(8,128)(2,1)} %get-tuple-element.60.swished), custom_call_target="tpu_custom_call" | custom-call | flops 2147483648 | bytes 8388608 | tf_op jit(solution)/shard_map/outer_w_out/pallas_call | solution.py:557
  68.3 0.6 copy-done.3
  68.9 5.0 %back_conv.3 = (bf16[1024,512]{1,0:T(8,128)(2,1)}, f32[16,256]{1,0:T(8,128)}) custom-call(s32[2,4]{1,0:T(2,128)} %stack.35.meta, f32[1,1]{1,0:T(1,128)} %bitcast.1.count, f32[8,2,256]{2,1,0:T(2,128)} %copy-done.5, f32[8,2,256]{2,1,0:T(2,128)} %copy-done.3, f32[1,256]{1,0:T(1,128)} %bitcast.26, f32[4,1040,256]{2,1,0:T(8,128)} %get-tuple-element.57.gn, ...), custom_call_target="tpu_custom_call" | custom-call | bytes 1024 | tf_op jit(solution)/shard_map/back_conv/pallas_call | solution.py:581
  73.9 5.0 %back_conv.4 = (bf16[1024,512]{1,0:T(8,128)(2,1)}, f32[16,256]{1,0:T(8,128)}) custom-call(s32[2,4]{1,0:T(2,128)} %stack.35.meta, f32[1,1]{1,0:T(1,128)} %bitcast.1.count, f32[8,2,256]{2,1,0:T(2,128)} %copy-done.5, f32[8,2,256]{2,1,0:T(2,128)} %copy-done.3, f32[1,256]{1,0:T(1,128)} %bitcast.27, f32[4,1040,256]{2,1,0:T(8,128)} %get-tuple-element.57.gn, ...), custom_call_target="tpu_custom_call" | custom-call | bytes 1024 | tf_op jit(solution)/shard_map/back_conv/pallas_call | solution.py:581
  79.5 4.2 %partial_in.3 = (bf16[8,1,32,1024]{3,2,1,0:T(8,128)(2,1)}, bf16[8,1,32,1024]{3,2,1,0:T(8,128)(2,1)}) custom-call(bf16[1024,512]{1,0:T(8,128)(2,1)} %get-tuple-element.62.own.refs_0_, bf16[1024,512]{1,0:T(8,128)(2,1)} %collective-permute-done.3.sibling, bf16[512,512]{1,0:T(8,128)(2,1)} %bitcast.21, bf16[512,512]{1,0:T(8,128)(2,1)} %copy-done.1, ...), custom_call_target="tpu_custom_call" | custom-call | bytes 1024 | tf_op jit(solution)/shard_map/partial_in/pallas_call | solution.py:610
  83.7 1.5 collective-permute-start.6
  85.2 8.8 %back_conv.5 = (bf16[2048,512]{1,0:T(8,128)(2,1)}, f32[16,256]{1,0:T(8,128)}) custom-call(s32[2,4]{1,0:T(2,128)} %stack.35.meta, f32[1,1]{1,0:T(1,128)} %bitcast.1.count, f32[8,2,256]{2,1,0:T(2,128)} %copy-done.5, f32[8,2,256]{2,1,0:T(2,128)} %copy-done.3, f32[1,256]{1,0:T(1,128)} %bitcast.28, f32[4,1040,256]{2,1,0:T(8,128)} %get-tuple-element.57.gn, ...), custom_call_target="tpu_custom_call" | custom-call | bytes 1024 | tf_op jit(solution)/shard_map/back_conv/pallas_call | solution.py:581
  94.2 4.3 %partial_in.4 = (bf16[8,1,32,1024]{3,2,1,0:T(8,128)(2,1)}, bf16[8,1,32,1024]{3,2,1,0:T(8,128)(2,1)}) custom-call(bf16[1024,512]{1,0:T(8,128)(2,1)} %get-tuple-element.64.own.refs_1_, bf16[1024,512]{1,0:T(8,128)(2,1)} %collective-permute-done.5.sibling, bf16[512,512]{1,0:T(8,128)(2,1)} %bitcast.22, bf16[512,512]{1,0:T(8,128)(2,1)} %copy-done.1, ...), custom_call_target="tpu_custom_call" | custom-call | bytes 1024 | tf_op jit(solution)/shard_map/partial_in/pallas_call | solution.py:610
  99.0 3.8 %add_join.1 = bf16[8,2,32,1024]{3,2,1,0:T(8,128)(2,1)} custom-call(bf16[8,1,32,1024]{3,2,1,0:T(8,128)(2,1)} %get-tuple-element.74.refs_0_, bf16[8,1,32,1024]{3,2,1,0:T(8,128)(2,1)} %collective-permute-done.6.refs_1_, bf16[8,1,32,1024]{3,2,1,0:T(8,128)(2,1)} %outer_w_out.1.refs_2_), custom_call_target="tpu_custom_call" | custom-call | flops 49999998976 | bytes 1024 | tf_op jit(solution)/shard_map/add_join/pallas_call | solution.py:657
  102.8 5.9 %all-to-all-start.2 = ((bf16[8,2,32,1024]{3,2,1,0:T(8,128)(2,1)}), bf16[8,2,32,1024]{3,2,1,0:T(8,128)(2,1)}, u32[]{:S(2)}, u32[]{:S(2)}) async-start(bf16[8,2,32,1024]{3,2,1,0:T(8,128)(2,1)} %add_join.1), calls=%async_computation.2 | async-start | bytes 2097152 | tf_op jit(solution)/shard_map/all_to_all | solution.py:413
  108.8 6.5 %partial_in.5 = (bf16[8,2,32,1024]{3,2,1,0:T(8,128)(2,1)}, bf16[8,2,32,1024]{3,2,1,0:T(8,128)(2,1)}) custom-call(bf16[2048,512]{1,0:T(8,128)(2,1)} %get-tuple-element.70.own.refs_2_, bf16[2048,512]{1,0:T(8,128)(2,1)} %collective-permute-done.4.sibling, bf16[512,512]{1,0:T(8,128)(2,1)} %bitcast.23, bf16[512,512]{1,0:T(8,128)(2,1)} %copy-done.1, ...), custom_call_target="tpu_custom_call" | custom-call | bytes 1024 | tf_op jit(solution)/shard_map/partial_in/pallas_call | solution.py:610
  115.3 1.5 collective-permute-start.9
  116.8 9.5 %outer_w_in.1 = (bf16[4,544,128]{2,1,0:T(8,128)(2,1)}, bf16[4,544,128]{2,1,0:T(8,128)(2,1)}) custom-call(s32[1,1]{1,0:T(1,128)} %bitcast.11.parity, bf16[4,1024,1024]{2,1,0:T(8,128)(2,1)} %x.4, bf16[1024,512]{1,0:T(8,128)(2,1)} %get-tuple-element.62.own.refs_0_, bf16[1024,512]{1,0:T(8,128)(2,1)} %get-tuple-element.64.own.refs_1_, ...), custom_call_target="tpu_custom_call" | custom-call | flops 49999998976 | bytes 1024 | tf_op jit(solution)/shard_map/outer_w_in/pallas_call | solution.py:686
  126.3 2.0 %collective-permute-start.7 = (bf16[4,544,128]{2,1,0:T(8,128)(2,1)}, bf16[4,544,128]{2,1,0:T(8,128)(2,1)}, u32[]{:S(2)}, u32[]{:S(2)}) collective-permute-start(bf16[4,544,128]{2,1,0:T(8,128)(2,1)} %get-tuple-element.82), channel_id=1, source_target_pairs={{0,4},{4,0},{8,12},{12,8},{16,20},{20,16},{24,28},{28,24},{1,5},{5... | collective-permute-start | bytes 1671176 | tf_op jit(solution)/shard_map/ppermute | solution.py:709
  128.3 0.8 copy-done.8
  129.1 2.0 %add.114 = bf16[8,1,32,1024]{3,2,1,0:T(8,128)(2,1)} custom-call(bf16[8,1,32,1024]{3,2,1,0:T(8,128)(2,1)} %get-tuple-element.84.refs_0_, bf16[8,1,32,1024]{3,2,1,0:T(8,128)(2,1)} %copy-done.8), custom_call_target="tpu_custom_call" | custom-call | flops 49999998976 | bytes 1024 | tf_op jit(solution)/shard_map/add/pallas_call | solution.py:645
  131.1 3.9 %all-to-all-done.2.moved.pieces = bf16[8,2,32,1024]{3,2,1,0:T(8,128)(2,1)} async-done(((bf16[8,2,32,1024]{3,2,1,0:T(8,128)(2,1)}), bf16[8,2,32,1024]{3,2,1,0:T(8,128)(2,1)}, u32[]{:S(2)}, u32[]{:S(2)}) %all-to-all-start.2) | async-done | bytes 1048608 | tf_op jit(solution)/shard_map/all_to_all | solution.py:413
  135.0 3.7 %all-to-all-start.3 = ((bf16[8,1,32,1024]{3,2,1,0:T(8,128)(2,1)}), bf16[8,1,32,1024]{3,2,1,0:T(8,128)(2,1)S(1)}, u32[]{:S(2)}, u32[]{:S(2)}) async-start(bf16[8,1,32,1024]{3,2,1,0:T(8,128)(2,1)} %add.114), calls=%async_computation.3 | async-start | bytes 1048576 | tf_op jit(solution)/shard_map/all_to_all | solution.py:413
  138.7 7.0 %collective-permute-done.7.other = bf16[4,544,128]{2,1,0:T(8,128)(2,1)} collective-permute-done((bf16[4,544,128]{2,1,0:T(8,128)(2,1)}, bf16[4,544,128]{2,1,0:T(8,128)(2,1)}, u32[]{:S(2)}, u32[]{:S(2)}) %collective-permute-start.7) | collective-permute-done | bytes 557088 | tf_op jit(solution)/shard_map/ppermute | solution.py:709
  145.7 3.7 %add.115 = bf16[8,2,32,1024]{3,2,1,0:T(8,128)(2,1)} custom-call(bf16[8,2,32,1024]{3,2,1,0:T(8,128)(2,1)} %get-tuple-element.85.refs_0_, bf16[8,2,32,1024]{3,2,1,0:T(8,128)(2,1)} %collective-permute-done.9.refs_1_), custom_call_target="tpu_custom_call" | custom-call | flops 49999998976 | bytes 1024 | tf_op jit(solution)/shard_map/add/pallas_call | solution.py:645
  149.4 4.0 %all-to-all-done.3.moved = bf16[8,1,32,1024]{3,2,1,0:T(8,128)(2,1)S(1)} async-done(((bf16[8,1,32,1024]{3,2,1,0:T(8,128)(2,1)}), bf16[8,1,32,1024]{3,2,1,0:T(8,128)(2,1)S(1)}, u32[]{:S(2)}, u32[]{:S(2)}) %all-to-all-start.3) | async-done | bytes 524320 | tf_op jit(solution)/shard_map/all_to_all | solution.py:413
  153.3 3.6 %all-to-all-start.4 = ((bf16[8,2,32,1024]{3,2,1,0:T(8,128)(2,1)}), bf16[8,2,32,1024]{3,2,1,0:T(8,128)(2,1)S(1)}, u32[]{:S(2)}, u32[]{:S(2)}) async-start(bf16[8,2,32,1024]{3,2,1,0:T(8,128)(2,1)} %add.115), calls=%async_computation.4 | async-start | bytes 2097152 | tf_op jit(solution)/shard_map/all_to_all | solution.py:413
  157.0 1.2 fold.2
  158.2 2.1 %collective-permute-start.10 = (bf16[2,544,128]{2,1,0:T(8,128)(2,1)S(1)}, bf16[2,544,128]{2,1,0:T(8,128)(2,1)S(1)}, u32[]{:S(2)}, u32[]{:S(2)}) collective-permute-start(bf16[2,544,128]{2,1,0:T(8,128)(2,1)S(1)} %get-tuple-element.90), channel_id=1, source_target_pairs={{0,8},{4,12},{8,0},{12,4},{16,24},{20,28},{24,16},{28,20},{1,9},{5... | collective-permute-start | bytes 835592 | tf_op jit(solution)/shard_map/ppermute | solution.py:709
  160.3 20.4 %collective-permute-done.10.other = bf16[2,544,128]{2,1,0:T(8,128)(2,1)S(1)} collective-permute-done((bf16[2,544,128]{2,1,0:T(8,128)(2,1)S(1)}, bf16[2,544,128]{2,1,0:T(8,128)(2,1)S(1)}, u32[]{:S(2)}, u32[]{:S(2)}) %collective-permute-start.10) | collective-permute-done | bytes 278560 | tf_op jit(solution)/shard_map/ppermute | solution.py:709
  180.7 4.2 %collective-permute-start.11 = (bf16[1,544,128]{2,1,0:T(8,128)(2,1)S(1)}, bf16[1,544,128]{2,1,0:T(8,128)(2,1)S(1)}, u32[]{:S(2)}, u32[]{:S(2)}) collective-permute-start(bf16[1,544,128]{2,1,0:T(8,128)(2,1)S(1)} %get-tuple-element.92), channel_id=1, source_target_pairs={{0,16},{4,20},{8,24},{12,28},{16,0},{20,4},{24,8},{28,12},{1,17},{... | collective-permute-start | bytes 417800 | tf_op jit(solution)/shard_map/ppermute | solution.py:709
  184.9 0.6 fusion.4
  185.5 1.9 place.3.refs_0_
  187.3 0.8 place.4.refs_0_
  188.2 2.5 %collective-permute-done.11.other = bf16[1,544,128]{2,1,0:T(8,128)(2,1)S(1)} collective-permute-done((bf16[1,544,128]{2,1,0:T(8,128)(2,1)S(1)}, bf16[1,544,128]{2,1,0:T(8,128)(2,1)S(1)}, u32[]{:S(2)}, u32[]{:S(2)}) %collective-permute-start.11) | collective-permute-done | bytes 139296 | tf_op jit(solution)/shard_map/ppermute | solution.py:709
  190.6 1.9 finish.1
  192.5 1.1 place.5
  (42 shorter events, 2.3 us)
Async XLA Ops:
  1.6 8.1 %collective-permute-start = (bf16[4,8,2048]{2,1,0:T(8,128)(2,1)S(1)}, bf16[4,8,2048]{2,1,0:T(8,128)(2,1)S(1)}, u32[]{:S(2)}, u32[]{:S(2)}) collective-permute-start(bf16[4,8,2048]{2,1,0:T(8,128)(2,1)S(1)} %pad_maximum_fusion.3), channel_id=1, source_target_pairs={{0,4},{4,8},{8,12},{12,16},{16,20},{20,24},{24,28},{1,5},{5,9},{9,... | collective-permute-start | bytes 393224 | tf_op jit(solution)/shard_map/ppermute | solution.py:453
  6.5 6.9 %collective-permute-start.1 = (bf16[4,8,2048]{2,1,0:T(8,128)(2,1)S(1)}, bf16[4,8,2048]{2,1,0:T(8,128)(2,1)S(1)}, u32[]{:S(2)}, u32[]{:S(2)}) collective-permute-start(bf16[4,8,2048]{2,1,0:T(8,128)(2,1)S(1)} %pad_maximum_fusion.4), channel_id=1, source_target_pairs={{4,0},{8,4},{12,8},{16,12},{20,16},{24,20},{28,24},{5,1},{9,5},{13... | collective-permute-start | bytes 393224 | tf_op jit(solution)/shard_map/ppermute | solution.py:453
  14.1 15.3 %copy-start.2 = (bf16[1024,256]{1,0:T(8,128)(2,1)S(1)}, bf16[1024,256]{1,0:T(8,128)(2,1)}, u32[]{:S(2)}) copy-start(bf16[1024,256]{1,0:T(8,128)(2,1)} %wv.1) | copy-start | bytes 1572868
  30.6 1.1 copy-start.6
  30.6 1.1 copy-start.7
  30.7 9.0 %collective-permute-start.2 = (bf16[512,512]{1,0:T(8,128)(2,1)S(1)}, bf16[512,512]{1,0:T(8,128)(2,1)S(1)}, u32[]{:S(2)}, u32[]{:S(2)}) collective-permute-start(bf16[512,512]{1,0:T(8,128)(2,1)S(1)} %bitcast.25), channel_id=1, source_target_pairs={{0,1},{1,0},{2,3},{3,2},{4,5},{5,4},{6,7},{7,6},{8,9},{9,8},{10,11... | collective-permute-start | bytes 1572872 | tf_op jit(solution)/shard_map/ppermute | solution.py:506
  33.2 12.3 %all-to-all-start = ((f32[8,2,256]{2,1,0:T(2,128)}), f32[8,2,256]{2,1,0:T(2,128)S(1)}, u32[]{:S(2)}, u32[]{:S(2)}) async-start(f32[8,2,256]{2,1,0:T(2,128)} %get-tuple-element.52), calls=%async_computation | async-start | bytes 32768 | tf_op jit(solution)/shard_map/all_to_all | solution.py:413
  39.7 18.4 %copy-start.1 = (bf16[512,512]{1,0:T(8,128)(2,1)}, bf16[512,512]{1,0:T(8,128)(2,1)S(1)}, u32[]{:S(2)}) copy-start(bf16[512,512]{1,0:T(8,128)(2,1)S(1)} %collective-permute-done.2.w_sibling) | copy-start | bytes 1572868
  45.5 0.6 copy-start.5
  58.2 10.1 %all-to-all-start.1 = ((f32[8,2,256]{2,1,0:T(2,128)}), f32[8,2,256]{2,1,0:T(2,128)S(1)}, u32[]{:S(2)}, u32[]{:S(2)}) async-start(f32[8,2,256]{2,1,0:T(2,128)} %get-tuple-element.56), calls=%async_computation.1 | async-start | bytes 32768 | tf_op jit(solution)/shard_map/all_to_all | solution.py:413
  68.3 0.6 copy-start.3
  73.9 5.6 %collective-permute-start.3 = (bf16[1024,512]{1,0:T(8,128)(2,1)}, bf16[1024,512]{1,0:T(8,128)(2,1)}, u32[]{:S(2)}, u32[]{:S(2)}) collective-permute-start(bf16[1024,512]{1,0:T(8,128)(2,1)} %get-tuple-element.62.own.refs_0_), channel_id=1, source_target_pairs={{0,1},{1,0},{2,3},{3,2},{4,5},{5,4},{6,7},{7,6},{8,9},{9,8},{10,11... | collective-permute-start | bytes 3145736 | tf_op jit(solution)/shard_map/ppermute | solution.py:608
  79.0 15.2 %collective-permute-start.5 = (bf16[1024,512]{1,0:T(8,128)(2,1)}, bf16[1024,512]{1,0:T(8,128)(2,1)}, u32[]{:S(2)}, u32[]{:S(2)}) collective-permute-start(bf16[1024,512]{1,0:T(8,128)(2,1)} %get-tuple-element.64.own.refs_1_), channel_id=1, source_target_pairs={{0,1},{1,0},{2,3},{3,2},{4,5},{5,4},{6,7},{7,6},{8,9},{9,8},{10,11... | collective-permute-start | bytes 3145736 | tf_op jit(solution)/shard_map/ppermute | solution.py:608
  83.7 15.3 %collective-permute-start.6 = (bf16[8,1,32,1024]{3,2,1,0:T(8,128)(2,1)}, bf16[8,1,32,1024]{3,2,1,0:T(8,128)(2,1)}, u32[]{:S(2)}, u32[]{:S(2)}) collective-permute-start(bf16[8,1,32,1024]{3,2,1,0:T(8,128)(2,1)} %get-tuple-element.68), channel_id=1, source_target_pairs={{0,2},{1,3},{2,0},{3,1},{4,6},{5,7},{6,4},{7,5},{8,10},{9,11},{10,... | collective-permute-start | bytes 1572872 | tf_op jit(solution)/shard_map/ppermute | solution.py:639
  94.1 14.7 %collective-permute-start.4 = (bf16[2048,512]{1,0:T(8,128)(2,1)}, bf16[2048,512]{1,0:T(8,128)(2,1)}, u32[]{:S(2)}, u32[]{:S(2)}) collective-permute-start(bf16[2048,512]{1,0:T(8,128)(2,1)} %get-tuple-element.70.own.refs_2_), channel_id=1, source_target_pairs={{0,1},{1,0},{2,3},{3,2},{4,5},{5,4},{6,7},{7,6},{8,9},{9,8},{10,11... | collective-permute-start | bytes 6291464 | tf_op jit(solution)/shard_map/ppermute | solution.py:608
  98.5 29.9 %collective-permute-start.8 = (bf16[8,1,32,1024]{3,2,1,0:T(8,128)(2,1)}, bf16[8,1,32,1024]{3,2,1,0:T(8,128)(2,1)S(1)}, u32[]{:S(2)}, u32[]{:S(2)}) collective-permute-start(bf16[8,1,32,1024]{3,2,1,0:T(8,128)(2,1)} %get-tuple-element.73), channel_id=1, source_target_pairs={{0,2},{1,3},{2,0},{3,1},{4,6},{5,7},{6,4},{7,5},{8,10},{9,11},{10,... | collective-permute-start | bytes 1572872 | tf_op jit(solution)/shard_map/ppermute | solution.py:639
  102.8 32.2 %all-to-all-start.2 = ((bf16[8,2,32,1024]{3,2,1,0:T(8,128)(2,1)}), bf16[8,2,32,1024]{3,2,1,0:T(8,128)(2,1)}, u32[]{:S(2)}, u32[]{:S(2)}) async-start(bf16[8,2,32,1024]{3,2,1,0:T(8,128)(2,1)} %add_join.1), calls=%async_computation.2 | async-start | bytes 2097152 | tf_op jit(solution)/shard_map/all_to_all | solution.py:413
  115.3 30.4 %collective-permute-start.9 = (bf16[8,2,32,1024]{3,2,1,0:T(8,128)(2,1)}, bf16[8,2,32,1024]{3,2,1,0:T(8,128)(2,1)}, u32[]{:S(2)}, u32[]{:S(2)}) collective-permute-start(bf16[8,2,32,1024]{3,2,1,0:T(8,128)(2,1)} %get-tuple-element.77), channel_id=1, source_target_pairs={{0,2},{1,3},{2,0},{3,1},{4,6},{5,7},{6,4},{7,5},{8,10},{9,11},{10,... | collective-permute-start | bytes 3145736 | tf_op jit(solution)/shard_map/ppermute | solution.py:639
  126.3 19.4 %collective-permute-start.7 = (bf16[4,544,128]{2,1,0:T(8,128)(2,1)}, bf16[4,544,128]{2,1,0:T(8,128)(2,1)}, u32[]{:S(2)}, u32[]{:S(2)}) collective-permute-start(bf16[4,544,128]{2,1,0:T(8,128)(2,1)} %get-tuple-element.82), channel_id=1, source_target_pairs={{0,4},{4,0},{8,12},{12,8},{16,20},{20,16},{24,28},{28,24},{1,5},{5... | collective-permute-start | bytes 1671176 | tf_op jit(solution)/shard_map/ppermute | solution.py:709
  128.3 0.8 copy-start.8
  135.0 18.3 %all-to-all-start.3 = ((bf16[8,1,32,1024]{3,2,1,0:T(8,128)(2,1)}), bf16[8,1,32,1024]{3,2,1,0:T(8,128)(2,1)S(1)}, u32[]{:S(2)}, u32[]{:S(2)}) async-start(bf16[8,1,32,1024]{3,2,1,0:T(8,128)(2,1)} %add.114), calls=%async_computation.3 | async-start | bytes 1048576 | tf_op jit(solution)/shard_map/all_to_all | solution.py:413
  149.4 7.6 %copy-start = (bf16[4,544,128]{2,1,0:T(8,128)(2,1)S(1)}, bf16[4,544,128]{2,1,0:T(8,128)(2,1)}, u32[]{:S(2)}) copy-start(bf16[4,544,128]{2,1,0:T(8,128)(2,1)} %get-tuple-element.88.own) | copy-start | bytes 1671172
  149.4 10.9 %copy-start.4 = (f32[8,2,256]{2,1,0:T(2,128)S(1)}, f32[8,2,256]{2,1,0:T(2,128)}, u32[]{:S(2)}) copy-start(f32[8,2,256]{2,1,0:T(2,128)} %copy-done.3) | copy-start | bytes 49156
  153.3 39.2 %all-to-all-start.4 = ((bf16[8,2,32,1024]{3,2,1,0:T(8,128)(2,1)}), bf16[8,2,32,1024]{3,2,1,0:T(8,128)(2,1)S(1)}, u32[]{:S(2)}, u32[]{:S(2)}) async-start(bf16[8,2,32,1024]{3,2,1,0:T(8,128)(2,1)} %add.115), calls=%async_computation.4 | async-start | bytes 2097152 | tf_op jit(solution)/shard_map/all_to_all | solution.py:413
  158.2 22.5 %collective-permute-start.10 = (bf16[2,544,128]{2,1,0:T(8,128)(2,1)S(1)}, bf16[2,544,128]{2,1,0:T(8,128)(2,1)S(1)}, u32[]{:S(2)}, u32[]{:S(2)}) collective-permute-start(bf16[2,544,128]{2,1,0:T(8,128)(2,1)S(1)} %get-tuple-element.90), channel_id=1, source_target_pairs={{0,8},{4,12},{8,0},{12,4},{16,24},{20,28},{24,16},{28,20},{1,9},{5... | collective-permute-start | bytes 835592 | tf_op jit(solution)/shard_map/ppermute | solution.py:709
  180.7 9.9 %collective-permute-start.11 = (bf16[1,544,128]{2,1,0:T(8,128)(2,1)S(1)}, bf16[1,544,128]{2,1,0:T(8,128)(2,1)S(1)}, u32[]{:S(2)}, u32[]{:S(2)}) collective-permute-start(bf16[1,544,128]{2,1,0:T(8,128)(2,1)S(1)} %get-tuple-element.92), channel_id=1, source_target_pairs={{0,16},{4,20},{8,24},{12,28},{16,0},{20,4},{24,8},{28,12},{1,17},{... | collective-permute-start | bytes 417800 | tf_op jit(solution)/shard_map/ppermute | solution.py:709

commit v22 on v21

--- a/solution.py
+++ b/solution.py
@@ -384,7 +384,7 @@
         write(send, 0)
 
 
-def finish_kernel(kernel, own, other, pieces, value, gate, out, taps):
+def finish_kernel(kernel, own, other, value, gate, taps):
     width = value.shape[1]
     shard = value.shape[0]
 
@@ -393,13 +393,17 @@
 
     value[...] = total(0, width).T
     gate[...] = total(width, width).T
+    for q in range(width // shard):
+        taps[:, q * shard : (q + 1) * shard] = total(2 * width + 16 * q, 16)[:kernel]
+
+
+def finish_out_kernel(pieces, out):
+    shard = out.shape[0]
     ready = pieces[0, 0].astype(F32)
     for s in range(1, pieces.shape[0]):
         ready = ready + pieces[s, 0].astype(F32)
     blocks = [ready[:, q * shard : (q + 1) * shard] for q in range(ready.shape[1] // shard)]
     out[...] = jnp.concatenate(blocks, axis=0).T
-    for q in range(width // shard):
-        taps[:, q * shard : (q + 1) * shard] = total(2 * width + 16 * q, 16)[:kernel]
 
 
 def place_kernel(moved, *refs):
@@ -725,23 +729,34 @@
             [whole(shape)] * 2,
             [sds(shape, BF16)] * 2,
             [],
-            0,
+            2 * LONG if bit == 4 else 0,
             1024,
             vmem=20,
         )(side, keep, others)
-    w_value, w_gate, w_out, grad_taps = call(
-        functools.partial(finish_kernel, kernel),
-        "finish",
+    w_out = call(
+        finish_out_kernel,
+        "finish_w_out",
         (1,),
-        [whole(keep.shape)] * 2
-        + [pl.BlockSpec((seqs, 1, piece, frames), lambda i: (0, 1, 0, 0))],
-        [whole((shard, width))] * 3 + [whole((kernel, width))],
-        [sds((shard, width), F32)] * 3 + [sds((kernel, width), F32)],
+        [pl.BlockSpec((seqs, 1, piece, frames), lambda i: (0, 1, 0, 0))],
+        whole((shard, width)),
+        sds((shard, width), F32),
         [],
         0,
         1024,
         vmem=20,
-    )(keep, others, moved[0])
+    )(moved[0])
+    w_value, w_gate, grad_taps = call(
+        functools.partial(finish_kernel, kernel),
+        "finish",
+        (1,),
+        [whole(keep.shape)] * 2,
+        [whole((shard, width))] * 2 + [whole((kernel, width))],
+        [sds((shard, width), F32)] * 2 + [sds((kernel, width), F32)],
+        [],
+        0,
+        1024,
+        vmem=20,
+    )(keep, others)
     grad_in = ()
     for (first, size), part in zip(groups, moved):
         grad_in = (

time: 195 us -> 193 us (0.990)
  starting transfers between devices: 41 us -> 38.8 us
    ppermute x3, starting transfers between devices: 8.25 us -> 5.66 us  [per_device(): others = lax.ppermute(send, 'seq', [(i, i ^ bit) for i in range(seqs)])]
  transfers between devices with their start and end apart: 17 -> 17, of which waited for: 7 -> 7; matrix products, arithmetic and copies ran while one was open for 3% -> 3% of each run, Pallas kernels for 31% -> 32%
where the time goes in v22:
time: 193 us; the launch traced here: 192 us
  Pallas kernels  94.8 us (49%)
  waiting for transfers between devices  45.7 us (24%)
  starting transfers between devices  38.8 us (20%)
  local copies, waits for them, and re-layouts  6.11 us (3%)
  other arithmetic  4.95 us (3%)
    ppermute x3, waiting for transfers between devices, per_device(): others = lax.ppermute(send, 'seq', [(i, i ^ bit) for i in range(seqs)])  29.9 us
    all_to_all x5, starting transfers between devices, exchange(): return lax.all_to_all(copies, axis, 0, 0, tiled=True)  22.8 us
    pallas_call x3, Pallas kernels, back(): call(functools.partial(back_kernel, first, blocks), 'back_conv', (size *...  18.9 us
    pallas_call x1, Pallas kernels, per_device(): call(gate_kernel, 'gate_conv', (recs,), [smem(), per_record((frames, mode...  15.3 us
    pallas_call x3, Pallas kernels, partials(): call(partial_kernel, 'partial_in', (size * parts_in,), [pl.BlockSpec((hal...  15.1 us
    all_to_all x5, waiting for transfers between devices, exchange(): return lax.all_to_all(copies, axis, 0, 0, tiled=True)  12.2 us
    pallas_call x1, Pallas kernels, per_device(): call(norm_kernel, 'swish_norm', (recs,), [smem(), smem(), whole((seqs, 2,...  12.1 us
    pallas_call x1, Pallas kernels, per_device(): call(functools.partial(outer_kernel, groups), 'outer_w_in', (recs,), [sme...  9.53 us
  transfers between devices with their start and end apart: 17, of which 7 were waited for; matrix products, arithmetic and copies ran while one was open for 3% of the time, Pallas kernels for 32%

profile of v22, /device:TPU:0, one launch (start us, length us, event | category | flops | bytes accessed | tf_op | source)
XLA Modules:
  0.0 191.9 jit_solution(3649218437160844957)
XLA Ops:
  0.6 1.0 fusion.1
  1.6 4.9 %collective-permute-start = (bf16[4,8,2048]{2,1,0:T(8,128)(2,1)S(1)}, bf16[4,8,2048]{2,1,0:T(8,128)(2,1)S(1)}, u32[]{:S(2)}, u32[]{:S(2)}) collective-permute-start(bf16[4,8,2048]{2,1,0:T(8,128)(2,1)S(1)} %pad_maximum_fusion.3), channel_id=1, source_target_pairs={{0,4},{4,8},{8,12},{12,16},{16,20},{20,24},{24,28},{1,5},{5,9},{9,... | collective-permute-start | bytes 393224 | tf_op jit(solution)/shard_map/ppermute | solution.py:457
  6.5 1.3 collective-permute-start.1
  7.8 1.3 fusion.5
  9.7 3.7 %collective-permute-done.1 = bf16[4,8,2048]{2,1,0:T(8,128)(2,1)S(1)} collective-permute-done((bf16[4,8,2048]{2,1,0:T(8,128)(2,1)S(1)}, bf16[4,8,2048]{2,1,0:T(8,128)(2,1)S(1)}, u32[]{:S(2)}, u32[]{:S(2)}) %collective-permute-start.1) | collective-permute-done | bytes 131104 | tf_op jit(solution)/shard_map/ppermute | solution.py:457
  13.4 0.7 fusion.3
  14.1 15.3 %gate_conv.1 = (f32[4,1024,256]{2,1,0:T(8,128)}, f32[4,1024,256]{2,1,0:T(8,128)}, f32[4,1040,256]{2,1,0:T(8,128)}, f32[8,2,256]{2,1,0:T(2,128)}) custom-call(s32[2,4]{1,0:T(2,128)} %stack.35.meta, bf16[4,1024,1024]{2,1,0:T(8,128)(2,1)} %x.4, bf16[4,16,1024]{2,1,0:T(8,128)(2,1)} %get-tuple-element.104.halo, bf16[1024,256]{1,0:T(8,128)(2,1)} %wv.1, ...), custom_call_target="tpu_custom_call" | custom-call | flops 4294967296 | bytes 20971520 | tf_op jit(solution)/shard_map/gate_conv/pallas_call | solution.py:471
  29.4 1.1 pad_maximum_fusion
  31.6 0.6 pad_maximum_fusion.5.affine
  32.2 1.0 fusion.select
  33.2 5.7 %all-to-all-start = ((f32[8,2,256]{2,1,0:T(2,128)}), f32[8,2,256]{2,1,0:T(2,128)S(1)}, u32[]{:S(2)}, u32[]{:S(2)}) async-start(f32[8,2,256]{2,1,0:T(2,128)} %get-tuple-element.51), calls=%async_computation | async-start | bytes 32768 | tf_op jit(solution)/shard_map/all_to_all | solution.py:417
  38.9 0.8 pad_maximum_fusion.1
  39.7 5.7 %all-to-all-done.stats = f32[8,2,256]{2,1,0:T(2,128)S(1)} async-done(((f32[8,2,256]{2,1,0:T(2,128)}), f32[8,2,256]{2,1,0:T(2,128)S(1)}, u32[]{:S(2)}, u32[]{:S(2)}) %all-to-all-start) | async-done | bytes 16416 | tf_op jit(solution)/shard_map/all_to_all | solution.py:417
  45.5 0.6 copy-done.5
  46.1 12.1 %swish_norm.1 = (bf16[4,1024,256]{2,1,0:T(8,128)(2,1)}, f32[4,1040,256]{2,1,0:T(8,128)}, bf16[4,256,1024]{2,1,0:T(8,128)(2,1)}, f32[8,2,256]{2,1,0:T(2,128)}) custom-call(s32[2,4]{1,0:T(2,128)} %stack.35.meta, f32[1,1]{1,0:T(1,128)} %bitcast.1.count, f32[8,2,256]{2,1,0:T(2,128)} %copy-done.5, f32[2,256]{1,0:T(2,128)} %pad_maximum_fusion.5.affine, ...), custom_call_target="tpu_custom_call" | custom-call | flops 4294967296 | bytes 20971520 | tf_op jit(solution)/shard_map/swish_norm/pallas_call | solution.py:516
  58.2 3.3 %all-to-all-start.1 = ((f32[8,2,256]{2,1,0:T(2,128)}), f32[8,2,256]{2,1,0:T(2,128)S(1)}, u32[]{:S(2)}, u32[]{:S(2)}) async-start(f32[8,2,256]{2,1,0:T(2,128)} %get-tuple-element.55), calls=%async_computation.1 | async-start | bytes 32768 | tf_op jit(solution)/shard_map/all_to_all | solution.py:417
  61.5 6.7 %outer_w_out.1.refs_2_ = bf16[8,1,32,1024]{3,2,1,0:T(8,128)(2,1)} custom-call(bf16[4,1024,1024]{2,1,0:T(8,128)(2,1)} %grads.3, bf16[4,1024,256]{2,1,0:T(8,128)(2,1)} %get-tuple-element.59.swished), custom_call_target="tpu_custom_call" | custom-call | flops 2147483648 | bytes 8388608 | tf_op jit(solution)/shard_map/outer_w_out/pallas_call | solution.py:561
  68.3 0.6 copy-done.3
  68.9 5.0 %back_conv.3 = (bf16[1024,512]{1,0:T(8,128)(2,1)}, f32[16,256]{1,0:T(8,128)}) custom-call(s32[2,4]{1,0:T(2,128)} %stack.35.meta, f32[1,1]{1,0:T(1,128)} %bitcast.1.count, f32[8,2,256]{2,1,0:T(2,128)} %copy-done.5, f32[8,2,256]{2,1,0:T(2,128)} %copy-done.3, f32[1,256]{1,0:T(1,128)} %bitcast.26, f32[4,1040,256]{2,1,0:T(8,128)} %get-tuple-element.56.gn, ...), custom_call_target="tpu_custom_call" | custom-call | bytes 1024 | tf_op jit(solution)/shard_map/back_conv/pallas_call | solution.py:585
  74.0 5.0 %back_conv.4 = (bf16[1024,512]{1,0:T(8,128)(2,1)}, f32[16,256]{1,0:T(8,128)}) custom-call(s32[2,4]{1,0:T(2,128)} %stack.35.meta, f32[1,1]{1,0:T(1,128)} %bitcast.1.count, f32[8,2,256]{2,1,0:T(2,128)} %copy-done.5, f32[8,2,256]{2,1,0:T(2,128)} %copy-done.3, f32[1,256]{1,0:T(1,128)} %bitcast.27, f32[4,1040,256]{2,1,0:T(8,128)} %get-tuple-element.56.gn, ...), custom_call_target="tpu_custom_call" | custom-call | bytes 1024 | tf_op jit(solution)/shard_map/back_conv/pallas_call | solution.py:585
  79.5 4.3 %partial_in.3 = (bf16[8,1,32,1024]{3,2,1,0:T(8,128)(2,1)}, bf16[8,1,32,1024]{3,2,1,0:T(8,128)(2,1)}) custom-call(bf16[1024,512]{1,0:T(8,128)(2,1)} %get-tuple-element.61.own.refs_0_, bf16[1024,512]{1,0:T(8,128)(2,1)} %collective-permute-done.3.sibling, bf16[512,512]{1,0:T(8,128)(2,1)} %bitcast.21, bf16[512,512]{1,0:T(8,128)(2,1)} %copy-done.1, ...), custom_call_target="tpu_custom_call" | custom-call | bytes 1024 | tf_op jit(solution)/shard_map/partial_in/pallas_call | solution.py:614
  83.8 1.5 collective-permute-start.6
  85.3 8.8 %back_conv.5 = (bf16[2048,512]{1,0:T(8,128)(2,1)}, f32[16,256]{1,0:T(8,128)}) custom-call(s32[2,4]{1,0:T(2,128)} %stack.35.meta, f32[1,1]{1,0:T(1,128)} %bitcast.1.count, f32[8,2,256]{2,1,0:T(2,128)} %copy-done.5, f32[8,2,256]{2,1,0:T(2,128)} %copy-done.3, f32[1,256]{1,0:T(1,128)} %bitcast.28, f32[4,1040,256]{2,1,0:T(8,128)} %get-tuple-element.56.gn, ...), custom_call_target="tpu_custom_call" | custom-call | bytes 1024 | tf_op jit(solution)/shard_map/back_conv/pallas_call | solution.py:585
  94.2 4.3 %partial_in.4 = (bf16[8,1,32,1024]{3,2,1,0:T(8,128)(2,1)}, bf16[8,1,32,1024]{3,2,1,0:T(8,128)(2,1)}) custom-call(bf16[1024,512]{1,0:T(8,128)(2,1)} %get-tuple-element.63.own.refs_1_, bf16[1024,512]{1,0:T(8,128)(2,1)} %collective-permute-done.5.sibling, bf16[512,512]{1,0:T(8,128)(2,1)} %bitcast.22, bf16[512,512]{1,0:T(8,128)(2,1)} %copy-done.1, ...), custom_call_target="tpu_custom_call" | custom-call | bytes 1024 | tf_op jit(solution)/shard_map/partial_in/pallas_call | solution.py:614
  99.0 0.8 copy-done.8
  99.9 3.8 %add_join.1 = bf16[8,2,32,1024]{3,2,1,0:T(8,128)(2,1)} custom-call(bf16[8,1,32,1024]{3,2,1,0:T(8,128)(2,1)} %get-tuple-element.73.refs_0_, bf16[8,1,32,1024]{3,2,1,0:T(8,128)(2,1)} %copy-done.8, bf16[8,1,32,1024]{3,2,1,0:T(8,128)(2,1)} %outer_w_out.1.refs_2_), custom_call_target="tpu_custom_call" | custom-call | flops 49999998976 | bytes 1024 | tf_op jit(solution)/shard_map/add_join/pallas_call | solution.py:661
  103.7 5.9 %all-to-all-start.2 = ((bf16[8,2,32,1024]{3,2,1,0:T(8,128)(2,1)}), bf16[8,2,32,1024]{3,2,1,0:T(8,128)(2,1)}, u32[]{:S(2)}, u32[]{:S(2)}) async-start(bf16[8,2,32,1024]{3,2,1,0:T(8,128)(2,1)} %add_join.1), calls=%async_computation.2 | async-start | bytes 2097152 | tf_op jit(solution)/shard_map/all_to_all | solution.py:417
  109.6 6.5 %partial_in.5 = (bf16[8,2,32,1024]{3,2,1,0:T(8,128)(2,1)}, bf16[8,2,32,1024]{3,2,1,0:T(8,128)(2,1)}) custom-call(bf16[2048,512]{1,0:T(8,128)(2,1)} %get-tuple-element.69.own.refs_2_, bf16[2048,512]{1,0:T(8,128)(2,1)} %collective-permute-done.4.sibling, bf16[512,512]{1,0:T(8,128)(2,1)} %bitcast.23, bf16[512,512]{1,0:T(8,128)(2,1)} %copy-done.1, ...), custom_call_target="tpu_custom_call" | custom-call | bytes 1024 | tf_op jit(solution)/shard_map/partial_in/pallas_call | solution.py:614
  116.1 1.5 collective-permute-start.9
  117.6 9.5 %outer_w_in.1 = (bf16[4,544,128]{2,1,0:T(8,128)(2,1)}, bf16[4,544,128]{2,1,0:T(8,128)(2,1)}) custom-call(s32[1,1]{1,0:T(1,128)} %bitcast.11.parity, bf16[4,1024,1024]{2,1,0:T(8,128)(2,1)} %x.4, bf16[1024,512]{1,0:T(8,128)(2,1)} %get-tuple-element.61.own.refs_0_, bf16[1024,512]{1,0:T(8,128)(2,1)} %get-tuple-element.63.own.refs_1_, ...), custom_call_target="tpu_custom_call" | custom-call | flops 49999998976 | bytes 1024 | tf_op jit(solution)/shard_map/outer_w_in/pallas_call | solution.py:690
  127.2 2.0 %collective-permute-start.7 = (bf16[4,544,128]{2,1,0:T(8,128)(2,1)}, bf16[4,544,128]{2,1,0:T(8,128)(2,1)}, u32[]{:S(2)}, u32[]{:S(2)}) collective-permute-start(bf16[4,544,128]{2,1,0:T(8,128)(2,1)} %get-tuple-element.81), channel_id=1, source_target_pairs={{0,4},{4,0},{8,12},{12,8},{16,20},{20,16},{24,28},{28,24},{1,5},{5... | collective-permute-start | bytes 1671176 | tf_op jit(solution)/shard_map/ppermute | solution.py:713
  129.2 2.0 %add.114 = bf16[8,1,32,1024]{3,2,1,0:T(8,128)(2,1)} custom-call(bf16[8,1,32,1024]{3,2,1,0:T(8,128)(2,1)} %get-tuple-element.83.refs_0_, bf16[8,1,32,1024]{3,2,1,0:T(8,128)(2,1)} %collective-permute-done.8.refs_1_), custom_call_target="tpu_custom_call" | custom-call | flops 49999998976 | bytes 1024 | tf_op jit(solution)/shard_map/add/pallas_call | solution.py:649
  131.1 4.7 %all-to-all-done.2.moved.pieces = bf16[8,2,32,1024]{3,2,1,0:T(8,128)(2,1)} async-done(((bf16[8,2,32,1024]{3,2,1,0:T(8,128)(2,1)}), bf16[8,2,32,1024]{3,2,1,0:T(8,128)(2,1)}, u32[]{:S(2)}, u32[]{:S(2)}) %all-to-all-start.2) | async-done | bytes 1048608 | tf_op jit(solution)/shard_map/all_to_all | solution.py:417
  135.8 3.7 %all-to-all-start.3 = ((bf16[8,1,32,1024]{3,2,1,0:T(8,128)(2,1)}), bf16[8,1,32,1024]{3,2,1,0:T(8,128)(2,1)S(1)}, u32[]{:S(2)}, u32[]{:S(2)}) async-start(bf16[8,1,32,1024]{3,2,1,0:T(8,128)(2,1)} %add.114), calls=%async_computation.3 | async-start | bytes 1048576 | tf_op jit(solution)/shard_map/all_to_all | solution.py:417
  139.5 7.0 %collective-permute-done.7.other = bf16[4,544,128]{2,1,0:T(8,128)(2,1)} collective-permute-done((bf16[4,544,128]{2,1,0:T(8,128)(2,1)}, bf16[4,544,128]{2,1,0:T(8,128)(2,1)}, u32[]{:S(2)}, u32[]{:S(2)}) %collective-permute-start.7) | collective-permute-done | bytes 557088 | tf_op jit(solution)/shard_map/ppermute | solution.py:713
  146.5 3.7 %add.115 = bf16[8,2,32,1024]{3,2,1,0:T(8,128)(2,1)} custom-call(bf16[8,2,32,1024]{3,2,1,0:T(8,128)(2,1)} %get-tuple-element.84.refs_0_, bf16[8,2,32,1024]{3,2,1,0:T(8,128)(2,1)} %collective-permute-done.9.refs_1_), custom_call_target="tpu_custom_call" | custom-call | flops 49999998976 | bytes 1024 | tf_op jit(solution)/shard_map/add/pallas_call | solution.py:649
  150.2 1.1 copy-done
  151.3 1.2 fold.2
  152.6 1.7 all-to-all-done.3.moved
  154.3 4.1 %all-to-all-start.4 = ((bf16[8,2,32,1024]{3,2,1,0:T(8,128)(2,1)}), bf16[8,2,32,1024]{3,2,1,0:T(8,128)(2,1)S(1)}, u32[]{:S(2)}, u32[]{:S(2)}) async-start(bf16[8,2,32,1024]{3,2,1,0:T(8,128)(2,1)} %add.115), calls=%async_computation.4 | async-start | bytes 2097152 | tf_op jit(solution)/shard_map/all_to_all | solution.py:417
  158.4 0.7 collective-permute-done.10.other
  159.2 3.6 %collective-permute-start.11 = (bf16[1,544,128]{2,1,0:T(8,128)(2,1)S(1)}, bf16[1,544,128]{2,1,0:T(8,128)(2,1)S(1)}, u32[]{:S(2)}, u32[]{:S(2)}) collective-permute-start(bf16[1,544,128]{2,1,0:T(8,128)(2,1)S(1)} %get-tuple-element.91), channel_id=1, source_target_pairs={{0,16},{4,20},{8,24},{12,28},{16,0},{20,4},{24,8},{28,12},{1,17},{... | collective-permute-start | bytes 417800 | tf_op jit(solution)/shard_map/ppermute | solution.py:713
  163.3 1.9 place.3.refs_0_
  165.2 1.8 finish_w_out.1
  167.0 0.8 place.4.refs_0_
  167.8 22.2 %collective-permute-done.11.other = bf16[1,544,128]{2,1,0:T(8,128)(2,1)S(1)} collective-permute-done((bf16[1,544,128]{2,1,0:T(8,128)(2,1)S(1)}, bf16[1,544,128]{2,1,0:T(8,128)(2,1)S(1)}, u32[]{:S(2)}, u32[]{:S(2)}) %collective-permute-start.11) | collective-permute-done | bytes 139296 | tf_op jit(solution)/shard_map/ppermute | solution.py:713
  190.0 0.8 finish.1
  190.9 1.1 place.5
  (43 shorter events, 2.9 us)
Async XLA Ops:
  1.6 8.1 %collective-permute-start = (bf16[4,8,2048]{2,1,0:T(8,128)(2,1)S(1)}, bf16[4,8,2048]{2,1,0:T(8,128)(2,1)S(1)}, u32[]{:S(2)}, u32[]{:S(2)}) collective-permute-start(bf16[4,8,2048]{2,1,0:T(8,128)(2,1)S(1)} %pad_maximum_fusion.3), channel_id=1, source_target_pairs={{0,4},{4,8},{8,12},{12,16},{16,20},{20,24},{24,28},{1,5},{5,9},{9,... | collective-permute-start | bytes 393224 | tf_op jit(solution)/shard_map/ppermute | solution.py:457
  6.5 6.9 %collective-permute-start.1 = (bf16[4,8,2048]{2,1,0:T(8,128)(2,1)S(1)}, bf16[4,8,2048]{2,1,0:T(8,128)(2,1)S(1)}, u32[]{:S(2)}, u32[]{:S(2)}) collective-permute-start(bf16[4,8,2048]{2,1,0:T(8,128)(2,1)S(1)} %pad_maximum_fusion.4), channel_id=1, source_target_pairs={{4,0},{8,4},{12,8},{16,12},{20,16},{24,20},{28,24},{5,1},{9,5},{13... | collective-permute-start | bytes 393224 | tf_op jit(solution)/shard_map/ppermute | solution.py:457
  14.1 15.3 %copy-start.2 = (bf16[1024,256]{1,0:T(8,128)(2,1)S(1)}, bf16[1024,256]{1,0:T(8,128)(2,1)}, u32[]{:S(2)}) copy-start(bf16[1024,256]{1,0:T(8,128)(2,1)} %wv.1) | copy-start | bytes 1572868
  30.6 1.1 copy-start.6
  30.6 1.1 copy-start.7
  30.7 9.0 %collective-permute-start.2 = (bf16[512,512]{1,0:T(8,128)(2,1)S(1)}, bf16[512,512]{1,0:T(8,128)(2,1)S(1)}, u32[]{:S(2)}, u32[]{:S(2)}) collective-permute-start(bf16[512,512]{1,0:T(8,128)(2,1)S(1)} %bitcast.25), channel_id=1, source_target_pairs={{0,1},{1,0},{2,3},{3,2},{4,5},{5,4},{6,7},{7,6},{8,9},{9,8},{10,11... | collective-permute-start | bytes 1572872 | tf_op jit(solution)/shard_map/ppermute | solution.py:510
  33.2 12.3 %all-to-all-start = ((f32[8,2,256]{2,1,0:T(2,128)}), f32[8,2,256]{2,1,0:T(2,128)S(1)}, u32[]{:S(2)}, u32[]{:S(2)}) async-start(f32[8,2,256]{2,1,0:T(2,128)} %get-tuple-element.51), calls=%async_computation | async-start | bytes 32768 | tf_op jit(solution)/shard_map/all_to_all | solution.py:417
  39.7 18.4 %copy-start.1 = (bf16[512,512]{1,0:T(8,128)(2,1)}, bf16[512,512]{1,0:T(8,128)(2,1)S(1)}, u32[]{:S(2)}) copy-start(bf16[512,512]{1,0:T(8,128)(2,1)S(1)} %collective-permute-done.2.w_sibling) | copy-start | bytes 1572868
  45.5 0.6 copy-start.5
  58.2 10.1 %all-to-all-start.1 = ((f32[8,2,256]{2,1,0:T(2,128)}), f32[8,2,256]{2,1,0:T(2,128)S(1)}, u32[]{:S(2)}, u32[]{:S(2)}) async-start(f32[8,2,256]{2,1,0:T(2,128)} %get-tuple-element.55), calls=%async_computation.1 | async-start | bytes 32768 | tf_op jit(solution)/shard_map/all_to_all | solution.py:417
  68.3 0.6 copy-start.3
  73.9 5.6 %collective-permute-start.3 = (bf16[1024,512]{1,0:T(8,128)(2,1)}, bf16[1024,512]{1,0:T(8,128)(2,1)}, u32[]{:S(2)}, u32[]{:S(2)}) collective-permute-start(bf16[1024,512]{1,0:T(8,128)(2,1)} %get-tuple-element.61.own.refs_0_), channel_id=1, source_target_pairs={{0,1},{1,0},{2,3},{3,2},{4,5},{5,4},{6,7},{7,6},{8,9},{9,8},{10,11... | collective-permute-start | bytes 3145736 | tf_op jit(solution)/shard_map/ppermute | solution.py:612
  79.0 15.2 %collective-permute-start.5 = (bf16[1024,512]{1,0:T(8,128)(2,1)}, bf16[1024,512]{1,0:T(8,128)(2,1)}, u32[]{:S(2)}, u32[]{:S(2)}) collective-permute-start(bf16[1024,512]{1,0:T(8,128)(2,1)} %get-tuple-element.63.own.refs_1_), channel_id=1, source_target_pairs={{0,1},{1,0},{2,3},{3,2},{4,5},{5,4},{6,7},{7,6},{8,9},{9,8},{10,11... | collective-permute-start | bytes 3145736 | tf_op jit(solution)/shard_map/ppermute | solution.py:612
  83.8 15.3 %collective-permute-start.6 = (bf16[8,1,32,1024]{3,2,1,0:T(8,128)(2,1)}, bf16[8,1,32,1024]{3,2,1,0:T(8,128)(2,1)S(1)}, u32[]{:S(2)}, u32[]{:S(2)}) collective-permute-start(bf16[8,1,32,1024]{3,2,1,0:T(8,128)(2,1)} %get-tuple-element.67), channel_id=1, source_target_pairs={{0,2},{1,3},{2,0},{3,1},{4,6},{5,7},{6,4},{7,5},{8,10},{9,11},{10,... | collective-permute-start | bytes 1572872 | tf_op jit(solution)/shard_map/ppermute | solution.py:643
  94.1 15.5 %collective-permute-start.4 = (bf16[2048,512]{1,0:T(8,128)(2,1)}, bf16[2048,512]{1,0:T(8,128)(2,1)}, u32[]{:S(2)}, u32[]{:S(2)}) collective-permute-start(bf16[2048,512]{1,0:T(8,128)(2,1)} %get-tuple-element.69.own.refs_2_), channel_id=1, source_target_pairs={{0,1},{1,0},{2,3},{3,2},{4,5},{5,4},{6,7},{7,6},{8,9},{9,8},{10,11... | collective-permute-start | bytes 6291464 | tf_op jit(solution)/shard_map/ppermute | solution.py:612
  98.5 30.7 %collective-permute-start.8 = (bf16[8,1,32,1024]{3,2,1,0:T(8,128)(2,1)}, bf16[8,1,32,1024]{3,2,1,0:T(8,128)(2,1)}, u32[]{:S(2)}, u32[]{:S(2)}) collective-permute-start(bf16[8,1,32,1024]{3,2,1,0:T(8,128)(2,1)} %get-tuple-element.72), channel_id=1, source_target_pairs={{0,2},{1,3},{2,0},{3,1},{4,6},{5,7},{6,4},{7,5},{8,10},{9,11},{10,... | collective-permute-start | bytes 1572872 | tf_op jit(solution)/shard_map/ppermute | solution.py:643
  99.0 0.8 copy-start.8
  103.7 32.2 %all-to-all-start.2 = ((bf16[8,2,32,1024]{3,2,1,0:T(8,128)(2,1)}), bf16[8,2,32,1024]{3,2,1,0:T(8,128)(2,1)}, u32[]{:S(2)}, u32[]{:S(2)}) async-start(bf16[8,2,32,1024]{3,2,1,0:T(8,128)(2,1)} %add_join.1), calls=%async_computation.2 | async-start | bytes 2097152 | tf_op jit(solution)/shard_map/all_to_all | solution.py:417
  116.1 30.4 %collective-permute-start.9 = (bf16[8,2,32,1024]{3,2,1,0:T(8,128)(2,1)}, bf16[8,2,32,1024]{3,2,1,0:T(8,128)(2,1)}, u32[]{:S(2)}, u32[]{:S(2)}) collective-permute-start(bf16[8,2,32,1024]{3,2,1,0:T(8,128)(2,1)} %get-tuple-element.76), channel_id=1, source_target_pairs={{0,2},{1,3},{2,0},{3,1},{4,6},{5,7},{6,4},{7,5},{8,10},{9,11},{10,... | collective-permute-start | bytes 3145736 | tf_op jit(solution)/shard_map/ppermute | solution.py:643
  127.2 19.4 %collective-permute-start.7 = (bf16[4,544,128]{2,1,0:T(8,128)(2,1)}, bf16[4,544,128]{2,1,0:T(8,128)(2,1)}, u32[]{:S(2)}, u32[]{:S(2)}) collective-permute-start(bf16[4,544,128]{2,1,0:T(8,128)(2,1)} %get-tuple-element.81), channel_id=1, source_target_pairs={{0,4},{4,0},{8,12},{12,8},{16,20},{20,16},{24,28},{28,24},{1,5},{5... | collective-permute-start | bytes 1671176 | tf_op jit(solution)/shard_map/ppermute | solution.py:713
  135.8 18.5 %all-to-all-start.3 = ((bf16[8,1,32,1024]{3,2,1,0:T(8,128)(2,1)}), bf16[8,1,32,1024]{3,2,1,0:T(8,128)(2,1)S(1)}, u32[]{:S(2)}, u32[]{:S(2)}) async-start(bf16[8,1,32,1024]{3,2,1,0:T(8,128)(2,1)} %add.114), calls=%async_computation.3 | async-start | bytes 1048576 | tf_op jit(solution)/shard_map/all_to_all | solution.py:417
  139.5 13.1 %copy-start.4 = (f32[8,2,256]{2,1,0:T(2,128)S(1)}, f32[8,2,256]{2,1,0:T(2,128)}, u32[]{:S(2)}) copy-start(f32[8,2,256]{2,1,0:T(2,128)} %copy-done.3) | copy-start | bytes 49156
  150.2 1.1 copy-start
  152.5 6.6 %collective-permute-start.10 = (bf16[2,544,128]{2,1,0:T(8,128)(2,1)S(1)}, bf16[2,544,128]{2,1,0:T(8,128)(2,1)S(1)}, u32[]{:S(2)}, u32[]{:S(2)}) collective-permute-start(bf16[2,544,128]{2,1,0:T(8,128)(2,1)S(1)} %get-tuple-element.89), channel_id=1, source_target_pairs={{0,8},{4,12},{8,0},{12,4},{16,24},{20,28},{24,16},{28,20},{1,9},{5... | collective-permute-start | bytes 835592 | tf_op jit(solution)/shard_map/ppermute | solution.py:713
  154.3 36.5 %all-to-all-start.4 = ((bf16[8,2,32,1024]{3,2,1,0:T(8,128)(2,1)}), bf16[8,2,32,1024]{3,2,1,0:T(8,128)(2,1)S(1)}, u32[]{:S(2)}, u32[]{:S(2)}) async-start(bf16[8,2,32,1024]{3,2,1,0:T(8,128)(2,1)} %add.115), calls=%async_computation.4 | async-start | bytes 2097152 | tf_op jit(solution)/shard_map/all_to_all | solution.py:417
  159.2 30.9 %collective-permute-start.11 = (bf16[1,544,128]{2,1,0:T(8,128)(2,1)S(1)}, bf16[1,544,128]{2,1,0:T(8,128)(2,1)S(1)}, u32[]{:S(2)}, u32[]{:S(2)}) collective-permute-start(bf16[1,544,128]{2,1,0:T(8,128)(2,1)S(1)} %get-tuple-element.91), channel_id=1, source_target_pairs={{0,16},{4,20},{8,24},{12,28},{16,0},{20,4},{24,8},{28,12},{1,17},{... | collective-permute-start | bytes 417800 | tf_op jit(solution)/shard_map/ppermute | solution.py:713

commit v23 on v22

--- a/solution.py
+++ b/solution.py
@@ -108,7 +108,7 @@
     put(2 * EDGE + frames, edge[EDGE:])
     put(3 * EDGE + frames, zero)
     step = block_rows(frames, 512)
-    small = block_rows(step, 64)
+    small = block_rows(step, 32)
     for base in range(0, frames, step):
         xb = x[0, base : base + step, :]
         vl_o[0, base : base + step, :] = dot(xb, wv[...])
@@ -187,7 +187,7 @@
     part(0, edge[:EDGE])
     part(frames + EDGE, edge[EDGE:])
     step = block_rows(frames, 512)
-    small = block_rows(step, 32)
+    small = block_rows(step, 16)
     s1 = jnp.zeros((8, conv.shape[2]), F32)
     s2 = s1
     held = (ping, pong)

time: 193 us -> 194 us (level)
  no operation moved by 1% of the time
where the time goes in v23:
time: 194 us; the launch traced here: 193 us
  Pallas kernels  95.8 us (49%)
  waiting for transfers between devices  45.2 us (23%)
  starting transfers between devices  39.4 us (20%)
  local copies, waits for them, and re-layouts  6.11 us (3%)
  other arithmetic  4.95 us (3%)
    ppermute x3, waiting for transfers between devices, per_device(): others = lax.ppermute(send, 'seq', [(i, i ^ bit) for i in range(seqs)])  29.3 us
    all_to_all x5, starting transfers between devices, exchange(): return lax.all_to_all(copies, axis, 0, 0, tiled=True)  22.8 us
    pallas_call x3, Pallas kernels, back(): call(functools.partial(back_kernel, first, blocks), 'back_conv', (size *...  18.9 us
    pallas_call x1, Pallas kernels, per_device(): call(gate_kernel, 'gate_conv', (recs,), [smem(), per_record((frames, mode...  16.2 us
    pallas_call x3, Pallas kernels, partials(): call(partial_kernel, 'partial_in', (size * parts_in,), [pl.BlockSpec((hal...  15.1 us
    all_to_all x5, waiting for transfers between devices, exchange(): return lax.all_to_all(copies, axis, 0, 0, tiled=True)  12.2 us
    pallas_call x1, Pallas kernels, per_device(): call(norm_kernel, 'swish_norm', (recs,), [smem(), smem(), whole((seqs, 2,...  12.1 us
    pallas_call x1, Pallas kernels, per_device(): call(functools.partial(outer_kernel, groups), 'outer_w_in', (recs,), [sme...  9.53 us
  transfers between devices with their start and end apart: 17, of which 7 were waited for; matrix products, arithmetic and copies ran while one was open for 3% of the time, Pallas kernels for 32%

profile of v23, /device:TPU:0, one launch (start us, length us, event | category | flops | bytes accessed | tf_op | source)
XLA Modules:
  0.0 193.0 jit_solution(13383170686200639857)
XLA Ops:
  0.6 1.0 fusion.1
  1.6 4.9 %collective-permute-start = (bf16[4,8,2048]{2,1,0:T(8,128)(2,1)S(1)}, bf16[4,8,2048]{2,1,0:T(8,128)(2,1)S(1)}, u32[]{:S(2)}, u32[]{:S(2)}) collective-permute-start(bf16[4,8,2048]{2,1,0:T(8,128)(2,1)S(1)} %pad_maximum_fusion.3), channel_id=1, source_target_pairs={{0,4},{4,8},{8,12},{12,16},{16,20},{20,24},{24,28},{1,5},{5,9},{9,... | collective-permute-start | bytes 393224 | tf_op jit(solution)/shard_map/ppermute | solution.py:457
  6.5 1.3 collective-permute-start.1
  7.8 1.3 fusion.5
  9.7 3.7 %collective-permute-done.1 = bf16[4,8,2048]{2,1,0:T(8,128)(2,1)S(1)} collective-permute-done((bf16[4,8,2048]{2,1,0:T(8,128)(2,1)S(1)}, bf16[4,8,2048]{2,1,0:T(8,128)(2,1)S(1)}, u32[]{:S(2)}, u32[]{:S(2)}) %collective-permute-start.1) | collective-permute-done | bytes 131104 | tf_op jit(solution)/shard_map/ppermute | solution.py:457
  13.4 0.7 fusion.3
  14.1 16.2 %gate_conv.1 = (f32[4,1024,256]{2,1,0:T(8,128)}, f32[4,1024,256]{2,1,0:T(8,128)}, f32[4,1040,256]{2,1,0:T(8,128)}, f32[8,2,256]{2,1,0:T(2,128)}) custom-call(s32[2,4]{1,0:T(2,128)} %stack.35.meta, bf16[4,1024,1024]{2,1,0:T(8,128)(2,1)} %x.4, bf16[4,16,1024]{2,1,0:T(8,128)(2,1)} %get-tuple-element.104.halo, bf16[1024,256]{1,0:T(8,128)(2,1)} %wv.1, ...), custom_call_target="tpu_custom_call" | custom-call | flops 4294967296 | bytes 20971520 | tf_op jit(solution)/shard_map/gate_conv/pallas_call | solution.py:471
  30.4 1.1 pad_maximum_fusion
  32.6 0.6 pad_maximum_fusion.5.affine
  33.2 1.0 fusion.select
  34.1 5.7 %all-to-all-start = ((f32[8,2,256]{2,1,0:T(2,128)}), f32[8,2,256]{2,1,0:T(2,128)S(1)}, u32[]{:S(2)}, u32[]{:S(2)}) async-start(f32[8,2,256]{2,1,0:T(2,128)} %get-tuple-element.51), calls=%async_computation | async-start | bytes 32768 | tf_op jit(solution)/shard_map/all_to_all | solution.py:417
  39.8 0.8 pad_maximum_fusion.1
  40.7 5.7 %all-to-all-done.stats = f32[8,2,256]{2,1,0:T(2,128)S(1)} async-done(((f32[8,2,256]{2,1,0:T(2,128)}), f32[8,2,256]{2,1,0:T(2,128)S(1)}, u32[]{:S(2)}, u32[]{:S(2)}) %all-to-all-start) | async-done | bytes 16416 | tf_op jit(solution)/shard_map/all_to_all | solution.py:417
  46.4 0.6 copy-done.5
  47.0 12.1 %swish_norm.1 = (bf16[4,1024,256]{2,1,0:T(8,128)(2,1)}, f32[4,1040,256]{2,1,0:T(8,128)}, bf16[4,256,1024]{2,1,0:T(8,128)(2,1)}, f32[8,2,256]{2,1,0:T(2,128)}) custom-call(s32[2,4]{1,0:T(2,128)} %stack.35.meta, f32[1,1]{1,0:T(1,128)} %bitcast.1.count, f32[8,2,256]{2,1,0:T(2,128)} %copy-done.5, f32[2,256]{1,0:T(2,128)} %pad_maximum_fusion.5.affine, ...), custom_call_target="tpu_custom_call" | custom-call | flops 4294967296 | bytes 20971520 | tf_op jit(solution)/shard_map/swish_norm/pallas_call | solution.py:516
  59.2 3.3 %all-to-all-start.1 = ((f32[8,2,256]{2,1,0:T(2,128)}), f32[8,2,256]{2,1,0:T(2,128)S(1)}, u32[]{:S(2)}, u32[]{:S(2)}) async-start(f32[8,2,256]{2,1,0:T(2,128)} %get-tuple-element.55), calls=%async_computation.1 | async-start | bytes 32768 | tf_op jit(solution)/shard_map/all_to_all | solution.py:417
  62.5 6.7 %outer_w_out.1.refs_2_ = bf16[8,1,32,1024]{3,2,1,0:T(8,128)(2,1)} custom-call(bf16[4,1024,1024]{2,1,0:T(8,128)(2,1)} %grads.3, bf16[4,1024,256]{2,1,0:T(8,128)(2,1)} %get-tuple-element.59.swished), custom_call_target="tpu_custom_call" | custom-call | flops 2147483648 | bytes 8388608 | tf_op jit(solution)/shard_map/outer_w_out/pallas_call | solution.py:561
  69.3 0.6 copy-done.3
  69.9 5.0 %back_conv.3 = (bf16[1024,512]{1,0:T(8,128)(2,1)}, f32[16,256]{1,0:T(8,128)}) custom-call(s32[2,4]{1,0:T(2,128)} %stack.35.meta, f32[1,1]{1,0:T(1,128)} %bitcast.1.count, f32[8,2,256]{2,1,0:T(2,128)} %copy-done.5, f32[8,2,256]{2,1,0:T(2,128)} %copy-done.3, f32[1,256]{1,0:T(1,128)} %bitcast.26, f32[4,1040,256]{2,1,0:T(8,128)} %get-tuple-element.56.gn, ...), custom_call_target="tpu_custom_call" | custom-call | bytes 1024 | tf_op jit(solution)/shard_map/back_conv/pallas_call | solution.py:585
  74.9 5.0 %back_conv.4 = (bf16[1024,512]{1,0:T(8,128)(2,1)}, f32[16,256]{1,0:T(8,128)}) custom-call(s32[2,4]{1,0:T(2,128)} %stack.35.meta, f32[1,1]{1,0:T(1,128)} %bitcast.1.count, f32[8,2,256]{2,1,0:T(2,128)} %copy-done.5, f32[8,2,256]{2,1,0:T(2,128)} %copy-done.3, f32[1,256]{1,0:T(1,128)} %bitcast.27, f32[4,1040,256]{2,1,0:T(8,128)} %get-tuple-element.56.gn, ...), custom_call_target="tpu_custom_call" | custom-call | bytes 1024 | tf_op jit(solution)/shard_map/back_conv/pallas_call | solution.py:585
  80.5 4.3 %partial_in.3 = (bf16[8,1,32,1024]{3,2,1,0:T(8,128)(2,1)}, bf16[8,1,32,1024]{3,2,1,0:T(8,128)(2,1)}) custom-call(bf16[1024,512]{1,0:T(8,128)(2,1)} %get-tuple-element.61.own.refs_0_, bf16[1024,512]{1,0:T(8,128)(2,1)} %collective-permute-done.3.sibling, bf16[512,512]{1,0:T(8,128)(2,1)} %bitcast.21, bf16[512,512]{1,0:T(8,128)(2,1)} %copy-done.1, ...), custom_call_target="tpu_custom_call" | custom-call | bytes 1024 | tf_op jit(solution)/shard_map/partial_in/pallas_call | solution.py:614
  84.8 1.5 collective-permute-start.6
  86.3 8.8 %back_conv.5 = (bf16[2048,512]{1,0:T(8,128)(2,1)}, f32[16,256]{1,0:T(8,128)}) custom-call(s32[2,4]{1,0:T(2,128)} %stack.35.meta, f32[1,1]{1,0:T(1,128)} %bitcast.1.count, f32[8,2,256]{2,1,0:T(2,128)} %copy-done.5, f32[8,2,256]{2,1,0:T(2,128)} %copy-done.3, f32[1,256]{1,0:T(1,128)} %bitcast.28, f32[4,1040,256]{2,1,0:T(8,128)} %get-tuple-element.56.gn, ...), custom_call_target="tpu_custom_call" | custom-call | bytes 1024 | tf_op jit(solution)/shard_map/back_conv/pallas_call | solution.py:585
  95.2 4.3 %partial_in.4 = (bf16[8,1,32,1024]{3,2,1,0:T(8,128)(2,1)}, bf16[8,1,32,1024]{3,2,1,0:T(8,128)(2,1)}) custom-call(bf16[1024,512]{1,0:T(8,128)(2,1)} %get-tuple-element.63.own.refs_1_, bf16[1024,512]{1,0:T(8,128)(2,1)} %collective-permute-done.5.sibling, bf16[512,512]{1,0:T(8,128)(2,1)} %bitcast.22, bf16[512,512]{1,0:T(8,128)(2,1)} %copy-done.1, ...), custom_call_target="tpu_custom_call" | custom-call | bytes 1024 | tf_op jit(solution)/shard_map/partial_in/pallas_call | solution.py:614
  100.0 0.8 copy-done.8
  100.9 3.8 %add_join.1 = bf16[8,2,32,1024]{3,2,1,0:T(8,128)(2,1)} custom-call(bf16[8,1,32,1024]{3,2,1,0:T(8,128)(2,1)} %get-tuple-element.73.refs_0_, bf16[8,1,32,1024]{3,2,1,0:T(8,128)(2,1)} %copy-done.8, bf16[8,1,32,1024]{3,2,1,0:T(8,128)(2,1)} %outer_w_out.1.refs_2_), custom_call_target="tpu_custom_call" | custom-call | flops 49999998976 | bytes 1024 | tf_op jit(solution)/shard_map/add_join/pallas_call | solution.py:661
  104.7 5.9 %all-to-all-start.2 = ((bf16[8,2,32,1024]{3,2,1,0:T(8,128)(2,1)}), bf16[8,2,32,1024]{3,2,1,0:T(8,128)(2,1)}, u32[]{:S(2)}, u32[]{:S(2)}) async-start(bf16[8,2,32,1024]{3,2,1,0:T(8,128)(2,1)} %add_join.1), calls=%async_computation.2 | async-start | bytes 2097152 | tf_op jit(solution)/shard_map/all_to_all | solution.py:417
  110.6 6.5 %partial_in.5 = (bf16[8,2,32,1024]{3,2,1,0:T(8,128)(2,1)}, bf16[8,2,32,1024]{3,2,1,0:T(8,128)(2,1)}) custom-call(bf16[2048,512]{1,0:T(8,128)(2,1)} %get-tuple-element.69.own.refs_2_, bf16[2048,512]{1,0:T(8,128)(2,1)} %collective-permute-done.4.sibling, bf16[512,512]{1,0:T(8,128)(2,1)} %bitcast.23, bf16[512,512]{1,0:T(8,128)(2,1)} %copy-done.1, ...), custom_call_target="tpu_custom_call" | custom-call | bytes 1024 | tf_op jit(solution)/shard_map/partial_in/pallas_call | solution.py:614
  117.1 1.5 collective-permute-start.9
  118.6 9.5 %outer_w_in.1 = (bf16[4,544,128]{2,1,0:T(8,128)(2,1)}, bf16[4,544,128]{2,1,0:T(8,128)(2,1)}) custom-call(s32[1,1]{1,0:T(1,128)} %bitcast.11.parity, bf16[4,1024,1024]{2,1,0:T(8,128)(2,1)} %x.4, bf16[1024,512]{1,0:T(8,128)(2,1)} %get-tuple-element.61.own.refs_0_, bf16[1024,512]{1,0:T(8,128)(2,1)} %get-tuple-element.63.own.refs_1_, ...), custom_call_target="tpu_custom_call" | custom-call | flops 49999998976 | bytes 1024 | tf_op jit(solution)/shard_map/outer_w_in/pallas_call | solution.py:690
  128.2 2.0 %collective-permute-start.7 = (bf16[4,544,128]{2,1,0:T(8,128)(2,1)}, bf16[4,544,128]{2,1,0:T(8,128)(2,1)}, u32[]{:S(2)}, u32[]{:S(2)}) collective-permute-start(bf16[4,544,128]{2,1,0:T(8,128)(2,1)} %get-tuple-element.81), channel_id=1, source_target_pairs={{0,4},{4,0},{8,12},{12,8},{16,20},{20,16},{24,28},{28,24},{1,5},{5... | collective-permute-start | bytes 1671176 | tf_op jit(solution)/shard_map/ppermute | solution.py:713
  130.2 2.0 %add.114 = bf16[8,1,32,1024]{3,2,1,0:T(8,128)(2,1)} custom-call(bf16[8,1,32,1024]{3,2,1,0:T(8,128)(2,1)} %get-tuple-element.83.refs_0_, bf16[8,1,32,1024]{3,2,1,0:T(8,128)(2,1)} %collective-permute-done.8.refs_1_), custom_call_target="tpu_custom_call" | custom-call | flops 49999998976 | bytes 1024 | tf_op jit(solution)/shard_map/add/pallas_call | solution.py:649
  132.1 4.7 %all-to-all-done.2.moved.pieces = bf16[8,2,32,1024]{3,2,1,0:T(8,128)(2,1)} async-done(((bf16[8,2,32,1024]{3,2,1,0:T(8,128)(2,1)}), bf16[8,2,32,1024]{3,2,1,0:T(8,128)(2,1)}, u32[]{:S(2)}, u32[]{:S(2)}) %all-to-all-start.2) | async-done | bytes 1048608 | tf_op jit(solution)/shard_map/all_to_all | solution.py:417
  136.9 3.7 %all-to-all-start.3 = ((bf16[8,1,32,1024]{3,2,1,0:T(8,128)(2,1)}), bf16[8,1,32,1024]{3,2,1,0:T(8,128)(2,1)S(1)}, u32[]{:S(2)}, u32[]{:S(2)}) async-start(bf16[8,1,32,1024]{3,2,1,0:T(8,128)(2,1)} %add.114), calls=%async_computation.3 | async-start | bytes 1048576 | tf_op jit(solution)/shard_map/all_to_all | solution.py:417
  140.5 7.0 %collective-permute-done.7.other = bf16[4,544,128]{2,1,0:T(8,128)(2,1)} collective-permute-done((bf16[4,544,128]{2,1,0:T(8,128)(2,1)}, bf16[4,544,128]{2,1,0:T(8,128)(2,1)}, u32[]{:S(2)}, u32[]{:S(2)}) %collective-permute-start.7) | collective-permute-done | bytes 557088 | tf_op jit(solution)/shard_map/ppermute | solution.py:713
  147.5 3.7 %add.115 = bf16[8,2,32,1024]{3,2,1,0:T(8,128)(2,1)} custom-call(bf16[8,2,32,1024]{3,2,1,0:T(8,128)(2,1)} %get-tuple-element.84.refs_0_, bf16[8,2,32,1024]{3,2,1,0:T(8,128)(2,1)} %collective-permute-done.9.refs_1_), custom_call_target="tpu_custom_call" | custom-call | flops 49999998976 | bytes 1024 | tf_op jit(solution)/shard_map/add/pallas_call | solution.py:649
  151.2 1.1 copy-done
  152.3 1.2 fold.2
  153.6 1.7 all-to-all-done.3.moved
  155.3 4.1 %all-to-all-start.4 = ((bf16[8,2,32,1024]{3,2,1,0:T(8,128)(2,1)}), bf16[8,2,32,1024]{3,2,1,0:T(8,128)(2,1)S(1)}, u32[]{:S(2)}, u32[]{:S(2)}) async-start(bf16[8,2,32,1024]{3,2,1,0:T(8,128)(2,1)} %add.115), calls=%async_computation.4 | async-start | bytes 2097152 | tf_op jit(solution)/shard_map/all_to_all | solution.py:417
  159.4 0.6 collective-permute-done.10.other
  160.1 4.1 %collective-permute-start.11 = (bf16[1,544,128]{2,1,0:T(8,128)(2,1)S(1)}, bf16[1,544,128]{2,1,0:T(8,128)(2,1)S(1)}, u32[]{:S(2)}, u32[]{:S(2)}) collective-permute-start(bf16[1,544,128]{2,1,0:T(8,128)(2,1)S(1)} %get-tuple-element.91), channel_id=1, source_target_pairs={{0,16},{4,20},{8,24},{12,28},{16,0},{20,4},{24,8},{28,12},{1,17},{... | collective-permute-start | bytes 417800 | tf_op jit(solution)/shard_map/ppermute | solution.py:713
  164.8 1.9 place.3.refs_0_
  166.7 1.8 finish_w_out.1
  168.5 0.8 place.4.refs_0_
  169.4 21.7 %collective-permute-done.11.other = bf16[1,544,128]{2,1,0:T(8,128)(2,1)S(1)} collective-permute-done((bf16[1,544,128]{2,1,0:T(8,128)(2,1)S(1)}, bf16[1,544,128]{2,1,0:T(8,128)(2,1)S(1)}, u32[]{:S(2)}, u32[]{:S(2)}) %collective-permute-start.11) | collective-permute-done | bytes 139296 | tf_op jit(solution)/shard_map/ppermute | solution.py:713
  191.1 0.8 finish.1
  191.9 1.1 place.5
  (43 shorter events, 2.9 us)
Async XLA Ops:
  1.6 8.1 %collective-permute-start = (bf16[4,8,2048]{2,1,0:T(8,128)(2,1)S(1)}, bf16[4,8,2048]{2,1,0:T(8,128)(2,1)S(1)}, u32[]{:S(2)}, u32[]{:S(2)}) collective-permute-start(bf16[4,8,2048]{2,1,0:T(8,128)(2,1)S(1)} %pad_maximum_fusion.3), channel_id=1, source_target_pairs={{0,4},{4,8},{8,12},{12,16},{16,20},{20,24},{24,28},{1,5},{5,9},{9,... | collective-permute-start | bytes 393224 | tf_op jit(solution)/shard_map/ppermute | solution.py:457
  6.5 6.9 %collective-permute-start.1 = (bf16[4,8,2048]{2,1,0:T(8,128)(2,1)S(1)}, bf16[4,8,2048]{2,1,0:T(8,128)(2,1)S(1)}, u32[]{:S(2)}, u32[]{:S(2)}) collective-permute-start(bf16[4,8,2048]{2,1,0:T(8,128)(2,1)S(1)} %pad_maximum_fusion.4), channel_id=1, source_target_pairs={{4,0},{8,4},{12,8},{16,12},{20,16},{24,20},{28,24},{5,1},{9,5},{13... | collective-permute-start | bytes 393224 | tf_op jit(solution)/shard_map/ppermute | solution.py:457
  14.1 16.3 %copy-start.2 = (bf16[1024,256]{1,0:T(8,128)(2,1)S(1)}, bf16[1024,256]{1,0:T(8,128)(2,1)}, u32[]{:S(2)}) copy-start(bf16[1024,256]{1,0:T(8,128)(2,1)} %wv.1) | copy-start | bytes 1572868
  31.5 1.1 copy-start.6
  31.5 1.1 copy-start.7
  31.7 9.0 %collective-permute-start.2 = (bf16[512,512]{1,0:T(8,128)(2,1)S(1)}, bf16[512,512]{1,0:T(8,128)(2,1)S(1)}, u32[]{:S(2)}, u32[]{:S(2)}) collective-permute-start(bf16[512,512]{1,0:T(8,128)(2,1)S(1)} %bitcast.25), channel_id=1, source_target_pairs={{0,1},{1,0},{2,3},{3,2},{4,5},{5,4},{6,7},{7,6},{8,9},{9,8},{10,11... | collective-permute-start | bytes 1572872 | tf_op jit(solution)/shard_map/ppermute | solution.py:510
  34.1 12.3 %all-to-all-start = ((f32[8,2,256]{2,1,0:T(2,128)}), f32[8,2,256]{2,1,0:T(2,128)S(1)}, u32[]{:S(2)}, u32[]{:S(2)}) async-start(f32[8,2,256]{2,1,0:T(2,128)} %get-tuple-element.51), calls=%async_computation | async-start | bytes 32768 | tf_op jit(solution)/shard_map/all_to_all | solution.py:417
  40.7 18.5 %copy-start.1 = (bf16[512,512]{1,0:T(8,128)(2,1)}, bf16[512,512]{1,0:T(8,128)(2,1)S(1)}, u32[]{:S(2)}) copy-start(bf16[512,512]{1,0:T(8,128)(2,1)S(1)} %collective-permute-done.2.w_sibling) | copy-start | bytes 1572868
  46.4 0.6 copy-start.5
  59.2 10.1 %all-to-all-start.1 = ((f32[8,2,256]{2,1,0:T(2,128)}), f32[8,2,256]{2,1,0:T(2,128)S(1)}, u32[]{:S(2)}, u32[]{:S(2)}) async-start(f32[8,2,256]{2,1,0:T(2,128)} %get-tuple-element.55), calls=%async_computation.1 | async-start | bytes 32768 | tf_op jit(solution)/shard_map/all_to_all | solution.py:417
  69.3 0.6 copy-start.3
  74.9 5.6 %collective-permute-start.3 = (bf16[1024,512]{1,0:T(8,128)(2,1)}, bf16[1024,512]{1,0:T(8,128)(2,1)}, u32[]{:S(2)}, u32[]{:S(2)}) collective-permute-start(bf16[1024,512]{1,0:T(8,128)(2,1)} %get-tuple-element.61.own.refs_0_), channel_id=1, source_target_pairs={{0,1},{1,0},{2,3},{3,2},{4,5},{5,4},{6,7},{7,6},{8,9},{9,8},{10,11... | collective-permute-start | bytes 3145736 | tf_op jit(solution)/shard_map/ppermute | solution.py:612
  80.0 15.2 %collective-permute-start.5 = (bf16[1024,512]{1,0:T(8,128)(2,1)}, bf16[1024,512]{1,0:T(8,128)(2,1)}, u32[]{:S(2)}, u32[]{:S(2)}) collective-permute-start(bf16[1024,512]{1,0:T(8,128)(2,1)} %get-tuple-element.63.own.refs_1_), channel_id=1, source_target_pairs={{0,1},{1,0},{2,3},{3,2},{4,5},{5,4},{6,7},{7,6},{8,9},{9,8},{10,11... | collective-permute-start | bytes 3145736 | tf_op jit(solution)/shard_map/ppermute | solution.py:612
  84.8 15.3 %collective-permute-start.6 = (bf16[8,1,32,1024]{3,2,1,0:T(8,128)(2,1)}, bf16[8,1,32,1024]{3,2,1,0:T(8,128)(2,1)S(1)}, u32[]{:S(2)}, u32[]{:S(2)}) collective-permute-start(bf16[8,1,32,1024]{3,2,1,0:T(8,128)(2,1)} %get-tuple-element.67), channel_id=1, source_target_pairs={{0,2},{1,3},{2,0},{3,1},{4,6},{5,7},{6,4},{7,5},{8,10},{9,11},{10,... | collective-permute-start | bytes 1572872 | tf_op jit(solution)/shard_map/ppermute | solution.py:643
  95.1 15.5 %collective-permute-start.4 = (bf16[2048,512]{1,0:T(8,128)(2,1)}, bf16[2048,512]{1,0:T(8,128)(2,1)}, u32[]{:S(2)}, u32[]{:S(2)}) collective-permute-start(bf16[2048,512]{1,0:T(8,128)(2,1)} %get-tuple-element.69.own.refs_2_), channel_id=1, source_target_pairs={{0,1},{1,0},{2,3},{3,2},{4,5},{5,4},{6,7},{7,6},{8,9},{9,8},{10,11... | collective-permute-start | bytes 6291464 | tf_op jit(solution)/shard_map/ppermute | solution.py:612
  99.5 30.7 %collective-permute-start.8 = (bf16[8,1,32,1024]{3,2,1,0:T(8,128)(2,1)}, bf16[8,1,32,1024]{3,2,1,0:T(8,128)(2,1)}, u32[]{:S(2)}, u32[]{:S(2)}) collective-permute-start(bf16[8,1,32,1024]{3,2,1,0:T(8,128)(2,1)} %get-tuple-element.72), channel_id=1, source_target_pairs={{0,2},{1,3},{2,0},{3,1},{4,6},{5,7},{6,4},{7,5},{8,10},{9,11},{10,... | collective-permute-start | bytes 1572872 | tf_op jit(solution)/shard_map/ppermute | solution.py:643
  100.0 0.8 copy-start.8
  104.7 32.2 %all-to-all-start.2 = ((bf16[8,2,32,1024]{3,2,1,0:T(8,128)(2,1)}), bf16[8,2,32,1024]{3,2,1,0:T(8,128)(2,1)}, u32[]{:S(2)}, u32[]{:S(2)}) async-start(bf16[8,2,32,1024]{3,2,1,0:T(8,128)(2,1)} %add_join.1), calls=%async_computation.2 | async-start | bytes 2097152 | tf_op jit(solution)/shard_map/all_to_all | solution.py:417
  117.1 30.4 %collective-permute-start.9 = (bf16[8,2,32,1024]{3,2,1,0:T(8,128)(2,1)}, bf16[8,2,32,1024]{3,2,1,0:T(8,128)(2,1)}, u32[]{:S(2)}, u32[]{:S(2)}) collective-permute-start(bf16[8,2,32,1024]{3,2,1,0:T(8,128)(2,1)} %get-tuple-element.76), channel_id=1, source_target_pairs={{0,2},{1,3},{2,0},{3,1},{4,6},{5,7},{6,4},{7,5},{8,10},{9,11},{10,... | collective-permute-start | bytes 3145736 | tf_op jit(solution)/shard_map/ppermute | solution.py:643
  128.2 19.4 %collective-permute-start.7 = (bf16[4,544,128]{2,1,0:T(8,128)(2,1)}, bf16[4,544,128]{2,1,0:T(8,128)(2,1)}, u32[]{:S(2)}, u32[]{:S(2)}) collective-permute-start(bf16[4,544,128]{2,1,0:T(8,128)(2,1)} %get-tuple-element.81), channel_id=1, source_target_pairs={{0,4},{4,0},{8,12},{12,8},{16,20},{20,16},{24,28},{28,24},{1,5},{5... | collective-permute-start | bytes 1671176 | tf_op jit(solution)/shard_map/ppermute | solution.py:713
  136.9 18.5 %all-to-all-start.3 = ((bf16[8,1,32,1024]{3,2,1,0:T(8,128)(2,1)}), bf16[8,1,32,1024]{3,2,1,0:T(8,128)(2,1)S(1)}, u32[]{:S(2)}, u32[]{:S(2)}) async-start(bf16[8,1,32,1024]{3,2,1,0:T(8,128)(2,1)} %add.114), calls=%async_computation.3 | async-start | bytes 1048576 | tf_op jit(solution)/shard_map/all_to_all | solution.py:417
  140.5 13.0 %copy-start.4 = (f32[8,2,256]{2,1,0:T(2,128)S(1)}, f32[8,2,256]{2,1,0:T(2,128)}, u32[]{:S(2)}) copy-start(f32[8,2,256]{2,1,0:T(2,128)} %copy-done.3) | copy-start | bytes 49156
  151.2 1.1 copy-start
  153.5 6.6 %collective-permute-start.10 = (bf16[2,544,128]{2,1,0:T(8,128)(2,1)S(1)}, bf16[2,544,128]{2,1,0:T(8,128)(2,1)S(1)}, u32[]{:S(2)}, u32[]{:S(2)}) collective-permute-start(bf16[2,544,128]{2,1,0:T(8,128)(2,1)S(1)} %get-tuple-element.89), channel_id=1, source_target_pairs={{0,8},{4,12},{8,0},{12,4},{16,24},{20,28},{24,16},{28,20},{1,9},{5... | collective-permute-start | bytes 835592 | tf_op jit(solution)/shard_map/ppermute | solution.py:713
  155.3 36.6 %all-to-all-start.4 = ((bf16[8,2,32,1024]{3,2,1,0:T(8,128)(2,1)}), bf16[8,2,32,1024]{3,2,1,0:T(8,128)(2,1)S(1)}, u32[]{:S(2)}, u32[]{:S(2)}) async-start(bf16[8,2,32,1024]{3,2,1,0:T(8,128)(2,1)} %add.115), calls=%async_computation.4 | async-start | bytes 2097152 | tf_op jit(solution)/shard_map/all_to_all | solution.py:417
  160.1 30.9 %collective-permute-start.11 = (bf16[1,544,128]{2,1,0:T(8,128)(2,1)S(1)}, bf16[1,544,128]{2,1,0:T(8,128)(2,1)S(1)}, u32[]{:S(2)}, u32[]{:S(2)}) collective-permute-start(bf16[1,544,128]{2,1,0:T(8,128)(2,1)S(1)} %get-tuple-element.91), channel_id=1, source_target_pairs={{0,16},{4,20},{8,24},{12,28},{16,0},{20,4},{24,8},{28,12},{1,17},{... | collective-permute-start | bytes 417800 | tf_op jit(solution)/shard_map/ppermute | solution.py:713
